TPU v7x, 32 devices: a whole 2x2x4 slice. The times are simulated.
32 devices in a mesh: sample: 8 (over y, x, core), cls: 4 (over z).
Axes of the slice: x: 2, y: 2, z: 4, core: 2. Of those that a mesh axis runs over, the one named last changes fastest.
Arguments:
- features: bfloat16 [4096, 2048], P('sample', 'cls'), may hold values from -1.5 to 1.5
- head: bfloat16 [2048, 8192], P('sample', 'cls'), may hold values from -1.5859375 to 1.5859375
- class_cap: bfloat16 [8192], P('cls'), may hold values from 0.5 to 4
Outputs:
- targets: bfloat16 [4096, 8192], P('sample', 'cls')
- grad_features: bfloat16 [4096, 2048], P('sample', 'cls')
- grad_head: bfloat16 [2048, 8192], P('sample', 'cls')
All inputs are finite; a program needn't handle non-finite values.
Results may differ from a plain program's by a relative error of at most 0.02.
Values may be sent and summed in bfloat16 or wider, within the bound.
No kernel may reach another device: no remote copies, remote signals or barrier semaphores. Data moves between devices by JAX's collectives and lax.ppermute only.
A program may use at most 64 MiB of HBM per device.

v0:
```python
import jax
import jax.numpy as jnp
from jax import lax
from jax.sharding import PartitionSpec as P

ITERS = 3


softcap = 15.0
sharpen = 2.0


def row_total(values):
    return lax.psum(jnp.sum(values, axis=1), "cls")


def per_device(features, head, class_cap):
    local_rows = features.shape[0]
    class_local = head.shape[1]
    sample_count = lax.axis_size("sample")
    class_groups = lax.axis_size("cls")
    ratio = local_rows * sample_count / (class_local * class_groups)
    whole = lax.all_gather(features, "cls", axis=1, tiled=True)
    head_full = lax.all_gather(head, "sample", axis=0, tiled=True)
    logits = jnp.dot(whole, head_full, preferred_element_type=jnp.float32)
    capped = softcap * jnp.tanh(logits / softcap)
    student = jnp.exp(capped)
    transport = jnp.exp(capped * sharpen)
    student_mass, plan_mass = lax.psum(
        (jnp.sum(student, axis=1), jnp.sum(transport, axis=1)), "cls"
    )
    student = student / student_mass[:, None]
    ceiling = class_cap.astype(jnp.float32) * ratio
    for iteration in range(ITERS):
        if iteration > 0:
            plan_mass = row_total(transport)
        transport = transport / plan_mass[:, None]
        column_mass = lax.psum(jnp.sum(transport, axis=0), "sample")
        transport = transport * jnp.minimum(1.0, ceiling / column_mass)
    targets = (transport / row_total(transport)[:, None]).astype(jnp.bfloat16)
    tanh_slope = 1.0 - (capped / softcap) ** 2
    grad_logits = ((student - targets.astype(jnp.float32)) * tanh_slope).astype(jnp.bfloat16)
    grad_head = lax.psum_scatter(
        lax.dot_general(
            whole, grad_logits, (((0,), (0,)), ((), ())), preferred_element_type=jnp.float32
        ).astype(jnp.bfloat16),
        "sample",
        scatter_dimension=0,
        tiled=True,
    )
    share = lax.psum_scatter(
        lax.dot_general(
            head_full, grad_logits, (((1,), (1,)), ((), ())), preferred_element_type=jnp.float32
        ).astype(jnp.bfloat16),
        "cls",
        scatter_dimension=0,
        tiled=True,
    ).astype(jnp.float32)
    grad_features = jnp.transpose(share).astype(jnp.bfloat16)
    return (targets, grad_features, grad_head)


def solution(mesh):
    return jax.shard_map(
        per_device,
        mesh=mesh,
        in_specs=(P("sample", "cls"), P("sample", "cls"), P("cls")),
        out_specs=(P("sample", "cls"), P("sample", "cls"), P("sample", "cls")),
        check_vma=False,
    )
```

profile of v0, /device:TPU:0, one launch (start us, length us, event | category | flops | bytes accessed | tf_op | source)
XLA Modules:
  0.0 356.0 jit_solution(3899395366310662426)
XLA Ops:
  7.2 0.0 all-gather.3.cloned.1.call-start
  7.2 0.7 all-gather.3.cloned.1.call-update
  7.9 0.0 all-gather.5.cloned.1.call-start
  7.9 0.7 all-gather.5.cloned.1.call-update
  8.6 0.0 reduce-scatter.5.cloned.1.call-start
  8.7 49.5 %all-gather.3.cloned.1.call-done = bf16[512,2048]{1,0:T(8,128)(2,1)} async-done(((bf16[512,512]{1,0:T(8,128)(2,1)}), bf16[512,2048]{1,0:T(8,128)(2,1)}) %all-gather.3.cloned.1.call-update) | async-done | bytes 2097168 | tf_op jit(solution)/shard_map/all_gather | solution.py:23
  58.2 55.0 %all-gather.5.cloned.1.call-done = bf16[2048,2048]{1,0:T(8,128)(2,1)} async-done(((bf16[256,2048]{1,0:T(8,128)(2,1)}), bf16[2048,2048]{1,0:T(8,128)(2,1)}) %all-gather.5.cloned.1.call-update) | async-done | bytes 8388624 | tf_op jit(solution)/shard_map/all_gather | solution.py:24
  113.3 10.8 %fusion = (f32[512]{0:T(512)S(1)}, f32[512]{0:T(512)S(1)}, f32[512,2048]{1,0:T(8,128)}) fusion(bf16[512,2048]{1,0:T(8,128)(2,1)} %all-gather.3.cloned.1.call-done, bf16[2048,2048]{1,0:T(8,128)(2,1)} %all-gather.5.cloned.1.call-done), kind=kOutput, calls=%fused_computation.3 | convolution fusion | flops 4300209152 | bytes 14684160 | tf_op jit(solution)/shard_map/dot_general | solution.py:25
  124.1 11.7 %psum.56 = f32[512]{0:T(512)S(1)} all-reduce(f32[512]{0:T(512)S(1)} %get-tuple-element.7), channel_id=1, replica_groups=mesh['sample'=8,'cls'=4] {'cls'}, use_global_device_ids=true, to_apply=%region_1.0 | all-reduce | flops 512 | bytes 4096 | tf_op jit(solution)/shard_map/psum | solution.py:29
  135.7 0.0 copy-start.2
  135.7 5.1 %fusion.6 = (f32[2048]{0:T(1024)S(1)}, f32[512,2048]{1,0:T(8,128)}) fusion(f32[512]{0:T(512)S(1)} %psum.56, f32[512,2048]{1,0:T(8,128)} %get-tuple-element.14), kind=kLoop, calls=%fused_computation.22 | loop fusion | flops 3143680 | bytes 8398848 | tf_op jit(solution)/shard_map/reduce_sum | solution.py:38
  140.8 12.1 %psum.57 = f32[2048]{0:T(1024)S(1)} all-reduce(f32[2048]{0:T(1024)S(1)} %get-tuple-element.12), channel_id=1, replica_groups=mesh['sample'=8,'cls'=4] {'sample'}, use_global_device_ids=true, to_apply=%region_3.0 | all-reduce | flops 2048 | bytes 16384 | tf_op jit(solution)/shard_map/psum | solution.py:38
  152.9 0.0 copy-done.2
  152.9 2.5 multiply_reduce_fusion.2
  155.5 8.4 %psum.58 = f32[512]{0:T(512)S(1)} all-reduce(f32[512]{0:T(512)S(1)} %multiply_reduce_fusion.2), channel_id=1, replica_groups=mesh['sample'=8,'cls'=4] {'cls'}, use_global_device_ids=true, to_apply=%region_5.0 | all-reduce | flops 512 | bytes 4096 | tf_op jit(solution)/shard_map/psum | solution.py:14
  163.9 2.8 fusion.4
  166.6 12.0 %psum.59 = f32[2048]{0:T(1024)S(1)} all-reduce(f32[2048]{0:T(1024)S(1)} %fusion.4), channel_id=1, replica_groups=mesh['sample'=8,'cls'=4] {'sample'}, use_global_device_ids=true, to_apply=%region_7.0 | all-reduce | flops 2048 | bytes 16384 | tf_op jit(solution)/shard_map/psum | solution.py:38
  178.7 2.9 multiply_reduce_fusion.1
  181.6 10.4 %psum.60 = f32[512]{0:T(512)S(1)} all-reduce(f32[512]{0:T(512)S(1)} %multiply_reduce_fusion.1), channel_id=1, replica_groups=mesh['sample'=8,'cls'=4] {'cls'}, use_global_device_ids=true, to_apply=%region_9.0 | all-reduce | flops 512 | bytes 4096 | tf_op jit(solution)/shard_map/psum | solution.py:14
  192.0 5.2 %fusion.5 = (f32[2048]{0:T(1024)S(1)}, f32[512,2048]{1,0:T(8,128)}) fusion(f32[512]{0:T(512)S(1)} %psum.60, f32[2048]{0:T(1024)S(1)} %divide_minimum_fusion.1, f32[512]{0:T(512)S(1)} %psum.58, f32[512,2048]{1,0:T(8,128)} %get-tuple-element.13, f32[2048]{0:T(1024)S(1)} %divide_minimum_fusion.2), kind=kLoop, calls=%fused_computation.21 | loop fusion | flops 5240832 | bytes 8417280 | tf_op jit(solution)/shard_map/reduce_sum | solution.py:38
  197.2 12.0 %psum.61 = f32[2048]{0:T(1024)S(1)} all-reduce(f32[2048]{0:T(1024)S(1)} %get-tuple-element.10), channel_id=1, replica_groups=mesh['sample'=8,'cls'=4] {'sample'}, use_global_device_ids=true, to_apply=%region_11.0 | all-reduce | flops 2048 | bytes 16384 | tf_op jit(solution)/shard_map/psum | solution.py:38
  209.2 2.5 multiply_reduce_fusion
  211.8 8.5 %all-reduce = (f32[512]{0:T(512)S(1)}, f32[512]{0:T(512)S(1)}) all-reduce(f32[512]{0:T(512)S(1)} %multiply_reduce_fusion, f32[512]{0:T(512)S(1)} %get-tuple-element.6), channel_id=1, replica_groups=mesh['sample'=8,'cls'=4] {'cls'}, use_global_device_ids=true, to_apply=%region_13.0 | all-reduce | flops 1024 | bytes 8192 | tf_op jit(solution)/shard_map/psum | solution.py:14
  220.3 0.0 copy-start
  220.3 3.0 divide_convert_fusion
  223.3 0.0 copy-start.1
  223.3 0.4 copy-done
  223.8 9.3 %convert_bitcast_fusion = bf16[2048,2048]{0,1:T(8,128)(2,1)} fusion(bf16[512,2048]{1,0:T(8,128)(2,1)} %all-gather.3.cloned.1.call-done, f32[512,2048]{1,0:T(8,128)S(1)} %copy-done, bf16[512,2048]{1,0:T(8,128)(2,1)S(1)} %divide_convert_fusion, f32[512]{0:T(512)S(1)} %get-tuple-element.9), kind=kOutput, calls=%fused_computation | convolution fusion | flops 4307550208 | bytes 16779264 | tf_op jit(solution)/shard_map/dot_general | solution.py:44
  233.1 0.0 reduce-scatter.5.cloned.1.call-update
  233.1 0.0 reduce-scatter.3.cloned.1.call-start
  233.1 0.0 copy-done.1
  233.1 11.5 %fusion.3 = bf16[2048,512]{0,1:T(8,128)(2,1)} fusion(bf16[2048,2048]{1,0:T(8,128)(2,1)} %all-gather.5.cloned.1.call-done, f32[512,2048]{1,0:T(8,128)} %get-tuple-element.14, bf16[512,2048]{1,0:T(8,128)(2,1)S(1)} %divide_convert_fusion, f32[512]{0:T(512)S(1)} %get-tuple-element.9), kind=kOutput, calls=%fused_computation.15 | convolution fusion | flops 4304404480 | bytes 16779264 | tf_op jit(solution)/shard_map/dot_general | solution.py:52
  244.6 0.0 reduce-scatter.3.cloned.1.call-update
  244.6 58.2 %reduce-scatter.5.cloned.1.call-done = bf16[256,2048]{0,1:T(8,128)(2,1)} async-done(((bf16[2048,2048]{0,1:T(8,128)(2,1)}), bf16[256,2048]{0,1:T(8,128)(2,1)}) %reduce-scatter.5.cloned.1.call-update) | async-done | bytes 1048592 | tf_op jit(solution)/shard_map/reduce_scatter | solution.py:43
  302.8 2.3 copy.6
  305.1 44.4 %reduce-scatter.3.cloned.1.call-done = bf16[512,512]{0,1:T(8,128)(2,1)} async-done(((bf16[2048,512]{0,1:T(8,128)(2,1)}), bf16[512,512]{0,1:T(8,128)(2,1)}) %reduce-scatter.3.cloned.1.call-update) | async-done | bytes 524304 | tf_op jit(solution)/shard_map/reduce_scatter | solution.py:51
  (3 shorter events, 0.0 us)
Async XLA Ops:
  7.2 51.1 %all-gather.3.cloned.1.call-start = ((), (), s32[]{:S(2)}) async-start(), calls=%async_computation.2 | async-start | bytes 2621440 | tf_op jit(solution)/shard_map/all_gather | solution.py:23
  7.9 105.4 %all-gather.5.cloned.1.call-start = ((), (), s32[]{:S(2)}) async-start(), calls=%async_computation.3 | async-start | bytes 9437184 | tf_op jit(solution)/shard_map/all_gather | solution.py:24
  8.6 294.2 %reduce-scatter.5.cloned.1.call-start = ((), (), s32[]{:S(2)}) async-start(), calls=%async_computation.5 | async-start | bytes 9437184 | tf_op jit(solution)/shard_map/reduce_scatter | solution.py:43
  135.7 17.2 %copy-start.2 = (bf16[2048]{0:T(1024)(128)(2,1)S(1)}, bf16[2048]{0:T(1024)(128)(2,1)}, u32[]{:S(2)}) copy-start(bf16[2048]{0:T(1024)(128)(2,1)} %param.5) | copy-start | bytes 12292
  220.3 3.4 copy-start
  223.3 9.8 %copy-start.1 = (bf16[512,2048]{1,0:T(8,128)(2,1)}, bf16[512,2048]{1,0:T(8,128)(2,1)S(1)}, u32[]{:S(2)}) copy-start(bf16[512,2048]{1,0:T(8,128)(2,1)S(1)} %divide_convert_fusion) | copy-start | bytes 6291460
  233.1 116.4 %reduce-scatter.3.cloned.1.call-start = ((), (), s32[]{:S(2)}) async-start(), calls=%async_computation.4 | async-start | bytes 2621440 | tf_op jit(solution)/shard_map/reduce_scatter | solution.py:51
Sparse Core Ops, SparseCore 0:
  9.6 48.6 all-gather.2
  60.1 53.0 all-gather.4
  233.2 69.5 reduce-scatter.4
  305.6 43.8 reduce-scatter.2
where the time goes:
time: 357 us; the launch traced here: 356 us
  waiting for transfers between devices  209 us (59%)
  blocking collectives  75.1 us (21%)
  matrix products  31.6 us (9%)
  other arithmetic  24.1 us (7%)
  between operations  13.8 us (4%)
    reduce_scatter x1, waiting for transfers between devices, per_device(): lax.psum_scatter(lax.dot_general(whole, grad_logits, (((0,), (0,)), ((),...  58.2 us
    all_gather x1, waiting for transfers between devices, per_device(): head_full = lax.all_gather(head, 'sample', axis=0, tiled=True)  55 us
    all_gather x1, waiting for transfers between devices, per_device(): whole = lax.all_gather(features, 'cls', axis=1, tiled=True)  49.5 us
    reduce_scatter x1, waiting for transfers between devices, per_device(): lax.psum_scatter(lax.dot_general(head_full, grad_logits, (((1,), (1,)), (...  44.4 us
    psum x3, blocking collectives, per_device(): column_mass = lax.psum(jnp.sum(transport, axis=0), 'sample')  36.2 us
    psum x3, blocking collectives, row_total(): return lax.psum(jnp.sum(values, axis=1), 'cls')  27.3 us
    reduce_sum x3, other arithmetic, per_device(): column_mass = lax.psum(jnp.sum(transport, axis=0), 'sample')  13.1 us
    psum x1, blocking collectives, per_device(): lax.psum((jnp.sum(student, axis=1), jnp.sum(transport, axis=1)), 'cls')  11.7 us
  transfers between devices with their start and end apart: 4, of which 4 were waited for; matrix products, arithmetic and copies ran while one was open for 4% of the time, Pallas kernels for 0%

commit v1 on v0

v1 whole, which is shorter than its diff:
```python
import jax
import jax.numpy as jnp
from jax import lax
from jax.sharding import PartitionSpec as P

ITERS = 3


softcap = 15.0
sharpen = 2.0
f32 = jnp.float32
bf16 = jnp.bfloat16


def matmul(left, right, dims):
    return lax.dot_general(left, right, (dims, ((), ())), preferred_element_type=f32)


def flip(value, axis, mask):
    size = lax.axis_size(axis)
    return lax.ppermute(value, axis, [(i, i ^ mask) for i in range(size)])


def step(value, axis, hop):
    size = lax.axis_size(axis)
    pairs = [(i, i + hop) for i in range(size) if 0 <= i + hop < size]
    return lax.ppermute(value, axis, pairs)


def row_total(value):
    size = lax.axis_size("cls")
    shifted = [
        lax.ppermute(value, "cls", [(i, (i + hop) % size) for i in range(size)])
        for hop in range(1, size)
    ]
    return sum(shifted, value)


def column_total(value):
    size = lax.axis_size("sample")
    value = value + flip(value, "sample", 1)
    others = [flip(value, "sample", mask) for mask in range(2, size, 2)]
    return sum(others, value)


def chip_axes(size):
    chips = size // 2
    bits = chips.bit_length() - 1
    low = 1 << ((bits + 1) // 2)
    first = [2 * m for m in range(1, low)]
    second = [2 * low * m for m in range(1, chips // low)]
    return first, second


def gather_head(head):
    size = lax.axis_size("sample")
    first, second = chip_axes(size)
    held = {0: head}
    for mask in first + second:
        held[mask] = flip(head, "sample", mask)
    half = head.shape[0] // 2
    for a in first:
        for b in second:
            top = flip(held[a][:half], "sample", b)
            bottom = flip(held[b][half:], "sample", a)
            held[a | b] = jnp.concatenate([top, bottom], axis=0)
    return held


def gather_features(features):
    size = lax.axis_size("cls")
    me = lax.axis_index("cls")
    right, left = [], []
    up = down = features
    for _ in range(1, size):
        up = step(up, "cls", 1)
        down = step(down, "cls", -1)
        right.append(up)
        left.append(down)
    blocks = [features] + [
        jnp.where(me >= hop, right[hop - 1], left[size - hop - 1]) for hop in range(1, size)
    ]
    width = features.shape[1]
    whole = jnp.zeros((features.shape[0], width * size), features.dtype)
    for hop, block in enumerate(blocks):
        whole = lax.dynamic_update_slice(whole, block, (0, lax.rem(me - hop + size, size) * width))
    return whole


def scatter_features(block_of):
    size = lax.axis_size("cls")
    me = lax.axis_index("cls")
    clip = lambda index: jnp.clip(index, 0, size - 1)
    up = down = None
    for t in range(1, size):
        right = block_of(clip(size - t + me))
        leftward = block_of(clip(me - (size - t)))
        if up is not None:
            right = (right.astype(f32) + up.astype(f32)).astype(bf16)
            leftward = (leftward.astype(f32) + down.astype(f32)).astype(bf16)
        up = step(right, "cls", 1)
        down = step(leftward, "cls", -1)
    return (block_of(me).astype(f32) + up.astype(f32) + down.astype(f32)).astype(bf16)


def scatter_head(partial_of):
    size = lax.axis_size("sample")
    first, second = chip_axes(size)

    def both(mask):
        other = flip(partial_of(mask | 1), "sample", 1)
        return partial_of(mask).astype(f32) + other.astype(f32)

    half = partial_of(0).shape[0] // 2
    tops, bottoms = {}, {}
    for a in first:
        for b in second:
            block = both(a | b).astype(bf16)
            tops.setdefault(b, []).append(flip(block[:half], "sample", a))
            bottoms.setdefault(a, []).append(flip(block[half:], "sample", b))
    total = None
    for mask in first + second:
        block = both(mask)
        top, bottom = block[:half], block[half:]
        for part in tops.get(mask, []):
            top = top + part.astype(f32)
        for part in bottoms.get(mask, []):
            bottom = bottom + part.astype(f32)
        sent = flip(jnp.concatenate([top, bottom], axis=0).astype(bf16), "sample", mask).astype(f32)
        total = sent if total is None else total + sent
    return (both(0) + total).astype(bf16)


def per_device(features, head, class_cap):
    local_rows = features.shape[0]
    depth = head.shape[0]
    class_local = head.shape[1]
    sample_count = lax.axis_size("sample")
    class_groups = lax.axis_size("cls")
    ratio = local_rows * sample_count / (class_local * class_groups)
    me = lax.axis_index("sample")
    core = me & 1

    same = gather_head(head)
    whole = gather_features(features)
    masks = sorted(same)
    pieces = []
    for mask in masks:
        sibling = flip(same[mask], "sample", 1)
        pieces.append(jnp.where(core == 0, same[mask], sibling))
        pieces.append(jnp.where(core == 0, sibling, same[mask]))
    head_full = jnp.concatenate(pieces, axis=0)
    wide = jnp.concatenate(
        [
            lax.dynamic_slice(whole, (0, ((me >> 1) ^ (mask >> 1)) * 2 * depth), (local_rows, 2 * depth))
            for mask in masks
        ],
        axis=1,
    )
    logits = matmul(wide, head_full, ((1,), (0,)))
    tanh = jnp.tanh(logits / softcap)
    student = jnp.exp(softcap * tanh)
    plan = student * student
    masses = row_total(jnp.stack([jnp.sum(student, axis=1), jnp.sum(plan, axis=1)]))
    ceiling = class_cap.astype(f32) * ratio
    row_mass = masses[1]
    scale = jnp.ones((class_local,), f32)
    for iteration in range(ITERS):
        if iteration > 0:
            row_mass = row_total(jnp.sum(plan * scale[None, :], axis=1))
        mass = column_total(jnp.sum(plan * (1.0 / row_mass)[:, None], axis=0) * scale)
        scale = scale * jnp.minimum(1.0, ceiling / mass)
    row_mass = row_total(jnp.sum(plan * scale[None, :], axis=1))
    targets = (plan * scale[None, :] * (1.0 / row_mass)[:, None]).astype(bf16)
    slope = 1.0 - tanh * tanh
    grad_logits = ((student * (1.0 / masses[0])[:, None] - targets.astype(f32)) * slope).astype(bf16)

    def head_partial(mask):
        first = (me ^ mask) * depth
        columns = lax.dynamic_slice(whole, (0, first), (local_rows, depth))
        return matmul(columns, grad_logits, ((0,), (0,))).astype(bf16)

    partials = {mask: head_partial(mask) for mask in range(sample_count)}
    shares = matmul(grad_logits, head_full, ((1,), (1,))).astype(bf16)
    width = features.shape[1]

    def feature_block(index):
        return lax.dynamic_slice(shares, (0, (index ^ (me >> 1)) * width), (local_rows, width))

    grad_features = scatter_features(feature_block)
    grad_head = scatter_head(lambda mask: partials[mask])
    return (targets, grad_features, grad_head)


def solution(mesh):
    return jax.shard_map(
        per_device,
        mesh=mesh,
        in_specs=(P("sample", "cls"), P("sample", "cls"), P("cls")),
        out_specs=(P("sample", "cls"), P("sample", "cls"), P("sample", "cls")),
        check_vma=False,
    )
```

time: 357 us -> 208 us (0.58)
  waiting for transfers between devices: 209 us -> 85.3 us
  blocking collectives: 75.1 us -> 0 us
  starting transfers between devices: 0.16 us -> 69.1 us
  between operations: 13.8 us -> 1.33 us
  matrix products: 31.6 us -> 22.2 us
    all_gather x2 -> x0, waiting for transfers between devices: 105 us -> none  [the longest x1 55 us: per_device(): head_full = lax.all_gather(head, 'sample', axis=0, tiled=True)]
    reduce_scatter x2 -> x0, waiting for transfers between devices: 103 us -> none  [the longest x1 58.2 us: per_device(): lax.psum_scatter(lax.dot_general(whole, grad_logits, (((0,), (0,)), ((),...]
    ppermute x0 -> x52, waiting for transfers between devices: none -> 85.3 us  [the longest x12 47.1 us: step(): return lax.ppermute(value, axis, pairs)]
    psum x7 -> x0, blocking collectives: 75.1 us -> none  [the longest x3 36.2 us: per_device(): column_mass = lax.psum(jnp.sum(transport, axis=0), 'sample')]
    ppermute x0 -> x52, starting transfers between devices: none -> 69.1 us  [the longest x12 33.7 us: step(): return lax.ppermute(value, axis, pairs)]
    reduce_sum x6, other arithmetic: 21.1 us -> 7.42 us  [the longest x3 4.9 us: per_device(): row_mass = row_total(jnp.sum(plan * scale[None, :], axis=1))]
    dot_general x3 -> x10, matrix products: 31.6 us -> 22.2 us  [matmul(): lax.dot_general(left, right, (dims, ((), ())), preferred_element_type=f32)]
    convert_element_type x1 -> x5, other arithmetic: 3 us -> 10.5 us  [the longest x1 4.33 us: per_device(): ((student * (1.0 / masses[0])[:, None] - targets.astype(f32)) * slope).as...]
  transfers between devices with their start and end apart: 4 -> 52, of which waited for: 4 -> 33; matrix products, arithmetic and copies ran while one was open for 4% -> 9% of each run, Pallas kernels for 0% -> 0%
where the time goes in v1:
time: 208 us; the launch traced here: 207 us
  waiting for transfers between devices  85.3 us (41%)
  starting transfers between devices  69.1 us (33%)
  other arithmetic  26 us (12%)
  matrix products  22.2 us (11%)
  local copies, waits for them, and re-layouts  2.9 us (1%)
    ppermute x12, waiting for transfers between devices, step(): return lax.ppermute(value, axis, pairs)  47.1 us
    ppermute x12, starting transfers between devices, step(): return lax.ppermute(value, axis, pairs)  33.7 us
    ppermute x28, waiting for transfers between devices, flip(): return lax.ppermute(value, axis, [(i, i ^ mask) for i in range(size)])  22.8 us
    dot_general x10, matrix products, matmul(): lax.dot_general(left, right, (dims, ((), ())), preferred_element_type=f32)  22.2 us
    ppermute x28, starting transfers between devices, flip(): return lax.ppermute(value, axis, [(i, i ^ mask) for i in range(size)])  21.1 us
    ppermute x12, waiting for transfers between devices, row_total(): lax.ppermute(value, 'cls', [(i, (i + hop) % size) for i in range(size)])  15.4 us
    ppermute x12, starting transfers between devices, row_total(): lax.ppermute(value, 'cls', [(i, (i + hop) % size) for i in range(size)])  14.3 us
    reduce_sum x3, other arithmetic, per_device(): row_mass = row_total(jnp.sum(plan * scale[None, :], axis=1))  4.9 us
  transfers between devices with their start and end apart: 52, of which 33 were waited for; matrix products, arithmetic and copies ran while one was open for 9% of the time, Pallas kernels for 0%

profile of v1, /device:TPU:0, one launch (start us, length us, event | category | flops | bytes accessed | tf_op | source)
XLA Modules:
  0.0 206.8 jit_solution(11459821488424667534)
XLA Ops:
  0.6 3.0 %collective-permute-start.7 = (bf16[256,2048]{1,0:T(8,128)(2,1)}, bf16[256,2048]{1,0:T(8,128)(2,1)S(1)}, u32[]{:S(2)}, u32[]{:S(2)}) collective-permute-start(bf16[256,2048]{1,0:T(8,128)(2,1)} %param.4), channel_id=1, source_target_pairs={{0,8},{4,12},{8,0},{12,4},{16,24},{20,28},{24,16},{28,20},{1,9},{5... | collective-permute-start | bytes 3145736 | tf_op jit(solution)/shard_map/ppermute | solution.py:21
  3.6 1.5 collective-permute-start.9
  5.2 1.3 collective-permute-start.1
  6.4 5.4 %collective-permute-start = (bf16[512,512]{1,0:T(8,128)(2,1)}, bf16[512,512]{1,0:T(8,128)(2,1)}, u32[]{:S(2)}, u32[]{:S(2)}) collective-permute-start(bf16[512,512]{1,0:T(8,128)(2,1)} %param.3), channel_id=1, source_target_pairs={{0,1},{1,2},{2,3},{4,5},{5,6},{6,7},{8,9},{9,10},{10,11},{12,13},{... | collective-permute-start | bytes 1572872 | tf_op jit(solution)/shard_map/ppermute | solution.py:27
  11.8 9.9 %collective-permute-done.1 = bf16[512,512]{1,0:T(8,128)(2,1)} collective-permute-done((bf16[512,512]{1,0:T(8,128)(2,1)}, bf16[512,512]{1,0:T(8,128)(2,1)}, u32[]{:S(2)}, u32[]{:S(2)}) %collective-permute-start.1) | collective-permute-done | bytes 524320 | tf_op jit(solution)/shard_map/ppermute | solution.py:27
  24.2 4.7 %collective-permute-start.4 = (bf16[512,512]{1,0:T(8,128)(2,1)}, bf16[512,512]{1,0:T(8,128)(2,1)S(1)}, u32[]{:S(2)}, u32[]{:S(2)}) collective-permute-start(bf16[512,512]{1,0:T(8,128)(2,1)} %collective-permute-done), channel_id=1, source_target_pairs={{0,1},{1,2},{2,3},{4,5},{5,6},{6,7},{8,9},{9,10},{10,11},{12,13},{... | collective-permute-start | bytes 1572872 | tf_op jit(solution)/shard_map/ppermute | solution.py:27
  30.5 7.0 %collective-permute-done.2 = bf16[512,512]{1,0:T(8,128)(2,1)} collective-permute-done((bf16[512,512]{1,0:T(8,128)(2,1)}, bf16[512,512]{1,0:T(8,128)(2,1)}, u32[]{:S(2)}, u32[]{:S(2)}) %collective-permute-start.2) | collective-permute-done | bytes 524320 | tf_op jit(solution)/shard_map/ppermute | solution.py:27
  37.4 1.3 collective-permute-start.3
  39.9 2.1 collective-permute-done.11
  42.0 3.5 %collective-permute-start.5 = (bf16[512,512]{1,0:T(8,128)(2,1)S(1)}, bf16[512,512]{1,0:T(8,128)(2,1)S(1)}, u32[]{:S(2)}, u32[]{:S(2)}) collective-permute-start(bf16[512,512]{1,0:T(8,128)(2,1)S(1)} %collective-permute-done.4), channel_id=1, source_target_pairs={{0,1},{1,2},{2,3},{4,5},{5,6},{6,7},{8,9},{9,10},{10,11},{12,13},{... | collective-permute-start | bytes 1572872 | tf_op jit(solution)/shard_map/ppermute | solution.py:27
  45.7 6.5 %collective-permute-done.3 = bf16[512,512]{1,0:T(8,128)(2,1)S(1)} collective-permute-done((bf16[512,512]{1,0:T(8,128)(2,1)}, bf16[512,512]{1,0:T(8,128)(2,1)S(1)}, u32[]{:S(2)}, u32[]{:S(2)}) %collective-permute-start.3) | collective-permute-done | bytes 524320 | tf_op jit(solution)/shard_map/ppermute | solution.py:27
  53.6 2.5 %collective-permute-done.5 = bf16[512,512]{1,0:T(8,128)(2,1)S(1)} collective-permute-done((bf16[512,512]{1,0:T(8,128)(2,1)S(1)}, bf16[512,512]{1,0:T(8,128)(2,1)S(1)}, u32[]{:S(2)}, u32[]{:S(2)}) %collective-permute-start.5) | collective-permute-done | bytes 524320 | tf_op jit(solution)/shard_map/ppermute | solution.py:27
  61.0 5.0 %fusion = (f32[512]{0:T(512)S(1)}, f32[512]{0:T(512)S(1)}, f32[512,2048]{1,0:T(8,128)S(1)}) fusion(bf16[2048,2048]{1,0:T(8,128)(2,1)S(1)} %select_dynamic-update-slice_fusion, bf16[512,512]{1,0:T(8,128)(2,1)S(1)} %get-tuple-element.12, bf16[512,512]{1,0:T(8,128)(2,1)S(1)} %get-tuple-element.13, bf16[512,512]{1,0:T(8,128)(2,1)S(1)} %get-tuple-element.14, ...), kind=kOutput, calls=%fused_computation.8 | convolution fusion | flops 4308597760 | bytes 14684160 | tf_op jit(solution)/shard_map/dot_general | solution.py:16
  66.1 4.2 %collective-permute-start.16 = (f32[2,512]{1,0:T(2,128)S(1)}, f32[2,512]{1,0:T(2,128)S(1)}, u32[]{:S(2)}, u32[]{:S(2)}) collective-permute-start(f32[2,512]{1,0:T(2,128)S(1)} %pad_maximum_fusion.2), channel_id=1, source_target_pairs={{0,3},{1,0},{2,1},{3,2},{4,7},{5,4},{6,5},{7,6},{8,11},{9,8},{10,9... | collective-permute-start | bytes 12296 | tf_op jit(solution)/shard_map/ppermute | solution.py:33
  70.3 1.3 collective-permute-start.14
  71.6 3.2 %collective-permute-done.15 = f32[2,512]{1,0:T(2,128)S(1)} collective-permute-done((f32[2,512]{1,0:T(2,128)S(1)}, f32[2,512]{1,0:T(2,128)S(1)}, u32[]{:S(2)}, u32[]{:S(2)}) %collective-permute-start.15) | collective-permute-done | bytes 4128 | tf_op jit(solution)/shard_map/ppermute | solution.py:33
  78.3 1.5 collective-permute-start.19
  79.8 1.5 collective-permute-start.18
  85.7 1.9 collective-permute-start.21
  88.1 1.5 collective-permute-done.22
  89.5 1.5 collective-permute-done.21
  93.2 1.4 collective-permute-start.27
  94.6 1.5 collective-permute-start.26
  98.3 1.5 collective-permute-done.25
  100.7 1.4 collective-permute-start.30
  104.3 2.3 %collective-permute-done.29 = f32[512]{0:T(512)S(1)} collective-permute-done((f32[512]{0:T(512)S(1)}, f32[512]{0:T(512)S(1)}, u32[]{:S(2)}, u32[]{:S(2)}) %collective-permute-start.29) | collective-permute-done | bytes 2080 | tf_op jit(solution)/shard_map/ppermute | solution.py:33
  110.3 1.5 collective-permute-start.33
  111.9 1.5 collective-permute-start.32
  115.5 3.1 %multiply_reduce_fusion.5 = f32[512]{0:T(512)S(1)} fusion(f32[2048]{0:T(1024)S(1)} %minimum_multiply_fusion, f32[512,2048]{1,0:T(8,128)} %copy-done), kind=kLoop, calls=%fused_computation.11 | loop fusion | flops 4193792 | bytes 4204544 | tf_op jit(solution)/shard_map/reduce_sum | solution.py:173
  119.6 1.9 collective-permute-start.35
  122.2 1.9 collective-permute-done.36
  125.0 4.3 %multiply_convert_fusion = (bf16[512,2048]{1,0:T(8,128)(2,1)S(1)}, bf16[512,2048]{1,0:T(8,128)(2,1)}) fusion(f32[512,2048]{1,0:T(8,128)} %copy-done, f32[512]{0:T(512)S(1)} %bitcast.15, f32[512]{0:T(512)S(1)} %add_divide_fusion, f32[2048]{0:T(1024)S(1)} %minimum_multiply_fusion), kind=kLoop, calls=%fused_computation | loop fusion | flops 12582912 | bytes 8400896 | tf_op jit(solution)/shard_map/convert_element_type | solution.py:176
  129.4 8.1 %convolution_convert_fusion = bf16[512,2048]{1,0:T(8,128)(2,1)S(1)} fusion(bf16[512,2048]{1,0:T(8,128)(2,1)S(1)} %get-tuple-element.5, bf16[2048,2048]{1,0:T(8,128)(2,1)} %copy-done.6), kind=kOutput, calls=%fused_computation.12 | convolution fusion | flops 4296015872 | bytes 12582912 | tf_op jit(solution)/shard_map/dot_general | solution.py:16
  137.6 2.3 %collective-permute-start.38 = (bf16[512,512]{1,0:T(8,128)(2,1)S(1)}, bf16[512,512]{1,0:T(8,128)(2,1)S(1)}, u32[]{:S(2)}, u32[]{:S(2)}) collective-permute-start(bf16[512,512]{1,0:T(8,128)(2,1)S(1)} %get-tuple-element.9), channel_id=1, source_target_pairs={{0,1},{1,2},{2,3},{4,5},{5,6},{6,7},{8,9},{9,10},{10,11},{12,13},{... | collective-permute-start | bytes 1572872 | tf_op jit(solution)/shard_map/ppermute | solution.py:27
  140.0 1.3 collective-permute-start.41
  143.4 5.2 %collective-permute-done.38 = bf16[512,512]{1,0:T(8,128)(2,1)S(1)} collective-permute-done((bf16[512,512]{1,0:T(8,128)(2,1)S(1)}, bf16[512,512]{1,0:T(8,128)(2,1)S(1)}, u32[]{:S(2)}, u32[]{:S(2)}) %collective-permute-start.38) | collective-permute-done | bytes 524320 | tf_op jit(solution)/shard_map/ppermute | solution.py:27
  148.8 4.4 %collective-permute-start.39 = (bf16[512,512]{1,0:T(8,128)(2,1)S(1)}, bf16[512,512]{1,0:T(8,128)(2,1)S(1)}, u32[]{:S(2)}, u32[]{:S(2)}) collective-permute-start(bf16[512,512]{1,0:T(8,128)(2,1)S(1)} %add_convert_fusion.4), channel_id=1, source_target_pairs={{0,1},{1,2},{2,3},{4,5},{5,6},{6,7},{8,9},{9,10},{10,11},{12,13},{... | collective-permute-start | bytes 1572872 | tf_op jit(solution)/shard_map/ppermute | solution.py:27
  155.4 5.5 %collective-permute-done.39 = bf16[512,512]{1,0:T(8,128)(2,1)S(1)} collective-permute-done((bf16[512,512]{1,0:T(8,128)(2,1)S(1)}, bf16[512,512]{1,0:T(8,128)(2,1)S(1)}, u32[]{:S(2)}, u32[]{:S(2)}) %collective-permute-start.39) | collective-permute-done | bytes 524320 | tf_op jit(solution)/shard_map/ppermute | solution.py:27
  160.9 1.4 add_convert_fusion.3
  162.3 1.5 collective-permute-start.42
  167.9 6.1 %collective-permute-done.50 = bf16[128,2048]{1,0:T(8,128)(2,1)S(1)} collective-permute-done((bf16[128,2048]{1,0:T(8,128)(2,1)S(1)}, bf16[128,2048]{1,0:T(8,128)(2,1)S(1)}, u32[]{:S(2)}, u32[]{:S(2)}) %collective-permute-start.50) | collective-permute-done | bytes 524320 | tf_op jit(solution)/shard_map/ppermute | solution.py:21
  175.8 3.7 %collective-permute-done.47 = bf16[128,2048]{1,0:T(8,128)(2,1)S(1)} collective-permute-done((bf16[128,2048]{1,0:T(8,128)(2,1)S(1)}, bf16[128,2048]{1,0:T(8,128)(2,1)S(1)}, u32[]{:S(2)}, u32[]{:S(2)}) %collective-permute-start.47) | collective-permute-done | bytes 524320 | tf_op jit(solution)/shard_map/ppermute | solution.py:21
  181.6 5.4 %collective-permute-start.40 = (bf16[512,512]{1,0:T(8,128)(2,1)}, bf16[512,512]{1,0:T(8,128)(2,1)}, u32[]{:S(2)}, u32[]{:S(2)}) collective-permute-start(bf16[512,512]{1,0:T(8,128)(2,1)} %get-tuple-element.7), channel_id=1, source_target_pairs={{0,1},{1,2},{2,3},{4,5},{5,6},{6,7},{8,9},{9,10},{10,11},{12,13},{... | collective-permute-start | bytes 1572872 | tf_op jit(solution)/shard_map/ppermute | solution.py:27
  187.0 2.2 %add_convert_fusion.1 = bf16[512,512]{1,0:T(8,128)(2,1)} fusion(bf16[512,512]{1,0:T(8,128)(2,1)} %collective-permute-done.42, bf16[512,2048]{1,0:T(8,128)(2,1)} %copy-done.3, s32[]{:T(128)S(6)} %select_n.152), kind=kLoop, calls=%fused_computation.48 | loop fusion | flops 1048576 | bytes 1572868 | tf_op jit(solution)/shard_map/convert_element_type | solution.py:100
  190.5 2.7 %collective-permute-done.40 = bf16[512,512]{1,0:T(8,128)(2,1)} collective-permute-done((bf16[512,512]{1,0:T(8,128)(2,1)}, bf16[512,512]{1,0:T(8,128)(2,1)}, u32[]{:S(2)}, u32[]{:S(2)}) %collective-permute-start.40) | collective-permute-done | bytes 524320 | tf_op jit(solution)/shard_map/ppermute | solution.py:27
  193.2 7.4 %collective-permute-done.43 = bf16[512,512]{1,0:T(8,128)(2,1)} collective-permute-done((bf16[512,512]{1,0:T(8,128)(2,1)}, bf16[512,512]{1,0:T(8,128)(2,1)}, u32[]{:S(2)}, u32[]{:S(2)}) %collective-permute-start.43) | collective-permute-done | bytes 524320 | tf_op jit(solution)/shard_map/ppermute | solution.py:27
  200.6 2.4 %add_convert_fusion = bf16[512,512]{1,0:T(8,128)(2,1)} fusion(bf16[512,512]{1,0:T(8,128)(2,1)} %collective-permute-done.43, bf16[512,512]{1,0:T(8,128)(2,1)} %collective-permute-done.40, bf16[512,2048]{1,0:T(8,128)(2,1)} %copy-done.3, s32[]{:T(128)S(6)} %select_n.148), kind=kLoop, calls=%fused_computation.47 | loop fusion | flops 1572864 | bytes 2097156 | tf_op jit(solution)/shard_map/convert_element_type | solution.py:103
  203.0 3.8 %fusion.5 = bf16[256,2048]{1,0:T(8,128)(2,1)} fusion(bf16[512,2048]{1,0:T(8,128)(2,1)S(1)} %get-tuple-element.5, bf16[256,2048]{1,0:T(8,128)(2,1)} %collective-permute-done.51, bf16[256,2048]{1,0:T(8,128)(2,1)} %collective-permute-done.48, bf16[256,2048]{1,0:T(8,128)(2,1)} %collective-permute-done.44, bf16[512,2048]{1,0:T(8,128)(2,1)} %copy-done.1, ...), kind=kOutput, calls=%fused_computation.24 | convolution fusion | flops 541589504 | bytes 6553604 | tf_op jit(solution)/shard_map/dot_general | solution.py:16
  (133 shorter events, 49.3 us)
Async XLA Ops:
  0.6 28.3 %collective-permute-start.7 = (bf16[256,2048]{1,0:T(8,128)(2,1)}, bf16[256,2048]{1,0:T(8,128)(2,1)S(1)}, u32[]{:S(2)}, u32[]{:S(2)}) collective-permute-start(bf16[256,2048]{1,0:T(8,128)(2,1)} %param.4), channel_id=1, source_target_pairs={{0,8},{4,12},{8,0},{12,4},{16,24},{20,28},{24,16},{28,20},{1,9},{5... | collective-permute-start | bytes 3145736 | tf_op jit(solution)/shard_map/ppermute | solution.py:21
  3.6 25.9 %collective-permute-start.9 = (bf16[256,2048]{1,0:T(8,128)(2,1)}, bf16[256,2048]{1,0:T(8,128)(2,1)S(1)}, u32[]{:S(2)}, u32[]{:S(2)}) collective-permute-start(bf16[256,2048]{1,0:T(8,128)(2,1)} %param.4), channel_id=1, source_target_pairs={{0,16},{4,20},{8,24},{12,28},{16,0},{20,4},{24,8},{28,12},{1,17},{... | collective-permute-start | bytes 3145736 | tf_op jit(solution)/shard_map/ppermute | solution.py:21
  5.2 25.3 %collective-permute-start.6 = (bf16[256,2048]{1,0:T(8,128)(2,1)}, bf16[256,2048]{1,0:T(8,128)(2,1)S(1)}, u32[]{:S(2)}, u32[]{:S(2)}) collective-permute-start(bf16[256,2048]{1,0:T(8,128)(2,1)} %param.4), channel_id=1, source_target_pairs={{0,4},{4,0},{8,12},{12,8},{16,20},{20,16},{24,28},{28,24},{1,5},{5... | collective-permute-start | bytes 3145736 | tf_op jit(solution)/shard_map/ppermute | solution.py:21
  5.2 16.5 %collective-permute-start.1 = (bf16[512,512]{1,0:T(8,128)(2,1)}, bf16[512,512]{1,0:T(8,128)(2,1)}, u32[]{:S(2)}, u32[]{:S(2)}) collective-permute-start(bf16[512,512]{1,0:T(8,128)(2,1)} %param.3), channel_id=1, source_target_pairs={{1,0},{2,1},{3,2},{5,4},{6,5},{7,6},{9,8},{10,9},{11,10},{13,12},{... | collective-permute-start | bytes 1572872 | tf_op jit(solution)/shard_map/ppermute | solution.py:27
  6.4 17.7 %collective-permute-start = (bf16[512,512]{1,0:T(8,128)(2,1)}, bf16[512,512]{1,0:T(8,128)(2,1)}, u32[]{:S(2)}, u32[]{:S(2)}) collective-permute-start(bf16[512,512]{1,0:T(8,128)(2,1)} %param.3), channel_id=1, source_target_pairs={{0,1},{1,2},{2,3},{4,5},{5,6},{6,7},{8,9},{9,10},{10,11},{12,13},{... | collective-permute-start | bytes 1572872 | tf_op jit(solution)/shard_map/ppermute | solution.py:27
  21.7 15.8 %collective-permute-start.2 = (bf16[512,512]{1,0:T(8,128)(2,1)}, bf16[512,512]{1,0:T(8,128)(2,1)}, u32[]{:S(2)}, u32[]{:S(2)}) collective-permute-start(bf16[512,512]{1,0:T(8,128)(2,1)} %collective-permute-done.1), channel_id=1, source_target_pairs={{1,0},{2,1},{3,2},{5,4},{6,5},{7,6},{9,8},{10,9},{11,10},{13,12},{... | collective-permute-start | bytes 1572872 | tf_op jit(solution)/shard_map/ppermute | solution.py:27
  24.2 15.8 %collective-permute-start.4 = (bf16[512,512]{1,0:T(8,128)(2,1)}, bf16[512,512]{1,0:T(8,128)(2,1)S(1)}, u32[]{:S(2)}, u32[]{:S(2)}) collective-permute-start(bf16[512,512]{1,0:T(8,128)(2,1)} %collective-permute-done), channel_id=1, source_target_pairs={{0,1},{1,2},{2,3},{4,5},{5,6},{6,7},{8,9},{9,10},{10,11},{12,13},{... | collective-permute-start | bytes 1572872 | tf_op jit(solution)/shard_map/ppermute | solution.py:27
  28.9 13.1 %collective-permute-start.11 = (bf16[128,2048]{1,0:T(8,128)(2,1)S(1)}, bf16[128,2048]{1,0:T(8,128)(2,1)S(1)}, u32[]{:S(2)}, u32[]{:S(2)}) collective-permute-start(bf16[128,2048]{1,0:T(8,128)(2,1)S(1)} %slice.42), channel_id=1, source_target_pairs={{0,16},{4,20},{8,24},{12,28},{16,0},{20,4},{24,8},{28,12},{1,17},{... | collective-permute-start | bytes 1572872 | tf_op jit(solution)/shard_map/ppermute | solution.py:21
  29.6 16.0 %collective-permute-start.12 = (bf16[128,2048]{1,0:T(8,128)(2,1)S(1)}, bf16[128,2048]{1,0:T(8,128)(2,1)S(1)}, u32[]{:S(2)}, u32[]{:S(2)}) collective-permute-start(bf16[128,2048]{1,0:T(8,128)(2,1)S(1)} %slice.43), channel_id=1, source_target_pairs={{0,8},{4,12},{8,0},{12,4},{16,24},{20,28},{24,16},{28,20},{1,9},{5... | collective-permute-start | bytes 1572872 | tf_op jit(solution)/shard_map/ppermute | solution.py:21
  30.5 28.1 %collective-permute-start.8 = (bf16[256,2048]{1,0:T(8,128)(2,1)S(1)}, bf16[256,2048]{1,0:T(8,128)(2,1)S(1)}, u32[]{:S(2)}, u32[]{:S(2)}) collective-permute-start(bf16[256,2048]{1,0:T(8,128)(2,1)S(1)} %collective-permute-done.7), channel_id=1, source_target_pairs={{0,4},{4,0},{8,12},{12,8},{16,20},{20,16},{24,28},{28,24},{1,5},{5... | collective-permute-start | bytes 3145736 | tf_op jit(solution)/shard_map/ppermute | solution.py:21
  37.4 14.8 %collective-permute-start.3 = (bf16[512,512]{1,0:T(8,128)(2,1)}, bf16[512,512]{1,0:T(8,128)(2,1)S(1)}, u32[]{:S(2)}, u32[]{:S(2)}) collective-permute-start(bf16[512,512]{1,0:T(8,128)(2,1)} %collective-permute-done.2), channel_id=1, source_target_pairs={{1,0},{2,1},{3,2},{5,4},{6,5},{7,6},{9,8},{10,9},{11,10},{13,12},{... | collective-permute-start | bytes 1572872 | tf_op jit(solution)/shard_map/ppermute | solution.py:27
  39.9 19.4 %collective-permute-start.10 = (bf16[256,2048]{1,0:T(8,128)(2,1)S(1)}, bf16[256,2048]{1,0:T(8,128)(2,1)S(1)}, u32[]{:S(2)}, u32[]{:S(2)}) collective-permute-start(bf16[256,2048]{1,0:T(8,128)(2,1)S(1)} %collective-permute-done.9), channel_id=1, source_target_pairs={{0,4},{4,0},{8,12},{12,8},{16,20},{20,16},{24,28},{28,24},{1,5},{5... | collective-permute-start | bytes 3145736 | tf_op jit(solution)/shard_map/ppermute | solution.py:21
  42.0 14.1 %collective-permute-start.5 = (bf16[512,512]{1,0:T(8,128)(2,1)S(1)}, bf16[512,512]{1,0:T(8,128)(2,1)S(1)}, u32[]{:S(2)}, u32[]{:S(2)}) collective-permute-start(bf16[512,512]{1,0:T(8,128)(2,1)S(1)} %collective-permute-done.4), channel_id=1, source_target_pairs={{0,1},{1,2},{2,3},{4,5},{5,6},{6,7},{8,9},{9,10},{10,11},{12,13},{... | collective-permute-start | bytes 1572872 | tf_op jit(solution)/shard_map/ppermute | solution.py:27
  45.6 14.6 %collective-permute-start.13 = (bf16[256,2048]{1,0:T(8,128)(2,1)S(1)}, bf16[256,2048]{1,0:T(8,128)(2,1)S(1)}, u32[]{:S(2)}, u32[]{:S(2)}) collective-permute-start(bf16[256,2048]{1,0:T(8,128)(2,1)S(1)} %constant_dynamic-update-slice_fusion), channel_id=1, source_target_pairs={{0,4},{4,0},{8,12},{12,8},{16,20},{20,16},{24,28},{28,24},{1,5},{5... | collective-permute-start | bytes 3145736 | tf_op jit(solution)/shard_map/ppermute | solution.py:21
  66.1 5.6 %collective-permute-start.16 = (f32[2,512]{1,0:T(2,128)S(1)}, f32[2,512]{1,0:T(2,128)S(1)}, u32[]{:S(2)}, u32[]{:S(2)}) collective-permute-start(f32[2,512]{1,0:T(2,128)S(1)} %pad_maximum_fusion.2), channel_id=1, source_target_pairs={{0,3},{1,0},{2,1},{3,2},{4,7},{5,4},{6,5},{7,6},{8,11},{9,8},{10,9... | collective-permute-start | bytes 12296 | tf_op jit(solution)/shard_map/ppermute | solution.py:33
  70.3 4.5 %collective-permute-start.15 = (f32[2,512]{1,0:T(2,128)S(1)}, f32[2,512]{1,0:T(2,128)S(1)}, u32[]{:S(2)}, u32[]{:S(2)}) collective-permute-start(f32[2,512]{1,0:T(2,128)S(1)} %pad_maximum_fusion.2), channel_id=1, source_target_pairs={{0,2},{1,3},{2,0},{3,1},{4,6},{5,7},{6,4},{7,5},{8,10},{9,11},{10,... | collective-permute-start | bytes 12296 | tf_op jit(solution)/shard_map/ppermute | solution.py:33
  70.3 5.4 %collective-permute-start.14 = (f32[2,512]{1,0:T(2,128)S(1)}, f32[2,512]{1,0:T(2,128)S(1)}, u32[]{:S(2)}, u32[]{:S(2)}) collective-permute-start(f32[2,512]{1,0:T(2,128)S(1)} %pad_maximum_fusion.2), channel_id=1, source_target_pairs={{0,1},{1,2},{2,3},{3,0},{4,5},{5,6},{6,7},{7,4},{8,9},{9,10},{10,1... | collective-permute-start | bytes 12296 | tf_op jit(solution)/shard_map/ppermute | solution.py:33
  77.8 4.5 %collective-permute-start.20 = (f32[2048]{0:T(1024)S(1)}, f32[2048]{0:T(1024)S(1)}, u32[]{:S(2)}, u32[]{:S(2)}) collective-permute-start(f32[2048]{0:T(1024)S(1)} %add.222), channel_id=1, source_target_pairs={{0,24},{4,28},{8,16},{12,20},{16,8},{20,12},{24,0},{28,4},{1,25},{... | collective-permute-start | bytes 24584 | tf_op jit(solution)/shard_map/ppermute | solution.py:21
  78.3 4.1 %collective-permute-start.19 = (f32[2048]{0:T(1024)S(1)}, f32[2048]{0:T(1024)S(1)}, u32[]{:S(2)}, u32[]{:S(2)}) collective-permute-start(f32[2048]{0:T(1024)S(1)} %add.222), channel_id=1, source_target_pairs={{0,16},{4,20},{8,24},{12,28},{16,0},{20,4},{24,8},{28,12},{1,17},{... | collective-permute-start | bytes 24584 | tf_op jit(solution)/shard_map/ppermute | solution.py:21
  79.8 3.7 %collective-permute-start.18 = (f32[2048]{0:T(1024)S(1)}, f32[2048]{0:T(1024)S(1)}, u32[]{:S(2)}, u32[]{:S(2)}) collective-permute-start(f32[2048]{0:T(1024)S(1)} %add.222), channel_id=1, source_target_pairs={{0,8},{4,12},{8,0},{12,4},{16,24},{20,28},{24,16},{28,20},{1,9},{5... | collective-permute-start | bytes 24584 | tf_op jit(solution)/shard_map/ppermute | solution.py:21
  84.4 3.6 %collective-permute-start.23 = (f32[512]{0:T(512)S(1)}, f32[512]{0:T(512)S(1)}, u32[]{:S(2)}, u32[]{:S(2)}) collective-permute-start(f32[512]{0:T(512)S(1)} %multiply_reduce_fusion.3), channel_id=1, source_target_pairs={{0,3},{1,0},{2,1},{3,2},{4,7},{5,4},{6,5},{7,6},{8,11},{9,8},{10,9... | collective-permute-start | bytes 6152 | tf_op jit(solution)/shard_map/ppermute | solution.py:33
  85.0 4.5 %collective-permute-start.22 = (f32[512]{0:T(512)S(1)}, f32[512]{0:T(512)S(1)}, u32[]{:S(2)}, u32[]{:S(2)}) collective-permute-start(f32[512]{0:T(512)S(1)} %multiply_reduce_fusion.3), channel_id=1, source_target_pairs={{0,2},{1,3},{2,0},{3,1},{4,6},{5,7},{6,4},{7,5},{8,10},{9,11},{10,... | collective-permute-start | bytes 6152 | tf_op jit(solution)/shard_map/ppermute | solution.py:33
  85.7 5.4 %collective-permute-start.21 = (f32[512]{0:T(512)S(1)}, f32[512]{0:T(512)S(1)}, u32[]{:S(2)}, u32[]{:S(2)}) collective-permute-start(f32[512]{0:T(512)S(1)} %multiply_reduce_fusion.3), channel_id=1, source_target_pairs={{0,1},{1,2},{2,3},{3,0},{4,5},{5,6},{6,7},{7,4},{8,9},{9,10},{10,1... | collective-permute-start | bytes 6152 | tf_op jit(solution)/shard_map/ppermute | solution.py:33
  93.2 4.5 %collective-permute-start.27 = (f32[2048]{0:T(1024)S(1)}, f32[2048]{0:T(1024)S(1)}, u32[]{:S(2)}, u32[]{:S(2)}) collective-permute-start(f32[2048]{0:T(1024)S(1)} %add.229), channel_id=1, source_target_pairs={{0,24},{4,28},{8,16},{12,20},{16,8},{20,12},{24,0},{28,4},{1,25},{... | collective-permute-start | bytes 24584 | tf_op jit(solution)/shard_map/ppermute | solution.py:21
  94.6 3.7 %collective-permute-start.26 = (f32[2048]{0:T(1024)S(1)}, f32[2048]{0:T(1024)S(1)}, u32[]{:S(2)}, u32[]{:S(2)}) collective-permute-start(f32[2048]{0:T(1024)S(1)} %add.229), channel_id=1, source_target_pairs={{0,16},{4,20},{8,24},{12,28},{16,0},{20,4},{24,8},{28,12},{1,17},{... | collective-permute-start | bytes 24584 | tf_op jit(solution)/shard_map/ppermute | solution.py:21
  96.1 3.7 %collective-permute-start.25 = (f32[2048]{0:T(1024)S(1)}, f32[2048]{0:T(1024)S(1)}, u32[]{:S(2)}, u32[]{:S(2)}) collective-permute-start(f32[2048]{0:T(1024)S(1)} %add.229), channel_id=1, source_target_pairs={{0,8},{4,12},{8,0},{12,4},{16,24},{20,28},{24,16},{28,20},{1,9},{5... | collective-permute-start | bytes 24584 | tf_op jit(solution)/shard_map/ppermute | solution.py:21
  102.1 4.5 %collective-permute-start.29 = (f32[512]{0:T(512)S(1)}, f32[512]{0:T(512)S(1)}, u32[]{:S(2)}, u32[]{:S(2)}) collective-permute-start(f32[512]{0:T(512)S(1)} %multiply_reduce_fusion.1), channel_id=1, source_target_pairs={{0,2},{1,3},{2,0},{3,1},{4,6},{5,7},{6,4},{7,5},{8,10},{9,11},{10,... | collective-permute-start | bytes 6152 | tf_op jit(solution)/shard_map/ppermute | solution.py:33
  102.4 5.4 %collective-permute-start.28 = (f32[512]{0:T(512)S(1)}, f32[512]{0:T(512)S(1)}, u32[]{:S(2)}, u32[]{:S(2)}) collective-permute-start(f32[512]{0:T(512)S(1)} %multiply_reduce_fusion.1), channel_id=1, source_target_pairs={{0,1},{1,2},{2,3},{3,0},{4,5},{5,6},{6,7},{7,4},{8,9},{9,10},{10,1... | collective-permute-start | bytes 6152 | tf_op jit(solution)/shard_map/ppermute | solution.py:33
  109.9 4.5 %collective-permute-start.34 = (f32[2048]{0:T(1024)S(1)}, f32[2048]{0:T(1024)S(1)}, u32[]{:S(2)}, u32[]{:S(2)}) collective-permute-start(f32[2048]{0:T(1024)S(1)} %add.236), channel_id=1, source_target_pairs={{0,24},{4,28},{8,16},{12,20},{16,8},{20,12},{24,0},{28,4},{1,25},{... | collective-permute-start | bytes 24584 | tf_op jit(solution)/shard_map/ppermute | solution.py:21
  110.3 4.1 %collective-permute-start.33 = (f32[2048]{0:T(1024)S(1)}, f32[2048]{0:T(1024)S(1)}, u32[]{:S(2)}, u32[]{:S(2)}) collective-permute-start(f32[2048]{0:T(1024)S(1)} %add.236), channel_id=1, source_target_pairs={{0,16},{4,20},{8,24},{12,28},{16,0},{20,4},{24,8},{28,12},{1,17},{... | collective-permute-start | bytes 24584 | tf_op jit(solution)/shard_map/ppermute | solution.py:21
  111.9 3.7 %collective-permute-start.32 = (f32[2048]{0:T(1024)S(1)}, f32[2048]{0:T(1024)S(1)}, u32[]{:S(2)}, u32[]{:S(2)}) collective-permute-start(f32[2048]{0:T(1024)S(1)} %add.236), channel_id=1, source_target_pairs={{0,8},{4,12},{8,0},{12,4},{16,24},{20,28},{24,16},{28,20},{1,9},{5... | collective-permute-start | bytes 24584 | tf_op jit(solution)/shard_map/ppermute | solution.py:21
  118.6 3.6 %collective-permute-start.37 = (f32[512]{0:T(512)S(1)}, f32[512]{0:T(512)S(1)}, u32[]{:S(2)}, u32[]{:S(2)}) collective-permute-start(f32[512]{0:T(512)S(1)} %multiply_reduce_fusion.5), channel_id=1, source_target_pairs={{0,3},{1,0},{2,1},{3,2},{4,7},{5,4},{6,5},{7,6},{8,11},{9,8},{10,9... | collective-permute-start | bytes 6152 | tf_op jit(solution)/shard_map/ppermute | solution.py:33
  119.6 4.5 %collective-permute-start.36 = (f32[512]{0:T(512)S(1)}, f32[512]{0:T(512)S(1)}, u32[]{:S(2)}, u32[]{:S(2)}) collective-permute-start(f32[512]{0:T(512)S(1)} %multiply_reduce_fusion.5), channel_id=1, source_target_pairs={{0,2},{1,3},{2,0},{3,1},{4,6},{5,7},{6,4},{7,5},{8,10},{9,11},{10,... | collective-permute-start | bytes 6152 | tf_op jit(solution)/shard_map/ppermute | solution.py:33
  119.6 5.4 %collective-permute-start.35 = (f32[512]{0:T(512)S(1)}, f32[512]{0:T(512)S(1)}, u32[]{:S(2)}, u32[]{:S(2)}) collective-permute-start(f32[512]{0:T(512)S(1)} %multiply_reduce_fusion.5), channel_id=1, source_target_pairs={{0,1},{1,2},{2,3},{3,0},{4,5},{5,6},{6,7},{7,4},{8,9},{9,10},{10,1... | collective-permute-start | bytes 6152 | tf_op jit(solution)/shard_map/ppermute | solution.py:33
  137.6 11.0 %collective-permute-start.38 = (bf16[512,512]{1,0:T(8,128)(2,1)S(1)}, bf16[512,512]{1,0:T(8,128)(2,1)S(1)}, u32[]{:S(2)}, u32[]{:S(2)}) collective-permute-start(bf16[512,512]{1,0:T(8,128)(2,1)S(1)} %get-tuple-element.9), channel_id=1, source_target_pairs={{0,1},{1,2},{2,3},{4,5},{5,6},{6,7},{8,9},{9,10},{10,11},{12,13},{... | collective-permute-start | bytes 1572872 | tf_op jit(solution)/shard_map/ppermute | solution.py:27
  140.0 14.8 %collective-permute-start.41 = (bf16[512,512]{1,0:T(8,128)(2,1)S(1)}, bf16[512,512]{1,0:T(8,128)(2,1)S(1)}, u32[]{:S(2)}, u32[]{:S(2)}) collective-permute-start(bf16[512,512]{1,0:T(8,128)(2,1)S(1)} %get-tuple-element.10), channel_id=1, source_target_pairs={{1,0},{2,1},{3,2},{5,4},{6,5},{7,6},{9,8},{10,9},{11,10},{13,12},{... | collective-permute-start | bytes 1572872 | tf_op jit(solution)/shard_map/ppermute | solution.py:27
  142.0 23.9 %collective-permute-start.49 = (bf16[256,2048]{1,0:T(8,128)(2,1)S(1)}, bf16[256,2048]{1,0:T(8,128)(2,1)S(1)}, u32[]{:S(2)}, u32[]{:S(2)}) collective-permute-start(bf16[256,2048]{1,0:T(8,128)(2,1)S(1)} %convolution_convert_fusion.1), channel_id=1, source_target_pairs={{0,4},{4,0},{8,12},{12,8},{16,20},{20,16},{24,28},{28,24},{1,5},{5... | collective-permute-start | bytes 3145736 | tf_op jit(solution)/shard_map/ppermute | solution.py:21
  142.9 21.0 %collective-permute-start.46 = (bf16[256,2048]{1,0:T(8,128)(2,1)S(1)}, bf16[256,2048]{1,0:T(8,128)(2,1)S(1)}, u32[]{:S(2)}, u32[]{:S(2)}) collective-permute-start(bf16[256,2048]{1,0:T(8,128)(2,1)S(1)} %convolution_convert_fusion.3), channel_id=1, source_target_pairs={{0,4},{4,0},{8,12},{12,8},{16,20},{20,16},{24,28},{28,24},{1,5},{5... | collective-permute-start | bytes 3145736 | tf_op jit(solution)/shard_map/ppermute | solution.py:21
  148.8 12.1 %collective-permute-start.39 = (bf16[512,512]{1,0:T(8,128)(2,1)S(1)}, bf16[512,512]{1,0:T(8,128)(2,1)S(1)}, u32[]{:S(2)}, u32[]{:S(2)}) collective-permute-start(bf16[512,512]{1,0:T(8,128)(2,1)S(1)} %add_convert_fusion.4), channel_id=1, source_target_pairs={{0,1},{1,2},{2,3},{4,5},{5,6},{6,7},{8,9},{9,10},{10,11},{12,13},{... | collective-permute-start | bytes 1572872 | tf_op jit(solution)/shard_map/ppermute | solution.py:27
  154.0 13.2 %collective-permute-start.45 = (bf16[256,2048]{1,0:T(8,128)(2,1)S(1)}, bf16[256,2048]{1,0:T(8,128)(2,1)S(1)}, u32[]{:S(2)}, u32[]{:S(2)}) collective-permute-start(bf16[256,2048]{1,0:T(8,128)(2,1)S(1)} %convolution_convert_fusion.5), channel_id=1, source_target_pairs={{0,4},{4,0},{8,12},{12,8},{16,20},{20,16},{24,28},{28,24},{1,5},{5... | collective-permute-start | bytes 3145736 | tf_op jit(solution)/shard_map/ppermute | solution.py:21
  154.8 48.2 %collective-permute-start.44 = (bf16[256,2048]{1,0:T(8,128)(2,1)S(1)}, bf16[256,2048]{1,0:T(8,128)(2,1)}, u32[]{:S(2)}, u32[]{:S(2)}) collective-permute-start(bf16[256,2048]{1,0:T(8,128)(2,1)S(1)} %convolution_convert_fusion.7), channel_id=1, source_target_pairs={{0,4},{4,0},{8,12},{12,8},{16,20},{20,16},{24,28},{28,24},{1,5},{5... | collective-permute-start | bytes 3145736 | tf_op jit(solution)/shard_map/ppermute | solution.py:21
  162.3 24.7 %collective-permute-start.42 = (bf16[512,512]{1,0:T(8,128)(2,1)}, bf16[512,512]{1,0:T(8,128)(2,1)}, u32[]{:S(2)}, u32[]{:S(2)}) collective-permute-start(bf16[512,512]{1,0:T(8,128)(2,1)} %get-tuple-element.8), channel_id=1, source_target_pairs={{1,0},{2,1},{3,2},{5,4},{6,5},{7,6},{9,8},{10,9},{11,10},{13,12},{... | collective-permute-start | bytes 1572872 | tf_op jit(solution)/shard_map/ppermute | solution.py:27
  164.7 9.4 %collective-permute-start.50 = (bf16[128,2048]{1,0:T(8,128)(2,1)S(1)}, bf16[128,2048]{1,0:T(8,128)(2,1)S(1)}, u32[]{:S(2)}, u32[]{:S(2)}) collective-permute-start(bf16[128,2048]{1,0:T(8,128)(2,1)S(1)} %get-tuple-element.16), channel_id=1, source_target_pairs={{0,8},{4,12},{8,0},{12,4},{16,24},{20,28},{24,16},{28,20},{1,9},{5... | collective-permute-start | bytes 1572872 | tf_op jit(solution)/shard_map/ppermute | solution.py:21
  166.8 12.6 %collective-permute-start.47 = (bf16[128,2048]{1,0:T(8,128)(2,1)S(1)}, bf16[128,2048]{1,0:T(8,128)(2,1)S(1)}, u32[]{:S(2)}, u32[]{:S(2)}) collective-permute-start(bf16[128,2048]{1,0:T(8,128)(2,1)S(1)} %get-tuple-element.15), channel_id=1, source_target_pairs={{0,16},{4,20},{8,24},{12,28},{16,0},{20,4},{24,8},{28,12},{1,17},{... | collective-permute-start | bytes 1572872 | tf_op jit(solution)/shard_map/ppermute | solution.py:21
  175.3 27.7 %collective-permute-start.51 = (bf16[256,2048]{1,0:T(8,128)(2,1)}, bf16[256,2048]{1,0:T(8,128)(2,1)}, u32[]{:S(2)}, u32[]{:S(2)}) collective-permute-start(bf16[256,2048]{1,0:T(8,128)(2,1)} %pad_maximum_fusion.1), channel_id=1, source_target_pairs={{0,16},{4,20},{8,24},{12,28},{16,0},{20,4},{24,8},{28,12},{1,17},{... | collective-permute-start | bytes 3145736 | tf_op jit(solution)/shard_map/ppermute | solution.py:21
  180.6 22.4 %collective-permute-start.48 = (bf16[256,2048]{1,0:T(8,128)(2,1)}, bf16[256,2048]{1,0:T(8,128)(2,1)}, u32[]{:S(2)}, u32[]{:S(2)}) collective-permute-start(bf16[256,2048]{1,0:T(8,128)(2,1)} %pad_maximum_fusion), channel_id=1, source_target_pairs={{0,8},{4,12},{8,0},{12,4},{16,24},{20,28},{24,16},{28,20},{1,9},{5... | collective-permute-start | bytes 3145736 | tf_op jit(solution)/shard_map/ppermute | solution.py:21
  181.6 11.6 %collective-permute-start.40 = (bf16[512,512]{1,0:T(8,128)(2,1)}, bf16[512,512]{1,0:T(8,128)(2,1)}, u32[]{:S(2)}, u32[]{:S(2)}) collective-permute-start(bf16[512,512]{1,0:T(8,128)(2,1)} %get-tuple-element.7), channel_id=1, source_target_pairs={{0,1},{1,2},{2,3},{4,5},{5,6},{6,7},{8,9},{9,10},{10,11},{12,13},{... | collective-permute-start | bytes 1572872 | tf_op jit(solution)/shard_map/ppermute | solution.py:27
  189.2 11.4 %collective-permute-start.43 = (bf16[512,512]{1,0:T(8,128)(2,1)}, bf16[512,512]{1,0:T(8,128)(2,1)}, u32[]{:S(2)}, u32[]{:S(2)}) collective-permute-start(bf16[512,512]{1,0:T(8,128)(2,1)} %add_convert_fusion.1), channel_id=1, source_target_pairs={{1,0},{2,1},{3,2},{5,4},{6,5},{7,6},{9,8},{10,9},{11,10},{13,12},{... | collective-permute-start | bytes 1572872 | tf_op jit(solution)/shard_map/ppermute | solution.py:27
  (12 other events, 106.0 us)

commit v2 on v0

v2 whole, which is shorter than its diff:
```python
import functools

import jax
import jax.numpy as jnp
from jax import lax
from jax.experimental import pallas as pl
from jax.experimental.pallas import tpu as pltpu
from jax.sharding import PartitionSpec as P

ITERS = 3


softcap = 15.0
sharpen = 2.0
f32 = jnp.float32
bf16 = jnp.bfloat16
VMEM = pltpu.VMEM
LANES = 128


def matmul(left, right, dims):
    return lax.dot_general(left, right, (dims, ((), ())), preferred_element_type=f32)


def flip(value, axis, mask):
    size = lax.axis_size(axis)
    return lax.ppermute(value, axis, [(i, i ^ mask) for i in range(size)])


def butterfly(value, axis):
    mask = 1
    while mask < lax.axis_size(axis):
        value = value + flip(value, axis, mask)
        mask *= 2
    return value


def row_total(value):
    return butterfly(value, "cls")


def column_total(value):
    return butterfly(value, "sample")


def link_pairs(parity, size):
    other = [((i + parity) ^ 1) - parity for i in range(size)]
    return [(i, j if 0 <= j < size else i) for i, j in enumerate(other)]


def swap(value, parity):
    return lax.ppermute(value, "cls", link_pairs(parity, lax.axis_size("cls")))


def line_source(parity, hop, me, size):
    rightward = (me & 1) == parity
    above, below = me + hop, me - hop
    above = jnp.where(above >= size, 2 * size - 1 - above, above)
    below = jnp.where(below < 0, -1 - below, below)
    return jnp.where(rightward, above, below)


def chip_axes(size):
    chips = size // 2
    bits = chips.bit_length() - 1
    low = 1 << ((bits + 1) // 2)
    first = [2 * m for m in range(1, low)]
    second = [2 * low * m for m in range(1, chips // low)]
    return first, second


def gather_head(head):
    size = lax.axis_size("sample")
    first, second = chip_axes(size)
    half = head.shape[0] // 2
    top, bottom = head[:half], head[half:]
    own = [(0, 0, head)]
    held = {}
    for mask in first:
        held[mask, 0] = flip(top, "sample", mask)
    for mask in second:
        held[mask, half] = flip(bottom, "sample", mask)
    for mask in first:
        held[mask, half] = flip(bottom, "sample", mask)
    for mask in second:
        held[mask, 0] = flip(top, "sample", mask)
    for a in first:
        for b in second:
            held[a | b, 0] = flip(held[a, 0], "sample", b)
            held[a | b, half] = flip(held[b, half], "sample", a)
    same = own + [(mask, offset, block) for (mask, offset), block in held.items()]
    return same + [(mask | 1, offset, flip(block, "sample", 1)) for mask, offset, block in same]


def gather_features(features):
    size = lax.axis_size("cls")
    pieces = [(0, 0, features)]
    even = odd = features
    for hop in range(1, size):
        even, odd = swap(odd, 0), swap(even, 1)
        pieces.append((0, hop, even))
        if hop < size - 1 or size % 2:
            pieces.append((1, hop, odd))
    return pieces


def scatter_features(block_of):
    size = lax.axis_size("cls")
    me = lax.axis_index("cls")
    has = {True: me > 0, False: me < size - 1}

    def joined(block, received, rightward):
        if received is None:
            return block
        keep = jnp.where(rightward, has[True], has[False])
        return (block.astype(f32) + jnp.where(keep, received.astype(f32), 0.0)).astype(bf16)

    received = {0: None, 1: None}
    for hop in range(1, size):
        sent = {}
        for parity in (0, 1):
            if parity == 1 and hop == 1 and size % 2 == 0:
                sent[1] = None
                continue
            rightward = (me & 1) == parity
            index = jnp.where(rightward, size - hop + me, me - (size - hop))
            block = block_of(jnp.clip(index, 0, size - 1))
            sent[parity] = swap(joined(block, received[1 - parity], rightward), parity)
        received = sent
    total = block_of(me).astype(f32)
    for parity in (0, 1):
        if received[parity] is None:
            continue
        from_right = (me & 1) == parity
        keep = jnp.where(from_right, has[False], has[True])
        total = total + jnp.where(keep, received[parity].astype(f32), 0.0)
    return total.astype(bf16)


def scatter_head(partial_of):
    size = lax.axis_size("sample")
    first, second = chip_axes(size)

    def both(mask):
        other = flip(partial_of(mask | 1), "sample", 1)
        return partial_of(mask).astype(f32) + other.astype(f32)

    half = partial_of(0).shape[0] // 2
    extra = {}
    for a in first:
        for b in second:
            block = both(a | b).astype(bf16)
            extra.setdefault((b, 0), []).append(flip(block[:half], "sample", a))
            extra.setdefault((a, 1), []).append(flip(block[half:], "sample", b))
    totals = {0: [], 1: []}
    for mask in first + second:
        block = both(mask)
        parts = {0: block[:half], 1: block[half:]}
        for part in sorted((0, 1), key=lambda part: (mask, part) in extra):
            value = parts[part]
            for more in extra.get((mask, part), []):
                value = value + more.astype(f32)
            totals[part].append(flip(value.astype(bf16), "sample", mask))
    own = both(0)
    halves = [sum((t.astype(f32) for t in totals[part]), own[part * half : (part + 1) * half]) for part in (0, 1)]
    return jnp.concatenate(halves, axis=0).astype(bf16)


def logits_kernel(features_at, head_at, depth, tile, *refs):
    count_f, count_h = len(features_at), len(head_at)
    feature_refs = refs[:count_f]
    head_refs = refs[count_f : count_f + count_h]
    student_ref, slope_ref, sums_ref, whole, acc, student_sum, plan_sum = refs[count_f + count_h :]
    me, place = lax.axis_index("sample"), lax.axis_index("cls")
    groups = lax.axis_size("cls")
    width = feature_refs[0].shape[1]
    for (parity, hop), ref in zip(features_at, feature_refs):
        source = line_source(parity, hop, place, groups) if hop else place
        whole[:, pl.ds(pl.multiple_of(source * width, LANES), width)] = ref[...]
    student_sum[...] = jnp.zeros_like(student_sum)
    plan_sum[...] = jnp.zeros_like(plan_sum)
    tiles = student_ref.shape[1] // tile

    def product(i, slot):
        columns = pl.ds(pl.multiple_of(i * tile, tile), tile)
        total = None
        for (mask, offset), ref in zip(head_at, head_refs):
            first = pl.multiple_of((me ^ mask) * depth + offset, LANES)
            part = jnp.dot(
                whole[:, pl.ds(first, ref.shape[0])], ref[:, columns], preferred_element_type=f32
            )
            total = part if total is None else total + part
        acc[slot] = total

    def finish(i, slot):
        columns = pl.ds(pl.multiple_of(i * tile, tile), tile)
        tanh = jnp.tanh(acc[slot] * (1.0 / softcap))
        student = jnp.exp(softcap * tanh)
        plan = student * student
        student_ref[:, columns] = student
        slope_ref[:, columns] = (1.0 - tanh * tanh).astype(bf16)
        for first in range(0, tile, LANES):
            student_sum[...] += student[:, first : first + LANES]
            plan_sum[...] += plan[:, first : first + LANES]

    product(0, 0)

    def body(i, carry):
        slot = lax.rem(i, 2)
        product(i, slot)
        finish(i - 1, 1 - slot)
        return carry

    lax.fori_loop(1, tiles, body, 0)
    finish(tiles - 1, (tiles - 1) % 2)
    sums_ref[0:1, :] = jnp.sum(jnp.transpose(student_sum[...]), axis=0, keepdims=True)
    sums_ref[1:2, :] = jnp.sum(jnp.transpose(plan_sum[...]), axis=0, keepdims=True)


def in_vmem(values):
    return [pltpu.with_memory_space_constraint(value, VMEM) for value in values]


def whole_spec():
    return pl.BlockSpec(memory_space=VMEM)


def logits_call(feature_pieces, head_pieces, depth):
    rows = feature_pieces[0][2].shape[0]
    classes = head_pieces[0][2].shape[1]
    width = feature_pieces[0][2].shape[1] * lax.axis_size("cls")
    tile = min(256, classes)
    kernel = functools.partial(
        logits_kernel,
        [(parity, hop) for parity, hop, _ in feature_pieces],
        [(mask, offset) for mask, offset, _ in head_pieces],
        depth,
        tile,
    )
    operands = [block for _, _, block in feature_pieces] + [block for _, _, block in head_pieces]
    return pl.pallas_call(
        kernel,
        out_shape=(
            jax.ShapeDtypeStruct((rows, classes), f32),
            jax.ShapeDtypeStruct((rows, classes), bf16),
            jax.ShapeDtypeStruct((2, rows), f32),
        ),
        in_specs=[whole_spec()] * len(operands),
        out_specs=(whole_spec(),) * 3,
        scratch_shapes=[
            pltpu.VMEM((rows, width), bf16),
            pltpu.VMEM((2, rows, tile), f32),
            pltpu.VMEM((rows, LANES), f32),
            pltpu.VMEM((rows, LANES), f32),
        ],
        compiler_params=pltpu.CompilerParams(vmem_limit_bytes=48 << 20),
        cost_estimate=pl.CostEstimate(
            flops=2 * rows * width * classes, bytes_accessed=2 * width * classes, transcendentals=2 * rows * classes
        ),
    )(*in_vmem(operands))


def shares_kernel(head_at, depth, grad_ref, *refs):
    head_refs, shares_ref = refs[:-1], refs[-1]
    me = lax.axis_index("sample")
    width = shares_ref.shape[2]
    for (mask, offset), ref in zip(head_at, head_refs):
        first = (me ^ mask) * depth + offset
        block = first // width
        column = pl.multiple_of(first - block * width, LANES)
        product = lax.dot_general(
            grad_ref[...], ref[...], (((1,), (1,)), ((), ())), preferred_element_type=f32
        )
        shares_ref[block, :, pl.ds(column, ref.shape[0])] = product.astype(bf16)


def shares_call(grad_logits, head_pieces, depth, width):
    rows = grad_logits.shape[0]
    groups = lax.axis_size("cls")
    kernel = functools.partial(shares_kernel, [(mask, offset) for mask, offset, _ in head_pieces], depth)
    operands = [grad_logits] + [block for _, _, block in head_pieces]
    return pl.pallas_call(
        kernel,
        out_shape=jax.ShapeDtypeStruct((groups, rows, width), bf16),
        in_specs=[whole_spec()] * len(operands),
        out_specs=whole_spec(),
        compiler_params=pltpu.CompilerParams(vmem_limit_bytes=48 << 20),
        cost_estimate=pl.CostEstimate(
            flops=2 * rows * grad_logits.shape[1] * width * groups,
            bytes_accessed=2 * width * groups * grad_logits.shape[1],
            transcendentals=0,
        ),
    )(*in_vmem(operands))


def per_device(features, head, class_cap):
    local_rows, width = features.shape
    depth, class_local = head.shape
    sample_count = lax.axis_size("sample")
    class_groups = lax.axis_size("cls")
    ratio = local_rows * sample_count / (class_local * class_groups)
    me = lax.axis_index("sample")
    place = lax.axis_index("cls")
    aligned = depth % (2 * LANES) == 0 and width % (2 * LANES) == 0 and local_rows % LANES == 0

    head_pieces = gather_head(head)
    feature_pieces = gather_features(features)
    whole = jnp.zeros((local_rows, width * class_groups), bf16)
    for parity, hop, block in feature_pieces:
        source = line_source(parity, hop, place, class_groups) if hop else place
        whole = lax.dynamic_update_slice(whole, block, (0, source * width))

    if aligned:
        student, slope, sums = logits_call(feature_pieces, head_pieces, depth)
    else:
        head_full = jnp.zeros((depth * sample_count, class_local), bf16)
        for mask, offset, block in head_pieces:
            head_full = lax.dynamic_update_slice(head_full, block, ((me ^ mask) * depth + offset, 0))
        tanh = jnp.tanh(matmul(whole, head_full, ((1,), (0,))) / softcap)
        student = jnp.exp(softcap * tanh)
        slope = 1.0 - tanh * tanh
        sums = jnp.stack([jnp.sum(student, axis=1), jnp.sum(student * student, axis=1)])

    masses = row_total(sums)
    ceiling = class_cap.astype(f32) * ratio
    row_mass = masses[1]
    scale = jnp.ones((class_local,), f32)
    for iteration in range(ITERS):
        if iteration > 0:
            row_mass = row_total(jnp.sum(student * student * scale[None, :], axis=1))
        mass = column_total(jnp.sum(student * student * (1.0 / row_mass)[:, None], axis=0) * scale)
        scale = scale * jnp.minimum(1.0, ceiling / mass)
    row_mass = row_total(jnp.sum(student * student * scale[None, :], axis=1))
    targets = (student * student * scale[None, :] * (1.0 / row_mass)[:, None]).astype(bf16)
    grad_logits = (
        (student * (1.0 / masses[0])[:, None] - targets.astype(f32)) * slope.astype(f32)
    ).astype(bf16)

    def head_partial(mask):
        first = (me ^ mask) * depth
        columns = lax.dynamic_slice(whole, (0, first), (local_rows, depth))
        return matmul(columns, grad_logits, ((0,), (0,))).astype(bf16)

    partials = {mask: head_partial(mask) for mask in range(sample_count)}
    if aligned:
        shares = shares_call(grad_logits, head_pieces, depth, width)
    else:
        product = matmul(grad_logits, head_full, ((1,), (1,))).astype(bf16)
        shares = jnp.transpose(product.reshape(local_rows, class_groups, width), (1, 0, 2))

    def feature_block(index):
        return lax.dynamic_index_in_dim(shares, index, 0, keepdims=False)

    grad_features = scatter_features(feature_block)
    grad_head = scatter_head(lambda mask: partials[mask])
    return (targets, grad_features, grad_head)


def solution(mesh):
    return jax.shard_map(
        per_device,
        mesh=mesh,
        in_specs=(P("sample", "cls"), P("sample", "cls"), P("cls")),
        out_specs=(P("sample", "cls"), P("sample", "cls"), P("sample", "cls")),
        check_vma=False,
    )
```

time: 357 us -> 231 us (0.65)
  waiting for transfers between devices: 209 us -> 125 us
  blocking collectives: 75.1 us -> 0 us
  starting transfers between devices: 0.16 us -> 40.6 us
  Pallas kernels: 0 us -> 22.6 us
  matrix products: 31.6 us -> 13.6 us
  between operations: 13.8 us -> 1.34 us
  local copies, waits for them, and re-layouts: 2.7 us -> 11 us
  other arithmetic: 24.1 us -> 16.3 us
    ppermute x0 -> x50, waiting for transfers between devices: none -> 125 us  [the longest x40 94.6 us: flip(): return lax.ppermute(value, axis, [(i, i ^ mask) for i in range(size)])]
    all_gather x2 -> x0, waiting for transfers between devices: 105 us -> none  [the longest x1 55 us: per_device(): head_full = lax.all_gather(head, 'sample', axis=0, tiled=True)]
    reduce_scatter x2 -> x0, waiting for transfers between devices: 103 us -> none  [the longest x1 58.2 us: per_device(): lax.psum_scatter(lax.dot_general(whole, grad_logits, (((0,), (0,)), ((),...]
    psum x7 -> x0, blocking collectives: 75.1 us -> none  [the longest x3 36.2 us: per_device(): column_mass = lax.psum(jnp.sum(transport, axis=0), 'sample')]
    ppermute x0 -> x50, starting transfers between devices: none -> 40.6 us  [the longest x40 25.1 us: flip(): return lax.ppermute(value, axis, [(i, i ^ mask) for i in range(size)])]
    pallas_call x0 -> x2, Pallas kernels: none -> 22.6 us  [the longest x1 13.3 us: logits_call(): pl.pallas_call(kernel, out_shape=(jax.ShapeDtypeStruct((rows, classes), f...]
    dot_general x3 -> x8, matrix products: 31.6 us -> 13.6 us  [matmul(): lax.dot_general(left, right, (dims, ((), ())), preferred_element_type=f32)]
    reduce_sum x6, other arithmetic: 21.1 us -> 9.73 us  [the longest x3 6.05 us: per_device(): jnp.sum(student * student * (1.0 / row_mass)[:, None], axis=0) * scale]
  transfers between devices with their start and end apart: 4 -> 50, of which waited for: 4 -> 30; matrix products, arithmetic and copies ran while one was open for 4% -> 10% of each run, Pallas kernels for 0% -> 0%
where the time goes in v2:
time: 231 us
  waiting for transfers between devices  125 us (54%)
  starting transfers between devices  40.6 us (18%)
  Pallas kernels  22.6 us (10%)
  other arithmetic  16.3 us (7%)
  matrix products  13.6 us (6%)
  local copies, waits for them, and re-layouts  11 us (5%)
    ppermute x40, waiting for transfers between devices, flip(): return lax.ppermute(value, axis, [(i, i ^ mask) for i in range(size)])  94.6 us
    ppermute x10, waiting for transfers between devices, swap(): return lax.ppermute(value, 'cls', link_pairs(parity, lax.axis_size('cls')))  30.5 us
    ppermute x40, starting transfers between devices, flip(): return lax.ppermute(value, axis, [(i, i ^ mask) for i in range(size)])  25.1 us
    ppermute x10, starting transfers between devices, swap(): return lax.ppermute(value, 'cls', link_pairs(parity, lax.axis_size('cls')))  15.5 us
    dot_general x8, matrix products, matmul(): lax.dot_general(left, right, (dims, ((), ())), preferred_element_type=f32)  13.6 us
    pallas_call x1, Pallas kernels, logits_call(): pl.pallas_call(kernel, out_shape=(jax.ShapeDtypeStruct((rows, classes), f...  13.3 us
    pallas_call x1, Pallas kernels, shares_call(): pl.pallas_call(kernel, out_shape=jax.ShapeDtypeStruct((groups, rows, widt...  9.34 us
    reduce_sum x3, other arithmetic, per_device(): jnp.sum(student * student * (1.0 / row_mass)[:, None], axis=0) * scale  6.05 us
  transfers between devices with their start and end apart: 50, of which 30 were waited for; matrix products, arithmetic and copies ran while one was open for 10% of the time, Pallas kernels for 0%

profile of v2, /device:TPU:0, one launch (start us, length us, event | category | flops | bytes accessed | tf_op | source)
XLA Modules:
  0.0 230.6 jit_solution(17009469068473112186)
XLA Ops:
  0.6 1.8 collective-permute-start.1
  2.5 4.9 %collective-permute-start = (bf16[512,512]{1,0:T(8,128)(2,1)}, bf16[512,512]{1,0:T(8,128)(2,1)S(1)}, u32[]{:S(2)}, u32[]{:S(2)}) collective-permute-start(bf16[512,512]{1,0:T(8,128)(2,1)} %refs_0_.2), channel_id=1, source_target_pairs={{0,1},{1,0},{2,3},{3,2},{4,5},{5,4},{6,7},{7,6},{8,9},{9,8},{10,11... | collective-permute-start | bytes 1572872 | tf_op jit(solution)/shard_map/ppermute | solution.py:52
  8.7 1.6 collective-permute-start.7
  12.8 6.4 %collective-permute-done.refs_1_ = bf16[512,512]{1,0:T(8,128)(2,1)S(1)} collective-permute-done((bf16[512,512]{1,0:T(8,128)(2,1)}, bf16[512,512]{1,0:T(8,128)(2,1)S(1)}, u32[]{:S(2)}, u32[]{:S(2)}) %collective-permute-start) | collective-permute-done | bytes 524320 | tf_op jit(solution)/shard_map/ppermute | solution.py:52
  19.2 1.9 collective-permute-start.2
  21.1 2.5 %collective-permute-done.7.refs_9_.refs_3_ = bf16[128,2048]{1,0:T(8,128)(2,1)S(1)} collective-permute-done((bf16[128,2048]{1,0:T(8,128)(2,1)S(1)}, bf16[128,2048]{1,0:T(8,128)(2,1)S(1)}, u32[]{:S(2)}, u32[]{:S(2)}) %collective-permute-start.7) | collective-permute-done | bytes 524320 | tf_op jit(solution)/shard_map/ppermute | solution.py:27
  25.1 9.2 %collective-permute-done.8.refs_10_.refs_4_ = bf16[128,2048]{1,0:T(8,128)(2,1)S(1)} collective-permute-done((bf16[128,2048]{1,0:T(8,128)(2,1)S(1)}, bf16[128,2048]{1,0:T(8,128)(2,1)S(1)}, u32[]{:S(2)}, u32[]{:S(2)}) %collective-permute-start.8) | collective-permute-done | bytes 524320 | tf_op jit(solution)/shard_map/ppermute | solution.py:27
  35.4 1.6 collective-permute-start.9
  37.8 10.9 %collective-permute-done.10.refs_12_.refs_6_ = bf16[128,2048]{1,0:T(8,128)(2,1)S(1)} collective-permute-done((bf16[128,2048]{1,0:T(8,128)(2,1)S(1)}, bf16[128,2048]{1,0:T(8,128)(2,1)S(1)}, u32[]{:S(2)}, u32[]{:S(2)}) %collective-permute-start.10) | collective-permute-done | bytes 524320 | tf_op jit(solution)/shard_map/ppermute | solution.py:27
  49.8 12.1 %collective-permute-done.4.refs_5_ = bf16[512,512]{1,0:T(8,128)(2,1)S(1)} collective-permute-done((bf16[512,512]{1,0:T(8,128)(2,1)S(1)}, bf16[512,512]{1,0:T(8,128)(2,1)S(1)}, u32[]{:S(2)}, u32[]{:S(2)}) %collective-permute-start.4) | collective-permute-done | bytes 524320 | tf_op jit(solution)/shard_map/ppermute | solution.py:52
  61.8 13.3 %shard_map.58 = (f32[512,2048]{1,0:T(8,128)}, bf16[512,2048]{1,0:T(8,128)(2,1)}, f32[2,512]{1,0:T(2,128)}) custom-call(bf16[512,512]{1,0:T(8,128)(2,1)S(1)} %copy-done.1, bf16[512,512]{1,0:T(8,128)(2,1)S(1)} %collective-permute-done.refs_1_, bf16[512,512]{1,0:T(8,128)(2,1)S(1)} %collective-permute-done.1.refs_2_, ...), custom_call_target="tpu_custom_call" | custom-call | flops 4294967296 | bytes 8388608 | tf_op jit(solution)/shard_map/pallas_call | solution.py:241
  75.7 3.5 %collective-permute-done.18 = f32[2,512]{1,0:T(2,128)S(1)} collective-permute-done((f32[2,512]{1,0:T(2,128)}, f32[2,512]{1,0:T(2,128)S(1)}, u32[]{:S(2)}, u32[]{:S(2)}) %collective-permute-start.18) | collective-permute-done | bytes 4128 | tf_op jit(solution)/shard_map/ppermute | solution.py:27
  80.9 3.5 %collective-permute-done.19 = f32[2,512]{1,0:T(2,128)S(1)} collective-permute-done((f32[2,512]{1,0:T(2,128)S(1)}, f32[2,512]{1,0:T(2,128)S(1)}, u32[]{:S(2)}, u32[]{:S(2)}) %collective-permute-start.19) | collective-permute-done | bytes 4128 | tf_op jit(solution)/shard_map/ppermute | solution.py:27
  84.4 2.8 %multiply_reduce_fusion.4 = f32[2048]{0:T(1024)S(1)} fusion(f32[512,2048]{1,0:T(8,128)} %get-tuple-element.6, f32[512]{0:T(512)S(1)} %bitcast.26), kind=kLoop, calls=%fused_computation.6 | loop fusion | flops 3143680 | bytes 4204544 | tf_op jit(solution)/shard_map/reduce_sum | solution.py:331
  89.0 3.1 %collective-permute-done.21 = f32[2048]{0:T(1024)S(1)} collective-permute-done((f32[2048]{0:T(1024)S(1)}, f32[2048]{0:T(1024)S(1)}, u32[]{:S(2)}, u32[]{:S(2)}) %collective-permute-start.21) | collective-permute-done | bytes 8224 | tf_op jit(solution)/shard_map/ppermute | solution.py:27
  92.1 1.5 collective-permute-start.22
  93.6 2.1 collective-permute-done.22
  96.6 3.3 %collective-permute-done.23 = f32[512]{0:T(512)S(1)} collective-permute-done((f32[512]{0:T(512)S(1)}, f32[512]{0:T(512)S(1)}, u32[]{:S(2)}, u32[]{:S(2)}) %collective-permute-start.23) | collective-permute-done | bytes 2080 | tf_op jit(solution)/shard_map/ppermute | solution.py:27
  100.9 3.5 %collective-permute-done.24 = f32[512]{0:T(512)S(1)} collective-permute-done((f32[512]{0:T(512)S(1)}, f32[512]{0:T(512)S(1)}, u32[]{:S(2)}, u32[]{:S(2)}) %collective-permute-start.24) | collective-permute-done | bytes 2080 | tf_op jit(solution)/shard_map/ppermute | solution.py:27
  106.7 3.1 %collective-permute-done.26 = f32[2048]{0:T(1024)S(1)} collective-permute-done((f32[2048]{0:T(1024)S(1)}, f32[2048]{0:T(1024)S(1)}, u32[]{:S(2)}, u32[]{:S(2)}) %collective-permute-start.26) | collective-permute-done | bytes 8224 | tf_op jit(solution)/shard_map/ppermute | solution.py:27
  111.3 1.6 broadcast_in_dim.10
  113.8 2.7 %multiply_reduce_fusion.1 = f32[512]{0:T(512)S(1)} fusion(f32[512,2048]{1,0:T(8,128)} %get-tuple-element.6, f32[2048]{0:T(1024)S(1)} %minimum_multiply_fusion.1), kind=kLoop, calls=%fused_computation.3 | loop fusion | flops 3145216 | bytes 4204544 | tf_op jit(solution)/shard_map/reduce_sum | solution.py:330
  116.9 3.3 %collective-permute-done.28 = f32[512]{0:T(512)S(1)} collective-permute-done((f32[512]{0:T(512)S(1)}, f32[512]{0:T(512)S(1)}, u32[]{:S(2)}, u32[]{:S(2)}) %collective-permute-start.28) | collective-permute-done | bytes 2080 | tf_op jit(solution)/shard_map/ppermute | solution.py:27
  121.1 3.5 %collective-permute-done.29 = f32[512]{0:T(512)S(1)} collective-permute-done((f32[512]{0:T(512)S(1)}, f32[512]{0:T(512)S(1)}, u32[]{:S(2)}, u32[]{:S(2)}) %collective-permute-start.29) | collective-permute-done | bytes 2080 | tf_op jit(solution)/shard_map/ppermute | solution.py:27
  124.6 2.8 %multiply_reduce_fusion = f32[2048]{0:T(1024)S(1)} fusion(f32[512,2048]{1,0:T(8,128)} %get-tuple-element.6, f32[512]{0:T(512)S(1)} %add_divide_fusion.1), kind=kLoop, calls=%fused_computation.2 | loop fusion | flops 3143680 | bytes 4204544 | tf_op jit(solution)/shard_map/reduce_sum | solution.py:331
  130.1 2.2 collective-permute-done.31
  134.4 1.6 collective-permute-done.32
  137.8 2.4 %collective-permute-done.33 = f32[512]{0:T(512)S(1)} collective-permute-done((f32[512]{0:T(512)S(1)}, f32[512]{0:T(512)S(1)}, u32[]{:S(2)}, u32[]{:S(2)}) %collective-permute-start.33) | collective-permute-done | bytes 2080 | tf_op jit(solution)/shard_map/ppermute | solution.py:27
  142.1 2.6 %collective-permute-done.34 = f32[512]{0:T(512)S(1)} collective-permute-done((f32[512]{0:T(512)S(1)}, f32[512]{0:T(512)S(1)}, u32[]{:S(2)}, u32[]{:S(2)}) %collective-permute-start.34) | collective-permute-done | bytes 2080 | tf_op jit(solution)/shard_map/ppermute | solution.py:27
  144.8 2.5 %multiply_convert_fusion = (bf16[512,2048]{1,0:T(8,128)(2,1)S(1)}, bf16[512,2048]{1,0:T(8,128)(2,1)}) fusion(bf16[512,2048]{1,0:T(8,128)(2,1)S(1)} %copy-done.35, f32[512,2048]{1,0:T(8,128)S(1)} %copy-done.33, f32[512]{0:T(512)S(1)} %bitcast.27, f32[512]{0:T(512)S(1)} %add_divide_fusion, f32[2048]{0:T(1024)S(1)} %minimum_multiply_fusion), kind=kLoop, calls=%fused_computation | loop fusion | flops 10485760 | bytes 10498048 | tf_op jit(solution)/shard_map/convert_element_type | solution.py:337
  148.6 9.3 %shard_map.59 = bf16[4,512,512]{2,1,0:T(8,128)(2,1)} custom-call(bf16[512,2048]{1,0:T(8,128)(2,1)S(1)} %get-tuple-element.9.grad_ref, bf16[256,2048]{1,0:T(8,128)(2,1)S(1)} %copy-done, bf16[128,2048]{1,0:T(8,128)(2,1)S(1)} %copy-done.15, bf16[128,2048]{1,0:T(8,128)(2,1)S(1)} %copy-done.11, bf16[128,2048]{1,0:T(8,128)(2,1)S(1)} %copy-done.9, ...), custom_call_target="tpu_custom_call" | custom-call | flops 4294967296 | bytes 8388608 | tf_op jit(solution)/shard_map/pallas_call | solution.py:282
  159.6 1.7 collective-permute-start.38
  161.3 1.7 convolution_convert_fusion.4
  163.0 1.7 convolution_convert_fusion
  165.3 1.7 convolution_convert_fusion.6
  167.0 1.8 convolution_convert_fusion.2
  168.9 5.2 %collective-permute-done.35 = bf16[512,512]{1,0:T(8,128)(2,1)S(1)} collective-permute-done((bf16[512,512]{1,0:T(8,128)(2,1)S(1)}, bf16[512,512]{1,0:T(8,128)(2,1)S(1)}, u32[]{:S(2)}, u32[]{:S(2)}) %collective-permute-start.35) | collective-permute-done | bytes 524320 | tf_op jit(solution)/shard_map/ppermute | solution.py:52
  175.0 1.7 fusion.3
  177.4 1.7 fusion.8
  179.2 1.5 collective-permute-start.45
  180.7 1.7 fusion.5
  184.9 17.5 %collective-permute-done.45 = bf16[128,2048]{1,0:T(8,128)(2,1)S(1)} collective-permute-done((bf16[128,2048]{1,0:T(8,128)(2,1)S(1)}, bf16[128,2048]{1,0:T(8,128)(2,1)S(1)}, u32[]{:S(2)}, u32[]{:S(2)}) %collective-permute-start.45) | collective-permute-done | bytes 524320 | tf_op jit(solution)/shard_map/ppermute | solution.py:27
  202.4 2.5 %collective-permute-start.37 = (bf16[512,512]{1,0:T(8,128)(2,1)S(1)}, bf16[512,512]{1,0:T(8,128)(2,1)S(1)}, u32[]{:S(2)}, u32[]{:S(2)}) collective-permute-start(bf16[512,512]{1,0:T(8,128)(2,1)S(1)} %get-tuple-element.13), channel_id=1, source_target_pairs={{0,1},{1,0},{2,3},{3,2},{4,5},{5,4},{6,7},{7,6},{8,9},{9,8},{10,11... | collective-permute-start | bytes 1572872 | tf_op jit(solution)/shard_map/ppermute | solution.py:52
  205.0 2.6 %collective-permute-done.47 = bf16[128,2048]{1,0:T(8,128)(2,1)S(1)} collective-permute-done((bf16[128,2048]{1,0:T(8,128)(2,1)S(1)}, bf16[128,2048]{1,0:T(8,128)(2,1)S(1)}, u32[]{:S(2)}, u32[]{:S(2)}) %collective-permute-start.47) | collective-permute-done | bytes 524320 | tf_op jit(solution)/shard_map/ppermute | solution.py:27
  209.6 6.8 %collective-permute-done.37 = bf16[512,512]{1,0:T(8,128)(2,1)S(1)} collective-permute-done((bf16[512,512]{1,0:T(8,128)(2,1)S(1)}, bf16[512,512]{1,0:T(8,128)(2,1)S(1)}, u32[]{:S(2)}, u32[]{:S(2)}) %collective-permute-start.37) | collective-permute-done | bytes 524320 | tf_op jit(solution)/shard_map/ppermute | solution.py:52
  216.9 1.7 fusion.1
  219.7 1.7 collective-permute-done.46
  221.4 7.6 %collective-permute-done.48 = bf16[128,2048]{1,0:T(8,128)(2,1)S(1)} collective-permute-done((bf16[128,2048]{1,0:T(8,128)(2,1)S(1)}, bf16[128,2048]{1,0:T(8,128)(2,1)S(1)}, u32[]{:S(2)}, u32[]{:S(2)}) %collective-permute-start.48) | collective-permute-done | bytes 524320 | tf_op jit(solution)/shard_map/ppermute | solution.py:27
  (182 shorter events, 41.5 us)
Async XLA Ops:
  0.6 11.6 %collective-permute-start.1 = (bf16[512,512]{1,0:T(8,128)(2,1)}, bf16[512,512]{1,0:T(8,128)(2,1)S(1)}, u32[]{:S(2)}, u32[]{:S(2)}) collective-permute-start(bf16[512,512]{1,0:T(8,128)(2,1)} %refs_0_.2), channel_id=1, source_target_pairs={{0,0},{1,2},{2,1},{3,3},{4,4},{5,6},{6,5},{7,7},{8,8},{9,10},{10,9... | collective-permute-start | bytes 1572872 | tf_op jit(solution)/shard_map/ppermute | solution.py:52
  2.5 16.7 %collective-permute-start = (bf16[512,512]{1,0:T(8,128)(2,1)}, bf16[512,512]{1,0:T(8,128)(2,1)S(1)}, u32[]{:S(2)}, u32[]{:S(2)}) collective-permute-start(bf16[512,512]{1,0:T(8,128)(2,1)} %refs_0_.2), channel_id=1, source_target_pairs={{0,1},{1,0},{2,3},{3,2},{4,5},{5,4},{6,7},{7,6},{8,9},{9,8},{10,11... | collective-permute-start | bytes 1572872 | tf_op jit(solution)/shard_map/ppermute | solution.py:52
  8.7 14.9 %collective-permute-start.7 = (bf16[128,2048]{1,0:T(8,128)(2,1)S(1)}, bf16[128,2048]{1,0:T(8,128)(2,1)S(1)}, u32[]{:S(2)}, u32[]{:S(2)}) collective-permute-start(bf16[128,2048]{1,0:T(8,128)(2,1)S(1)} %get-tuple-element.19), channel_id=1, source_target_pairs={{0,8},{4,12},{8,0},{12,4},{16,24},{20,28},{24,16},{28,20},{1,9},{5... | collective-permute-start | bytes 1572872 | tf_op jit(solution)/shard_map/ppermute | solution.py:27
  10.2 14.9 %collective-permute-start.6 = (bf16[128,2048]{1,0:T(8,128)(2,1)S(1)}, bf16[128,2048]{1,0:T(8,128)(2,1)S(1)}, u32[]{:S(2)}, u32[]{:S(2)}) collective-permute-start(bf16[128,2048]{1,0:T(8,128)(2,1)S(1)} %get-tuple-element.19), channel_id=1, source_target_pairs={{0,16},{4,20},{8,24},{12,28},{16,0},{20,4},{24,8},{28,12},{1,17},{... | collective-permute-start | bytes 1572872 | tf_op jit(solution)/shard_map/ppermute | solution.py:27
  11.7 22.5 %collective-permute-start.8 = (bf16[128,2048]{1,0:T(8,128)(2,1)S(1)}, bf16[128,2048]{1,0:T(8,128)(2,1)S(1)}, u32[]{:S(2)}, u32[]{:S(2)}) collective-permute-start(bf16[128,2048]{1,0:T(8,128)(2,1)S(1)} %get-tuple-element.20), channel_id=1, source_target_pairs={{0,16},{4,20},{8,24},{12,28},{16,0},{20,4},{24,8},{28,12},{1,17},{... | collective-permute-start | bytes 1572872 | tf_op jit(solution)/shard_map/ppermute | solution.py:27
  12.3 22.0 %collective-permute-start.5 = (bf16[128,2048]{1,0:T(8,128)(2,1)S(1)}, bf16[128,2048]{1,0:T(8,128)(2,1)S(1)}, u32[]{:S(2)}, u32[]{:S(2)}) collective-permute-start(bf16[128,2048]{1,0:T(8,128)(2,1)S(1)} %get-tuple-element.20), channel_id=1, source_target_pairs={{0,8},{4,12},{8,0},{12,4},{16,24},{20,28},{24,16},{28,20},{1,9},{5... | collective-permute-start | bytes 1572872 | tf_op jit(solution)/shard_map/ppermute | solution.py:27
  19.2 15.6 %collective-permute-start.2 = (bf16[512,512]{1,0:T(8,128)(2,1)S(1)}, bf16[512,512]{1,0:T(8,128)(2,1)S(1)}, u32[]{:S(2)}, u32[]{:S(2)}) collective-permute-start(bf16[512,512]{1,0:T(8,128)(2,1)S(1)} %collective-permute-done.1.refs_2_), channel_id=1, source_target_pairs={{0,1},{1,0},{2,3},{3,2},{4,5},{5,4},{6,7},{7,6},{8,9},{9,8},{10,11... | collective-permute-start | bytes 1572872 | tf_op jit(solution)/shard_map/ppermute | solution.py:52
  23.6 11.7 %collective-permute-start.3 = (bf16[512,512]{1,0:T(8,128)(2,1)S(1)}, bf16[512,512]{1,0:T(8,128)(2,1)S(1)}, u32[]{:S(2)}, u32[]{:S(2)}) collective-permute-start(bf16[512,512]{1,0:T(8,128)(2,1)S(1)} %collective-permute-done.refs_1_), channel_id=1, source_target_pairs={{0,0},{1,2},{2,1},{3,3},{4,4},{5,6},{6,5},{7,7},{8,8},{9,10},{10,9... | collective-permute-start | bytes 1572872 | tf_op jit(solution)/shard_map/ppermute | solution.py:52
  25.1 10.3 %collective-permute-start.14 = (bf16[128,2048]{1,0:T(8,128)(2,1)S(1)}, bf16[128,2048]{1,0:T(8,128)(2,1)S(1)}, u32[]{:S(2)}, u32[]{:S(2)}) collective-permute-start(bf16[128,2048]{1,0:T(8,128)(2,1)S(1)} %collective-permute-done.7.refs_9_.refs_3_), channel_id=1, source_target_pairs={{0,4},{4,0},{8,12},{12,8},{16,20},{20,16},{24,28},{28,24},{1,5},{5... | collective-permute-start | bytes 1572872 | tf_op jit(solution)/shard_map/ppermute | solution.py:27
  34.3 15.4 %collective-permute-start.11 = (bf16[256,2048]{1,0:T(8,128)(2,1)S(1)}, bf16[256,2048]{1,0:T(8,128)(2,1)S(1)}, u32[]{:S(2)}, u32[]{:S(2)}) collective-permute-start(bf16[256,2048]{1,0:T(8,128)(2,1)S(1)} %copy-done), channel_id=1, source_target_pairs={{0,4},{4,0},{8,12},{12,8},{16,20},{20,16},{24,28},{28,24},{1,5},{5... | collective-permute-start | bytes 3145736 | tf_op jit(solution)/shard_map/ppermute | solution.py:27
  34.3 3.4 %collective-permute-start.13 = (bf16[128,2048]{1,0:T(8,128)(2,1)S(1)}, bf16[128,2048]{1,0:T(8,128)(2,1)S(1)}, u32[]{:S(2)}, u32[]{:S(2)}) collective-permute-start(bf16[128,2048]{1,0:T(8,128)(2,1)S(1)} %collective-permute-done.6.refs_8_.refs_2_), channel_id=1, source_target_pairs={{0,4},{4,0},{8,12},{12,8},{16,20},{20,16},{24,28},{28,24},{1,5},{5... | collective-permute-start | bytes 1572872 | tf_op jit(solution)/shard_map/ppermute | solution.py:27
  34.8 13.9 %collective-permute-start.10 = (bf16[128,2048]{1,0:T(8,128)(2,1)S(1)}, bf16[128,2048]{1,0:T(8,128)(2,1)S(1)}, u32[]{:S(2)}, u32[]{:S(2)}) collective-permute-start(bf16[128,2048]{1,0:T(8,128)(2,1)S(1)} %collective-permute-done.6.refs_8_.refs_2_), channel_id=1, source_target_pairs={{0,8},{4,12},{8,0},{12,4},{16,24},{20,28},{24,16},{28,20},{1,9},{5... | collective-permute-start | bytes 1572872 | tf_op jit(solution)/shard_map/ppermute | solution.py:27
  35.4 13.7 %collective-permute-start.15 = (bf16[128,2048]{1,0:T(8,128)(2,1)S(1)}, bf16[128,2048]{1,0:T(8,128)(2,1)S(1)}, u32[]{:S(2)}, u32[]{:S(2)}) collective-permute-start(bf16[128,2048]{1,0:T(8,128)(2,1)S(1)} %collective-permute-done.8.refs_10_.refs_4_), channel_id=1, source_target_pairs={{0,4},{4,0},{8,12},{12,8},{16,20},{20,16},{24,28},{28,24},{1,5},{5... | collective-permute-start | bytes 1572872 | tf_op jit(solution)/shard_map/ppermute | solution.py:27
  35.4 14.3 %collective-permute-start.9 = (bf16[128,2048]{1,0:T(8,128)(2,1)S(1)}, bf16[128,2048]{1,0:T(8,128)(2,1)S(1)}, u32[]{:S(2)}, u32[]{:S(2)}) collective-permute-start(bf16[128,2048]{1,0:T(8,128)(2,1)S(1)} %collective-permute-done.5.refs_7_.refs_1_), channel_id=1, source_target_pairs={{0,16},{4,20},{8,24},{12,28},{16,0},{20,4},{24,8},{28,12},{1,17},{... | collective-permute-start | bytes 1572872 | tf_op jit(solution)/shard_map/ppermute | solution.py:27
  37.7 12.0 %collective-permute-start.12 = (bf16[128,2048]{1,0:T(8,128)(2,1)S(1)}, bf16[128,2048]{1,0:T(8,128)(2,1)S(1)}, u32[]{:S(2)}, u32[]{:S(2)}) collective-permute-start(bf16[128,2048]{1,0:T(8,128)(2,1)S(1)} %collective-permute-done.5.refs_7_.refs_1_), channel_id=1, source_target_pairs={{0,4},{4,0},{8,12},{12,8},{16,20},{20,16},{24,28},{28,24},{1,5},{5... | collective-permute-start | bytes 1572872 | tf_op jit(solution)/shard_map/ppermute | solution.py:27
  48.7 13.1 %collective-permute-start.4 = (bf16[512,512]{1,0:T(8,128)(2,1)S(1)}, bf16[512,512]{1,0:T(8,128)(2,1)S(1)}, u32[]{:S(2)}, u32[]{:S(2)}) collective-permute-start(bf16[512,512]{1,0:T(8,128)(2,1)S(1)} %collective-permute-done.3.refs_4_), channel_id=1, source_target_pairs={{0,1},{1,0},{2,3},{3,2},{4,5},{5,4},{6,7},{7,6},{8,9},{9,8},{10,11... | collective-permute-start | bytes 1572872 | tf_op jit(solution)/shard_map/ppermute | solution.py:52
  49.0 12.8 %collective-permute-start.17 = (bf16[128,2048]{1,0:T(8,128)(2,1)S(1)}, bf16[128,2048]{1,0:T(8,128)(2,1)S(1)}, u32[]{:S(2)}, u32[]{:S(2)}) collective-permute-start(bf16[128,2048]{1,0:T(8,128)(2,1)S(1)} %collective-permute-done.10.refs_12_.refs_6_), channel_id=1, source_target_pairs={{0,4},{4,0},{8,12},{12,8},{16,20},{20,16},{24,28},{28,24},{1,5},{5... | collective-permute-start | bytes 1572872 | tf_op jit(solution)/shard_map/ppermute | solution.py:27
  49.7 12.1 %collective-permute-start.16 = (bf16[128,2048]{1,0:T(8,128)(2,1)S(1)}, bf16[128,2048]{1,0:T(8,128)(2,1)S(1)}, u32[]{:S(2)}, u32[]{:S(2)}) collective-permute-start(bf16[128,2048]{1,0:T(8,128)(2,1)S(1)} %collective-permute-done.9.refs_11_.refs_5_), channel_id=1, source_target_pairs={{0,4},{4,0},{8,12},{12,8},{16,20},{20,16},{24,28},{28,24},{1,5},{5... | collective-permute-start | bytes 1572872 | tf_op jit(solution)/shard_map/ppermute | solution.py:27
  75.3 3.9 %collective-permute-start.18 = (f32[2,512]{1,0:T(2,128)}, f32[2,512]{1,0:T(2,128)S(1)}, u32[]{:S(2)}, u32[]{:S(2)}) collective-permute-start(f32[2,512]{1,0:T(2,128)} %get-tuple-element.7), channel_id=1, source_target_pairs={{0,1},{1,0},{2,3},{3,2},{4,5},{5,4},{6,7},{7,6},{8,9},{9,8},{10,11... | collective-permute-start | bytes 12296 | tf_op jit(solution)/shard_map/ppermute | solution.py:27
  79.8 4.5 %collective-permute-start.19 = (f32[2,512]{1,0:T(2,128)S(1)}, f32[2,512]{1,0:T(2,128)S(1)}, u32[]{:S(2)}, u32[]{:S(2)}) collective-permute-start(f32[2,512]{1,0:T(2,128)S(1)} %add.166), channel_id=1, source_target_pairs={{0,2},{1,3},{2,0},{3,1},{4,6},{5,7},{6,4},{7,5},{8,10},{9,11},{10,... | collective-permute-start | bytes 12296 | tf_op jit(solution)/shard_map/ppermute | solution.py:27
  87.2 1.2 collective-permute-start.20
  88.4 3.7 %collective-permute-start.21 = (f32[2048]{0:T(1024)S(1)}, f32[2048]{0:T(1024)S(1)}, u32[]{:S(2)}, u32[]{:S(2)}) collective-permute-start(f32[2048]{0:T(1024)S(1)} %add.168), channel_id=1, source_target_pairs={{0,8},{4,12},{8,0},{12,4},{16,24},{20,28},{24,16},{28,20},{1,9},{5... | collective-permute-start | bytes 24584 | tf_op jit(solution)/shard_map/ppermute | solution.py:27
  92.1 3.7 %collective-permute-start.22 = (f32[2048]{0:T(1024)S(1)}, f32[2048]{0:T(1024)S(1)}, u32[]{:S(2)}, u32[]{:S(2)}) collective-permute-start(f32[2048]{0:T(1024)S(1)} %add.169), channel_id=1, source_target_pairs={{0,16},{4,20},{8,24},{12,28},{16,0},{20,4},{24,8},{28,12},{1,17},{... | collective-permute-start | bytes 24584 | tf_op jit(solution)/shard_map/ppermute | solution.py:27
  96.3 3.6 %collective-permute-start.23 = (f32[512]{0:T(512)S(1)}, f32[512]{0:T(512)S(1)}, u32[]{:S(2)}, u32[]{:S(2)}) collective-permute-start(f32[512]{0:T(512)S(1)} %multiply_reduce_fusion.3), channel_id=1, source_target_pairs={{0,1},{1,0},{2,3},{3,2},{4,5},{5,4},{6,7},{7,6},{8,9},{9,8},{10,11... | collective-permute-start | bytes 6152 | tf_op jit(solution)/shard_map/ppermute | solution.py:27
  99.9 4.5 %collective-permute-start.24 = (f32[512]{0:T(512)S(1)}, f32[512]{0:T(512)S(1)}, u32[]{:S(2)}, u32[]{:S(2)}) collective-permute-start(f32[512]{0:T(512)S(1)} %add.171), channel_id=1, source_target_pairs={{0,2},{1,3},{2,0},{3,1},{4,6},{5,7},{6,4},{7,5},{8,10},{9,11},{10,... | collective-permute-start | bytes 6152 | tf_op jit(solution)/shard_map/ppermute | solution.py:27
  106.1 3.7 %collective-permute-start.26 = (f32[2048]{0:T(1024)S(1)}, f32[2048]{0:T(1024)S(1)}, u32[]{:S(2)}, u32[]{:S(2)}) collective-permute-start(f32[2048]{0:T(1024)S(1)} %add.173), channel_id=1, source_target_pairs={{0,8},{4,12},{8,0},{12,4},{16,24},{20,28},{24,16},{28,20},{1,9},{5... | collective-permute-start | bytes 24584 | tf_op jit(solution)/shard_map/ppermute | solution.py:27
  109.8 4.0 %collective-permute-start.27 = (f32[2048]{0:T(1024)S(1)}, f32[2048]{0:T(1024)S(1)}, u32[]{:S(2)}, u32[]{:S(2)}) collective-permute-start(f32[2048]{0:T(1024)S(1)} %add.174), channel_id=1, source_target_pairs={{0,16},{4,20},{8,24},{12,28},{16,0},{20,4},{24,8},{28,12},{1,17},{... | collective-permute-start | bytes 24584 | tf_op jit(solution)/shard_map/ppermute | solution.py:27
  116.5 3.6 %collective-permute-start.28 = (f32[512]{0:T(512)S(1)}, f32[512]{0:T(512)S(1)}, u32[]{:S(2)}, u32[]{:S(2)}) collective-permute-start(f32[512]{0:T(512)S(1)} %multiply_reduce_fusion.1), channel_id=1, source_target_pairs={{0,1},{1,0},{2,3},{3,2},{4,5},{5,4},{6,7},{7,6},{8,9},{9,8},{10,11... | collective-permute-start | bytes 6152 | tf_op jit(solution)/shard_map/ppermute | solution.py:27
  120.2 4.5 %collective-permute-start.29 = (f32[512]{0:T(512)S(1)}, f32[512]{0:T(512)S(1)}, u32[]{:S(2)}, u32[]{:S(2)}) collective-permute-start(f32[512]{0:T(512)S(1)} %add.176), channel_id=1, source_target_pairs={{0,2},{1,3},{2,0},{3,1},{4,6},{5,7},{6,4},{7,5},{8,10},{9,11},{10,... | collective-permute-start | bytes 6152 | tf_op jit(solution)/shard_map/ppermute | solution.py:27
  128.7 3.7 %collective-permute-start.31 = (f32[2048]{0:T(1024)S(1)}, f32[2048]{0:T(1024)S(1)}, u32[]{:S(2)}, u32[]{:S(2)}) collective-permute-start(f32[2048]{0:T(1024)S(1)} %add.178), channel_id=1, source_target_pairs={{0,8},{4,12},{8,0},{12,4},{16,24},{20,28},{24,16},{28,20},{1,9},{5... | collective-permute-start | bytes 24584 | tf_op jit(solution)/shard_map/ppermute | solution.py:27
  132.4 3.7 %collective-permute-start.32 = (f32[2048]{0:T(1024)S(1)}, f32[2048]{0:T(1024)S(1)}, u32[]{:S(2)}, u32[]{:S(2)}) collective-permute-start(f32[2048]{0:T(1024)S(1)} %add.179), channel_id=1, source_target_pairs={{0,16},{4,20},{8,24},{12,28},{16,0},{20,4},{24,8},{28,12},{1,17},{... | collective-permute-start | bytes 24584 | tf_op jit(solution)/shard_map/ppermute | solution.py:27
  136.6 3.7 %collective-permute-start.33 = (f32[512]{0:T(512)S(1)}, f32[512]{0:T(512)S(1)}, u32[]{:S(2)}, u32[]{:S(2)}) collective-permute-start(f32[512]{0:T(512)S(1)} %multiply_reduce_fusion.5), channel_id=1, source_target_pairs={{0,1},{1,0},{2,3},{3,2},{4,5},{5,4},{6,7},{7,6},{8,9},{9,8},{10,11... | collective-permute-start | bytes 6152 | tf_op jit(solution)/shard_map/ppermute | solution.py:27
  140.2 4.5 %collective-permute-start.34 = (f32[512]{0:T(512)S(1)}, f32[512]{0:T(512)S(1)}, u32[]{:S(2)}, u32[]{:S(2)}) collective-permute-start(f32[512]{0:T(512)S(1)} %add.181), channel_id=1, source_target_pairs={{0,2},{1,3},{2,0},{3,1},{4,6},{5,7},{6,4},{7,5},{8,10},{9,11},{10,... | collective-permute-start | bytes 6152 | tf_op jit(solution)/shard_map/ppermute | solution.py:27
  159.2 14.9 %collective-permute-start.35 = (bf16[512,512]{1,0:T(8,128)(2,1)S(1)}, bf16[512,512]{1,0:T(8,128)(2,1)S(1)}, u32[]{:S(2)}, u32[]{:S(2)}) collective-permute-start(bf16[512,512]{1,0:T(8,128)(2,1)S(1)} %get-tuple-element.15), channel_id=1, source_target_pairs={{0,1},{1,0},{2,3},{3,2},{4,5},{5,4},{6,7},{7,6},{8,9},{9,8},{10,11... | collective-permute-start | bytes 1572872 | tf_op jit(solution)/shard_map/ppermute | solution.py:52
  159.6 22.9 %collective-permute-start.38 = (bf16[512,512]{1,0:T(8,128)(2,1)S(1)}, bf16[512,512]{1,0:T(8,128)(2,1)S(1)}, u32[]{:S(2)}, u32[]{:S(2)}) collective-permute-start(bf16[512,512]{1,0:T(8,128)(2,1)S(1)} %get-tuple-element.16), channel_id=1, source_target_pairs={{0,1},{1,0},{2,3},{3,2},{4,5},{5,4},{6,7},{7,6},{8,9},{9,8},{10,11... | collective-permute-start | bytes 1572872 | tf_op jit(solution)/shard_map/ppermute | solution.py:52
  162.9 11.3 %collective-permute-start.41 = (bf16[256,2048]{1,0:T(8,128)(2,1)S(1)}, bf16[256,2048]{1,0:T(8,128)(2,1)S(1)}, u32[]{:S(2)}, u32[]{:S(2)}) collective-permute-start(bf16[256,2048]{1,0:T(8,128)(2,1)S(1)} %convolution_convert_fusion.4), channel_id=1, source_target_pairs={{0,4},{4,0},{8,12},{12,8},{16,20},{20,16},{24,28},{28,24},{1,5},{5... | collective-permute-start | bytes 3145736 | tf_op jit(solution)/shard_map/ppermute | solution.py:27
  164.7 12.0 %collective-permute-start.44 = (bf16[256,2048]{1,0:T(8,128)(2,1)S(1)}, bf16[256,2048]{1,0:T(8,128)(2,1)S(1)}, u32[]{:S(2)}, u32[]{:S(2)}) collective-permute-start(bf16[256,2048]{1,0:T(8,128)(2,1)S(1)} %convolution_convert_fusion), channel_id=1, source_target_pairs={{0,4},{4,0},{8,12},{12,8},{16,20},{20,16},{24,28},{28,24},{1,5},{5... | collective-permute-start | bytes 3145736 | tf_op jit(solution)/shard_map/ppermute | solution.py:27
  167.0 41.4 %collective-permute-start.40 = (bf16[256,2048]{1,0:T(8,128)(2,1)S(1)}, bf16[256,2048]{1,0:T(8,128)(2,1)S(1)}, u32[]{:S(2)}, u32[]{:S(2)}) collective-permute-start(bf16[256,2048]{1,0:T(8,128)(2,1)S(1)} %convolution_convert_fusion.6), channel_id=1, source_target_pairs={{0,4},{4,0},{8,12},{12,8},{16,20},{20,16},{24,28},{28,24},{1,5},{5... | collective-permute-start | bytes 3145736 | tf_op jit(solution)/shard_map/ppermute | solution.py:27
  174.1 5.1 %collective-permute-start.43 = (bf16[256,2048]{1,0:T(8,128)(2,1)S(1)}, bf16[256,2048]{1,0:T(8,128)(2,1)S(1)}, u32[]{:S(2)}, u32[]{:S(2)}) collective-permute-start(bf16[256,2048]{1,0:T(8,128)(2,1)S(1)} %convolution_convert_fusion.2), channel_id=1, source_target_pairs={{0,4},{4,0},{8,12},{12,8},{16,20},{20,16},{24,28},{28,24},{1,5},{5... | collective-permute-start | bytes 3145736 | tf_op jit(solution)/shard_map/ppermute | solution.py:27
  174.3 9.4 %collective-permute-start.36 = (bf16[512,512]{1,0:T(8,128)(2,1)S(1)}, bf16[512,512]{1,0:T(8,128)(2,1)S(1)}, u32[]{:S(2)}, u32[]{:S(2)}) collective-permute-start(bf16[512,512]{1,0:T(8,128)(2,1)S(1)} %fusion.16), channel_id=1, source_target_pairs={{0,0},{1,2},{2,1},{3,3},{4,4},{5,6},{6,5},{7,7},{8,8},{9,10},{10,9... | collective-permute-start | bytes 1572872 | tf_op jit(solution)/shard_map/ppermute | solution.py:52
  176.8 42.9 %collective-permute-start.42 = (bf16[128,2048]{1,0:T(8,128)(2,1)S(1)}, bf16[128,2048]{1,0:T(8,128)(2,1)S(1)}, u32[]{:S(2)}, u32[]{:S(2)}) collective-permute-start(bf16[128,2048]{1,0:T(8,128)(2,1)S(1)} %slice.81), channel_id=1, source_target_pairs={{0,8},{4,12},{8,0},{12,4},{16,24},{20,28},{24,16},{28,20},{1,9},{5... | collective-permute-start | bytes 1572872 | tf_op jit(solution)/shard_map/ppermute | solution.py:27
  179.2 23.2 %collective-permute-start.45 = (bf16[128,2048]{1,0:T(8,128)(2,1)S(1)}, bf16[128,2048]{1,0:T(8,128)(2,1)S(1)}, u32[]{:S(2)}, u32[]{:S(2)}) collective-permute-start(bf16[128,2048]{1,0:T(8,128)(2,1)S(1)} %get-tuple-element.17), channel_id=1, source_target_pairs={{0,8},{4,12},{8,0},{12,4},{16,24},{20,28},{24,16},{28,20},{1,9},{5... | collective-permute-start | bytes 1572872 | tf_op jit(solution)/shard_map/ppermute | solution.py:27
  182.5 37.2 %collective-permute-start.49 = (bf16[128,2048]{1,0:T(8,128)(2,1)S(1)}, bf16[128,2048]{1,0:T(8,128)(2,1)S(1)}, u32[]{:S(2)}, u32[]{:S(2)}) collective-permute-start(bf16[128,2048]{1,0:T(8,128)(2,1)S(1)} %slice.80), channel_id=1, source_target_pairs={{0,16},{4,20},{8,24},{12,28},{16,0},{20,4},{24,8},{28,12},{1,17},{... | collective-permute-start | bytes 1572872 | tf_op jit(solution)/shard_map/ppermute | solution.py:27
  183.7 23.9 %collective-permute-start.47 = (bf16[128,2048]{1,0:T(8,128)(2,1)S(1)}, bf16[128,2048]{1,0:T(8,128)(2,1)S(1)}, u32[]{:S(2)}, u32[]{:S(2)}) collective-permute-start(bf16[128,2048]{1,0:T(8,128)(2,1)S(1)} %get-tuple-element.18), channel_id=1, source_target_pairs={{0,16},{4,20},{8,24},{12,28},{16,0},{20,4},{24,8},{28,12},{1,17},{... | collective-permute-start | bytes 1572872 | tf_op jit(solution)/shard_map/ppermute | solution.py:27
  202.4 14.0 %collective-permute-start.37 = (bf16[512,512]{1,0:T(8,128)(2,1)S(1)}, bf16[512,512]{1,0:T(8,128)(2,1)S(1)}, u32[]{:S(2)}, u32[]{:S(2)}) collective-permute-start(bf16[512,512]{1,0:T(8,128)(2,1)S(1)} %get-tuple-element.13), channel_id=1, source_target_pairs={{0,1},{1,0},{2,3},{3,2},{4,5},{5,4},{6,7},{7,6},{8,9},{9,8},{10,11... | collective-permute-start | bytes 1572872 | tf_op jit(solution)/shard_map/ppermute | solution.py:52
  207.6 11.0 %collective-permute-start.39 = (bf16[512,512]{1,0:T(8,128)(2,1)S(1)}, bf16[512,512]{1,0:T(8,128)(2,1)S(1)}, u32[]{:S(2)}, u32[]{:S(2)}) collective-permute-start(bf16[512,512]{1,0:T(8,128)(2,1)S(1)} %get-tuple-element.14), channel_id=1, source_target_pairs={{0,0},{1,2},{2,1},{3,3},{4,4},{5,6},{6,5},{7,7},{8,8},{9,10},{10,9... | collective-permute-start | bytes 1572872 | tf_op jit(solution)/shard_map/ppermute | solution.py:52
  208.4 13.0 %collective-permute-start.46 = (bf16[128,2048]{1,0:T(8,128)(2,1)S(1)}, bf16[128,2048]{1,0:T(8,128)(2,1)S(1)}, u32[]{:S(2)}, u32[]{:S(2)}) collective-permute-start(bf16[128,2048]{1,0:T(8,128)(2,1)S(1)} %fusion.12), channel_id=1, source_target_pairs={{0,16},{4,20},{8,24},{12,28},{16,0},{20,4},{24,8},{28,12},{1,17},{... | collective-permute-start | bytes 1572872 | tf_op jit(solution)/shard_map/ppermute | solution.py:27
  216.4 12.6 %collective-permute-start.48 = (bf16[128,2048]{1,0:T(8,128)(2,1)S(1)}, bf16[128,2048]{1,0:T(8,128)(2,1)S(1)}, u32[]{:S(2)}, u32[]{:S(2)}) collective-permute-start(bf16[128,2048]{1,0:T(8,128)(2,1)S(1)} %fusion.9), channel_id=1, source_target_pairs={{0,8},{4,12},{8,0},{12,4},{16,24},{20,28},{24,16},{28,20},{1,9},{5... | collective-permute-start | bytes 1572872 | tf_op jit(solution)/shard_map/ppermute | solution.py:27
  (39 other events, 666.4 us)

commit v3 on v0

v3 whole, which is shorter than its diff:
```python
import jax
import jax.numpy as jnp
from jax import lax
from jax.sharding import PartitionSpec as P

ITERS = 3


softcap = 15.0
sharpen = 2.0
f32 = jnp.float32
bf16 = jnp.bfloat16


def matmul(left, right, dims):
    return lax.dot_general(left, right, (dims, ((), ())), preferred_element_type=f32)


def flip(value, mask):
    size = lax.axis_size("sample")
    return lax.ppermute(value, "sample", [(i, i ^ mask) for i in range(size)])


def swap(value, parity):
    samples, size = lax.axis_size("sample"), lax.axis_size("cls")
    pairs = []
    for sample in range(samples):
        for i in range(size):
            j = ((i + parity) ^ 1) - parity
            there = sample * size + j if 0 <= j < size else (sample ^ 1) * size + i
            pairs.append((sample * size + i, there))
    return lax.ppermute(value, ("sample", "cls"), pairs)


def total_over(value, axis):
    copies = jnp.broadcast_to(value[None], (lax.axis_size(axis),) + value.shape)
    return jnp.sum(lax.all_to_all(copies, axis, 0, 0), axis=0)


def row_total(value):
    return total_over(value, "cls")


def column_total(value):
    return total_over(value, "sample")


def after(value, *others):
    return lax.optimization_barrier((value,) + others)[0]


def chip_axes(size):
    chips = size // 2
    bits = chips.bit_length() - 1
    low = 1 << ((bits + 1) // 2)
    first = [2 * m for m in range(1, low)]
    second = [2 * low * m for m in range(1, chips // low)]
    return first, second


def gather_head(head):
    size = lax.axis_size("sample")
    first, second = chip_axes(size)
    half = head.shape[0] // 2
    held = {mask: flip(head, mask) for mask in first + second}
    same = [(0, 0, head)] + [(mask, 0, block) for mask, block in held.items()]
    for a in first:
        for b in second:
            same.append((a | b, 0, flip(held[a][:half], b)))
            same.append((a | b, half, flip(held[b][half:], a)))
    return same + [(mask | 1, offset, flip(block, 1)) for mask, offset, block in same]


def gather_features(features):
    size = lax.axis_size("cls")
    me = lax.axis_index("cls")
    rows, width = features.shape
    pieces = []
    even = odd = features
    for hop in range(1, size):
        even, odd = swap(odd, 0), swap(even, 1)
        pieces.append((0, hop, even))
        if hop < size - 1 or size % 2:
            pieces.append((1, hop, odd))
    whole = jnp.zeros((rows, width * size), features.dtype)
    for parity, hop, block in reversed(pieces):
        above, below = me + hop, me - hop
        above = jnp.where(above >= size, 2 * size - 1 - above, above)
        below = jnp.where(below < 0, -1 - below, below)
        source = jnp.where((me & 1) == parity, above, below)
        whole = lax.dynamic_update_slice(whole, block, (0, source * width))
    return lax.dynamic_update_slice(whole, features, (0, me * width))


def per_device(features, head, class_cap):
    local_rows, width = features.shape
    depth, class_local = head.shape
    samples = lax.axis_size("sample")
    groups = lax.axis_size("cls")
    ratio = local_rows * samples / (class_local * groups)
    me = lax.axis_index("sample")
    place = lax.axis_index("cls")
    first, second = chip_axes(samples)
    half = depth // 2

    pieces = {(mask, offset): block for mask, offset, block in gather_head(head)}
    whole = gather_features(features)
    parts, columns = [], []
    for mask in range(0, samples, 2):
        offsets = [offset for m, offset in pieces if m == mask]
        same = [pieces[mask, offset] for offset in offsets]
        other = [pieces[mask | 1, offset] for offset in offsets]
        lead = (me & 1) == 0
        parts += [jnp.where(lead, s, o) for s, o in zip(same, other)]
        parts += [jnp.where(lead, o, s) for s, o in zip(same, other)]
        columns.append(lax.dynamic_slice(whole, (0, ((me ^ mask) // 2) * 2 * depth), (local_rows, 2 * depth)))
    head_full = jnp.concatenate(parts, axis=0)
    wide = jnp.concatenate(columns, axis=1)

    logits = matmul(wide, head_full, ((1,), (0,)))
    tanh = jnp.tanh(logits / softcap)
    student = jnp.exp(softcap * tanh)
    plan = student * student
    masses = row_total(jnp.stack([jnp.sum(student, axis=1), jnp.sum(plan, axis=1)]))
    ceiling = class_cap.astype(f32) * ratio
    row_mass = masses[1]
    scale = jnp.ones((class_local,), f32)
    for iteration in range(ITERS):
        if iteration > 0:
            row_mass = row_total(jnp.sum(plan * scale[None, :], axis=1))
        mass = column_total(jnp.sum(plan * (1.0 / row_mass)[:, None], axis=0) * scale)
        scale = scale * jnp.minimum(1.0, ceiling / mass)
    row_mass = row_total(jnp.sum(plan * scale[None, :], axis=1))
    targets = (plan * scale[None, :] * (1.0 / row_mass)[:, None]).astype(bf16)
    slope = 1.0 - tanh * tanh
    grad = ((student * (1.0 / masses[0])[:, None] - targets.astype(f32)) * slope).astype(bf16)

    def head_partial(mask, grad):
        blocks = lax.dynamic_slice(whole, (0, (me ^ mask) * depth), (local_rows, depth))
        return matmul(blocks, grad, ((0,), (0,))).astype(bf16)

    def both(mask, grad):
        theirs = head_partial(mask | 1, grad)
        mine = head_partial(mask, grad)
        return mine, flip(theirs, 1)

    def share(index, grad):
        rows = lax.dynamic_slice(
            head_full, (((jnp.clip(index, 0, groups - 1) * width // (2 * depth)) ^ (me // 2)) * 2 * depth, 0), (width, class_local)
        )
        return matmul(grad, rows, ((1,), (1,)))

    extra = {}
    for a in first:
        for b in second:
            mine, theirs = both(a | b, grad)
            grad = after(grad, mine)
            block = (mine.astype(f32) + theirs.astype(f32)).astype(bf16)
            extra.setdefault((b, 0), []).append(flip(block[:half], a))
            extra.setdefault((a, 1), []).append(flip(block[half:], b))

    def line_block(hop, parity, grad):
        rightward = (place & 1) == parity
        index = jnp.where(rightward, groups - hop + place, place - (groups - hop))
        return rightward, share(index, grad)

    has_left, has_right = place > 0, place < groups - 1
    received = {0: None, 1: None}
    mixed = {}
    for hop in range(1, groups):
        sent = {0: None, 1: None}
        for parity in (0, 1):
            if parity == 1 and hop == 1 and groups % 2 == 0:
                continue
            rightward, block = line_block(hop, parity, grad)
            if received[1 - parity] is not None:
                keep = jnp.where(rightward, has_left, has_right)
                block = block + jnp.where(keep, received[1 - parity].astype(f32), 0.0)
            block = block.astype(bf16)
            grad = after(grad, block) if hop == 1 else grad
            sent[parity] = swap(block, parity)
        received = sent
        if hop == 1:
            for mask in first + second:
                mixed[mask] = both(mask, grad)
            mixed[0] = both(0, grad)
    total = share(place, grad)
    for parity in (0, 1):
        if received[parity] is not None:
            keep = jnp.where((place & 1) == parity, has_right, has_left)
            total = total + jnp.where(keep, received[parity].astype(f32), 0.0)
    grad_features = total.astype(bf16)

    total = mixed[0][0].astype(f32) + mixed[0][1].astype(f32)
    for mask in first + second:
        block = mixed[mask][0].astype(f32) + mixed[mask][1].astype(f32)
        halves = [block[:half], block[half:]]
        for part in (0, 1):
            for more in extra.get((mask, part), []):
                halves[part] = halves[part] + more.astype(f32)
        total = total + flip(jnp.concatenate(halves, axis=0).astype(bf16), mask).astype(f32)
    return (targets, grad_features, total.astype(bf16))


def solution(mesh):
    return jax.shard_map(
        per_device,
        mesh=mesh,
        in_specs=(P("sample", "cls"), P("sample", "cls"), P("cls")),
        out_specs=(P("sample", "cls"), P("sample", "cls"), P("sample", "cls")),
        check_vma=False,
    )
```

time: 357 us -> 220 us (0.62)
  waiting for transfers between devices: 209 us -> 71.3 us
  starting transfers between devices: 0.16 us -> 33.1 us
  blocking collectives: 75.1 us -> 47.5 us
  between operations: 13.8 us -> 1.39 us
  other arithmetic: 24.1 us -> 30 us
    all_gather x2 -> x0, waiting for transfers between devices: 105 us -> none  [the longest x1 55 us: per_device(): head_full = lax.all_gather(head, 'sample', axis=0, tiled=True)]
    reduce_scatter x2 -> x0, waiting for transfers between devices: 103 us -> none  [the longest x1 58.2 us: per_device(): lax.psum_scatter(lax.dot_general(whole, grad_logits, (((0,), (0,)), ((),...]
    psum x7 -> x0, blocking collectives: 75.1 us -> none  [the longest x3 36.2 us: per_device(): column_mass = lax.psum(jnp.sum(transport, axis=0), 'sample')]
    ppermute x0 -> x27, waiting for transfers between devices: none -> 66 us  [the longest x10 46.4 us: swap(): return lax.ppermute(value, ('sample', 'cls'), pairs)]
    all_to_all x0 -> x6, blocking collectives: none -> 47.5 us  [total_over(): return jnp.sum(lax.all_to_all(copies, axis, 0, 0), axis=0)]
    ppermute x0 -> x27, starting transfers between devices: none -> 29.9 us  [the longest x10 18.2 us: swap(): return lax.ppermute(value, ('sample', 'cls'), pairs)]
    all_to_all x0 -> x1, waiting for transfers between devices: none -> 5.35 us  [total_over(): return jnp.sum(lax.all_to_all(copies, axis, 0, 0), axis=0)]
    unnamed x0 -> x10, other arithmetic: none -> 3.94 us
  transfers between devices with their start and end apart: 4 -> 28, of which waited for: 4 -> 10; matrix products, arithmetic and copies ran while one was open for 4% -> 12% of each run, Pallas kernels for 0% -> 0%
where the time goes in v3:
time: 220 us; the launch traced here: 219 us
  waiting for transfers between devices  71.3 us (32%)
  blocking collectives  47.5 us (22%)
  starting transfers between devices  33.1 us (15%)
  other arithmetic  30 us (14%)
  matrix products  29.6 us (13%)
  local copies, waits for them, and re-layouts  6.19 us (3%)
    all_to_all x6, blocking collectives, total_over(): return jnp.sum(lax.all_to_all(copies, axis, 0, 0), axis=0)  47.5 us
    ppermute x10, waiting for transfers between devices, swap(): return lax.ppermute(value, ('sample', 'cls'), pairs)  46.4 us
    dot_general x15, matrix products, matmul(): lax.dot_general(left, right, (dims, ((), ())), preferred_element_type=f32)  29.6 us
    ppermute x17, waiting for transfers between devices, flip(): return lax.ppermute(value, 'sample', [(i, i ^ mask) for i in range(size)])  19.6 us
    ppermute x10, starting transfers between devices, swap(): return lax.ppermute(value, ('sample', 'cls'), pairs)  18.2 us
    ppermute x17, starting transfers between devices, flip(): return lax.ppermute(value, 'sample', [(i, i ^ mask) for i in range(size)])  11.7 us
    reduce_sum x3, other arithmetic, per_device(): row_mass = row_total(jnp.sum(plan * scale[None, :], axis=1))  9.26 us
    reduce_sum x3, other arithmetic, per_device(): jnp.sum(plan * (1.0 / row_mass)[:, None], axis=0) * scale  9.08 us
  transfers between devices with their start and end apart: 28, of which 10 were waited for; matrix products, arithmetic and copies ran while one was open for 12% of the time, Pallas kernels for 0%

profile of v3, /device:TPU:0, one launch (start us, length us, event | category | flops | bytes accessed | tf_op | source)
XLA Modules:
  0.0 219.1 jit_solution(7783274248198579773)
XLA Ops:
  0.6 3.0 %collective-permute-start.6 = (bf16[256,2048]{1,0:T(8,128)(2,1)}, bf16[256,2048]{1,0:T(8,128)(2,1)S(1)}, u32[]{:S(2)}, u32[]{:S(2)}) collective-permute-start(bf16[256,2048]{1,0:T(8,128)(2,1)} %param.4), channel_id=1, source_target_pairs={{0,8},{4,12},{8,0},{12,4},{16,24},{20,28},{24,16},{28,20},{1,9},{5... | collective-permute-start | bytes 3145736 | tf_op jit(solution)/shard_map/ppermute | solution.py:21
  3.6 1.5 collective-permute-start.8
  5.2 1.6 collective-permute-start
  7.0 12.8 %collective-permute-done = bf16[512,512]{1,0:T(8,128)(2,1)} collective-permute-done((bf16[512,512]{1,0:T(8,128)(2,1)}, bf16[512,512]{1,0:T(8,128)(2,1)}, u32[]{:S(2)}, u32[]{:S(2)}) %collective-permute-start) | collective-permute-done | bytes 524320 | tf_op jit(solution)/shard_map/ppermute | solution.py:32
  19.8 3.2 %collective-permute-start.4 = (bf16[512,512]{1,0:T(8,128)(2,1)}, bf16[512,512]{1,0:T(8,128)(2,1)S(1)}, u32[]{:S(2)}, u32[]{:S(2)}) collective-permute-start(bf16[512,512]{1,0:T(8,128)(2,1)} %collective-permute-done.3), channel_id=1, source_target_pairs={{0,1},{1,0},{2,3},{3,2},{4,5},{5,4},{6,7},{7,6},{8,9},{9,8},{10,11... | collective-permute-start | bytes 1572872 | tf_op jit(solution)/shard_map/ppermute | solution.py:32
  23.0 4.0 %collective-permute-done.6 = bf16[256,2048]{1,0:T(8,128)(2,1)S(1)} collective-permute-done((bf16[256,2048]{1,0:T(8,128)(2,1)}, bf16[256,2048]{1,0:T(8,128)(2,1)S(1)}, u32[]{:S(2)}, u32[]{:S(2)}) %collective-permute-start.6) | collective-permute-done | bytes 1048608 | tf_op jit(solution)/shard_map/ppermute | solution.py:21
  27.1 1.8 collective-permute-start.10
  28.9 1.6 collective-permute-start.12
  30.5 4.8 %collective-permute-start.2 = (bf16[512,512]{1,0:T(8,128)(2,1)}, bf16[512,512]{1,0:T(8,128)(2,1)S(1)}, u32[]{:S(2)}, u32[]{:S(2)}) collective-permute-start(bf16[512,512]{1,0:T(8,128)(2,1)} %collective-permute-done.1), channel_id=1, source_target_pairs={{0,1},{1,0},{2,3},{3,2},{4,5},{5,4},{6,7},{7,6},{8,9},{9,8},{10,11... | collective-permute-start | bytes 1572872 | tf_op jit(solution)/shard_map/ppermute | solution.py:32
  35.6 1.6 select_dynamic-update-slice_fusion.4
  37.3 3.0 %collective-permute-done.10 = bf16[128,2048]{1,0:T(8,128)(2,1)S(1)} collective-permute-done((bf16[128,2048]{1,0:T(8,128)(2,1)S(1)}, bf16[128,2048]{1,0:T(8,128)(2,1)S(1)}, u32[]{:S(2)}, u32[]{:S(2)}) %collective-permute-start.10) | collective-permute-done | bytes 524320 | tf_op jit(solution)/shard_map/ppermute | solution.py:21
  40.2 1.3 collective-permute-done.12
  41.5 4.9 %collective-permute-done.2 = bf16[512,512]{1,0:T(8,128)(2,1)S(1)} collective-permute-done((bf16[512,512]{1,0:T(8,128)(2,1)}, bf16[512,512]{1,0:T(8,128)(2,1)S(1)}, u32[]{:S(2)}, u32[]{:S(2)}) %collective-permute-start.2) | collective-permute-done | bytes 524320 | tf_op jit(solution)/shard_map/ppermute | solution.py:32
  46.7 1.2 constant_dynamic-update-slice_fusion.4
  48.0 1.1 constant_dynamic-update-slice_fusion.2
  49.1 1.1 constant_dynamic-update-slice_fusion.1
  50.6 1.1 copy-done
  53.8 6.5 %fusion = (f32[512]{0:T(512)S(1)}, f32[512]{0:T(512)S(1)}, f32[512,2048]{1,0:T(8,128)}) fusion(bf16[2048,2048]{1,0:T(8,128)(2,1)S(1)} %select_dynamic-update-slice_fusion.6, bf16[512,512]{1,0:T(8,128)(2,1)S(1)} %get-tuple-element.12, bf16[512,512]{1,0:T(8,128)(2,1)S(1)} %get-tuple-element.13, bf16[512,512]{1,0:T(8,128)(2,1)S(1)} %get-tuple-element.14, ...), kind=kOutput, calls=%fused_computation.8 | convolution fusion | flops 4308597760 | bytes 14684160 | tf_op jit(solution)/shard_map/dot_general | solution.py:16
  60.4 9.5 %all_to_all.41 = f32[4,2,512]{2,1,0:T(2,128)S(1)} all-to-all(f32[4,2,512]{2,1,0:T(2,128)S(1)} %broadcast_in_dim.24), channel_id=1, replica_groups=mesh['sample'=8,'cls'=4] {'cls'}, dimensions={0} | all-to-all | bytes 32768 | tf_op jit(solution)/shard_map/all_to_all | solution.py:37
  69.9 3.0 %multiply_reduce_fusion.4 = f32[2048]{0:T(1024)S(1)} fusion(f32[512]{0:T(512)S(1)} %bitcast.22, f32[512,2048]{1,0:T(8,128)} %get-tuple-element.19), kind=kLoop, calls=%fused_computation.6 | loop fusion | flops 4192256 | bytes 4204544 | tf_op jit(solution)/shard_map/reduce_sum | solution.py:131
  73.0 7.4 %all_to_all.42 = f32[8,1,2048]{2,1,0:T(1,128)S(1)} all-to-all(f32[8,1,2048]{2,1,0:T(1,128)S(1)} %broadcast_in_dim.25), channel_id=1, replica_groups=mesh['sample'=8,'cls'=4] {'sample'}, dimensions={0} | all-to-all | bytes 131072 | tf_op jit(solution)/shard_map/all_to_all | solution.py:37
  80.5 3.1 %multiply_reduce_fusion.3 = f32[512]{0:T(512)S(1)} fusion(f32[2048]{0:T(1024)S(1)} %divide_minimum_fusion, f32[512,2048]{1,0:T(8,128)} %get-tuple-element.19), kind=kLoop, calls=%fused_computation.5 | loop fusion | flops 4193792 | bytes 4204544 | tf_op jit(solution)/shard_map/reduce_sum | solution.py:130
  83.6 7.9 %all_to_all.43 = f32[4,1,512]{2,1,0:T(1,128)S(1)} all-to-all(f32[4,1,512]{2,1,0:T(1,128)S(1)} %broadcast_in_dim.26), channel_id=1, replica_groups=mesh['sample'=8,'cls'=4] {'cls'}, dimensions={0} | all-to-all | bytes 16384 | tf_op jit(solution)/shard_map/all_to_all | solution.py:37
  91.6 3.0 %multiply_reduce_fusion.2 = f32[2048]{0:T(1024)S(1)} fusion(f32[512]{0:T(512)S(1)} %broadcast_divide_fusion.2, f32[512,2048]{1,0:T(8,128)} %get-tuple-element.19), kind=kLoop, calls=%fused_computation.4 | loop fusion | flops 4192256 | bytes 4204544 | tf_op jit(solution)/shard_map/reduce_sum | solution.py:131
  94.7 7.4 %all_to_all.44 = f32[8,1,2048]{2,1,0:T(1,128)S(1)} all-to-all(f32[8,1,2048]{2,1,0:T(1,128)S(1)} %broadcast_in_dim.27), channel_id=1, replica_groups=mesh['sample'=8,'cls'=4] {'sample'}, dimensions={0} | all-to-all | bytes 131072 | tf_op jit(solution)/shard_map/all_to_all | solution.py:37
  102.1 3.1 %multiply_reduce_fusion.1 = f32[512]{0:T(512)S(1)} fusion(f32[2048]{0:T(1024)S(1)} %minimum_multiply_fusion.1, f32[512,2048]{1,0:T(8,128)} %get-tuple-element.19), kind=kLoop, calls=%fused_computation.3 | loop fusion | flops 4193792 | bytes 4204544 | tf_op jit(solution)/shard_map/reduce_sum | solution.py:130
  105.2 7.9 %all_to_all.45 = f32[4,1,512]{2,1,0:T(1,128)S(1)} all-to-all(f32[4,1,512]{2,1,0:T(1,128)S(1)} %broadcast_in_dim.28), channel_id=1, replica_groups=mesh['sample'=8,'cls'=4] {'cls'}, dimensions={0} | all-to-all | bytes 16384 | tf_op jit(solution)/shard_map/all_to_all | solution.py:37
  113.2 3.0 %multiply_reduce_fusion = f32[2048]{0:T(1024)S(1)} fusion(f32[512]{0:T(512)S(1)} %broadcast_divide_fusion.1, f32[512,2048]{1,0:T(8,128)} %get-tuple-element.19), kind=kLoop, calls=%fused_computation.2 | loop fusion | flops 4192256 | bytes 4204544 | tf_op jit(solution)/shard_map/reduce_sum | solution.py:131
  116.3 7.4 %all_to_all.46 = f32[8,1,2048]{2,1,0:T(1,128)S(1)} all-to-all(f32[8,1,2048]{2,1,0:T(1,128)S(1)} %broadcast_in_dim.29), channel_id=1, replica_groups=mesh['sample'=8,'cls'=4] {'sample'}, dimensions={0} | all-to-all | bytes 131072 | tf_op jit(solution)/shard_map/all_to_all | solution.py:37
  123.7 3.1 %multiply_reduce_fusion.5 = f32[512]{0:T(512)S(1)} fusion(f32[2048]{0:T(1024)S(1)} %minimum_multiply_fusion, f32[512,2048]{1,0:T(8,128)} %get-tuple-element.19), kind=kLoop, calls=%fused_computation.11 | loop fusion | flops 4193792 | bytes 4204544 | tf_op jit(solution)/shard_map/reduce_sum | solution.py:133
  127.4 3.2 %all-to-all-start.6 = ((f32[4,1,512]{2,1,0:T(1,128)}), f32[4,1,512]{2,1,0:T(1,128)S(1)}, u32[]{:S(2)}, u32[]{:S(2)}) async-start(f32[4,1,512]{2,1,0:T(1,128)} %broadcast_in_dim.30), calls=%async_computation.6 | async-start | bytes 16384 | tf_op jit(solution)/shard_map/all_to_all | solution.py:37
  130.9 5.3 %all-to-all-done.6 = f32[4,1,512]{2,1,0:T(1,128)S(1)} async-done(((f32[4,1,512]{2,1,0:T(1,128)}), f32[4,1,512]{2,1,0:T(1,128)S(1)}, u32[]{:S(2)}, u32[]{:S(2)}) %all-to-all-start.6) | async-done | bytes 8224 | tf_op jit(solution)/shard_map/all_to_all | solution.py:37
  136.3 4.5 %multiply_convert_fusion = (bf16[512,2048]{1,0:T(8,128)(2,1)S(1)}, bf16[512,2048]{1,0:T(8,128)(2,1)}) fusion(f32[512,2048]{1,0:T(8,128)} %get-tuple-element.19, f32[512]{0:T(512)S(1)} %bitcast.21, f32[512]{0:T(512)S(1)} %broadcast_divide_fusion, f32[2048]{0:T(1024)S(1)} %minimum_multiply_fusion), kind=kLoop, calls=%fused_computation | loop fusion | flops 12582912 | bytes 8400896 | tf_op jit(solution)/shard_map/convert_element_type | solution.py:136
  141.5 3.2 %fusion.48 = bf16[512,512]{1,0:T(8,128)(2,1)S(1)} fusion(bf16[512,2048]{1,0:T(8,128)(2,1)S(1)} %get-tuple-element.6, bf16[2048,2048]{1,0:T(8,128)(2,1)} %copy-done.4, s32[]{:T(128)S(6)} %select_n.294), kind=kOutput, calls=%fused_computation.55 | convolution fusion | flops 1074003968 | bytes 4718596 | tf_op jit(solution)/shard_map/dot_general | solution.py:16
  145.5 1.3 fusion.51
  146.8 1.5 collective-permute-start.17
  152.0 16.5 %collective-permute-done.17 = bf16[512,512]{1,0:T(8,128)(2,1)S(1)} collective-permute-done((bf16[512,512]{1,0:T(8,128)(2,1)S(1)}, bf16[512,512]{1,0:T(8,128)(2,1)S(1)}, u32[]{:S(2)}, u32[]{:S(2)}) %collective-permute-start.17) | collective-permute-done | bytes 524320 | tf_op jit(solution)/shard_map/ppermute | solution.py:32
  168.4 2.1 fusion.54
  171.0 1.3 fusion.57
  172.9 0.9 collective-permute-start.25
  176.1 11.2 %collective-permute-done.25 = bf16[128,2048]{1,0:T(8,128)(2,1)S(1)} collective-permute-done((bf16[128,2048]{1,0:T(8,128)(2,1)S(1)}, bf16[128,2048]{1,0:T(8,128)(2,1)S(1)}, u32[]{:S(2)}, u32[]{:S(2)}) %collective-permute-start.25) | collective-permute-done | bytes 524320 | tf_op jit(solution)/shard_map/ppermute | solution.py:21
  187.4 1.0 pad_maximum_fusion.1
  189.4 1.1 pad_maximum_fusion
  191.2 2.1 fusion.60
  193.3 5.7 %collective-permute-start.16 = (bf16[512,512]{1,0:T(8,128)(2,1)}, bf16[512,512]{1,0:T(8,128)(2,1)}, u32[]{:S(2)}, u32[]{:S(2)}) collective-permute-start(bf16[512,512]{1,0:T(8,128)(2,1)} %fusion.60), channel_id=1, source_target_pairs={{0,1},{1,0},{2,3},{3,2},{4,5},{5,4},{6,7},{7,6},{8,9},{9,8},{10,11... | collective-permute-start | bytes 1572872 | tf_op jit(solution)/shard_map/ppermute | solution.py:32
  199.0 12.2 %collective-permute-done.16 = bf16[512,512]{1,0:T(8,128)(2,1)} collective-permute-done((bf16[512,512]{1,0:T(8,128)(2,1)}, bf16[512,512]{1,0:T(8,128)(2,1)}, u32[]{:S(2)}, u32[]{:S(2)}) %collective-permute-start.16) | collective-permute-done | bytes 524320 | tf_op jit(solution)/shard_map/ppermute | solution.py:32
  211.2 3.9 %fusion.45 = bf16[512,512]{1,0:T(8,128)(2,1)} fusion(bf16[512,2048]{1,0:T(8,128)(2,1)S(1)} %get-tuple-element.6, bf16[2048,2048]{1,0:T(8,128)(2,1)} %copy-done.4, s32[]{:T(128)S(6)} %select_n.296, bf16[512,512]{1,0:T(8,128)(2,1)} %collective-permute-done.18, bf16[512,512]{1,0:T(8,128)(2,1)} %collective-permute-done.16, pred[]{:T(512)S(6)} %select_n.312, ...), kind=kOutput, calls=%fused_computation.54 | convolution fusion | flops 1075576832 | bytes 5767174 | tf_op jit(solution)/shard_map/dot_general | solution.py:16
  215.3 3.9 %fusion.6 = bf16[256,2048]{1,0:T(8,128)(2,1)} fusion(bf16[512,2048]{1,0:T(8,128)(2,1)S(1)} %get-tuple-element.6, bf16[256,2048]{1,0:T(8,128)(2,1)} %collective-permute-done.26, bf16[256,2048]{1,0:T(8,128)(2,1)} %collective-permute-done.23, bf16[256,2048]{1,0:T(8,128)(2,1)} %collective-permute-done.19, bf16[512,2048]{1,0:T(8,128)(2,1)} %copy-done, ...), kind=kOutput, calls=%fused_computation.24 | convolution fusion | flops 541589504 | bytes 6553604 | tf_op jit(solution)/shard_map/dot_general | solution.py:16
  (105 shorter events, 14.8 us)
Async XLA Ops:
  0.6 34.6 %copy-start.2 = (bf16[256,2048]{1,0:T(8,128)(2,1)S(1)}, bf16[256,2048]{1,0:T(8,128)(2,1)}, u32[]{:S(2)}) copy-start(bf16[256,2048]{1,0:T(8,128)(2,1)} %param.4) | copy-start | bytes 3145732
  0.6 26.4 %collective-permute-start.6 = (bf16[256,2048]{1,0:T(8,128)(2,1)}, bf16[256,2048]{1,0:T(8,128)(2,1)S(1)}, u32[]{:S(2)}, u32[]{:S(2)}) collective-permute-start(bf16[256,2048]{1,0:T(8,128)(2,1)} %param.4), channel_id=1, source_target_pairs={{0,8},{4,12},{8,0},{12,4},{16,24},{20,28},{24,16},{28,20},{1,9},{5... | collective-permute-start | bytes 3145736 | tf_op jit(solution)/shard_map/ppermute | solution.py:21
  3.6 25.3 %collective-permute-start.8 = (bf16[256,2048]{1,0:T(8,128)(2,1)}, bf16[256,2048]{1,0:T(8,128)(2,1)S(1)}, u32[]{:S(2)}, u32[]{:S(2)}) collective-permute-start(bf16[256,2048]{1,0:T(8,128)(2,1)} %param.4), channel_id=1, source_target_pairs={{0,16},{4,20},{8,24},{12,28},{16,0},{20,4},{24,8},{28,12},{1,17},{... | collective-permute-start | bytes 3145736 | tf_op jit(solution)/shard_map/ppermute | solution.py:21
  5.2 25.3 %collective-permute-start.5 = (bf16[256,2048]{1,0:T(8,128)(2,1)}, bf16[256,2048]{1,0:T(8,128)(2,1)}, u32[]{:S(2)}, u32[]{:S(2)}) collective-permute-start(bf16[256,2048]{1,0:T(8,128)(2,1)} %param.4), channel_id=1, source_target_pairs={{0,4},{4,0},{8,12},{12,8},{16,20},{20,16},{24,28},{28,24},{1,5},{5... | collective-permute-start | bytes 3145736 | tf_op jit(solution)/shard_map/ppermute | solution.py:21
  5.2 14.7 %collective-permute-start = (bf16[512,512]{1,0:T(8,128)(2,1)}, bf16[512,512]{1,0:T(8,128)(2,1)}, u32[]{:S(2)}, u32[]{:S(2)}) collective-permute-start(bf16[512,512]{1,0:T(8,128)(2,1)} %param.3), channel_id=1, source_target_pairs={{0,1},{1,0},{2,3},{3,2},{4,5},{5,4},{6,7},{7,6},{8,9},{9,8},{10,11... | collective-permute-start | bytes 1572872 | tf_op jit(solution)/shard_map/ppermute | solution.py:32
  6.7 13.1 %collective-permute-start.3 = (bf16[512,512]{1,0:T(8,128)(2,1)}, bf16[512,512]{1,0:T(8,128)(2,1)}, u32[]{:S(2)}, u32[]{:S(2)}) collective-permute-start(bf16[512,512]{1,0:T(8,128)(2,1)} %param.3), channel_id=1, source_target_pairs={{0,4},{1,2},{2,1},{3,7},{4,0},{5,6},{6,5},{7,3},{8,12},{9,10},{10,... | collective-permute-start | bytes 1572872 | tf_op jit(solution)/shard_map/ppermute | solution.py:32
  19.8 10.7 %collective-permute-start.1 = (bf16[512,512]{1,0:T(8,128)(2,1)}, bf16[512,512]{1,0:T(8,128)(2,1)}, u32[]{:S(2)}, u32[]{:S(2)}) collective-permute-start(bf16[512,512]{1,0:T(8,128)(2,1)} %collective-permute-done), channel_id=1, source_target_pairs={{0,4},{1,2},{2,1},{3,7},{4,0},{5,6},{6,5},{7,3},{8,12},{9,10},{10,... | collective-permute-start | bytes 1572872 | tf_op jit(solution)/shard_map/ppermute | solution.py:32
  19.8 28.1 %collective-permute-start.4 = (bf16[512,512]{1,0:T(8,128)(2,1)}, bf16[512,512]{1,0:T(8,128)(2,1)S(1)}, u32[]{:S(2)}, u32[]{:S(2)}) collective-permute-start(bf16[512,512]{1,0:T(8,128)(2,1)} %collective-permute-done.3), channel_id=1, source_target_pairs={{0,1},{1,0},{2,3},{3,2},{4,5},{5,4},{6,7},{7,6},{8,9},{9,8},{10,11... | collective-permute-start | bytes 1572872 | tf_op jit(solution)/shard_map/ppermute | solution.py:32
  27.1 13.2 %collective-permute-start.10 = (bf16[128,2048]{1,0:T(8,128)(2,1)S(1)}, bf16[128,2048]{1,0:T(8,128)(2,1)S(1)}, u32[]{:S(2)}, u32[]{:S(2)}) collective-permute-start(bf16[128,2048]{1,0:T(8,128)(2,1)S(1)} %slice.42), channel_id=1, source_target_pairs={{0,16},{4,20},{8,24},{12,28},{16,0},{20,4},{24,8},{28,12},{1,17},{... | collective-permute-start | bytes 1572872 | tf_op jit(solution)/shard_map/ppermute | solution.py:21
  28.9 12.6 %collective-permute-start.12 = (bf16[128,2048]{1,0:T(8,128)(2,1)S(1)}, bf16[128,2048]{1,0:T(8,128)(2,1)S(1)}, u32[]{:S(2)}, u32[]{:S(2)}) collective-permute-start(bf16[128,2048]{1,0:T(8,128)(2,1)S(1)} %slice.43), channel_id=1, source_target_pairs={{0,8},{4,12},{8,0},{12,4},{16,24},{20,28},{24,16},{28,20},{1,9},{5... | collective-permute-start | bytes 1572872 | tf_op jit(solution)/shard_map/ppermute | solution.py:21
  30.5 21.2 %collective-permute-start.7 = (bf16[256,2048]{1,0:T(8,128)(2,1)S(1)}, bf16[256,2048]{1,0:T(8,128)(2,1)S(1)}, u32[]{:S(2)}, u32[]{:S(2)}) collective-permute-start(bf16[256,2048]{1,0:T(8,128)(2,1)S(1)} %collective-permute-done.6), channel_id=1, source_target_pairs={{0,4},{4,0},{8,12},{12,8},{16,20},{20,16},{24,28},{28,24},{1,5},{5... | collective-permute-start | bytes 3145736 | tf_op jit(solution)/shard_map/ppermute | solution.py:21
  30.5 15.9 %collective-permute-start.2 = (bf16[512,512]{1,0:T(8,128)(2,1)}, bf16[512,512]{1,0:T(8,128)(2,1)S(1)}, u32[]{:S(2)}, u32[]{:S(2)}) collective-permute-start(bf16[512,512]{1,0:T(8,128)(2,1)} %collective-permute-done.1), channel_id=1, source_target_pairs={{0,1},{1,0},{2,3},{3,2},{4,5},{5,4},{6,7},{7,6},{8,9},{9,8},{10,11... | collective-permute-start | bytes 1572872 | tf_op jit(solution)/shard_map/ppermute | solution.py:32
  40.2 12.2 %collective-permute-start.9 = (bf16[256,2048]{1,0:T(8,128)(2,1)S(1)}, bf16[256,2048]{1,0:T(8,128)(2,1)S(1)}, u32[]{:S(2)}, u32[]{:S(2)}) collective-permute-start(bf16[256,2048]{1,0:T(8,128)(2,1)S(1)} %collective-permute-done.8), channel_id=1, source_target_pairs={{0,4},{4,0},{8,12},{12,8},{16,20},{20,16},{24,28},{28,24},{1,5},{5... | collective-permute-start | bytes 3145736 | tf_op jit(solution)/shard_map/ppermute | solution.py:21
  41.5 11.8 %collective-permute-start.11 = (bf16[128,2048]{1,0:T(8,128)(2,1)S(1)}, bf16[128,2048]{1,0:T(8,128)(2,1)S(1)}, u32[]{:S(2)}, u32[]{:S(2)}) collective-permute-start(bf16[128,2048]{1,0:T(8,128)(2,1)S(1)} %collective-permute-done.10), channel_id=1, source_target_pairs={{0,4},{4,0},{8,12},{12,8},{16,20},{20,16},{24,28},{28,24},{1,5},{5... | collective-permute-start | bytes 1572872 | tf_op jit(solution)/shard_map/ppermute | solution.py:21
  46.4 7.0 %collective-permute-start.13 = (bf16[128,2048]{1,0:T(8,128)(2,1)S(1)}, bf16[128,2048]{1,0:T(8,128)(2,1)S(1)}, u32[]{:S(2)}, u32[]{:S(2)}) collective-permute-start(bf16[128,2048]{1,0:T(8,128)(2,1)S(1)} %collective-permute-done.12), channel_id=1, source_target_pairs={{0,4},{4,0},{8,12},{12,8},{16,20},{20,16},{24,28},{28,24},{1,5},{5... | collective-permute-start | bytes 1572872 | tf_op jit(solution)/shard_map/ppermute | solution.py:21
  46.7 3.5 %copy-start.3 = (bf16[512,512]{1,0:T(8,128)(2,1)S(1)}, bf16[512,512]{1,0:T(8,128)(2,1)}, u32[]{:S(2)}) copy-start(bf16[512,512]{1,0:T(8,128)(2,1)} %param.3) | copy-start | bytes 1572868
  50.3 1.4 copy-start
  53.8 6.5 %copy-start.4 = (bf16[2048,2048]{1,0:T(8,128)(2,1)}, bf16[2048,2048]{1,0:T(8,128)(2,1)S(1)}, u32[]{:S(2)}) copy-start(bf16[2048,2048]{1,0:T(8,128)(2,1)S(1)} %select_dynamic-update-slice_fusion.6) | copy-start | bytes 25165828
  69.9 10.5 %copy-start.5 = (bf16[2048]{0:T(1024)(128)(2,1)S(1)}, bf16[2048]{0:T(1024)(128)(2,1)}, u32[]{:S(2)}) copy-start(bf16[2048]{0:T(1024)(128)(2,1)} %param.5) | copy-start | bytes 12292
  127.4 8.8 %all-to-all-start.6 = ((f32[4,1,512]{2,1,0:T(1,128)}), f32[4,1,512]{2,1,0:T(1,128)S(1)}, u32[]{:S(2)}, u32[]{:S(2)}) async-start(f32[4,1,512]{2,1,0:T(1,128)} %broadcast_in_dim.30), calls=%async_computation.6 | async-start | bytes 16384 | tf_op jit(solution)/shard_map/all_to_all | solution.py:37
  136.3 4.5 %copy-start.1 = (bf16[512,2048]{1,0:T(8,128)(2,1)S(1)}, bf16[512,2048]{1,0:T(8,128)(2,1)}, u32[]{:S(2)}) copy-start(bf16[512,2048]{1,0:T(8,128)(2,1)} %copy-done) | copy-start | bytes 6291460
  136.3 9.2 %slice-start = ((s8[8388608]{0:T(1024)(128)(4,1)}), s8[4194304]{0:T(1024)(128)(4,1)S(1)}, s32[]{:S(2)}) async-start(s8[8388608]{0:T(1024)(128)(4,1)} %bitcast.19), calls=%async_computation.7 | async-start | bytes 8388608
  140.8 4.7 %slice-start.1 = ((s8[8388608]{0:T(1024)(128)(4,1)}), s8[4194304]{0:T(1024)(128)(4,1)S(1)}, s32[]{:S(2)}) async-start(s8[8388608]{0:T(1024)(128)(4,1)} %bitcast.19), calls=%async_computation.8 | async-start | bytes 8388608
  144.8 25.7 %collective-permute-start.14 = (bf16[512,512]{1,0:T(8,128)(2,1)S(1)}, bf16[512,512]{1,0:T(8,128)(2,1)S(1)}, u32[]{:S(2)}, u32[]{:S(2)}) collective-permute-start(bf16[512,512]{1,0:T(8,128)(2,1)S(1)} %fusion.48), channel_id=1, source_target_pairs={{0,1},{1,0},{2,3},{3,2},{4,5},{5,4},{6,7},{7,6},{8,9},{9,8},{10,11... | collective-permute-start | bytes 1572872 | tf_op jit(solution)/shard_map/ppermute | solution.py:32
  146.8 21.7 %collective-permute-start.17 = (bf16[512,512]{1,0:T(8,128)(2,1)S(1)}, bf16[512,512]{1,0:T(8,128)(2,1)S(1)}, u32[]{:S(2)}, u32[]{:S(2)}) collective-permute-start(bf16[512,512]{1,0:T(8,128)(2,1)S(1)} %fusion.51), channel_id=1, source_target_pairs={{0,1},{1,0},{2,3},{3,2},{4,5},{5,4},{6,7},{7,6},{8,9},{9,8},{10,11... | collective-permute-start | bytes 1572872 | tf_op jit(solution)/shard_map/ppermute | solution.py:32
  149.0 23.9 %collective-permute-start.24 = (bf16[256,2048]{1,0:T(8,128)(2,1)S(1)}, bf16[256,2048]{1,0:T(8,128)(2,1)S(1)}, u32[]{:S(2)}, u32[]{:S(2)}) collective-permute-start(bf16[256,2048]{1,0:T(8,128)(2,1)S(1)} %convolution_convert_fusion), channel_id=1, source_target_pairs={{0,4},{4,0},{8,12},{12,8},{16,20},{20,16},{24,28},{28,24},{1,5},{5... | collective-permute-start | bytes 3145736 | tf_op jit(solution)/shard_map/ppermute | solution.py:21
  149.8 22.5 %collective-permute-start.21 = (bf16[256,2048]{1,0:T(8,128)(2,1)S(1)}, bf16[256,2048]{1,0:T(8,128)(2,1)S(1)}, u32[]{:S(2)}, u32[]{:S(2)}) collective-permute-start(bf16[256,2048]{1,0:T(8,128)(2,1)S(1)} %convolution_convert_fusion.2), channel_id=1, source_target_pairs={{0,4},{4,0},{8,12},{12,8},{16,20},{20,16},{24,28},{28,24},{1,5},{5... | collective-permute-start | bytes 3145736 | tf_op jit(solution)/shard_map/ppermute | solution.py:21
  151.1 23.5 %collective-permute-start.20 = (bf16[256,2048]{1,0:T(8,128)(2,1)S(1)}, bf16[256,2048]{1,0:T(8,128)(2,1)S(1)}, u32[]{:S(2)}, u32[]{:S(2)}) collective-permute-start(bf16[256,2048]{1,0:T(8,128)(2,1)S(1)} %convolution_convert_fusion.3), channel_id=1, source_target_pairs={{0,4},{4,0},{8,12},{12,8},{16,20},{20,16},{24,28},{28,24},{1,5},{5... | collective-permute-start | bytes 3145736 | tf_op jit(solution)/shard_map/ppermute | solution.py:21
  168.4 46.7 %collective-permute-start.19 = (bf16[256,2048]{1,0:T(8,128)(2,1)S(1)}, bf16[256,2048]{1,0:T(8,128)(2,1)}, u32[]{:S(2)}, u32[]{:S(2)}) collective-permute-start(bf16[256,2048]{1,0:T(8,128)(2,1)S(1)} %convolution_convert_fusion.5), channel_id=1, source_target_pairs={{0,4},{4,0},{8,12},{12,8},{16,20},{20,16},{24,28},{28,24},{1,5},{5... | collective-permute-start | bytes 3145736 | tf_op jit(solution)/shard_map/ppermute | solution.py:21
  170.5 28.5 %collective-permute-start.18 = (bf16[512,512]{1,0:T(8,128)(2,1)}, bf16[512,512]{1,0:T(8,128)(2,1)}, u32[]{:S(2)}, u32[]{:S(2)}) collective-permute-start(bf16[512,512]{1,0:T(8,128)(2,1)} %fusion.54), channel_id=1, source_target_pairs={{0,4},{1,2},{2,1},{3,7},{4,0},{5,6},{6,5},{7,3},{8,12},{9,10},{10,... | collective-permute-start | bytes 1572872 | tf_op jit(solution)/shard_map/ppermute | solution.py:32
  172.3 18.8 %collective-permute-start.15 = (bf16[512,512]{1,0:T(8,128)(2,1)S(1)}, bf16[512,512]{1,0:T(8,128)(2,1)S(1)}, u32[]{:S(2)}, u32[]{:S(2)}) collective-permute-start(bf16[512,512]{1,0:T(8,128)(2,1)S(1)} %fusion.57), channel_id=1, source_target_pairs={{0,4},{1,2},{2,1},{3,7},{4,0},{5,6},{6,5},{7,3},{8,12},{9,10},{10,... | collective-permute-start | bytes 1572872 | tf_op jit(solution)/shard_map/ppermute | solution.py:32
  172.9 14.4 %collective-permute-start.25 = (bf16[128,2048]{1,0:T(8,128)(2,1)S(1)}, bf16[128,2048]{1,0:T(8,128)(2,1)S(1)}, u32[]{:S(2)}, u32[]{:S(2)}) collective-permute-start(bf16[128,2048]{1,0:T(8,128)(2,1)S(1)} %get-tuple-element.16), channel_id=1, source_target_pairs={{0,8},{4,12},{8,0},{12,4},{16,24},{20,28},{24,16},{28,20},{1,9},{5... | collective-permute-start | bytes 1572872 | tf_op jit(solution)/shard_map/ppermute | solution.py:21
  174.7 14.6 %collective-permute-start.22 = (bf16[128,2048]{1,0:T(8,128)(2,1)S(1)}, bf16[128,2048]{1,0:T(8,128)(2,1)S(1)}, u32[]{:S(2)}, u32[]{:S(2)}) collective-permute-start(bf16[128,2048]{1,0:T(8,128)(2,1)S(1)} %get-tuple-element.15), channel_id=1, source_target_pairs={{0,16},{4,20},{8,24},{12,28},{16,0},{20,4},{24,8},{28,12},{1,17},{... | collective-permute-start | bytes 1572872 | tf_op jit(solution)/shard_map/ppermute | solution.py:21
  188.5 26.7 %collective-permute-start.26 = (bf16[256,2048]{1,0:T(8,128)(2,1)}, bf16[256,2048]{1,0:T(8,128)(2,1)}, u32[]{:S(2)}, u32[]{:S(2)}) collective-permute-start(bf16[256,2048]{1,0:T(8,128)(2,1)} %pad_maximum_fusion.1), channel_id=1, source_target_pairs={{0,16},{4,20},{8,24},{12,28},{16,0},{20,4},{24,8},{28,12},{1,17},{... | collective-permute-start | bytes 3145736 | tf_op jit(solution)/shard_map/ppermute | solution.py:21
  190.4 24.8 %collective-permute-start.23 = (bf16[256,2048]{1,0:T(8,128)(2,1)}, bf16[256,2048]{1,0:T(8,128)(2,1)}, u32[]{:S(2)}, u32[]{:S(2)}) collective-permute-start(bf16[256,2048]{1,0:T(8,128)(2,1)} %pad_maximum_fusion), channel_id=1, source_target_pairs={{0,8},{4,12},{8,0},{12,4},{16,24},{20,28},{24,16},{28,20},{1,9},{5... | collective-permute-start | bytes 3145736 | tf_op jit(solution)/shard_map/ppermute | solution.py:21
  193.3 18.0 %collective-permute-start.16 = (bf16[512,512]{1,0:T(8,128)(2,1)}, bf16[512,512]{1,0:T(8,128)(2,1)}, u32[]{:S(2)}, u32[]{:S(2)}) collective-permute-start(bf16[512,512]{1,0:T(8,128)(2,1)} %fusion.60), channel_id=1, source_target_pairs={{0,1},{1,0},{2,3},{3,2},{4,5},{5,4},{6,7},{7,6},{8,9},{9,8},{10,11... | collective-permute-start | bytes 1572872 | tf_op jit(solution)/shard_map/ppermute | solution.py:32

commit v4 on v3

v4 whole, which is shorter than its diff:
```python
import jax
import jax.numpy as jnp
from jax import lax
from jax.sharding import PartitionSpec as P

ITERS = 3


softcap = 15.0
sharpen = 2.0
f32 = jnp.float32
bf16 = jnp.bfloat16


def matmul(left, right, dims):
    return lax.dot_general(left, right, (dims, ((), ())), preferred_element_type=f32)


def flip(value, mask):
    size = lax.axis_size("sample")
    return lax.ppermute(value, "sample", [(i, i ^ mask) for i in range(size)])


def swap(value, parity):
    samples, size = lax.axis_size("sample"), lax.axis_size("cls")
    pairs = []
    for sample in range(samples):
        for i in range(size):
            j = ((i + parity) ^ 1) - parity
            there = sample * size + j if 0 <= j < size else (sample ^ 1) * size + i
            pairs.append((sample * size + i, there))
    return lax.ppermute(value, ("sample", "cls"), pairs)


def row_total(value):
    return jnp.sum(lax.all_gather(value, "cls", axis=0), axis=0)


def column_total(value):
    value = value + flip(value, 1)
    return sum([flip(value, mask) for mask in range(2, lax.axis_size("sample"), 2)], value)


def after(value, *others):
    return lax.optimization_barrier((value,) + others)[0]


def wide(value):
    return value.astype(f32)


def chip_axes(size):
    chips = size // 2
    bits = chips.bit_length() - 1
    low = 1 << ((bits + 1) // 2)
    first = [2 * m for m in range(1, low)]
    second = [2 * low * m for m in range(1, chips // low)]
    return first, second


def gather_head(head):
    size = lax.axis_size("sample")
    first, second = chip_axes(size)
    half = head.shape[0] // 2
    held = {mask: flip(head, mask) for mask in first + second}
    same = [(0, 0, head)] + [(mask, 0, block) for mask, block in held.items()]
    for a in first:
        for b in second:
            same.append((a | b, 0, flip(held[a][:half], b)))
            same.append((a | b, half, flip(held[b][half:], a)))
    return same + [(mask | 1, offset, flip(block, 1)) for mask, offset, block in same]


def cut(value):
    half = value.shape[0] // 2
    return value[:half], value[half:]


def gather_features(features):
    size = lax.axis_size("cls")
    me = lax.axis_index("cls")
    rows, width = features.shape
    pieces = []
    even = odd = cut(features)
    for hop in range(1, size):
        even, odd = [swap(part, 0) for part in odd], [swap(part, 1) for part in even]
        pieces.append((0, hop, even))
        if hop < size - 1 or size % 2:
            pieces.append((1, hop, odd))
    whole = jnp.zeros((size, rows, width), features.dtype)
    for parity, hop, parts in reversed(pieces):
        above, below = me + hop, me - hop
        above = jnp.where(above >= size, 2 * size - 1 - above, above)
        below = jnp.where(below < 0, -1 - below, below)
        source = jnp.where((me & 1) == parity, above, below)
        for i, part in enumerate(parts):
            whole = lax.dynamic_update_slice(whole, part[None], (source, i * (rows // 2), 0))
    return lax.dynamic_update_slice(whole, features[None], (me, 0, 0))


def per_device(features, head, class_cap):
    local_rows, width = features.shape
    depth, class_local = head.shape
    samples = lax.axis_size("sample")
    groups = lax.axis_size("cls")
    ratio = local_rows * samples / (class_local * groups)
    me = lax.axis_index("sample")
    place = lax.axis_index("cls")
    chip, core = me // 2, me & 1
    first, second = chip_axes(samples)
    half = depth // 2

    pieces = {(mask, offset): block for mask, offset, block in gather_head(head)}
    blocks = gather_features(features)

    def feature_columns(start, count):
        group = start // width
        return lax.dynamic_slice(blocks, (group, 0, start - group * width), (1, local_rows, count))[0]

    heads, logits = {}, None
    for mask in sorted({m for m, _ in pieces if m % 2 == 0}, key=lambda m: (bin(m).count("1"), m)):
        offsets = [offset for m, offset in pieces if m == mask]
        same = [pieces[mask, offset] for offset in offsets]
        other = [pieces[mask | 1, offset] for offset in offsets]
        parts = [jnp.where(core == 0, s, o) for s, o in zip(same, other)]
        parts += [jnp.where(core == 0, o, s) for s, o in zip(same, other)]
        heads[mask] = lax.optimization_barrier(jnp.concatenate(parts, axis=0))
        product = matmul(feature_columns((chip ^ (mask // 2)) * 2 * depth, 2 * depth), heads[mask], ((1,), (0,)))
        logits = product if logits is None else logits + product

    tanh = jnp.tanh(logits / softcap)
    student = jnp.exp(softcap * tanh)
    slope = (1.0 - tanh * tanh).astype(bf16)
    sums = jnp.stack([jnp.sum(student, axis=1), jnp.sum(student * student, axis=1)])
    student, slope, sums = lax.optimization_barrier((student, slope, sums))
    masses = row_total(sums)
    ceiling = class_cap.astype(f32) * ratio
    row_mass = masses[1]
    scale = jnp.ones((class_local,), f32)
    for iteration in range(ITERS):
        if iteration > 0:
            row_mass = row_total(jnp.sum(student * student * scale[None, :], axis=1))
        mass = column_total(jnp.sum(student * student * (1.0 / row_mass)[:, None], axis=0) * scale)
        scale = scale * jnp.minimum(1.0, ceiling / mass)
    row_mass = row_total(jnp.sum(student * student * scale[None, :], axis=1))
    targets = (student * student * scale[None, :] * (1.0 / row_mass)[:, None]).astype(bf16)
    grad = ((student * (1.0 / masses[0])[:, None] - wide(targets)) * wide(slope)).astype(bf16)

    def head_partial(mask, grad):
        return matmul(feature_columns((me ^ mask) * depth, depth), grad, ((0,), (0,))).astype(bf16)

    def both(mask, grad):
        theirs = head_partial(mask | 1, grad)
        mine = head_partial(mask, grad)
        return mine, flip(theirs, 1), (mine, theirs)

    stacked = jnp.stack([heads[mask] for mask in range(0, samples, 2)])

    def share(index, grad):
        start = jnp.clip(index, 0, groups - 1) * width
        group = start // (2 * depth)
        rows = lax.dynamic_slice(stacked, (group ^ chip, start - group * 2 * depth, 0), (1, width, class_local))[0]
        return matmul(grad, rows, ((1,), (1,))).astype(bf16)

    def line_share(hop, parity, grad):
        index = jnp.where((place & 1) == parity, groups - hop + place, place - (groups - hop))
        return share(index, grad)

    diagonal = {}
    for a in first:
        for b in second:
            mine, theirs, made = both(a | b, grad)
            grad = after(grad, *made)
            diagonal[a, b] = mine, theirs
    hops = [(hop, parity) for hop in range(1, groups) for parity in (0, 1)]
    hops = [(hop, parity) for hop, parity in hops if not (parity and hop == 1 and groups % 2 == 0)]
    shares = {at: line_share(*at, grad) for at in hops if at[0] == 1}
    sums = {at: (wide(mine) + wide(theirs)).astype(bf16) for at, (mine, theirs) in diagonal.items()}
    ready = lax.optimization_barrier(tuple(sums.values()) + tuple(shares.values()) + (grad,))
    grad = ready[-1]
    sums, shares = dict(zip(list(sums), ready)), dict(zip(list(shares), ready[len(sums):]))
    extra = {}
    for (a, b), block in sums.items():
        top, bottom = cut(block)
        extra.setdefault((b, 0), []).append(flip(top, a))
        extra.setdefault((a, 1), []).append(flip(bottom, b))

    mixed = {}
    for mask in first + second + [0]:
        mine, theirs, made = both(mask, grad)
        grad = after(grad, *made)
        mixed[mask] = mine, theirs
    rest = [at for at in hops if at[0] > 1]
    late = lax.optimization_barrier(tuple(line_share(*at, grad) for at in rest) + (share(place, grad),))
    own_share = late[-1]

    totals = {0: [], 1: []}
    waiting = []
    for mask in first + second:
        parts = cut(wide(mixed[mask][0]) + wide(mixed[mask][1]))
        for part in (0, 1):
            if (mask, part) in extra:
                waiting.append((mask, part, parts[part]))
            else:
                totals[part].append(flip(parts[part].astype(bf16), mask))
    own = cut(lax.optimization_barrier(wide(mixed[0][0]) + wide(mixed[0][1])))

    has_left, has_right = place > 0, place < groups - 1
    received = {0: None, 1: None}
    late = dict(zip(rest, late))
    for hop in range(1, groups):
        sent = {0: None, 1: None}
        for parity in (0, 1):
            if (hop, parity) not in hops:
                continue
            parts = cut(shares[hop, parity] if hop == 1 else late[hop, parity])
            if received[1 - parity] is not None:
                keep = jnp.where((place & 1) == parity, has_left, has_right)
                parts = [
                    (wide(part) + jnp.where(keep, wide(more), 0.0)).astype(bf16)
                    for part, more in zip(parts, received[1 - parity])
                ]
            sent[parity] = [swap(part, parity) for part in parts]
        received = sent
    totals_f = [wide(part) for part in cut(own_share)]
    for parity in (0, 1):
        if received[parity] is not None:
            keep = jnp.where((place & 1) == parity, has_right, has_left)
            totals_f = [t + jnp.where(keep, wide(more), 0.0) for t, more in zip(totals_f, received[parity])]
    grad_features = jnp.concatenate(totals_f, axis=0).astype(bf16)

    for mask, part, value in waiting:
        for more in extra[mask, part]:
            value = value + wide(more)
        totals[part].append(flip(value.astype(bf16), mask))
    halves = [sum([wide(t) for t in totals[part]], own[part]) for part in (0, 1)]
    grad_head = jnp.concatenate(halves, axis=0).astype(bf16)
    return (targets, grad_features, grad_head)


def solution(mesh):
    return jax.shard_map(
        per_device,
        mesh=mesh,
        in_specs=(P("sample", "cls"), P("sample", "cls"), P("cls")),
        out_specs=(P("sample", "cls"), P("sample", "cls"), P("sample", "cls")),
        check_vma=False,
    )
```

time: 220 us -> 275 us (1.25)
  waiting for transfers between devices: 71.3 us -> 106 us
  starting transfers between devices: 33.1 us -> 49.4 us
  local copies, waits for them, and re-layouts: 6.19 us -> 9.74 us
    all_gather x0 -> x4, blocking collectives: none -> 48.9 us  [row_total(): return jnp.sum(lax.all_gather(value, 'cls', axis=0), axis=0)]
    all_to_all x6 -> x0, blocking collectives: 47.5 us -> none  [total_over(): return jnp.sum(lax.all_to_all(copies, axis, 0, 0), axis=0)]
    ppermute x17 -> x31, waiting for transfers between devices: 19.6 us -> 57.5 us  [flip(): return lax.ppermute(value, 'sample', [(i, i ^ mask) for i in range(size)])]
    ppermute x17 -> x31, starting transfers between devices: 11.7 us -> 23.3 us  [flip(): return lax.ppermute(value, 'sample', [(i, i ^ mask) for i in range(size)])]
    ppermute x10 -> x20, starting transfers between devices: 18.2 us -> 26.1 us  [swap(): return lax.ppermute(value, ('sample', 'cls'), pairs)]
    all_to_all x1 -> x0, waiting for transfers between devices: 5.35 us -> none  [total_over(): return jnp.sum(lax.all_to_all(copies, axis, 0, 0), axis=0)]
    convert_element_type x2 -> x7, other arithmetic: 4.87 us -> 9.48 us  [the longest x1 5.43 us: per_device(): ((student * (1.0 / masses[0])[:, None] - wide(targets)) * wide(slope)).as...]
    reduce_sum x13 -> x10, other arithmetic: 18.6 us -> 14 us  [the longest x3 8.08 us: per_device(): jnp.sum(student * student * (1.0 / row_mass)[:, None], axis=0) * scale]
  transfers between devices with their start and end apart: 28 -> 51, of which waited for: 10 -> 31; matrix products, arithmetic and copies ran while one was open for 12% -> 7% of each run, Pallas kernels for 0% -> 0%
where the time goes in v4:
time: 275 us
  waiting for transfers between devices  106 us (39%)
  starting transfers between devices  49.4 us (18%)
  blocking collectives  48.9 us (18%)
  other arithmetic  30.1 us (11%)
  matrix products  28.7 us (10%)
  local copies, waits for them, and re-layouts  9.74 us (4%)
    ppermute x31, waiting for transfers between devices, flip(): return lax.ppermute(value, 'sample', [(i, i ^ mask) for i in range(size)])  57.5 us
    all_gather x4, blocking collectives, row_total(): return jnp.sum(lax.all_gather(value, 'cls', axis=0), axis=0)  48.9 us
    ppermute x20, waiting for transfers between devices, swap(): return lax.ppermute(value, ('sample', 'cls'), pairs)  48.6 us
    dot_general x18, matrix products, matmul(): lax.dot_general(left, right, (dims, ((), ())), preferred_element_type=f32)  28.7 us
    ppermute x20, starting transfers between devices, swap(): return lax.ppermute(value, ('sample', 'cls'), pairs)  26.1 us
    ppermute x31, starting transfers between devices, flip(): return lax.ppermute(value, 'sample', [(i, i ^ mask) for i in range(size)])  23.3 us
    reduce_sum x3, other arithmetic, per_device(): jnp.sum(student * student * (1.0 / row_mass)[:, None], axis=0) * scale  8.08 us
    reduce_sum x3, other arithmetic, per_device(): row_mass = row_total(jnp.sum(student * student * scale[None, :], axis=1))  5.87 us
  transfers between devices with their start and end apart: 51, of which 31 were waited for; matrix products, arithmetic and copies ran while one was open for 7% of the time, Pallas kernels for 0%

profile of v4, /device:TPU:0, one launch (start us, length us, event | category | flops | bytes accessed | tf_op | source)
XLA Modules:
  0.0 274.6 jit_solution(16290092312074053520)
XLA Ops:
  0.6 1.9 fusion.91
  2.5 3.0 %collective-permute-start = (bf16[256,512]{1,0:T(8,128)(2,1)}, bf16[256,512]{1,0:T(8,128)(2,1)S(1)}, u32[]{:S(2)}, u32[]{:S(2)}) collective-permute-start(bf16[256,512]{1,0:T(8,128)(2,1)} %get-tuple-element.66), channel_id=1, source_target_pairs={{0,1},{1,0},{2,3},{3,2},{4,5},{5,4},{6,7},{7,6},{8,9},{9,8},{10,11... | collective-permute-start | bytes 786440 | tf_op jit(solution)/shard_map/ppermute | solution.py:32
  5.5 7.3 %collective-permute-done = bf16[256,512]{1,0:T(8,128)(2,1)S(1)} collective-permute-done((bf16[256,512]{1,0:T(8,128)(2,1)}, bf16[256,512]{1,0:T(8,128)(2,1)S(1)}, u32[]{:S(2)}, u32[]{:S(2)}) %collective-permute-start) | collective-permute-done | bytes 262176 | tf_op jit(solution)/shard_map/ppermute | solution.py:32
  12.9 4.8 %collective-permute-done.3 = bf16[256,512]{1,0:T(8,128)(2,1)S(1)} collective-permute-done((bf16[256,512]{1,0:T(8,128)(2,1)}, bf16[256,512]{1,0:T(8,128)(2,1)S(1)}, u32[]{:S(2)}, u32[]{:S(2)}) %collective-permute-start.3) | collective-permute-done | bytes 262176 | tf_op jit(solution)/shard_map/ppermute | solution.py:32
  17.7 3.9 %collective-permute-start.2 = (bf16[256,512]{1,0:T(8,128)(2,1)S(1)}, bf16[256,512]{1,0:T(8,128)(2,1)S(1)}, u32[]{:S(2)}, u32[]{:S(2)}) collective-permute-start(bf16[256,512]{1,0:T(8,128)(2,1)S(1)} %collective-permute-done.1), channel_id=1, source_target_pairs={{0,1},{1,0},{2,3},{3,2},{4,5},{5,4},{6,7},{7,6},{8,9},{9,8},{10,11... | collective-permute-start | bytes 786440 | tf_op jit(solution)/shard_map/ppermute | solution.py:32
  22.1 6.7 %collective-permute-start.5 = (bf16[256,512]{1,0:T(8,128)(2,1)}, bf16[256,512]{1,0:T(8,128)(2,1)}, u32[]{:S(2)}, u32[]{:S(2)}) collective-permute-start(bf16[256,512]{1,0:T(8,128)(2,1)} %collective-permute-done.4), channel_id=1, source_target_pairs={{0,1},{1,0},{2,3},{3,2},{4,5},{5,4},{6,7},{7,6},{8,9},{9,8},{10,11... | collective-permute-start | bytes 786440 | tf_op jit(solution)/shard_map/ppermute | solution.py:32
  32.0 1.6 collective-permute-start.13
  33.5 4.7 %collective-permute-start.7 = (bf16[256,512]{1,0:T(8,128)(2,1)}, bf16[256,512]{1,0:T(8,128)(2,1)S(1)}, u32[]{:S(2)}, u32[]{:S(2)}) collective-permute-start(bf16[256,512]{1,0:T(8,128)(2,1)} %collective-permute-done.6), channel_id=1, source_target_pairs={{0,1},{1,0},{2,3},{3,2},{4,5},{5,4},{6,7},{7,6},{8,9},{9,8},{10,11... | collective-permute-start | bytes 786440 | tf_op jit(solution)/shard_map/ppermute | solution.py:32
  40.3 5.3 %collective-permute-done.7 = bf16[256,512]{1,0:T(8,128)(2,1)S(1)} collective-permute-done((bf16[256,512]{1,0:T(8,128)(2,1)}, bf16[256,512]{1,0:T(8,128)(2,1)S(1)}, u32[]{:S(2)}, u32[]{:S(2)}) %collective-permute-start.7) | collective-permute-done | bytes 262176 | tf_op jit(solution)/shard_map/ppermute | solution.py:32
  45.7 3.2 %collective-permute-done.9 = bf16[256,512]{1,0:T(8,128)(2,1)S(1)} collective-permute-done((bf16[256,512]{1,0:T(8,128)(2,1)}, bf16[256,512]{1,0:T(8,128)(2,1)S(1)}, u32[]{:S(2)}, u32[]{:S(2)}) %collective-permute-start.9) | collective-permute-done | bytes 262176 | tf_op jit(solution)/shard_map/ppermute | solution.py:32
  51.1 1.6 collective-permute-start.15
  52.7 5.3 %collective-permute-done.13 = bf16[256,2048]{1,0:T(8,128)(2,1)S(1)} collective-permute-done((bf16[256,2048]{1,0:T(8,128)(2,1)S(1)}, bf16[256,2048]{1,0:T(8,128)(2,1)S(1)}, u32[]{:S(2)}, u32[]{:S(2)}) %collective-permute-start.13) | collective-permute-done | bytes 1048608 | tf_op jit(solution)/shard_map/ppermute | solution.py:21
  61.0 7.9 %collective-permute-done.15 = bf16[128,2048]{1,0:T(8,128)(2,1)S(1)} collective-permute-done((bf16[128,2048]{1,0:T(8,128)(2,1)S(1)}, bf16[128,2048]{1,0:T(8,128)(2,1)S(1)}, u32[]{:S(2)}, u32[]{:S(2)}) %collective-permute-start.15) | collective-permute-done | bytes 524320 | tf_op jit(solution)/shard_map/ppermute | solution.py:21
  68.8 2.4 collective-permute-done.17
  76.0 4.5 %fusion.87 = (f32[512]{0:T(512)S(1)}, f32[512]{0:T(512)S(1)}, bf16[512,2048]{1,0:T(8,128)(2,1)}, f32[512,2048]{1,0:T(8,128)}) fusion(bf16[512,2048]{1,0:T(8,128)(2,1)S(1)} %pad_maximum_fusion.4, bf16[4,512,512]{2,1,0:T(8,128)(2,1)S(1)} %bitcast_dynamic-update-slice_fusion, s32[]{:T(128)S(6)} %select_n.366, f32[512,2048]{1,0:T(8,128)S(1)} %fusion.43, ...), kind=kOutput, calls=%fused_computation.151 | convolution fusion | flops 1085275136 | bytes 21499908 | tf_op jit(solution)/shard_map/dot_general | solution.py:16
  80.6 13.1 %all-gather.4 = f32[4,2,512]{2,1,0:T(2,128)S(1)} all-gather(f32[1,2,512]{2,1,0:T(2,128)S(1)} %bitcast.124), channel_id=2, replica_groups=mesh['sample'=8,'cls'=4] {'cls'}, dimensions={0}, use_global_device_ids=true | all-gather | bytes 20480 | tf_op jit(solution)/shard_map/all_gather | solution.py:36
  93.8 2.8 %multiply_reduce_fusion.4 = f32[2048]{0:T(1024)S(1)} fusion(f32[512,2048]{1,0:T(8,128)} %get-tuple-element.18, f32[512]{0:T(512)S(1)} %bitcast.130), kind=kLoop, calls=%fused_computation.7 | loop fusion | flops 3143680 | bytes 4204544 | tf_op jit(solution)/shard_map/reduce_sum | solution.py:143
  102.0 2.4 collective-permute-done.22
  104.9 11.9 %all-gather.5 = f32[4,1,512]{2,1,0:T(1,128)S(1)} all-gather(f32[1,1,512]{2,1,0:T(1,128)S(1)} %bitcast.125), channel_id=3, replica_groups=mesh['sample'=8,'cls'=4] {'cls'}, dimensions={0}, use_global_device_ids=true | all-gather | bytes 10240 | tf_op jit(solution)/shard_map/all_gather | solution.py:36
  116.9 2.6 multiply_reduce_fusion.2
  127.3 2.7 multiply_reduce_fusion.1
  130.0 12.1 %all-gather.6 = f32[4,1,512]{2,1,0:T(1,128)S(1)} all-gather(f32[1,1,512]{2,1,0:T(1,128)S(1)} %bitcast.126), channel_id=4, replica_groups=mesh['sample'=8,'cls'=4] {'cls'}, dimensions={0}, use_global_device_ids=true | all-gather | bytes 10240 | tf_op jit(solution)/shard_map/all_gather | solution.py:36
  142.1 2.6 multiply_reduce_fusion
  150.2 2.4 collective-permute-done.30
  152.6 2.7 multiply_reduce_fusion.6
  155.3 11.9 %all-gather.7 = f32[4,1,512]{2,1,0:T(1,128)S(1)} all-gather(f32[1,1,512]{2,1,0:T(1,128)S(1)} %bitcast.127), channel_id=5, replica_groups=mesh['sample'=8,'cls'=4] {'cls'}, dimensions={0}, use_global_device_ids=true | all-gather | bytes 10240 | tf_op jit(solution)/shard_map/all_gather | solution.py:36
  167.2 5.4 %multiply_convert_fusion = (bf16[512,2048]{1,0:T(8,128)(2,1)S(1)}, bf16[512,2048]{1,0:T(8,128)(2,1)}) fusion(bf16[512,2048]{1,0:T(8,128)(2,1)} %get-tuple-element.20, f32[512,2048]{1,0:T(8,128)} %get-tuple-element.18, f32[512]{0:T(512)S(1)} %bitcast.131, f32[512]{0:T(512)S(1)} %broadcast_divide_fusion, f32[2048]{0:T(1024)S(1)} %minimum_multiply_fusion), kind=kLoop, calls=%fused_computation.1 | loop fusion | flops 10485760 | bytes 10498048 | tf_op jit(solution)/shard_map/convert_element_type | solution.py:147
  177.8 1.7 convolution_convert_fusion.4
  179.5 1.8 convolution_convert_fusion.5
  181.3 1.7 convolution_convert_fusion.2
  183.0 1.7 convolution_convert_fusion.3
  184.7 1.7 convolution_convert_fusion
  186.4 1.7 convolution_convert_fusion.1
  188.2 2.1 fusion.33
  194.2 2.0 collective-permute-start.37
  198.5 1.9 collective-permute-start.40
  200.4 3.0 %collective-permute-done.32 = bf16[256,512]{1,0:T(8,128)(2,1)S(1)} collective-permute-done((bf16[256,512]{1,0:T(8,128)(2,1)S(1)}, bf16[256,512]{1,0:T(8,128)(2,1)S(1)}, u32[]{:S(2)}, u32[]{:S(2)}) %collective-permute-start.32) | collective-permute-done | bytes 262176 | tf_op jit(solution)/shard_map/ppermute | solution.py:32
  203.4 5.6 %collective-permute-done.37 = bf16[256,512]{1,0:T(8,128)(2,1)S(1)} collective-permute-done((bf16[256,512]{1,0:T(8,128)(2,1)S(1)}, bf16[256,512]{1,0:T(8,128)(2,1)S(1)}, u32[]{:S(2)}, u32[]{:S(2)}) %collective-permute-start.37) | collective-permute-done | bytes 262176 | tf_op jit(solution)/shard_map/ppermute | solution.py:32
  210.5 4.1 %collective-permute-done.35 = bf16[256,512]{1,0:T(8,128)(2,1)S(1)} collective-permute-done((bf16[256,512]{1,0:T(8,128)(2,1)}, bf16[256,512]{1,0:T(8,128)(2,1)S(1)}, u32[]{:S(2)}, u32[]{:S(2)}) %collective-permute-start.35) | collective-permute-done | bytes 262176 | tf_op jit(solution)/shard_map/ppermute | solution.py:32
  214.7 4.5 %collective-permute-done.40 = bf16[256,512]{1,0:T(8,128)(2,1)} collective-permute-done((bf16[256,512]{1,0:T(8,128)(2,1)}, bf16[256,512]{1,0:T(8,128)(2,1)}, u32[]{:S(2)}, u32[]{:S(2)}) %collective-permute-start.40) | collective-permute-done | bytes 262176 | tf_op jit(solution)/shard_map/ppermute | solution.py:32
  222.2 1.7 collective-permute-start.34
  225.0 6.4 %collective-permute-done.34 = bf16[256,512]{1,0:T(8,128)(2,1)S(1)} collective-permute-done((bf16[256,512]{1,0:T(8,128)(2,1)S(1)}, bf16[256,512]{1,0:T(8,128)(2,1)S(1)}, u32[]{:S(2)}, u32[]{:S(2)}) %collective-permute-start.34) | collective-permute-done | bytes 262176 | tf_op jit(solution)/shard_map/ppermute | solution.py:32
  232.0 4.3 %collective-permute-done.39 = bf16[256,512]{1,0:T(8,128)(2,1)S(1)} collective-permute-done((bf16[256,512]{1,0:T(8,128)(2,1)S(1)}, bf16[256,512]{1,0:T(8,128)(2,1)S(1)}, u32[]{:S(2)}, u32[]{:S(2)}) %collective-permute-start.39) | collective-permute-done | bytes 262176 | tf_op jit(solution)/shard_map/ppermute | solution.py:32
  239.3 4.5 %collective-permute-done.49 = bf16[128,2048]{1,0:T(8,128)(2,1)S(1)} collective-permute-done((bf16[128,2048]{1,0:T(8,128)(2,1)S(1)}, bf16[128,2048]{1,0:T(8,128)(2,1)S(1)}, u32[]{:S(2)}, u32[]{:S(2)}) %collective-permute-start.49) | collective-permute-done | bytes 524320 | tf_op jit(solution)/shard_map/ppermute | solution.py:21
  243.9 1.6 collective-permute-start.50
  246.4 4.7 %collective-permute-done.46 = bf16[128,2048]{1,0:T(8,128)(2,1)S(1)} collective-permute-done((bf16[128,2048]{1,0:T(8,128)(2,1)S(1)}, bf16[128,2048]{1,0:T(8,128)(2,1)S(1)}, u32[]{:S(2)}, u32[]{:S(2)}) %collective-permute-start.46) | collective-permute-done | bytes 524320 | tf_op jit(solution)/shard_map/ppermute | solution.py:21
  253.7 8.6 %collective-permute-done.50 = bf16[128,2048]{1,0:T(8,128)(2,1)S(1)} collective-permute-done((bf16[128,2048]{1,0:T(8,128)(2,1)S(1)}, bf16[128,2048]{1,0:T(8,128)(2,1)S(1)}, u32[]{:S(2)}, u32[]{:S(2)}) %collective-permute-start.50) | collective-permute-done | bytes 524320 | tf_op jit(solution)/shard_map/ppermute | solution.py:21
  262.4 9.5 %collective-permute-done.44 = bf16[128,2048]{1,0:T(8,128)(2,1)S(1)} collective-permute-done((bf16[128,2048]{1,0:T(8,128)(2,1)S(1)}, bf16[128,2048]{1,0:T(8,128)(2,1)S(1)}, u32[]{:S(2)}, u32[]{:S(2)}) %collective-permute-start.44) | collective-permute-done | bytes 524320 | tf_op jit(solution)/shard_map/ppermute | solution.py:21
  (193 shorter events, 61.3 us)
Async XLA Ops:
  2.5 10.4 %collective-permute-start = (bf16[256,512]{1,0:T(8,128)(2,1)}, bf16[256,512]{1,0:T(8,128)(2,1)S(1)}, u32[]{:S(2)}, u32[]{:S(2)}) collective-permute-start(bf16[256,512]{1,0:T(8,128)(2,1)} %get-tuple-element.66), channel_id=1, source_target_pairs={{0,1},{1,0},{2,3},{3,2},{4,5},{5,4},{6,7},{7,6},{8,9},{9,8},{10,11... | collective-permute-start | bytes 786440 | tf_op jit(solution)/shard_map/ppermute | solution.py:32
  5.5 12.1 %collective-permute-start.3 = (bf16[256,512]{1,0:T(8,128)(2,1)}, bf16[256,512]{1,0:T(8,128)(2,1)S(1)}, u32[]{:S(2)}, u32[]{:S(2)}) collective-permute-start(bf16[256,512]{1,0:T(8,128)(2,1)} %get-tuple-element.65), channel_id=1, source_target_pairs={{0,1},{1,0},{2,3},{3,2},{4,5},{5,4},{6,7},{7,6},{8,9},{9,8},{10,11... | collective-permute-start | bytes 786440 | tf_op jit(solution)/shard_map/ppermute | solution.py:32
  12.8 4.8 %collective-permute-start.1 = (bf16[256,512]{1,0:T(8,128)(2,1)S(1)}, bf16[256,512]{1,0:T(8,128)(2,1)S(1)}, u32[]{:S(2)}, u32[]{:S(2)}) collective-permute-start(bf16[256,512]{1,0:T(8,128)(2,1)S(1)} %collective-permute-done), channel_id=1, source_target_pairs={{0,4},{1,2},{2,1},{3,7},{4,0},{5,6},{6,5},{7,3},{8,12},{9,10},{10,... | collective-permute-start | bytes 786440 | tf_op jit(solution)/shard_map/ppermute | solution.py:32
  17.6 4.4 %collective-permute-start.4 = (bf16[256,512]{1,0:T(8,128)(2,1)S(1)}, bf16[256,512]{1,0:T(8,128)(2,1)}, u32[]{:S(2)}, u32[]{:S(2)}) collective-permute-start(bf16[256,512]{1,0:T(8,128)(2,1)S(1)} %collective-permute-done.3), channel_id=1, source_target_pairs={{0,4},{1,2},{2,1},{3,7},{4,0},{5,6},{6,5},{7,3},{8,12},{9,10},{10,... | collective-permute-start | bytes 786440 | tf_op jit(solution)/shard_map/ppermute | solution.py:32
  17.7 12.6 %collective-permute-start.2 = (bf16[256,512]{1,0:T(8,128)(2,1)S(1)}, bf16[256,512]{1,0:T(8,128)(2,1)S(1)}, u32[]{:S(2)}, u32[]{:S(2)}) collective-permute-start(bf16[256,512]{1,0:T(8,128)(2,1)S(1)} %collective-permute-done.1), channel_id=1, source_target_pairs={{0,1},{1,0},{2,3},{3,2},{4,5},{5,4},{6,7},{7,6},{8,9},{9,8},{10,11... | collective-permute-start | bytes 786440 | tf_op jit(solution)/shard_map/ppermute | solution.py:32
  21.6 10.4 %collective-permute-start.6 = (bf16[256,512]{1,0:T(8,128)(2,1)}, bf16[256,512]{1,0:T(8,128)(2,1)}, u32[]{:S(2)}, u32[]{:S(2)}) collective-permute-start(bf16[256,512]{1,0:T(8,128)(2,1)} %get-tuple-element.66), channel_id=1, source_target_pairs={{0,4},{1,2},{2,1},{3,7},{4,0},{5,6},{6,5},{7,3},{8,12},{9,10},{10,... | collective-permute-start | bytes 786440 | tf_op jit(solution)/shard_map/ppermute | solution.py:32
  21.6 12.0 %collective-permute-start.8 = (bf16[256,512]{1,0:T(8,128)(2,1)}, bf16[256,512]{1,0:T(8,128)(2,1)}, u32[]{:S(2)}, u32[]{:S(2)}) collective-permute-start(bf16[256,512]{1,0:T(8,128)(2,1)} %get-tuple-element.65), channel_id=1, source_target_pairs={{0,4},{1,2},{2,1},{3,7},{4,0},{5,6},{6,5},{7,3},{8,12},{9,10},{10,... | collective-permute-start | bytes 786440 | tf_op jit(solution)/shard_map/ppermute | solution.py:32
  22.1 16.2 %collective-permute-start.5 = (bf16[256,512]{1,0:T(8,128)(2,1)}, bf16[256,512]{1,0:T(8,128)(2,1)}, u32[]{:S(2)}, u32[]{:S(2)}) collective-permute-start(bf16[256,512]{1,0:T(8,128)(2,1)} %collective-permute-done.4), channel_id=1, source_target_pairs={{0,1},{1,0},{2,3},{3,2},{4,5},{5,4},{6,7},{7,6},{8,9},{9,8},{10,11... | collective-permute-start | bytes 786440 | tf_op jit(solution)/shard_map/ppermute | solution.py:32
  28.7 22.3 %collective-permute-start.11 = (bf16[256,2048]{1,0:T(8,128)(2,1)}, bf16[256,2048]{1,0:T(8,128)(2,1)S(1)}, u32[]{:S(2)}, u32[]{:S(2)}) collective-permute-start(bf16[256,2048]{1,0:T(8,128)(2,1)} %param.4), channel_id=1, source_target_pairs={{0,8},{4,12},{8,0},{12,4},{16,24},{20,28},{24,16},{28,20},{1,9},{5... | collective-permute-start | bytes 3145736 | tf_op jit(solution)/shard_map/ppermute | solution.py:21
  30.9 28.2 %collective-permute-start.10 = (bf16[256,2048]{1,0:T(8,128)(2,1)}, bf16[256,2048]{1,0:T(8,128)(2,1)S(1)}, u32[]{:S(2)}, u32[]{:S(2)}) collective-permute-start(bf16[256,2048]{1,0:T(8,128)(2,1)} %param.4), channel_id=1, source_target_pairs={{0,4},{4,0},{8,12},{12,8},{16,20},{20,16},{24,28},{28,24},{1,5},{5... | collective-permute-start | bytes 3145736 | tf_op jit(solution)/shard_map/ppermute | solution.py:21
  32.0 26.0 %collective-permute-start.13 = (bf16[256,2048]{1,0:T(8,128)(2,1)S(1)}, bf16[256,2048]{1,0:T(8,128)(2,1)S(1)}, u32[]{:S(2)}, u32[]{:S(2)}) collective-permute-start(bf16[256,2048]{1,0:T(8,128)(2,1)S(1)} %copy-done.13), channel_id=1, source_target_pairs={{0,16},{4,20},{8,24},{12,28},{16,0},{20,4},{24,8},{28,12},{1,17},{... | collective-permute-start | bytes 3145736 | tf_op jit(solution)/shard_map/ppermute | solution.py:21
  33.5 12.1 %collective-permute-start.7 = (bf16[256,512]{1,0:T(8,128)(2,1)}, bf16[256,512]{1,0:T(8,128)(2,1)S(1)}, u32[]{:S(2)}, u32[]{:S(2)}) collective-permute-start(bf16[256,512]{1,0:T(8,128)(2,1)} %collective-permute-done.6), channel_id=1, source_target_pairs={{0,1},{1,0},{2,3},{3,2},{4,5},{5,4},{6,7},{7,6},{8,9},{9,8},{10,11... | collective-permute-start | bytes 786440 | tf_op jit(solution)/shard_map/ppermute | solution.py:32
  38.2 10.7 %collective-permute-start.9 = (bf16[256,512]{1,0:T(8,128)(2,1)}, bf16[256,512]{1,0:T(8,128)(2,1)S(1)}, u32[]{:S(2)}, u32[]{:S(2)}) collective-permute-start(bf16[256,512]{1,0:T(8,128)(2,1)} %collective-permute-done.8), channel_id=1, source_target_pairs={{0,1},{1,0},{2,3},{3,2},{4,5},{5,4},{6,7},{7,6},{8,9},{9,8},{10,11... | collective-permute-start | bytes 786440 | tf_op jit(solution)/shard_map/ppermute | solution.py:32
  51.1 17.7 %collective-permute-start.15 = (bf16[128,2048]{1,0:T(8,128)(2,1)S(1)}, bf16[128,2048]{1,0:T(8,128)(2,1)S(1)}, u32[]{:S(2)}, u32[]{:S(2)}) collective-permute-start(bf16[128,2048]{1,0:T(8,128)(2,1)S(1)} %slice.106), channel_id=1, source_target_pairs={{0,16},{4,20},{8,24},{12,28},{16,0},{20,4},{24,8},{28,12},{1,17},{... | collective-permute-start | bytes 1572872 | tf_op jit(solution)/shard_map/ppermute | solution.py:21
  58.0 13.2 %collective-permute-start.17 = (bf16[128,2048]{1,0:T(8,128)(2,1)S(1)}, bf16[128,2048]{1,0:T(8,128)(2,1)S(1)}, u32[]{:S(2)}, u32[]{:S(2)}) collective-permute-start(bf16[128,2048]{1,0:T(8,128)(2,1)S(1)} %slice.107), channel_id=1, source_target_pairs={{0,8},{4,12},{8,0},{12,4},{16,24},{20,28},{24,16},{28,20},{1,9},{5... | collective-permute-start | bytes 1572872 | tf_op jit(solution)/shard_map/ppermute | solution.py:21
  58.6 12.6 %collective-permute-start.12 = (bf16[256,2048]{1,0:T(8,128)(2,1)S(1)}, bf16[256,2048]{1,0:T(8,128)(2,1)S(1)}, u32[]{:S(2)}, u32[]{:S(2)}) collective-permute-start(bf16[256,2048]{1,0:T(8,128)(2,1)S(1)} %collective-permute-done.11), channel_id=1, source_target_pairs={{0,4},{4,0},{8,12},{12,8},{16,20},{20,16},{24,28},{28,24},{1,5},{5... | collective-permute-start | bytes 3145736 | tf_op jit(solution)/shard_map/ppermute | solution.py:21
  58.6 12.8 %collective-permute-start.14 = (bf16[256,2048]{1,0:T(8,128)(2,1)S(1)}, bf16[256,2048]{1,0:T(8,128)(2,1)S(1)}, u32[]{:S(2)}, u32[]{:S(2)}) collective-permute-start(bf16[256,2048]{1,0:T(8,128)(2,1)S(1)} %collective-permute-done.13), channel_id=1, source_target_pairs={{0,4},{4,0},{8,12},{12,8},{16,20},{20,16},{24,28},{28,24},{1,5},{5... | collective-permute-start | bytes 3145736 | tf_op jit(solution)/shard_map/ppermute | solution.py:21
  68.8 3.4 %collective-permute-start.16 = (bf16[128,2048]{1,0:T(8,128)(2,1)S(1)}, bf16[128,2048]{1,0:T(8,128)(2,1)S(1)}, u32[]{:S(2)}, u32[]{:S(2)}) collective-permute-start(bf16[128,2048]{1,0:T(8,128)(2,1)S(1)} %collective-permute-done.15), channel_id=1, source_target_pairs={{0,4},{4,0},{8,12},{12,8},{16,20},{20,16},{24,28},{28,24},{1,5},{5... | collective-permute-start | bytes 1572872 | tf_op jit(solution)/shard_map/ppermute | solution.py:21
  71.3 1.9 collective-permute-start.18
  97.8 3.7 %collective-permute-start.20 = (f32[2048]{0:T(1024)S(1)}, f32[2048]{0:T(1024)S(1)}, u32[]{:S(2)}, u32[]{:S(2)}) collective-permute-start(f32[2048]{0:T(1024)S(1)} %add.270), channel_id=1, source_target_pairs={{0,8},{4,12},{8,0},{12,4},{16,24},{20,28},{24,16},{28,20},{1,9},{5... | collective-permute-start | bytes 24584 | tf_op jit(solution)/shard_map/ppermute | solution.py:21
  98.4 3.7 %collective-permute-start.21 = (f32[2048]{0:T(1024)S(1)}, f32[2048]{0:T(1024)S(1)}, u32[]{:S(2)}, u32[]{:S(2)}) collective-permute-start(f32[2048]{0:T(1024)S(1)} %add.270), channel_id=1, source_target_pairs={{0,16},{4,20},{8,24},{12,28},{16,0},{20,4},{24,8},{28,12},{1,17},{... | collective-permute-start | bytes 24584 | tf_op jit(solution)/shard_map/ppermute | solution.py:21
  99.9 4.5 %collective-permute-start.22 = (f32[2048]{0:T(1024)S(1)}, f32[2048]{0:T(1024)S(1)}, u32[]{:S(2)}, u32[]{:S(2)}) collective-permute-start(f32[2048]{0:T(1024)S(1)} %add.270), channel_id=1, source_target_pairs={{0,24},{4,28},{8,16},{12,20},{16,8},{20,12},{24,0},{28,4},{1,25},{... | collective-permute-start | bytes 24584 | tf_op jit(solution)/shard_map/ppermute | solution.py:21
  120.8 3.7 %collective-permute-start.24 = (f32[2048]{0:T(1024)S(1)}, f32[2048]{0:T(1024)S(1)}, u32[]{:S(2)}, u32[]{:S(2)}) collective-permute-start(f32[2048]{0:T(1024)S(1)} %add.274), channel_id=1, source_target_pairs={{0,8},{4,12},{8,0},{12,4},{16,24},{20,28},{24,16},{28,20},{1,9},{5... | collective-permute-start | bytes 24584 | tf_op jit(solution)/shard_map/ppermute | solution.py:21
  122.2 3.7 %collective-permute-start.25 = (f32[2048]{0:T(1024)S(1)}, f32[2048]{0:T(1024)S(1)}, u32[]{:S(2)}, u32[]{:S(2)}) collective-permute-start(f32[2048]{0:T(1024)S(1)} %add.274), channel_id=1, source_target_pairs={{0,16},{4,20},{8,24},{12,28},{16,0},{20,4},{24,8},{28,12},{1,17},{... | collective-permute-start | bytes 24584 | tf_op jit(solution)/shard_map/ppermute | solution.py:21
  122.8 4.5 %collective-permute-start.26 = (f32[2048]{0:T(1024)S(1)}, f32[2048]{0:T(1024)S(1)}, u32[]{:S(2)}, u32[]{:S(2)}) collective-permute-start(f32[2048]{0:T(1024)S(1)} %add.274), channel_id=1, source_target_pairs={{0,24},{4,28},{8,16},{12,20},{16,8},{20,12},{24,0},{28,4},{1,25},{... | collective-permute-start | bytes 24584 | tf_op jit(solution)/shard_map/ppermute | solution.py:21
  146.0 3.7 %collective-permute-start.28 = (f32[2048]{0:T(1024)S(1)}, f32[2048]{0:T(1024)S(1)}, u32[]{:S(2)}, u32[]{:S(2)}) collective-permute-start(f32[2048]{0:T(1024)S(1)} %add.278), channel_id=1, source_target_pairs={{0,8},{4,12},{8,0},{12,4},{16,24},{20,28},{24,16},{28,20},{1,9},{5... | collective-permute-start | bytes 24584 | tf_op jit(solution)/shard_map/ppermute | solution.py:21
  146.5 3.7 %collective-permute-start.29 = (f32[2048]{0:T(1024)S(1)}, f32[2048]{0:T(1024)S(1)}, u32[]{:S(2)}, u32[]{:S(2)}) collective-permute-start(f32[2048]{0:T(1024)S(1)} %add.278), channel_id=1, source_target_pairs={{0,16},{4,20},{8,24},{12,28},{16,0},{20,4},{24,8},{28,12},{1,17},{... | collective-permute-start | bytes 24584 | tf_op jit(solution)/shard_map/ppermute | solution.py:21
  148.0 4.5 %collective-permute-start.30 = (f32[2048]{0:T(1024)S(1)}, f32[2048]{0:T(1024)S(1)}, u32[]{:S(2)}, u32[]{:S(2)}) collective-permute-start(f32[2048]{0:T(1024)S(1)} %add.278), channel_id=1, source_target_pairs={{0,24},{4,28},{8,16},{12,20},{16,8},{20,12},{24,0},{28,4},{1,25},{... | collective-permute-start | bytes 24584 | tf_op jit(solution)/shard_map/ppermute | solution.py:21
  173.4 4.0 %collective-permute-start.31 = (bf16[256,2048]{1,0:T(8,128)(2,1)S(1)}, bf16[256,2048]{1,0:T(8,128)(2,1)S(1)}, u32[]{:S(2)}, u32[]{:S(2)}) collective-permute-start(bf16[256,2048]{1,0:T(8,128)(2,1)S(1)} %convolution_convert_fusion.6), channel_id=1, source_target_pairs={{0,4},{4,0},{8,12},{12,8},{16,20},{20,16},{24,28},{28,24},{1,5},{5... | collective-permute-start | bytes 3145736 | tf_op jit(solution)/shard_map/ppermute | solution.py:21
  194.2 9.3 %collective-permute-start.32 = (bf16[256,512]{1,0:T(8,128)(2,1)S(1)}, bf16[256,512]{1,0:T(8,128)(2,1)S(1)}, u32[]{:S(2)}, u32[]{:S(2)}) collective-permute-start(bf16[256,512]{1,0:T(8,128)(2,1)S(1)} %get-tuple-element.59), channel_id=1, source_target_pairs={{0,1},{1,0},{2,3},{3,2},{4,5},{5,4},{6,7},{7,6},{8,9},{9,8},{10,11... | collective-permute-start | bytes 786440 | tf_op jit(solution)/shard_map/ppermute | solution.py:32
  194.2 14.8 %collective-permute-start.37 = (bf16[256,512]{1,0:T(8,128)(2,1)S(1)}, bf16[256,512]{1,0:T(8,128)(2,1)S(1)}, u32[]{:S(2)}, u32[]{:S(2)}) collective-permute-start(bf16[256,512]{1,0:T(8,128)(2,1)S(1)} %get-tuple-element.60), channel_id=1, source_target_pairs={{0,1},{1,0},{2,3},{3,2},{4,5},{5,4},{6,7},{7,6},{8,9},{9,8},{10,11... | collective-permute-start | bytes 786440 | tf_op jit(solution)/shard_map/ppermute | solution.py:32
  198.4 16.3 %collective-permute-start.35 = (bf16[256,512]{1,0:T(8,128)(2,1)}, bf16[256,512]{1,0:T(8,128)(2,1)S(1)}, u32[]{:S(2)}, u32[]{:S(2)}) collective-permute-start(bf16[256,512]{1,0:T(8,128)(2,1)} %get-tuple-element.63), channel_id=1, source_target_pairs={{0,1},{1,0},{2,3},{3,2},{4,5},{5,4},{6,7},{7,6},{8,9},{9,8},{10,11... | collective-permute-start | bytes 786440 | tf_op jit(solution)/shard_map/ppermute | solution.py:32
  198.5 20.7 %collective-permute-start.40 = (bf16[256,512]{1,0:T(8,128)(2,1)}, bf16[256,512]{1,0:T(8,128)(2,1)}, u32[]{:S(2)}, u32[]{:S(2)}) collective-permute-start(bf16[256,512]{1,0:T(8,128)(2,1)} %get-tuple-element.64), channel_id=1, source_target_pairs={{0,1},{1,0},{2,3},{3,2},{4,5},{5,4},{6,7},{7,6},{8,9},{9,8},{10,11... | collective-permute-start | bytes 786440 | tf_op jit(solution)/shard_map/ppermute | solution.py:32
  210.0 10.9 %collective-permute-start.33 = (bf16[256,512]{1,0:T(8,128)(2,1)}, bf16[256,512]{1,0:T(8,128)(2,1)}, u32[]{:S(2)}, u32[]{:S(2)}) collective-permute-start(bf16[256,512]{1,0:T(8,128)(2,1)} %get-tuple-element.57), channel_id=1, source_target_pairs={{0,4},{1,2},{2,1},{3,7},{4,0},{5,6},{6,5},{7,3},{8,12},{9,10},{10,... | collective-permute-start | bytes 786440 | tf_op jit(solution)/shard_map/ppermute | solution.py:32
  210.0 10.9 %collective-permute-start.38 = (bf16[256,512]{1,0:T(8,128)(2,1)}, bf16[256,512]{1,0:T(8,128)(2,1)}, u32[]{:S(2)}, u32[]{:S(2)}) collective-permute-start(bf16[256,512]{1,0:T(8,128)(2,1)} %get-tuple-element.58), channel_id=1, source_target_pairs={{0,4},{1,2},{2,1},{3,7},{4,0},{5,6},{6,5},{7,3},{8,12},{9,10},{10,... | collective-permute-start | bytes 786440 | tf_op jit(solution)/shard_map/ppermute | solution.py:32
  210.5 28.3 %collective-permute-start.43 = (bf16[256,2048]{1,0:T(8,128)(2,1)S(1)}, bf16[256,2048]{1,0:T(8,128)(2,1)S(1)}, u32[]{:S(2)}, u32[]{:S(2)}) collective-permute-start(bf16[256,2048]{1,0:T(8,128)(2,1)S(1)} %copy-done.16), channel_id=1, source_target_pairs={{0,4},{4,0},{8,12},{12,8},{16,20},{20,16},{24,28},{28,24},{1,5},{5... | collective-permute-start | bytes 3145736 | tf_op jit(solution)/shard_map/ppermute | solution.py:21
  220.3 4.2 %collective-permute-start.36 = (bf16[256,512]{1,0:T(8,128)(2,1)S(1)}, bf16[256,512]{1,0:T(8,128)(2,1)S(1)}, u32[]{:S(2)}, u32[]{:S(2)}) collective-permute-start(bf16[256,512]{1,0:T(8,128)(2,1)S(1)} %get-tuple-element.61), channel_id=1, source_target_pairs={{0,4},{1,2},{2,1},{3,7},{4,0},{5,6},{6,5},{7,3},{8,12},{9,10},{10,... | collective-permute-start | bytes 786440 | tf_op jit(solution)/shard_map/ppermute | solution.py:32
  220.4 4.2 %collective-permute-start.41 = (bf16[256,512]{1,0:T(8,128)(2,1)S(1)}, bf16[256,512]{1,0:T(8,128)(2,1)S(1)}, u32[]{:S(2)}, u32[]{:S(2)}) collective-permute-start(bf16[256,512]{1,0:T(8,128)(2,1)S(1)} %get-tuple-element.62), channel_id=1, source_target_pairs={{0,4},{1,2},{2,1},{3,7},{4,0},{5,6},{6,5},{7,3},{8,12},{9,10},{10,... | collective-permute-start | bytes 786440 | tf_op jit(solution)/shard_map/ppermute | solution.py:32
  222.2 9.2 %collective-permute-start.34 = (bf16[256,512]{1,0:T(8,128)(2,1)S(1)}, bf16[256,512]{1,0:T(8,128)(2,1)S(1)}, u32[]{:S(2)}, u32[]{:S(2)}) collective-permute-start(bf16[256,512]{1,0:T(8,128)(2,1)S(1)} %get-tuple-element.55), channel_id=1, source_target_pairs={{0,1},{1,0},{2,3},{3,2},{4,5},{5,4},{6,7},{7,6},{8,9},{9,8},{10,11... | collective-permute-start | bytes 786440 | tf_op jit(solution)/shard_map/ppermute | solution.py:32
  223.9 12.3 %collective-permute-start.39 = (bf16[256,512]{1,0:T(8,128)(2,1)S(1)}, bf16[256,512]{1,0:T(8,128)(2,1)S(1)}, u32[]{:S(2)}, u32[]{:S(2)}) collective-permute-start(bf16[256,512]{1,0:T(8,128)(2,1)S(1)} %get-tuple-element.56), channel_id=1, source_target_pairs={{0,1},{1,0},{2,3},{3,2},{4,5},{5,4},{6,7},{7,6},{8,9},{9,8},{10,11... | collective-permute-start | bytes 786440 | tf_op jit(solution)/shard_map/ppermute | solution.py:32
  224.5 21.5 %collective-permute-start.45 = (bf16[256,2048]{1,0:T(8,128)(2,1)S(1)}, bf16[256,2048]{1,0:T(8,128)(2,1)S(1)}, u32[]{:S(2)}, u32[]{:S(2)}) collective-permute-start(bf16[256,2048]{1,0:T(8,128)(2,1)S(1)} %copy-done.15), channel_id=1, source_target_pairs={{0,4},{4,0},{8,12},{12,8},{16,20},{20,16},{24,28},{28,24},{1,5},{5... | collective-permute-start | bytes 3145736 | tf_op jit(solution)/shard_map/ppermute | solution.py:21
  224.6 28.8 %collective-permute-start.42 = (bf16[256,2048]{1,0:T(8,128)(2,1)S(1)}, bf16[256,2048]{1,0:T(8,128)(2,1)S(1)}, u32[]{:S(2)}, u32[]{:S(2)}) collective-permute-start(bf16[256,2048]{1,0:T(8,128)(2,1)S(1)} %copy-done.14), channel_id=1, source_target_pairs={{0,4},{4,0},{8,12},{12,8},{16,20},{20,16},{24,28},{28,24},{1,5},{5... | collective-permute-start | bytes 3145736 | tf_op jit(solution)/shard_map/ppermute | solution.py:21
  231.5 12.3 %collective-permute-start.49 = (bf16[128,2048]{1,0:T(8,128)(2,1)S(1)}, bf16[128,2048]{1,0:T(8,128)(2,1)S(1)}, u32[]{:S(2)}, u32[]{:S(2)}) collective-permute-start(bf16[128,2048]{1,0:T(8,128)(2,1)S(1)} %get-tuple-element.48), channel_id=1, source_target_pairs={{0,16},{4,20},{8,24},{12,28},{16,0},{20,4},{24,8},{28,12},{1,17},{... | collective-permute-start | bytes 1572872 | tf_op jit(solution)/shard_map/ppermute | solution.py:21
  236.3 14.9 %collective-permute-start.46 = (bf16[128,2048]{1,0:T(8,128)(2,1)S(1)}, bf16[128,2048]{1,0:T(8,128)(2,1)S(1)}, u32[]{:S(2)}, u32[]{:S(2)}) collective-permute-start(bf16[128,2048]{1,0:T(8,128)(2,1)S(1)} %get-tuple-element.47), channel_id=1, source_target_pairs={{0,8},{4,12},{8,0},{12,4},{16,24},{20,28},{24,16},{28,20},{1,9},{5... | collective-permute-start | bytes 1572872 | tf_op jit(solution)/shard_map/ppermute | solution.py:21
  243.9 18.5 %collective-permute-start.50 = (bf16[128,2048]{1,0:T(8,128)(2,1)S(1)}, bf16[128,2048]{1,0:T(8,128)(2,1)S(1)}, u32[]{:S(2)}, u32[]{:S(2)}) collective-permute-start(bf16[128,2048]{1,0:T(8,128)(2,1)S(1)} %fusion.36), channel_id=1, source_target_pairs={{0,8},{4,12},{8,0},{12,4},{16,24},{20,28},{24,16},{28,20},{1,9},{5... | collective-permute-start | bytes 1572872 | tf_op jit(solution)/shard_map/ppermute | solution.py:21
  245.5 26.4 %collective-permute-start.44 = (bf16[128,2048]{1,0:T(8,128)(2,1)S(1)}, bf16[128,2048]{1,0:T(8,128)(2,1)S(1)}, u32[]{:S(2)}, u32[]{:S(2)}) collective-permute-start(bf16[128,2048]{1,0:T(8,128)(2,1)S(1)} %slice.145), channel_id=1, source_target_pairs={{0,8},{4,12},{8,0},{12,4},{16,24},{20,28},{24,16},{28,20},{1,9},{5... | collective-permute-start | bytes 1572872 | tf_op jit(solution)/shard_map/ppermute | solution.py:21
  251.2 20.6 %collective-permute-start.47 = (bf16[128,2048]{1,0:T(8,128)(2,1)S(1)}, bf16[128,2048]{1,0:T(8,128)(2,1)S(1)}, u32[]{:S(2)}, u32[]{:S(2)}) collective-permute-start(bf16[128,2048]{1,0:T(8,128)(2,1)S(1)} %fusion.39), channel_id=1, source_target_pairs={{0,16},{4,20},{8,24},{12,28},{16,0},{20,4},{24,8},{28,12},{1,17},{... | collective-permute-start | bytes 1572872 | tf_op jit(solution)/shard_map/ppermute | solution.py:21
  251.8 21.2 %collective-permute-start.48 = (bf16[128,2048]{1,0:T(8,128)(2,1)S(1)}, bf16[128,2048]{1,0:T(8,128)(2,1)S(1)}, u32[]{:S(2)}, u32[]{:S(2)}) collective-permute-start(bf16[128,2048]{1,0:T(8,128)(2,1)S(1)} %slice.144), channel_id=1, source_target_pairs={{0,16},{4,20},{8,24},{12,28},{16,0},{20,4},{24,8},{28,12},{1,17},{... | collective-permute-start | bytes 1572872 | tf_op jit(solution)/shard_map/ppermute | solution.py:21
  (28 other events, 188.3 us)

commit v5 on v0

v5 whole, which is shorter than its diff:
```python
import functools

import jax
import jax.numpy as jnp
from jax import lax
from jax.experimental import pallas as pl
from jax.experimental.pallas import tpu as pltpu
from jax.sharding import PartitionSpec as P

ITERS = 3


softcap = 15.0
sharpen = 2.0
f32 = jnp.float32
bf16 = jnp.bfloat16
LANES = 128


def wide(value):
    return value.astype(f32)


def matmul(left, right, dims):
    return lax.dot_general(left, right, (dims, ((), ())), preferred_element_type=f32)


def flip(value, axis, mask):
    return lax.ppermute(value, axis, [(i, i ^ mask) for i in range(lax.axis_size(axis))])


def cut(value):
    half = value.shape[0] // 2
    return value[:half], value[half:]


def chip_axes(size):
    chips = size // 2
    bits = chips.bit_length() - 1
    low = 1 << ((bits + 1) // 2)
    first = [2 * m for m in range(1, low)]
    second = [2 * low * m for m in range(1, chips // low)]
    return first, second


def gather_head(head):
    size = lax.axis_size("sample")
    first, second = chip_axes(size)
    held = {mask: [flip(head, "sample", mask)] for mask in first + second}
    held[0] = [head]
    for a in first:
        for b in second:
            top, bottom = cut(held[a][0])[0], cut(held[b][0])[1]
            held[a | b] = [flip(top, "sample", b), flip(bottom, "sample", a)]
    for mask in list(held):
        held[mask | 1] = [flip(part, "sample", 1) for part in held[mask]]
    return held


def gather_features(features):
    size = lax.axis_size("cls")
    held = {0: features}
    for mask in list(range(2, size, 2)) + [1]:
        held[mask] = flip(features, "cls", mask)
    for mask in range(2, size, 2):
        held[mask | 1] = flip(held[mask], "cls", 1)
    return [held[mask] for mask in range(size)]


def fast(value):
    return pltpu.with_memory_space_constraint(value, pltpu.VMEM)


def call(kernel, outputs, operands, scratch=(), extra=(), limit=24):
    spec = pl.BlockSpec(memory_space=pltpu.VMEM)
    return pl.pallas_call(
        kernel,
        out_shape=tuple(pltpu.VMEM(shape, dtype) for shape, dtype in outputs),
        in_specs=[spec] * len(operands) + [pl.BlockSpec(memory_space=pl.ANY)] * len(extra),
        out_specs=(spec,) * len(outputs),
        scratch_shapes=list(scratch),
        compiler_params=pltpu.CompilerParams(vmem_limit_bytes=limit << 20),
        cost_estimate=pl.CostEstimate(flops=1, bytes_accessed=1, transcendentals=0),
    )(*[fast(operand) for operand in operands], *extra)


def as_column(row):
    return jnp.transpose(jnp.broadcast_to(row, (LANES, row.shape[1])))


def row_kernel(count, student_ref, scale_ref, ceiling_ref, *refs):
    part_refs, (new_ref, total_ref, partial) = refs[:count], refs[count:]
    mass = part_refs[0][...]
    for ref in part_refs[1:]:
        mass = mass + ref[...]
    new_ref[...] = scale_ref[...] * jnp.minimum(1.0, ceiling_ref[...] / mass)
    rows, columns = student_ref.shape
    block = 64

    def body(i, carry):
        at = pl.ds(pl.multiple_of(i * block, block), block)
        total = jnp.zeros((block, LANES), f32)
        for j in range(0, columns, LANES):
            value = student_ref[at, j : j + LANES]
            total = total + value * value * new_ref[:, j : j + LANES]
        partial[at, :] = total
        return carry

    lax.fori_loop(0, rows // block, body, 0)
    total_ref[...] = jnp.sum(jnp.transpose(partial[...]), axis=0, keepdims=True)


def column_kernel(count, student_ref, scale_ref, *refs):
    part_refs, (total_ref, inverse) = refs[:count], refs[count:]
    mass = part_refs[0][...]
    for ref in part_refs[1:]:
        mass = mass + ref[...]
    inverse[...] = as_column(1.0 / mass)
    rows, columns = student_ref.shape
    block = 8

    def body(i, total):
        at = pl.ds(pl.multiple_of(i * block, block), block)
        factor = inverse[at, :]
        new = []
        for j in range(0, columns, LANES):
            value = student_ref[at, j : j + LANES]
            new.append(total[j // LANES] + value * value * factor)
        return tuple(new)

    start = tuple(jnp.zeros((block, LANES), f32) for _ in range(0, columns, LANES))
    total = lax.fori_loop(0, rows // block, body, start, unroll=4)
    for j, value in enumerate(total):
        at = slice(j * LANES, (j + 1) * LANES)
        total_ref[:, at] = jnp.sum(value, axis=0, keepdims=True) * scale_ref[:, at]


def split_by_core(result, core, depth):
    top, bottom = result[:depth], result[depth:]
    return jnp.where(core == 0, top, bottom), jnp.where(core == 0, bottom, top)


def gradient_kernel(count, depth, far, masks, student_ref, slope_ref, scale_ref, students_ref, turned_ref, *refs):
    part_refs, head_refs = refs[:count], refs[count : count + len(masks)]
    targets_ref, grad_ref, mine_ref, theirs_ref, share_ref, inverse, students = refs[count + len(masks) :]
    me, place = lax.axis_index("sample"), lax.axis_index("cls")
    chip, core = me // 2, me % 2
    groups = lax.axis_size("cls")
    mass = part_refs[0][...]
    for ref in part_refs[1:]:
        mass = mass + ref[...]
    inverse[...] = as_column(1.0 / mass)
    students[...] = as_column(1.0 / students_ref[...])
    columns = student_ref.shape[1]
    tile = min(256, columns)
    turned = turned_ref.at[place ^ chip ^ far]

    def body(i, carry):
        for j in range(0, tile, LANES):
            at = pl.ds(pl.multiple_of(i * tile + j, LANES), LANES)
            student = student_ref[:, at]
            target = (student * student * scale_ref[:, at] * inverse[...]).astype(bf16)
            targets_ref[:, at] = target
            grad_ref[:, at] = ((student * students[...] - wide(target)) * wide(slope_ref[:, at])).astype(bf16)
        at = pl.ds(pl.multiple_of(i * tile, tile), tile)
        result = jnp.dot(turned[...], grad_ref[:, at], preferred_element_type=f32)
        mine, theirs = split_by_core(result, core, depth)
        mine_ref[:, at] = mine.astype(bf16)
        theirs_ref[:, at] = theirs.astype(bf16)
        return carry

    lax.fori_loop(0, columns // tile, body, 0)
    for mask, ref in zip(masks, head_refs):

        @pl.when((chip ^ mask) == (place ^ (groups - 1)))
        def _():
            share_ref[...] = matmul(grad_ref[...], ref[...], ((1,), (1,))).astype(bf16)


def products_kernel(count, depth, near, masks, grad_ref, turned_ref, *refs):
    head_refs, refs = refs[: len(masks)], refs[len(masks) + count :]
    pairs, (shares_ref,) = refs[:-1], refs[-1:]
    me, place = lax.axis_index("sample"), lax.axis_index("cls")
    chip, core = me // 2, me % 2
    columns = grad_ref.shape[1]
    tile = min(256, columns)
    for index, mask in enumerate(near):
        mine_ref, theirs_ref = pairs[2 * index], pairs[2 * index + 1]
        turned = turned_ref.at[place ^ chip ^ mask]

        def body(i, carry):
            at = pl.ds(pl.multiple_of(i * tile, tile), tile)
            result = jnp.dot(turned[...], grad_ref[:, at], preferred_element_type=f32)
            mine, theirs = split_by_core(result, core, depth)
            mine_ref[:, at] = mine.astype(bf16)
            theirs_ref[:, at] = theirs.astype(bf16)
            return carry

        lax.fori_loop(0, columns // tile, body, 0)
    for mask, ref in zip(masks, head_refs):
        shares_ref[chip ^ mask ^ place] = matmul(grad_ref[...], ref[...], ((1,), (1,))).astype(bf16)


def per_device(features, head, class_cap):
    rows, width = features.shape
    depth, classes = head.shape
    samples = lax.axis_size("sample")
    groups = lax.axis_size("cls")
    ratio = rows * samples / (classes * groups)
    me = lax.axis_index("sample")
    place = lax.axis_index("cls")
    chip, core = me // 2, me % 2
    first, second = chip_axes(samples)

    pieces = gather_head(head)
    blocks = jnp.stack(gather_features(features))

    order = [0] + first + second + [a | b for a in first for b in second]
    heads, logits = {}, None
    for mask in order:
        same, other = pieces[mask], pieces[mask | 1]
        parts = [jnp.where(core == 0, s, o) for s, o in zip(same, other)]
        parts += [jnp.where(core == 0, o, s) for s, o in zip(same, other)]
        heads[mask] = lax.optimization_barrier(jnp.concatenate(parts, axis=0))
        group = lax.dynamic_index_in_dim(blocks, chip ^ (mask // 2) ^ place, 0, keepdims=False)
        product = matmul(group, heads[mask], ((1,), (0,)))
        logits = product if logits is None else logits + product

    tanh = jnp.tanh(logits / softcap)
    student = jnp.exp(softcap * tanh)
    slope = (1.0 - tanh * tanh).astype(bf16)
    sums = jnp.stack([jnp.sum(student, axis=1), jnp.sum(student * student, axis=1)])
    student, slope, sums = lax.optimization_barrier((student, slope, sums))
    turned = lax.optimization_barrier(jnp.transpose(blocks, (0, 2, 1)))

    def row_parts(value):
        return [value] + [flip(value, "cls", mask) for mask in range(1, groups)]

    def column_parts(value):
        value = value + flip(value, "sample", 1)
        return [value] + [flip(value, "sample", mask) for mask in range(2, samples, 2)]

    ceiling = (wide(class_cap) * ratio)[None]
    parts = row_parts(sums)
    students_mass = sum([part[0:1] for part in parts[1:]], parts[0][0:1])
    parts = [part[1:2] for part in parts]
    scale = jnp.ones((1, classes), f32)
    for _ in range(ITERS):
        (mass,) = call(
            functools.partial(column_kernel, len(parts)),
            [((1, classes), f32)],
            [student, scale] + parts,
            [pltpu.VMEM((rows, LANES), f32)],
        )
        sent = column_parts(mass)
        scale, mass = call(
            functools.partial(row_kernel, len(sent)),
            [((1, classes), f32), ((1, rows), f32)],
            [student, scale, ceiling] + sent,
            [pltpu.VMEM((rows, LANES), f32)],
        )
        parts = row_parts(mass)

    chip_masks = [mask // 2 for mask in order]
    head_list = [heads[mask] for mask in order]
    near = [mask // 2 for mask in first + second] + [0]
    diagonal = [(a, b) for a in first for b in second]
    far = (diagonal[-1][0] | diagonal[-1][1]) // 2
    near = [(a | b) // 2 for a, b in diagonal[:-1]] + near
    targets, grad, mine, theirs, share = call(
        functools.partial(gradient_kernel, len(parts), depth, far, chip_masks),
        [((rows, classes), bf16)] * 2 + [((depth, classes), bf16)] * 2 + [((rows, width), bf16)],
        [student, slope, scale, students_mass, turned] + parts + head_list,
        [pltpu.VMEM((rows, LANES), f32)] * 2,
    )
    extra = {}

    def send_diagonal(a, b, top, bottom):
        extra.setdefault((b, 0), []).append(flip(top, "sample", a))
        extra.setdefault((a, 1), []).append(flip(bottom, "sample", b))

    block = (wide(mine) + wide(flip(theirs, "sample", 1))).astype(bf16)
    halves = lax.optimization_barrier(cut(block))
    send_diagonal(*diagonal[-1], *halves)
    share_from = {groups - 2: flip(share, "cls", 1)}

    results = call(
        functools.partial(products_kernel, len(halves), depth, near, chip_masks),
        [((depth, classes), bf16)] * (2 * len(near)) + [((groups, rows, width), bf16)],
        [grad, turned] + head_list,
        extra=halves,
    )
    shares = results[-1]
    mixed = {
        2 * mask: wide(results[2 * i]) + wide(flip(results[2 * i + 1], "sample", 1)) for i, mask in enumerate(near)
    }
    for a, b in diagonal[:-1]:
        send_diagonal(a, b, *cut(mixed[a | b].astype(bf16)))

    total = wide(shares[0]) + wide(flip(shares[1], "cls", 1))
    for mask in range(2, groups, 2):
        received = share_from[mask] if mask in share_from else flip(shares[mask | 1], "cls", 1)
        total = total + wide(flip((wide(shares[mask]) + wide(received)).astype(bf16), "cls", mask))
    grad_features = total.astype(bf16)

    halves = list(cut(mixed[0]))
    for late in (False, True):
        for mask in first + second:
            for part, value in enumerate(cut(mixed[mask])):
                if ((mask, part) in extra) == late:
                    for more in extra.get((mask, part), []):
                        value = value + wide(more)
                    halves[part] = halves[part] + wide(flip(value.astype(bf16), "sample", mask))
    grad_head = jnp.concatenate(halves, axis=0).astype(bf16)
    return (targets, grad_features, grad_head)


def solution(mesh):
    return jax.shard_map(
        per_device,
        mesh=mesh,
        in_specs=(P("sample", "cls"), P("sample", "cls"), P("cls")),
        out_specs=(P("sample", "cls"), P("sample", "cls"), P("sample", "cls")),
        check_vma=False,
    )
```

time: 357 us -> 201 us (0.56)
  waiting for transfers between devices: 209 us -> 102 us
  blocking collectives: 75.1 us -> 0 us
  starting transfers between devices: 0.16 us -> 51.2 us
  matrix products: 31.6 us -> 6.72 us
  Pallas kernels: 0 us -> 23.8 us
  other arithmetic: 24.1 us -> 10.7 us
  between operations: 13.8 us -> 1.05 us
    all_gather x2 -> x0, waiting for transfers between devices: 105 us -> none  [the longest x1 55 us: per_device(): head_full = lax.all_gather(head, 'sample', axis=0, tiled=True)]
    reduce_scatter x2 -> x0, waiting for transfers between devices: 103 us -> none  [the longest x1 58.2 us: per_device(): lax.psum_scatter(lax.dot_general(whole, grad_logits, (((0,), (0,)), ((),...]
    ppermute x0 -> x49, waiting for transfers between devices: none -> 102 us  [flip(): lax.ppermute(value, axis, [(i, i ^ mask) for i in range(lax.axis_size(axi...]
    psum x7 -> x0, blocking collectives: 75.1 us -> none  [the longest x3 36.2 us: per_device(): column_mass = lax.psum(jnp.sum(transport, axis=0), 'sample')]
    ppermute x0 -> x49, starting transfers between devices: none -> 51.2 us  [flip(): lax.ppermute(value, axis, [(i, i ^ mask) for i in range(lax.axis_size(axi...]
    dot_general x3 -> x4, matrix products: 31.6 us -> 6.72 us  [matmul(): lax.dot_general(left, right, (dims, ((), ())), preferred_element_type=f32)]
    pallas_call x0 -> x8, Pallas kernels: none -> 23.8 us  [call(): pl.pallas_call(kernel, out_shape=tuple((pltpu.VMEM(shape, dtype) for shap...]
    reduce_sum x6 -> x0, other arithmetic: 21.1 us -> none  [the longest x3 13.1 us: per_device(): column_mass = lax.psum(jnp.sum(transport, axis=0), 'sample')]
  transfers between devices with their start and end apart: 4 -> 49, of which waited for: 4 -> 30; matrix products, arithmetic and copies ran while one was open for 4% -> 8% of each run, Pallas kernels for 0% -> 6%
where the time goes in v5:
time: 201 us
  waiting for transfers between devices  102 us (51%)
  starting transfers between devices  51.2 us (25%)
  Pallas kernels  23.8 us (12%)
  other arithmetic  10.7 us (5%)
  matrix products  6.72 us (3%)
  local copies, waits for them, and re-layouts  5.07 us (3%)
    ppermute x49, waiting for transfers between devices, flip(): lax.ppermute(value, axis, [(i, i ^ mask) for i in range(lax.axis_size(axi...  102 us
    ppermute x49, starting transfers between devices, flip(): lax.ppermute(value, axis, [(i, i ^ mask) for i in range(lax.axis_size(axi...  51.2 us
    pallas_call x8, Pallas kernels, call(): pl.pallas_call(kernel, out_shape=tuple((pltpu.VMEM(shape, dtype) for shap...  23.8 us
    dot_general x4, matrix products, matmul(): lax.dot_general(left, right, (dims, ((), ())), preferred_element_type=f32)  6.72 us
    select_n x5, other arithmetic, per_device(): parts = [jnp.where(core == 0, s, o) for s, o in zip(same, other)]  4.25 us
  transfers between devices with their start and end apart: 49, of which 30 were waited for; matrix products, arithmetic and copies ran while one was open for 8% of the time, Pallas kernels for 6%

profile of v5, /device:TPU:0, one launch (start us, length us, event | category | flops | bytes accessed | tf_op | source)
XLA Modules:
  0.0 200.5 jit_solution(10795304686977834406)
XLA Ops:
  0.6 3.0 %collective-permute-start.4 = (bf16[256,2048]{1,0:T(8,128)(2,1)}, bf16[256,2048]{1,0:T(8,128)(2,1)}, u32[]{:S(2)}, u32[]{:S(2)}) collective-permute-start(bf16[256,2048]{1,0:T(8,128)(2,1)} %param.4), channel_id=1, source_target_pairs={{0,8},{4,12},{8,0},{12,4},{16,24},{20,28},{24,16},{28,20},{1,9},{5... | collective-permute-start | bytes 3145736 | tf_op jit(solution)/shard_map/ppermute | solution.py:29
  4.9 2.7 %collective-permute-start.1 = (bf16[512,512]{0,1:T(8,128)(2,1)S(1)}, bf16[512,512]{0,1:T(8,128)(2,1)S(1)}, u32[]{:S(2)}, u32[]{:S(2)}) collective-permute-start(bf16[512,512]{0,1:T(8,128)(2,1)S(1)} %copy.6), channel_id=1, source_target_pairs={{0,2},{1,3},{2,0},{3,1},{4,6},{5,7},{6,4},{7,5},{8,10},{9,11},{10,... | collective-permute-start | bytes 1572872 | tf_op jit(solution)/shard_map/ppermute | solution.py:29
  7.5 1.5 collective-permute-start.6
  9.1 1.6 collective-permute-start
  10.6 20.9 %collective-permute-done.1 = bf16[512,512]{0,1:T(8,128)(2,1)S(1)} collective-permute-done((bf16[512,512]{0,1:T(8,128)(2,1)S(1)}, bf16[512,512]{0,1:T(8,128)(2,1)S(1)}, u32[]{:S(2)}, u32[]{:S(2)}) %collective-permute-start.1) | collective-permute-done | bytes 524320 | tf_op jit(solution)/shard_map/ppermute | solution.py:29
  32.2 1.4 broadcast_select_fusion.5
  34.9 1.5 collective-permute-start.8
  38.1 6.9 %collective-permute-done.2 = bf16[512,512]{0,1:T(8,128)(2,1)S(1)} collective-permute-done((bf16[512,512]{0,1:T(8,128)(2,1)S(1)}, bf16[512,512]{0,1:T(8,128)(2,1)S(1)}, u32[]{:S(2)}, u32[]{:S(2)}) %collective-permute-start.2) | collective-permute-done | bytes 524320 | tf_op jit(solution)/shard_map/ppermute | solution.py:29
  45.0 1.4 fusion.25
  47.7 1.6 collective-permute-done.8
  49.3 2.3 %collective-permute-done.10 = bf16[128,2048]{1,0:T(8,128)(2,1)S(1)} collective-permute-done((bf16[128,2048]{1,0:T(8,128)(2,1)S(1)}, bf16[128,2048]{1,0:T(8,128)(2,1)S(1)}, u32[]{:S(2)}, u32[]{:S(2)}) %collective-permute-start.10) | collective-permute-done | bytes 524320 | tf_op jit(solution)/shard_map/ppermute | solution.py:29
  51.6 1.4 broadcast_select_fusion.3
  53.0 1.4 broadcast_select_fusion.1
  57.7 2.8 %fusion.24 = (f32[512]{0:T(512)S(1)}, f32[512]{0:T(512)S(1)}, bf16[512,2048]{1,0:T(8,128)(2,1)S(1)}, f32[512,2048]{1,0:T(8,128)S(1)}) fusion(bf16[512,2048]{1,0:T(8,128)(2,1)S(1)} %pad_maximum_fusion.4.refs_7_.refs_3_, bf16[4,512,512]{1,2,0:T(8,128)(2,1)S(1)} %get-tuple-element.56, s32[]{:T(128)S(6)} %select_n.84, f32[512,2048]{1,0:T(8,128)S(1)} %fusion.10, ...), kind=kOutput, calls=%fused_computation.62 | convolution fusion | flops 1085275136 | bytes 21499908 | tf_op jit(solution)/shard_map/dot_general | solution.py:25
  60.6 1.5 collective-permute-start.12
  62.1 2.0 %collective-permute-start.13 = (f32[2,512]{1,0:T(2,128)S(1)}, f32[2,512]{1,0:T(2,128)S(1)}, u32[]{:S(2)}, u32[]{:S(2)}) collective-permute-start(f32[2,512]{1,0:T(2,128)S(1)} %pad_maximum_fusion.6), channel_id=1, source_target_pairs={{0,2},{1,3},{2,0},{3,1},{4,6},{5,7},{6,4},{7,5},{8,10},{9,11},{10,... | collective-permute-start | bytes 12296 | tf_op jit(solution)/shard_map/ppermute | solution.py:29
  64.1 1.4 collective-permute-start.14
  66.6 2.9 %collective-permute-done.14 = f32[2,512]{1,0:T(2,128)S(1)} collective-permute-done((f32[2,512]{1,0:T(2,128)S(1)}, f32[2,512]{1,0:T(2,128)S(1)}, u32[]{:S(2)}, u32[]{:S(2)}) %collective-permute-start.14) | collective-permute-done | bytes 4128 | tf_op jit(solution)/shard_map/ppermute | solution.py:29
  72.8 2.4 %collective-permute-start.18 = (f32[1,2048]{1,0:T(1,128)S(1)}, f32[1,2048]{1,0:T(1,128)S(1)}, u32[]{:S(2)}, u32[]{:S(2)}) collective-permute-start(f32[1,2048]{1,0:T(1,128)S(1)} %add.92.refs_0_), channel_id=1, source_target_pairs={{0,24},{4,28},{8,16},{12,20},{16,8},{20,12},{24,0},{28,4},{1,25},{... | collective-permute-start | bytes 24584 | tf_op jit(solution)/shard_map/ppermute | solution.py:29
  75.9 1.5 collective-permute-done.18.refs_3_
  78.2 1.8 collective-permute-start.20
  80.0 2.4 %collective-permute-start.21 = (f32[1,512]{1,0:T(1,128)S(1)}, f32[1,512]{1,0:T(1,128)S(1)}, u32[]{:S(2)}, u32[]{:S(2)}) collective-permute-start(f32[1,512]{1,0:T(1,128)S(1)} %get-tuple-element.30.refs_0_), channel_id=1, source_target_pairs={{0,3},{1,2},{2,1},{3,0},{4,7},{5,6},{6,5},{7,4},{8,11},{9,10},{10,... | collective-permute-start | bytes 6152 | tf_op jit(solution)/shard_map/ppermute | solution.py:29
  82.7 2.7 %collective-permute-done.21.refs_3_ = f32[1,512]{1,0:T(1,128)S(1)} collective-permute-done((f32[1,512]{1,0:T(1,128)S(1)}, f32[1,512]{1,0:T(1,128)S(1)}, u32[]{:S(2)}, u32[]{:S(2)}) %collective-permute-start.21) | collective-permute-done | bytes 2080 | tf_op jit(solution)/shard_map/ppermute | solution.py:29
  87.3 1.6 collective-permute-start.23
  88.9 1.4 collective-permute-start.24
  91.1 1.5 collective-permute-done.24.refs_2_
  92.6 2.3 %collective-permute-done.25.refs_3_ = f32[1,2048]{1,0:T(1,128)S(1)} collective-permute-done((f32[1,2048]{1,0:T(1,128)S(1)}, f32[1,2048]{1,0:T(1,128)S(1)}, u32[]{:S(2)}, u32[]{:S(2)}) %collective-permute-start.25) | collective-permute-done | bytes 8224 | tf_op jit(solution)/shard_map/ppermute | solution.py:29
  95.6 3.0 %collective-permute-start.27 = (f32[1,512]{1,0:T(1,128)S(1)}, f32[1,512]{1,0:T(1,128)S(1)}, u32[]{:S(2)}, u32[]{:S(2)}) collective-permute-start(f32[1,512]{1,0:T(1,128)S(1)} %get-tuple-element.32.refs_0_), channel_id=1, source_target_pairs={{0,2},{1,3},{2,0},{3,1},{4,6},{5,7},{6,4},{7,5},{8,10},{9,11},{10,... | collective-permute-start | bytes 6152 | tf_op jit(solution)/shard_map/ppermute | solution.py:29
  98.6 1.4 collective-permute-start.28
  100.2 3.8 %collective-permute-done.28.refs_3_ = f32[1,512]{1,0:T(1,128)S(1)} collective-permute-done((f32[1,512]{1,0:T(1,128)S(1)}, f32[1,512]{1,0:T(1,128)S(1)}, u32[]{:S(2)}, u32[]{:S(2)}) %collective-permute-start.28) | collective-permute-done | bytes 2080 | tf_op jit(solution)/shard_map/ppermute | solution.py:29
  107.1 2.4 %collective-permute-start.32 = (f32[1,2048]{1,0:T(1,128)S(1)}, f32[1,2048]{1,0:T(1,128)S(1)}, u32[]{:S(2)}, u32[]{:S(2)}) collective-permute-start(f32[1,2048]{1,0:T(1,128)S(1)} %add.94.refs_0_), channel_id=1, source_target_pairs={{0,24},{4,28},{8,16},{12,20},{16,8},{20,12},{24,0},{28,4},{1,25},{... | collective-permute-start | bytes 24584 | tf_op jit(solution)/shard_map/ppermute | solution.py:29
  110.2 1.5 collective-permute-done.32.refs_3_
  112.4 1.9 collective-permute-start.34
  114.3 2.4 %collective-permute-start.35 = (f32[1,512]{1,0:T(1,128)S(1)}, f32[1,512]{1,0:T(1,128)S(1)}, u32[]{:S(2)}, u32[]{:S(2)}) collective-permute-start(f32[1,512]{1,0:T(1,128)S(1)} %get-tuple-element.34.refs_0_), channel_id=1, source_target_pairs={{0,3},{1,2},{2,1},{3,0},{4,7},{5,6},{6,5},{7,4},{8,11},{9,10},{10,... | collective-permute-start | bytes 6152 | tf_op jit(solution)/shard_map/ppermute | solution.py:29
  116.9 2.8 %collective-permute-done.35.refs_3_ = f32[1,512]{1,0:T(1,128)S(1)} collective-permute-done((f32[1,512]{1,0:T(1,128)S(1)}, f32[1,512]{1,0:T(1,128)S(1)}, u32[]{:S(2)}, u32[]{:S(2)}) %collective-permute-start.35) | collective-permute-done | bytes 2080 | tf_op jit(solution)/shard_map/ppermute | solution.py:29
  119.7 7.6 %shard_map.64 = (bf16[512,2048]{1,0:T(8,128)(2,1)S(1)}, bf16[512,2048]{1,0:T(8,128)(2,1)S(1)}, bf16[256,2048]{1,0:T(8,128)(2,1)S(1)}, bf16[256,2048]{1,0:T(8,128)(2,1)S(1)}, bf16[512,512]{1,0:T(8,128)(2,1)S(1)}) custom-call(f32[512,2048]{1,0:T(8,128)S(1)} %get-tuple-element.26.student_ref, bf16[512,2048]{1,0:T(8,128)(2,1)S(1)} %get-tuple-element.27.slope_ref, ...), custom_call_target="tpu_custom_call" | custom-call | flops 1 | bytes 1 | tf_op jit(solution)/shard_map/pallas_call | solution.py:76
  127.4 2.6 %collective-permute-done.36 = bf16[256,2048]{1,0:T(8,128)(2,1)S(1)} collective-permute-done((bf16[256,2048]{1,0:T(8,128)(2,1)S(1)}, bf16[256,2048]{1,0:T(8,128)(2,1)S(1)}, u32[]{:S(2)}, u32[]{:S(2)}) %collective-permute-start.36) | collective-permute-done | bytes 1048608 | tf_op jit(solution)/shard_map/ppermute | solution.py:29
  130.5 12.1 %shard_map.65 = (bf16[256,2048]{1,0:T(8,128)(2,1)S(1)}, bf16[256,2048]{1,0:T(8,128)(2,1)S(1)}, bf16[256,2048]{1,0:T(8,128)(2,1)S(1)}, bf16[256,2048]{1,0:T(8,128...) custom-call(bf16[512,2048]{1,0:T(8,128)(2,1)S(1)} %get-tuple-element.36.g, ...), custom_call_target="tpu_custom_call" | custom-call | flops 1 | bytes 1 | tf_op jit(solution)/shard_map/pallas_call | solution.py:76
  143.1 3.1 %collective-permute-start.39 = (bf16[512,512]{1,0:T(8,128)(2,1)S(1)}, bf16[512,512]{1,0:T(8,128)(2,1)S(1)}, u32[]{:S(2)}, u32[]{:S(2)}) collective-permute-start(bf16[512,512]{1,0:T(8,128)(2,1)S(1)} %fusion.6), channel_id=1, source_target_pairs={{0,2},{1,3},{2,0},{3,1},{4,6},{5,7},{6,4},{7,5},{8,10},{9,11},{10,... | collective-permute-start | bytes 1572872 | tf_op jit(solution)/shard_map/ppermute | solution.py:29
  147.5 1.4 collective-permute-start.47
  148.9 1.5 collective-permute-start.44
  150.5 17.5 %collective-permute-done.37 = bf16[512,512]{1,0:T(8,128)(2,1)S(1)} collective-permute-done((bf16[512,512]{1,0:T(8,128)(2,1)S(1)}, bf16[512,512]{1,0:T(8,128)(2,1)S(1)}, u32[]{:S(2)}, u32[]{:S(2)}) %collective-permute-start.37) | collective-permute-done | bytes 524320 | tf_op jit(solution)/shard_map/ppermute | solution.py:29
  168.0 1.7 collective-permute-done.39
  171.2 1.5 collective-permute-start.48
  173.8 1.5 collective-permute-start.45
  176.3 9.7 %collective-permute-done.48 = bf16[128,2048]{1,0:T(8,128)(2,1)S(1)} collective-permute-done((bf16[128,2048]{1,0:T(8,128)(2,1)S(1)}, bf16[128,2048]{1,0:T(8,128)(2,1)S(1)}, u32[]{:S(2)}, u32[]{:S(2)}) %collective-permute-start.48) | collective-permute-done | bytes 524320 | tf_op jit(solution)/shard_map/ppermute | solution.py:29
  186.0 10.9 %collective-permute-done.42 = bf16[128,2048]{1,0:T(8,128)(2,1)S(1)} collective-permute-done((bf16[128,2048]{1,0:T(8,128)(2,1)S(1)}, bf16[128,2048]{1,0:T(8,128)(2,1)S(1)}, u32[]{:S(2)}, u32[]{:S(2)}) %collective-permute-start.42) | collective-permute-done | bytes 524320 | tf_op jit(solution)/shard_map/ppermute | solution.py:29
  196.8 2.1 %collective-permute-done.46 = bf16[128,2048]{1,0:T(8,128)(2,1)S(1)} collective-permute-done((bf16[128,2048]{1,0:T(8,128)(2,1)S(1)}, bf16[128,2048]{1,0:T(8,128)(2,1)S(1)}, u32[]{:S(2)}, u32[]{:S(2)}) %collective-permute-start.46) | collective-permute-done | bytes 524320 | tf_op jit(solution)/shard_map/ppermute | solution.py:29
  (103 shorter events, 31.4 us)
Async XLA Ops:
  0.6 31.5 %collective-permute-start.4 = (bf16[256,2048]{1,0:T(8,128)(2,1)}, bf16[256,2048]{1,0:T(8,128)(2,1)}, u32[]{:S(2)}, u32[]{:S(2)}) collective-permute-start(bf16[256,2048]{1,0:T(8,128)(2,1)} %param.4), channel_id=1, source_target_pairs={{0,8},{4,12},{8,0},{12,4},{16,24},{20,28},{24,16},{28,20},{1,9},{5... | collective-permute-start | bytes 3145736 | tf_op jit(solution)/shard_map/ppermute | solution.py:29
  3.6 28.5 %collective-permute-start.3 = (bf16[256,2048]{1,0:T(8,128)(2,1)}, bf16[256,2048]{1,0:T(8,128)(2,1)S(1)}, u32[]{:S(2)}, u32[]{:S(2)}) collective-permute-start(bf16[256,2048]{1,0:T(8,128)(2,1)} %param.4), channel_id=1, source_target_pairs={{0,4},{4,0},{8,12},{12,8},{16,20},{20,16},{24,28},{28,24},{1,5},{5... | collective-permute-start | bytes 3145736 | tf_op jit(solution)/shard_map/ppermute | solution.py:29
  4.9 26.6 %collective-permute-start.1 = (bf16[512,512]{0,1:T(8,128)(2,1)S(1)}, bf16[512,512]{0,1:T(8,128)(2,1)S(1)}, u32[]{:S(2)}, u32[]{:S(2)}) collective-permute-start(bf16[512,512]{0,1:T(8,128)(2,1)S(1)} %copy.6), channel_id=1, source_target_pairs={{0,2},{1,3},{2,0},{3,1},{4,6},{5,7},{6,4},{7,5},{8,10},{9,11},{10,... | collective-permute-start | bytes 1572872 | tf_op jit(solution)/shard_map/ppermute | solution.py:29
  7.5 28.9 %collective-permute-start.6 = (bf16[256,2048]{1,0:T(8,128)(2,1)}, bf16[256,2048]{1,0:T(8,128)(2,1)}, u32[]{:S(2)}, u32[]{:S(2)}) collective-permute-start(bf16[256,2048]{1,0:T(8,128)(2,1)} %param.4), channel_id=1, source_target_pairs={{0,16},{4,20},{8,24},{12,28},{16,0},{20,4},{24,8},{28,12},{1,17},{... | collective-permute-start | bytes 3145736 | tf_op jit(solution)/shard_map/ppermute | solution.py:29
  9.1 29.1 %collective-permute-start = (bf16[512,512]{0,1:T(8,128)(2,1)S(1)}, bf16[512,512]{0,1:T(8,128)(2,1)}, u32[]{:S(2)}, u32[]{:S(2)}) collective-permute-start(bf16[512,512]{0,1:T(8,128)(2,1)S(1)} %copy.6), channel_id=1, source_target_pairs={{0,1},{1,0},{2,3},{3,2},{4,5},{5,4},{6,7},{7,6},{8,9},{9,8},{10,11... | collective-permute-start | bytes 1572872 | tf_op jit(solution)/shard_map/ppermute | solution.py:29
  31.5 13.5 %collective-permute-start.2 = (bf16[512,512]{0,1:T(8,128)(2,1)S(1)}, bf16[512,512]{0,1:T(8,128)(2,1)S(1)}, u32[]{:S(2)}, u32[]{:S(2)}) collective-permute-start(bf16[512,512]{0,1:T(8,128)(2,1)S(1)} %collective-permute-done.1), channel_id=1, source_target_pairs={{0,1},{1,0},{2,3},{3,2},{4,5},{5,4},{6,7},{7,6},{8,9},{9,8},{10,11... | collective-permute-start | bytes 1572872 | tf_op jit(solution)/shard_map/ppermute | solution.py:29
  32.2 19.5 %collective-permute-start.5 = (bf16[256,2048]{1,0:T(8,128)(2,1)}, bf16[256,2048]{1,0:T(8,128)(2,1)S(1)}, u32[]{:S(2)}, u32[]{:S(2)}) collective-permute-start(bf16[256,2048]{1,0:T(8,128)(2,1)} %collective-permute-done.4), channel_id=1, source_target_pairs={{0,4},{4,0},{8,12},{12,8},{16,20},{20,16},{24,28},{28,24},{1,5},{5... | collective-permute-start | bytes 3145736 | tf_op jit(solution)/shard_map/ppermute | solution.py:29
  34.9 14.4 %collective-permute-start.8 = (bf16[128,2048]{1,0:T(8,128)(2,1)S(1)}, bf16[128,2048]{1,0:T(8,128)(2,1)S(1)}, u32[]{:S(2)}, u32[]{:S(2)}) collective-permute-start(bf16[128,2048]{1,0:T(8,128)(2,1)S(1)} %slice.86), channel_id=1, source_target_pairs={{0,16},{4,20},{8,24},{12,28},{16,0},{20,4},{24,8},{28,12},{1,17},{... | collective-permute-start | bytes 1572872 | tf_op jit(solution)/shard_map/ppermute | solution.py:29
  37.5 14.1 %collective-permute-start.10 = (bf16[128,2048]{1,0:T(8,128)(2,1)S(1)}, bf16[128,2048]{1,0:T(8,128)(2,1)S(1)}, u32[]{:S(2)}, u32[]{:S(2)}) collective-permute-start(bf16[128,2048]{1,0:T(8,128)(2,1)S(1)} %slice.87), channel_id=1, source_target_pairs={{0,8},{4,12},{8,0},{12,4},{16,24},{20,28},{24,16},{28,20},{1,9},{5... | collective-permute-start | bytes 1572872 | tf_op jit(solution)/shard_map/ppermute | solution.py:29
  38.1 14.9 %collective-permute-start.7 = (bf16[256,2048]{1,0:T(8,128)(2,1)}, bf16[256,2048]{1,0:T(8,128)(2,1)S(1)}, u32[]{:S(2)}, u32[]{:S(2)}) collective-permute-start(bf16[256,2048]{1,0:T(8,128)(2,1)} %collective-permute-done.6), channel_id=1, source_target_pairs={{0,4},{4,0},{8,12},{12,8},{16,20},{20,16},{24,28},{28,24},{1,5},{5... | collective-permute-start | bytes 3145736 | tf_op jit(solution)/shard_map/ppermute | solution.py:29
  49.3 5.5 %collective-permute-start.9 = (bf16[128,2048]{1,0:T(8,128)(2,1)S(1)}, bf16[128,2048]{1,0:T(8,128)(2,1)S(1)}, u32[]{:S(2)}, u32[]{:S(2)}) collective-permute-start(bf16[128,2048]{1,0:T(8,128)(2,1)S(1)} %collective-permute-done.8), channel_id=1, source_target_pairs={{0,4},{4,0},{8,12},{12,8},{16,20},{20,16},{24,28},{28,24},{1,5},{5... | collective-permute-start | bytes 1572872 | tf_op jit(solution)/shard_map/ppermute | solution.py:29
  51.6 3.2 %collective-permute-start.11 = (bf16[128,2048]{1,0:T(8,128)(2,1)S(1)}, bf16[128,2048]{1,0:T(8,128)(2,1)S(1)}, u32[]{:S(2)}, u32[]{:S(2)}) collective-permute-start(bf16[128,2048]{1,0:T(8,128)(2,1)S(1)} %collective-permute-done.10), channel_id=1, source_target_pairs={{0,4},{4,0},{8,12},{12,8},{16,20},{20,16},{24,28},{28,24},{1,5},{5... | collective-permute-start | bytes 1572872 | tf_op jit(solution)/shard_map/ppermute | solution.py:29
  60.6 4.9 %collective-permute-start.12 = (f32[2,512]{1,0:T(2,128)S(1)}, f32[2,512]{1,0:T(2,128)S(1)}, u32[]{:S(2)}, u32[]{:S(2)}) collective-permute-start(f32[2,512]{1,0:T(2,128)S(1)} %pad_maximum_fusion.6), channel_id=1, source_target_pairs={{0,1},{1,0},{2,3},{3,2},{4,5},{5,4},{6,7},{7,6},{8,9},{9,8},{10,11... | collective-permute-start | bytes 12296 | tf_op jit(solution)/shard_map/ppermute | solution.py:29
  62.1 4.5 %collective-permute-start.13 = (f32[2,512]{1,0:T(2,128)S(1)}, f32[2,512]{1,0:T(2,128)S(1)}, u32[]{:S(2)}, u32[]{:S(2)}) collective-permute-start(f32[2,512]{1,0:T(2,128)S(1)} %pad_maximum_fusion.6), channel_id=1, source_target_pairs={{0,2},{1,3},{2,0},{3,1},{4,6},{5,7},{6,4},{7,5},{8,10},{9,11},{10,... | collective-permute-start | bytes 12296 | tf_op jit(solution)/shard_map/ppermute | solution.py:29
  64.1 5.4 %collective-permute-start.14 = (f32[2,512]{1,0:T(2,128)S(1)}, f32[2,512]{1,0:T(2,128)S(1)}, u32[]{:S(2)}, u32[]{:S(2)}) collective-permute-start(f32[2,512]{1,0:T(2,128)S(1)} %pad_maximum_fusion.6), channel_id=1, source_target_pairs={{0,3},{1,2},{2,1},{3,0},{4,7},{5,6},{6,5},{7,4},{8,11},{9,10},{10,... | collective-permute-start | bytes 12296 | tf_op jit(solution)/shard_map/ppermute | solution.py:29
  70.4 1.2 collective-permute-start.15
  71.6 3.7 %collective-permute-start.16 = (f32[1,2048]{1,0:T(1,128)S(1)}, f32[1,2048]{1,0:T(1,128)S(1)}, u32[]{:S(2)}, u32[]{:S(2)}) collective-permute-start(f32[1,2048]{1,0:T(1,128)S(1)} %add.92.refs_0_), channel_id=1, source_target_pairs={{0,8},{4,12},{8,0},{12,4},{16,24},{20,28},{24,16},{28,20},{1,9},{5... | collective-permute-start | bytes 24584 | tf_op jit(solution)/shard_map/ppermute | solution.py:29
  72.2 3.7 %collective-permute-start.17 = (f32[1,2048]{1,0:T(1,128)S(1)}, f32[1,2048]{1,0:T(1,128)S(1)}, u32[]{:S(2)}, u32[]{:S(2)}) collective-permute-start(f32[1,2048]{1,0:T(1,128)S(1)} %add.92.refs_0_), channel_id=1, source_target_pairs={{0,16},{4,20},{8,24},{12,28},{16,0},{20,4},{24,8},{28,12},{1,17},{... | collective-permute-start | bytes 24584 | tf_op jit(solution)/shard_map/ppermute | solution.py:29
  72.8 4.5 %collective-permute-start.18 = (f32[1,2048]{1,0:T(1,128)S(1)}, f32[1,2048]{1,0:T(1,128)S(1)}, u32[]{:S(2)}, u32[]{:S(2)}) collective-permute-start(f32[1,2048]{1,0:T(1,128)S(1)} %add.92.refs_0_), channel_id=1, source_target_pairs={{0,24},{4,28},{8,16},{12,20},{16,8},{20,12},{24,0},{28,4},{1,25},{... | collective-permute-start | bytes 24584 | tf_op jit(solution)/shard_map/ppermute | solution.py:29
  78.0 4.5 %collective-permute-start.19 = (f32[1,512]{1,0:T(1,128)S(1)}, f32[1,512]{1,0:T(1,128)S(1)}, u32[]{:S(2)}, u32[]{:S(2)}) collective-permute-start(f32[1,512]{1,0:T(1,128)S(1)} %get-tuple-element.30.refs_0_), channel_id=1, source_target_pairs={{0,1},{1,0},{2,3},{3,2},{4,5},{5,4},{6,7},{7,6},{8,9},{9,8},{10,11... | collective-permute-start | bytes 6152 | tf_op jit(solution)/shard_map/ppermute | solution.py:29
  78.2 4.5 %collective-permute-start.20 = (f32[1,512]{1,0:T(1,128)S(1)}, f32[1,512]{1,0:T(1,128)S(1)}, u32[]{:S(2)}, u32[]{:S(2)}) collective-permute-start(f32[1,512]{1,0:T(1,128)S(1)} %get-tuple-element.30.refs_0_), channel_id=1, source_target_pairs={{0,2},{1,3},{2,0},{3,1},{4,6},{5,7},{6,4},{7,5},{8,10},{9,11},{10,... | collective-permute-start | bytes 6152 | tf_op jit(solution)/shard_map/ppermute | solution.py:29
  80.0 5.4 %collective-permute-start.21 = (f32[1,512]{1,0:T(1,128)S(1)}, f32[1,512]{1,0:T(1,128)S(1)}, u32[]{:S(2)}, u32[]{:S(2)}) collective-permute-start(f32[1,512]{1,0:T(1,128)S(1)} %get-tuple-element.30.refs_0_), channel_id=1, source_target_pairs={{0,3},{1,2},{2,1},{3,0},{4,7},{5,6},{6,5},{7,4},{8,11},{9,10},{10,... | collective-permute-start | bytes 6152 | tf_op jit(solution)/shard_map/ppermute | solution.py:29
  86.1 1.2 collective-permute-start.22
  87.3 3.7 %collective-permute-start.23 = (f32[1,2048]{1,0:T(1,128)S(1)}, f32[1,2048]{1,0:T(1,128)S(1)}, u32[]{:S(2)}, u32[]{:S(2)}) collective-permute-start(f32[1,2048]{1,0:T(1,128)S(1)} %add.93.refs_0_), channel_id=1, source_target_pairs={{0,8},{4,12},{8,0},{12,4},{16,24},{20,28},{24,16},{28,20},{1,9},{5... | collective-permute-start | bytes 24584 | tf_op jit(solution)/shard_map/ppermute | solution.py:29
  88.9 3.7 %collective-permute-start.24 = (f32[1,2048]{1,0:T(1,128)S(1)}, f32[1,2048]{1,0:T(1,128)S(1)}, u32[]{:S(2)}, u32[]{:S(2)}) collective-permute-start(f32[1,2048]{1,0:T(1,128)S(1)} %add.93.refs_0_), channel_id=1, source_target_pairs={{0,16},{4,20},{8,24},{12,28},{16,0},{20,4},{24,8},{28,12},{1,17},{... | collective-permute-start | bytes 24584 | tf_op jit(solution)/shard_map/ppermute | solution.py:29
  90.3 4.5 %collective-permute-start.25 = (f32[1,2048]{1,0:T(1,128)S(1)}, f32[1,2048]{1,0:T(1,128)S(1)}, u32[]{:S(2)}, u32[]{:S(2)}) collective-permute-start(f32[1,2048]{1,0:T(1,128)S(1)} %add.93.refs_0_), channel_id=1, source_target_pairs={{0,24},{4,28},{8,16},{12,20},{16,8},{20,12},{24,0},{28,4},{1,25},{... | collective-permute-start | bytes 24584 | tf_op jit(solution)/shard_map/ppermute | solution.py:29
  95.5 4.5 %collective-permute-start.26 = (f32[1,512]{1,0:T(1,128)S(1)}, f32[1,512]{1,0:T(1,128)S(1)}, u32[]{:S(2)}, u32[]{:S(2)}) collective-permute-start(f32[1,512]{1,0:T(1,128)S(1)} %get-tuple-element.32.refs_0_), channel_id=1, source_target_pairs={{0,1},{1,0},{2,3},{3,2},{4,5},{5,4},{6,7},{7,6},{8,9},{9,8},{10,11... | collective-permute-start | bytes 6152 | tf_op jit(solution)/shard_map/ppermute | solution.py:29
  95.6 4.6 %collective-permute-start.27 = (f32[1,512]{1,0:T(1,128)S(1)}, f32[1,512]{1,0:T(1,128)S(1)}, u32[]{:S(2)}, u32[]{:S(2)}) collective-permute-start(f32[1,512]{1,0:T(1,128)S(1)} %get-tuple-element.32.refs_0_), channel_id=1, source_target_pairs={{0,2},{1,3},{2,0},{3,1},{4,6},{5,7},{6,4},{7,5},{8,10},{9,11},{10,... | collective-permute-start | bytes 6152 | tf_op jit(solution)/shard_map/ppermute | solution.py:29
  98.6 5.4 %collective-permute-start.28 = (f32[1,512]{1,0:T(1,128)S(1)}, f32[1,512]{1,0:T(1,128)S(1)}, u32[]{:S(2)}, u32[]{:S(2)}) collective-permute-start(f32[1,512]{1,0:T(1,128)S(1)} %get-tuple-element.32.refs_0_), channel_id=1, source_target_pairs={{0,3},{1,2},{2,1},{3,0},{4,7},{5,6},{6,5},{7,4},{8,11},{9,10},{10,... | collective-permute-start | bytes 6152 | tf_op jit(solution)/shard_map/ppermute | solution.py:29
  105.9 3.7 %collective-permute-start.30 = (f32[1,2048]{1,0:T(1,128)S(1)}, f32[1,2048]{1,0:T(1,128)S(1)}, u32[]{:S(2)}, u32[]{:S(2)}) collective-permute-start(f32[1,2048]{1,0:T(1,128)S(1)} %add.94.refs_0_), channel_id=1, source_target_pairs={{0,8},{4,12},{8,0},{12,4},{16,24},{20,28},{24,16},{28,20},{1,9},{5... | collective-permute-start | bytes 24584 | tf_op jit(solution)/shard_map/ppermute | solution.py:29
  106.5 3.7 %collective-permute-start.31 = (f32[1,2048]{1,0:T(1,128)S(1)}, f32[1,2048]{1,0:T(1,128)S(1)}, u32[]{:S(2)}, u32[]{:S(2)}) collective-permute-start(f32[1,2048]{1,0:T(1,128)S(1)} %add.94.refs_0_), channel_id=1, source_target_pairs={{0,16},{4,20},{8,24},{12,28},{16,0},{20,4},{24,8},{28,12},{1,17},{... | collective-permute-start | bytes 24584 | tf_op jit(solution)/shard_map/ppermute | solution.py:29
  107.1 4.5 %collective-permute-start.32 = (f32[1,2048]{1,0:T(1,128)S(1)}, f32[1,2048]{1,0:T(1,128)S(1)}, u32[]{:S(2)}, u32[]{:S(2)}) collective-permute-start(f32[1,2048]{1,0:T(1,128)S(1)} %add.94.refs_0_), channel_id=1, source_target_pairs={{0,24},{4,28},{8,16},{12,20},{16,8},{20,12},{24,0},{28,4},{1,25},{... | collective-permute-start | bytes 24584 | tf_op jit(solution)/shard_map/ppermute | solution.py:29
  112.3 4.5 %collective-permute-start.33 = (f32[1,512]{1,0:T(1,128)S(1)}, f32[1,512]{1,0:T(1,128)S(1)}, u32[]{:S(2)}, u32[]{:S(2)}) collective-permute-start(f32[1,512]{1,0:T(1,128)S(1)} %get-tuple-element.34.refs_0_), channel_id=1, source_target_pairs={{0,1},{1,0},{2,3},{3,2},{4,5},{5,4},{6,7},{7,6},{8,9},{9,8},{10,11... | collective-permute-start | bytes 6152 | tf_op jit(solution)/shard_map/ppermute | solution.py:29
  112.4 4.5 %collective-permute-start.34 = (f32[1,512]{1,0:T(1,128)S(1)}, f32[1,512]{1,0:T(1,128)S(1)}, u32[]{:S(2)}, u32[]{:S(2)}) collective-permute-start(f32[1,512]{1,0:T(1,128)S(1)} %get-tuple-element.34.refs_0_), channel_id=1, source_target_pairs={{0,2},{1,3},{2,0},{3,1},{4,6},{5,7},{6,4},{7,5},{8,10},{9,11},{10,... | collective-permute-start | bytes 6152 | tf_op jit(solution)/shard_map/ppermute | solution.py:29
  114.3 5.4 %collective-permute-start.35 = (f32[1,512]{1,0:T(1,128)S(1)}, f32[1,512]{1,0:T(1,128)S(1)}, u32[]{:S(2)}, u32[]{:S(2)}) collective-permute-start(f32[1,512]{1,0:T(1,128)S(1)} %get-tuple-element.34.refs_0_), channel_id=1, source_target_pairs={{0,3},{1,2},{2,1},{3,0},{4,7},{5,6},{6,5},{7,4},{8,11},{9,10},{10,... | collective-permute-start | bytes 6152 | tf_op jit(solution)/shard_map/ppermute | solution.py:29
  127.3 2.7 %collective-permute-start.36 = (bf16[256,2048]{1,0:T(8,128)(2,1)S(1)}, bf16[256,2048]{1,0:T(8,128)(2,1)S(1)}, u32[]{:S(2)}, u32[]{:S(2)}) collective-permute-start(bf16[256,2048]{1,0:T(8,128)(2,1)S(1)} %get-tuple-element.38), channel_id=1, source_target_pairs={{0,4},{4,0},{8,12},{12,8},{16,20},{20,16},{24,28},{28,24},{1,5},{5... | collective-permute-start | bytes 3145736 | tf_op jit(solution)/shard_map/ppermute | solution.py:29
  127.3 15.6 %collective-permute-start.38 = (bf16[512,512]{1,0:T(8,128)(2,1)S(1)}, bf16[512,512]{1,0:T(8,128)(2,1)S(1)}, u32[]{:S(2)}, u32[]{:S(2)}) collective-permute-start(bf16[512,512]{1,0:T(8,128)(2,1)S(1)} %get-tuple-element.42), channel_id=1, source_target_pairs={{0,1},{1,0},{2,3},{3,2},{4,5},{5,4},{6,7},{7,6},{8,9},{9,8},{10,11... | collective-permute-start | bytes 1572872 | tf_op jit(solution)/shard_map/ppermute | solution.py:29
  142.7 28.0 %collective-permute-start.41 = (bf16[256,2048]{1,0:T(8,128)(2,1)S(1)}, bf16[256,2048]{1,0:T(8,128)(2,1)S(1)}, u32[]{:S(2)}, u32[]{:S(2)}) collective-permute-start(bf16[256,2048]{1,0:T(8,128)(2,1)S(1)} %get-tuple-element.46), channel_id=1, source_target_pairs={{0,4},{4,0},{8,12},{12,8},{16,20},{20,16},{24,28},{28,24},{1,5},{5... | collective-permute-start | bytes 3145736 | tf_op jit(solution)/shard_map/ppermute | solution.py:29
  142.9 25.1 %collective-permute-start.37 = (bf16[512,512]{1,0:T(8,128)(2,1)S(1)}, bf16[512,512]{1,0:T(8,128)(2,1)S(1)}, u32[]{:S(2)}, u32[]{:S(2)}) collective-permute-start(bf16[512,512]{1,0:T(8,128)(2,1)S(1)} %slice_bitcast_fusion), channel_id=1, source_target_pairs={{0,1},{1,0},{2,3},{3,2},{4,5},{5,4},{6,7},{7,6},{8,9},{9,8},{10,11... | collective-permute-start | bytes 1572872 | tf_op jit(solution)/shard_map/ppermute | solution.py:29
  143.1 26.5 %collective-permute-start.39 = (bf16[512,512]{1,0:T(8,128)(2,1)S(1)}, bf16[512,512]{1,0:T(8,128)(2,1)S(1)}, u32[]{:S(2)}, u32[]{:S(2)}) collective-permute-start(bf16[512,512]{1,0:T(8,128)(2,1)S(1)} %fusion.6), channel_id=1, source_target_pairs={{0,2},{1,3},{2,0},{3,1},{4,6},{5,7},{6,4},{7,5},{8,10},{9,11},{10,... | collective-permute-start | bytes 1572872 | tf_op jit(solution)/shard_map/ppermute | solution.py:29
  147.5 23.6 %collective-permute-start.47 = (bf16[128,2048]{1,0:T(8,128)(2,1)S(1)}, bf16[128,2048]{1,0:T(8,128)(2,1)S(1)}, u32[]{:S(2)}, u32[]{:S(2)}) collective-permute-start(bf16[128,2048]{1,0:T(8,128)(2,1)S(1)} %get-tuple-element.40.refs_5_), channel_id=1, source_target_pairs={{0,16},{4,20},{8,24},{12,28},{16,0},{20,4},{24,8},{28,12},{1,17},{... | collective-permute-start | bytes 1572872 | tf_op jit(solution)/shard_map/ppermute | solution.py:29
  148.9 24.8 %collective-permute-start.44 = (bf16[128,2048]{1,0:T(8,128)(2,1)S(1)}, bf16[128,2048]{1,0:T(8,128)(2,1)S(1)}, u32[]{:S(2)}, u32[]{:S(2)}) collective-permute-start(bf16[128,2048]{1,0:T(8,128)(2,1)S(1)} %get-tuple-element.39.refs_4_), channel_id=1, source_target_pairs={{0,8},{4,12},{8,0},{12,4},{16,24},{20,28},{24,16},{28,20},{1,9},{5... | collective-permute-start | bytes 1572872 | tf_op jit(solution)/shard_map/ppermute | solution.py:29
  168.0 5.3 %collective-permute-start.43 = (bf16[256,2048]{1,0:T(8,128)(2,1)S(1)}, bf16[256,2048]{1,0:T(8,128)(2,1)S(1)}, u32[]{:S(2)}, u32[]{:S(2)}) collective-permute-start(bf16[256,2048]{1,0:T(8,128)(2,1)S(1)} %get-tuple-element.48), channel_id=1, source_target_pairs={{0,4},{4,0},{8,12},{12,8},{16,20},{20,16},{24,28},{28,24},{1,5},{5... | collective-permute-start | bytes 3145736 | tf_op jit(solution)/shard_map/ppermute | solution.py:29
  169.6 6.3 %collective-permute-start.40 = (bf16[256,2048]{1,0:T(8,128)(2,1)S(1)}, bf16[256,2048]{1,0:T(8,128)(2,1)S(1)}, u32[]{:S(2)}, u32[]{:S(2)}) collective-permute-start(bf16[256,2048]{1,0:T(8,128)(2,1)S(1)} %get-tuple-element.44), channel_id=1, source_target_pairs={{0,4},{4,0},{8,12},{12,8},{16,20},{20,16},{24,28},{28,24},{1,5},{5... | collective-permute-start | bytes 3145736 | tf_op jit(solution)/shard_map/ppermute | solution.py:29
  171.2 14.8 %collective-permute-start.48 = (bf16[128,2048]{1,0:T(8,128)(2,1)S(1)}, bf16[128,2048]{1,0:T(8,128)(2,1)S(1)}, u32[]{:S(2)}, u32[]{:S(2)}) collective-permute-start(bf16[128,2048]{1,0:T(8,128)(2,1)S(1)} %fusion), channel_id=1, source_target_pairs={{0,8},{4,12},{8,0},{12,4},{16,24},{20,28},{24,16},{28,20},{1,9},{5... | collective-permute-start | bytes 1572872 | tf_op jit(solution)/shard_map/ppermute | solution.py:29
  172.7 24.1 %collective-permute-start.42 = (bf16[128,2048]{1,0:T(8,128)(2,1)S(1)}, bf16[128,2048]{1,0:T(8,128)(2,1)S(1)}, u32[]{:S(2)}, u32[]{:S(2)}) collective-permute-start(bf16[128,2048]{1,0:T(8,128)(2,1)S(1)} %slice.132), channel_id=1, source_target_pairs={{0,8},{4,12},{8,0},{12,4},{16,24},{20,28},{24,16},{28,20},{1,9},{5... | collective-permute-start | bytes 1572872 | tf_op jit(solution)/shard_map/ppermute | solution.py:29
  173.8 23.0 %collective-permute-start.45 = (bf16[128,2048]{1,0:T(8,128)(2,1)S(1)}, bf16[128,2048]{1,0:T(8,128)(2,1)S(1)}, u32[]{:S(2)}, u32[]{:S(2)}) collective-permute-start(bf16[128,2048]{1,0:T(8,128)(2,1)S(1)} %fusion.3), channel_id=1, source_target_pairs={{0,16},{4,20},{8,24},{12,28},{16,0},{20,4},{24,8},{28,12},{1,17},{... | collective-permute-start | bytes 1572872 | tf_op jit(solution)/shard_map/ppermute | solution.py:29
  175.3 23.6 %collective-permute-start.46 = (bf16[128,2048]{1,0:T(8,128)(2,1)S(1)}, bf16[128,2048]{1,0:T(8,128)(2,1)S(1)}, u32[]{:S(2)}, u32[]{:S(2)}) collective-permute-start(bf16[128,2048]{1,0:T(8,128)(2,1)S(1)} %slice.131), channel_id=1, source_target_pairs={{0,16},{4,20},{8,24},{12,28},{16,0},{20,4},{24,8},{28,12},{1,17},{... | collective-permute-start | bytes 1572872 | tf_op jit(solution)/shard_map/ppermute | solution.py:29
  (4 other events, 20.2 us)

commit v6 on v5

--- a/solution.py
+++ b/solution.py
@@ -52,8 +52,6 @@
         for b in second:
             top, bottom = cut(held[a][0])[0], cut(held[b][0])[1]
             held[a | b] = [flip(top, "sample", b), flip(bottom, "sample", a)]
-    for mask in list(held):
-        held[mask | 1] = [flip(part, "sample", 1) for part in held[mask]]
     return held
 
 
@@ -110,8 +108,13 @@
     total_ref[...] = jnp.sum(jnp.transpose(partial[...]), axis=0, keepdims=True)
 
 
-def column_kernel(count, student_ref, scale_ref, *refs):
-    part_refs, (total_ref, inverse) = refs[:count], refs[count:]
+def turn_kernel(blocks_ref, turned_ref):
+    for i in range(blocks_ref.shape[0]):
+        turned_ref[i] = jnp.transpose(blocks_ref[i])
+
+
+def column_kernel(count, early, student_ref, scale_ref, *refs):
+    part_refs, (total_ref, inverse) = refs[:count], refs[count + early :]
     mass = part_refs[0][...]
     for ref in part_refs[1:]:
         mass = mass + ref[...]
@@ -135,9 +138,10 @@
         total_ref[:, at] = jnp.sum(value, axis=0, keepdims=True) * scale_ref[:, at]
 
 
-def split_by_core(result, core, depth):
-    top, bottom = result[:depth], result[depth:]
-    return jnp.where(core == 0, top, bottom), jnp.where(core == 0, bottom, top)
+def head_products(turned_ref, core, depth, grad_ref, at, mine_ref, theirs_ref):
+    for where, out_ref in ((core, mine_ref), (1 - core, theirs_ref)):
+        left = turned_ref[pl.ds(pl.multiple_of(where * depth, depth), depth), :]
+        out_ref[:, at] = jnp.dot(left, grad_ref[:, at], preferred_element_type=f32).astype(bf16)
 
 
 def gradient_kernel(count, depth, far, masks, student_ref, slope_ref, scale_ref, students_ref, turned_ref, *refs):
@@ -155,21 +159,14 @@
     tile = min(256, columns)
     turned = turned_ref.at[place ^ chip ^ far]
 
-    def body(i, carry):
-        for j in range(0, tile, LANES):
-            at = pl.ds(pl.multiple_of(i * tile + j, LANES), LANES)
+    for i in range(0, columns, tile):
+        for j in range(i, i + tile, LANES):
+            at = slice(j, j + LANES)
             student = student_ref[:, at]
             target = (student * student * scale_ref[:, at] * inverse[...]).astype(bf16)
             targets_ref[:, at] = target
             grad_ref[:, at] = ((student * students[...] - wide(target)) * wide(slope_ref[:, at])).astype(bf16)
-        at = pl.ds(pl.multiple_of(i * tile, tile), tile)
-        result = jnp.dot(turned[...], grad_ref[:, at], preferred_element_type=f32)
-        mine, theirs = split_by_core(result, core, depth)
-        mine_ref[:, at] = mine.astype(bf16)
-        theirs_ref[:, at] = theirs.astype(bf16)
-        return carry
-
-    lax.fori_loop(0, columns // tile, body, 0)
+        head_products(turned, core, depth, grad_ref, slice(i, i + tile), mine_ref, theirs_ref)
     for mask, ref in zip(masks, head_refs):
 
         @pl.when((chip ^ mask) == (place ^ (groups - 1)))
@@ -187,16 +184,8 @@
     for index, mask in enumerate(near):
         mine_ref, theirs_ref = pairs[2 * index], pairs[2 * index + 1]
         turned = turned_ref.at[place ^ chip ^ mask]
-
-        def body(i, carry):
-            at = pl.ds(pl.multiple_of(i * tile, tile), tile)
-            result = jnp.dot(turned[...], grad_ref[:, at], preferred_element_type=f32)
-            mine, theirs = split_by_core(result, core, depth)
-            mine_ref[:, at] = mine.astype(bf16)
-            theirs_ref[:, at] = theirs.astype(bf16)
-            return carry
-
-        lax.fori_loop(0, columns // tile, body, 0)
+        for i in range(0, columns, tile):
+            head_products(turned, core, depth, grad_ref, slice(i, i + tile), mine_ref, theirs_ref)
     for mask, ref in zip(masks, head_refs):
         shares_ref[chip ^ mask ^ place] = matmul(grad_ref[...], ref[...], ((1,), (1,))).astype(bf16)
 
@@ -218,7 +207,10 @@
     order = [0] + first + second + [a | b for a in first for b in second]
     heads, logits = {}, None
     for mask in order:
-        same, other = pieces[mask], pieces[mask | 1]
+        same = pieces[mask]
+        if len(same) > 1:
+            same = list(lax.optimization_barrier((logits, *same))[1:])
+        other = [flip(part, "sample", 1) for part in same]
         parts = [jnp.where(core == 0, s, o) for s, o in zip(same, other)]
         parts += [jnp.where(core == 0, o, s) for s, o in zip(same, other)]
         heads[mask] = lax.optimization_barrier(jnp.concatenate(parts, axis=0))
@@ -231,26 +223,28 @@
     slope = (1.0 - tanh * tanh).astype(bf16)
     sums = jnp.stack([jnp.sum(student, axis=1), jnp.sum(student * student, axis=1)])
     student, slope, sums = lax.optimization_barrier((student, slope, sums))
-    turned = lax.optimization_barrier(jnp.transpose(blocks, (0, 2, 1)))
+    (turned,) = call(turn_kernel, [((groups, width, rows), bf16)], [blocks])
 
     def row_parts(value):
-        return [value] + [flip(value, "cls", mask) for mask in range(1, groups)]
+        return [value] + [flip(value, "cls", mask) for mask in range(groups - 1, 0, -1)]
 
     def column_parts(value):
         value = value + flip(value, "sample", 1)
-        return [value] + [flip(value, "sample", mask) for mask in range(2, samples, 2)]
+        return [value] + [flip(value, "sample", mask) for mask in range(samples - 2, 0, -2)]
 
     ceiling = (wide(class_cap) * ratio)[None]
     parts = row_parts(sums)
     students_mass = sum([part[0:1] for part in parts[1:]], parts[0][0:1])
     parts = [part[1:2] for part in parts]
     scale = jnp.ones((1, classes), f32)
-    for _ in range(ITERS):
+    for iteration in range(ITERS):
+        early = [turned] if iteration == 0 else []
         (mass,) = call(
-            functools.partial(column_kernel, len(parts)),
+            functools.partial(column_kernel, len(parts), len(early)),
             [((1, classes), f32)],
             [student, scale] + parts,
             [pltpu.VMEM((rows, LANES), f32)],
+            early,
         )
         sent = column_parts(mass)
         scale, mass = call(
@@ -291,26 +285,34 @@
         extra=halves,
     )
     shares = results[-1]
+    arrived = [part for parts in extra.values() for part in parts]
+    theirs = lax.optimization_barrier((*results[1:-1:2], *arrived))
+    arrived = iter(theirs[len(near) :])
+    extra = {at: [next(arrived) for _ in parts] for at, parts in extra.items()}
     mixed = {
-        2 * mask: wide(results[2 * i]) + wide(flip(results[2 * i + 1], "sample", 1)) for i, mask in enumerate(near)
+        2 * mask: wide(results[2 * i]) + wide(flip(theirs[i], "sample", 1)) for i, mask in enumerate(near)
     }
     for a, b in diagonal[:-1]:
         send_diagonal(a, b, *cut(mixed[a | b].astype(bf16)))
 
-    total = wide(shares[0]) + wide(flip(shares[1], "cls", 1))
+    returned = [flip(shares[1], "cls", 1)]
     for mask in range(2, groups, 2):
         received = share_from[mask] if mask in share_from else flip(shares[mask | 1], "cls", 1)
-        total = total + wide(flip((wide(shares[mask]) + wide(received)).astype(bf16), "cls", mask))
-    grad_features = total.astype(bf16)
+        returned.append(flip((wide(shares[mask]) + wide(received)).astype(bf16), "cls", mask))
 
     halves = list(cut(mixed[0]))
+    sent = {}
     for late in (False, True):
         for mask in first + second:
             for part, value in enumerate(cut(mixed[mask])):
                 if ((mask, part) in extra) == late:
                     for more in extra.get((mask, part), []):
                         value = value + wide(more)
-                    halves[part] = halves[part] + wide(flip(value.astype(bf16), "sample", mask))
+                    sent[mask, part] = value.astype(bf16)
+    for (mask, part), value in sent.items():
+        halves[part] = halves[part] + wide(flip(value, "sample", mask))
+    returned = lax.optimization_barrier((*returned, *sent.values()))[: len(returned)]
+    grad_features = sum([wide(value) for value in returned], wide(shares[0])).astype(bf16)
     grad_head = jnp.concatenate(halves, axis=0).astype(bf16)
     return (targets, grad_features, grad_head)
 

time: 201 us -> 207 us (1.030)
  waiting for transfers between devices: 102 us -> 110 us
  Pallas kernels: 23.8 us -> 16.5 us
  starting transfers between devices: 51.2 us -> 53.6 us
    ppermute x49, waiting for transfers between devices: 102 us -> 110 us  [flip(): lax.ppermute(value, axis, [(i, i ^ mask) for i in range(lax.axis_size(axi...]
    pallas_call x8 -> x9, Pallas kernels: 23.8 us -> 16.5 us  [call(): pl.pallas_call(kernel, out_shape=tuple((pltpu.VMEM(shape, dtype) for shap...]
    ppermute x49, starting transfers between devices: 51.2 us -> 53.6 us  [flip(): lax.ppermute(value, axis, [(i, i ^ mask) for i in range(lax.axis_size(axi...]
  transfers between devices with their start and end apart: 49 -> 49, of which waited for: 30 -> 33; matrix products, arithmetic and copies ran while one was open for 8% -> 9% of each run, Pallas kernels for 6% -> 4%
where the time goes in v6:
time: 207 us; the launch traced here: 206 us
  waiting for transfers between devices  110 us (53%)
  starting transfers between devices  53.6 us (26%)
  Pallas kernels  16.5 us (8%)
  other arithmetic  12.6 us (6%)
  matrix products  8.15 us (4%)
  local copies, waits for them, and re-layouts  4.58 us (2%)
    ppermute x49, waiting for transfers between devices, flip(): lax.ppermute(value, axis, [(i, i ^ mask) for i in range(lax.axis_size(axi...  110 us
    ppermute x49, starting transfers between devices, flip(): lax.ppermute(value, axis, [(i, i ^ mask) for i in range(lax.axis_size(axi...  53.6 us
    pallas_call x9, Pallas kernels, call(): pl.pallas_call(kernel, out_shape=tuple((pltpu.VMEM(shape, dtype) for shap...  16.5 us
    dot_general x4, matrix products, matmul(): lax.dot_general(left, right, (dims, ((), ())), preferred_element_type=f32)  8.15 us
    select_n x5, other arithmetic, per_device(): parts = [jnp.where(core == 0, s, o) for s, o in zip(same, other)]  6.01 us
  transfers between devices with their start and end apart: 49, of which 33 were waited for; matrix products, arithmetic and copies ran while one was open for 9% of the time, Pallas kernels for 4%

profile of v6, /device:TPU:0, one launch (start us, length us, event | category | flops | bytes accessed | tf_op | source)
XLA Modules:
  0.0 206.2 jit_solution(16301563816590776327)
XLA Ops:
  0.6 3.0 %collective-permute-start.6 = (bf16[256,2048]{1,0:T(8,128)(2,1)}, bf16[256,2048]{1,0:T(8,128)(2,1)S(1)}, u32[]{:S(2)}, u32[]{:S(2)}) collective-permute-start(bf16[256,2048]{1,0:T(8,128)(2,1)} %param.4), channel_id=1, source_target_pairs={{0,16},{4,20},{8,24},{12,28},{16,0},{20,4},{24,8},{28,12},{1,17},{... | collective-permute-start | bytes 3145736 | tf_op jit(solution)/shard_map/ppermute | solution.py:29
  3.7 2.6 %collective-permute-start.1 = (bf16[512,512]{1,0:T(8,128)(2,1)}, bf16[512,512]{1,0:T(8,128)(2,1)}, u32[]{:S(2)}, u32[]{:S(2)}) collective-permute-start(bf16[512,512]{1,0:T(8,128)(2,1)} %param.3), channel_id=1, source_target_pairs={{0,2},{1,3},{2,0},{3,1},{4,6},{5,7},{6,4},{7,5},{8,10},{9,11},{10,... | collective-permute-start | bytes 1572872 | tf_op jit(solution)/shard_map/ppermute | solution.py:29
  6.3 1.5 collective-permute-start.4
  7.7 1.6 collective-permute-start
  9.3 21.2 %collective-permute-done.1 = bf16[512,512]{1,0:T(8,128)(2,1)} collective-permute-done((bf16[512,512]{1,0:T(8,128)(2,1)}, bf16[512,512]{1,0:T(8,128)(2,1)}, u32[]{:S(2)}, u32[]{:S(2)}) %collective-permute-start.1) | collective-permute-done | bytes 524320 | tf_op jit(solution)/shard_map/ppermute | solution.py:29
  32.8 1.5 collective-permute-start.9
  35.9 8.3 %collective-permute-done.2 = bf16[512,512]{1,0:T(8,128)(2,1)S(1)} collective-permute-done((bf16[512,512]{1,0:T(8,128)(2,1)}, bf16[512,512]{1,0:T(8,128)(2,1)S(1)}, u32[]{:S(2)}, u32[]{:S(2)}) %collective-permute-start.2) | collective-permute-done | bytes 524320 | tf_op jit(solution)/shard_map/ppermute | solution.py:29
  44.3 1.5 pad_maximum_fusion.blocks_ref
  47.4 2.1 %broadcast_select_fusion.3 = (bf16[256,2048]{1,0:T(8,128)(2,1)S(1)}, bf16[256,2048]{1,0:T(8,128)(2,1)S(1)}) fusion(bf16[256,2048]{1,0:T(8,128)(2,1)} %collective-permute-done.4, bf16[256,2048]{1,0:T(8,128)(2,1)S(1)} %collective-permute-done.5, pred[]{:T(512)S(6)} %eq.4), kind=kLoop, calls=%fused_computation.35 | loop fusion | flops 1048576 | bytes 4194305 | tf_op jit(solution)/shard_map/jit(_where)/select_n | solution.py:214
  51.1 3.3 %add_add_fusion = f32[512,2048]{1,0:T(8,128)} fusion(f32[512,2048]{1,0:T(8,128)S(1)} %fusion.13, f32[512,2048]{1,0:T(8,128)S(1)} %fusion.11, bf16[512,2048]{1,0:T(8,128)(2,1)S(1)} %pad_maximum_fusion.3.refs_6_.refs_2_, bf16[4,512,512]{2,1,0:T(8,128)(2,1)S(1)} %pad_maximum_fusion.blocks_ref, s32[]{:T(128)S(6)} %select_n.81), kind=kOutput, calls=%fused_computation.4 | convolution fusion | flops 1075838976 | bytes 15204356 | tf_op jit(solution)/shard_map/dot_general | solution.py:25
  54.9 1.6 collective-permute-done.10
  60.9 2.4 %fusion.23 = (f32[512]{0:T(512)S(1)}, f32[512]{0:T(512)S(1)}, bf16[512,2048]{1,0:T(8,128)(2,1)S(1)}, f32[512,2048]{1,0:T(8,128)S(1)}) fusion(f32[512,2048]{1,0:T(8,128)S(1)} %copy-done.6, bf16[512,2048]{1,0:T(8,128)(2,1)S(1)} %pad_maximum_fusion.4.refs_7_.refs_3_, bf16[4,512,512]{2,1,0:T(8,128)(2,1)S(1)} %copy-done.5, s32[]{:T(128)S(6)} %select_n.84), kind=kOutput, calls=%fused_computation.62 | convolution fusion | flops 1083177984 | bytes 13111300 | tf_op jit(solution)/shard_map/dot_general | solution.py:25
  64.4 3.4 %collective-permute-start.13 = (f32[2,512]{1,0:T(2,128)S(1)}, f32[2,512]{1,0:T(2,128)S(1)}, u32[]{:S(2)}, u32[]{:S(2)}) collective-permute-start(f32[2,512]{1,0:T(2,128)S(1)} %pad_maximum_fusion.6), channel_id=1, source_target_pairs={{0,2},{1,3},{2,0},{3,1},{4,6},{5,7},{6,4},{7,5},{8,10},{9,11},{10,... | collective-permute-start | bytes 12296 | tf_op jit(solution)/shard_map/ppermute | solution.py:29
  69.4 3.8 %collective-permute-done.12 = f32[2,512]{1,0:T(2,128)S(1)} collective-permute-done((f32[2,512]{1,0:T(2,128)S(1)}, f32[2,512]{1,0:T(2,128)S(1)}, u32[]{:S(2)}, u32[]{:S(2)}) %collective-permute-start.12) | collective-permute-done | bytes 4128 | tf_op jit(solution)/shard_map/ppermute | solution.py:29
  75.3 1.5 collective-permute-start.18
  77.3 1.5 collective-permute-start.16
  79.0 1.5 collective-permute-done.17.refs_2_
  80.5 1.4 collective-permute-done.16.refs_1_
  83.2 3.8 %collective-permute-start.19 = (f32[1,512]{1,0:T(1,128)S(1)}, f32[1,512]{1,0:T(1,128)S(1)}, u32[]{:S(2)}, u32[]{:S(2)}) collective-permute-start(f32[1,512]{1,0:T(1,128)S(1)} %get-tuple-element.41.refs_0_), channel_id=1, source_target_pairs={{0,3},{1,2},{2,1},{3,0},{4,7},{5,6},{6,5},{7,4},{8,11},{9,10},{10,... | collective-permute-start | bytes 6152 | tf_op jit(solution)/shard_map/ppermute | solution.py:29
  87.1 1.4 collective-permute-done.19.refs_1_
  91.2 1.4 collective-permute-start.24
  92.7 1.4 collective-permute-start.23
  94.9 2.3 %collective-permute-done.23.refs_1_ = f32[1,2048]{1,0:T(1,128)S(1)} collective-permute-done((f32[1,2048]{1,0:T(1,128)S(1)}, f32[1,2048]{1,0:T(1,128)S(1)}, u32[]{:S(2)}, u32[]{:S(2)}) %collective-permute-start.23) | collective-permute-done | bytes 8224 | tf_op jit(solution)/shard_map/ppermute | solution.py:29
  98.4 3.8 %collective-permute-start.27 = (f32[1,512]{1,0:T(1,128)S(1)}, f32[1,512]{1,0:T(1,128)S(1)}, u32[]{:S(2)}, u32[]{:S(2)}) collective-permute-start(f32[1,512]{1,0:T(1,128)S(1)} %get-tuple-element.43.refs_0_), channel_id=1, source_target_pairs={{0,2},{1,3},{2,0},{3,1},{4,6},{5,7},{6,4},{7,5},{8,10},{9,11},{10,... | collective-permute-start | bytes 6152 | tf_op jit(solution)/shard_map/ppermute | solution.py:29
  102.3 1.5 collective-permute-done.27.refs_2_
  103.8 3.8 %collective-permute-done.26.refs_1_ = f32[1,512]{1,0:T(1,128)S(1)} collective-permute-done((f32[1,512]{1,0:T(1,128)S(1)}, f32[1,512]{1,0:T(1,128)S(1)}, u32[]{:S(2)}, u32[]{:S(2)}) %collective-permute-start.26) | collective-permute-done | bytes 2080 | tf_op jit(solution)/shard_map/ppermute | solution.py:29
  109.6 1.5 collective-permute-start.32
  111.6 1.5 collective-permute-start.30
  113.3 1.5 collective-permute-done.31.refs_2_
  114.8 1.4 collective-permute-done.30.refs_1_
  117.5 3.8 %collective-permute-start.33 = (f32[1,512]{1,0:T(1,128)S(1)}, f32[1,512]{1,0:T(1,128)S(1)}, u32[]{:S(2)}, u32[]{:S(2)}) collective-permute-start(f32[1,512]{1,0:T(1,128)S(1)} %get-tuple-element.45.refs_0_), channel_id=1, source_target_pairs={{0,3},{1,2},{2,1},{3,0},{4,7},{5,6},{6,5},{7,4},{8,11},{9,10},{10,... | collective-permute-start | bytes 6152 | tf_op jit(solution)/shard_map/ppermute | solution.py:29
  121.4 1.4 collective-permute-done.33.refs_1_
  122.8 4.0 %shard_map.65 = (bf16[512,2048]{1,0:T(8,128)(2,1)S(1)}, bf16[512,2048]{1,0:T(8,128)(2,1)S(1)}, bf16[256,2048]{1,0:T(8,128)(2,1)S(1)}, bf16[256,2048]{1,0:T(8,128)(2,1)S(1)}, bf16[512,512]{1,0:T(8,128)(2,1)S(1)}) custom-call(f32[512,2048]{1,0:T(8,128)S(1)} %get-tuple-element.37.student_ref, bf16[512,2048]{1,0:T(8,128)(2,1)S(1)} %get-tuple-element.38.slope_ref, ...), custom_call_target="tpu_custom_call" | custom-call | flops 1 | bytes 1 | tf_op jit(solution)/shard_map/pallas_call | solution.py:74
  127.0 2.6 %collective-permute-done.36 = bf16[256,2048]{1,0:T(8,128)(2,1)S(1)} collective-permute-done((bf16[256,2048]{1,0:T(8,128)(2,1)S(1)}, bf16[256,2048]{1,0:T(8,128)(2,1)S(1)}, u32[]{:S(2)}, u32[]{:S(2)}) %collective-permute-start.36) | collective-permute-done | bytes 1048608 | tf_op jit(solution)/shard_map/ppermute | solution.py:29
  130.9 1.4 collective-permute-start.41
  132.3 7.8 %shard_map.66 = (bf16[256,2048]{1,0:T(8,128)(2,1)S(1)}, bf16[256,2048]{1,0:T(8,128)(2,1)S(1)}, bf16[256,2048]{1,0:T(8,128)(2,1)S(1)}, bf16[256,2048]{1,0:T(8,128...) custom-call(bf16[512,2048]{1,0:T(8,128)(2,1)S(1)} %get-tuple-element.47.g, ...), custom_call_target="tpu_custom_call" | custom-call | flops 1 | bytes 1 | tf_op jit(solution)/shard_map/pallas_call | solution.py:74
  140.0 4.1 %collective-permute-done.40 = bf16[128,2048]{1,0:T(8,128)(2,1)S(1)} collective-permute-done((bf16[128,2048]{1,0:T(8,128)(2,1)S(1)}, bf16[128,2048]{1,0:T(8,128)(2,1)S(1)}, u32[]{:S(2)}, u32[]{:S(2)}) %collective-permute-start.40) | collective-permute-done | bytes 524320 | tf_op jit(solution)/shard_map/ppermute | solution.py:29
  146.3 1.6 collective-permute-start.37
  148.0 11.3 %collective-permute-done.38 = bf16[512,512]{1,0:T(8,128)(2,1)S(1)} collective-permute-done((bf16[512,512]{1,0:T(8,128)(2,1)S(1)}, bf16[512,512]{1,0:T(8,128)(2,1)S(1)}, u32[]{:S(2)}, u32[]{:S(2)}) %collective-permute-start.38) | collective-permute-done | bytes 524320 | tf_op jit(solution)/shard_map/ppermute | solution.py:29
  159.4 2.4 %collective-permute-start.39 = (bf16[512,512]{1,0:T(8,128)(2,1)S(1)}, bf16[512,512]{1,0:T(8,128)(2,1)S(1)}, u32[]{:S(2)}, u32[]{:S(2)}) collective-permute-start(bf16[512,512]{1,0:T(8,128)(2,1)S(1)} %fusion.6), channel_id=1, source_target_pairs={{0,2},{1,3},{2,0},{3,1},{4,6},{5,7},{6,4},{7,5},{8,10},{9,11},{10,... | collective-permute-start | bytes 1572872 | tf_op jit(solution)/shard_map/ppermute | solution.py:29
  162.7 1.5 collective-permute-start.45
  164.4 1.4 collective-permute-start.48
  166.4 13.4 %collective-permute-done.37 = bf16[512,512]{1,0:T(8,128)(2,1)S(1)} collective-permute-done((bf16[512,512]{1,0:T(8,128)(2,1)S(1)}, bf16[512,512]{1,0:T(8,128)(2,1)S(1)}, u32[]{:S(2)}, u32[]{:S(2)}) %collective-permute-start.37) | collective-permute-done | bytes 524320 | tf_op jit(solution)/shard_map/ppermute | solution.py:29
  179.9 1.4 collective-permute-start.47
  181.3 3.6 %collective-permute-done.39 = bf16[512,512]{1,0:T(8,128)(2,1)S(1)} collective-permute-done((bf16[512,512]{1,0:T(8,128)(2,1)S(1)}, bf16[512,512]{1,0:T(8,128)(2,1)S(1)}, u32[]{:S(2)}, u32[]{:S(2)}) %collective-permute-start.39) | collective-permute-done | bytes 524320 | tf_op jit(solution)/shard_map/ppermute | solution.py:29
  184.9 1.5 collective-permute-start.46
  187.9 6.8 %collective-permute-done.47 = bf16[128,2048]{1,0:T(8,128)(2,1)S(1)} collective-permute-done((bf16[128,2048]{1,0:T(8,128)(2,1)S(1)}, bf16[128,2048]{1,0:T(8,128)(2,1)S(1)}, u32[]{:S(2)}, u32[]{:S(2)}) %collective-permute-start.47) | collective-permute-done | bytes 524320 | tf_op jit(solution)/shard_map/ppermute | solution.py:29
  194.7 10.0 %collective-permute-done.46 = bf16[128,2048]{1,0:T(8,128)(2,1)S(1)} collective-permute-done((bf16[128,2048]{1,0:T(8,128)(2,1)S(1)}, bf16[128,2048]{1,0:T(8,128)(2,1)S(1)}, u32[]{:S(2)}, u32[]{:S(2)}) %collective-permute-start.46) | collective-permute-done | bytes 524320 | tf_op jit(solution)/shard_map/ppermute | solution.py:29
  (115 shorter events, 35.9 us)
Async XLA Ops:
  0.6 30.5 %collective-permute-start.6 = (bf16[256,2048]{1,0:T(8,128)(2,1)}, bf16[256,2048]{1,0:T(8,128)(2,1)S(1)}, u32[]{:S(2)}, u32[]{:S(2)}) collective-permute-start(bf16[256,2048]{1,0:T(8,128)(2,1)} %param.4), channel_id=1, source_target_pairs={{0,16},{4,20},{8,24},{12,28},{16,0},{20,4},{24,8},{28,12},{1,17},{... | collective-permute-start | bytes 3145736 | tf_op jit(solution)/shard_map/ppermute | solution.py:29
  3.7 27.5 %collective-permute-start.3 = (bf16[256,2048]{1,0:T(8,128)(2,1)}, bf16[256,2048]{1,0:T(8,128)(2,1)S(1)}, u32[]{:S(2)}, u32[]{:S(2)}) collective-permute-start(bf16[256,2048]{1,0:T(8,128)(2,1)} %param.4), channel_id=1, source_target_pairs={{0,4},{4,0},{8,12},{12,8},{16,20},{20,16},{24,28},{28,24},{1,5},{5... | collective-permute-start | bytes 3145736 | tf_op jit(solution)/shard_map/ppermute | solution.py:29
  3.7 26.9 %collective-permute-start.1 = (bf16[512,512]{1,0:T(8,128)(2,1)}, bf16[512,512]{1,0:T(8,128)(2,1)}, u32[]{:S(2)}, u32[]{:S(2)}) collective-permute-start(bf16[512,512]{1,0:T(8,128)(2,1)} %param.3), channel_id=1, source_target_pairs={{0,2},{1,3},{2,0},{3,1},{4,6},{5,7},{6,4},{7,5},{8,10},{9,11},{10,... | collective-permute-start | bytes 1572872 | tf_op jit(solution)/shard_map/ppermute | solution.py:29
  6.3 28.0 %collective-permute-start.4 = (bf16[256,2048]{1,0:T(8,128)(2,1)}, bf16[256,2048]{1,0:T(8,128)(2,1)}, u32[]{:S(2)}, u32[]{:S(2)}) collective-permute-start(bf16[256,2048]{1,0:T(8,128)(2,1)} %param.4), channel_id=1, source_target_pairs={{0,8},{4,12},{8,0},{12,4},{16,24},{20,28},{24,16},{28,20},{1,9},{5... | collective-permute-start | bytes 3145736 | tf_op jit(solution)/shard_map/ppermute | solution.py:29
  7.7 28.2 %collective-permute-start = (bf16[512,512]{1,0:T(8,128)(2,1)}, bf16[512,512]{1,0:T(8,128)(2,1)}, u32[]{:S(2)}, u32[]{:S(2)}) collective-permute-start(bf16[512,512]{1,0:T(8,128)(2,1)} %param.3), channel_id=1, source_target_pairs={{0,1},{1,0},{2,3},{3,2},{4,5},{5,4},{6,7},{7,6},{8,9},{9,8},{10,11... | collective-permute-start | bytes 1572872 | tf_op jit(solution)/shard_map/ppermute | solution.py:29
  30.6 13.7 %collective-permute-start.2 = (bf16[512,512]{1,0:T(8,128)(2,1)}, bf16[512,512]{1,0:T(8,128)(2,1)S(1)}, u32[]{:S(2)}, u32[]{:S(2)}) collective-permute-start(bf16[512,512]{1,0:T(8,128)(2,1)} %collective-permute-done.1), channel_id=1, source_target_pairs={{0,1},{1,0},{2,3},{3,2},{4,5},{5,4},{6,7},{7,6},{8,9},{9,8},{10,11... | collective-permute-start | bytes 1572872 | tf_op jit(solution)/shard_map/ppermute | solution.py:29
  31.2 15.8 %collective-permute-start.7 = (bf16[256,2048]{1,0:T(8,128)(2,1)S(1)}, bf16[256,2048]{1,0:T(8,128)(2,1)S(1)}, u32[]{:S(2)}, u32[]{:S(2)}) collective-permute-start(bf16[256,2048]{1,0:T(8,128)(2,1)S(1)} %collective-permute-done.6), channel_id=1, source_target_pairs={{0,4},{4,0},{8,12},{12,8},{16,20},{20,16},{24,28},{28,24},{1,5},{5... | collective-permute-start | bytes 3145736 | tf_op jit(solution)/shard_map/ppermute | solution.py:29
  32.8 21.6 %collective-permute-start.9 = (bf16[128,2048]{1,0:T(8,128)(2,1)S(1)}, bf16[128,2048]{1,0:T(8,128)(2,1)}, u32[]{:S(2)}, u32[]{:S(2)}) collective-permute-start(bf16[128,2048]{1,0:T(8,128)(2,1)S(1)} %slice.87), channel_id=1, source_target_pairs={{0,8},{4,12},{8,0},{12,4},{16,24},{20,28},{24,16},{28,20},{1,9},{5... | collective-permute-start | bytes 1572872 | tf_op jit(solution)/shard_map/ppermute | solution.py:29
  35.4 19.0 %collective-permute-start.8 = (bf16[128,2048]{1,0:T(8,128)(2,1)S(1)}, bf16[128,2048]{1,0:T(8,128)(2,1)}, u32[]{:S(2)}, u32[]{:S(2)}) collective-permute-start(bf16[128,2048]{1,0:T(8,128)(2,1)S(1)} %slice.86), channel_id=1, source_target_pairs={{0,16},{4,20},{8,24},{12,28},{16,0},{20,4},{24,8},{28,12},{1,17},{... | collective-permute-start | bytes 1572872 | tf_op jit(solution)/shard_map/ppermute | solution.py:29
  35.9 11.5 %collective-permute-start.5 = (bf16[256,2048]{1,0:T(8,128)(2,1)}, bf16[256,2048]{1,0:T(8,128)(2,1)S(1)}, u32[]{:S(2)}, u32[]{:S(2)}) collective-permute-start(bf16[256,2048]{1,0:T(8,128)(2,1)} %collective-permute-done.4), channel_id=1, source_target_pairs={{0,4},{4,0},{8,12},{12,8},{16,20},{20,16},{24,28},{28,24},{1,5},{5... | collective-permute-start | bytes 3145736 | tf_op jit(solution)/shard_map/ppermute | solution.py:29
  54.4 2.1 %collective-permute-start.10 = (bf16[128,2048]{1,0:T(8,128)(2,1)}, bf16[128,2048]{1,0:T(8,128)(2,1)S(1)}, u32[]{:S(2)}, u32[]{:S(2)}) collective-permute-start(bf16[128,2048]{1,0:T(8,128)(2,1)} %collective-permute-done.8), channel_id=1, source_target_pairs={{0,4},{4,0},{8,12},{12,8},{16,20},{20,16},{24,28},{28,24},{1,5},{5... | collective-permute-start | bytes 1572872 | tf_op jit(solution)/shard_map/ppermute | solution.py:29
  54.4 3.2 %collective-permute-start.11 = (bf16[128,2048]{1,0:T(8,128)(2,1)}, bf16[128,2048]{1,0:T(8,128)(2,1)S(1)}, u32[]{:S(2)}, u32[]{:S(2)}) collective-permute-start(bf16[128,2048]{1,0:T(8,128)(2,1)} %collective-permute-done.9), channel_id=1, source_target_pairs={{0,4},{4,0},{8,12},{12,8},{16,20},{20,16},{24,28},{28,24},{1,5},{5... | collective-permute-start | bytes 1572872 | tf_op jit(solution)/shard_map/ppermute | solution.py:29
  63.3 5.1 %collective-permute-start.14 = (f32[2,512]{1,0:T(2,128)S(1)}, f32[2,512]{1,0:T(2,128)S(1)}, u32[]{:S(2)}, u32[]{:S(2)}) collective-permute-start(f32[2,512]{1,0:T(2,128)S(1)} %pad_maximum_fusion.6), channel_id=1, source_target_pairs={{0,1},{1,0},{2,3},{3,2},{4,5},{5,4},{6,7},{7,6},{8,9},{9,8},{10,11... | collective-permute-start | bytes 12296 | tf_op jit(solution)/shard_map/ppermute | solution.py:29
  64.4 5.0 %collective-permute-start.13 = (f32[2,512]{1,0:T(2,128)S(1)}, f32[2,512]{1,0:T(2,128)S(1)}, u32[]{:S(2)}, u32[]{:S(2)}) collective-permute-start(f32[2,512]{1,0:T(2,128)S(1)} %pad_maximum_fusion.6), channel_id=1, source_target_pairs={{0,2},{1,3},{2,0},{3,1},{4,6},{5,7},{6,4},{7,5},{8,10},{9,11},{10,... | collective-permute-start | bytes 12296 | tf_op jit(solution)/shard_map/ppermute | solution.py:29
  67.7 5.4 %collective-permute-start.12 = (f32[2,512]{1,0:T(2,128)S(1)}, f32[2,512]{1,0:T(2,128)S(1)}, u32[]{:S(2)}, u32[]{:S(2)}) collective-permute-start(f32[2,512]{1,0:T(2,128)S(1)} %pad_maximum_fusion.6), channel_id=1, source_target_pairs={{0,3},{1,2},{2,1},{3,0},{4,7},{5,6},{6,5},{7,4},{8,11},{9,10},{10,... | collective-permute-start | bytes 12296 | tf_op jit(solution)/shard_map/ppermute | solution.py:29
  74.0 1.2 collective-permute-start.15
  75.3 3.7 %collective-permute-start.18 = (f32[1,2048]{1,0:T(1,128)S(1)}, f32[1,2048]{1,0:T(1,128)S(1)}, u32[]{:S(2)}, u32[]{:S(2)}) collective-permute-start(f32[1,2048]{1,0:T(1,128)S(1)} %add.92.refs_0_), channel_id=1, source_target_pairs={{0,8},{4,12},{8,0},{12,4},{16,24},{20,28},{24,16},{28,20},{1,9},{5... | collective-permute-start | bytes 24584 | tf_op jit(solution)/shard_map/ppermute | solution.py:29
  76.8 3.7 %collective-permute-start.17 = (f32[1,2048]{1,0:T(1,128)S(1)}, f32[1,2048]{1,0:T(1,128)S(1)}, u32[]{:S(2)}, u32[]{:S(2)}) collective-permute-start(f32[1,2048]{1,0:T(1,128)S(1)} %add.92.refs_0_), channel_id=1, source_target_pairs={{0,16},{4,20},{8,24},{12,28},{16,0},{20,4},{24,8},{28,12},{1,17},{... | collective-permute-start | bytes 24584 | tf_op jit(solution)/shard_map/ppermute | solution.py:29
  77.3 4.5 %collective-permute-start.16 = (f32[1,2048]{1,0:T(1,128)S(1)}, f32[1,2048]{1,0:T(1,128)S(1)}, u32[]{:S(2)}, u32[]{:S(2)}) collective-permute-start(f32[1,2048]{1,0:T(1,128)S(1)} %add.92.refs_0_), channel_id=1, source_target_pairs={{0,24},{4,28},{8,16},{12,20},{16,8},{20,12},{24,0},{28,4},{1,25},{... | collective-permute-start | bytes 24584 | tf_op jit(solution)/shard_map/ppermute | solution.py:29
  82.5 4.5 %collective-permute-start.21 = (f32[1,512]{1,0:T(1,128)S(1)}, f32[1,512]{1,0:T(1,128)S(1)}, u32[]{:S(2)}, u32[]{:S(2)}) collective-permute-start(f32[1,512]{1,0:T(1,128)S(1)} %get-tuple-element.41.refs_0_), channel_id=1, source_target_pairs={{0,1},{1,0},{2,3},{3,2},{4,5},{5,4},{6,7},{7,6},{8,9},{9,8},{10,11... | collective-permute-start | bytes 6152 | tf_op jit(solution)/shard_map/ppermute | solution.py:29
  82.6 4.5 %collective-permute-start.20 = (f32[1,512]{1,0:T(1,128)S(1)}, f32[1,512]{1,0:T(1,128)S(1)}, u32[]{:S(2)}, u32[]{:S(2)}) collective-permute-start(f32[1,512]{1,0:T(1,128)S(1)} %get-tuple-element.41.refs_0_), channel_id=1, source_target_pairs={{0,2},{1,3},{2,0},{3,1},{4,6},{5,7},{6,4},{7,5},{8,10},{9,11},{10,... | collective-permute-start | bytes 6152 | tf_op jit(solution)/shard_map/ppermute | solution.py:29
  83.2 5.4 %collective-permute-start.19 = (f32[1,512]{1,0:T(1,128)S(1)}, f32[1,512]{1,0:T(1,128)S(1)}, u32[]{:S(2)}, u32[]{:S(2)}) collective-permute-start(f32[1,512]{1,0:T(1,128)S(1)} %get-tuple-element.41.refs_0_), channel_id=1, source_target_pairs={{0,3},{1,2},{2,1},{3,0},{4,7},{5,6},{6,5},{7,4},{8,11},{9,10},{10,... | collective-permute-start | bytes 6152 | tf_op jit(solution)/shard_map/ppermute | solution.py:29
  90.5 3.7 %collective-permute-start.25 = (f32[1,2048]{1,0:T(1,128)S(1)}, f32[1,2048]{1,0:T(1,128)S(1)}, u32[]{:S(2)}, u32[]{:S(2)}) collective-permute-start(f32[1,2048]{1,0:T(1,128)S(1)} %add.93.refs_0_), channel_id=1, source_target_pairs={{0,8},{4,12},{8,0},{12,4},{16,24},{20,28},{24,16},{28,20},{1,9},{5... | collective-permute-start | bytes 24584 | tf_op jit(solution)/shard_map/ppermute | solution.py:29
  91.2 3.7 %collective-permute-start.24 = (f32[1,2048]{1,0:T(1,128)S(1)}, f32[1,2048]{1,0:T(1,128)S(1)}, u32[]{:S(2)}, u32[]{:S(2)}) collective-permute-start(f32[1,2048]{1,0:T(1,128)S(1)} %add.93.refs_0_), channel_id=1, source_target_pairs={{0,16},{4,20},{8,24},{12,28},{16,0},{20,4},{24,8},{28,12},{1,17},{... | collective-permute-start | bytes 24584 | tf_op jit(solution)/shard_map/ppermute | solution.py:29
  92.7 4.5 %collective-permute-start.23 = (f32[1,2048]{1,0:T(1,128)S(1)}, f32[1,2048]{1,0:T(1,128)S(1)}, u32[]{:S(2)}, u32[]{:S(2)}) collective-permute-start(f32[1,2048]{1,0:T(1,128)S(1)} %add.93.refs_0_), channel_id=1, source_target_pairs={{0,24},{4,28},{8,16},{12,20},{16,8},{20,12},{24,0},{28,4},{1,25},{... | collective-permute-start | bytes 24584 | tf_op jit(solution)/shard_map/ppermute | solution.py:29
  97.8 4.5 %collective-permute-start.28 = (f32[1,512]{1,0:T(1,128)S(1)}, f32[1,512]{1,0:T(1,128)S(1)}, u32[]{:S(2)}, u32[]{:S(2)}) collective-permute-start(f32[1,512]{1,0:T(1,128)S(1)} %get-tuple-element.43.refs_0_), channel_id=1, source_target_pairs={{0,1},{1,0},{2,3},{3,2},{4,5},{5,4},{6,7},{7,6},{8,9},{9,8},{10,11... | collective-permute-start | bytes 6152 | tf_op jit(solution)/shard_map/ppermute | solution.py:29
  98.4 5.4 %collective-permute-start.27 = (f32[1,512]{1,0:T(1,128)S(1)}, f32[1,512]{1,0:T(1,128)S(1)}, u32[]{:S(2)}, u32[]{:S(2)}) collective-permute-start(f32[1,512]{1,0:T(1,128)S(1)} %get-tuple-element.43.refs_0_), channel_id=1, source_target_pairs={{0,2},{1,3},{2,0},{3,1},{4,6},{5,7},{6,4},{7,5},{8,10},{9,11},{10,... | collective-permute-start | bytes 6152 | tf_op jit(solution)/shard_map/ppermute | solution.py:29
  102.3 5.4 %collective-permute-start.26 = (f32[1,512]{1,0:T(1,128)S(1)}, f32[1,512]{1,0:T(1,128)S(1)}, u32[]{:S(2)}, u32[]{:S(2)}) collective-permute-start(f32[1,512]{1,0:T(1,128)S(1)} %get-tuple-element.43.refs_0_), channel_id=1, source_target_pairs={{0,3},{1,2},{2,1},{3,0},{4,7},{5,6},{6,5},{7,4},{8,11},{9,10},{10,... | collective-permute-start | bytes 6152 | tf_op jit(solution)/shard_map/ppermute | solution.py:29
  108.3 1.2 collective-permute-start.29
  109.6 3.7 %collective-permute-start.32 = (f32[1,2048]{1,0:T(1,128)S(1)}, f32[1,2048]{1,0:T(1,128)S(1)}, u32[]{:S(2)}, u32[]{:S(2)}) collective-permute-start(f32[1,2048]{1,0:T(1,128)S(1)} %add.94.refs_0_), channel_id=1, source_target_pairs={{0,8},{4,12},{8,0},{12,4},{16,24},{20,28},{24,16},{28,20},{1,9},{5... | collective-permute-start | bytes 24584 | tf_op jit(solution)/shard_map/ppermute | solution.py:29
  111.1 3.7 %collective-permute-start.31 = (f32[1,2048]{1,0:T(1,128)S(1)}, f32[1,2048]{1,0:T(1,128)S(1)}, u32[]{:S(2)}, u32[]{:S(2)}) collective-permute-start(f32[1,2048]{1,0:T(1,128)S(1)} %add.94.refs_0_), channel_id=1, source_target_pairs={{0,16},{4,20},{8,24},{12,28},{16,0},{20,4},{24,8},{28,12},{1,17},{... | collective-permute-start | bytes 24584 | tf_op jit(solution)/shard_map/ppermute | solution.py:29
  111.6 4.5 %collective-permute-start.30 = (f32[1,2048]{1,0:T(1,128)S(1)}, f32[1,2048]{1,0:T(1,128)S(1)}, u32[]{:S(2)}, u32[]{:S(2)}) collective-permute-start(f32[1,2048]{1,0:T(1,128)S(1)} %add.94.refs_0_), channel_id=1, source_target_pairs={{0,24},{4,28},{8,16},{12,20},{16,8},{20,12},{24,0},{28,4},{1,25},{... | collective-permute-start | bytes 24584 | tf_op jit(solution)/shard_map/ppermute | solution.py:29
  116.8 4.5 %collective-permute-start.35 = (f32[1,512]{1,0:T(1,128)S(1)}, f32[1,512]{1,0:T(1,128)S(1)}, u32[]{:S(2)}, u32[]{:S(2)}) collective-permute-start(f32[1,512]{1,0:T(1,128)S(1)} %get-tuple-element.45.refs_0_), channel_id=1, source_target_pairs={{0,1},{1,0},{2,3},{3,2},{4,5},{5,4},{6,7},{7,6},{8,9},{9,8},{10,11... | collective-permute-start | bytes 6152 | tf_op jit(solution)/shard_map/ppermute | solution.py:29
  116.9 4.5 %collective-permute-start.34 = (f32[1,512]{1,0:T(1,128)S(1)}, f32[1,512]{1,0:T(1,128)S(1)}, u32[]{:S(2)}, u32[]{:S(2)}) collective-permute-start(f32[1,512]{1,0:T(1,128)S(1)} %get-tuple-element.45.refs_0_), channel_id=1, source_target_pairs={{0,2},{1,3},{2,0},{3,1},{4,6},{5,7},{6,4},{7,5},{8,10},{9,11},{10,... | collective-permute-start | bytes 6152 | tf_op jit(solution)/shard_map/ppermute | solution.py:29
  117.5 5.4 %collective-permute-start.33 = (f32[1,512]{1,0:T(1,128)S(1)}, f32[1,512]{1,0:T(1,128)S(1)}, u32[]{:S(2)}, u32[]{:S(2)}) collective-permute-start(f32[1,512]{1,0:T(1,128)S(1)} %get-tuple-element.45.refs_0_), channel_id=1, source_target_pairs={{0,3},{1,2},{2,1},{3,0},{4,7},{5,6},{6,5},{7,4},{8,11},{9,10},{10,... | collective-permute-start | bytes 6152 | tf_op jit(solution)/shard_map/ppermute | solution.py:29
  126.9 2.7 %collective-permute-start.36 = (bf16[256,2048]{1,0:T(8,128)(2,1)S(1)}, bf16[256,2048]{1,0:T(8,128)(2,1)S(1)}, u32[]{:S(2)}, u32[]{:S(2)}) collective-permute-start(bf16[256,2048]{1,0:T(8,128)(2,1)S(1)} %get-tuple-element.49), channel_id=1, source_target_pairs={{0,4},{4,0},{8,12},{12,8},{16,20},{20,16},{24,28},{28,24},{1,5},{5... | collective-permute-start | bytes 3145736 | tf_op jit(solution)/shard_map/ppermute | solution.py:29
  130.1 14.0 %collective-permute-start.40 = (bf16[128,2048]{1,0:T(8,128)(2,1)S(1)}, bf16[128,2048]{1,0:T(8,128)(2,1)S(1)}, u32[]{:S(2)}, u32[]{:S(2)}) collective-permute-start(bf16[128,2048]{1,0:T(8,128)(2,1)S(1)} %get-tuple-element.50.refs_4_), channel_id=1, source_target_pairs={{0,8},{4,12},{8,0},{12,4},{16,24},{20,28},{24,16},{28,20},{1,9},{5... | collective-permute-start | bytes 1572872 | tf_op jit(solution)/shard_map/ppermute | solution.py:29
  130.9 13.7 %collective-permute-start.41 = (bf16[128,2048]{1,0:T(8,128)(2,1)S(1)}, bf16[128,2048]{1,0:T(8,128)(2,1)S(1)}, u32[]{:S(2)}, u32[]{:S(2)}) collective-permute-start(bf16[128,2048]{1,0:T(8,128)(2,1)S(1)} %get-tuple-element.51.refs_5_), channel_id=1, source_target_pairs={{0,16},{4,20},{8,24},{12,28},{16,0},{20,4},{24,8},{28,12},{1,17},{... | collective-permute-start | bytes 1572872 | tf_op jit(solution)/shard_map/ppermute | solution.py:29
  144.5 17.8 %collective-permute-start.42 = (bf16[256,2048]{1,0:T(8,128)(2,1)S(1)}, bf16[256,2048]{1,0:T(8,128)(2,1)S(1)}, u32[]{:S(2)}, u32[]{:S(2)}) collective-permute-start(bf16[256,2048]{1,0:T(8,128)(2,1)S(1)} %get-tuple-element.58), channel_id=1, source_target_pairs={{0,4},{4,0},{8,12},{12,8},{16,20},{20,16},{24,28},{28,24},{1,5},{5... | collective-permute-start | bytes 3145736 | tf_op jit(solution)/shard_map/ppermute | solution.py:29
  144.5 14.7 %collective-permute-start.38 = (bf16[512,512]{1,0:T(8,128)(2,1)S(1)}, bf16[512,512]{1,0:T(8,128)(2,1)S(1)}, u32[]{:S(2)}, u32[]{:S(2)}) collective-permute-start(bf16[512,512]{1,0:T(8,128)(2,1)S(1)} %get-tuple-element.53), channel_id=1, source_target_pairs={{0,1},{1,0},{2,3},{3,2},{4,5},{5,4},{6,7},{7,6},{8,9},{9,8},{10,11... | collective-permute-start | bytes 1572872 | tf_op jit(solution)/shard_map/ppermute | solution.py:29
  146.3 33.5 %collective-permute-start.37 = (bf16[512,512]{1,0:T(8,128)(2,1)S(1)}, bf16[512,512]{1,0:T(8,128)(2,1)S(1)}, u32[]{:S(2)}, u32[]{:S(2)}) collective-permute-start(bf16[512,512]{1,0:T(8,128)(2,1)S(1)} %slice_bitcast_fusion), channel_id=1, source_target_pairs={{0,1},{1,0},{2,3},{3,2},{4,5},{5,4},{6,7},{7,6},{8,9},{9,8},{10,11... | collective-permute-start | bytes 1572872 | tf_op jit(solution)/shard_map/ppermute | solution.py:29
  159.4 25.5 %collective-permute-start.39 = (bf16[512,512]{1,0:T(8,128)(2,1)S(1)}, bf16[512,512]{1,0:T(8,128)(2,1)S(1)}, u32[]{:S(2)}, u32[]{:S(2)}) collective-permute-start(bf16[512,512]{1,0:T(8,128)(2,1)S(1)} %fusion.6), channel_id=1, source_target_pairs={{0,2},{1,3},{2,0},{3,1},{4,6},{5,7},{6,4},{7,5},{8,10},{9,11},{10,... | collective-permute-start | bytes 1572872 | tf_op jit(solution)/shard_map/ppermute | solution.py:29
  161.8 2.7 %collective-permute-start.43 = (bf16[256,2048]{1,0:T(8,128)(2,1)S(1)}, bf16[256,2048]{1,0:T(8,128)(2,1)S(1)}, u32[]{:S(2)}, u32[]{:S(2)}) collective-permute-start(bf16[256,2048]{1,0:T(8,128)(2,1)S(1)} %get-tuple-element.60), channel_id=1, source_target_pairs={{0,4},{4,0},{8,12},{12,8},{16,20},{20,16},{24,28},{28,24},{1,5},{5... | collective-permute-start | bytes 3145736 | tf_op jit(solution)/shard_map/ppermute | solution.py:29
  161.8 25.6 %collective-permute-start.44 = (bf16[256,2048]{1,0:T(8,128)(2,1)S(1)}, bf16[256,2048]{1,0:T(8,128)(2,1)S(1)}, u32[]{:S(2)}, u32[]{:S(2)}) collective-permute-start(bf16[256,2048]{1,0:T(8,128)(2,1)S(1)} %get-tuple-element.66), channel_id=1, source_target_pairs={{0,4},{4,0},{8,12},{12,8},{16,20},{20,16},{24,28},{28,24},{1,5},{5... | collective-permute-start | bytes 3145736 | tf_op jit(solution)/shard_map/ppermute | solution.py:29
  162.7 25.0 %collective-permute-start.45 = (bf16[128,2048]{1,0:T(8,128)(2,1)S(1)}, bf16[128,2048]{1,0:T(8,128)(2,1)S(1)}, u32[]{:S(2)}, u32[]{:S(2)}) collective-permute-start(bf16[128,2048]{1,0:T(8,128)(2,1)S(1)} %slice.132), channel_id=1, source_target_pairs={{0,8},{4,12},{8,0},{12,4},{16,24},{20,28},{24,16},{28,20},{1,9},{5... | collective-permute-start | bytes 1572872 | tf_op jit(solution)/shard_map/ppermute | solution.py:29
  164.4 23.4 %collective-permute-start.48 = (bf16[128,2048]{1,0:T(8,128)(2,1)S(1)}, bf16[128,2048]{1,0:T(8,128)(2,1)S(1)}, u32[]{:S(2)}, u32[]{:S(2)}) collective-permute-start(bf16[128,2048]{1,0:T(8,128)(2,1)S(1)} %fusion.5), channel_id=1, source_target_pairs={{0,8},{4,12},{8,0},{12,4},{16,24},{20,28},{24,16},{28,20},{1,9},{5... | collective-permute-start | bytes 1572872 | tf_op jit(solution)/shard_map/ppermute | solution.py:29
  179.9 14.8 %collective-permute-start.47 = (bf16[128,2048]{1,0:T(8,128)(2,1)S(1)}, bf16[128,2048]{1,0:T(8,128)(2,1)S(1)}, u32[]{:S(2)}, u32[]{:S(2)}) collective-permute-start(bf16[128,2048]{1,0:T(8,128)(2,1)S(1)} %slice.131), channel_id=1, source_target_pairs={{0,16},{4,20},{8,24},{12,28},{16,0},{20,4},{24,8},{28,12},{1,17},{... | collective-permute-start | bytes 1572872 | tf_op jit(solution)/shard_map/ppermute | solution.py:29
  184.9 19.8 %collective-permute-start.46 = (bf16[128,2048]{1,0:T(8,128)(2,1)S(1)}, bf16[128,2048]{1,0:T(8,128)(2,1)S(1)}, u32[]{:S(2)}, u32[]{:S(2)}) collective-permute-start(bf16[128,2048]{1,0:T(8,128)(2,1)S(1)} %fusion.4), channel_id=1, source_target_pairs={{0,16},{4,20},{8,24},{12,28},{16,0},{20,4},{24,8},{28,12},{1,17},{... | collective-permute-start | bytes 1572872 | tf_op jit(solution)/shard_map/ppermute | solution.py:29
  (10 other events, 59.6 us)

commit v7 on v6

--- a/solution.py
+++ b/solution.py
@@ -69,7 +69,7 @@
     return pltpu.with_memory_space_constraint(value, pltpu.VMEM)
 
 
-def call(kernel, outputs, operands, scratch=(), extra=(), limit=24):
+def call(kernel, outputs, operands, scratch=(), extra=(), limit=16):
     spec = pl.BlockSpec(memory_space=pltpu.VMEM)
     return pl.pallas_call(
         kernel,
@@ -108,13 +108,69 @@
     total_ref[...] = jnp.sum(jnp.transpose(partial[...]), axis=0, keepdims=True)
 
 
-def turn_kernel(blocks_ref, turned_ref):
-    for i in range(blocks_ref.shape[0]):
-        turned_ref[i] = jnp.transpose(blocks_ref[i])
-
-
-def column_kernel(count, early, student_ref, scale_ref, *refs):
-    part_refs, (total_ref, inverse) = refs[:count], refs[count + early :]
+def rows_at(depth, side, paired):
+    if paired:
+        return 0
+    core = lax.axis_index("sample") % 2
+    return pl.multiple_of((core if side == 0 else 1 - core) * depth, LANES)
+
+
+def products(at, parts, refs, blocks_ref, depth, paired):
+    chip, place = lax.axis_index("sample") // 2, lax.axis_index("cls")
+    total = None
+    for (mask, side), ref in zip(parts, refs):
+        left = blocks_ref[chip ^ mask ^ place, :, pl.ds(rows_at(depth, side, paired), ref.shape[0])]
+        part = jnp.dot(left, ref[:, at], preferred_element_type=f32)
+        total = part if total is None else total + part
+    return total
+
+
+def partial_kernel(count, depth, paired, parts, *refs):
+    feature_refs, head_refs = refs[:count], refs[count : count + len(parts)]
+    blocks_ref, turned_ref, logits_ref = refs[count + len(parts) :]
+    for i, ref in enumerate(feature_refs):
+        blocks_ref[i] = ref[...]
+    columns = logits_ref.shape[1]
+    tile = min(256, columns)
+    for i in range(0, columns, tile):
+        at = slice(i, i + tile)
+        logits_ref[:, at] = products(at, parts, head_refs, blocks_ref, depth, paired)
+    for i, ref in enumerate(feature_refs):
+        turned_ref[i] = jnp.transpose(ref[...])
+
+
+def student_kernel(depth, paired, parts, logits_ref, blocks_ref, *refs):
+    head_refs = refs[: len(parts)]
+    student_ref, slope_ref, sums_ref, buffer, student_sum, plan_sum = refs[len(parts) :]
+    rows, columns = logits_ref.shape
+    tile = min(256, columns)
+    block = min(128, rows)
+    for i in range(0, columns, tile):
+        at = slice(i, i + tile)
+        slot = (i // tile) % 2
+        buffer[slot] = logits_ref[:, at] + products(at, parts, head_refs, blocks_ref, depth, paired)
+        for first in range(0, rows, block):
+            row = slice(first, first + block)
+            student_total = plan_total = None
+            for j in range(0, tile, LANES):
+                out = slice(i + j, i + j + LANES)
+                tanh = jnp.tanh(buffer[slot, row, j : j + LANES] * (1.0 / softcap))
+                student = jnp.exp(softcap * tanh)
+                plan = student * student
+                student_ref[row, out] = student
+                slope_ref[row, out] = (1.0 - tanh * tanh).astype(bf16)
+                student_total = student if student_total is None else student_total + student
+                plan_total = plan if plan_total is None else plan_total + plan
+            if i > 0:
+                student_total, plan_total = student_total + student_sum[row, :], plan_total + plan_sum[row, :]
+            student_sum[row, :] = student_total
+            plan_sum[row, :] = plan_total
+    sums_ref[0:1, :] = jnp.sum(jnp.transpose(student_sum[...]), axis=0, keepdims=True)
+    sums_ref[1:2, :] = jnp.sum(jnp.transpose(plan_sum[...]), axis=0, keepdims=True)
+
+
+def column_kernel(count, student_ref, scale_ref, *refs):
+    part_refs, (total_ref, inverse) = refs[:count], refs[count:]
     mass = part_refs[0][...]
     for ref in part_refs[1:]:
         mass = mass + ref[...]
@@ -144,9 +200,9 @@
         out_ref[:, at] = jnp.dot(left, grad_ref[:, at], preferred_element_type=f32).astype(bf16)
 
 
-def gradient_kernel(count, depth, far, masks, student_ref, slope_ref, scale_ref, students_ref, turned_ref, *refs):
-    part_refs, head_refs = refs[:count], refs[count : count + len(masks)]
-    targets_ref, grad_ref, mine_ref, theirs_ref, share_ref, inverse, students = refs[count + len(masks) :]
+def gradient_kernel(count, depth, paired, far, parts, student_ref, slope_ref, scale_ref, students_ref, turned_ref, *refs):
+    part_refs, head_refs = refs[:count], refs[count : count + len(parts)]
+    targets_ref, grad_ref, mine_ref, theirs_ref, share_ref, inverse, students = refs[count + len(parts) :]
     me, place = lax.axis_index("sample"), lax.axis_index("cls")
     chip, core = me // 2, me % 2
     groups = lax.axis_size("cls")
@@ -167,15 +223,16 @@
             targets_ref[:, at] = target
             grad_ref[:, at] = ((student * students[...] - wide(target)) * wide(slope_ref[:, at])).astype(bf16)
         head_products(turned, core, depth, grad_ref, slice(i, i + tile), mine_ref, theirs_ref)
-    for mask, ref in zip(masks, head_refs):
+    for (mask, side), ref in zip(parts, head_refs):
 
         @pl.when((chip ^ mask) == (place ^ (groups - 1)))
         def _():
-            share_ref[...] = matmul(grad_ref[...], ref[...], ((1,), (1,))).astype(bf16)
-
-
-def products_kernel(count, depth, near, masks, grad_ref, turned_ref, *refs):
-    head_refs, refs = refs[: len(masks)], refs[len(masks) + count :]
+            at = pl.ds(rows_at(depth, side, paired), ref.shape[0])
+            share_ref[:, at] = matmul(grad_ref[...], ref[...], ((1,), (1,))).astype(bf16)
+
+
+def products_kernel(count, depth, paired, near, parts, grad_ref, turned_ref, *refs):
+    head_refs, refs = refs[: len(parts)], refs[len(parts) + count :]
     pairs, (shares_ref,) = refs[:-1], refs[-1:]
     me, place = lax.axis_index("sample"), lax.axis_index("cls")
     chip, core = me // 2, me % 2
@@ -186,8 +243,9 @@
         turned = turned_ref.at[place ^ chip ^ mask]
         for i in range(0, columns, tile):
             head_products(turned, core, depth, grad_ref, slice(i, i + tile), mine_ref, theirs_ref)
-    for mask, ref in zip(masks, head_refs):
-        shares_ref[chip ^ mask ^ place] = matmul(grad_ref[...], ref[...], ((1,), (1,))).astype(bf16)
+    for (mask, side), ref in zip(parts, head_refs):
+        at = pl.ds(rows_at(depth, side, paired), ref.shape[0])
+        shares_ref[chip ^ mask ^ place, :, at] = matmul(grad_ref[...], ref[...], ((1,), (1,))).astype(bf16)
 
 
 def per_device(features, head, class_cap):
@@ -202,28 +260,33 @@
     first, second = chip_axes(samples)
 
     pieces = gather_head(head)
-    blocks = jnp.stack(gather_features(features))
-
-    order = [0] + first + second + [a | b for a in first for b in second]
-    heads, logits = {}, None
-    for mask in order:
-        same = pieces[mask]
-        if len(same) > 1:
-            same = list(lax.optimization_barrier((logits, *same))[1:])
+    features_from = gather_features(features)
+    paired = depth % LANES != 0
+
+    def sides(mask, same):
         other = [flip(part, "sample", 1) for part in same]
-        parts = [jnp.where(core == 0, s, o) for s, o in zip(same, other)]
-        parts += [jnp.where(core == 0, o, s) for s, o in zip(same, other)]
-        heads[mask] = lax.optimization_barrier(jnp.concatenate(parts, axis=0))
-        group = lax.dynamic_index_in_dim(blocks, chip ^ (mask // 2) ^ place, 0, keepdims=False)
-        product = matmul(group, heads[mask], ((1,), (0,)))
-        logits = product if logits is None else logits + product
-
-    tanh = jnp.tanh(logits / softcap)
-    student = jnp.exp(softcap * tanh)
-    slope = (1.0 - tanh * tanh).astype(bf16)
-    sums = jnp.stack([jnp.sum(student, axis=1), jnp.sum(student * student, axis=1)])
-    student, slope, sums = lax.optimization_barrier((student, slope, sums))
-    (turned,) = call(turn_kernel, [((groups, width, rows), bf16)], [blocks])
+        if paired:
+            pairs = [(jnp.where(core == 0, s, o), jnp.where(core == 0, o, s)) for s, o in zip(same, other)]
+            return [((mask // 2, 0), jnp.concatenate([p[0] for p in pairs] + [p[1] for p in pairs], axis=0))]
+        both = [part[0] if len(part) == 1 else jnp.concatenate(part, axis=0) for part in (same, other)]
+        return [((mask // 2, side), part) for side, part in enumerate(both)]
+
+    early = [part for mask in [0] + first + second for part in sides(mask, pieces[mask])]
+    blocks, turned, logits = call(
+        functools.partial(partial_kernel, groups, depth, paired, [at for at, _ in early]),
+        [((groups, rows, width), bf16), ((groups, width, rows), bf16), ((rows, classes), f32)],
+        features_from + [part for _, part in early],
+    )
+    late = []
+    for mask in [a | b for a in first for b in second]:
+        late += sides(mask, list(lax.optimization_barrier((logits, *pieces[mask]))[1:]))
+    tile = min(256, classes)
+    student, slope, sums = call(
+        functools.partial(student_kernel, depth, paired, [at for at, _ in late]),
+        [((rows, classes), f32), ((rows, classes), bf16), ((2, rows), f32)],
+        [logits, blocks] + [part for _, part in late],
+        [pltpu.VMEM((2, rows, tile), f32), pltpu.VMEM((rows, LANES), f32), pltpu.VMEM((rows, LANES), f32)],
+    )
 
     def row_parts(value):
         return [value] + [flip(value, "cls", mask) for mask in range(groups - 1, 0, -1)]
@@ -237,14 +300,12 @@
     students_mass = sum([part[0:1] for part in parts[1:]], parts[0][0:1])
     parts = [part[1:2] for part in parts]
     scale = jnp.ones((1, classes), f32)
-    for iteration in range(ITERS):
-        early = [turned] if iteration == 0 else []
+    for _ in range(ITERS):
         (mass,) = call(
-            functools.partial(column_kernel, len(parts), len(early)),
+            functools.partial(column_kernel, len(parts)),
             [((1, classes), f32)],
             [student, scale] + parts,
             [pltpu.VMEM((rows, LANES), f32)],
-            early,
         )
         sent = column_parts(mass)
         scale, mass = call(
@@ -255,14 +316,14 @@
         )
         parts = row_parts(mass)
 
-    chip_masks = [mask // 2 for mask in order]
-    head_list = [heads[mask] for mask in order]
+    head_at = [at for at, _ in early + late]
+    head_list = [part for _, part in early + late]
     near = [mask // 2 for mask in first + second] + [0]
     diagonal = [(a, b) for a in first for b in second]
     far = (diagonal[-1][0] | diagonal[-1][1]) // 2
     near = [(a | b) // 2 for a, b in diagonal[:-1]] + near
     targets, grad, mine, theirs, share = call(
-        functools.partial(gradient_kernel, len(parts), depth, far, chip_masks),
+        functools.partial(gradient_kernel, len(parts), depth, paired, far, head_at),
         [((rows, classes), bf16)] * 2 + [((depth, classes), bf16)] * 2 + [((rows, width), bf16)],
         [student, slope, scale, students_mass, turned] + parts + head_list,
         [pltpu.VMEM((rows, LANES), f32)] * 2,
@@ -279,16 +340,17 @@
     share_from = {groups - 2: flip(share, "cls", 1)}
 
     results = call(
-        functools.partial(products_kernel, len(halves), depth, near, chip_masks),
+        functools.partial(products_kernel, len(halves), depth, paired, near, head_at),
         [((depth, classes), bf16)] * (2 * len(near)) + [((groups, rows, width), bf16)],
         [grad, turned] + head_list,
         extra=halves,
     )
     shares = results[-1]
-    arrived = [part for parts in extra.values() for part in parts]
+    arrived = [part for parts in extra.values() for part in parts] + list(share_from.values())
     theirs = lax.optimization_barrier((*results[1:-1:2], *arrived))
     arrived = iter(theirs[len(near) :])
     extra = {at: [next(arrived) for _ in parts] for at, parts in extra.items()}
+    share_from = {mask: next(arrived) for mask in share_from}
     mixed = {
         2 * mask: wide(results[2 * i]) + wide(flip(theirs[i], "sample", 1)) for i, mask in enumerate(near)
     }
@@ -300,20 +362,16 @@
         received = share_from[mask] if mask in share_from else flip(shares[mask | 1], "cls", 1)
         returned.append(flip((wide(shares[mask]) + wide(received)).astype(bf16), "cls", mask))
 
-    halves = list(cut(mixed[0]))
-    sent = {}
-    for late in (False, True):
-        for mask in first + second:
-            for part, value in enumerate(cut(mixed[mask])):
-                if ((mask, part) in extra) == late:
-                    for more in extra.get((mask, part), []):
-                        value = value + wide(more)
-                    sent[mask, part] = value.astype(bf16)
-    for (mask, part), value in sent.items():
-        halves[part] = halves[part] + wide(flip(value, "sample", mask))
-    returned = lax.optimization_barrier((*returned, *sent.values()))[: len(returned)]
+    received = []
+    for mask in first + second:
+        halves = list(cut(mixed[mask]))
+        for part in (0, 1):
+            for more in extra.get((mask, part), []):
+                halves[part] = halves[part] + wide(more)
+        received.append(flip(jnp.concatenate(halves, axis=0).astype(bf16), "sample", mask))
+    grad_head = sum([wide(part) for part in received], mixed[0]).astype(bf16)
+    returned = lax.optimization_barrier((*returned, *received))[: len(returned)]
     grad_features = sum([wide(value) for value in returned], wide(shares[0])).astype(bf16)
-    grad_head = jnp.concatenate(halves, axis=0).astype(bf16)
     return (targets, grad_features, grad_head)
 
 

time: 207 us -> 182 us (0.88)
  waiting for transfers between devices: 110 us -> 101 us
  other arithmetic: 12.6 us -> 4.37 us
  matrix products: 8.15 us -> 0 us
  Pallas kernels: 16.5 us -> 21.8 us
  local copies, waits for them, and re-layouts: 4.58 us -> 1.84 us
    ppermute x49 -> x47, waiting for transfers between devices: 110 us -> 101 us  [flip(): lax.ppermute(value, axis, [(i, i ^ mask) for i in range(lax.axis_size(axi...]
    dot_general x4 -> x0, matrix products: 8.15 us -> none  [matmul(): lax.dot_general(left, right, (dims, ((), ())), preferred_element_type=f32)]
    select_n x5 -> x0, other arithmetic: 6.01 us -> none  [per_device(): parts = [jnp.where(core == 0, s, o) for s, o in zip(same, other)]]
    pallas_call x9 -> x10, Pallas kernels: 16.5 us -> 21.8 us  [call(): pl.pallas_call(kernel, out_shape=tuple((pltpu.VMEM(shape, dtype) for shap...]
    ppermute x49 -> x47, starting transfers between devices: 53.6 us -> 51.9 us  [flip(): lax.ppermute(value, axis, [(i, i ^ mask) for i in range(lax.axis_size(axi...]
  transfers between devices with their start and end apart: 49 -> 47, of which waited for: 33 -> 35; matrix products, arithmetic and copies ran while one was open for 9% -> 2% of each run, Pallas kernels for 4% -> 6%
where the time goes in v7:
time: 182 us
  waiting for transfers between devices  101 us (55%)
  starting transfers between devices  51.9 us (29%)
  Pallas kernels  21.8 us (12%)
  other arithmetic  4.37 us (2%)
  local copies, waits for them, and re-layouts  1.84 us (1%)
    ppermute x47, waiting for transfers between devices, flip(): lax.ppermute(value, axis, [(i, i ^ mask) for i in range(lax.axis_size(axi...  101 us
    ppermute x47, starting transfers between devices, flip(): lax.ppermute(value, axis, [(i, i ^ mask) for i in range(lax.axis_size(axi...  51.9 us
    pallas_call x10, Pallas kernels, call(): pl.pallas_call(kernel, out_shape=tuple((pltpu.VMEM(shape, dtype) for shap...  21.8 us
  transfers between devices with their start and end apart: 47, of which 35 were waited for; matrix products, arithmetic and copies ran while one was open for 2% of the time, Pallas kernels for 6%

profile of v7, /device:TPU:0, one launch (start us, length us, event | category | flops | bytes accessed | tf_op | source)
XLA Modules:
  0.0 182.1 jit_solution(8553780739555540867)
XLA Ops:
  0.6 3.0 %collective-permute-start.6 = (bf16[256,2048]{1,0:T(8,128)(2,1)}, bf16[256,2048]{1,0:T(8,128)(2,1)S(1)}, u32[]{:S(2)}, u32[]{:S(2)}) collective-permute-start(bf16[256,2048]{1,0:T(8,128)(2,1)} %refs_0_.3), channel_id=1, source_target_pairs={{0,16},{4,20},{8,24},{12,28},{16,0},{20,4},{24,8},{28,12},{1,17},{... | collective-permute-start | bytes 3145736 | tf_op jit(solution)/shard_map/ppermute | solution.py:29
  3.7 1.5 collective-permute-start.4
  5.2 2.6 %collective-permute-start.1 = (bf16[512,512]{1,0:T(8,128)(2,1)}, bf16[512,512]{1,0:T(8,128)(2,1)S(1)}, u32[]{:S(2)}, u32[]{:S(2)}) collective-permute-start(bf16[512,512]{1,0:T(8,128)(2,1)} %refs_0_.2), channel_id=1, source_target_pairs={{0,2},{1,3},{2,0},{3,1},{4,6},{5,7},{6,4},{7,5},{8,10},{9,11},{10,... | collective-permute-start | bytes 1572872 | tf_op jit(solution)/shard_map/ppermute | solution.py:29
  7.8 1.6 collective-permute-start
  9.3 17.7 %collective-permute-done.6.refs_8_.refs_4_ = bf16[256,2048]{1,0:T(8,128)(2,1)S(1)} collective-permute-done((bf16[256,2048]{1,0:T(8,128)(2,1)}, bf16[256,2048]{1,0:T(8,128)(2,1)S(1)}, u32[]{:S(2)}, u32[]{:S(2)}) %collective-permute-start.6) | collective-permute-done | bytes 1048608 | tf_op jit(solution)/shard_map/ppermute | solution.py:29
  27.1 1.5 collective-permute-done.4.refs_6_.refs_2_
  28.5 2.2 %collective-permute-done.1.refs_2_ = bf16[512,512]{1,0:T(8,128)(2,1)S(1)} collective-permute-done((bf16[512,512]{1,0:T(8,128)(2,1)}, bf16[512,512]{1,0:T(8,128)(2,1)S(1)}, u32[]{:S(2)}, u32[]{:S(2)}) %collective-permute-start.1) | collective-permute-done | bytes 524320 | tf_op jit(solution)/shard_map/ppermute | solution.py:29
  32.1 11.4 %collective-permute-done.2.refs_3_ = bf16[512,512]{1,0:T(8,128)(2,1)S(1)} collective-permute-done((bf16[512,512]{1,0:T(8,128)(2,1)S(1)}, bf16[512,512]{1,0:T(8,128)(2,1)S(1)}, u32[]{:S(2)}, u32[]{:S(2)}) %collective-permute-start.2) | collective-permute-done | bytes 524320 | tf_op jit(solution)/shard_map/ppermute | solution.py:29
  44.0 3.6 %shard_map.58 = (bf16[4,512,512]{2,1,0:T(8,128)(2,1)S(1)}, bf16[4,512,512]{2,1,0:T(8,128)(2,1)S(1)}, f32[512,2048]{1,0:T(8,128)S(1)}) custom-call(bf16[512,512]{1,0:T(8,128)(2,1)S(1)} %copy-done.1, bf16[512,512]{1,0:T(8,128)(2,1)S(1)} %collective-permute-done.refs_1_, bf16[512,512]{1,0:T(8,128)(2,1)S(1)} %collective-permute-done.1.refs_2_, ...), custom_call_target="tpu_custom_call" | custom-call | flops 1 | bytes 1 | tf_op jit(solution)/shard_map/pallas_call | solution.py:74
  47.6 8.2 %collective-permute-done.8 = bf16[128,2048]{1,0:T(8,128)(2,1)S(1)} collective-permute-done((bf16[128,2048]{1,0:T(8,128)(2,1)S(1)}, bf16[128,2048]{1,0:T(8,128)(2,1)S(1)}, u32[]{:S(2)}, u32[]{:S(2)}) %collective-permute-start.8) | collective-permute-done | bytes 524320 | tf_op jit(solution)/shard_map/ppermute | solution.py:29
  56.4 1.3 collective-permute-done.10
  58.5 2.4 %shard_map.59 = (f32[512,2048]{1,0:T(8,128)S(1)}, bf16[512,2048]{1,0:T(8,128)(2,1)S(1)}, f32[2,512]{1,0:T(2,128)S(1)}) custom-call(f32[512,2048]{1,0:T(8,128)S(1)} %get-tuple-element.39.logits_ref, bf16[4,512,512]{2,1,0:T(8,128)(2,1)S(1)} %get-tuple-element.40.blocks_ref, bf16[256,2048]{1,0:T(8,128)(2,1)S(1)} %constant_dynamic-update-slice_fusion.refs_0_.refs_10_.refs_6_, ...), custom_call_target="tpu_custom_call" | custom-call | flops 1 | bytes 1 | tf_op jit(solution)/shard_map/pallas_call | solution.py:74
  60.9 2.5 %collective-permute-start.14 = (f32[2,512]{1,0:T(2,128)S(1)}, f32[2,512]{1,0:T(2,128)S(1)}, u32[]{:S(2)}, u32[]{:S(2)}) collective-permute-start(f32[2,512]{1,0:T(2,128)S(1)} %get-tuple-element.45), channel_id=1, source_target_pairs={{0,1},{1,0},{2,3},{3,2},{4,5},{5,4},{6,7},{7,6},{8,9},{9,8},{10,11... | collective-permute-start | bytes 12296 | tf_op jit(solution)/shard_map/ppermute | solution.py:29
  63.4 3.3 %collective-permute-start.13 = (f32[2,512]{1,0:T(2,128)S(1)}, f32[2,512]{1,0:T(2,128)S(1)}, u32[]{:S(2)}, u32[]{:S(2)}) collective-permute-start(f32[2,512]{1,0:T(2,128)S(1)} %get-tuple-element.45), channel_id=1, source_target_pairs={{0,2},{1,3},{2,0},{3,1},{4,6},{5,7},{6,4},{7,5},{8,10},{9,11},{10,... | collective-permute-start | bytes 12296 | tf_op jit(solution)/shard_map/ppermute | solution.py:29
  66.7 1.5 collective-permute-done.13
  68.3 3.8 %collective-permute-done.12 = f32[2,512]{1,0:T(2,128)S(1)} collective-permute-done((f32[2,512]{1,0:T(2,128)S(1)}, f32[2,512]{1,0:T(2,128)S(1)}, u32[]{:S(2)}, u32[]{:S(2)}) %collective-permute-start.12) | collective-permute-done | bytes 4128 | tf_op jit(solution)/shard_map/ppermute | solution.py:29
  72.9 1.2 collective-permute-done.15
  75.2 2.4 %collective-permute-start.16 = (f32[1,2048]{1,0:T(1,128)S(1)}, f32[1,2048]{1,0:T(1,128)S(1)}, u32[]{:S(2)}, u32[]{:S(2)}) collective-permute-start(f32[1,2048]{1,0:T(1,128)S(1)} %add.51.refs_0_), channel_id=1, source_target_pairs={{0,24},{4,28},{8,16},{12,20},{16,8},{20,12},{24,0},{28,4},{1,25},{... | collective-permute-start | bytes 24584 | tf_op jit(solution)/shard_map/ppermute | solution.py:29
  78.4 1.4 collective-permute-done.16.refs_1_
  81.1 3.8 %collective-permute-start.19 = (f32[1,512]{1,0:T(1,128)S(1)}, f32[1,512]{1,0:T(1,128)S(1)}, u32[]{:S(2)}, u32[]{:S(2)}) collective-permute-start(f32[1,512]{1,0:T(1,128)S(1)} %get-tuple-element.47.refs_0_), channel_id=1, source_target_pairs={{0,3},{1,2},{2,1},{3,0},{4,7},{5,6},{6,5},{7,4},{8,11},{9,10},{10,... | collective-permute-start | bytes 6152 | tf_op jit(solution)/shard_map/ppermute | solution.py:29
  85.0 1.4 collective-permute-done.19.refs_1_
  87.2 1.2 collective-permute-done.22
  88.4 1.6 collective-permute-start.25
  89.9 1.5 collective-permute-start.24
  92.1 1.5 collective-permute-done.24.refs_2_
  93.6 2.4 %collective-permute-done.23.refs_1_ = f32[1,2048]{1,0:T(1,128)S(1)} collective-permute-done((f32[1,2048]{1,0:T(1,128)S(1)}, f32[1,2048]{1,0:T(1,128)S(1)}, u32[]{:S(2)}, u32[]{:S(2)}) %collective-permute-start.23) | collective-permute-done | bytes 8224 | tf_op jit(solution)/shard_map/ppermute | solution.py:29
  97.2 3.8 %collective-permute-start.27 = (f32[1,512]{1,0:T(1,128)S(1)}, f32[1,512]{1,0:T(1,128)S(1)}, u32[]{:S(2)}, u32[]{:S(2)}) collective-permute-start(f32[1,512]{1,0:T(1,128)S(1)} %get-tuple-element.49.refs_0_), channel_id=1, source_target_pairs={{0,2},{1,3},{2,0},{3,1},{4,6},{5,7},{6,4},{7,5},{8,10},{9,11},{10,... | collective-permute-start | bytes 6152 | tf_op jit(solution)/shard_map/ppermute | solution.py:29
  101.1 1.5 collective-permute-done.27.refs_2_
  102.6 3.8 %collective-permute-done.26.refs_1_ = f32[1,512]{1,0:T(1,128)S(1)} collective-permute-done((f32[1,512]{1,0:T(1,128)S(1)}, f32[1,512]{1,0:T(1,128)S(1)}, u32[]{:S(2)}, u32[]{:S(2)}) %collective-permute-start.26) | collective-permute-done | bytes 2080 | tf_op jit(solution)/shard_map/ppermute | solution.py:29
  109.5 2.4 %collective-permute-start.30 = (f32[1,2048]{1,0:T(1,128)S(1)}, f32[1,2048]{1,0:T(1,128)S(1)}, u32[]{:S(2)}, u32[]{:S(2)}) collective-permute-start(f32[1,2048]{1,0:T(1,128)S(1)} %add.53.refs_0_), channel_id=1, source_target_pairs={{0,24},{4,28},{8,16},{12,20},{16,8},{20,12},{24,0},{28,4},{1,25},{... | collective-permute-start | bytes 24584 | tf_op jit(solution)/shard_map/ppermute | solution.py:29
  112.6 1.4 collective-permute-done.30.refs_1_
  115.3 3.8 %collective-permute-start.33 = (f32[1,512]{1,0:T(1,128)S(1)}, f32[1,512]{1,0:T(1,128)S(1)}, u32[]{:S(2)}, u32[]{:S(2)}) collective-permute-start(f32[1,512]{1,0:T(1,128)S(1)} %get-tuple-element.52.refs_0_), channel_id=1, source_target_pairs={{0,3},{1,2},{2,1},{3,0},{4,7},{5,6},{6,5},{7,4},{8,11},{9,10},{10,... | collective-permute-start | bytes 6152 | tf_op jit(solution)/shard_map/ppermute | solution.py:29
  119.3 1.4 collective-permute-done.33.refs_1_
  120.7 4.0 %shard_map.66 = (bf16[512,2048]{1,0:T(8,128)(2,1)S(1)}, bf16[512,2048]{1,0:T(8,128)(2,1)S(1)}, bf16[256,2048]{1,0:T(8,128)(2,1)S(1)}, bf16[256,2048]{1,0:T(8,128)(2,1)S(1)}, bf16[512,512]{1,0:T(8,128)(2,1)S(1)}) custom-call(f32[512,2048]{1,0:T(8,128)S(1)} %get-tuple-element.43.student_ref, bf16[512,2048]{1,0:T(8,128)(2,1)S(1)} %get-tuple-element.44.slope_ref, ...), custom_call_target="tpu_custom_call" | custom-call | flops 1 | bytes 1 | tf_op jit(solution)/shard_map/pallas_call | solution.py:74
  125.4 2.1 %collective-permute-done.36 = bf16[256,2048]{1,0:T(8,128)(2,1)S(1)} collective-permute-done((bf16[256,2048]{1,0:T(8,128)(2,1)S(1)}, bf16[256,2048]{1,0:T(8,128)(2,1)S(1)}, u32[]{:S(2)}, u32[]{:S(2)}) %collective-permute-start.36) | collective-permute-done | bytes 1048608 | tf_op jit(solution)/shard_map/ppermute | solution.py:29
  128.0 1.6 collective-permute-start.38
  129.5 1.5 collective-permute-start.39
  131.0 7.9 %shard_map.67 = (bf16[256,2048]{1,0:T(8,128)(2,1)S(1)}, bf16[256,2048]{1,0:T(8,128)(2,1)S(1)}, bf16[256,2048]{1,0:T(8,128)(2,1)S(1)}, bf16[256,2048]{1,0:T(8,128...) custom-call(bf16[512,2048]{1,0:T(8,128)(2,1)S(1)} %get-tuple-element.54.g, ...), custom_call_target="tpu_custom_call" | custom-call | flops 1 | bytes 1 | tf_op jit(solution)/shard_map/pallas_call | solution.py:74
  139.1 2.8 %collective-permute-done.38 = bf16[128,2048]{1,0:T(8,128)(2,1)S(1)} collective-permute-done((bf16[128,2048]{1,0:T(8,128)(2,1)S(1)}, bf16[128,2048]{1,0:T(8,128)(2,1)S(1)}, u32[]{:S(2)}, u32[]{:S(2)}) %collective-permute-start.38) | collective-permute-done | bytes 524320 | tf_op jit(solution)/shard_map/ppermute | solution.py:29
  142.0 1.2 collective-permute-done.39
  143.7 2.1 %collective-permute-done.42 = bf16[256,2048]{1,0:T(8,128)(2,1)S(1)} collective-permute-done((bf16[256,2048]{1,0:T(8,128)(2,1)S(1)}, bf16[256,2048]{1,0:T(8,128)(2,1)S(1)}, u32[]{:S(2)}, u32[]{:S(2)}) %collective-permute-start.42) | collective-permute-done | bytes 1048608 | tf_op jit(solution)/shard_map/ppermute | solution.py:29
  145.9 1.5 collective-permute-done.44
  149.3 1.6 collective-permute-start.45
  151.6 3.9 %collective-permute-start.41 = (bf16[512,512]{1,0:T(8,128)(2,1)S(1)}, bf16[512,512]{1,0:T(8,128)(2,1)S(1)}, u32[]{:S(2)}, u32[]{:S(2)}) collective-permute-start(bf16[512,512]{1,0:T(8,128)(2,1)S(1)} %fusion.2), channel_id=1, source_target_pairs={{0,2},{1,3},{2,0},{3,1},{4,6},{5,7},{6,4},{7,5},{8,10},{9,11},{10,... | collective-permute-start | bytes 1572872 | tf_op jit(solution)/shard_map/ppermute | solution.py:29
  155.5 1.3 copy.8
  156.9 17.1 %collective-permute-done.37 = bf16[512,512]{1,0:T(8,128)(2,1)S(1)} collective-permute-done((bf16[512,512]{1,0:T(8,128)(2,1)S(1)}, bf16[512,512]{1,0:T(8,128)(2,1)S(1)}, u32[]{:S(2)}, u32[]{:S(2)}) %collective-permute-start.37) | collective-permute-done | bytes 524320 | tf_op jit(solution)/shard_map/ppermute | solution.py:29
  174.0 5.4 %collective-permute-done.41 = bf16[512,512]{1,0:T(8,128)(2,1)S(1)} collective-permute-done((bf16[512,512]{1,0:T(8,128)(2,1)S(1)}, bf16[512,512]{1,0:T(8,128)(2,1)S(1)}, u32[]{:S(2)}, u32[]{:S(2)}) %collective-permute-start.41) | collective-permute-done | bytes 524320 | tf_op jit(solution)/shard_map/ppermute | solution.py:29
  180.4 1.6 add_convert_fusion
  (88 shorter events, 20.8 us)
Async XLA Ops:
  0.6 43.4 %copy-start = (bf16[256,2048]{1,0:T(8,128)(2,1)S(1)}, bf16[256,2048]{1,0:T(8,128)(2,1)}, u32[]{:S(2)}) copy-start(bf16[256,2048]{1,0:T(8,128)(2,1)} %refs_0_.3) | copy-start | bytes 3145732
  0.6 26.4 %collective-permute-start.6 = (bf16[256,2048]{1,0:T(8,128)(2,1)}, bf16[256,2048]{1,0:T(8,128)(2,1)S(1)}, u32[]{:S(2)}, u32[]{:S(2)}) collective-permute-start(bf16[256,2048]{1,0:T(8,128)(2,1)} %refs_0_.3), channel_id=1, source_target_pairs={{0,16},{4,20},{8,24},{12,28},{16,0},{20,4},{24,8},{28,12},{1,17},{... | collective-permute-start | bytes 3145736 | tf_op jit(solution)/shard_map/ppermute | solution.py:29
  3.7 24.8 %collective-permute-start.4 = (bf16[256,2048]{1,0:T(8,128)(2,1)}, bf16[256,2048]{1,0:T(8,128)(2,1)S(1)}, u32[]{:S(2)}, u32[]{:S(2)}) collective-permute-start(bf16[256,2048]{1,0:T(8,128)(2,1)} %refs_0_.3), channel_id=1, source_target_pairs={{0,8},{4,12},{8,0},{12,4},{16,24},{20,28},{24,16},{28,20},{1,9},{5... | collective-permute-start | bytes 3145736 | tf_op jit(solution)/shard_map/ppermute | solution.py:29
  5.2 25.6 %collective-permute-start.1 = (bf16[512,512]{1,0:T(8,128)(2,1)}, bf16[512,512]{1,0:T(8,128)(2,1)S(1)}, u32[]{:S(2)}, u32[]{:S(2)}) collective-permute-start(bf16[512,512]{1,0:T(8,128)(2,1)} %refs_0_.2), channel_id=1, source_target_pairs={{0,2},{1,3},{2,0},{3,1},{4,6},{5,7},{6,4},{7,5},{8,10},{9,11},{10,... | collective-permute-start | bytes 1572872 | tf_op jit(solution)/shard_map/ppermute | solution.py:29
  7.8 23.7 %collective-permute-start = (bf16[512,512]{1,0:T(8,128)(2,1)}, bf16[512,512]{1,0:T(8,128)(2,1)S(1)}, u32[]{:S(2)}, u32[]{:S(2)}) collective-permute-start(bf16[512,512]{1,0:T(8,128)(2,1)} %refs_0_.2), channel_id=1, source_target_pairs={{0,1},{1,0},{2,3},{3,2},{4,5},{5,4},{6,7},{7,6},{8,9},{9,8},{10,11... | collective-permute-start | bytes 1572872 | tf_op jit(solution)/shard_map/ppermute | solution.py:29
  9.3 34.7 %collective-permute-start.3 = (bf16[256,2048]{1,0:T(8,128)(2,1)}, bf16[256,2048]{1,0:T(8,128)(2,1)S(1)}, u32[]{:S(2)}, u32[]{:S(2)}) collective-permute-start(bf16[256,2048]{1,0:T(8,128)(2,1)} %refs_0_.3), channel_id=1, source_target_pairs={{0,4},{4,0},{8,12},{12,8},{16,20},{20,16},{24,28},{28,24},{1,5},{5... | collective-permute-start | bytes 3145736 | tf_op jit(solution)/shard_map/ppermute | solution.py:29
  27.1 17.0 %collective-permute-start.7 = (bf16[256,2048]{1,0:T(8,128)(2,1)S(1)}, bf16[256,2048]{1,0:T(8,128)(2,1)S(1)}, u32[]{:S(2)}, u32[]{:S(2)}) collective-permute-start(bf16[256,2048]{1,0:T(8,128)(2,1)S(1)} %collective-permute-done.6.refs_8_.refs_4_), channel_id=1, source_target_pairs={{0,4},{4,0},{8,12},{12,8},{16,20},{20,16},{24,28},{28,24},{1,5},{5... | collective-permute-start | bytes 3145736 | tf_op jit(solution)/shard_map/ppermute | solution.py:29
  28.5 15.5 %collective-permute-start.5 = (bf16[256,2048]{1,0:T(8,128)(2,1)S(1)}, bf16[256,2048]{1,0:T(8,128)(2,1)S(1)}, u32[]{:S(2)}, u32[]{:S(2)}) collective-permute-start(bf16[256,2048]{1,0:T(8,128)(2,1)S(1)} %collective-permute-done.4.refs_6_.refs_2_), channel_id=1, source_target_pairs={{0,4},{4,0},{8,12},{12,8},{16,20},{20,16},{24,28},{28,24},{1,5},{5... | collective-permute-start | bytes 3145736 | tf_op jit(solution)/shard_map/ppermute | solution.py:29
  30.7 12.8 %collective-permute-start.2 = (bf16[512,512]{1,0:T(8,128)(2,1)S(1)}, bf16[512,512]{1,0:T(8,128)(2,1)S(1)}, u32[]{:S(2)}, u32[]{:S(2)}) collective-permute-start(bf16[512,512]{1,0:T(8,128)(2,1)S(1)} %collective-permute-done.1.refs_2_), channel_id=1, source_target_pairs={{0,1},{1,0},{2,3},{3,2},{4,5},{5,4},{6,7},{7,6},{8,9},{9,8},{10,11... | collective-permute-start | bytes 1572872 | tf_op jit(solution)/shard_map/ppermute | solution.py:29
  31.5 16.1 %collective-permute-start.9 = (bf16[128,2048]{1,0:T(8,128)(2,1)S(1)}, bf16[128,2048]{1,0:T(8,128)(2,1)S(1)}, u32[]{:S(2)}, u32[]{:S(2)}) collective-permute-start(bf16[128,2048]{1,0:T(8,128)(2,1)S(1)} %slice.79), channel_id=1, source_target_pairs={{0,8},{4,12},{8,0},{12,4},{16,24},{20,28},{24,16},{28,20},{1,9},{5... | collective-permute-start | bytes 1572872 | tf_op jit(solution)/shard_map/ppermute | solution.py:29
  43.5 12.3 %collective-permute-start.8 = (bf16[128,2048]{1,0:T(8,128)(2,1)S(1)}, bf16[128,2048]{1,0:T(8,128)(2,1)S(1)}, u32[]{:S(2)}, u32[]{:S(2)}) collective-permute-start(bf16[128,2048]{1,0:T(8,128)(2,1)S(1)} %slice.78), channel_id=1, source_target_pairs={{0,16},{4,20},{8,24},{12,28},{16,0},{20,4},{24,8},{28,12},{1,17},{... | collective-permute-start | bytes 1572872 | tf_op jit(solution)/shard_map/ppermute | solution.py:29
  55.8 1.9 %collective-permute-start.10 = (bf16[128,2048]{1,0:T(8,128)(2,1)S(1)}, bf16[128,2048]{1,0:T(8,128)(2,1)S(1)}, u32[]{:S(2)}, u32[]{:S(2)}) collective-permute-start(bf16[128,2048]{1,0:T(8,128)(2,1)S(1)} %collective-permute-done.8), channel_id=1, source_target_pairs={{0,4},{4,0},{8,12},{12,8},{16,20},{20,16},{24,28},{28,24},{1,5},{5... | collective-permute-start | bytes 1572872 | tf_op jit(solution)/shard_map/ppermute | solution.py:29
  55.8 2.7 %collective-permute-start.11 = (bf16[128,2048]{1,0:T(8,128)(2,1)S(1)}, bf16[128,2048]{1,0:T(8,128)(2,1)S(1)}, u32[]{:S(2)}, u32[]{:S(2)}) collective-permute-start(bf16[128,2048]{1,0:T(8,128)(2,1)S(1)} %collective-permute-done.9), channel_id=1, source_target_pairs={{0,4},{4,0},{8,12},{12,8},{16,20},{20,16},{24,28},{28,24},{1,5},{5... | collective-permute-start | bytes 1572872 | tf_op jit(solution)/shard_map/ppermute | solution.py:29
  60.9 5.9 %collective-permute-start.14 = (f32[2,512]{1,0:T(2,128)S(1)}, f32[2,512]{1,0:T(2,128)S(1)}, u32[]{:S(2)}, u32[]{:S(2)}) collective-permute-start(f32[2,512]{1,0:T(2,128)S(1)} %get-tuple-element.45), channel_id=1, source_target_pairs={{0,1},{1,0},{2,3},{3,2},{4,5},{5,4},{6,7},{7,6},{8,9},{9,8},{10,11... | collective-permute-start | bytes 12296 | tf_op jit(solution)/shard_map/ppermute | solution.py:29
  63.4 4.9 %collective-permute-start.13 = (f32[2,512]{1,0:T(2,128)S(1)}, f32[2,512]{1,0:T(2,128)S(1)}, u32[]{:S(2)}, u32[]{:S(2)}) collective-permute-start(f32[2,512]{1,0:T(2,128)S(1)} %get-tuple-element.45), channel_id=1, source_target_pairs={{0,2},{1,3},{2,0},{3,1},{4,6},{5,7},{6,4},{7,5},{8,10},{9,11},{10,... | collective-permute-start | bytes 12296 | tf_op jit(solution)/shard_map/ppermute | solution.py:29
  66.7 5.4 %collective-permute-start.12 = (f32[2,512]{1,0:T(2,128)S(1)}, f32[2,512]{1,0:T(2,128)S(1)}, u32[]{:S(2)}, u32[]{:S(2)}) collective-permute-start(f32[2,512]{1,0:T(2,128)S(1)} %get-tuple-element.45), channel_id=1, source_target_pairs={{0,3},{1,2},{2,1},{3,0},{4,7},{5,6},{6,5},{7,4},{8,11},{9,10},{10,... | collective-permute-start | bytes 12296 | tf_op jit(solution)/shard_map/ppermute | solution.py:29
  72.8 1.2 collective-permute-start.15
  74.1 3.7 %collective-permute-start.18 = (f32[1,2048]{1,0:T(1,128)S(1)}, f32[1,2048]{1,0:T(1,128)S(1)}, u32[]{:S(2)}, u32[]{:S(2)}) collective-permute-start(f32[1,2048]{1,0:T(1,128)S(1)} %add.51.refs_0_), channel_id=1, source_target_pairs={{0,8},{4,12},{8,0},{12,4},{16,24},{20,28},{24,16},{28,20},{1,9},{5... | collective-permute-start | bytes 24584 | tf_op jit(solution)/shard_map/ppermute | solution.py:29
  74.7 3.7 %collective-permute-start.17 = (f32[1,2048]{1,0:T(1,128)S(1)}, f32[1,2048]{1,0:T(1,128)S(1)}, u32[]{:S(2)}, u32[]{:S(2)}) collective-permute-start(f32[1,2048]{1,0:T(1,128)S(1)} %add.51.refs_0_), channel_id=1, source_target_pairs={{0,16},{4,20},{8,24},{12,28},{16,0},{20,4},{24,8},{28,12},{1,17},{... | collective-permute-start | bytes 24584 | tf_op jit(solution)/shard_map/ppermute | solution.py:29
  75.2 4.5 %collective-permute-start.16 = (f32[1,2048]{1,0:T(1,128)S(1)}, f32[1,2048]{1,0:T(1,128)S(1)}, u32[]{:S(2)}, u32[]{:S(2)}) collective-permute-start(f32[1,2048]{1,0:T(1,128)S(1)} %add.51.refs_0_), channel_id=1, source_target_pairs={{0,24},{4,28},{8,16},{12,20},{16,8},{20,12},{24,0},{28,4},{1,25},{... | collective-permute-start | bytes 24584 | tf_op jit(solution)/shard_map/ppermute | solution.py:29
  80.4 4.5 %collective-permute-start.21 = (f32[1,512]{1,0:T(1,128)S(1)}, f32[1,512]{1,0:T(1,128)S(1)}, u32[]{:S(2)}, u32[]{:S(2)}) collective-permute-start(f32[1,512]{1,0:T(1,128)S(1)} %get-tuple-element.47.refs_0_), channel_id=1, source_target_pairs={{0,1},{1,0},{2,3},{3,2},{4,5},{5,4},{6,7},{7,6},{8,9},{9,8},{10,11... | collective-permute-start | bytes 6152 | tf_op jit(solution)/shard_map/ppermute | solution.py:29
  80.5 4.5 %collective-permute-start.20 = (f32[1,512]{1,0:T(1,128)S(1)}, f32[1,512]{1,0:T(1,128)S(1)}, u32[]{:S(2)}, u32[]{:S(2)}) collective-permute-start(f32[1,512]{1,0:T(1,128)S(1)} %get-tuple-element.47.refs_0_), channel_id=1, source_target_pairs={{0,2},{1,3},{2,0},{3,1},{4,6},{5,7},{6,4},{7,5},{8,10},{9,11},{10,... | collective-permute-start | bytes 6152 | tf_op jit(solution)/shard_map/ppermute | solution.py:29
  81.1 5.4 %collective-permute-start.19 = (f32[1,512]{1,0:T(1,128)S(1)}, f32[1,512]{1,0:T(1,128)S(1)}, u32[]{:S(2)}, u32[]{:S(2)}) collective-permute-start(f32[1,512]{1,0:T(1,128)S(1)} %get-tuple-element.47.refs_0_), channel_id=1, source_target_pairs={{0,3},{1,2},{2,1},{3,0},{4,7},{5,6},{6,5},{7,4},{8,11},{9,10},{10,... | collective-permute-start | bytes 6152 | tf_op jit(solution)/shard_map/ppermute | solution.py:29
  87.1 1.2 collective-permute-start.22
  88.4 3.7 %collective-permute-start.25 = (f32[1,2048]{1,0:T(1,128)S(1)}, f32[1,2048]{1,0:T(1,128)S(1)}, u32[]{:S(2)}, u32[]{:S(2)}) collective-permute-start(f32[1,2048]{1,0:T(1,128)S(1)} %add.52.refs_0_), channel_id=1, source_target_pairs={{0,8},{4,12},{8,0},{12,4},{16,24},{20,28},{24,16},{28,20},{1,9},{5... | collective-permute-start | bytes 24584 | tf_op jit(solution)/shard_map/ppermute | solution.py:29
  89.9 3.7 %collective-permute-start.24 = (f32[1,2048]{1,0:T(1,128)S(1)}, f32[1,2048]{1,0:T(1,128)S(1)}, u32[]{:S(2)}, u32[]{:S(2)}) collective-permute-start(f32[1,2048]{1,0:T(1,128)S(1)} %add.52.refs_0_), channel_id=1, source_target_pairs={{0,16},{4,20},{8,24},{12,28},{16,0},{20,4},{24,8},{28,12},{1,17},{... | collective-permute-start | bytes 24584 | tf_op jit(solution)/shard_map/ppermute | solution.py:29
  91.4 4.5 %collective-permute-start.23 = (f32[1,2048]{1,0:T(1,128)S(1)}, f32[1,2048]{1,0:T(1,128)S(1)}, u32[]{:S(2)}, u32[]{:S(2)}) collective-permute-start(f32[1,2048]{1,0:T(1,128)S(1)} %add.52.refs_0_), channel_id=1, source_target_pairs={{0,24},{4,28},{8,16},{12,20},{16,8},{20,12},{24,0},{28,4},{1,25},{... | collective-permute-start | bytes 24584 | tf_op jit(solution)/shard_map/ppermute | solution.py:29
  96.6 4.5 %collective-permute-start.28 = (f32[1,512]{1,0:T(1,128)S(1)}, f32[1,512]{1,0:T(1,128)S(1)}, u32[]{:S(2)}, u32[]{:S(2)}) collective-permute-start(f32[1,512]{1,0:T(1,128)S(1)} %get-tuple-element.49.refs_0_), channel_id=1, source_target_pairs={{0,1},{1,0},{2,3},{3,2},{4,5},{5,4},{6,7},{7,6},{8,9},{9,8},{10,11... | collective-permute-start | bytes 6152 | tf_op jit(solution)/shard_map/ppermute | solution.py:29
  97.2 5.4 %collective-permute-start.27 = (f32[1,512]{1,0:T(1,128)S(1)}, f32[1,512]{1,0:T(1,128)S(1)}, u32[]{:S(2)}, u32[]{:S(2)}) collective-permute-start(f32[1,512]{1,0:T(1,128)S(1)} %get-tuple-element.49.refs_0_), channel_id=1, source_target_pairs={{0,2},{1,3},{2,0},{3,1},{4,6},{5,7},{6,4},{7,5},{8,10},{9,11},{10,... | collective-permute-start | bytes 6152 | tf_op jit(solution)/shard_map/ppermute | solution.py:29
  101.0 5.4 %collective-permute-start.26 = (f32[1,512]{1,0:T(1,128)S(1)}, f32[1,512]{1,0:T(1,128)S(1)}, u32[]{:S(2)}, u32[]{:S(2)}) collective-permute-start(f32[1,512]{1,0:T(1,128)S(1)} %get-tuple-element.49.refs_0_), channel_id=1, source_target_pairs={{0,3},{1,2},{2,1},{3,0},{4,7},{5,6},{6,5},{7,4},{8,11},{9,10},{10,... | collective-permute-start | bytes 6152 | tf_op jit(solution)/shard_map/ppermute | solution.py:29
  107.1 1.2 collective-permute-start.29
  108.4 3.7 %collective-permute-start.32 = (f32[1,2048]{1,0:T(1,128)S(1)}, f32[1,2048]{1,0:T(1,128)S(1)}, u32[]{:S(2)}, u32[]{:S(2)}) collective-permute-start(f32[1,2048]{1,0:T(1,128)S(1)} %add.53.refs_0_), channel_id=1, source_target_pairs={{0,8},{4,12},{8,0},{12,4},{16,24},{20,28},{24,16},{28,20},{1,9},{5... | collective-permute-start | bytes 24584 | tf_op jit(solution)/shard_map/ppermute | solution.py:29
  109.0 3.7 %collective-permute-start.31 = (f32[1,2048]{1,0:T(1,128)S(1)}, f32[1,2048]{1,0:T(1,128)S(1)}, u32[]{:S(2)}, u32[]{:S(2)}) collective-permute-start(f32[1,2048]{1,0:T(1,128)S(1)} %add.53.refs_0_), channel_id=1, source_target_pairs={{0,16},{4,20},{8,24},{12,28},{16,0},{20,4},{24,8},{28,12},{1,17},{... | collective-permute-start | bytes 24584 | tf_op jit(solution)/shard_map/ppermute | solution.py:29
  109.5 4.5 %collective-permute-start.30 = (f32[1,2048]{1,0:T(1,128)S(1)}, f32[1,2048]{1,0:T(1,128)S(1)}, u32[]{:S(2)}, u32[]{:S(2)}) collective-permute-start(f32[1,2048]{1,0:T(1,128)S(1)} %add.53.refs_0_), channel_id=1, source_target_pairs={{0,24},{4,28},{8,16},{12,20},{16,8},{20,12},{24,0},{28,4},{1,25},{... | collective-permute-start | bytes 24584 | tf_op jit(solution)/shard_map/ppermute | solution.py:29
  114.7 4.5 %collective-permute-start.35 = (f32[1,512]{1,0:T(1,128)S(1)}, f32[1,512]{1,0:T(1,128)S(1)}, u32[]{:S(2)}, u32[]{:S(2)}) collective-permute-start(f32[1,512]{1,0:T(1,128)S(1)} %get-tuple-element.52.refs_0_), channel_id=1, source_target_pairs={{0,1},{1,0},{2,3},{3,2},{4,5},{5,4},{6,7},{7,6},{8,9},{9,8},{10,11... | collective-permute-start | bytes 6152 | tf_op jit(solution)/shard_map/ppermute | solution.py:29
  114.7 4.5 %collective-permute-start.34 = (f32[1,512]{1,0:T(1,128)S(1)}, f32[1,512]{1,0:T(1,128)S(1)}, u32[]{:S(2)}, u32[]{:S(2)}) collective-permute-start(f32[1,512]{1,0:T(1,128)S(1)} %get-tuple-element.52.refs_0_), channel_id=1, source_target_pairs={{0,2},{1,3},{2,0},{3,1},{4,6},{5,7},{6,4},{7,5},{8,10},{9,11},{10,... | collective-permute-start | bytes 6152 | tf_op jit(solution)/shard_map/ppermute | solution.py:29
  115.3 5.4 %collective-permute-start.33 = (f32[1,512]{1,0:T(1,128)S(1)}, f32[1,512]{1,0:T(1,128)S(1)}, u32[]{:S(2)}, u32[]{:S(2)}) collective-permute-start(f32[1,512]{1,0:T(1,128)S(1)} %get-tuple-element.52.refs_0_), channel_id=1, source_target_pairs={{0,3},{1,2},{2,1},{3,0},{4,7},{5,6},{6,5},{7,4},{8,11},{9,10},{10,... | collective-permute-start | bytes 6152 | tf_op jit(solution)/shard_map/ppermute | solution.py:29
  124.7 2.7 %collective-permute-start.36 = (bf16[256,2048]{1,0:T(8,128)(2,1)S(1)}, bf16[256,2048]{1,0:T(8,128)(2,1)S(1)}, u32[]{:S(2)}, u32[]{:S(2)}) collective-permute-start(bf16[256,2048]{1,0:T(8,128)(2,1)S(1)} %get-tuple-element.56), channel_id=1, source_target_pairs={{0,4},{4,0},{8,12},{12,8},{16,20},{20,16},{24,28},{28,24},{1,5},{5... | collective-permute-start | bytes 3145736 | tf_op jit(solution)/shard_map/ppermute | solution.py:29
  124.8 14.3 %collective-permute-start.40 = (bf16[512,512]{1,0:T(8,128)(2,1)S(1)}, bf16[512,512]{1,0:T(8,128)(2,1)S(1)}, u32[]{:S(2)}, u32[]{:S(2)}) collective-permute-start(bf16[512,512]{1,0:T(8,128)(2,1)S(1)} %get-tuple-element.63), channel_id=1, source_target_pairs={{0,1},{1,0},{2,3},{3,2},{4,5},{5,4},{6,7},{7,6},{8,9},{9,8},{10,11... | collective-permute-start | bytes 1572872 | tf_op jit(solution)/shard_map/ppermute | solution.py:29
  128.0 14.0 %collective-permute-start.38 = (bf16[128,2048]{1,0:T(8,128)(2,1)S(1)}, bf16[128,2048]{1,0:T(8,128)(2,1)S(1)}, u32[]{:S(2)}, u32[]{:S(2)}) collective-permute-start(bf16[128,2048]{1,0:T(8,128)(2,1)S(1)} %get-tuple-element.57.refs_8_), channel_id=1, source_target_pairs={{0,8},{4,12},{8,0},{12,4},{16,24},{20,28},{24,16},{28,20},{1,9},{5... | collective-permute-start | bytes 1572872 | tf_op jit(solution)/shard_map/ppermute | solution.py:29
  129.5 13.7 %collective-permute-start.39 = (bf16[128,2048]{1,0:T(8,128)(2,1)S(1)}, bf16[128,2048]{1,0:T(8,128)(2,1)S(1)}, u32[]{:S(2)}, u32[]{:S(2)}) collective-permute-start(bf16[128,2048]{1,0:T(8,128)(2,1)S(1)} %get-tuple-element.58.refs_9_), channel_id=1, source_target_pairs={{0,16},{4,20},{8,24},{12,28},{16,0},{20,4},{24,8},{28,12},{1,17},{... | collective-permute-start | bytes 1572872 | tf_op jit(solution)/shard_map/ppermute | solution.py:29
  143.2 2.7 %collective-permute-start.42 = (bf16[256,2048]{1,0:T(8,128)(2,1)S(1)}, bf16[256,2048]{1,0:T(8,128)(2,1)S(1)}, u32[]{:S(2)}, u32[]{:S(2)}) collective-permute-start(bf16[256,2048]{1,0:T(8,128)(2,1)S(1)} %get-tuple-element.66), channel_id=1, source_target_pairs={{0,4},{4,0},{8,12},{12,8},{16,20},{20,16},{24,28},{28,24},{1,5},{5... | collective-permute-start | bytes 3145736 | tf_op jit(solution)/shard_map/ppermute | solution.py:29
  143.2 4.2 %collective-permute-start.44 = (bf16[256,2048]{1,0:T(8,128)(2,1)S(1)}, bf16[256,2048]{1,0:T(8,128)(2,1)S(1)}, u32[]{:S(2)}, u32[]{:S(2)}) collective-permute-start(bf16[256,2048]{1,0:T(8,128)(2,1)S(1)} %get-tuple-element.69), channel_id=1, source_target_pairs={{0,4},{4,0},{8,12},{12,8},{16,20},{20,16},{24,28},{28,24},{1,5},{5... | collective-permute-start | bytes 3145736 | tf_op jit(solution)/shard_map/ppermute | solution.py:29
  148.6 30.8 %collective-permute-start.43 = (bf16[256,2048]{1,0:T(8,128)(2,1)S(1)}, bf16[256,2048]{1,0:T(8,128)(2,1)S(1)}, u32[]{:S(2)}, u32[]{:S(2)}) collective-permute-start(bf16[256,2048]{1,0:T(8,128)(2,1)S(1)} %pad_maximum_fusion), channel_id=1, source_target_pairs={{0,8},{4,12},{8,0},{12,4},{16,24},{20,28},{24,16},{28,20},{1,9},{5... | collective-permute-start | bytes 3145736 | tf_op jit(solution)/shard_map/ppermute | solution.py:29
  149.3 30.1 %collective-permute-start.45 = (bf16[256,2048]{1,0:T(8,128)(2,1)S(1)}, bf16[256,2048]{1,0:T(8,128)(2,1)S(1)}, u32[]{:S(2)}, u32[]{:S(2)}) collective-permute-start(bf16[256,2048]{1,0:T(8,128)(2,1)S(1)} %pad_maximum_fusion.1), channel_id=1, source_target_pairs={{0,16},{4,20},{8,24},{12,28},{16,0},{20,4},{24,8},{28,12},{1,17},{... | collective-permute-start | bytes 3145736 | tf_op jit(solution)/shard_map/ppermute | solution.py:29
  150.9 23.1 %collective-permute-start.37 = (bf16[512,512]{1,0:T(8,128)(2,1)S(1)}, bf16[512,512]{1,0:T(8,128)(2,1)S(1)}, u32[]{:S(2)}, u32[]{:S(2)}) collective-permute-start(bf16[512,512]{1,0:T(8,128)(2,1)S(1)} %slice_bitcast_fusion), channel_id=1, source_target_pairs={{0,1},{1,0},{2,3},{3,2},{4,5},{5,4},{6,7},{7,6},{8,9},{9,8},{10,11... | collective-permute-start | bytes 1572872 | tf_op jit(solution)/shard_map/ppermute | solution.py:29
  151.5 28.9 %collective-permute-start.46 = (bf16[256,2048]{1,0:T(8,128)(2,1)S(1)}, bf16[256,2048]{1,0:T(8,128)(2,1)S(1)}, u32[]{:S(2)}, u32[]{:S(2)}) collective-permute-start(bf16[256,2048]{1,0:T(8,128)(2,1)S(1)} %get-tuple-element.74), channel_id=1, source_target_pairs={{0,4},{4,0},{8,12},{12,8},{16,20},{20,16},{24,28},{28,24},{1,5},{5... | collective-permute-start | bytes 3145736 | tf_op jit(solution)/shard_map/ppermute | solution.py:29
  151.6 27.8 %collective-permute-start.41 = (bf16[512,512]{1,0:T(8,128)(2,1)S(1)}, bf16[512,512]{1,0:T(8,128)(2,1)S(1)}, u32[]{:S(2)}, u32[]{:S(2)}) collective-permute-start(bf16[512,512]{1,0:T(8,128)(2,1)S(1)} %fusion.2), channel_id=1, source_target_pairs={{0,2},{1,3},{2,0},{3,1},{4,6},{5,7},{6,4},{7,5},{8,10},{9,11},{10,... | collective-permute-start | bytes 1572872 | tf_op jit(solution)/shard_map/ppermute | solution.py:29
  (2 other events, 48.9 us)

commit v8 on v7

--- a/solution.py
+++ b/solution.py
@@ -29,9 +29,9 @@
     return lax.ppermute(value, axis, [(i, i ^ mask) for i in range(lax.axis_size(axis))])
 
 
-def cut(value):
-    half = value.shape[0] // 2
-    return value[:half], value[half:]
+def cross(value, even, odd):
+    size = lax.axis_size("sample")
+    return lax.ppermute(value, "sample", [(i, i ^ (odd if i % 2 else even)) for i in range(size)])
 
 
 def chip_axes(size):
@@ -45,14 +45,16 @@
 
 def gather_head(head):
     size = lax.axis_size("sample")
+    core = lax.axis_index("sample") % 2
     first, second = chip_axes(size)
-    held = {mask: [flip(head, "sample", mask)] for mask in first + second}
-    held[0] = [head]
+    held = {mask: flip(head, "sample", mask) for mask in first + second}
+    held[0] = head
+    sibling = flip(head, "sample", 1)
     for a in first:
         for b in second:
-            top, bottom = cut(held[a][0])[0], cut(held[b][0])[1]
-            held[a | b] = [flip(top, "sample", b), flip(bottom, "sample", a)]
-    return held
+            passed = lax.optimization_barrier((jnp.where(core == 0, held[a], held[b]), sibling))[0]
+            held[a | b] = cross(passed, b, a)
+    return held, sibling
 
 
 def gather_features(features):
@@ -61,7 +63,7 @@
     for mask in list(range(2, size, 2)) + [1]:
         held[mask] = flip(features, "cls", mask)
     for mask in range(2, size, 2):
-        held[mask | 1] = flip(held[mask], "cls", 1)
+        held[mask | 1] = flip(lax.optimization_barrier((held[mask], held[1]))[0], "cls", 1)
     return [held[mask] for mask in range(size)]
 
 
@@ -86,12 +88,8 @@
     return jnp.transpose(jnp.broadcast_to(row, (LANES, row.shape[1])))
 
 
-def row_kernel(count, student_ref, scale_ref, ceiling_ref, *refs):
-    part_refs, (new_ref, total_ref, partial) = refs[:count], refs[count:]
-    mass = part_refs[0][...]
-    for ref in part_refs[1:]:
-        mass = mass + ref[...]
-    new_ref[...] = scale_ref[...] * jnp.minimum(1.0, ceiling_ref[...] / mass)
+def row_kernel(student_ref, scale_ref, ceiling_ref, mass_ref, new_ref, total_ref, partial):
+    new_ref[...] = scale_ref[...] * jnp.minimum(1.0, ceiling_ref[...] / mass_ref[...])
     rows, columns = student_ref.shape
     block = 64
 
@@ -169,12 +167,8 @@
     sums_ref[1:2, :] = jnp.sum(jnp.transpose(plan_sum[...]), axis=0, keepdims=True)
 
 
-def column_kernel(count, student_ref, scale_ref, *refs):
-    part_refs, (total_ref, inverse) = refs[:count], refs[count:]
-    mass = part_refs[0][...]
-    for ref in part_refs[1:]:
-        mass = mass + ref[...]
-    inverse[...] = as_column(1.0 / mass)
+def column_kernel(student_ref, scale_ref, mass_ref, total_ref, inverse):
+    inverse[...] = as_column(1.0 / mass_ref[...])
     rows, columns = student_ref.shape
     block = 8
 
@@ -200,16 +194,15 @@
         out_ref[:, at] = jnp.dot(left, grad_ref[:, at], preferred_element_type=f32).astype(bf16)
 
 
-def gradient_kernel(count, depth, paired, far, parts, student_ref, slope_ref, scale_ref, students_ref, turned_ref, *refs):
-    part_refs, head_refs = refs[:count], refs[count : count + len(parts)]
-    targets_ref, grad_ref, mine_ref, theirs_ref, share_ref, inverse, students = refs[count + len(parts) :]
+def gradient_kernel(
+    depth, paired, far, parts, student_ref, slope_ref, scale_ref, students_ref, mass_ref, turned_ref, *refs
+):
+    head_refs = refs[: len(parts)]
+    targets_ref, grad_ref, mine_ref, theirs_ref, share_ref, inverse, students = refs[len(parts) :]
     me, place = lax.axis_index("sample"), lax.axis_index("cls")
     chip, core = me // 2, me % 2
     groups = lax.axis_size("cls")
-    mass = part_refs[0][...]
-    for ref in part_refs[1:]:
-        mass = mass + ref[...]
-    inverse[...] = as_column(1.0 / mass)
+    inverse[...] = as_column(1.0 / mass_ref[...])
     students[...] = as_column(1.0 / students_ref[...])
     columns = student_ref.shape[1]
     tile = min(256, columns)
@@ -259,17 +252,16 @@
     chip, core = me // 2, me % 2
     first, second = chip_axes(samples)
 
-    pieces = gather_head(head)
+    pieces, sibling = gather_head(head)
     features_from = gather_features(features)
     paired = depth % LANES != 0
 
     def sides(mask, same):
-        other = [flip(part, "sample", 1) for part in same]
+        other = flip(same, "sample", 1) if mask else sibling
         if paired:
-            pairs = [(jnp.where(core == 0, s, o), jnp.where(core == 0, o, s)) for s, o in zip(same, other)]
-            return [((mask // 2, 0), jnp.concatenate([p[0] for p in pairs] + [p[1] for p in pairs], axis=0))]
-        both = [part[0] if len(part) == 1 else jnp.concatenate(part, axis=0) for part in (same, other)]
-        return [((mask // 2, side), part) for side, part in enumerate(both)]
+            pair = jnp.where(core == 0, same, other), jnp.where(core == 0, other, same)
+            return [((mask // 2, 0), jnp.concatenate(pair, axis=0))]
+        return [((mask // 2, 0), same), ((mask // 2, 1), other)]
 
     early = [part for mask in [0] + first + second for part in sides(mask, pieces[mask])]
     blocks, turned, logits = call(
@@ -279,7 +271,7 @@
     )
     late = []
     for mask in [a | b for a in first for b in second]:
-        late += sides(mask, list(lax.optimization_barrier((logits, *pieces[mask]))[1:]))
+        late += sides(mask, lax.optimization_barrier((logits, pieces[mask]))[1])
     tile = min(256, classes)
     student, slope, sums = call(
         functools.partial(student_kernel, depth, paired, [at for at, _ in late]),
@@ -288,33 +280,35 @@
         [pltpu.VMEM((2, rows, tile), f32), pltpu.VMEM((rows, LANES), f32), pltpu.VMEM((rows, LANES), f32)],
     )
 
-    def row_parts(value):
-        return [value] + [flip(value, "cls", mask) for mask in range(groups - 1, 0, -1)]
-
-    def column_parts(value):
-        value = value + flip(value, "sample", 1)
-        return [value] + [flip(value, "sample", mask) for mask in range(samples - 2, 0, -2)]
+    def total(value, axis, masks):
+        for part in [flip(value, axis, mask) for mask in reversed(masks)]:
+            value = lax.optimization_barrier(value + part)
+        return value
+
+    def row_total(value):
+        return total(value, "cls", range(1, groups))
+
+    def column_total(value):
+        return total(value + flip(value, "sample", 1), "sample", range(2, samples, 2))
 
     ceiling = (wide(class_cap) * ratio)[None]
-    parts = row_parts(sums)
-    students_mass = sum([part[0:1] for part in parts[1:]], parts[0][0:1])
-    parts = [part[1:2] for part in parts]
+    sums = row_total(sums)
+    students_mass, mass = sums[0:1], sums[1:2]
     scale = jnp.ones((1, classes), f32)
     for _ in range(ITERS):
         (mass,) = call(
-            functools.partial(column_kernel, len(parts)),
+            column_kernel,
             [((1, classes), f32)],
-            [student, scale] + parts,
+            [student, scale, mass],
             [pltpu.VMEM((rows, LANES), f32)],
         )
-        sent = column_parts(mass)
         scale, mass = call(
-            functools.partial(row_kernel, len(sent)),
+            row_kernel,
             [((1, classes), f32), ((1, rows), f32)],
-            [student, scale, ceiling] + sent,
+            [student, scale, ceiling, column_total(mass)],
             [pltpu.VMEM((rows, LANES), f32)],
         )
-        parts = row_parts(mass)
+        mass = row_total(mass)
 
     head_at = [at for at, _ in early + late]
     head_list = [part for _, part in early + late]
@@ -323,55 +317,52 @@
     far = (diagonal[-1][0] | diagonal[-1][1]) // 2
     near = [(a | b) // 2 for a, b in diagonal[:-1]] + near
     targets, grad, mine, theirs, share = call(
-        functools.partial(gradient_kernel, len(parts), depth, paired, far, head_at),
+        functools.partial(gradient_kernel, depth, paired, far, head_at),
         [((rows, classes), bf16)] * 2 + [((depth, classes), bf16)] * 2 + [((rows, width), bf16)],
-        [student, slope, scale, students_mass, turned] + parts + head_list,
+        [student, slope, scale, students_mass, mass, turned] + head_list,
         [pltpu.VMEM((rows, LANES), f32)] * 2,
     )
-    extra = {}
-
-    def send_diagonal(a, b, top, bottom):
-        extra.setdefault((b, 0), []).append(flip(top, "sample", a))
-        extra.setdefault((a, 1), []).append(flip(bottom, "sample", b))
-
-    block = (wide(mine) + wide(flip(theirs, "sample", 1))).astype(bf16)
-    halves = lax.optimization_barrier(cut(block))
-    send_diagonal(*diagonal[-1], *halves)
+    block = lax.optimization_barrier((wide(mine) + wide(flip(theirs, "sample", 1))).astype(bf16))
+    passed = {diagonal[-1]: cross(block, *diagonal[-1])}
     share_from = {groups - 2: flip(share, "cls", 1)}
 
     results = call(
-        functools.partial(products_kernel, len(halves), depth, paired, near, head_at),
+        functools.partial(products_kernel, 1, depth, paired, near, head_at),
         [((depth, classes), bf16)] * (2 * len(near)) + [((groups, rows, width), bf16)],
         [grad, turned] + head_list,
-        extra=halves,
+        extra=[block],
     )
     shares = results[-1]
-    arrived = [part for parts in extra.values() for part in parts] + list(share_from.values())
+    arrived = list(passed.values()) + list(share_from.values())
     theirs = lax.optimization_barrier((*results[1:-1:2], *arrived))
     arrived = iter(theirs[len(near) :])
-    extra = {at: [next(arrived) for _ in parts] for at, parts in extra.items()}
+    passed = {at: next(arrived) for at in passed}
     share_from = {mask: next(arrived) for mask in share_from}
+
+    onward = {1: shares[1]}
+    for mask in range(2, groups, 2):
+        received = share_from[mask] if mask in share_from else flip(shares[mask | 1], "cls", 1)
+        onward[mask] = (wide(shares[mask]) + wide(received)).astype(bf16)
+    ready = lax.optimization_barrier((*onward.values(), *theirs[: len(near)]))
+    theirs = ready[len(onward) :]
+    returned = [flip(value, "cls", mask) for mask, value in zip(onward, ready)]
+    grad_features = sum([wide(value) for value in returned], wide(shares[0])).astype(bf16)
+
     mixed = {
         2 * mask: wide(results[2 * i]) + wide(flip(theirs[i], "sample", 1)) for i, mask in enumerate(near)
     }
     for a, b in diagonal[:-1]:
-        send_diagonal(a, b, *cut(mixed[a | b].astype(bf16)))
-
-    returned = [flip(shares[1], "cls", 1)]
-    for mask in range(2, groups, 2):
-        received = share_from[mask] if mask in share_from else flip(shares[mask | 1], "cls", 1)
-        returned.append(flip((wide(shares[mask]) + wide(received)).astype(bf16), "cls", mask))
-
+        passed[a, b] = cross(mixed[a | b].astype(bf16), a, b)
     received = []
     for mask in first + second:
-        halves = list(cut(mixed[mask]))
-        for part in (0, 1):
-            for more in extra.get((mask, part), []):
-                halves[part] = halves[part] + wide(more)
-        received.append(flip(jnp.concatenate(halves, axis=0).astype(bf16), "sample", mask))
-    grad_head = sum([wide(part) for part in received], mixed[0]).astype(bf16)
-    returned = lax.optimization_barrier((*returned, *received))[: len(returned)]
-    grad_features = sum([wide(value) for value in returned], wide(shares[0])).astype(bf16)
+        block = mixed[mask]
+        for (a, b), more in passed.items():
+            if mask == (b if mask in second else a):
+                block = block + jnp.where((core == 0) == (mask in second), wide(more), 0.0)
+        received.append(flip(block.astype(bf16), "sample", mask))
+    received = lax.optimization_barrier((*received, grad_features))
+    grad_features = received[-1]
+    grad_head = sum([wide(part) for part in received[:-1]], mixed[0]).astype(bf16)
     return (targets, grad_features, grad_head)
 
 

time: 182 us -> 176 us (0.967)
  waiting for transfers between devices: 101 us -> 87 us
  Pallas kernels: 21.8 us -> 26.7 us
  starting transfers between devices: 51.9 us -> 47.5 us
  other arithmetic: 4.37 us -> 8.72 us
  local copies, waits for them, and re-layouts: 1.84 us -> 4.83 us
    ppermute x47 -> x42, waiting for transfers between devices: 101 us -> 87 us  [flip(): lax.ppermute(value, axis, [(i, i ^ mask) for i in range(lax.axis_size(axi...]
    ppermute x47 -> x42, starting transfers between devices: 51.9 us -> 44.5 us  [flip(): lax.ppermute(value, axis, [(i, i ^ mask) for i in range(lax.axis_size(axi...]
    pallas_call x10, Pallas kernels: 21.8 us -> 26.7 us  [call(): pl.pallas_call(kernel, out_shape=tuple((pltpu.VMEM(shape, dtype) for shap...]
    convert_element_type x3 -> x4, other arithmetic: 2.16 us -> 6.39 us  [the longest x1 3.39 us: per_device(): received.append(flip(block.astype(bf16), 'sample', mask))]
    ppermute x0 -> x2, starting transfers between devices: none -> 3.07 us  [cross(): lax.ppermute(value, 'sample', [(i, i ^ (odd if i % 2 else even)) for i in...]
    unnamed x9 -> x33, local copies, waits for them, and re-layouts: 1.41 us -> 3.98 us
  transfers between devices with their start and end apart: 47 -> 44, of which waited for: 35 -> 29; matrix products, arithmetic and copies ran while one was open for 2% -> 3% of each run, Pallas kernels for 6% -> 9%
where the time goes in v8:
time: 176 us
  waiting for transfers between devices  87 us (49%)
  starting transfers between devices  47.5 us (27%)
  Pallas kernels  26.7 us (15%)
  other arithmetic  8.72 us (5%)
  local copies, waits for them, and re-layouts  4.83 us (3%)
    ppermute x42, waiting for transfers between devices, flip(): lax.ppermute(value, axis, [(i, i ^ mask) for i in range(lax.axis_size(axi...  87 us
    ppermute x42, starting transfers between devices, flip(): lax.ppermute(value, axis, [(i, i ^ mask) for i in range(lax.axis_size(axi...  44.5 us
    pallas_call x10, Pallas kernels, call(): pl.pallas_call(kernel, out_shape=tuple((pltpu.VMEM(shape, dtype) for shap...  26.7 us
    unnamed x33, local copies, waits for them, and re-layouts  3.98 us
  transfers between devices with their start and end apart: 44, of which 29 were waited for; matrix products, arithmetic and copies ran while one was open for 3% of the time, Pallas kernels for 9%

profile of v8, /device:TPU:0, one launch (start us, length us, event | category | flops | bytes accessed | tf_op | source)
XLA Modules:
  0.0 175.8 jit_solution(10673856825293090731)
XLA Ops:
  0.6 3.0 %collective-permute-start.4 = (bf16[256,2048]{1,0:T(8,128)(2,1)}, bf16[256,2048]{1,0:T(8,128)(2,1)S(1)}, u32[]{:S(2)}, u32[]{:S(2)}) collective-permute-start(bf16[256,2048]{1,0:T(8,128)(2,1)} %refs_0_.5), channel_id=1, source_target_pairs={{0,8},{4,12},{8,0},{12,4},{16,24},{20,28},{24,16},{28,20},{1,9},{5... | collective-permute-start | bytes 3145736 | tf_op jit(solution)/shard_map/ppermute | solution.py:29
  3.6 1.5 collective-permute-start.6
  5.2 1.6 collective-permute-start
  6.7 2.6 %collective-permute-start.1 = (bf16[512,512]{1,0:T(8,128)(2,1)}, bf16[512,512]{1,0:T(8,128)(2,1)}, u32[]{:S(2)}, u32[]{:S(2)}) collective-permute-start(bf16[512,512]{1,0:T(8,128)(2,1)} %refs_0_.3), channel_id=1, source_target_pairs={{0,2},{1,3},{2,0},{3,1},{4,6},{5,7},{6,4},{7,5},{8,10},{9,11},{10,... | collective-permute-start | bytes 1572872 | tf_op jit(solution)/shard_map/ppermute | solution.py:29
  9.3 17.7 %collective-permute-done.4.refs_6_.refs_2_ = bf16[256,2048]{1,0:T(8,128)(2,1)S(1)} collective-permute-done((bf16[256,2048]{1,0:T(8,128)(2,1)}, bf16[256,2048]{1,0:T(8,128)(2,1)S(1)}, u32[]{:S(2)}, u32[]{:S(2)}) %collective-permute-start.4) | collective-permute-done | bytes 1048608 | tf_op jit(solution)/shard_map/ppermute | solution.py:29
  27.0 1.5 collective-permute-done.6.refs_8_.refs_4_
  29.2 1.5 collective-permute-start.8
  30.9 2.4 %collective-permute-done.1.refs_2_ = bf16[512,512]{1,0:T(8,128)(2,1)} collective-permute-done((bf16[512,512]{1,0:T(8,128)(2,1)}, bf16[512,512]{1,0:T(8,128)(2,1)}, u32[]{:S(2)}, u32[]{:S(2)}) %collective-permute-start.1) | collective-permute-done | bytes 524320 | tf_op jit(solution)/shard_map/ppermute | solution.py:29
  33.7 12.0 %collective-permute-done.2.refs_3_ = bf16[512,512]{1,0:T(8,128)(2,1)S(1)} collective-permute-done((bf16[512,512]{1,0:T(8,128)(2,1)}, bf16[512,512]{1,0:T(8,128)(2,1)S(1)}, u32[]{:S(2)}, u32[]{:S(2)}) %collective-permute-start.2) | collective-permute-done | bytes 524320 | tf_op jit(solution)/shard_map/ppermute | solution.py:29
  45.7 5.1 %shard_map.58 = (bf16[4,512,512]{2,1,0:T(8,128)(2,1)S(1)}, bf16[4,512,512]{2,1,0:T(8,128)(2,1)S(1)}, f32[512,2048]{1,0:T(8,128)S(1)}) custom-call(bf16[512,512]{1,0:T(8,128)(2,1)S(1)} %copy-done.10, bf16[512,512]{1,0:T(8,128)(2,1)} %collective-permute-done.refs_1_, bf16[512,512]{1,0:T(8,128)(2,1)} %collective-permute-done.1.refs_2_, ...), custom_call_target="tpu_custom_call" | custom-call | flops 1 | bytes 1 | tf_op jit(solution)/shard_map/pallas_call | solution.py:76
  51.0 2.6 %collective-permute-done.9.refs_1_.refs_7_ = bf16[256,2048]{1,0:T(8,128)(2,1)S(1)} collective-permute-done((bf16[256,2048]{1,0:T(8,128)(2,1)S(1)}, bf16[256,2048]{1,0:T(8,128)(2,1)S(1)}, u32[]{:S(2)}, u32[]{:S(2)}) %collective-permute-start.9) | collective-permute-done | bytes 1048608 | tf_op jit(solution)/shard_map/ppermute | solution.py:29
  53.6 2.4 %shard_map.59 = (f32[512,2048]{1,0:T(8,128)S(1)}, bf16[512,2048]{1,0:T(8,128)(2,1)S(1)}, f32[2,512]{1,0:T(2,128)S(1)}) custom-call(f32[512,2048]{1,0:T(8,128)S(1)} %get-tuple-element.44.logits_ref, bf16[4,512,512]{2,1,0:T(8,128)(2,1)S(1)} %get-tuple-element.45.blocks_ref, bf16[256,2048]{1,0:T(8,128)(2,1)S(1)} %collective-permute-done.8.refs_0_.refs_6_, ...), custom_call_target="tpu_custom_call" | custom-call | flops 1 | bytes 1 | tf_op jit(solution)/shard_map/pallas_call | solution.py:76
  56.0 3.6 %collective-permute-start.10 = (f32[2,512]{1,0:T(2,128)S(1)}, f32[2,512]{1,0:T(2,128)S(1)}, u32[]{:S(2)}, u32[]{:S(2)}) collective-permute-start(f32[2,512]{1,0:T(2,128)S(1)} %get-tuple-element.50), channel_id=1, source_target_pairs={{0,3},{1,2},{2,1},{3,0},{4,7},{5,6},{6,5},{7,4},{8,11},{9,10},{10,... | collective-permute-start | bytes 12296 | tf_op jit(solution)/shard_map/ppermute | solution.py:29
  61.5 2.6 %collective-permute-done.11 = f32[2,512]{1,0:T(2,128)S(1)} collective-permute-done((f32[2,512]{1,0:T(2,128)S(1)}, f32[2,512]{1,0:T(2,128)S(1)}, u32[]{:S(2)}, u32[]{:S(2)}) %collective-permute-start.11) | collective-permute-done | bytes 4128 | tf_op jit(solution)/shard_map/ppermute | solution.py:29
  64.9 1.2 collective-permute-done.13
  66.6 1.5 collective-permute-start.15
  68.2 1.5 collective-permute-start.16
  70.7 1.1 collective-permute-done.16
  72.5 1.5 collective-permute-start.17
  74.6 2.3 %collective-permute-start.19 = (f32[1,512]{1,0:T(1,128)S(1)}, f32[1,512]{1,0:T(1,128)S(1)}, u32[]{:S(2)}, u32[]{:S(2)}) collective-permute-start(f32[1,512]{1,0:T(1,128)S(1)} %get-tuple-element.52), channel_id=1, source_target_pairs={{0,1},{1,0},{2,3},{3,2},{4,5},{5,4},{6,7},{7,6},{8,9},{9,8},{10,11... | collective-permute-start | bytes 6152 | tf_op jit(solution)/shard_map/ppermute | solution.py:29
  79.2 1.2 collective-permute-done.20
  80.4 1.5 collective-permute-start.21
  81.9 1.5 collective-permute-start.22
  84.0 1.1 collective-permute-done.21
  85.6 1.5 collective-permute-done.23
  87.7 2.6 %collective-permute-start.24 = (f32[1,512]{1,0:T(1,128)S(1)}, f32[1,512]{1,0:T(1,128)S(1)}, u32[]{:S(2)}, u32[]{:S(2)}) collective-permute-start(f32[1,512]{1,0:T(1,128)S(1)} %get-tuple-element.54), channel_id=1, source_target_pairs={{0,3},{1,2},{2,1},{3,0},{4,7},{5,6},{6,5},{7,4},{8,11},{9,10},{10,... | collective-permute-start | bytes 6152 | tf_op jit(solution)/shard_map/ppermute | solution.py:29
  93.2 1.7 collective-permute-done.25
  95.6 1.2 collective-permute-done.27
  97.4 1.5 collective-permute-start.29
  98.9 1.5 collective-permute-start.30
  100.4 1.1 collective-permute-done.28
  101.5 1.1 collective-permute-done.30
  103.2 1.5 collective-permute-start.31
  105.6 2.0 %collective-permute-start.33 = (f32[1,512]{1,0:T(1,128)S(1)}, f32[1,512]{1,0:T(1,128)S(1)}, u32[]{:S(2)}, u32[]{:S(2)}) collective-permute-start(f32[1,512]{1,0:T(1,128)S(1)} %get-tuple-element.56), channel_id=1, source_target_pairs={{0,1},{1,0},{2,3},{3,2},{4,5},{5,4},{6,7},{7,6},{8,9},{9,8},{10,11... | collective-permute-start | bytes 6152 | tf_op jit(solution)/shard_map/ppermute | solution.py:29
  109.2 5.2 %shard_map.66 = (bf16[512,2048]{1,0:T(8,128)(2,1)S(1)}, bf16[512,2048]{1,0:T(8,128)(2,1)S(1)}, bf16[256,2048]{1,0:T(8,128)(2,1)S(1)}, bf16[256,2048]{1,0:T(8,128)(2,1)S(1)}, bf16[512,512]{1,0:T(8,128)(2,1)S(1)}) custom-call(f32[512,2048]{1,0:T(8,128)S(1)} %get-tuple-element.48.student_ref, bf16[512,2048]{1,0:T(8,128)(2,1)S(1)} %get-tuple-element.49.slope_ref, ...), custom_call_target="tpu_custom_call" | custom-call | flops 1 | bytes 1 | tf_op jit(solution)/shard_map/pallas_call | solution.py:76
  114.6 2.6 %collective-permute-done.34 = bf16[256,2048]{1,0:T(8,128)(2,1)S(1)} collective-permute-done((bf16[256,2048]{1,0:T(8,128)(2,1)S(1)}, bf16[256,2048]{1,0:T(8,128)(2,1)S(1)}, u32[]{:S(2)}, u32[]{:S(2)}) %collective-permute-start.34) | collective-permute-done | bytes 1048608 | tf_op jit(solution)/shard_map/ppermute | solution.py:29
  117.6 1.6 collective-permute-start.35
  119.1 2.0 %collective-permute-start.36 = (bf16[512,512]{1,0:T(8,128)(2,1)S(1)}, bf16[512,512]{1,0:T(8,128)(2,1)S(1)}, u32[]{:S(2)}, u32[]{:S(2)}) collective-permute-start(bf16[512,512]{1,0:T(8,128)(2,1)S(1)} %get-tuple-element.67), channel_id=1, source_target_pairs={{0,1},{1,0},{2,3},{3,2},{4,5},{5,4},{6,7},{7,6},{8,9},{9,8},{10,11... | collective-permute-start | bytes 1572872 | tf_op jit(solution)/shard_map/ppermute | solution.py:29
  121.2 10.1 %shard_map.67 = (bf16[256,2048]{1,0:T(8,128)(2,1)S(1)}, bf16[256,2048]{1,0:T(8,128)(2,1)}, bf16[256,2048]{1,0:T(8,128)(2,1)S(1)}, bf16[256,2048]{1,0:T(8,128)(2,...) custom-call(bf16[512,2048]{1,0:T(8,128)(2,1)S(1)} %get-tuple-element.59.grad_ref,, ...), custom_call_target="tpu_custom_call" | custom-call | flops 1 | bytes 1 | tf_op jit(solution)/shard_map/pallas_call | solution.py:76
  136.1 2.5 %collective-permute-done.37 = bf16[256,2048]{1,0:T(8,128)(2,1)} collective-permute-done((bf16[256,2048]{1,0:T(8,128)(2,1)}, bf16[256,2048]{1,0:T(8,128)(2,1)}, u32[]{:S(2)}, u32[]{:S(2)}) %collective-permute-start.37) | collective-permute-done | bytes 1048608 | tf_op jit(solution)/shard_map/ppermute | solution.py:29
  138.6 1.5 collective-permute-done.39
  140.1 3.4 %fusion.3 = (bf16[256,2048]{1,0:T(8,128)(2,1)S(1)}, bf16[256,2048]{1,0:T(8,128)(2,1)S(1)}) fusion(bf16[256,2048]{1,0:T(8,128)(2,1)} %collective-permute-done.35, bf16[256,2048]{1,0:T(8,128)(2,1)} %collective-permute-done.39, bf16[256,2048]{1,0:T(8,128)(2,1)S(1)} %copy-done.9, pred[]{:T(512)S(6)} %eq.11, pred[]{:T(512)S(6)} %eq.12, ...), kind=kLoop, calls=%fused_computation.5 | loop fusion | flops 6815744 | bytes 7340034 | tf_op jit(solution)/shard_map/convert_element_type | solution.py:362
  145.9 1.1 collective-permute-start.42
  147.0 1.3 copy.6
  148.3 21.1 %collective-permute-done.41 = bf16[512,512]{1,0:T(8,128)(2,1)S(1)} collective-permute-done((bf16[512,512]{1,0:T(8,128)(2,1)S(1)}, bf16[512,512]{1,0:T(8,128)(2,1)S(1)}, u32[]{:S(2)}, u32[]{:S(2)}) %collective-permute-start.41) | collective-permute-done | bytes 524320 | tf_op jit(solution)/shard_map/ppermute | solution.py:29
  169.4 2.6 %collective-permute-done.42 = bf16[512,512]{1,0:T(8,128)(2,1)S(1)} collective-permute-done((bf16[512,512]{1,0:T(8,128)(2,1)S(1)}, bf16[512,512]{1,0:T(8,128)(2,1)S(1)}, u32[]{:S(2)}, u32[]{:S(2)}) %collective-permute-start.42) | collective-permute-done | bytes 524320 | tf_op jit(solution)/shard_map/ppermute | solution.py:29
  172.0 2.0 %fusion.5 = bf16[512,512]{1,0:T(8,128)(2,1)} fusion(bf16[512,512]{1,0:T(8,128)(2,1)S(1)} %collective-permute-done.42, bf16[512,512]{1,0:T(8,128)(2,1)S(1)} %collective-permute-done.41, bf16[4,512,512]{2,1,0:T(8,128)(2,1)} %copy-done.4), kind=kLoop, calls=%fused_computation.10 | loop fusion | flops 1572864 | bytes 2097152 | tf_op jit(solution)/shard_map/convert_element_type | solution.py:349
  174.1 1.7 add_convert_fusion
  (117 shorter events, 26.1 us)
Async XLA Ops:
  0.6 45.1 %copy-start.2 = (bf16[256,2048]{1,0:T(8,128)(2,1)S(1)}, bf16[256,2048]{1,0:T(8,128)(2,1)}, u32[]{:S(2)}) copy-start(bf16[256,2048]{1,0:T(8,128)(2,1)} %refs_0_.5) | copy-start | bytes 3145732
  0.6 26.4 %collective-permute-start.4 = (bf16[256,2048]{1,0:T(8,128)(2,1)}, bf16[256,2048]{1,0:T(8,128)(2,1)S(1)}, u32[]{:S(2)}, u32[]{:S(2)}) collective-permute-start(bf16[256,2048]{1,0:T(8,128)(2,1)} %refs_0_.5), channel_id=1, source_target_pairs={{0,8},{4,12},{8,0},{12,4},{16,24},{20,28},{24,16},{28,20},{1,9},{5... | collective-permute-start | bytes 3145736 | tf_op jit(solution)/shard_map/ppermute | solution.py:29
  3.6 24.8 %collective-permute-start.6 = (bf16[256,2048]{1,0:T(8,128)(2,1)}, bf16[256,2048]{1,0:T(8,128)(2,1)S(1)}, u32[]{:S(2)}, u32[]{:S(2)}) collective-permute-start(bf16[256,2048]{1,0:T(8,128)(2,1)} %refs_0_.5), channel_id=1, source_target_pairs={{0,16},{4,20},{8,24},{12,28},{16,0},{20,4},{24,8},{28,12},{1,17},{... | collective-permute-start | bytes 3145736 | tf_op jit(solution)/shard_map/ppermute | solution.py:29
  5.2 23.4 %collective-permute-start.3 = (bf16[256,2048]{1,0:T(8,128)(2,1)}, bf16[256,2048]{1,0:T(8,128)(2,1)}, u32[]{:S(2)}, u32[]{:S(2)}) collective-permute-start(bf16[256,2048]{1,0:T(8,128)(2,1)} %refs_0_.5), channel_id=1, source_target_pairs={{0,4},{4,0},{8,12},{12,8},{16,20},{20,16},{24,28},{28,24},{1,5},{5... | collective-permute-start | bytes 3145736 | tf_op jit(solution)/shard_map/ppermute | solution.py:29
  5.2 25.8 %collective-permute-start = (bf16[512,512]{1,0:T(8,128)(2,1)}, bf16[512,512]{1,0:T(8,128)(2,1)}, u32[]{:S(2)}, u32[]{:S(2)}) collective-permute-start(bf16[512,512]{1,0:T(8,128)(2,1)} %refs_0_.3), channel_id=1, source_target_pairs={{0,1},{1,0},{2,3},{3,2},{4,5},{5,4},{6,7},{7,6},{8,9},{9,8},{10,11... | collective-permute-start | bytes 1572872 | tf_op jit(solution)/shard_map/ppermute | solution.py:29
  6.7 26.6 %collective-permute-start.1 = (bf16[512,512]{1,0:T(8,128)(2,1)}, bf16[512,512]{1,0:T(8,128)(2,1)}, u32[]{:S(2)}, u32[]{:S(2)}) collective-permute-start(bf16[512,512]{1,0:T(8,128)(2,1)} %refs_0_.3), channel_id=1, source_target_pairs={{0,2},{1,3},{2,0},{3,1},{4,6},{5,7},{6,4},{7,5},{8,10},{9,11},{10,... | collective-permute-start | bytes 1572872 | tf_op jit(solution)/shard_map/ppermute | solution.py:29
  9.3 36.4 %copy-start.10 = (bf16[512,512]{1,0:T(8,128)(2,1)S(1)}, bf16[512,512]{1,0:T(8,128)(2,1)}, u32[]{:S(2)}) copy-start(bf16[512,512]{1,0:T(8,128)(2,1)} %refs_0_.3) | copy-start | bytes 1572868
  28.5 22.4 %copy-start = (bf16[256,2048]{1,0:T(8,128)(2,1)}, bf16[256,2048]{1,0:T(8,128)(2,1)S(1)}, u32[]{:S(2)}) copy-start(bf16[256,2048]{1,0:T(8,128)(2,1)S(1)} %collective-permute-done.6.refs_8_.refs_4_) | copy-start | bytes 3145732
  28.6 17.1 %collective-permute-start.5 = (bf16[256,2048]{1,0:T(8,128)(2,1)S(1)}, bf16[256,2048]{1,0:T(8,128)(2,1)S(1)}, u32[]{:S(2)}, u32[]{:S(2)}) collective-permute-start(bf16[256,2048]{1,0:T(8,128)(2,1)S(1)} %collective-permute-done.4.refs_6_.refs_2_), channel_id=1, source_target_pairs={{0,4},{4,0},{8,12},{12,8},{16,20},{20,16},{24,28},{28,24},{1,5},{5... | collective-permute-start | bytes 3145736 | tf_op jit(solution)/shard_map/ppermute | solution.py:29
  28.7 17.0 %collective-permute-start.7 = (bf16[256,2048]{1,0:T(8,128)(2,1)S(1)}, bf16[256,2048]{1,0:T(8,128)(2,1)S(1)}, u32[]{:S(2)}, u32[]{:S(2)}) collective-permute-start(bf16[256,2048]{1,0:T(8,128)(2,1)S(1)} %collective-permute-done.6.refs_8_.refs_4_), channel_id=1, source_target_pairs={{0,4},{4,0},{8,12},{12,8},{16,20},{20,16},{24,28},{28,24},{1,5},{5... | collective-permute-start | bytes 3145736 | tf_op jit(solution)/shard_map/ppermute | solution.py:29
  29.2 21.7 %collective-permute-start.8 = (bf16[256,2048]{1,0:T(8,128)(2,1)S(1)}, bf16[256,2048]{1,0:T(8,128)(2,1)S(1)}, u32[]{:S(2)}, u32[]{:S(2)}) collective-permute-start(bf16[256,2048]{1,0:T(8,128)(2,1)S(1)} %broadcast_select_fusion), channel_id=1, source_target_pairs={{0,16},{4,12},{8,24},{12,4},{16,0},{20,28},{24,8},{28,20},{1,17},{... | collective-permute-start | bytes 3145736 | tf_op jit(solution)/shard_map/ppermute | solution.py:34
  33.3 12.4 %collective-permute-start.2 = (bf16[512,512]{1,0:T(8,128)(2,1)}, bf16[512,512]{1,0:T(8,128)(2,1)S(1)}, u32[]{:S(2)}, u32[]{:S(2)}) collective-permute-start(bf16[512,512]{1,0:T(8,128)(2,1)} %collective-permute-done.1.refs_2_), channel_id=1, source_target_pairs={{0,1},{1,0},{2,3},{3,2},{4,5},{5,4},{6,7},{7,6},{8,9},{9,8},{10,11... | collective-permute-start | bytes 1572872 | tf_op jit(solution)/shard_map/ppermute | solution.py:29
  50.9 2.7 %collective-permute-start.9 = (bf16[256,2048]{1,0:T(8,128)(2,1)S(1)}, bf16[256,2048]{1,0:T(8,128)(2,1)S(1)}, u32[]{:S(2)}, u32[]{:S(2)}) collective-permute-start(bf16[256,2048]{1,0:T(8,128)(2,1)S(1)} %collective-permute-done.8.refs_0_.refs_6_), channel_id=1, source_target_pairs={{0,4},{4,0},{8,12},{12,8},{16,20},{20,16},{24,28},{28,24},{1,5},{5... | collective-permute-start | bytes 3145736 | tf_op jit(solution)/shard_map/ppermute | solution.py:29
  56.0 5.5 %collective-permute-start.10 = (f32[2,512]{1,0:T(2,128)S(1)}, f32[2,512]{1,0:T(2,128)S(1)}, u32[]{:S(2)}, u32[]{:S(2)}) collective-permute-start(f32[2,512]{1,0:T(2,128)S(1)} %get-tuple-element.50), channel_id=1, source_target_pairs={{0,3},{1,2},{2,1},{3,0},{4,7},{5,6},{6,5},{7,4},{8,11},{9,10},{10,... | collective-permute-start | bytes 12296 | tf_op jit(solution)/shard_map/ppermute | solution.py:29
  59.6 4.5 %collective-permute-start.11 = (f32[2,512]{1,0:T(2,128)S(1)}, f32[2,512]{1,0:T(2,128)S(1)}, u32[]{:S(2)}, u32[]{:S(2)}) collective-permute-start(f32[2,512]{1,0:T(2,128)S(1)} %get-tuple-element.50), channel_id=1, source_target_pairs={{0,2},{1,3},{2,0},{3,1},{4,6},{5,7},{6,4},{7,5},{8,10},{9,11},{10,... | collective-permute-start | bytes 12296 | tf_op jit(solution)/shard_map/ppermute | solution.py:29
  59.6 4.5 %collective-permute-start.12 = (f32[2,512]{1,0:T(2,128)S(1)}, f32[2,512]{1,0:T(2,128)S(1)}, u32[]{:S(2)}, u32[]{:S(2)}) collective-permute-start(f32[2,512]{1,0:T(2,128)S(1)} %get-tuple-element.50), channel_id=1, source_target_pairs={{0,1},{1,0},{2,3},{3,2},{4,5},{5,4},{6,7},{7,6},{8,9},{9,8},{10,11... | collective-permute-start | bytes 12296 | tf_op jit(solution)/shard_map/ppermute | solution.py:29
  64.8 1.2 collective-permute-start.13
  66.1 4.6 %collective-permute-start.14 = (f32[1,2048]{1,0:T(1,128)S(1)}, f32[1,2048]{1,0:T(1,128)S(1)}, u32[]{:S(2)}, u32[]{:S(2)}) collective-permute-start(f32[1,2048]{1,0:T(1,128)S(1)} %add.114), channel_id=1, source_target_pairs={{0,24},{4,28},{8,16},{12,20},{16,8},{20,12},{24,0},{28,4},{1,25},{... | collective-permute-start | bytes 24584 | tf_op jit(solution)/shard_map/ppermute | solution.py:29
  66.6 4.1 %collective-permute-start.15 = (f32[1,2048]{1,0:T(1,128)S(1)}, f32[1,2048]{1,0:T(1,128)S(1)}, u32[]{:S(2)}, u32[]{:S(2)}) collective-permute-start(f32[1,2048]{1,0:T(1,128)S(1)} %add.114), channel_id=1, source_target_pairs={{0,16},{4,20},{8,24},{12,28},{16,0},{20,4},{24,8},{28,12},{1,17},{... | collective-permute-start | bytes 24584 | tf_op jit(solution)/shard_map/ppermute | solution.py:29
  68.2 3.7 %collective-permute-start.16 = (f32[1,2048]{1,0:T(1,128)S(1)}, f32[1,2048]{1,0:T(1,128)S(1)}, u32[]{:S(2)}, u32[]{:S(2)}) collective-permute-start(f32[1,2048]{1,0:T(1,128)S(1)} %add.114), channel_id=1, source_target_pairs={{0,8},{4,12},{8,0},{12,4},{16,24},{20,28},{24,16},{28,20},{1,9},{5... | collective-permute-start | bytes 24584 | tf_op jit(solution)/shard_map/ppermute | solution.py:29
  72.5 5.4 %collective-permute-start.17 = (f32[1,512]{1,0:T(1,128)S(1)}, f32[1,512]{1,0:T(1,128)S(1)}, u32[]{:S(2)}, u32[]{:S(2)}) collective-permute-start(f32[1,512]{1,0:T(1,128)S(1)} %get-tuple-element.52), channel_id=1, source_target_pairs={{0,3},{1,2},{2,1},{3,0},{4,7},{5,6},{6,5},{7,4},{8,11},{9,10},{10,... | collective-permute-start | bytes 6152 | tf_op jit(solution)/shard_map/ppermute | solution.py:29
  74.0 4.5 %collective-permute-start.18 = (f32[1,512]{1,0:T(1,128)S(1)}, f32[1,512]{1,0:T(1,128)S(1)}, u32[]{:S(2)}, u32[]{:S(2)}) collective-permute-start(f32[1,512]{1,0:T(1,128)S(1)} %get-tuple-element.52), channel_id=1, source_target_pairs={{0,2},{1,3},{2,0},{3,1},{4,6},{5,7},{6,4},{7,5},{8,10},{9,11},{10,... | collective-permute-start | bytes 6152 | tf_op jit(solution)/shard_map/ppermute | solution.py:29
  74.6 3.9 %collective-permute-start.19 = (f32[1,512]{1,0:T(1,128)S(1)}, f32[1,512]{1,0:T(1,128)S(1)}, u32[]{:S(2)}, u32[]{:S(2)}) collective-permute-start(f32[1,512]{1,0:T(1,128)S(1)} %get-tuple-element.52), channel_id=1, source_target_pairs={{0,1},{1,0},{2,3},{3,2},{4,5},{5,4},{6,7},{7,6},{8,9},{9,8},{10,11... | collective-permute-start | bytes 6152 | tf_op jit(solution)/shard_map/ppermute | solution.py:29
  79.2 1.2 collective-permute-start.20
  80.4 4.6 %collective-permute-start.21 = (f32[1,2048]{1,0:T(1,128)S(1)}, f32[1,2048]{1,0:T(1,128)S(1)}, u32[]{:S(2)}, u32[]{:S(2)}) collective-permute-start(f32[1,2048]{1,0:T(1,128)S(1)} %add.121), channel_id=1, source_target_pairs={{0,24},{4,28},{8,16},{12,20},{16,8},{20,12},{24,0},{28,4},{1,25},{... | collective-permute-start | bytes 24584 | tf_op jit(solution)/shard_map/ppermute | solution.py:29
  81.9 3.7 %collective-permute-start.22 = (f32[1,2048]{1,0:T(1,128)S(1)}, f32[1,2048]{1,0:T(1,128)S(1)}, u32[]{:S(2)}, u32[]{:S(2)}) collective-permute-start(f32[1,2048]{1,0:T(1,128)S(1)} %add.121), channel_id=1, source_target_pairs={{0,16},{4,20},{8,24},{12,28},{16,0},{20,4},{24,8},{28,12},{1,17},{... | collective-permute-start | bytes 24584 | tf_op jit(solution)/shard_map/ppermute | solution.py:29
  83.4 3.7 %collective-permute-start.23 = (f32[1,2048]{1,0:T(1,128)S(1)}, f32[1,2048]{1,0:T(1,128)S(1)}, u32[]{:S(2)}, u32[]{:S(2)}) collective-permute-start(f32[1,2048]{1,0:T(1,128)S(1)} %add.121), channel_id=1, source_target_pairs={{0,8},{4,12},{8,0},{12,4},{16,24},{20,28},{24,16},{28,20},{1,9},{5... | collective-permute-start | bytes 24584 | tf_op jit(solution)/shard_map/ppermute | solution.py:29
  87.7 5.4 %collective-permute-start.24 = (f32[1,512]{1,0:T(1,128)S(1)}, f32[1,512]{1,0:T(1,128)S(1)}, u32[]{:S(2)}, u32[]{:S(2)}) collective-permute-start(f32[1,512]{1,0:T(1,128)S(1)} %get-tuple-element.54), channel_id=1, source_target_pairs={{0,3},{1,2},{2,1},{3,0},{4,7},{5,6},{6,5},{7,4},{8,11},{9,10},{10,... | collective-permute-start | bytes 6152 | tf_op jit(solution)/shard_map/ppermute | solution.py:29
  90.4 4.5 %collective-permute-start.25 = (f32[1,512]{1,0:T(1,128)S(1)}, f32[1,512]{1,0:T(1,128)S(1)}, u32[]{:S(2)}, u32[]{:S(2)}) collective-permute-start(f32[1,512]{1,0:T(1,128)S(1)} %get-tuple-element.54), channel_id=1, source_target_pairs={{0,2},{1,3},{2,0},{3,1},{4,6},{5,7},{6,4},{7,5},{8,10},{9,11},{10,... | collective-permute-start | bytes 6152 | tf_op jit(solution)/shard_map/ppermute | solution.py:29
  91.3 3.6 %collective-permute-start.26 = (f32[1,512]{1,0:T(1,128)S(1)}, f32[1,512]{1,0:T(1,128)S(1)}, u32[]{:S(2)}, u32[]{:S(2)}) collective-permute-start(f32[1,512]{1,0:T(1,128)S(1)} %get-tuple-element.54), channel_id=1, source_target_pairs={{0,1},{1,0},{2,3},{3,2},{4,5},{5,4},{6,7},{7,6},{8,9},{9,8},{10,11... | collective-permute-start | bytes 6152 | tf_op jit(solution)/shard_map/ppermute | solution.py:29
  95.6 1.2 collective-permute-start.27
  96.8 4.6 %collective-permute-start.28 = (f32[1,2048]{1,0:T(1,128)S(1)}, f32[1,2048]{1,0:T(1,128)S(1)}, u32[]{:S(2)}, u32[]{:S(2)}) collective-permute-start(f32[1,2048]{1,0:T(1,128)S(1)} %add.128), channel_id=1, source_target_pairs={{0,24},{4,28},{8,16},{12,20},{16,8},{20,12},{24,0},{28,4},{1,25},{... | collective-permute-start | bytes 24584 | tf_op jit(solution)/shard_map/ppermute | solution.py:29
  97.4 4.1 %collective-permute-start.29 = (f32[1,2048]{1,0:T(1,128)S(1)}, f32[1,2048]{1,0:T(1,128)S(1)}, u32[]{:S(2)}, u32[]{:S(2)}) collective-permute-start(f32[1,2048]{1,0:T(1,128)S(1)} %add.128), channel_id=1, source_target_pairs={{0,16},{4,20},{8,24},{12,28},{16,0},{20,4},{24,8},{28,12},{1,17},{... | collective-permute-start | bytes 24584 | tf_op jit(solution)/shard_map/ppermute | solution.py:29
  98.9 3.7 %collective-permute-start.30 = (f32[1,2048]{1,0:T(1,128)S(1)}, f32[1,2048]{1,0:T(1,128)S(1)}, u32[]{:S(2)}, u32[]{:S(2)}) collective-permute-start(f32[1,2048]{1,0:T(1,128)S(1)} %add.128), channel_id=1, source_target_pairs={{0,8},{4,12},{8,0},{12,4},{16,24},{20,28},{24,16},{28,20},{1,9},{5... | collective-permute-start | bytes 24584 | tf_op jit(solution)/shard_map/ppermute | solution.py:29
  103.2 5.4 %collective-permute-start.31 = (f32[1,512]{1,0:T(1,128)S(1)}, f32[1,512]{1,0:T(1,128)S(1)}, u32[]{:S(2)}, u32[]{:S(2)}) collective-permute-start(f32[1,512]{1,0:T(1,128)S(1)} %get-tuple-element.56), channel_id=1, source_target_pairs={{0,3},{1,2},{2,1},{3,0},{4,7},{5,6},{6,5},{7,4},{8,11},{9,10},{10,... | collective-permute-start | bytes 6152 | tf_op jit(solution)/shard_map/ppermute | solution.py:29
  104.7 4.5 %collective-permute-start.32 = (f32[1,512]{1,0:T(1,128)S(1)}, f32[1,512]{1,0:T(1,128)S(1)}, u32[]{:S(2)}, u32[]{:S(2)}) collective-permute-start(f32[1,512]{1,0:T(1,128)S(1)} %get-tuple-element.56), channel_id=1, source_target_pairs={{0,2},{1,3},{2,0},{3,1},{4,6},{5,7},{6,4},{7,5},{8,10},{9,11},{10,... | collective-permute-start | bytes 6152 | tf_op jit(solution)/shard_map/ppermute | solution.py:29
  105.6 3.6 %collective-permute-start.33 = (f32[1,512]{1,0:T(1,128)S(1)}, f32[1,512]{1,0:T(1,128)S(1)}, u32[]{:S(2)}, u32[]{:S(2)}) collective-permute-start(f32[1,512]{1,0:T(1,128)S(1)} %get-tuple-element.56), channel_id=1, source_target_pairs={{0,1},{1,0},{2,3},{3,2},{4,5},{5,4},{6,7},{7,6},{8,9},{9,8},{10,11... | collective-permute-start | bytes 6152 | tf_op jit(solution)/shard_map/ppermute | solution.py:29
  114.5 2.7 %collective-permute-start.34 = (bf16[256,2048]{1,0:T(8,128)(2,1)S(1)}, bf16[256,2048]{1,0:T(8,128)(2,1)S(1)}, u32[]{:S(2)}, u32[]{:S(2)}) collective-permute-start(bf16[256,2048]{1,0:T(8,128)(2,1)S(1)} %get-tuple-element.61), channel_id=1, source_target_pairs={{0,4},{4,0},{8,12},{12,8},{16,20},{20,16},{24,28},{28,24},{1,5},{5... | collective-permute-start | bytes 3145736 | tf_op jit(solution)/shard_map/ppermute | solution.py:29
  117.6 16.5 %collective-permute-start.35 = (bf16[256,2048]{1,0:T(8,128)(2,1)S(1)}, bf16[256,2048]{1,0:T(8,128)(2,1)}, u32[]{:S(2)}, u32[]{:S(2)}) collective-permute-start(bf16[256,2048]{1,0:T(8,128)(2,1)S(1)} %add_convert_fusion.1.refs_8_), channel_id=1, source_target_pairs={{0,8},{4,20},{8,0},{12,28},{16,24},{20,4},{24,16},{28,12},{1,9},{5... | collective-permute-start | bytes 3145736 | tf_op jit(solution)/shard_map/ppermute | solution.py:34
  119.1 14.9 %collective-permute-start.36 = (bf16[512,512]{1,0:T(8,128)(2,1)S(1)}, bf16[512,512]{1,0:T(8,128)(2,1)S(1)}, u32[]{:S(2)}, u32[]{:S(2)}) collective-permute-start(bf16[512,512]{1,0:T(8,128)(2,1)S(1)} %get-tuple-element.67), channel_id=1, source_target_pairs={{0,1},{1,0},{2,3},{3,2},{4,5},{5,4},{6,7},{7,6},{8,9},{9,8},{10,11... | collective-permute-start | bytes 1572872 | tf_op jit(solution)/shard_map/ppermute | solution.py:29
  135.6 3.0 %collective-permute-start.37 = (bf16[256,2048]{1,0:T(8,128)(2,1)}, bf16[256,2048]{1,0:T(8,128)(2,1)}, u32[]{:S(2)}, u32[]{:S(2)}) collective-permute-start(bf16[256,2048]{1,0:T(8,128)(2,1)} %get-tuple-element.72), channel_id=1, source_target_pairs={{0,4},{4,0},{8,12},{12,8},{16,20},{20,16},{24,28},{28,24},{1,5},{5... | collective-permute-start | bytes 3145736 | tf_op jit(solution)/shard_map/ppermute | solution.py:29
  135.6 4.5 %collective-permute-start.39 = (bf16[256,2048]{1,0:T(8,128)(2,1)}, bf16[256,2048]{1,0:T(8,128)(2,1)}, u32[]{:S(2)}, u32[]{:S(2)}) collective-permute-start(bf16[256,2048]{1,0:T(8,128)(2,1)} %get-tuple-element.75), channel_id=1, source_target_pairs={{0,4},{4,0},{8,12},{12,8},{16,20},{20,16},{24,28},{28,24},{1,5},{5... | collective-permute-start | bytes 3145736 | tf_op jit(solution)/shard_map/ppermute | solution.py:29
  143.5 30.6 %collective-permute-start.38 = (bf16[256,2048]{1,0:T(8,128)(2,1)S(1)}, bf16[256,2048]{1,0:T(8,128)(2,1)S(1)}, u32[]{:S(2)}, u32[]{:S(2)}) collective-permute-start(bf16[256,2048]{1,0:T(8,128)(2,1)S(1)} %get-tuple-element.84), channel_id=1, source_target_pairs={{0,8},{4,12},{8,0},{12,4},{16,24},{20,28},{24,16},{28,20},{1,9},{5... | collective-permute-start | bytes 3145736 | tf_op jit(solution)/shard_map/ppermute | solution.py:29
  144.2 29.9 %collective-permute-start.40 = (bf16[256,2048]{1,0:T(8,128)(2,1)S(1)}, bf16[256,2048]{1,0:T(8,128)(2,1)S(1)}, u32[]{:S(2)}, u32[]{:S(2)}) collective-permute-start(bf16[256,2048]{1,0:T(8,128)(2,1)S(1)} %get-tuple-element.83), channel_id=1, source_target_pairs={{0,16},{4,20},{8,24},{12,28},{16,0},{20,4},{24,8},{28,12},{1,17},{... | collective-permute-start | bytes 3145736 | tf_op jit(solution)/shard_map/ppermute | solution.py:29
  144.8 29.3 %collective-permute-start.43 = (bf16[256,2048]{1,0:T(8,128)(2,1)S(1)}, bf16[256,2048]{1,0:T(8,128)(2,1)S(1)}, u32[]{:S(2)}, u32[]{:S(2)}) collective-permute-start(bf16[256,2048]{1,0:T(8,128)(2,1)S(1)} %copy-done.12), channel_id=1, source_target_pairs={{0,4},{4,0},{8,12},{12,8},{16,20},{20,16},{24,28},{28,24},{1,5},{5... | collective-permute-start | bytes 3145736 | tf_op jit(solution)/shard_map/ppermute | solution.py:29
  144.8 24.6 %collective-permute-start.41 = (bf16[512,512]{1,0:T(8,128)(2,1)S(1)}, bf16[512,512]{1,0:T(8,128)(2,1)S(1)}, u32[]{:S(2)}, u32[]{:S(2)}) collective-permute-start(bf16[512,512]{1,0:T(8,128)(2,1)S(1)} %copy-done.14), channel_id=1, source_target_pairs={{0,1},{1,0},{2,3},{3,2},{4,5},{5,4},{6,7},{7,6},{8,9},{9,8},{10,11... | collective-permute-start | bytes 1572872 | tf_op jit(solution)/shard_map/ppermute | solution.py:29
  145.9 26.2 %collective-permute-start.42 = (bf16[512,512]{1,0:T(8,128)(2,1)S(1)}, bf16[512,512]{1,0:T(8,128)(2,1)S(1)}, u32[]{:S(2)}, u32[]{:S(2)}) collective-permute-start(bf16[512,512]{1,0:T(8,128)(2,1)S(1)} %copy-done.13), channel_id=1, source_target_pairs={{0,2},{1,3},{2,0},{3,1},{4,6},{5,7},{6,4},{7,5},{8,10},{9,11},{10,... | collective-permute-start | bytes 1572872 | tf_op jit(solution)/shard_map/ppermute | solution.py:29
  148.3 25.8 %copy-start.6 = (bf16[256,2048]{1,0:T(8,128)(2,1)S(1)}, bf16[256,2048]{1,0:T(8,128)(2,1)}, u32[]{:S(2)}) copy-start(bf16[256,2048]{1,0:T(8,128)(2,1)} %copy-done.5) | copy-start | bytes 3145732
  (12 other events, 49.2 us)

commit v9 on v8

--- a/solution.py
+++ b/solution.py
@@ -43,35 +43,32 @@
     return first, second
 
 
-def gather_head(head):
-    size = lax.axis_size("sample")
+def gather(features, head):
+    samples, groups = lax.axis_size("sample"), lax.axis_size("cls")
     core = lax.axis_index("sample") % 2
-    first, second = chip_axes(size)
+    first, second = chip_axes(samples)
+    blocks = {mask: flip(features, "cls", mask) for mask in range(2, groups, 2)}
     held = {mask: flip(head, "sample", mask) for mask in first + second}
-    held[0] = head
+    blocks[1] = flip(features, "cls", 1)
     sibling = flip(head, "sample", 1)
+    for mask in range(2, groups, 2):
+        blocks[mask | 1] = flip(blocks[mask], "cls", 1)
+    ready = lax.optimization_barrier((*held.values(), *[blocks[mask] for mask in range(2, groups, 2)]))
+    held = dict(zip(held, ready))
     for a in first:
         for b in second:
-            passed = lax.optimization_barrier((jnp.where(core == 0, held[a], held[b]), sibling))[0]
+            passed = jnp.where(core == 0, held[a], held[b])
+            passed = lax.optimization_barrier((passed, sibling, blocks[1]))[0]
             held[a | b] = cross(passed, b, a)
-    return held, sibling
-
-
-def gather_features(features):
-    size = lax.axis_size("cls")
-    held = {0: features}
-    for mask in list(range(2, size, 2)) + [1]:
-        held[mask] = flip(features, "cls", mask)
-    for mask in range(2, size, 2):
-        held[mask | 1] = flip(lax.optimization_barrier((held[mask], held[1]))[0], "cls", 1)
-    return [held[mask] for mask in range(size)]
+    blocks[0], held[0] = features, head
+    return [blocks[mask] for mask in range(groups)], held, sibling
 
 
 def fast(value):
     return pltpu.with_memory_space_constraint(value, pltpu.VMEM)
 
 
-def call(kernel, outputs, operands, scratch=(), extra=(), limit=16):
+def call(kernel, outputs, operands, scratch=(), extra=(), aliases=None, limit=6):
     spec = pl.BlockSpec(memory_space=pltpu.VMEM)
     return pl.pallas_call(
         kernel,
@@ -79,6 +76,7 @@
         in_specs=[spec] * len(operands) + [pl.BlockSpec(memory_space=pl.ANY)] * len(extra),
         out_specs=(spec,) * len(outputs),
         scratch_shapes=list(scratch),
+        input_output_aliases=aliases or {},
         compiler_params=pltpu.CompilerParams(vmem_limit_bytes=limit << 20),
         cost_estimate=pl.CostEstimate(flops=1, bytes_accessed=1, transcendentals=0),
     )(*[fast(operand) for operand in operands], *extra)
@@ -125,7 +123,7 @@
 
 def partial_kernel(count, depth, paired, parts, *refs):
     feature_refs, head_refs = refs[:count], refs[count : count + len(parts)]
-    blocks_ref, turned_ref, logits_ref = refs[count + len(parts) :]
+    blocks_ref, logits_ref = refs[count + len(parts) :]
     for i, ref in enumerate(feature_refs):
         blocks_ref[i] = ref[...]
     columns = logits_ref.shape[1]
@@ -133,8 +131,11 @@
     for i in range(0, columns, tile):
         at = slice(i, i + tile)
         logits_ref[:, at] = products(at, parts, head_refs, blocks_ref, depth, paired)
-    for i, ref in enumerate(feature_refs):
-        turned_ref[i] = jnp.transpose(ref[...])
+
+
+def turn_kernel(blocks_ref, turned_ref):
+    for i in range(blocks_ref.shape[0]):
+        turned_ref[i] = jnp.transpose(blocks_ref[i])
 
 
 def student_kernel(depth, paired, parts, logits_ref, blocks_ref, *refs):
@@ -167,7 +168,8 @@
     sums_ref[1:2, :] = jnp.sum(jnp.transpose(plan_sum[...]), axis=0, keepdims=True)
 
 
-def column_kernel(student_ref, scale_ref, mass_ref, total_ref, inverse):
+def column_kernel(student_ref, scale_ref, mass_ref, *refs):
+    total_ref, inverse = refs[-2:]
     inverse[...] = as_column(1.0 / mass_ref[...])
     rows, columns = student_ref.shape
     block = 8
@@ -224,21 +226,24 @@
             share_ref[:, at] = matmul(grad_ref[...], ref[...], ((1,), (1,))).astype(bf16)
 
 
-def products_kernel(count, depth, paired, near, parts, grad_ref, turned_ref, *refs):
-    head_refs, refs = refs[: len(parts)], refs[len(parts) + count :]
-    pairs, (shares_ref,) = refs[:-1], refs[-1:]
+def near_kernel(depth, near, grad_ref, turned_ref, *refs):
     me, place = lax.axis_index("sample"), lax.axis_index("cls")
     chip, core = me // 2, me % 2
     columns = grad_ref.shape[1]
     tile = min(256, columns)
     for index, mask in enumerate(near):
-        mine_ref, theirs_ref = pairs[2 * index], pairs[2 * index + 1]
         turned = turned_ref.at[place ^ chip ^ mask]
         for i in range(0, columns, tile):
-            head_products(turned, core, depth, grad_ref, slice(i, i + tile), mine_ref, theirs_ref)
+            head_products(turned, core, depth, grad_ref, slice(i, i + tile), refs[2 * index], refs[2 * index + 1])
+
+
+def shares_kernel(depth, paired, parts, grad_ref, turned_ref, *refs):
+    head_refs, pair, shares_ref = refs[: len(parts)], refs[-3:-1], refs[-1]
+    chip, place = lax.axis_index("sample") // 2, lax.axis_index("cls")
     for (mask, side), ref in zip(parts, head_refs):
         at = pl.ds(rows_at(depth, side, paired), ref.shape[0])
         shares_ref[chip ^ mask ^ place, :, at] = matmul(grad_ref[...], ref[...], ((1,), (1,))).astype(bf16)
+    near_kernel(depth, [0], grad_ref, turned_ref, *pair)
 
 
 def per_device(features, head, class_cap):
@@ -252,8 +257,7 @@
     chip, core = me // 2, me % 2
     first, second = chip_axes(samples)
 
-    pieces, sibling = gather_head(head)
-    features_from = gather_features(features)
+    features_from, pieces, sibling = gather(features, head)
     paired = depth % LANES != 0
 
     def sides(mask, same):
@@ -264,9 +268,9 @@
         return [((mask // 2, 0), same), ((mask // 2, 1), other)]
 
     early = [part for mask in [0] + first + second for part in sides(mask, pieces[mask])]
-    blocks, turned, logits = call(
+    blocks, logits = call(
         functools.partial(partial_kernel, groups, depth, paired, [at for at, _ in early]),
-        [((groups, rows, width), bf16), ((groups, width, rows), bf16), ((rows, classes), f32)],
+        [((groups, rows, width), bf16), ((rows, classes), f32)],
         features_from + [part for _, part in early],
     )
     late = []
@@ -278,7 +282,9 @@
         [((rows, classes), f32), ((rows, classes), bf16), ((2, rows), f32)],
         [logits, blocks] + [part for _, part in late],
         [pltpu.VMEM((2, rows, tile), f32), pltpu.VMEM((rows, LANES), f32), pltpu.VMEM((rows, LANES), f32)],
-    )
+        aliases={0: 0},
+    )
+    (turned,) = call(turn_kernel, [((groups, width, rows), bf16)], [blocks])
 
     def total(value, axis, masks):
         for part in [flip(value, axis, mask) for mask in reversed(masks)]:
@@ -295,12 +301,13 @@
     sums = row_total(sums)
     students_mass, mass = sums[0:1], sums[1:2]
     scale = jnp.ones((1, classes), f32)
-    for _ in range(ITERS):
+    for iteration in range(ITERS):
         (mass,) = call(
             column_kernel,
             [((1, classes), f32)],
             [student, scale, mass],
             [pltpu.VMEM((rows, LANES), f32)],
+            [turned] if iteration == 0 else [],
         )
         scale, mass = call(
             row_kernel,
@@ -312,57 +319,59 @@
 
     head_at = [at for at, _ in early + late]
     head_list = [part for _, part in early + late]
-    near = [mask // 2 for mask in first + second] + [0]
+    near = first + second
     diagonal = [(a, b) for a in first for b in second]
     far = (diagonal[-1][0] | diagonal[-1][1]) // 2
-    near = [(a | b) // 2 for a, b in diagonal[:-1]] + near
+    near = [a | b for a, b in diagonal[:-1]] + near
     targets, grad, mine, theirs, share = call(
         functools.partial(gradient_kernel, depth, paired, far, head_at),
         [((rows, classes), bf16)] * 2 + [((depth, classes), bf16)] * 2 + [((rows, width), bf16)],
         [student, slope, scale, students_mass, mass, turned] + head_list,
         [pltpu.VMEM((rows, LANES), f32)] * 2,
     )
-    block = lax.optimization_barrier((wide(mine) + wide(flip(theirs, "sample", 1))).astype(bf16))
+    theirs = flip(theirs, "sample", 1)
+    pairs = call(
+        functools.partial(near_kernel, depth, [mask // 2 for mask in near]),
+        [((depth, classes), bf16)] * (2 * len(near)),
+        [grad, turned],
+    )
+    theirs, *pairs = lax.optimization_barrier((theirs, *pairs))
+    block = lax.optimization_barrier((wide(mine) + wide(theirs)).astype(bf16))
     passed = {diagonal[-1]: cross(block, *diagonal[-1])}
     share_from = {groups - 2: flip(share, "cls", 1)}
-
-    results = call(
-        functools.partial(products_kernel, 1, depth, paired, near, head_at),
-        [((depth, classes), bf16)] * (2 * len(near)) + [((groups, rows, width), bf16)],
+    others = {mask: flip(pairs[2 * i + 1], "sample", 1) for i, mask in enumerate(near)}
+    mine, theirs, shares = call(
+        functools.partial(shares_kernel, depth, paired, head_at),
+        [((depth, classes), bf16)] * 2 + [((groups, rows, width), bf16)],
         [grad, turned] + head_list,
         extra=[block],
     )
-    shares = results[-1]
-    arrived = list(passed.values()) + list(share_from.values())
-    theirs = lax.optimization_barrier((*results[1:-1:2], *arrived))
-    arrived = iter(theirs[len(near) :])
-    passed = {at: next(arrived) for at in passed}
-    share_from = {mask: next(arrived) for mask in share_from}
 
     onward = {1: shares[1]}
     for mask in range(2, groups, 2):
         received = share_from[mask] if mask in share_from else flip(shares[mask | 1], "cls", 1)
         onward[mask] = (wide(shares[mask]) + wide(received)).astype(bf16)
-    ready = lax.optimization_barrier((*onward.values(), *theirs[: len(near)]))
-    theirs = ready[len(onward) :]
-    returned = [flip(value, "cls", mask) for mask, value in zip(onward, ready)]
+    ready = lax.optimization_barrier((*onward.values(), *others.values(), *passed.values(), theirs))
+    onward = dict(zip(onward, ready))
+    others = dict(zip(others, ready[len(onward) :]))
+    passed = dict(zip(passed, ready[len(onward) + len(others) :]))
+    own = wide(mine) + wide(flip(ready[-1], "sample", 1))
+    returned = [flip(value, "cls", mask) for mask, value in onward.items()]
     grad_features = sum([wide(value) for value in returned], wide(shares[0])).astype(bf16)
 
-    mixed = {
-        2 * mask: wide(results[2 * i]) + wide(flip(theirs[i], "sample", 1)) for i, mask in enumerate(near)
-    }
+    mixed = {mask: wide(pairs[2 * i]) + wide(others[mask]) for i, mask in enumerate(near)}
     for a, b in diagonal[:-1]:
         passed[a, b] = cross(mixed[a | b].astype(bf16), a, b)
     received = []
     for mask in first + second:
-        block = mixed[mask]
+        total_of = mixed[mask]
         for (a, b), more in passed.items():
             if mask == (b if mask in second else a):
-                block = block + jnp.where((core == 0) == (mask in second), wide(more), 0.0)
-        received.append(flip(block.astype(bf16), "sample", mask))
+                total_of = total_of + jnp.where((core == 0) == (mask in second), wide(more), 0.0)
+        received.append(flip(total_of.astype(bf16), "sample", mask))
     received = lax.optimization_barrier((*received, grad_features))
     grad_features = received[-1]
-    grad_head = sum([wide(part) for part in received[:-1]], mixed[0]).astype(bf16)
+    grad_head = sum([wide(part) for part in received[:-1]], own).astype(bf16)
     return (targets, grad_features, grad_head)
 
 

time: 176 us -> 182 us (1.034)
  local copies, waits for them, and re-layouts: 4.83 us -> 14.3 us
  waiting for transfers between devices: 87 us -> 81.8 us
  Pallas kernels: 26.7 us -> 30.1 us
  starting transfers between devices: 47.5 us -> 45.6 us
    unnamed x33 -> x49, local copies, waits for them, and re-layouts: 3.98 us -> 14.2 us
    ppermute x42, waiting for transfers between devices: 87 us -> 81.8 us  [flip(): lax.ppermute(value, axis, [(i, i ^ mask) for i in range(lax.axis_size(axi...]
    pallas_call x10 -> x12, Pallas kernels: 26.7 us -> 30.1 us  [call(): pl.pallas_call(kernel, out_shape=tuple((pltpu.VMEM(shape, dtype) for shap...]
    ppermute x2, starting transfers between devices: 3.07 us -> 1.03 us  [cross(): lax.ppermute(value, 'sample', [(i, i ^ (odd if i % 2 else even)) for i in...]
  transfers between devices with their start and end apart: 44 -> 44, of which waited for: 29 -> 25; matrix products, arithmetic and copies ran while one was open for 3% -> 2% of each run, Pallas kernels for 9% -> 9%
where the time goes in v9:
time: 182 us
  waiting for transfers between devices  81.8 us (45%)
  starting transfers between devices  45.6 us (25%)
  Pallas kernels  30.1 us (17%)
  local copies, waits for them, and re-layouts  14.3 us (8%)
  other arithmetic  8.54 us (5%)
    ppermute x42, waiting for transfers between devices, flip(): lax.ppermute(value, axis, [(i, i ^ mask) for i in range(lax.axis_size(axi...  81.8 us
    ppermute x42, starting transfers between devices, flip(): lax.ppermute(value, axis, [(i, i ^ mask) for i in range(lax.axis_size(axi...  44.6 us
    pallas_call x12, Pallas kernels, call(): pl.pallas_call(kernel, out_shape=tuple((pltpu.VMEM(shape, dtype) for shap...  30.1 us
    unnamed x49, local copies, waits for them, and re-layouts  14.2 us
  transfers between devices with their start and end apart: 44, of which 25 were waited for; matrix products, arithmetic and copies ran while one was open for 2% of the time, Pallas kernels for 9%

profile of v9, /device:TPU:0, one launch (start us, length us, event | category | flops | bytes accessed | tf_op | source)
XLA Modules:
  0.0 181.5 jit_solution(12902709090795517743)
XLA Ops:
  0.6 3.0 %collective-permute-start.4 = (bf16[256,2048]{1,0:T(8,128)(2,1)}, bf16[256,2048]{1,0:T(8,128)(2,1)S(1)}, u32[]{:S(2)}, u32[]{:S(2)}) collective-permute-start(bf16[256,2048]{1,0:T(8,128)(2,1)} %refs_0_.5), channel_id=1, source_target_pairs={{0,8},{4,12},{8,0},{12,4},{16,24},{20,28},{24,16},{28,20},{1,9},{5... | collective-permute-start | bytes 3145736 | tf_op jit(solution)/shard_map/ppermute | solution.py:29
  3.6 1.5 collective-permute-start.5
  5.2 2.6 %collective-permute-start.1 = (bf16[512,512]{1,0:T(8,128)(2,1)}, bf16[512,512]{1,0:T(8,128)(2,1)}, u32[]{:S(2)}, u32[]{:S(2)}) collective-permute-start(bf16[512,512]{1,0:T(8,128)(2,1)} %refs_0_.3), channel_id=1, source_target_pairs={{0,2},{1,3},{2,0},{3,1},{4,6},{5,7},{6,4},{7,5},{8,10},{9,11},{10,... | collective-permute-start | bytes 1572872 | tf_op jit(solution)/shard_map/ppermute | solution.py:29
  7.8 1.6 collective-permute-start
  9.3 21.5 %collective-permute-done.1.refs_2_ = bf16[512,512]{1,0:T(8,128)(2,1)} collective-permute-done((bf16[512,512]{1,0:T(8,128)(2,1)}, bf16[512,512]{1,0:T(8,128)(2,1)}, u32[]{:S(2)}, u32[]{:S(2)}) %collective-permute-start.1) | collective-permute-done | bytes 524320 | tf_op jit(solution)/shard_map/ppermute | solution.py:29
  33.0 13.5 %collective-permute-done.2.refs_3_ = bf16[512,512]{1,0:T(8,128)(2,1)S(1)} collective-permute-done((bf16[512,512]{1,0:T(8,128)(2,1)}, bf16[512,512]{1,0:T(8,128)(2,1)S(1)}, u32[]{:S(2)}, u32[]{:S(2)}) %collective-permute-start.2) | collective-permute-done | bytes 524320 | tf_op jit(solution)/shard_map/ppermute | solution.py:29
  46.6 5.8 %shard_map.58 = (bf16[4,512,512]{2,1,0:T(8,128)(2,1)S(1)}, f32[512,2048]{1,0:T(8,128)S(1)}) custom-call(bf16[512,512]{1,0:T(8,128)(2,1)S(1)} %copy-done.22, bf16[512,512]{1,0:T(8,128)(2,1)} %collective-permute-done.refs_1_, bf16[512,512]{1,0:T(8,128)(2,1)} %collective-permute-done.1.refs_2_, bf16[512,512]{1,0:T(8,128)(2,1)S(1)} %collective-permute-done.2.refs_3_, ...), custom_call_target="tpu_custom_call" | custom-call | flops 1 | bytes 1 | tf_op jit(solution)/shard_map/pallas_call | solution.py:73
  52.6 2.6 %collective-permute-done.9.refs_1_.refs_7_ = bf16[256,2048]{1,0:T(8,128)(2,1)S(1)} collective-permute-done((bf16[256,2048]{1,0:T(8,128)(2,1)S(1)}, bf16[256,2048]{1,0:T(8,128)(2,1)S(1)}, u32[]{:S(2)}, u32[]{:S(2)}) %collective-permute-start.9) | collective-permute-done | bytes 1048608 | tf_op jit(solution)/shard_map/ppermute | solution.py:29
  55.2 3.5 %shard_map.59 = (f32[512,2048]{1,0:T(8,128)S(1)}, bf16[512,2048]{1,0:T(8,128)(2,1)S(1)}, f32[2,512]{1,0:T(2,128)S(1)}) custom-call(f32[512,2048]{1,0:T(8,128)S(1)} %get-tuple-element.46.logits_ref, bf16[4,512,512]{2,1,0:T(8,128)(2,1)S(1)} %get-tuple-element.47.blocks_ref, ...), custom_call_target="tpu_custom_call", output_to_operand_aliasing={{0}: (0, {})} | custom-call | flops 1 | bytes 1 | tf_op jit(solution)/shard_map/pallas_call | solution.py:73
  58.7 3.0 %collective-permute-start.10 = (f32[2,512]{1,0:T(2,128)S(1)}, f32[2,512]{1,0:T(2,128)S(1)}, u32[]{:S(2)}, u32[]{:S(2)}) collective-permute-start(f32[2,512]{1,0:T(2,128)S(1)} %get-tuple-element.52), channel_id=1, source_target_pairs={{0,3},{1,2},{2,1},{3,0},{4,7},{5,6},{6,5},{7,4},{8,11},{9,10},{10,... | collective-permute-start | bytes 12296 | tf_op jit(solution)/shard_map/ppermute | solution.py:29
  61.7 1.5 collective-permute-start.12
  64.2 2.0 %collective-permute-done.11 = f32[2,512]{1,0:T(2,128)S(1)} collective-permute-done((f32[2,512]{1,0:T(2,128)S(1)}, f32[2,512]{1,0:T(2,128)S(1)}, u32[]{:S(2)}, u32[]{:S(2)}) %collective-permute-start.11) | collective-permute-done | bytes 4128 | tf_op jit(solution)/shard_map/ppermute | solution.py:29
  68.1 1.5 collective-permute-start.14
  69.6 1.5 collective-permute-start.15
  73.3 1.5 collective-permute-done.16
  75.5 1.5 collective-permute-start.17
  77.6 2.3 %collective-permute-start.19 = (f32[1,512]{1,0:T(1,128)S(1)}, f32[1,512]{1,0:T(1,128)S(1)}, u32[]{:S(2)}, u32[]{:S(2)}) collective-permute-start(f32[1,512]{1,0:T(1,128)S(1)} %get-tuple-element.54), channel_id=1, source_target_pairs={{0,1},{1,0},{2,3},{3,2},{4,5},{5,4},{6,7},{7,6},{8,9},{9,8},{10,11... | collective-permute-start | bytes 6152 | tf_op jit(solution)/shard_map/ppermute | solution.py:29
  82.3 1.2 collective-permute-done.20
  84.0 1.5 collective-permute-start.22
  85.5 1.5 collective-permute-start.23
  89.8 2.6 %collective-permute-start.24 = (f32[1,512]{1,0:T(1,128)S(1)}, f32[1,512]{1,0:T(1,128)S(1)}, u32[]{:S(2)}, u32[]{:S(2)}) collective-permute-start(f32[1,512]{1,0:T(1,128)S(1)} %get-tuple-element.56), channel_id=1, source_target_pairs={{0,3},{1,2},{2,1},{3,0},{4,7},{5,6},{6,5},{7,4},{8,11},{9,10},{10,... | collective-permute-start | bytes 6152 | tf_op jit(solution)/shard_map/ppermute | solution.py:29
  95.3 1.7 collective-permute-done.25
  98.9 1.5 collective-permute-start.28
  100.4 1.5 collective-permute-start.29
  104.0 1.5 collective-permute-done.30
  106.2 1.5 collective-permute-start.31
  108.7 2.0 %collective-permute-start.33 = (f32[1,512]{1,0:T(1,128)S(1)}, f32[1,512]{1,0:T(1,128)S(1)}, u32[]{:S(2)}, u32[]{:S(2)}) collective-permute-start(f32[1,512]{1,0:T(1,128)S(1)} %get-tuple-element.58), channel_id=1, source_target_pairs={{0,1},{1,0},{2,3},{3,2},{4,5},{5,4},{6,7},{7,6},{8,9},{9,8},{10,11... | collective-permute-start | bytes 6152 | tf_op jit(solution)/shard_map/ppermute | solution.py:29
  112.3 6.0 %shard_map.67 = (bf16[512,2048]{1,0:T(8,128)(2,1)S(1)}, bf16[512,2048]{1,0:T(8,128)(2,1)S(1)}, bf16[256,2048]{1,0:T(8,128)(2,1)S(1)}, bf16[256,2048]{1,0:T(8,128)(2,1)S(1)}, bf16[512,512]{1,0:T(8,128)(2,1)}) custom-call(f32[512,2048]{1,0:T(8,128)S(1)} %get-tuple-element.50.student_ref, bf16[512,2048]{1,0:T(8,128)(2,1)S(1)} %get-tuple-element.51.slope_ref, ...), custom_call_target="tpu_custom_call" | custom-call | flops 1 | bytes 1 | tf_op jit(solution)/shard_map/pallas_call | solution.py:73
  118.4 3.4 %shard_map.68 = (bf16[256,2048]{1,0:T(8,128)(2,1)S(1)}, bf16[256,2048]{1,0:T(8,128)(2,1)}, bf16[256,2048]{1,0:T(8,128)(2,1)S(1)}, bf16[256,2048]{1,0:T(8,128)(2,1)}) custom-call(bf16[512,2048]{1,0:T(8,128)(2,1)S(1)} %get-tuple-element.61.grad_ref, bf16[4,512,512]{2,1,0:T(8,128)(2,1)S(1)} %shard_map.60.refs_0_.turned_ref), custom_call_target="tpu_custom_call" | custom-call | flops 1 | bytes 1 | tf_op jit(solution)/shard_map/pallas_call | solution.py:73
  123.7 1.4 add_convert_fusion.1.refs_8_
  126.1 2.0 %collective-permute-start.35 = (bf16[512,512]{1,0:T(8,128)(2,1)}, bf16[512,512]{1,0:T(8,128)(2,1)}, u32[]{:S(2)}, u32[]{:S(2)}) collective-permute-start(bf16[512,512]{1,0:T(8,128)(2,1)} %get-tuple-element.70), channel_id=1, source_target_pairs={{0,1},{1,0},{2,3},{3,2},{4,5},{5,4},{6,7},{7,6},{8,9},{9,8},{10,11... | collective-permute-start | bytes 1572872 | tf_op jit(solution)/shard_map/ppermute | solution.py:29
  128.2 1.6 copy-done.1
  129.8 1.2 copy-done.4
  131.0 1.2 copy-done.7
  132.2 1.2 copy-done.9
  133.4 1.2 copy-done.11
  134.7 1.2 copy-done.13
  135.9 1.2 copy-done.15
  137.1 1.6 copy-done.17
  138.7 6.9 %shard_map.69 = (bf16[256,2048]{1,0:T(8,128)(2,1)S(1)}, bf16[256,2048]{1,0:T(8,128)(2,1)S(1)}, bf16[4,512,512]{2,1,0:T(8,128)(2,1)S(1)}) custom-call(bf16[512,2048]{1,0:T(8,128)(2,1)S(1)} %copy-done.17, bf16[4,512,512]{2,1,0:T(8,128)(2,1)S(1)} %copy-done.1, bf16[256,2048]{1,0:T(8,128)(2,1)S(1)} %copy-done.7, ...), custom_call_target="tpu_custom_call" | custom-call | flops 1 | bytes 1 | tf_op jit(solution)/shard_map/pallas_call | solution.py:73
  145.7 1.3 fusion.6
  147.4 2.9 %fusion.3 = (bf16[256,2048]{1,0:T(8,128)(2,1)S(1)}, bf16[256,2048]{1,0:T(8,128)(2,1)S(1)}) fusion(bf16[256,2048]{1,0:T(8,128)(2,1)} %collective-permute-done.38, bf16[256,2048]{1,0:T(8,128)(2,1)} %collective-permute-done.37, bf16[256,2048]{1,0:T(8,128)(2,1)S(1)} %copy-done.21, pred[]{:T(512)S(6)} %eq.11, pred[]{:T(512)S(6)} %eq.12, ...), kind=kLoop, calls=%fused_computation.5 | loop fusion | flops 6815744 | bytes 7340034 | tf_op jit(solution)/shard_map/convert_element_type | solution.py:371
  150.3 1.6 collective-permute-start.39
  152.4 2.0 %collective-permute-start.42 = (bf16[512,512]{1,0:T(8,128)(2,1)S(1)}, bf16[512,512]{1,0:T(8,128)(2,1)S(1)}, u32[]{:S(2)}, u32[]{:S(2)}) collective-permute-start(bf16[512,512]{1,0:T(8,128)(2,1)S(1)} %fusion.6), channel_id=1, source_target_pairs={{0,2},{1,3},{2,0},{3,1},{4,6},{5,7},{6,4},{7,5},{8,10},{9,11},{10,... | collective-permute-start | bytes 1572872 | tf_op jit(solution)/shard_map/ppermute | solution.py:29
  154.4 1.3 copy.8
  155.7 21.9 %collective-permute-done.41 = bf16[512,512]{1,0:T(8,128)(2,1)S(1)} collective-permute-done((bf16[512,512]{1,0:T(8,128)(2,1)S(1)}, bf16[512,512]{1,0:T(8,128)(2,1)S(1)}, u32[]{:S(2)}, u32[]{:S(2)}) %collective-permute-start.41) | collective-permute-done | bytes 524320 | tf_op jit(solution)/shard_map/ppermute | solution.py:29
  177.6 1.3 collective-permute-done.42
  179.9 1.7 add_convert_fusion
  (135 shorter events, 29.3 us)
Async XLA Ops:
  0.6 30.2 %collective-permute-start.4 = (bf16[256,2048]{1,0:T(8,128)(2,1)}, bf16[256,2048]{1,0:T(8,128)(2,1)S(1)}, u32[]{:S(2)}, u32[]{:S(2)}) collective-permute-start(bf16[256,2048]{1,0:T(8,128)(2,1)} %refs_0_.5), channel_id=1, source_target_pairs={{0,8},{4,12},{8,0},{12,4},{16,24},{20,28},{24,16},{28,20},{1,9},{5... | collective-permute-start | bytes 3145736 | tf_op jit(solution)/shard_map/ppermute | solution.py:29
  3.6 27.2 %collective-permute-start.5 = (bf16[256,2048]{1,0:T(8,128)(2,1)}, bf16[256,2048]{1,0:T(8,128)(2,1)S(1)}, u32[]{:S(2)}, u32[]{:S(2)}) collective-permute-start(bf16[256,2048]{1,0:T(8,128)(2,1)} %refs_0_.5), channel_id=1, source_target_pairs={{0,16},{4,20},{8,24},{12,28},{16,0},{20,4},{24,8},{28,12},{1,17},{... | collective-permute-start | bytes 3145736 | tf_op jit(solution)/shard_map/ppermute | solution.py:29
  5.2 25.7 %collective-permute-start.1 = (bf16[512,512]{1,0:T(8,128)(2,1)}, bf16[512,512]{1,0:T(8,128)(2,1)}, u32[]{:S(2)}, u32[]{:S(2)}) collective-permute-start(bf16[512,512]{1,0:T(8,128)(2,1)} %refs_0_.3), channel_id=1, source_target_pairs={{0,2},{1,3},{2,0},{3,1},{4,6},{5,7},{6,4},{7,5},{8,10},{9,11},{10,... | collective-permute-start | bytes 1572872 | tf_op jit(solution)/shard_map/ppermute | solution.py:29
  7.8 24.8 %collective-permute-start.3 = (bf16[256,2048]{1,0:T(8,128)(2,1)}, bf16[256,2048]{1,0:T(8,128)(2,1)}, u32[]{:S(2)}, u32[]{:S(2)}) collective-permute-start(bf16[256,2048]{1,0:T(8,128)(2,1)} %refs_0_.5), channel_id=1, source_target_pairs={{0,4},{4,0},{8,12},{12,8},{16,20},{20,16},{24,28},{28,24},{1,5},{5... | collective-permute-start | bytes 3145736 | tf_op jit(solution)/shard_map/ppermute | solution.py:29
  7.8 24.8 %collective-permute-start = (bf16[512,512]{1,0:T(8,128)(2,1)}, bf16[512,512]{1,0:T(8,128)(2,1)}, u32[]{:S(2)}, u32[]{:S(2)}) collective-permute-start(bf16[512,512]{1,0:T(8,128)(2,1)} %refs_0_.3), channel_id=1, source_target_pairs={{0,1},{1,0},{2,3},{3,2},{4,5},{5,4},{6,7},{7,6},{8,9},{9,8},{10,11... | collective-permute-start | bytes 1572872 | tf_op jit(solution)/shard_map/ppermute | solution.py:29
  30.8 15.7 %collective-permute-start.6 = (bf16[256,2048]{1,0:T(8,128)(2,1)S(1)}, bf16[256,2048]{1,0:T(8,128)(2,1)S(1)}, u32[]{:S(2)}, u32[]{:S(2)}) collective-permute-start(bf16[256,2048]{1,0:T(8,128)(2,1)S(1)} %collective-permute-done.4.refs_6_.refs_2_), channel_id=1, source_target_pairs={{0,4},{4,0},{8,12},{12,8},{16,20},{20,16},{24,28},{28,24},{1,5},{5... | collective-permute-start | bytes 3145736 | tf_op jit(solution)/shard_map/ppermute | solution.py:29
  30.9 15.6 %collective-permute-start.7 = (bf16[256,2048]{1,0:T(8,128)(2,1)S(1)}, bf16[256,2048]{1,0:T(8,128)(2,1)S(1)}, u32[]{:S(2)}, u32[]{:S(2)}) collective-permute-start(bf16[256,2048]{1,0:T(8,128)(2,1)S(1)} %collective-permute-done.5.refs_8_.refs_4_), channel_id=1, source_target_pairs={{0,4},{4,0},{8,12},{12,8},{16,20},{20,16},{24,28},{28,24},{1,5},{5... | collective-permute-start | bytes 3145736 | tf_op jit(solution)/shard_map/ppermute | solution.py:29
  32.5 19.9 %collective-permute-start.8 = (bf16[256,2048]{1,0:T(8,128)(2,1)S(1)}, bf16[256,2048]{1,0:T(8,128)(2,1)S(1)}, u32[]{:S(2)}, u32[]{:S(2)}) collective-permute-start(bf16[256,2048]{1,0:T(8,128)(2,1)S(1)} %broadcast_select_fusion), channel_id=1, source_target_pairs={{0,16},{4,12},{8,24},{12,4},{16,0},{20,28},{24,8},{28,20},{1,17},{... | collective-permute-start | bytes 3145736 | tf_op jit(solution)/shard_map/ppermute | solution.py:34
  33.0 13.5 %collective-permute-start.2 = (bf16[512,512]{1,0:T(8,128)(2,1)}, bf16[512,512]{1,0:T(8,128)(2,1)S(1)}, u32[]{:S(2)}, u32[]{:S(2)}) collective-permute-start(bf16[512,512]{1,0:T(8,128)(2,1)} %collective-permute-done.1.refs_2_), channel_id=1, source_target_pairs={{0,1},{1,0},{2,3},{3,2},{4,5},{5,4},{6,7},{7,6},{8,9},{9,8},{10,11... | collective-permute-start | bytes 1572872 | tf_op jit(solution)/shard_map/ppermute | solution.py:29
  46.6 65.7 %copy-start.8 = (bf16[256,2048]{1,0:T(8,128)(2,1)}, bf16[256,2048]{1,0:T(8,128)(2,1)S(1)}, u32[]{:S(2)}) copy-start(bf16[256,2048]{1,0:T(8,128)(2,1)S(1)} %collective-permute-done.6.refs_7_.refs_3_) | copy-start | bytes 3145732
  46.6 65.7 %copy-start.10 = (bf16[256,2048]{1,0:T(8,128)(2,1)}, bf16[256,2048]{1,0:T(8,128)(2,1)S(1)}, u32[]{:S(2)}) copy-start(bf16[256,2048]{1,0:T(8,128)(2,1)S(1)} %collective-permute-done.7.refs_9_.refs_5_) | copy-start | bytes 3145732
  52.5 59.8 %copy-start.12 = (bf16[256,2048]{1,0:T(8,128)(2,1)}, bf16[256,2048]{1,0:T(8,128)(2,1)S(1)}, u32[]{:S(2)}) copy-start(bf16[256,2048]{1,0:T(8,128)(2,1)S(1)} %collective-permute-done.8.refs_0_.refs_6_) | copy-start | bytes 3145732
  52.5 2.7 %collective-permute-start.9 = (bf16[256,2048]{1,0:T(8,128)(2,1)S(1)}, bf16[256,2048]{1,0:T(8,128)(2,1)S(1)}, u32[]{:S(2)}, u32[]{:S(2)}) collective-permute-start(bf16[256,2048]{1,0:T(8,128)(2,1)S(1)} %collective-permute-done.8.refs_0_.refs_6_), channel_id=1, source_target_pairs={{0,4},{4,0},{8,12},{12,8},{16,20},{20,16},{24,28},{28,24},{1,5},{5... | collective-permute-start | bytes 3145736 | tf_op jit(solution)/shard_map/ppermute | solution.py:29
  55.2 57.1 %copy-start.14 = (bf16[256,2048]{1,0:T(8,128)(2,1)}, bf16[256,2048]{1,0:T(8,128)(2,1)S(1)}, u32[]{:S(2)}) copy-start(bf16[256,2048]{1,0:T(8,128)(2,1)S(1)} %collective-permute-done.9.refs_1_.refs_7_) | copy-start | bytes 3145732
  58.7 5.5 %collective-permute-start.10 = (f32[2,512]{1,0:T(2,128)S(1)}, f32[2,512]{1,0:T(2,128)S(1)}, u32[]{:S(2)}, u32[]{:S(2)}) collective-permute-start(f32[2,512]{1,0:T(2,128)S(1)} %get-tuple-element.52), channel_id=1, source_target_pairs={{0,3},{1,2},{2,1},{3,0},{4,7},{5,6},{6,5},{7,4},{8,11},{9,10},{10,... | collective-permute-start | bytes 12296 | tf_op jit(solution)/shard_map/ppermute | solution.py:29
  61.6 4.5 %collective-permute-start.11 = (f32[2,512]{1,0:T(2,128)S(1)}, f32[2,512]{1,0:T(2,128)S(1)}, u32[]{:S(2)}, u32[]{:S(2)}) collective-permute-start(f32[2,512]{1,0:T(2,128)S(1)} %get-tuple-element.52), channel_id=1, source_target_pairs={{0,2},{1,3},{2,0},{3,1},{4,6},{5,7},{6,4},{7,5},{8,10},{9,11},{10,... | collective-permute-start | bytes 12296 | tf_op jit(solution)/shard_map/ppermute | solution.py:29
  61.7 4.5 %collective-permute-start.12 = (f32[2,512]{1,0:T(2,128)S(1)}, f32[2,512]{1,0:T(2,128)S(1)}, u32[]{:S(2)}, u32[]{:S(2)}) collective-permute-start(f32[2,512]{1,0:T(2,128)S(1)} %get-tuple-element.52), channel_id=1, source_target_pairs={{0,1},{1,0},{2,3},{3,2},{4,5},{5,4},{6,7},{7,6},{8,9},{9,8},{10,11... | collective-permute-start | bytes 12296 | tf_op jit(solution)/shard_map/ppermute | solution.py:29
  66.9 1.2 collective-permute-start.13
  68.1 4.6 %collective-permute-start.14 = (f32[1,2048]{1,0:T(1,128)S(1)}, f32[1,2048]{1,0:T(1,128)S(1)}, u32[]{:S(2)}, u32[]{:S(2)}) collective-permute-start(f32[1,2048]{1,0:T(1,128)S(1)} %add.114), channel_id=1, source_target_pairs={{0,24},{4,28},{8,16},{12,20},{16,8},{20,12},{24,0},{28,4},{1,25},{... | collective-permute-start | bytes 24584 | tf_op jit(solution)/shard_map/ppermute | solution.py:29
  69.6 3.7 %collective-permute-start.15 = (f32[1,2048]{1,0:T(1,128)S(1)}, f32[1,2048]{1,0:T(1,128)S(1)}, u32[]{:S(2)}, u32[]{:S(2)}) collective-permute-start(f32[1,2048]{1,0:T(1,128)S(1)} %add.114), channel_id=1, source_target_pairs={{0,16},{4,20},{8,24},{12,28},{16,0},{20,4},{24,8},{28,12},{1,17},{... | collective-permute-start | bytes 24584 | tf_op jit(solution)/shard_map/ppermute | solution.py:29
  71.2 3.7 %collective-permute-start.16 = (f32[1,2048]{1,0:T(1,128)S(1)}, f32[1,2048]{1,0:T(1,128)S(1)}, u32[]{:S(2)}, u32[]{:S(2)}) collective-permute-start(f32[1,2048]{1,0:T(1,128)S(1)} %add.114), channel_id=1, source_target_pairs={{0,8},{4,12},{8,0},{12,4},{16,24},{20,28},{24,16},{28,20},{1,9},{5... | collective-permute-start | bytes 24584 | tf_op jit(solution)/shard_map/ppermute | solution.py:29
  75.5 5.4 %collective-permute-start.17 = (f32[1,512]{1,0:T(1,128)S(1)}, f32[1,512]{1,0:T(1,128)S(1)}, u32[]{:S(2)}, u32[]{:S(2)}) collective-permute-start(f32[1,512]{1,0:T(1,128)S(1)} %get-tuple-element.54), channel_id=1, source_target_pairs={{0,3},{1,2},{2,1},{3,0},{4,7},{5,6},{6,5},{7,4},{8,11},{9,10},{10,... | collective-permute-start | bytes 6152 | tf_op jit(solution)/shard_map/ppermute | solution.py:29
  77.0 4.5 %collective-permute-start.18 = (f32[1,512]{1,0:T(1,128)S(1)}, f32[1,512]{1,0:T(1,128)S(1)}, u32[]{:S(2)}, u32[]{:S(2)}) collective-permute-start(f32[1,512]{1,0:T(1,128)S(1)} %get-tuple-element.54), channel_id=1, source_target_pairs={{0,2},{1,3},{2,0},{3,1},{4,6},{5,7},{6,4},{7,5},{8,10},{9,11},{10,... | collective-permute-start | bytes 6152 | tf_op jit(solution)/shard_map/ppermute | solution.py:29
  77.6 3.9 %collective-permute-start.19 = (f32[1,512]{1,0:T(1,128)S(1)}, f32[1,512]{1,0:T(1,128)S(1)}, u32[]{:S(2)}, u32[]{:S(2)}) collective-permute-start(f32[1,512]{1,0:T(1,128)S(1)} %get-tuple-element.54), channel_id=1, source_target_pairs={{0,1},{1,0},{2,3},{3,2},{4,5},{5,4},{6,7},{7,6},{8,9},{9,8},{10,11... | collective-permute-start | bytes 6152 | tf_op jit(solution)/shard_map/ppermute | solution.py:29
  82.2 1.2 collective-permute-start.20
  83.4 4.6 %collective-permute-start.21 = (f32[1,2048]{1,0:T(1,128)S(1)}, f32[1,2048]{1,0:T(1,128)S(1)}, u32[]{:S(2)}, u32[]{:S(2)}) collective-permute-start(f32[1,2048]{1,0:T(1,128)S(1)} %add.121), channel_id=1, source_target_pairs={{0,24},{4,28},{8,16},{12,20},{16,8},{20,12},{24,0},{28,4},{1,25},{... | collective-permute-start | bytes 24584 | tf_op jit(solution)/shard_map/ppermute | solution.py:29
  84.0 4.1 %collective-permute-start.22 = (f32[1,2048]{1,0:T(1,128)S(1)}, f32[1,2048]{1,0:T(1,128)S(1)}, u32[]{:S(2)}, u32[]{:S(2)}) collective-permute-start(f32[1,2048]{1,0:T(1,128)S(1)} %add.121), channel_id=1, source_target_pairs={{0,16},{4,20},{8,24},{12,28},{16,0},{20,4},{24,8},{28,12},{1,17},{... | collective-permute-start | bytes 24584 | tf_op jit(solution)/shard_map/ppermute | solution.py:29
  85.5 3.7 %collective-permute-start.23 = (f32[1,2048]{1,0:T(1,128)S(1)}, f32[1,2048]{1,0:T(1,128)S(1)}, u32[]{:S(2)}, u32[]{:S(2)}) collective-permute-start(f32[1,2048]{1,0:T(1,128)S(1)} %add.121), channel_id=1, source_target_pairs={{0,8},{4,12},{8,0},{12,4},{16,24},{20,28},{24,16},{28,20},{1,9},{5... | collective-permute-start | bytes 24584 | tf_op jit(solution)/shard_map/ppermute | solution.py:29
  89.8 5.4 %collective-permute-start.24 = (f32[1,512]{1,0:T(1,128)S(1)}, f32[1,512]{1,0:T(1,128)S(1)}, u32[]{:S(2)}, u32[]{:S(2)}) collective-permute-start(f32[1,512]{1,0:T(1,128)S(1)} %get-tuple-element.56), channel_id=1, source_target_pairs={{0,3},{1,2},{2,1},{3,0},{4,7},{5,6},{6,5},{7,4},{8,11},{9,10},{10,... | collective-permute-start | bytes 6152 | tf_op jit(solution)/shard_map/ppermute | solution.py:29
  92.4 4.5 %collective-permute-start.25 = (f32[1,512]{1,0:T(1,128)S(1)}, f32[1,512]{1,0:T(1,128)S(1)}, u32[]{:S(2)}, u32[]{:S(2)}) collective-permute-start(f32[1,512]{1,0:T(1,128)S(1)} %get-tuple-element.56), channel_id=1, source_target_pairs={{0,2},{1,3},{2,0},{3,1},{4,6},{5,7},{6,4},{7,5},{8,10},{9,11},{10,... | collective-permute-start | bytes 6152 | tf_op jit(solution)/shard_map/ppermute | solution.py:29
  93.3 3.6 %collective-permute-start.26 = (f32[1,512]{1,0:T(1,128)S(1)}, f32[1,512]{1,0:T(1,128)S(1)}, u32[]{:S(2)}, u32[]{:S(2)}) collective-permute-start(f32[1,512]{1,0:T(1,128)S(1)} %get-tuple-element.56), channel_id=1, source_target_pairs={{0,1},{1,0},{2,3},{3,2},{4,5},{5,4},{6,7},{7,6},{8,9},{9,8},{10,11... | collective-permute-start | bytes 6152 | tf_op jit(solution)/shard_map/ppermute | solution.py:29
  97.6 1.2 collective-permute-start.27
  98.9 4.6 %collective-permute-start.28 = (f32[1,2048]{1,0:T(1,128)S(1)}, f32[1,2048]{1,0:T(1,128)S(1)}, u32[]{:S(2)}, u32[]{:S(2)}) collective-permute-start(f32[1,2048]{1,0:T(1,128)S(1)} %add.128), channel_id=1, source_target_pairs={{0,24},{4,28},{8,16},{12,20},{16,8},{20,12},{24,0},{28,4},{1,25},{... | collective-permute-start | bytes 24584 | tf_op jit(solution)/shard_map/ppermute | solution.py:29
  100.4 3.7 %collective-permute-start.29 = (f32[1,2048]{1,0:T(1,128)S(1)}, f32[1,2048]{1,0:T(1,128)S(1)}, u32[]{:S(2)}, u32[]{:S(2)}) collective-permute-start(f32[1,2048]{1,0:T(1,128)S(1)} %add.128), channel_id=1, source_target_pairs={{0,16},{4,20},{8,24},{12,28},{16,0},{20,4},{24,8},{28,12},{1,17},{... | collective-permute-start | bytes 24584 | tf_op jit(solution)/shard_map/ppermute | solution.py:29
  101.9 3.7 %collective-permute-start.30 = (f32[1,2048]{1,0:T(1,128)S(1)}, f32[1,2048]{1,0:T(1,128)S(1)}, u32[]{:S(2)}, u32[]{:S(2)}) collective-permute-start(f32[1,2048]{1,0:T(1,128)S(1)} %add.128), channel_id=1, source_target_pairs={{0,8},{4,12},{8,0},{12,4},{16,24},{20,28},{24,16},{28,20},{1,9},{5... | collective-permute-start | bytes 24584 | tf_op jit(solution)/shard_map/ppermute | solution.py:29
  106.2 5.4 %collective-permute-start.31 = (f32[1,512]{1,0:T(1,128)S(1)}, f32[1,512]{1,0:T(1,128)S(1)}, u32[]{:S(2)}, u32[]{:S(2)}) collective-permute-start(f32[1,512]{1,0:T(1,128)S(1)} %get-tuple-element.58), channel_id=1, source_target_pairs={{0,3},{1,2},{2,1},{3,0},{4,7},{5,6},{6,5},{7,4},{8,11},{9,10},{10,... | collective-permute-start | bytes 6152 | tf_op jit(solution)/shard_map/ppermute | solution.py:29
  107.7 4.5 %collective-permute-start.32 = (f32[1,512]{1,0:T(1,128)S(1)}, f32[1,512]{1,0:T(1,128)S(1)}, u32[]{:S(2)}, u32[]{:S(2)}) collective-permute-start(f32[1,512]{1,0:T(1,128)S(1)} %get-tuple-element.58), channel_id=1, source_target_pairs={{0,2},{1,3},{2,0},{3,1},{4,6},{5,7},{6,4},{7,5},{8,10},{9,11},{10,... | collective-permute-start | bytes 6152 | tf_op jit(solution)/shard_map/ppermute | solution.py:29
  108.7 3.6 %collective-permute-start.33 = (f32[1,512]{1,0:T(1,128)S(1)}, f32[1,512]{1,0:T(1,128)S(1)}, u32[]{:S(2)}, u32[]{:S(2)}) collective-permute-start(f32[1,512]{1,0:T(1,128)S(1)} %get-tuple-element.58), channel_id=1, source_target_pairs={{0,1},{1,0},{2,3},{3,2},{4,5},{5,4},{6,7},{7,6},{8,9},{9,8},{10,11... | collective-permute-start | bytes 6152 | tf_op jit(solution)/shard_map/ppermute | solution.py:29
  118.3 5.4 %collective-permute-start.34 = (bf16[256,2048]{1,0:T(8,128)(2,1)S(1)}, bf16[256,2048]{1,0:T(8,128)(2,1)S(1)}, u32[]{:S(2)}, u32[]{:S(2)}) collective-permute-start(bf16[256,2048]{1,0:T(8,128)(2,1)S(1)} %get-tuple-element.60), channel_id=1, source_target_pairs={{0,4},{4,0},{8,12},{12,8},{16,20},{20,16},{24,28},{28,24},{1,5},{5... | collective-permute-start | bytes 3145736 | tf_op jit(solution)/shard_map/ppermute | solution.py:29
  125.1 21.9 %collective-permute-start.38 = (bf16[256,2048]{1,0:T(8,128)(2,1)}, bf16[256,2048]{1,0:T(8,128)(2,1)}, u32[]{:S(2)}, u32[]{:S(2)}) collective-permute-start(bf16[256,2048]{1,0:T(8,128)(2,1)} %add_convert_fusion.1.refs_8_), channel_id=1, source_target_pairs={{0,8},{4,20},{8,0},{12,28},{16,24},{20,4},{24,16},{28,12},{1,9},{5... | collective-permute-start | bytes 3145736 | tf_op jit(solution)/shard_map/ppermute | solution.py:34
  125.6 21.4 %collective-permute-start.36 = (bf16[256,2048]{1,0:T(8,128)(2,1)}, bf16[256,2048]{1,0:T(8,128)(2,1)}, u32[]{:S(2)}, u32[]{:S(2)}) collective-permute-start(bf16[256,2048]{1,0:T(8,128)(2,1)} %get-tuple-element.71), channel_id=1, source_target_pairs={{0,4},{4,0},{8,12},{12,8},{16,20},{20,16},{24,28},{28,24},{1,5},{5... | collective-permute-start | bytes 3145736 | tf_op jit(solution)/shard_map/ppermute | solution.py:29
  125.8 21.2 %collective-permute-start.37 = (bf16[256,2048]{1,0:T(8,128)(2,1)}, bf16[256,2048]{1,0:T(8,128)(2,1)}, u32[]{:S(2)}, u32[]{:S(2)}) collective-permute-start(bf16[256,2048]{1,0:T(8,128)(2,1)} %get-tuple-element.72), channel_id=1, source_target_pairs={{0,4},{4,0},{8,12},{12,8},{16,20},{20,16},{24,28},{28,24},{1,5},{5... | collective-permute-start | bytes 3145736 | tf_op jit(solution)/shard_map/ppermute | solution.py:29
  126.1 19.6 %collective-permute-start.35 = (bf16[512,512]{1,0:T(8,128)(2,1)}, bf16[512,512]{1,0:T(8,128)(2,1)}, u32[]{:S(2)}, u32[]{:S(2)}) collective-permute-start(bf16[512,512]{1,0:T(8,128)(2,1)} %get-tuple-element.70), channel_id=1, source_target_pairs={{0,1},{1,0},{2,3},{3,2},{4,5},{5,4},{6,7},{7,6},{8,9},{9,8},{10,11... | collective-permute-start | bytes 1572872 | tf_op jit(solution)/shard_map/ppermute | solution.py:29
  150.3 29.6 %collective-permute-start.39 = (bf16[256,2048]{1,0:T(8,128)(2,1)S(1)}, bf16[256,2048]{1,0:T(8,128)(2,1)S(1)}, u32[]{:S(2)}, u32[]{:S(2)}) collective-permute-start(bf16[256,2048]{1,0:T(8,128)(2,1)S(1)} %get-tuple-element.86), channel_id=1, source_target_pairs={{0,8},{4,12},{8,0},{12,4},{16,24},{20,28},{24,16},{28,20},{1,9},{5... | collective-permute-start | bytes 3145736 | tf_op jit(solution)/shard_map/ppermute | solution.py:29
  151.8 28.0 %collective-permute-start.40 = (bf16[256,2048]{1,0:T(8,128)(2,1)S(1)}, bf16[256,2048]{1,0:T(8,128)(2,1)S(1)}, u32[]{:S(2)}, u32[]{:S(2)}) collective-permute-start(bf16[256,2048]{1,0:T(8,128)(2,1)S(1)} %get-tuple-element.85), channel_id=1, source_target_pairs={{0,16},{4,20},{8,24},{12,28},{16,0},{20,4},{24,8},{28,12},{1,17},{... | collective-permute-start | bytes 3145736 | tf_op jit(solution)/shard_map/ppermute | solution.py:29
  152.3 27.5 %collective-permute-start.43 = (bf16[256,2048]{1,0:T(8,128)(2,1)S(1)}, bf16[256,2048]{1,0:T(8,128)(2,1)S(1)}, u32[]{:S(2)}, u32[]{:S(2)}) collective-permute-start(bf16[256,2048]{1,0:T(8,128)(2,1)S(1)} %get-tuple-element.82), channel_id=1, source_target_pairs={{0,4},{4,0},{8,12},{12,8},{16,20},{20,16},{24,28},{28,24},{1,5},{5... | collective-permute-start | bytes 3145736 | tf_op jit(solution)/shard_map/ppermute | solution.py:29
  152.3 25.3 %collective-permute-start.41 = (bf16[512,512]{1,0:T(8,128)(2,1)S(1)}, bf16[512,512]{1,0:T(8,128)(2,1)S(1)}, u32[]{:S(2)}, u32[]{:S(2)}) collective-permute-start(bf16[512,512]{1,0:T(8,128)(2,1)S(1)} %slice_bitcast_fusion), channel_id=1, source_target_pairs={{0,1},{1,0},{2,3},{3,2},{4,5},{5,4},{6,7},{7,6},{8,9},{9,8},{10,11... | collective-permute-start | bytes 1572872 | tf_op jit(solution)/shard_map/ppermute | solution.py:29
  152.4 26.5 %collective-permute-start.42 = (bf16[512,512]{1,0:T(8,128)(2,1)S(1)}, bf16[512,512]{1,0:T(8,128)(2,1)S(1)}, u32[]{:S(2)}, u32[]{:S(2)}) collective-permute-start(bf16[512,512]{1,0:T(8,128)(2,1)S(1)} %fusion.6), channel_id=1, source_target_pairs={{0,2},{1,3},{2,0},{3,1},{4,6},{5,7},{6,4},{7,5},{8,10},{9,11},{10,... | collective-permute-start | bytes 1572872 | tf_op jit(solution)/shard_map/ppermute | solution.py:29
  (20 other events, 197.4 us)

commit v10 on v9

--- a/solution.py
+++ b/solution.py
@@ -68,13 +68,16 @@
     return pltpu.with_memory_space_constraint(value, pltpu.VMEM)
 
 
-def call(kernel, outputs, operands, scratch=(), extra=(), aliases=None, limit=6):
+def call(kernel, outputs, operands, scratch=(), extra=(), aliases=None, slow=(), limit=16):
     spec = pl.BlockSpec(memory_space=pltpu.VMEM)
     return pl.pallas_call(
         kernel,
-        out_shape=tuple(pltpu.VMEM(shape, dtype) for shape, dtype in outputs),
+        out_shape=tuple(
+            jax.ShapeDtypeStruct(shape, dtype) if i in slow else pltpu.VMEM(shape, dtype)
+            for i, (shape, dtype) in enumerate(outputs)
+        ),
         in_specs=[spec] * len(operands) + [pl.BlockSpec(memory_space=pl.ANY)] * len(extra),
-        out_specs=(spec,) * len(outputs),
+        out_specs=tuple(pl.BlockSpec(memory_space=pl.ANY) if i in slow else spec for i in range(len(outputs))),
         scratch_shapes=list(scratch),
         input_output_aliases=aliases or {},
         compiler_params=pltpu.CompilerParams(vmem_limit_bytes=limit << 20),
@@ -200,7 +203,7 @@
     depth, paired, far, parts, student_ref, slope_ref, scale_ref, students_ref, mass_ref, turned_ref, *refs
 ):
     head_refs = refs[: len(parts)]
-    targets_ref, grad_ref, mine_ref, theirs_ref, share_ref, inverse, students = refs[len(parts) :]
+    out_ref, grad_ref, mine_ref, theirs_ref, share_ref, inverse, students, targets_ref, sent = refs[len(parts) :]
     me, place = lax.axis_index("sample"), lax.axis_index("cls")
     chip, core = me // 2, me % 2
     groups = lax.axis_size("cls")
@@ -218,12 +221,16 @@
             targets_ref[:, at] = target
             grad_ref[:, at] = ((student * students[...] - wide(target)) * wide(slope_ref[:, at])).astype(bf16)
         head_products(turned, core, depth, grad_ref, slice(i, i + tile), mine_ref, theirs_ref)
+    copy = pltpu.make_async_copy(targets_ref, out_ref, sent)
+    copy.start()
     for (mask, side), ref in zip(parts, head_refs):
 
         @pl.when((chip ^ mask) == (place ^ (groups - 1)))
         def _():
             at = pl.ds(rows_at(depth, side, paired), ref.shape[0])
             share_ref[:, at] = matmul(grad_ref[...], ref[...], ((1,), (1,))).astype(bf16)
+
+    copy.wait()
 
 
 def near_kernel(depth, near, grad_ref, turned_ref, *refs):
@@ -237,14 +244,12 @@
             head_products(turned, core, depth, grad_ref, slice(i, i + tile), refs[2 * index], refs[2 * index + 1])
 
 
-def shares_kernel(depth, paired, parts, grad_ref, turned_ref, *refs):
-    head_refs, pair, shares_ref = refs[: len(parts)], refs[-3:-1], refs[-1]
+def shares_kernel(depth, paired, parts, grad_ref, *refs):
+    head_refs, shares_ref = refs[: len(parts)], refs[-1]
     chip, place = lax.axis_index("sample") // 2, lax.axis_index("cls")
     for (mask, side), ref in zip(parts, head_refs):
         at = pl.ds(rows_at(depth, side, paired), ref.shape[0])
         shares_ref[chip ^ mask ^ place, :, at] = matmul(grad_ref[...], ref[...], ((1,), (1,))).astype(bf16)
-    near_kernel(depth, [0], grad_ref, turned_ref, *pair)
-
 
 def per_device(features, head, class_cap):
     rows, width = features.shape
@@ -319,7 +324,7 @@
 
     head_at = [at for at, _ in early + late]
     head_list = [part for _, part in early + late]
-    near = first + second
+    near = first + second + [0]
     diagonal = [(a, b) for a in first for b in second]
     far = (diagonal[-1][0] | diagonal[-1][1]) // 2
     near = [a | b for a, b in diagonal[:-1]] + near
@@ -327,7 +332,8 @@
         functools.partial(gradient_kernel, depth, paired, far, head_at),
         [((rows, classes), bf16)] * 2 + [((depth, classes), bf16)] * 2 + [((rows, width), bf16)],
         [student, slope, scale, students_mass, mass, turned] + head_list,
-        [pltpu.VMEM((rows, LANES), f32)] * 2,
+        [pltpu.VMEM((rows, LANES), f32)] * 2 + [pltpu.VMEM((rows, classes), bf16), pltpu.SemaphoreType.DMA],
+        slow=(0,),
     )
     theirs = flip(theirs, "sample", 1)
     pairs = call(
@@ -339,11 +345,11 @@
     block = lax.optimization_barrier((wide(mine) + wide(theirs)).astype(bf16))
     passed = {diagonal[-1]: cross(block, *diagonal[-1])}
     share_from = {groups - 2: flip(share, "cls", 1)}
-    others = {mask: flip(pairs[2 * i + 1], "sample", 1) for i, mask in enumerate(near)}
-    mine, theirs, shares = call(
+    others = {mask: flip(pairs[2 * i + 1], "sample", 1) for i, mask in enumerate(near) if mask}
+    (shares,) = call(
         functools.partial(shares_kernel, depth, paired, head_at),
-        [((depth, classes), bf16)] * 2 + [((groups, rows, width), bf16)],
-        [grad, turned] + head_list,
+        [((groups, rows, width), bf16)],
+        [grad] + head_list,
         extra=[block],
     )
 
@@ -351,15 +357,15 @@
     for mask in range(2, groups, 2):
         received = share_from[mask] if mask in share_from else flip(shares[mask | 1], "cls", 1)
         onward[mask] = (wide(shares[mask]) + wide(received)).astype(bf16)
-    ready = lax.optimization_barrier((*onward.values(), *others.values(), *passed.values(), theirs))
+    ready = lax.optimization_barrier((*onward.values(), *others.values(), *passed.values(), pairs[-1]))
     onward = dict(zip(onward, ready))
     others = dict(zip(others, ready[len(onward) :]))
     passed = dict(zip(passed, ready[len(onward) + len(others) :]))
-    own = wide(mine) + wide(flip(ready[-1], "sample", 1))
+    own = wide(pairs[-2]) + wide(flip(ready[-1], "sample", 1))
     returned = [flip(value, "cls", mask) for mask, value in onward.items()]
     grad_features = sum([wide(value) for value in returned], wide(shares[0])).astype(bf16)
 
-    mixed = {mask: wide(pairs[2 * i]) + wide(others[mask]) for i, mask in enumerate(near)}
+    mixed = {mask: wide(pairs[2 * i]) + wide(others[mask]) for i, mask in enumerate(near) if mask}
     for a, b in diagonal[:-1]:
         passed[a, b] = cross(mixed[a | b].astype(bf16), a, b)
     received = []

time: 182 us -> 179 us (0.984)
  local copies, waits for them, and re-layouts: 14.3 us -> 8.71 us
  waiting for transfers between devices: 81.8 us -> 83.9 us
    unnamed x49 -> x42, local copies, waits for them, and re-layouts: 14.2 us -> 8.67 us
    ppermute x42, waiting for transfers between devices: 81.8 us -> 83.9 us  [flip(): lax.ppermute(value, axis, [(i, i ^ mask) for i in range(lax.axis_size(axi...]
  transfers between devices with their start and end apart: 44 -> 44, of which waited for: 25 -> 26; matrix products, arithmetic and copies ran while one was open for 2% -> 1% of each run, Pallas kernels for 9% -> 9%
where the time goes in v10:
time: 179 us; the launch traced here: 178 us
  waiting for transfers between devices  83.9 us (47%)
  starting transfers between devices  46.3 us (26%)
  Pallas kernels  29.2 us (16%)
  other arithmetic  9.09 us (5%)
  local copies, waits for them, and re-layouts  8.71 us (5%)
    ppermute x42, waiting for transfers between devices, flip(): lax.ppermute(value, axis, [(i, i ^ mask) for i in range(lax.axis_size(axi...  83.9 us
    ppermute x42, starting transfers between devices, flip(): lax.ppermute(value, axis, [(i, i ^ mask) for i in range(lax.axis_size(axi...  45.3 us
    pallas_call x12, Pallas kernels, call(): pl.pallas_call(kernel, out_shape=tuple((jax.ShapeDtypeStruct(shape, dtype...  29.2 us
    unnamed x42, local copies, waits for them, and re-layouts  8.67 us
  transfers between devices with their start and end apart: 44, of which 26 were waited for; matrix products, arithmetic and copies ran while one was open for 1% of the time, Pallas kernels for 9%

profile of v10, /device:TPU:0, one launch (start us, length us, event | category | flops | bytes accessed | tf_op | source)
XLA Modules:
  0.0 178.3 jit_solution(18182219271102081334)
XLA Ops:
  0.6 3.0 %collective-permute-start.4 = (bf16[256,2048]{1,0:T(8,128)(2,1)}, bf16[256,2048]{1,0:T(8,128)(2,1)S(1)}, u32[]{:S(2)}, u32[]{:S(2)}) collective-permute-start(bf16[256,2048]{1,0:T(8,128)(2,1)} %refs_0_.5), channel_id=1, source_target_pairs={{0,8},{4,12},{8,0},{12,4},{16,24},{20,28},{24,16},{28,20},{1,9},{5... | collective-permute-start | bytes 3145736 | tf_op jit(solution)/shard_map/ppermute | solution.py:29
  3.6 1.5 collective-permute-start.5
  5.2 2.6 %collective-permute-start.1 = (bf16[512,512]{1,0:T(8,128)(2,1)}, bf16[512,512]{1,0:T(8,128)(2,1)}, u32[]{:S(2)}, u32[]{:S(2)}) collective-permute-start(bf16[512,512]{1,0:T(8,128)(2,1)} %refs_0_.3), channel_id=1, source_target_pairs={{0,2},{1,3},{2,0},{3,1},{4,6},{5,7},{6,4},{7,5},{8,10},{9,11},{10,... | collective-permute-start | bytes 1572872 | tf_op jit(solution)/shard_map/ppermute | solution.py:29
  7.8 1.6 collective-permute-start
  9.3 21.5 %collective-permute-done.1.refs_2_ = bf16[512,512]{1,0:T(8,128)(2,1)} collective-permute-done((bf16[512,512]{1,0:T(8,128)(2,1)}, bf16[512,512]{1,0:T(8,128)(2,1)}, u32[]{:S(2)}, u32[]{:S(2)}) %collective-permute-start.1) | collective-permute-done | bytes 524320 | tf_op jit(solution)/shard_map/ppermute | solution.py:29
  31.5 1.1 collective-permute-done.refs_1_
  33.0 13.5 %collective-permute-done.2.refs_3_ = bf16[512,512]{1,0:T(8,128)(2,1)S(1)} collective-permute-done((bf16[512,512]{1,0:T(8,128)(2,1)}, bf16[512,512]{1,0:T(8,128)(2,1)S(1)}, u32[]{:S(2)}, u32[]{:S(2)}) %collective-permute-start.2) | collective-permute-done | bytes 524320 | tf_op jit(solution)/shard_map/ppermute | solution.py:29
  46.6 5.8 %shard_map.58 = (bf16[4,512,512]{2,1,0:T(8,128)(2,1)S(1)}, f32[512,2048]{1,0:T(8,128)S(1)}) custom-call(bf16[512,512]{1,0:T(8,128)(2,1)S(1)} %copy-done.17, bf16[512,512]{1,0:T(8,128)(2,1)} %collective-permute-done.refs_1_, bf16[512,512]{1,0:T(8,128)(2,1)} %collective-permute-done.1.refs_2_, bf16[512,512]{1,0:T(8,128)(2,1)S(1)} %collective-permute-done.2.refs_3_, ...), custom_call_target="tpu_custom_call" | custom-call | flops 1 | bytes 1 | tf_op jit(solution)/shard_map/pallas_call | solution.py:73
  52.5 2.6 %collective-permute-done.9.refs_1_.refs_7_ = bf16[256,2048]{1,0:T(8,128)(2,1)S(1)} collective-permute-done((bf16[256,2048]{1,0:T(8,128)(2,1)S(1)}, bf16[256,2048]{1,0:T(8,128)(2,1)S(1)}, u32[]{:S(2)}, u32[]{:S(2)}) %collective-permute-start.9) | collective-permute-done | bytes 1048608 | tf_op jit(solution)/shard_map/ppermute | solution.py:29
  55.2 3.5 %shard_map.59 = (f32[512,2048]{1,0:T(8,128)S(1)}, bf16[512,2048]{1,0:T(8,128)(2,1)S(1)}, f32[2,512]{1,0:T(2,128)S(1)}) custom-call(f32[512,2048]{1,0:T(8,128)S(1)} %get-tuple-element.47.logits_ref, bf16[4,512,512]{2,1,0:T(8,128)(2,1)S(1)} %get-tuple-element.48.blocks_ref, ...), custom_call_target="tpu_custom_call", output_to_operand_aliasing={{0}: (0, {})} | custom-call | flops 1 | bytes 1 | tf_op jit(solution)/shard_map/pallas_call | solution.py:73
  58.6 2.9 %collective-permute-start.10 = (f32[2,512]{1,0:T(2,128)S(1)}, f32[2,512]{1,0:T(2,128)S(1)}, u32[]{:S(2)}, u32[]{:S(2)}) collective-permute-start(f32[2,512]{1,0:T(2,128)S(1)} %get-tuple-element.53), channel_id=1, source_target_pairs={{0,3},{1,2},{2,1},{3,0},{4,7},{5,6},{6,5},{7,4},{8,11},{9,10},{10,... | collective-permute-start | bytes 12296 | tf_op jit(solution)/shard_map/ppermute | solution.py:29
  61.6 1.5 collective-permute-start.12
  64.1 2.0 %collective-permute-done.11 = f32[2,512]{1,0:T(2,128)S(1)} collective-permute-done((f32[2,512]{1,0:T(2,128)S(1)}, f32[2,512]{1,0:T(2,128)S(1)}, u32[]{:S(2)}, u32[]{:S(2)}) %collective-permute-start.11) | collective-permute-done | bytes 4128 | tf_op jit(solution)/shard_map/ppermute | solution.py:29
  66.9 1.2 collective-permute-done.13
  68.1 1.5 collective-permute-start.14
  69.6 1.5 collective-permute-start.15
  73.2 1.5 collective-permute-done.16
  75.4 1.5 collective-permute-start.17
  77.5 2.3 %collective-permute-start.19 = (f32[1,512]{1,0:T(1,128)S(1)}, f32[1,512]{1,0:T(1,128)S(1)}, u32[]{:S(2)}, u32[]{:S(2)}) collective-permute-start(f32[1,512]{1,0:T(1,128)S(1)} %get-tuple-element.55), channel_id=1, source_target_pairs={{0,1},{1,0},{2,3},{3,2},{4,5},{5,4},{6,7},{7,6},{8,9},{9,8},{10,11... | collective-permute-start | bytes 6152 | tf_op jit(solution)/shard_map/ppermute | solution.py:29
  82.2 1.2 collective-permute-done.20
  83.9 1.5 collective-permute-start.22
  85.4 1.5 collective-permute-start.23
  89.7 2.6 %collective-permute-start.24 = (f32[1,512]{1,0:T(1,128)S(1)}, f32[1,512]{1,0:T(1,128)S(1)}, u32[]{:S(2)}, u32[]{:S(2)}) collective-permute-start(f32[1,512]{1,0:T(1,128)S(1)} %get-tuple-element.57), channel_id=1, source_target_pairs={{0,3},{1,2},{2,1},{3,0},{4,7},{5,6},{6,5},{7,4},{8,11},{9,10},{10,... | collective-permute-start | bytes 6152 | tf_op jit(solution)/shard_map/ppermute | solution.py:29
  95.2 1.7 collective-permute-done.25
  97.6 1.2 collective-permute-done.27
  98.8 1.5 collective-permute-start.28
  100.3 1.5 collective-permute-start.29
  104.0 1.5 collective-permute-done.30
  106.1 1.5 collective-permute-start.31
  108.5 2.0 %collective-permute-start.33 = (f32[1,512]{1,0:T(1,128)S(1)}, f32[1,512]{1,0:T(1,128)S(1)}, u32[]{:S(2)}, u32[]{:S(2)}) collective-permute-start(f32[1,512]{1,0:T(1,128)S(1)} %get-tuple-element.59), channel_id=1, source_target_pairs={{0,1},{1,0},{2,3},{3,2},{4,5},{5,4},{6,7},{7,6},{8,9},{9,8},{10,11... | collective-permute-start | bytes 6152 | tf_op jit(solution)/shard_map/ppermute | solution.py:29
  112.2 6.1 %shard_map.67 = (bf16[512,2048]{1,0:T(8,128)(2,1)}, bf16[512,2048]{1,0:T(8,128)(2,1)S(1)}, bf16[256,2048]{1,0:T(8,128)(2,1)S(1)}, bf16[256,2048]{1,0:T(8,128)(2,1)S(1)}, bf16[512,512]{1,0:T(8,128)(2,1)}) custom-call(f32[512,2048]{1,0:T(8,128)S(1)} %get-tuple-element.51.student_ref, bf16[512,2048]{1,0:T(8,128)(2,1)S(1)} %get-tuple-element.52.slope_ref, ...), custom_call_target="tpu_custom_call" | custom-call | flops 1 | bytes 1 | tf_op jit(solution)/shard_map/pallas_call | solution.py:73
  118.3 3.4 %shard_map.68 = (bf16[256,2048]{1,0:T(8,128)(2,1)S(1)}, bf16[256,2048]{1,0:T(8,128)(2,1)}, bf16[256,2048]{1,0:T(8,128)(2,1)S(1)}, bf16[256,2048]{1,0:T(8,128)(2,...) custom-call(bf16[512,2048]{1,0:T(8,128)(2,1)S(1)} %get-tuple-element.62.grad_ref, ...), custom_call_target="tpu_custom_call" | custom-call | flops 1 | bytes 1 | tf_op jit(solution)/shard_map/pallas_call | solution.py:73
  123.8 1.7 add_convert_fusion.1.refs_8_
  126.6 2.0 %collective-permute-start.35 = (bf16[512,512]{1,0:T(8,128)(2,1)}, bf16[512,512]{1,0:T(8,128)(2,1)}, u32[]{:S(2)}, u32[]{:S(2)}) collective-permute-start(bf16[512,512]{1,0:T(8,128)(2,1)} %get-tuple-element.72), channel_id=1, source_target_pairs={{0,1},{1,0},{2,3},{3,2},{4,5},{5,4},{6,7},{7,6},{8,9},{9,8},{10,11... | collective-permute-start | bytes 1572872 | tf_op jit(solution)/shard_map/ppermute | solution.py:29
  128.6 1.2 copy-done.2
  129.8 1.2 copy-done.4
  131.0 1.2 copy-done.6
  132.3 1.2 copy-done.8
  133.5 1.6 copy-done.10
  135.1 5.9 %shard_map.69 = bf16[4,512,512]{2,1,0:T(8,128)(2,1)S(1)} custom-call(bf16[512,2048]{1,0:T(8,128)(2,1)S(1)} %copy-done.10, bf16[256,2048]{1,0:T(8,128)(2,1)S(1)} %copy-done, bf16[256,2048]{1,0:T(8,128)(2,1)} %collective-permute-done.3.refs_5_.refs_1_, bf16[256,2048]{1,0:T(8,128)(2,1)S(1)} %collective-permute-done.4.refs_6_.refs_2_, ...), custom_call_target="tpu_custom_call" | custom-call | flops 1 | bytes 1 | tf_op jit(solution)/shard_map/pallas_call | solution.py:73
  141.2 1.3 fusion.6
  142.7 3.1 %fusion.3 = (bf16[256,2048]{1,0:T(8,128)(2,1)S(1)}, bf16[256,2048]{1,0:T(8,128)(2,1)S(1)}) fusion(bf16[256,2048]{1,0:T(8,128)(2,1)} %collective-permute-done.38, bf16[256,2048]{1,0:T(8,128)(2,1)} %collective-permute-done.37, bf16[256,2048]{1,0:T(8,128)(2,1)S(1)} %copy-done.16, pred[]{:T(512)S(6)} %eq.11, pred[]{:T(512)S(6)} %eq.12, ...), kind=kLoop, calls=%fused_computation.5 | loop fusion | flops 6815744 | bytes 7340034 | tf_op jit(solution)/shard_map/convert_element_type | solution.py:377
  145.8 1.5 collective-permute-start.39
  147.8 1.6 collective-permute-start.41
  149.4 1.1 collective-permute-start.42
  150.5 21.7 %collective-permute-done.41 = bf16[512,512]{1,0:T(8,128)(2,1)S(1)} collective-permute-done((bf16[512,512]{1,0:T(8,128)(2,1)S(1)}, bf16[512,512]{1,0:T(8,128)(2,1)S(1)}, u32[]{:S(2)}, u32[]{:S(2)}) %collective-permute-start.41) | collective-permute-done | bytes 524320 | tf_op jit(solution)/shard_map/ppermute | solution.py:29
  172.2 3.4 %collective-permute-done.42 = bf16[512,512]{1,0:T(8,128)(2,1)S(1)} collective-permute-done((bf16[512,512]{1,0:T(8,128)(2,1)S(1)}, bf16[512,512]{1,0:T(8,128)(2,1)S(1)}, u32[]{:S(2)}, u32[]{:S(2)}) %collective-permute-start.42) | collective-permute-done | bytes 524320 | tf_op jit(solution)/shard_map/ppermute | solution.py:29
  176.6 1.7 add_convert_fusion
  (128 shorter events, 26.0 us)
Async XLA Ops:
  0.6 30.2 %collective-permute-start.4 = (bf16[256,2048]{1,0:T(8,128)(2,1)}, bf16[256,2048]{1,0:T(8,128)(2,1)S(1)}, u32[]{:S(2)}, u32[]{:S(2)}) collective-permute-start(bf16[256,2048]{1,0:T(8,128)(2,1)} %refs_0_.5), channel_id=1, source_target_pairs={{0,8},{4,12},{8,0},{12,4},{16,24},{20,28},{24,16},{28,20},{1,9},{5... | collective-permute-start | bytes 3145736 | tf_op jit(solution)/shard_map/ppermute | solution.py:29
  3.6 27.2 %collective-permute-start.5 = (bf16[256,2048]{1,0:T(8,128)(2,1)}, bf16[256,2048]{1,0:T(8,128)(2,1)S(1)}, u32[]{:S(2)}, u32[]{:S(2)}) collective-permute-start(bf16[256,2048]{1,0:T(8,128)(2,1)} %refs_0_.5), channel_id=1, source_target_pairs={{0,16},{4,20},{8,24},{12,28},{16,0},{20,4},{24,8},{28,12},{1,17},{... | collective-permute-start | bytes 3145736 | tf_op jit(solution)/shard_map/ppermute | solution.py:29
  5.2 25.7 %collective-permute-start.1 = (bf16[512,512]{1,0:T(8,128)(2,1)}, bf16[512,512]{1,0:T(8,128)(2,1)}, u32[]{:S(2)}, u32[]{:S(2)}) collective-permute-start(bf16[512,512]{1,0:T(8,128)(2,1)} %refs_0_.3), channel_id=1, source_target_pairs={{0,2},{1,3},{2,0},{3,1},{4,6},{5,7},{6,4},{7,5},{8,10},{9,11},{10,... | collective-permute-start | bytes 1572872 | tf_op jit(solution)/shard_map/ppermute | solution.py:29
  7.8 24.8 %collective-permute-start.3 = (bf16[256,2048]{1,0:T(8,128)(2,1)}, bf16[256,2048]{1,0:T(8,128)(2,1)}, u32[]{:S(2)}, u32[]{:S(2)}) collective-permute-start(bf16[256,2048]{1,0:T(8,128)(2,1)} %refs_0_.5), channel_id=1, source_target_pairs={{0,4},{4,0},{8,12},{12,8},{16,20},{20,16},{24,28},{28,24},{1,5},{5... | collective-permute-start | bytes 3145736 | tf_op jit(solution)/shard_map/ppermute | solution.py:29
  7.8 24.8 %collective-permute-start = (bf16[512,512]{1,0:T(8,128)(2,1)}, bf16[512,512]{1,0:T(8,128)(2,1)}, u32[]{:S(2)}, u32[]{:S(2)}) collective-permute-start(bf16[512,512]{1,0:T(8,128)(2,1)} %refs_0_.3), channel_id=1, source_target_pairs={{0,1},{1,0},{2,3},{3,2},{4,5},{5,4},{6,7},{7,6},{8,9},{9,8},{10,11... | collective-permute-start | bytes 1572872 | tf_op jit(solution)/shard_map/ppermute | solution.py:29
  30.8 15.7 %collective-permute-start.6 = (bf16[256,2048]{1,0:T(8,128)(2,1)S(1)}, bf16[256,2048]{1,0:T(8,128)(2,1)S(1)}, u32[]{:S(2)}, u32[]{:S(2)}) collective-permute-start(bf16[256,2048]{1,0:T(8,128)(2,1)S(1)} %collective-permute-done.4.refs_6_.refs_2_), channel_id=1, source_target_pairs={{0,4},{4,0},{8,12},{12,8},{16,20},{20,16},{24,28},{28,24},{1,5},{5... | collective-permute-start | bytes 3145736 | tf_op jit(solution)/shard_map/ppermute | solution.py:29
  30.8 15.7 %collective-permute-start.7 = (bf16[256,2048]{1,0:T(8,128)(2,1)S(1)}, bf16[256,2048]{1,0:T(8,128)(2,1)S(1)}, u32[]{:S(2)}, u32[]{:S(2)}) collective-permute-start(bf16[256,2048]{1,0:T(8,128)(2,1)S(1)} %collective-permute-done.5.refs_8_.refs_4_), channel_id=1, source_target_pairs={{0,4},{4,0},{8,12},{12,8},{16,20},{20,16},{24,28},{28,24},{1,5},{5... | collective-permute-start | bytes 3145736 | tf_op jit(solution)/shard_map/ppermute | solution.py:29
  32.5 19.9 %collective-permute-start.8 = (bf16[256,2048]{1,0:T(8,128)(2,1)S(1)}, bf16[256,2048]{1,0:T(8,128)(2,1)S(1)}, u32[]{:S(2)}, u32[]{:S(2)}) collective-permute-start(bf16[256,2048]{1,0:T(8,128)(2,1)S(1)} %broadcast_select_fusion), channel_id=1, source_target_pairs={{0,16},{4,12},{8,24},{12,4},{16,0},{20,28},{24,8},{28,20},{1,17},{... | collective-permute-start | bytes 3145736 | tf_op jit(solution)/shard_map/ppermute | solution.py:34
  33.0 13.5 %collective-permute-start.2 = (bf16[512,512]{1,0:T(8,128)(2,1)}, bf16[512,512]{1,0:T(8,128)(2,1)S(1)}, u32[]{:S(2)}, u32[]{:S(2)}) collective-permute-start(bf16[512,512]{1,0:T(8,128)(2,1)} %collective-permute-done.1.refs_2_), channel_id=1, source_target_pairs={{0,1},{1,0},{2,3},{3,2},{4,5},{5,4},{6,7},{7,6},{8,9},{9,8},{10,11... | collective-permute-start | bytes 1572872 | tf_op jit(solution)/shard_map/ppermute | solution.py:29
  46.6 65.6 %copy-start.1 = (bf16[256,2048]{1,0:T(8,128)(2,1)}, bf16[256,2048]{1,0:T(8,128)(2,1)S(1)}, u32[]{:S(2)}) copy-start(bf16[256,2048]{1,0:T(8,128)(2,1)S(1)} %collective-permute-done.6.refs_7_.refs_3_) | copy-start | bytes 3145732
  46.6 65.5 %copy-start.3 = (bf16[256,2048]{1,0:T(8,128)(2,1)}, bf16[256,2048]{1,0:T(8,128)(2,1)S(1)}, u32[]{:S(2)}) copy-start(bf16[256,2048]{1,0:T(8,128)(2,1)S(1)} %collective-permute-done.7.refs_9_.refs_5_) | copy-start | bytes 3145732
  52.5 59.7 %copy-start.5 = (bf16[256,2048]{1,0:T(8,128)(2,1)}, bf16[256,2048]{1,0:T(8,128)(2,1)S(1)}, u32[]{:S(2)}) copy-start(bf16[256,2048]{1,0:T(8,128)(2,1)S(1)} %collective-permute-done.8.refs_0_.refs_6_) | copy-start | bytes 3145732
  52.5 2.7 %collective-permute-start.9 = (bf16[256,2048]{1,0:T(8,128)(2,1)S(1)}, bf16[256,2048]{1,0:T(8,128)(2,1)S(1)}, u32[]{:S(2)}, u32[]{:S(2)}) collective-permute-start(bf16[256,2048]{1,0:T(8,128)(2,1)S(1)} %collective-permute-done.8.refs_0_.refs_6_), channel_id=1, source_target_pairs={{0,4},{4,0},{8,12},{12,8},{16,20},{20,16},{24,28},{28,24},{1,5},{5... | collective-permute-start | bytes 3145736 | tf_op jit(solution)/shard_map/ppermute | solution.py:29
  55.2 57.0 %copy-start.7 = (bf16[256,2048]{1,0:T(8,128)(2,1)}, bf16[256,2048]{1,0:T(8,128)(2,1)S(1)}, u32[]{:S(2)}) copy-start(bf16[256,2048]{1,0:T(8,128)(2,1)S(1)} %collective-permute-done.9.refs_1_.refs_7_) | copy-start | bytes 3145732
  58.6 5.5 %collective-permute-start.10 = (f32[2,512]{1,0:T(2,128)S(1)}, f32[2,512]{1,0:T(2,128)S(1)}, u32[]{:S(2)}, u32[]{:S(2)}) collective-permute-start(f32[2,512]{1,0:T(2,128)S(1)} %get-tuple-element.53), channel_id=1, source_target_pairs={{0,3},{1,2},{2,1},{3,0},{4,7},{5,6},{6,5},{7,4},{8,11},{9,10},{10,... | collective-permute-start | bytes 12296 | tf_op jit(solution)/shard_map/ppermute | solution.py:29
  61.6 4.5 %collective-permute-start.11 = (f32[2,512]{1,0:T(2,128)S(1)}, f32[2,512]{1,0:T(2,128)S(1)}, u32[]{:S(2)}, u32[]{:S(2)}) collective-permute-start(f32[2,512]{1,0:T(2,128)S(1)} %get-tuple-element.53), channel_id=1, source_target_pairs={{0,2},{1,3},{2,0},{3,1},{4,6},{5,7},{6,4},{7,5},{8,10},{9,11},{10,... | collective-permute-start | bytes 12296 | tf_op jit(solution)/shard_map/ppermute | solution.py:29
  61.6 4.5 %collective-permute-start.12 = (f32[2,512]{1,0:T(2,128)S(1)}, f32[2,512]{1,0:T(2,128)S(1)}, u32[]{:S(2)}, u32[]{:S(2)}) collective-permute-start(f32[2,512]{1,0:T(2,128)S(1)} %get-tuple-element.53), channel_id=1, source_target_pairs={{0,1},{1,0},{2,3},{3,2},{4,5},{5,4},{6,7},{7,6},{8,9},{9,8},{10,11... | collective-permute-start | bytes 12296 | tf_op jit(solution)/shard_map/ppermute | solution.py:29
  66.8 1.2 collective-permute-start.13
  68.1 4.6 %collective-permute-start.14 = (f32[1,2048]{1,0:T(1,128)S(1)}, f32[1,2048]{1,0:T(1,128)S(1)}, u32[]{:S(2)}, u32[]{:S(2)}) collective-permute-start(f32[1,2048]{1,0:T(1,128)S(1)} %add.114), channel_id=1, source_target_pairs={{0,24},{4,28},{8,16},{12,20},{16,8},{20,12},{24,0},{28,4},{1,25},{... | collective-permute-start | bytes 24584 | tf_op jit(solution)/shard_map/ppermute | solution.py:29
  69.6 3.7 %collective-permute-start.15 = (f32[1,2048]{1,0:T(1,128)S(1)}, f32[1,2048]{1,0:T(1,128)S(1)}, u32[]{:S(2)}, u32[]{:S(2)}) collective-permute-start(f32[1,2048]{1,0:T(1,128)S(1)} %add.114), channel_id=1, source_target_pairs={{0,16},{4,20},{8,24},{12,28},{16,0},{20,4},{24,8},{28,12},{1,17},{... | collective-permute-start | bytes 24584 | tf_op jit(solution)/shard_map/ppermute | solution.py:29
  71.1 3.7 %collective-permute-start.16 = (f32[1,2048]{1,0:T(1,128)S(1)}, f32[1,2048]{1,0:T(1,128)S(1)}, u32[]{:S(2)}, u32[]{:S(2)}) collective-permute-start(f32[1,2048]{1,0:T(1,128)S(1)} %add.114), channel_id=1, source_target_pairs={{0,8},{4,12},{8,0},{12,4},{16,24},{20,28},{24,16},{28,20},{1,9},{5... | collective-permute-start | bytes 24584 | tf_op jit(solution)/shard_map/ppermute | solution.py:29
  75.4 5.4 %collective-permute-start.17 = (f32[1,512]{1,0:T(1,128)S(1)}, f32[1,512]{1,0:T(1,128)S(1)}, u32[]{:S(2)}, u32[]{:S(2)}) collective-permute-start(f32[1,512]{1,0:T(1,128)S(1)} %get-tuple-element.55), channel_id=1, source_target_pairs={{0,3},{1,2},{2,1},{3,0},{4,7},{5,6},{6,5},{7,4},{8,11},{9,10},{10,... | collective-permute-start | bytes 6152 | tf_op jit(solution)/shard_map/ppermute | solution.py:29
  76.9 4.5 %collective-permute-start.18 = (f32[1,512]{1,0:T(1,128)S(1)}, f32[1,512]{1,0:T(1,128)S(1)}, u32[]{:S(2)}, u32[]{:S(2)}) collective-permute-start(f32[1,512]{1,0:T(1,128)S(1)} %get-tuple-element.55), channel_id=1, source_target_pairs={{0,2},{1,3},{2,0},{3,1},{4,6},{5,7},{6,4},{7,5},{8,10},{9,11},{10,... | collective-permute-start | bytes 6152 | tf_op jit(solution)/shard_map/ppermute | solution.py:29
  77.5 3.9 %collective-permute-start.19 = (f32[1,512]{1,0:T(1,128)S(1)}, f32[1,512]{1,0:T(1,128)S(1)}, u32[]{:S(2)}, u32[]{:S(2)}) collective-permute-start(f32[1,512]{1,0:T(1,128)S(1)} %get-tuple-element.55), channel_id=1, source_target_pairs={{0,1},{1,0},{2,3},{3,2},{4,5},{5,4},{6,7},{7,6},{8,9},{9,8},{10,11... | collective-permute-start | bytes 6152 | tf_op jit(solution)/shard_map/ppermute | solution.py:29
  82.1 1.2 collective-permute-start.20
  83.3 4.6 %collective-permute-start.21 = (f32[1,2048]{1,0:T(1,128)S(1)}, f32[1,2048]{1,0:T(1,128)S(1)}, u32[]{:S(2)}, u32[]{:S(2)}) collective-permute-start(f32[1,2048]{1,0:T(1,128)S(1)} %add.121), channel_id=1, source_target_pairs={{0,24},{4,28},{8,16},{12,20},{16,8},{20,12},{24,0},{28,4},{1,25},{... | collective-permute-start | bytes 24584 | tf_op jit(solution)/shard_map/ppermute | solution.py:29
  83.9 4.1 %collective-permute-start.22 = (f32[1,2048]{1,0:T(1,128)S(1)}, f32[1,2048]{1,0:T(1,128)S(1)}, u32[]{:S(2)}, u32[]{:S(2)}) collective-permute-start(f32[1,2048]{1,0:T(1,128)S(1)} %add.121), channel_id=1, source_target_pairs={{0,16},{4,20},{8,24},{12,28},{16,0},{20,4},{24,8},{28,12},{1,17},{... | collective-permute-start | bytes 24584 | tf_op jit(solution)/shard_map/ppermute | solution.py:29
  85.4 3.7 %collective-permute-start.23 = (f32[1,2048]{1,0:T(1,128)S(1)}, f32[1,2048]{1,0:T(1,128)S(1)}, u32[]{:S(2)}, u32[]{:S(2)}) collective-permute-start(f32[1,2048]{1,0:T(1,128)S(1)} %add.121), channel_id=1, source_target_pairs={{0,8},{4,12},{8,0},{12,4},{16,24},{20,28},{24,16},{28,20},{1,9},{5... | collective-permute-start | bytes 24584 | tf_op jit(solution)/shard_map/ppermute | solution.py:29
  89.7 5.4 %collective-permute-start.24 = (f32[1,512]{1,0:T(1,128)S(1)}, f32[1,512]{1,0:T(1,128)S(1)}, u32[]{:S(2)}, u32[]{:S(2)}) collective-permute-start(f32[1,512]{1,0:T(1,128)S(1)} %get-tuple-element.57), channel_id=1, source_target_pairs={{0,3},{1,2},{2,1},{3,0},{4,7},{5,6},{6,5},{7,4},{8,11},{9,10},{10,... | collective-permute-start | bytes 6152 | tf_op jit(solution)/shard_map/ppermute | solution.py:29
  92.3 4.5 %collective-permute-start.25 = (f32[1,512]{1,0:T(1,128)S(1)}, f32[1,512]{1,0:T(1,128)S(1)}, u32[]{:S(2)}, u32[]{:S(2)}) collective-permute-start(f32[1,512]{1,0:T(1,128)S(1)} %get-tuple-element.57), channel_id=1, source_target_pairs={{0,2},{1,3},{2,0},{3,1},{4,6},{5,7},{6,4},{7,5},{8,10},{9,11},{10,... | collective-permute-start | bytes 6152 | tf_op jit(solution)/shard_map/ppermute | solution.py:29
  93.3 3.6 %collective-permute-start.26 = (f32[1,512]{1,0:T(1,128)S(1)}, f32[1,512]{1,0:T(1,128)S(1)}, u32[]{:S(2)}, u32[]{:S(2)}) collective-permute-start(f32[1,512]{1,0:T(1,128)S(1)} %get-tuple-element.57), channel_id=1, source_target_pairs={{0,1},{1,0},{2,3},{3,2},{4,5},{5,4},{6,7},{7,6},{8,9},{9,8},{10,11... | collective-permute-start | bytes 6152 | tf_op jit(solution)/shard_map/ppermute | solution.py:29
  97.5 1.2 collective-permute-start.27
  98.8 4.6 %collective-permute-start.28 = (f32[1,2048]{1,0:T(1,128)S(1)}, f32[1,2048]{1,0:T(1,128)S(1)}, u32[]{:S(2)}, u32[]{:S(2)}) collective-permute-start(f32[1,2048]{1,0:T(1,128)S(1)} %add.128), channel_id=1, source_target_pairs={{0,24},{4,28},{8,16},{12,20},{16,8},{20,12},{24,0},{28,4},{1,25},{... | collective-permute-start | bytes 24584 | tf_op jit(solution)/shard_map/ppermute | solution.py:29
  100.3 3.7 %collective-permute-start.29 = (f32[1,2048]{1,0:T(1,128)S(1)}, f32[1,2048]{1,0:T(1,128)S(1)}, u32[]{:S(2)}, u32[]{:S(2)}) collective-permute-start(f32[1,2048]{1,0:T(1,128)S(1)} %add.128), channel_id=1, source_target_pairs={{0,16},{4,20},{8,24},{12,28},{16,0},{20,4},{24,8},{28,12},{1,17},{... | collective-permute-start | bytes 24584 | tf_op jit(solution)/shard_map/ppermute | solution.py:29
  101.8 3.7 %collective-permute-start.30 = (f32[1,2048]{1,0:T(1,128)S(1)}, f32[1,2048]{1,0:T(1,128)S(1)}, u32[]{:S(2)}, u32[]{:S(2)}) collective-permute-start(f32[1,2048]{1,0:T(1,128)S(1)} %add.128), channel_id=1, source_target_pairs={{0,8},{4,12},{8,0},{12,4},{16,24},{20,28},{24,16},{28,20},{1,9},{5... | collective-permute-start | bytes 24584 | tf_op jit(solution)/shard_map/ppermute | solution.py:29
  106.1 5.4 %collective-permute-start.31 = (f32[1,512]{1,0:T(1,128)S(1)}, f32[1,512]{1,0:T(1,128)S(1)}, u32[]{:S(2)}, u32[]{:S(2)}) collective-permute-start(f32[1,512]{1,0:T(1,128)S(1)} %get-tuple-element.59), channel_id=1, source_target_pairs={{0,3},{1,2},{2,1},{3,0},{4,7},{5,6},{6,5},{7,4},{8,11},{9,10},{10,... | collective-permute-start | bytes 6152 | tf_op jit(solution)/shard_map/ppermute | solution.py:29
  107.6 4.5 %collective-permute-start.32 = (f32[1,512]{1,0:T(1,128)S(1)}, f32[1,512]{1,0:T(1,128)S(1)}, u32[]{:S(2)}, u32[]{:S(2)}) collective-permute-start(f32[1,512]{1,0:T(1,128)S(1)} %get-tuple-element.59), channel_id=1, source_target_pairs={{0,2},{1,3},{2,0},{3,1},{4,6},{5,7},{6,4},{7,5},{8,10},{9,11},{10,... | collective-permute-start | bytes 6152 | tf_op jit(solution)/shard_map/ppermute | solution.py:29
  108.5 3.6 %collective-permute-start.33 = (f32[1,512]{1,0:T(1,128)S(1)}, f32[1,512]{1,0:T(1,128)S(1)}, u32[]{:S(2)}, u32[]{:S(2)}) collective-permute-start(f32[1,512]{1,0:T(1,128)S(1)} %get-tuple-element.59), channel_id=1, source_target_pairs={{0,1},{1,0},{2,3},{3,2},{4,5},{5,4},{6,7},{7,6},{8,9},{9,8},{10,11... | collective-permute-start | bytes 6152 | tf_op jit(solution)/shard_map/ppermute | solution.py:29
  118.2 5.5 %collective-permute-start.34 = (bf16[256,2048]{1,0:T(8,128)(2,1)S(1)}, bf16[256,2048]{1,0:T(8,128)(2,1)S(1)}, u32[]{:S(2)}, u32[]{:S(2)}) collective-permute-start(bf16[256,2048]{1,0:T(8,128)(2,1)S(1)} %get-tuple-element.61), channel_id=1, source_target_pairs={{0,4},{4,0},{8,12},{12,8},{16,20},{20,16},{24,28},{28,24},{1,5},{5... | collective-permute-start | bytes 3145736 | tf_op jit(solution)/shard_map/ppermute | solution.py:29
  125.5 16.9 %collective-permute-start.38 = (bf16[256,2048]{1,0:T(8,128)(2,1)}, bf16[256,2048]{1,0:T(8,128)(2,1)}, u32[]{:S(2)}, u32[]{:S(2)}) collective-permute-start(bf16[256,2048]{1,0:T(8,128)(2,1)} %add_convert_fusion.1.refs_8_), channel_id=1, source_target_pairs={{0,8},{4,20},{8,0},{12,28},{16,24},{20,4},{24,16},{28,12},{1,9},{5... | collective-permute-start | bytes 3145736 | tf_op jit(solution)/shard_map/ppermute | solution.py:34
  126.0 16.4 %collective-permute-start.36 = (bf16[256,2048]{1,0:T(8,128)(2,1)}, bf16[256,2048]{1,0:T(8,128)(2,1)}, u32[]{:S(2)}, u32[]{:S(2)}) collective-permute-start(bf16[256,2048]{1,0:T(8,128)(2,1)} %get-tuple-element.73), channel_id=1, source_target_pairs={{0,4},{4,0},{8,12},{12,8},{16,20},{20,16},{24,28},{28,24},{1,5},{5... | collective-permute-start | bytes 3145736 | tf_op jit(solution)/shard_map/ppermute | solution.py:29
  126.2 16.2 %collective-permute-start.37 = (bf16[256,2048]{1,0:T(8,128)(2,1)}, bf16[256,2048]{1,0:T(8,128)(2,1)}, u32[]{:S(2)}, u32[]{:S(2)}) collective-permute-start(bf16[256,2048]{1,0:T(8,128)(2,1)} %get-tuple-element.74), channel_id=1, source_target_pairs={{0,4},{4,0},{8,12},{12,8},{16,20},{20,16},{24,28},{28,24},{1,5},{5... | collective-permute-start | bytes 3145736 | tf_op jit(solution)/shard_map/ppermute | solution.py:29
  126.6 14.6 %collective-permute-start.35 = (bf16[512,512]{1,0:T(8,128)(2,1)}, bf16[512,512]{1,0:T(8,128)(2,1)}, u32[]{:S(2)}, u32[]{:S(2)}) collective-permute-start(bf16[512,512]{1,0:T(8,128)(2,1)} %get-tuple-element.72), channel_id=1, source_target_pairs={{0,1},{1,0},{2,3},{3,2},{4,5},{5,4},{6,7},{7,6},{8,9},{9,8},{10,11... | collective-permute-start | bytes 1572872 | tf_op jit(solution)/shard_map/ppermute | solution.py:29
  145.8 30.8 %collective-permute-start.39 = (bf16[256,2048]{1,0:T(8,128)(2,1)S(1)}, bf16[256,2048]{1,0:T(8,128)(2,1)S(1)}, u32[]{:S(2)}, u32[]{:S(2)}) collective-permute-start(bf16[256,2048]{1,0:T(8,128)(2,1)S(1)} %get-tuple-element.88), channel_id=1, source_target_pairs={{0,8},{4,12},{8,0},{12,4},{16,24},{20,28},{24,16},{28,20},{1,9},{5... | collective-permute-start | bytes 3145736 | tf_op jit(solution)/shard_map/ppermute | solution.py:29
  147.3 29.4 %collective-permute-start.40 = (bf16[256,2048]{1,0:T(8,128)(2,1)S(1)}, bf16[256,2048]{1,0:T(8,128)(2,1)S(1)}, u32[]{:S(2)}, u32[]{:S(2)}) collective-permute-start(bf16[256,2048]{1,0:T(8,128)(2,1)S(1)} %get-tuple-element.87), channel_id=1, source_target_pairs={{0,16},{4,20},{8,24},{12,28},{16,0},{20,4},{24,8},{28,12},{1,17},{... | collective-permute-start | bytes 3145736 | tf_op jit(solution)/shard_map/ppermute | solution.py:29
  147.8 28.8 %collective-permute-start.43 = (bf16[256,2048]{1,0:T(8,128)(2,1)S(1)}, bf16[256,2048]{1,0:T(8,128)(2,1)S(1)}, u32[]{:S(2)}, u32[]{:S(2)}) collective-permute-start(bf16[256,2048]{1,0:T(8,128)(2,1)S(1)} %copy-done.19), channel_id=1, source_target_pairs={{0,4},{4,0},{8,12},{12,8},{16,20},{20,16},{24,28},{28,24},{1,5},{5... | collective-permute-start | bytes 3145736 | tf_op jit(solution)/shard_map/ppermute | solution.py:29
  147.8 24.4 %collective-permute-start.41 = (bf16[512,512]{1,0:T(8,128)(2,1)S(1)}, bf16[512,512]{1,0:T(8,128)(2,1)S(1)}, u32[]{:S(2)}, u32[]{:S(2)}) collective-permute-start(bf16[512,512]{1,0:T(8,128)(2,1)S(1)} %slice_bitcast_fusion.2), channel_id=1, source_target_pairs={{0,1},{1,0},{2,3},{3,2},{4,5},{5,4},{6,7},{7,6},{8,9},{9,8},{10,11... | collective-permute-start | bytes 1572872 | tf_op jit(solution)/shard_map/ppermute | solution.py:29
  149.4 26.2 %collective-permute-start.42 = (bf16[512,512]{1,0:T(8,128)(2,1)S(1)}, bf16[512,512]{1,0:T(8,128)(2,1)S(1)}, u32[]{:S(2)}, u32[]{:S(2)}) collective-permute-start(bf16[512,512]{1,0:T(8,128)(2,1)S(1)} %fusion.6), channel_id=1, source_target_pairs={{0,2},{1,3},{2,0},{3,1},{4,6},{5,7},{6,4},{7,5},{8,10},{9,11},{10,... | collective-permute-start | bytes 1572872 | tf_op jit(solution)/shard_map/ppermute | solution.py:29
  (17 other events, 144.2 us)

commit v11 on v10

--- a/solution.py
+++ b/solution.py
@@ -68,7 +68,7 @@
     return pltpu.with_memory_space_constraint(value, pltpu.VMEM)
 
 
-def call(kernel, outputs, operands, scratch=(), extra=(), aliases=None, slow=(), limit=16):
+def call(kernel, outputs, operands, scratch=(), extra=(), slow=(), limit=16):
     spec = pl.BlockSpec(memory_space=pltpu.VMEM)
     return pl.pallas_call(
         kernel,
@@ -79,7 +79,6 @@
         in_specs=[spec] * len(operands) + [pl.BlockSpec(memory_space=pl.ANY)] * len(extra),
         out_specs=tuple(pl.BlockSpec(memory_space=pl.ANY) if i in slow else spec for i in range(len(outputs))),
         scratch_shapes=list(scratch),
-        input_output_aliases=aliases or {},
         compiler_params=pltpu.CompilerParams(vmem_limit_bytes=limit << 20),
         cost_estimate=pl.CostEstimate(flops=1, bytes_accessed=1, transcendentals=0),
     )(*[fast(operand) for operand in operands], *extra)
@@ -287,7 +286,6 @@
         [((rows, classes), f32), ((rows, classes), bf16), ((2, rows), f32)],
         [logits, blocks] + [part for _, part in late],
         [pltpu.VMEM((2, rows, tile), f32), pltpu.VMEM((rows, LANES), f32), pltpu.VMEM((rows, LANES), f32)],
-        aliases={0: 0},
     )
     (turned,) = call(turn_kernel, [((groups, width, rows), bf16)], [blocks])
 

time: 179 us -> 177 us (0.989)
  no operation moved by 1% of the time
where the time goes in v11:
time: 177 us; the launch traced here: 176 us
  waiting for transfers between devices  83.9 us (47%)
  starting transfers between devices  46.3 us (26%)
  Pallas kernels  28.2 us (16%)
  other arithmetic  9.01 us (5%)
  local copies, waits for them, and re-layouts  7.75 us (4%)
    ppermute x42, waiting for transfers between devices, flip(): lax.ppermute(value, axis, [(i, i ^ mask) for i in range(lax.axis_size(axi...  83.9 us
    ppermute x42, starting transfers between devices, flip(): lax.ppermute(value, axis, [(i, i ^ mask) for i in range(lax.axis_size(axi...  45.2 us
    pallas_call x12, Pallas kernels, call(): pl.pallas_call(kernel, out_shape=tuple((jax.ShapeDtypeStruct(shape, dtype...  28.2 us
    unnamed x42, local copies, waits for them, and re-layouts  7.7 us
  transfers between devices with their start and end apart: 44, of which 26 were waited for; matrix products, arithmetic and copies ran while one was open for 1% of the time, Pallas kernels for 9%

profile of v11, /device:TPU:0, one launch (start us, length us, event | category | flops | bytes accessed | tf_op | source)
XLA Modules:
  0.0 176.2 jit_solution(11406462842677937385)
XLA Ops:
  0.6 3.0 %collective-permute-start.4 = (bf16[256,2048]{1,0:T(8,128)(2,1)}, bf16[256,2048]{1,0:T(8,128)(2,1)S(1)}, u32[]{:S(2)}, u32[]{:S(2)}) collective-permute-start(bf16[256,2048]{1,0:T(8,128)(2,1)} %refs_0_.5), channel_id=1, source_target_pairs={{0,8},{4,12},{8,0},{12,4},{16,24},{20,28},{24,16},{28,20},{1,9},{5... | collective-permute-start | bytes 3145736 | tf_op jit(solution)/shard_map/ppermute | solution.py:29
  3.6 1.5 collective-permute-start.5
  5.2 2.6 %collective-permute-start.1 = (bf16[512,512]{1,0:T(8,128)(2,1)}, bf16[512,512]{1,0:T(8,128)(2,1)}, u32[]{:S(2)}, u32[]{:S(2)}) collective-permute-start(bf16[512,512]{1,0:T(8,128)(2,1)} %refs_0_.3), channel_id=1, source_target_pairs={{0,2},{1,3},{2,0},{3,1},{4,6},{5,7},{6,4},{7,5},{8,10},{9,11},{10,... | collective-permute-start | bytes 1572872 | tf_op jit(solution)/shard_map/ppermute | solution.py:29
  7.8 1.6 collective-permute-start
  9.3 21.5 %collective-permute-done.1.refs_2_ = bf16[512,512]{1,0:T(8,128)(2,1)} collective-permute-done((bf16[512,512]{1,0:T(8,128)(2,1)}, bf16[512,512]{1,0:T(8,128)(2,1)}, u32[]{:S(2)}, u32[]{:S(2)}) %collective-permute-start.1) | collective-permute-done | bytes 524320 | tf_op jit(solution)/shard_map/ppermute | solution.py:29
  31.5 1.1 collective-permute-done.refs_1_
  33.0 13.5 %collective-permute-done.2.refs_3_ = bf16[512,512]{1,0:T(8,128)(2,1)S(1)} collective-permute-done((bf16[512,512]{1,0:T(8,128)(2,1)}, bf16[512,512]{1,0:T(8,128)(2,1)S(1)}, u32[]{:S(2)}, u32[]{:S(2)}) %collective-permute-start.2) | collective-permute-done | bytes 524320 | tf_op jit(solution)/shard_map/ppermute | solution.py:29
  46.6 5.8 %shard_map.58 = (bf16[4,512,512]{2,1,0:T(8,128)(2,1)S(1)}, f32[512,2048]{1,0:T(8,128)S(1)}) custom-call(bf16[512,512]{1,0:T(8,128)(2,1)S(1)} %copy-done.17, bf16[512,512]{1,0:T(8,128)(2,1)} %collective-permute-done.refs_1_, bf16[512,512]{1,0:T(8,128)(2,1)} %collective-permute-done.1.refs_2_, bf16[512,512]{1,0:T(8,128)(2,1)S(1)} %collective-permute-done.2.refs_3_, ...), custom_call_target="tpu_custom_call" | custom-call | flops 1 | bytes 1 | tf_op jit(solution)/shard_map/pallas_call | solution.py:73
  52.5 2.6 %collective-permute-done.9.refs_1_.refs_7_ = bf16[256,2048]{1,0:T(8,128)(2,1)S(1)} collective-permute-done((bf16[256,2048]{1,0:T(8,128)(2,1)S(1)}, bf16[256,2048]{1,0:T(8,128)(2,1)S(1)}, u32[]{:S(2)}, u32[]{:S(2)}) %collective-permute-start.9) | collective-permute-done | bytes 1048608 | tf_op jit(solution)/shard_map/ppermute | solution.py:29
  55.2 2.5 %shard_map.59 = (f32[512,2048]{1,0:T(8,128)S(1)}, bf16[512,2048]{1,0:T(8,128)(2,1)S(1)}, f32[2,512]{1,0:T(2,128)S(1)}) custom-call(f32[512,2048]{1,0:T(8,128)S(1)} %get-tuple-element.47.logits_ref, bf16[4,512,512]{2,1,0:T(8,128)(2,1)S(1)} %get-tuple-element.48.blocks_ref, bf16[256,2048]{1,0:T(8,128)(2,1)S(1)} %collective-permute-done.8.refs_0_.refs_6_, ...), custom_call_target="tpu_custom_call" | custom-call | flops 1 | bytes 1 | tf_op jit(solution)/shard_map/pallas_call | solution.py:73
  57.7 2.9 %collective-permute-start.10 = (f32[2,512]{1,0:T(2,128)S(1)}, f32[2,512]{1,0:T(2,128)S(1)}, u32[]{:S(2)}, u32[]{:S(2)}) collective-permute-start(f32[2,512]{1,0:T(2,128)S(1)} %get-tuple-element.53), channel_id=1, source_target_pairs={{0,3},{1,2},{2,1},{3,0},{4,7},{5,6},{6,5},{7,4},{8,11},{9,10},{10,... | collective-permute-start | bytes 12296 | tf_op jit(solution)/shard_map/ppermute | solution.py:29
  60.6 1.5 collective-permute-start.12
  63.1 1.9 %collective-permute-done.11 = f32[2,512]{1,0:T(2,128)S(1)} collective-permute-done((f32[2,512]{1,0:T(2,128)S(1)}, f32[2,512]{1,0:T(2,128)S(1)}, u32[]{:S(2)}, u32[]{:S(2)}) %collective-permute-start.11) | collective-permute-done | bytes 4128 | tf_op jit(solution)/shard_map/ppermute | solution.py:29
  65.9 1.2 collective-permute-done.13
  67.1 1.5 collective-permute-start.14
  68.6 1.5 collective-permute-start.15
  72.2 1.5 collective-permute-done.16
  74.4 1.5 collective-permute-start.17
  76.5 2.3 %collective-permute-start.19 = (f32[1,512]{1,0:T(1,128)S(1)}, f32[1,512]{1,0:T(1,128)S(1)}, u32[]{:S(2)}, u32[]{:S(2)}) collective-permute-start(f32[1,512]{1,0:T(1,128)S(1)} %get-tuple-element.55), channel_id=1, source_target_pairs={{0,1},{1,0},{2,3},{3,2},{4,5},{5,4},{6,7},{7,6},{8,9},{9,8},{10,11... | collective-permute-start | bytes 6152 | tf_op jit(solution)/shard_map/ppermute | solution.py:29
  81.2 1.2 collective-permute-done.20
  82.9 1.5 collective-permute-start.22
  84.4 1.5 collective-permute-start.23
  88.7 2.6 %collective-permute-start.24 = (f32[1,512]{1,0:T(1,128)S(1)}, f32[1,512]{1,0:T(1,128)S(1)}, u32[]{:S(2)}, u32[]{:S(2)}) collective-permute-start(f32[1,512]{1,0:T(1,128)S(1)} %get-tuple-element.57), channel_id=1, source_target_pairs={{0,3},{1,2},{2,1},{3,0},{4,7},{5,6},{6,5},{7,4},{8,11},{9,10},{10,... | collective-permute-start | bytes 6152 | tf_op jit(solution)/shard_map/ppermute | solution.py:29
  94.2 1.7 collective-permute-done.25
  96.6 1.2 collective-permute-done.27
  97.8 1.5 collective-permute-start.28
  99.3 1.5 collective-permute-start.29
  102.9 1.5 collective-permute-done.30
  105.1 1.5 collective-permute-start.31
  107.5 2.0 %collective-permute-start.33 = (f32[1,512]{1,0:T(1,128)S(1)}, f32[1,512]{1,0:T(1,128)S(1)}, u32[]{:S(2)}, u32[]{:S(2)}) collective-permute-start(f32[1,512]{1,0:T(1,128)S(1)} %get-tuple-element.59), channel_id=1, source_target_pairs={{0,1},{1,0},{2,3},{3,2},{4,5},{5,4},{6,7},{7,6},{8,9},{9,8},{10,11... | collective-permute-start | bytes 6152 | tf_op jit(solution)/shard_map/ppermute | solution.py:29
  111.2 6.1 %shard_map.67 = (bf16[512,2048]{1,0:T(8,128)(2,1)}, bf16[512,2048]{1,0:T(8,128)(2,1)S(1)}, bf16[256,2048]{1,0:T(8,128)(2,1)S(1)}, bf16[256,2048]{1,0:T(8,128)(2,1)S(1)}, bf16[512,512]{1,0:T(8,128)(2,1)}) custom-call(f32[512,2048]{1,0:T(8,128)S(1)} %get-tuple-element.51.student_ref, bf16[512,2048]{1,0:T(8,128)(2,1)S(1)} %get-tuple-element.52.slope_ref, ...), custom_call_target="tpu_custom_call" | custom-call | flops 1 | bytes 1 | tf_op jit(solution)/shard_map/pallas_call | solution.py:73
  117.3 3.4 %shard_map.68 = (bf16[256,2048]{1,0:T(8,128)(2,1)S(1)}, bf16[256,2048]{1,0:T(8,128)(2,1)}, bf16[256,2048]{1,0:T(8,128)(2,1)S(1)}, bf16[256,2048]{1,0:T(8,128)(2,...) custom-call(bf16[512,2048]{1,0:T(8,128)(2,1)S(1)} %get-tuple-element.62.grad_ref, ...), custom_call_target="tpu_custom_call" | custom-call | flops 1 | bytes 1 | tf_op jit(solution)/shard_map/pallas_call | solution.py:73
  121.8 1.7 add_convert_fusion.1.refs_8_
  124.5 2.0 %collective-permute-start.35 = (bf16[512,512]{1,0:T(8,128)(2,1)}, bf16[512,512]{1,0:T(8,128)(2,1)}, u32[]{:S(2)}, u32[]{:S(2)}) collective-permute-start(bf16[512,512]{1,0:T(8,128)(2,1)} %get-tuple-element.72), channel_id=1, source_target_pairs={{0,1},{1,0},{2,3},{3,2},{4,5},{5,4},{6,7},{7,6},{8,9},{9,8},{10,11... | collective-permute-start | bytes 1572872 | tf_op jit(solution)/shard_map/ppermute | solution.py:29
  126.5 1.2 copy-done.2
  127.8 1.2 copy-done.4
  129.0 1.2 copy-done.6
  130.2 1.2 copy-done.8
  131.4 1.6 copy-done.10
  133.0 5.9 %shard_map.69 = bf16[4,512,512]{2,1,0:T(8,128)(2,1)S(1)} custom-call(bf16[512,2048]{1,0:T(8,128)(2,1)S(1)} %copy-done.10, bf16[256,2048]{1,0:T(8,128)(2,1)S(1)} %copy-done, bf16[256,2048]{1,0:T(8,128)(2,1)} %collective-permute-done.3.refs_5_.refs_1_, bf16[256,2048]{1,0:T(8,128)(2,1)S(1)} %collective-permute-done.4.refs_6_.refs_2_, ...), custom_call_target="tpu_custom_call" | custom-call | flops 1 | bytes 1 | tf_op jit(solution)/shard_map/pallas_call | solution.py:73
  139.1 1.3 fusion.6
  140.6 3.1 %fusion.3 = (bf16[256,2048]{1,0:T(8,128)(2,1)S(1)}, bf16[256,2048]{1,0:T(8,128)(2,1)S(1)}) fusion(bf16[256,2048]{1,0:T(8,128)(2,1)} %collective-permute-done.38, bf16[256,2048]{1,0:T(8,128)(2,1)} %collective-permute-done.37, bf16[256,2048]{1,0:T(8,128)(2,1)S(1)} %copy-done.16, pred[]{:T(512)S(6)} %eq.11, pred[]{:T(512)S(6)} %eq.12, ...), kind=kLoop, calls=%fused_computation.5 | loop fusion | flops 6815744 | bytes 7340034 | tf_op jit(solution)/shard_map/convert_element_type | solution.py:375
  143.7 1.5 collective-permute-start.39
  145.7 1.6 collective-permute-start.41
  147.3 1.1 collective-permute-start.42
  148.4 21.7 %collective-permute-done.41 = bf16[512,512]{1,0:T(8,128)(2,1)S(1)} collective-permute-done((bf16[512,512]{1,0:T(8,128)(2,1)S(1)}, bf16[512,512]{1,0:T(8,128)(2,1)S(1)}, u32[]{:S(2)}, u32[]{:S(2)}) %collective-permute-start.41) | collective-permute-done | bytes 524320 | tf_op jit(solution)/shard_map/ppermute | solution.py:29
  170.2 3.4 %collective-permute-done.42 = bf16[512,512]{1,0:T(8,128)(2,1)S(1)} collective-permute-done((bf16[512,512]{1,0:T(8,128)(2,1)S(1)}, bf16[512,512]{1,0:T(8,128)(2,1)S(1)}, u32[]{:S(2)}, u32[]{:S(2)}) %collective-permute-start.42) | collective-permute-done | bytes 524320 | tf_op jit(solution)/shard_map/ppermute | solution.py:29
  174.6 1.7 add_convert_fusion
  (128 shorter events, 25.0 us)
Async XLA Ops:
  0.6 30.2 %collective-permute-start.4 = (bf16[256,2048]{1,0:T(8,128)(2,1)}, bf16[256,2048]{1,0:T(8,128)(2,1)S(1)}, u32[]{:S(2)}, u32[]{:S(2)}) collective-permute-start(bf16[256,2048]{1,0:T(8,128)(2,1)} %refs_0_.5), channel_id=1, source_target_pairs={{0,8},{4,12},{8,0},{12,4},{16,24},{20,28},{24,16},{28,20},{1,9},{5... | collective-permute-start | bytes 3145736 | tf_op jit(solution)/shard_map/ppermute | solution.py:29
  3.6 27.2 %collective-permute-start.5 = (bf16[256,2048]{1,0:T(8,128)(2,1)}, bf16[256,2048]{1,0:T(8,128)(2,1)S(1)}, u32[]{:S(2)}, u32[]{:S(2)}) collective-permute-start(bf16[256,2048]{1,0:T(8,128)(2,1)} %refs_0_.5), channel_id=1, source_target_pairs={{0,16},{4,20},{8,24},{12,28},{16,0},{20,4},{24,8},{28,12},{1,17},{... | collective-permute-start | bytes 3145736 | tf_op jit(solution)/shard_map/ppermute | solution.py:29
  5.2 25.7 %collective-permute-start.1 = (bf16[512,512]{1,0:T(8,128)(2,1)}, bf16[512,512]{1,0:T(8,128)(2,1)}, u32[]{:S(2)}, u32[]{:S(2)}) collective-permute-start(bf16[512,512]{1,0:T(8,128)(2,1)} %refs_0_.3), channel_id=1, source_target_pairs={{0,2},{1,3},{2,0},{3,1},{4,6},{5,7},{6,4},{7,5},{8,10},{9,11},{10,... | collective-permute-start | bytes 1572872 | tf_op jit(solution)/shard_map/ppermute | solution.py:29
  7.8 24.8 %collective-permute-start.3 = (bf16[256,2048]{1,0:T(8,128)(2,1)}, bf16[256,2048]{1,0:T(8,128)(2,1)}, u32[]{:S(2)}, u32[]{:S(2)}) collective-permute-start(bf16[256,2048]{1,0:T(8,128)(2,1)} %refs_0_.5), channel_id=1, source_target_pairs={{0,4},{4,0},{8,12},{12,8},{16,20},{20,16},{24,28},{28,24},{1,5},{5... | collective-permute-start | bytes 3145736 | tf_op jit(solution)/shard_map/ppermute | solution.py:29
  7.8 24.8 %collective-permute-start = (bf16[512,512]{1,0:T(8,128)(2,1)}, bf16[512,512]{1,0:T(8,128)(2,1)}, u32[]{:S(2)}, u32[]{:S(2)}) collective-permute-start(bf16[512,512]{1,0:T(8,128)(2,1)} %refs_0_.3), channel_id=1, source_target_pairs={{0,1},{1,0},{2,3},{3,2},{4,5},{5,4},{6,7},{7,6},{8,9},{9,8},{10,11... | collective-permute-start | bytes 1572872 | tf_op jit(solution)/shard_map/ppermute | solution.py:29
  30.8 15.7 %collective-permute-start.6 = (bf16[256,2048]{1,0:T(8,128)(2,1)S(1)}, bf16[256,2048]{1,0:T(8,128)(2,1)S(1)}, u32[]{:S(2)}, u32[]{:S(2)}) collective-permute-start(bf16[256,2048]{1,0:T(8,128)(2,1)S(1)} %collective-permute-done.4.refs_6_.refs_2_), channel_id=1, source_target_pairs={{0,4},{4,0},{8,12},{12,8},{16,20},{20,16},{24,28},{28,24},{1,5},{5... | collective-permute-start | bytes 3145736 | tf_op jit(solution)/shard_map/ppermute | solution.py:29
  30.8 15.7 %collective-permute-start.7 = (bf16[256,2048]{1,0:T(8,128)(2,1)S(1)}, bf16[256,2048]{1,0:T(8,128)(2,1)S(1)}, u32[]{:S(2)}, u32[]{:S(2)}) collective-permute-start(bf16[256,2048]{1,0:T(8,128)(2,1)S(1)} %collective-permute-done.5.refs_8_.refs_4_), channel_id=1, source_target_pairs={{0,4},{4,0},{8,12},{12,8},{16,20},{20,16},{24,28},{28,24},{1,5},{5... | collective-permute-start | bytes 3145736 | tf_op jit(solution)/shard_map/ppermute | solution.py:29
  32.5 19.9 %collective-permute-start.8 = (bf16[256,2048]{1,0:T(8,128)(2,1)S(1)}, bf16[256,2048]{1,0:T(8,128)(2,1)S(1)}, u32[]{:S(2)}, u32[]{:S(2)}) collective-permute-start(bf16[256,2048]{1,0:T(8,128)(2,1)S(1)} %broadcast_select_fusion), channel_id=1, source_target_pairs={{0,16},{4,12},{8,24},{12,4},{16,0},{20,28},{24,8},{28,20},{1,17},{... | collective-permute-start | bytes 3145736 | tf_op jit(solution)/shard_map/ppermute | solution.py:34
  33.0 13.5 %collective-permute-start.2 = (bf16[512,512]{1,0:T(8,128)(2,1)}, bf16[512,512]{1,0:T(8,128)(2,1)S(1)}, u32[]{:S(2)}, u32[]{:S(2)}) collective-permute-start(bf16[512,512]{1,0:T(8,128)(2,1)} %collective-permute-done.1.refs_2_), channel_id=1, source_target_pairs={{0,1},{1,0},{2,3},{3,2},{4,5},{5,4},{6,7},{7,6},{8,9},{9,8},{10,11... | collective-permute-start | bytes 1572872 | tf_op jit(solution)/shard_map/ppermute | solution.py:29
  46.6 64.6 %copy-start.1 = (bf16[256,2048]{1,0:T(8,128)(2,1)}, bf16[256,2048]{1,0:T(8,128)(2,1)S(1)}, u32[]{:S(2)}) copy-start(bf16[256,2048]{1,0:T(8,128)(2,1)S(1)} %collective-permute-done.6.refs_7_.refs_3_) | copy-start | bytes 3145732
  46.6 64.5 %copy-start.3 = (bf16[256,2048]{1,0:T(8,128)(2,1)}, bf16[256,2048]{1,0:T(8,128)(2,1)S(1)}, u32[]{:S(2)}) copy-start(bf16[256,2048]{1,0:T(8,128)(2,1)S(1)} %collective-permute-done.7.refs_9_.refs_5_) | copy-start | bytes 3145732
  52.5 58.7 %copy-start.5 = (bf16[256,2048]{1,0:T(8,128)(2,1)}, bf16[256,2048]{1,0:T(8,128)(2,1)S(1)}, u32[]{:S(2)}) copy-start(bf16[256,2048]{1,0:T(8,128)(2,1)S(1)} %collective-permute-done.8.refs_0_.refs_6_) | copy-start | bytes 3145732
  52.5 2.7 %collective-permute-start.9 = (bf16[256,2048]{1,0:T(8,128)(2,1)S(1)}, bf16[256,2048]{1,0:T(8,128)(2,1)S(1)}, u32[]{:S(2)}, u32[]{:S(2)}) collective-permute-start(bf16[256,2048]{1,0:T(8,128)(2,1)S(1)} %collective-permute-done.8.refs_0_.refs_6_), channel_id=1, source_target_pairs={{0,4},{4,0},{8,12},{12,8},{16,20},{20,16},{24,28},{28,24},{1,5},{5... | collective-permute-start | bytes 3145736 | tf_op jit(solution)/shard_map/ppermute | solution.py:29
  55.2 56.0 %copy-start.7 = (bf16[256,2048]{1,0:T(8,128)(2,1)}, bf16[256,2048]{1,0:T(8,128)(2,1)S(1)}, u32[]{:S(2)}) copy-start(bf16[256,2048]{1,0:T(8,128)(2,1)S(1)} %collective-permute-done.9.refs_1_.refs_7_) | copy-start | bytes 3145732
  57.7 5.5 %collective-permute-start.10 = (f32[2,512]{1,0:T(2,128)S(1)}, f32[2,512]{1,0:T(2,128)S(1)}, u32[]{:S(2)}, u32[]{:S(2)}) collective-permute-start(f32[2,512]{1,0:T(2,128)S(1)} %get-tuple-element.53), channel_id=1, source_target_pairs={{0,3},{1,2},{2,1},{3,0},{4,7},{5,6},{6,5},{7,4},{8,11},{9,10},{10,... | collective-permute-start | bytes 12296 | tf_op jit(solution)/shard_map/ppermute | solution.py:29
  60.6 4.5 %collective-permute-start.11 = (f32[2,512]{1,0:T(2,128)S(1)}, f32[2,512]{1,0:T(2,128)S(1)}, u32[]{:S(2)}, u32[]{:S(2)}) collective-permute-start(f32[2,512]{1,0:T(2,128)S(1)} %get-tuple-element.53), channel_id=1, source_target_pairs={{0,2},{1,3},{2,0},{3,1},{4,6},{5,7},{6,4},{7,5},{8,10},{9,11},{10,... | collective-permute-start | bytes 12296 | tf_op jit(solution)/shard_map/ppermute | solution.py:29
  60.6 4.5 %collective-permute-start.12 = (f32[2,512]{1,0:T(2,128)S(1)}, f32[2,512]{1,0:T(2,128)S(1)}, u32[]{:S(2)}, u32[]{:S(2)}) collective-permute-start(f32[2,512]{1,0:T(2,128)S(1)} %get-tuple-element.53), channel_id=1, source_target_pairs={{0,1},{1,0},{2,3},{3,2},{4,5},{5,4},{6,7},{7,6},{8,9},{9,8},{10,11... | collective-permute-start | bytes 12296 | tf_op jit(solution)/shard_map/ppermute | solution.py:29
  65.8 1.2 collective-permute-start.13
  67.1 4.6 %collective-permute-start.14 = (f32[1,2048]{1,0:T(1,128)S(1)}, f32[1,2048]{1,0:T(1,128)S(1)}, u32[]{:S(2)}, u32[]{:S(2)}) collective-permute-start(f32[1,2048]{1,0:T(1,128)S(1)} %add.114), channel_id=1, source_target_pairs={{0,24},{4,28},{8,16},{12,20},{16,8},{20,12},{24,0},{28,4},{1,25},{... | collective-permute-start | bytes 24584 | tf_op jit(solution)/shard_map/ppermute | solution.py:29
  68.6 3.7 %collective-permute-start.15 = (f32[1,2048]{1,0:T(1,128)S(1)}, f32[1,2048]{1,0:T(1,128)S(1)}, u32[]{:S(2)}, u32[]{:S(2)}) collective-permute-start(f32[1,2048]{1,0:T(1,128)S(1)} %add.114), channel_id=1, source_target_pairs={{0,16},{4,20},{8,24},{12,28},{16,0},{20,4},{24,8},{28,12},{1,17},{... | collective-permute-start | bytes 24584 | tf_op jit(solution)/shard_map/ppermute | solution.py:29
  70.1 3.7 %collective-permute-start.16 = (f32[1,2048]{1,0:T(1,128)S(1)}, f32[1,2048]{1,0:T(1,128)S(1)}, u32[]{:S(2)}, u32[]{:S(2)}) collective-permute-start(f32[1,2048]{1,0:T(1,128)S(1)} %add.114), channel_id=1, source_target_pairs={{0,8},{4,12},{8,0},{12,4},{16,24},{20,28},{24,16},{28,20},{1,9},{5... | collective-permute-start | bytes 24584 | tf_op jit(solution)/shard_map/ppermute | solution.py:29
  74.4 5.4 %collective-permute-start.17 = (f32[1,512]{1,0:T(1,128)S(1)}, f32[1,512]{1,0:T(1,128)S(1)}, u32[]{:S(2)}, u32[]{:S(2)}) collective-permute-start(f32[1,512]{1,0:T(1,128)S(1)} %get-tuple-element.55), channel_id=1, source_target_pairs={{0,3},{1,2},{2,1},{3,0},{4,7},{5,6},{6,5},{7,4},{8,11},{9,10},{10,... | collective-permute-start | bytes 6152 | tf_op jit(solution)/shard_map/ppermute | solution.py:29
  75.9 4.5 %collective-permute-start.18 = (f32[1,512]{1,0:T(1,128)S(1)}, f32[1,512]{1,0:T(1,128)S(1)}, u32[]{:S(2)}, u32[]{:S(2)}) collective-permute-start(f32[1,512]{1,0:T(1,128)S(1)} %get-tuple-element.55), channel_id=1, source_target_pairs={{0,2},{1,3},{2,0},{3,1},{4,6},{5,7},{6,4},{7,5},{8,10},{9,11},{10,... | collective-permute-start | bytes 6152 | tf_op jit(solution)/shard_map/ppermute | solution.py:29
  76.5 3.9 %collective-permute-start.19 = (f32[1,512]{1,0:T(1,128)S(1)}, f32[1,512]{1,0:T(1,128)S(1)}, u32[]{:S(2)}, u32[]{:S(2)}) collective-permute-start(f32[1,512]{1,0:T(1,128)S(1)} %get-tuple-element.55), channel_id=1, source_target_pairs={{0,1},{1,0},{2,3},{3,2},{4,5},{5,4},{6,7},{7,6},{8,9},{9,8},{10,11... | collective-permute-start | bytes 6152 | tf_op jit(solution)/shard_map/ppermute | solution.py:29
  81.1 1.2 collective-permute-start.20
  82.3 4.6 %collective-permute-start.21 = (f32[1,2048]{1,0:T(1,128)S(1)}, f32[1,2048]{1,0:T(1,128)S(1)}, u32[]{:S(2)}, u32[]{:S(2)}) collective-permute-start(f32[1,2048]{1,0:T(1,128)S(1)} %add.121), channel_id=1, source_target_pairs={{0,24},{4,28},{8,16},{12,20},{16,8},{20,12},{24,0},{28,4},{1,25},{... | collective-permute-start | bytes 24584 | tf_op jit(solution)/shard_map/ppermute | solution.py:29
  82.9 4.1 %collective-permute-start.22 = (f32[1,2048]{1,0:T(1,128)S(1)}, f32[1,2048]{1,0:T(1,128)S(1)}, u32[]{:S(2)}, u32[]{:S(2)}) collective-permute-start(f32[1,2048]{1,0:T(1,128)S(1)} %add.121), channel_id=1, source_target_pairs={{0,16},{4,20},{8,24},{12,28},{16,0},{20,4},{24,8},{28,12},{1,17},{... | collective-permute-start | bytes 24584 | tf_op jit(solution)/shard_map/ppermute | solution.py:29
  84.4 3.7 %collective-permute-start.23 = (f32[1,2048]{1,0:T(1,128)S(1)}, f32[1,2048]{1,0:T(1,128)S(1)}, u32[]{:S(2)}, u32[]{:S(2)}) collective-permute-start(f32[1,2048]{1,0:T(1,128)S(1)} %add.121), channel_id=1, source_target_pairs={{0,8},{4,12},{8,0},{12,4},{16,24},{20,28},{24,16},{28,20},{1,9},{5... | collective-permute-start | bytes 24584 | tf_op jit(solution)/shard_map/ppermute | solution.py:29
  88.7 5.4 %collective-permute-start.24 = (f32[1,512]{1,0:T(1,128)S(1)}, f32[1,512]{1,0:T(1,128)S(1)}, u32[]{:S(2)}, u32[]{:S(2)}) collective-permute-start(f32[1,512]{1,0:T(1,128)S(1)} %get-tuple-element.57), channel_id=1, source_target_pairs={{0,3},{1,2},{2,1},{3,0},{4,7},{5,6},{6,5},{7,4},{8,11},{9,10},{10,... | collective-permute-start | bytes 6152 | tf_op jit(solution)/shard_map/ppermute | solution.py:29
  91.3 4.5 %collective-permute-start.25 = (f32[1,512]{1,0:T(1,128)S(1)}, f32[1,512]{1,0:T(1,128)S(1)}, u32[]{:S(2)}, u32[]{:S(2)}) collective-permute-start(f32[1,512]{1,0:T(1,128)S(1)} %get-tuple-element.57), channel_id=1, source_target_pairs={{0,2},{1,3},{2,0},{3,1},{4,6},{5,7},{6,4},{7,5},{8,10},{9,11},{10,... | collective-permute-start | bytes 6152 | tf_op jit(solution)/shard_map/ppermute | solution.py:29
  92.3 3.6 %collective-permute-start.26 = (f32[1,512]{1,0:T(1,128)S(1)}, f32[1,512]{1,0:T(1,128)S(1)}, u32[]{:S(2)}, u32[]{:S(2)}) collective-permute-start(f32[1,512]{1,0:T(1,128)S(1)} %get-tuple-element.57), channel_id=1, source_target_pairs={{0,1},{1,0},{2,3},{3,2},{4,5},{5,4},{6,7},{7,6},{8,9},{9,8},{10,11... | collective-permute-start | bytes 6152 | tf_op jit(solution)/shard_map/ppermute | solution.py:29
  96.5 1.2 collective-permute-start.27
  97.8 4.6 %collective-permute-start.28 = (f32[1,2048]{1,0:T(1,128)S(1)}, f32[1,2048]{1,0:T(1,128)S(1)}, u32[]{:S(2)}, u32[]{:S(2)}) collective-permute-start(f32[1,2048]{1,0:T(1,128)S(1)} %add.128), channel_id=1, source_target_pairs={{0,24},{4,28},{8,16},{12,20},{16,8},{20,12},{24,0},{28,4},{1,25},{... | collective-permute-start | bytes 24584 | tf_op jit(solution)/shard_map/ppermute | solution.py:29
  99.3 3.7 %collective-permute-start.29 = (f32[1,2048]{1,0:T(1,128)S(1)}, f32[1,2048]{1,0:T(1,128)S(1)}, u32[]{:S(2)}, u32[]{:S(2)}) collective-permute-start(f32[1,2048]{1,0:T(1,128)S(1)} %add.128), channel_id=1, source_target_pairs={{0,16},{4,20},{8,24},{12,28},{16,0},{20,4},{24,8},{28,12},{1,17},{... | collective-permute-start | bytes 24584 | tf_op jit(solution)/shard_map/ppermute | solution.py:29
  100.8 3.7 %collective-permute-start.30 = (f32[1,2048]{1,0:T(1,128)S(1)}, f32[1,2048]{1,0:T(1,128)S(1)}, u32[]{:S(2)}, u32[]{:S(2)}) collective-permute-start(f32[1,2048]{1,0:T(1,128)S(1)} %add.128), channel_id=1, source_target_pairs={{0,8},{4,12},{8,0},{12,4},{16,24},{20,28},{24,16},{28,20},{1,9},{5... | collective-permute-start | bytes 24584 | tf_op jit(solution)/shard_map/ppermute | solution.py:29
  105.1 5.4 %collective-permute-start.31 = (f32[1,512]{1,0:T(1,128)S(1)}, f32[1,512]{1,0:T(1,128)S(1)}, u32[]{:S(2)}, u32[]{:S(2)}) collective-permute-start(f32[1,512]{1,0:T(1,128)S(1)} %get-tuple-element.59), channel_id=1, source_target_pairs={{0,3},{1,2},{2,1},{3,0},{4,7},{5,6},{6,5},{7,4},{8,11},{9,10},{10,... | collective-permute-start | bytes 6152 | tf_op jit(solution)/shard_map/ppermute | solution.py:29
  106.6 4.5 %collective-permute-start.32 = (f32[1,512]{1,0:T(1,128)S(1)}, f32[1,512]{1,0:T(1,128)S(1)}, u32[]{:S(2)}, u32[]{:S(2)}) collective-permute-start(f32[1,512]{1,0:T(1,128)S(1)} %get-tuple-element.59), channel_id=1, source_target_pairs={{0,2},{1,3},{2,0},{3,1},{4,6},{5,7},{6,4},{7,5},{8,10},{9,11},{10,... | collective-permute-start | bytes 6152 | tf_op jit(solution)/shard_map/ppermute | solution.py:29
  107.5 3.6 %collective-permute-start.33 = (f32[1,512]{1,0:T(1,128)S(1)}, f32[1,512]{1,0:T(1,128)S(1)}, u32[]{:S(2)}, u32[]{:S(2)}) collective-permute-start(f32[1,512]{1,0:T(1,128)S(1)} %get-tuple-element.59), channel_id=1, source_target_pairs={{0,1},{1,0},{2,3},{3,2},{4,5},{5,4},{6,7},{7,6},{8,9},{9,8},{10,11... | collective-permute-start | bytes 6152 | tf_op jit(solution)/shard_map/ppermute | solution.py:29
  117.2 4.5 %collective-permute-start.34 = (bf16[256,2048]{1,0:T(8,128)(2,1)S(1)}, bf16[256,2048]{1,0:T(8,128)(2,1)S(1)}, u32[]{:S(2)}, u32[]{:S(2)}) collective-permute-start(bf16[256,2048]{1,0:T(8,128)(2,1)S(1)} %get-tuple-element.61), channel_id=1, source_target_pairs={{0,4},{4,0},{8,12},{12,8},{16,20},{20,16},{24,28},{28,24},{1,5},{5... | collective-permute-start | bytes 3145736 | tf_op jit(solution)/shard_map/ppermute | solution.py:29
  123.5 16.9 %collective-permute-start.38 = (bf16[256,2048]{1,0:T(8,128)(2,1)}, bf16[256,2048]{1,0:T(8,128)(2,1)}, u32[]{:S(2)}, u32[]{:S(2)}) collective-permute-start(bf16[256,2048]{1,0:T(8,128)(2,1)} %add_convert_fusion.1.refs_8_), channel_id=1, source_target_pairs={{0,8},{4,20},{8,0},{12,28},{16,24},{20,4},{24,16},{28,12},{1,9},{5... | collective-permute-start | bytes 3145736 | tf_op jit(solution)/shard_map/ppermute | solution.py:34
  124.0 16.4 %collective-permute-start.36 = (bf16[256,2048]{1,0:T(8,128)(2,1)}, bf16[256,2048]{1,0:T(8,128)(2,1)}, u32[]{:S(2)}, u32[]{:S(2)}) collective-permute-start(bf16[256,2048]{1,0:T(8,128)(2,1)} %get-tuple-element.73), channel_id=1, source_target_pairs={{0,4},{4,0},{8,12},{12,8},{16,20},{20,16},{24,28},{28,24},{1,5},{5... | collective-permute-start | bytes 3145736 | tf_op jit(solution)/shard_map/ppermute | solution.py:29
  124.2 16.3 %collective-permute-start.37 = (bf16[256,2048]{1,0:T(8,128)(2,1)}, bf16[256,2048]{1,0:T(8,128)(2,1)}, u32[]{:S(2)}, u32[]{:S(2)}) collective-permute-start(bf16[256,2048]{1,0:T(8,128)(2,1)} %get-tuple-element.74), channel_id=1, source_target_pairs={{0,4},{4,0},{8,12},{12,8},{16,20},{20,16},{24,28},{28,24},{1,5},{5... | collective-permute-start | bytes 3145736 | tf_op jit(solution)/shard_map/ppermute | solution.py:29
  124.5 14.6 %collective-permute-start.35 = (bf16[512,512]{1,0:T(8,128)(2,1)}, bf16[512,512]{1,0:T(8,128)(2,1)}, u32[]{:S(2)}, u32[]{:S(2)}) collective-permute-start(bf16[512,512]{1,0:T(8,128)(2,1)} %get-tuple-element.72), channel_id=1, source_target_pairs={{0,1},{1,0},{2,3},{3,2},{4,5},{5,4},{6,7},{7,6},{8,9},{9,8},{10,11... | collective-permute-start | bytes 1572872 | tf_op jit(solution)/shard_map/ppermute | solution.py:29
  143.7 30.8 %collective-permute-start.39 = (bf16[256,2048]{1,0:T(8,128)(2,1)S(1)}, bf16[256,2048]{1,0:T(8,128)(2,1)S(1)}, u32[]{:S(2)}, u32[]{:S(2)}) collective-permute-start(bf16[256,2048]{1,0:T(8,128)(2,1)S(1)} %get-tuple-element.88), channel_id=1, source_target_pairs={{0,8},{4,12},{8,0},{12,4},{16,24},{20,28},{24,16},{28,20},{1,9},{5... | collective-permute-start | bytes 3145736 | tf_op jit(solution)/shard_map/ppermute | solution.py:29
  145.2 29.3 %collective-permute-start.40 = (bf16[256,2048]{1,0:T(8,128)(2,1)S(1)}, bf16[256,2048]{1,0:T(8,128)(2,1)S(1)}, u32[]{:S(2)}, u32[]{:S(2)}) collective-permute-start(bf16[256,2048]{1,0:T(8,128)(2,1)S(1)} %get-tuple-element.87), channel_id=1, source_target_pairs={{0,16},{4,20},{8,24},{12,28},{16,0},{20,4},{24,8},{28,12},{1,17},{... | collective-permute-start | bytes 3145736 | tf_op jit(solution)/shard_map/ppermute | solution.py:29
  145.7 28.8 %collective-permute-start.43 = (bf16[256,2048]{1,0:T(8,128)(2,1)S(1)}, bf16[256,2048]{1,0:T(8,128)(2,1)S(1)}, u32[]{:S(2)}, u32[]{:S(2)}) collective-permute-start(bf16[256,2048]{1,0:T(8,128)(2,1)S(1)} %copy-done.19), channel_id=1, source_target_pairs={{0,4},{4,0},{8,12},{12,8},{16,20},{20,16},{24,28},{28,24},{1,5},{5... | collective-permute-start | bytes 3145736 | tf_op jit(solution)/shard_map/ppermute | solution.py:29
  145.7 24.4 %collective-permute-start.41 = (bf16[512,512]{1,0:T(8,128)(2,1)S(1)}, bf16[512,512]{1,0:T(8,128)(2,1)S(1)}, u32[]{:S(2)}, u32[]{:S(2)}) collective-permute-start(bf16[512,512]{1,0:T(8,128)(2,1)S(1)} %slice_bitcast_fusion.2), channel_id=1, source_target_pairs={{0,1},{1,0},{2,3},{3,2},{4,5},{5,4},{6,7},{7,6},{8,9},{9,8},{10,11... | collective-permute-start | bytes 1572872 | tf_op jit(solution)/shard_map/ppermute | solution.py:29
  147.3 26.2 %collective-permute-start.42 = (bf16[512,512]{1,0:T(8,128)(2,1)S(1)}, bf16[512,512]{1,0:T(8,128)(2,1)S(1)}, u32[]{:S(2)}, u32[]{:S(2)}) collective-permute-start(bf16[512,512]{1,0:T(8,128)(2,1)S(1)} %fusion.6), channel_id=1, source_target_pairs={{0,2},{1,3},{2,0},{3,1},{4,6},{5,7},{6,4},{7,5},{8,10},{9,11},{10,... | collective-permute-start | bytes 1572872 | tf_op jit(solution)/shard_map/ppermute | solution.py:29
  (17 other events, 145.4 us)

commit v12 on v11

--- a/solution.py
+++ b/solution.py
@@ -211,6 +211,7 @@
     columns = student_ref.shape[1]
     tile = min(256, columns)
     turned = turned_ref.at[place ^ chip ^ far]
+    copies = []
 
     for i in range(0, columns, tile):
         for j in range(i, i + tile, LANES):
@@ -219,9 +220,10 @@
             target = (student * student * scale_ref[:, at] * inverse[...]).astype(bf16)
             targets_ref[:, at] = target
             grad_ref[:, at] = ((student * students[...] - wide(target)) * wide(slope_ref[:, at])).astype(bf16)
-        head_products(turned, core, depth, grad_ref, slice(i, i + tile), mine_ref, theirs_ref)
-    copy = pltpu.make_async_copy(targets_ref, out_ref, sent)
-    copy.start()
+        at = slice(i, i + tile)
+        copies.append(pltpu.make_async_copy(targets_ref.at[:, at], out_ref.at[:, at], sent.at[i // tile]))
+        copies[-1].start()
+        head_products(turned, core, depth, grad_ref, at, mine_ref, theirs_ref)
     for (mask, side), ref in zip(parts, head_refs):
 
         @pl.when((chip ^ mask) == (place ^ (groups - 1)))
@@ -229,7 +231,8 @@
             at = pl.ds(rows_at(depth, side, paired), ref.shape[0])
             share_ref[:, at] = matmul(grad_ref[...], ref[...], ((1,), (1,))).astype(bf16)
 
-    copy.wait()
+    for copy in copies:
+        copy.wait()
 
 
 def near_kernel(depth, near, grad_ref, turned_ref, *refs):
@@ -244,11 +247,19 @@
 
 
 def shares_kernel(depth, paired, parts, grad_ref, *refs):
-    head_refs, shares_ref = refs[: len(parts)], refs[-1]
+    count = len(parts)
+    head_refs, shares_ref, buffers, arrived = refs[:count], refs[count + 1], refs[count + 2 : -1], refs[-1]
     chip, place = lax.axis_index("sample") // 2, lax.axis_index("cls")
-    for (mask, side), ref in zip(parts, head_refs):
-        at = pl.ds(rows_at(depth, side, paired), ref.shape[0])
-        shares_ref[chip ^ mask ^ place, :, at] = matmul(grad_ref[...], ref[...], ((1,), (1,))).astype(bf16)
+    copies = [
+        pltpu.make_async_copy(ref, buffer, arrived.at[i]) for i, (ref, buffer) in enumerate(zip(head_refs, buffers))
+    ]
+    for copy in copies:
+        copy.start()
+    for (mask, side), buffer, copy in zip(parts, buffers, copies):
+        copy.wait()
+        at = pl.ds(rows_at(depth, side, paired), buffer.shape[0])
+        shares_ref[chip ^ mask ^ place, :, at] = matmul(grad_ref[...], buffer[...], ((1,), (1,))).astype(bf16)
+
 
 def per_device(features, head, class_cap):
     rows, width = features.shape
@@ -330,7 +341,7 @@
         functools.partial(gradient_kernel, depth, paired, far, head_at),
         [((rows, classes), bf16)] * 2 + [((depth, classes), bf16)] * 2 + [((rows, width), bf16)],
         [student, slope, scale, students_mass, mass, turned] + head_list,
-        [pltpu.VMEM((rows, LANES), f32)] * 2 + [pltpu.VMEM((rows, classes), bf16), pltpu.SemaphoreType.DMA],
+        [pltpu.VMEM((rows, LANES), f32)] * 2 + [pltpu.VMEM((rows, classes), bf16), pltpu.SemaphoreType.DMA((classes // tile,))],
         slow=(0,),
     )
     theirs = flip(theirs, "sample", 1)
@@ -347,8 +358,9 @@
     (shares,) = call(
         functools.partial(shares_kernel, depth, paired, head_at),
         [((groups, rows, width), bf16)],
-        [grad] + head_list,
-        extra=[block],
+        [grad],
+        [pltpu.VMEM(part.shape, bf16) for part in head_list] + [pltpu.SemaphoreType.DMA((len(head_list),))],
+        extra=head_list + [block],
     )
 
     onward = {1: shares[1]}

time: 177 us -> 180 us (1.017)
  Pallas kernels: 28.2 us -> 33.2 us
    pallas_call x12, Pallas kernels: 28.2 us -> 33.2 us  [call(): pl.pallas_call(kernel, out_shape=tuple((jax.ShapeDtypeStruct(shape, dtype...]
  transfers between devices with their start and end apart: 44 -> 44, of which waited for: 26 -> 25; matrix products, arithmetic and copies ran while one was open for 1% -> 1% of each run, Pallas kernels for 9% -> 11%
where the time goes in v12:
time: 180 us
  waiting for transfers between devices  83.1 us (46%)
  starting transfers between devices  45.7 us (25%)
  Pallas kernels  33.2 us (18%)
  other arithmetic  8.96 us (5%)
  local copies, waits for them, and re-layouts  7.84 us (4%)
    ppermute x42, waiting for transfers between devices, flip(): lax.ppermute(value, axis, [(i, i ^ mask) for i in range(lax.axis_size(axi...  83.1 us
    ppermute x42, starting transfers between devices, flip(): lax.ppermute(value, axis, [(i, i ^ mask) for i in range(lax.axis_size(axi...  44.6 us
    pallas_call x12, Pallas kernels, call(): pl.pallas_call(kernel, out_shape=tuple((jax.ShapeDtypeStruct(shape, dtype...  33.2 us
    unnamed x42, local copies, waits for them, and re-layouts  7.79 us
  transfers between devices with their start and end apart: 44, of which 25 were waited for; matrix products, arithmetic and copies ran while one was open for 1% of the time, Pallas kernels for 11%

profile of v12, /device:TPU:0, one launch (start us, length us, event | category | flops | bytes accessed | tf_op | source)
XLA Modules:
  0.0 179.9 jit_solution(3870754939968155118)
XLA Ops:
  0.6 3.0 %collective-permute-start.4 = (bf16[256,2048]{1,0:T(8,128)(2,1)}, bf16[256,2048]{1,0:T(8,128)(2,1)S(1)}, u32[]{:S(2)}, u32[]{:S(2)}) collective-permute-start(bf16[256,2048]{1,0:T(8,128)(2,1)} %refs_0_.5), channel_id=1, source_target_pairs={{0,8},{4,12},{8,0},{12,4},{16,24},{20,28},{24,16},{28,20},{1,9},{5... | collective-permute-start | bytes 3145736 | tf_op jit(solution)/shard_map/ppermute | solution.py:29
  3.6 1.5 collective-permute-start.5
  5.2 2.6 %collective-permute-start.1 = (bf16[512,512]{1,0:T(8,128)(2,1)}, bf16[512,512]{1,0:T(8,128)(2,1)}, u32[]{:S(2)}, u32[]{:S(2)}) collective-permute-start(bf16[512,512]{1,0:T(8,128)(2,1)} %refs_0_.3), channel_id=1, source_target_pairs={{0,2},{1,3},{2,0},{3,1},{4,6},{5,7},{6,4},{7,5},{8,10},{9,11},{10,... | collective-permute-start | bytes 1572872 | tf_op jit(solution)/shard_map/ppermute | solution.py:29
  7.8 1.6 collective-permute-start
  9.3 21.5 %collective-permute-done.1.refs_2_ = bf16[512,512]{1,0:T(8,128)(2,1)} collective-permute-done((bf16[512,512]{1,0:T(8,128)(2,1)}, bf16[512,512]{1,0:T(8,128)(2,1)}, u32[]{:S(2)}, u32[]{:S(2)}) %collective-permute-start.1) | collective-permute-done | bytes 524320 | tf_op jit(solution)/shard_map/ppermute | solution.py:29
  31.5 1.1 collective-permute-done.refs_1_
  33.0 13.5 %collective-permute-done.2.refs_3_ = bf16[512,512]{1,0:T(8,128)(2,1)S(1)} collective-permute-done((bf16[512,512]{1,0:T(8,128)(2,1)}, bf16[512,512]{1,0:T(8,128)(2,1)S(1)}, u32[]{:S(2)}, u32[]{:S(2)}) %collective-permute-start.2) | collective-permute-done | bytes 524320 | tf_op jit(solution)/shard_map/ppermute | solution.py:29
  46.6 5.8 %shard_map.58 = (bf16[4,512,512]{2,1,0:T(8,128)(2,1)S(1)}, f32[512,2048]{1,0:T(8,128)S(1)}) custom-call(bf16[512,512]{1,0:T(8,128)(2,1)S(1)} %copy-done.17, bf16[512,512]{1,0:T(8,128)(2,1)} %collective-permute-done.refs_1_, bf16[512,512]{1,0:T(8,128)(2,1)} %collective-permute-done.1.refs_2_, bf16[512,512]{1,0:T(8,128)(2,1)S(1)} %collective-permute-done.2.refs_3_, ...), custom_call_target="tpu_custom_call" | custom-call | flops 1 | bytes 1 | tf_op jit(solution)/shard_map/pallas_call | solution.py:73
  52.5 2.6 %collective-permute-done.9.refs_1_.refs_7_ = bf16[256,2048]{1,0:T(8,128)(2,1)S(1)} collective-permute-done((bf16[256,2048]{1,0:T(8,128)(2,1)S(1)}, bf16[256,2048]{1,0:T(8,128)(2,1)S(1)}, u32[]{:S(2)}, u32[]{:S(2)}) %collective-permute-start.9) | collective-permute-done | bytes 1048608 | tf_op jit(solution)/shard_map/ppermute | solution.py:29
  55.2 2.5 %shard_map.59 = (f32[512,2048]{1,0:T(8,128)S(1)}, bf16[512,2048]{1,0:T(8,128)(2,1)S(1)}, f32[2,512]{1,0:T(2,128)S(1)}) custom-call(f32[512,2048]{1,0:T(8,128)S(1)} %get-tuple-element.47.logits_ref, bf16[4,512,512]{2,1,0:T(8,128)(2,1)S(1)} %get-tuple-element.48.blocks_ref, bf16[256,2048]{1,0:T(8,128)(2,1)S(1)} %collective-permute-done.8.refs_0_.refs_6_, ...), custom_call_target="tpu_custom_call" | custom-call | flops 1 | bytes 1 | tf_op jit(solution)/shard_map/pallas_call | solution.py:73
  57.7 2.9 %collective-permute-start.10 = (f32[2,512]{1,0:T(2,128)S(1)}, f32[2,512]{1,0:T(2,128)S(1)}, u32[]{:S(2)}, u32[]{:S(2)}) collective-permute-start(f32[2,512]{1,0:T(2,128)S(1)} %get-tuple-element.53), channel_id=1, source_target_pairs={{0,3},{1,2},{2,1},{3,0},{4,7},{5,6},{6,5},{7,4},{8,11},{9,10},{10,... | collective-permute-start | bytes 12296 | tf_op jit(solution)/shard_map/ppermute | solution.py:29
  60.6 1.5 collective-permute-start.12
  63.1 1.9 %collective-permute-done.11 = f32[2,512]{1,0:T(2,128)S(1)} collective-permute-done((f32[2,512]{1,0:T(2,128)S(1)}, f32[2,512]{1,0:T(2,128)S(1)}, u32[]{:S(2)}, u32[]{:S(2)}) %collective-permute-start.11) | collective-permute-done | bytes 4128 | tf_op jit(solution)/shard_map/ppermute | solution.py:29
  65.9 1.2 collective-permute-done.13
  67.1 1.5 collective-permute-start.14
  68.6 1.5 collective-permute-start.15
  72.2 1.5 collective-permute-done.16
  74.4 1.5 collective-permute-start.17
  76.5 2.3 %collective-permute-start.19 = (f32[1,512]{1,0:T(1,128)S(1)}, f32[1,512]{1,0:T(1,128)S(1)}, u32[]{:S(2)}, u32[]{:S(2)}) collective-permute-start(f32[1,512]{1,0:T(1,128)S(1)} %get-tuple-element.55), channel_id=1, source_target_pairs={{0,1},{1,0},{2,3},{3,2},{4,5},{5,4},{6,7},{7,6},{8,9},{9,8},{10,11... | collective-permute-start | bytes 6152 | tf_op jit(solution)/shard_map/ppermute | solution.py:29
  81.2 1.2 collective-permute-done.20
  82.9 1.5 collective-permute-start.22
  84.4 1.5 collective-permute-start.23
  85.9 1.1 collective-permute-done.21
  88.7 2.6 %collective-permute-start.24 = (f32[1,512]{1,0:T(1,128)S(1)}, f32[1,512]{1,0:T(1,128)S(1)}, u32[]{:S(2)}, u32[]{:S(2)}) collective-permute-start(f32[1,512]{1,0:T(1,128)S(1)} %get-tuple-element.57), channel_id=1, source_target_pairs={{0,3},{1,2},{2,1},{3,0},{4,7},{5,6},{6,5},{7,4},{8,11},{9,10},{10,... | collective-permute-start | bytes 6152 | tf_op jit(solution)/shard_map/ppermute | solution.py:29
  94.2 1.7 collective-permute-done.25
  96.6 1.2 collective-permute-done.27
  97.8 1.5 collective-permute-start.28
  99.3 1.5 collective-permute-start.29
  102.9 1.5 collective-permute-done.30
  105.1 1.5 collective-permute-start.31
  107.5 2.0 %collective-permute-start.33 = (f32[1,512]{1,0:T(1,128)S(1)}, f32[1,512]{1,0:T(1,128)S(1)}, u32[]{:S(2)}, u32[]{:S(2)}) collective-permute-start(f32[1,512]{1,0:T(1,128)S(1)} %get-tuple-element.59), channel_id=1, source_target_pairs={{0,1},{1,0},{2,3},{3,2},{4,5},{5,4},{6,7},{7,6},{8,9},{9,8},{10,11... | collective-permute-start | bytes 6152 | tf_op jit(solution)/shard_map/ppermute | solution.py:29
  111.2 6.2 %shard_map.67 = (bf16[512,2048]{1,0:T(8,128)(2,1)}, bf16[512,2048]{1,0:T(8,128)(2,1)S(1)}, bf16[256,2048]{1,0:T(8,128)(2,1)S(1)}, bf16[256,2048]{1,0:T(8,128)(2,1)S(1)}, bf16[512,512]{1,0:T(8,128)(2,1)}) custom-call(f32[512,2048]{1,0:T(8,128)S(1)} %get-tuple-element.51.student_ref, bf16[512,2048]{1,0:T(8,128)(2,1)S(1)} %get-tuple-element.52.slope_ref, ...), custom_call_target="tpu_custom_call" | custom-call | flops 1 | bytes 1 | tf_op jit(solution)/shard_map/pallas_call | solution.py:73
  117.5 3.4 %shard_map.68 = (bf16[256,2048]{1,0:T(8,128)(2,1)S(1)}, bf16[256,2048]{1,0:T(8,128)(2,1)}, bf16[256,2048]{1,0:T(8,128)(2,1)S(1)}, bf16[256,2048]{1,0:T(8,128)(2,...) custom-call(bf16[512,2048]{1,0:T(8,128)(2,1)S(1)} %get-tuple-element.62.grad_ref, ...), custom_call_target="tpu_custom_call" | custom-call | flops 1 | bytes 1 | tf_op jit(solution)/shard_map/pallas_call | solution.py:73
  122.0 1.7 add_convert_fusion.1.refs_8_
  124.7 2.0 %collective-permute-start.35 = (bf16[512,512]{1,0:T(8,128)(2,1)}, bf16[512,512]{1,0:T(8,128)(2,1)}, u32[]{:S(2)}, u32[]{:S(2)}) collective-permute-start(bf16[512,512]{1,0:T(8,128)(2,1)} %get-tuple-element.72), channel_id=1, source_target_pairs={{0,1},{1,0},{2,3},{3,2},{4,5},{5,4},{6,7},{7,6},{8,9},{9,8},{10,11... | collective-permute-start | bytes 1572872 | tf_op jit(solution)/shard_map/ppermute | solution.py:29
  126.7 1.2 copy-done.2
  127.9 1.2 copy-done.4
  129.2 1.2 copy-done.6
  130.4 1.2 copy-done.8
  131.6 1.6 copy-done.10
  133.2 10.7 %shard_map.69 = bf16[4,512,512]{2,1,0:T(8,128)(2,1)S(1)} custom-call(bf16[512,2048]{1,0:T(8,128)(2,1)S(1)} %copy-done.10, bf16[256,2048]{1,0:T(8,128)(2,1)S(1)} %copy-done, bf16[256,2048]{1,0:T(8,128)(2,1)} %collective-permute-done.3.refs_5_.refs_1_, bf16[256,2048]{1,0:T(8,128)(2,1)S(1)} %collective-permute-done.4.refs_6_.refs_2_, ...), custom_call_target="tpu_custom_call" | custom-call | flops 1 | bytes 1 | tf_op jit(solution)/shard_map/pallas_call | solution.py:73
  143.9 1.3 fusion.6
  145.6 3.0 %fusion.3 = (bf16[256,2048]{1,0:T(8,128)(2,1)S(1)}, bf16[256,2048]{1,0:T(8,128)(2,1)S(1)}) fusion(bf16[256,2048]{1,0:T(8,128)(2,1)} %collective-permute-done.38, bf16[256,2048]{1,0:T(8,128)(2,1)} %collective-permute-done.37, bf16[256,2048]{1,0:T(8,128)(2,1)S(1)} %copy-done.16, pred[]{:T(512)S(6)} %eq.11, pred[]{:T(512)S(6)} %eq.12, ...), kind=kLoop, calls=%fused_computation.5 | loop fusion | flops 6815744 | bytes 7340034 | tf_op jit(solution)/shard_map/convert_element_type | solution.py:387
  148.6 1.5 collective-permute-start.39
  150.7 2.0 %collective-permute-start.42 = (bf16[512,512]{1,0:T(8,128)(2,1)S(1)}, bf16[512,512]{1,0:T(8,128)(2,1)S(1)}, u32[]{:S(2)}, u32[]{:S(2)}) collective-permute-start(bf16[512,512]{1,0:T(8,128)(2,1)S(1)} %fusion.6), channel_id=1, source_target_pairs={{0,2},{1,3},{2,0},{3,1},{4,6},{5,7},{6,4},{7,5},{8,10},{9,11},{10,... | collective-permute-start | bytes 1572872 | tf_op jit(solution)/shard_map/ppermute | solution.py:29
  152.7 23.2 %collective-permute-done.41 = bf16[512,512]{1,0:T(8,128)(2,1)S(1)} collective-permute-done((bf16[512,512]{1,0:T(8,128)(2,1)S(1)}, bf16[512,512]{1,0:T(8,128)(2,1)S(1)}, u32[]{:S(2)}, u32[]{:S(2)}) %collective-permute-start.41) | collective-permute-done | bytes 524320 | tf_op jit(solution)/shard_map/ppermute | solution.py:29
  175.9 1.2 collective-permute-done.42
  178.2 1.7 add_convert_fusion
  (128 shorter events, 23.9 us)
Async XLA Ops:
  0.6 30.2 %collective-permute-start.4 = (bf16[256,2048]{1,0:T(8,128)(2,1)}, bf16[256,2048]{1,0:T(8,128)(2,1)S(1)}, u32[]{:S(2)}, u32[]{:S(2)}) collective-permute-start(bf16[256,2048]{1,0:T(8,128)(2,1)} %refs_0_.5), channel_id=1, source_target_pairs={{0,8},{4,12},{8,0},{12,4},{16,24},{20,28},{24,16},{28,20},{1,9},{5... | collective-permute-start | bytes 3145736 | tf_op jit(solution)/shard_map/ppermute | solution.py:29
  3.6 27.2 %collective-permute-start.5 = (bf16[256,2048]{1,0:T(8,128)(2,1)}, bf16[256,2048]{1,0:T(8,128)(2,1)S(1)}, u32[]{:S(2)}, u32[]{:S(2)}) collective-permute-start(bf16[256,2048]{1,0:T(8,128)(2,1)} %refs_0_.5), channel_id=1, source_target_pairs={{0,16},{4,20},{8,24},{12,28},{16,0},{20,4},{24,8},{28,12},{1,17},{... | collective-permute-start | bytes 3145736 | tf_op jit(solution)/shard_map/ppermute | solution.py:29
  5.2 25.7 %collective-permute-start.1 = (bf16[512,512]{1,0:T(8,128)(2,1)}, bf16[512,512]{1,0:T(8,128)(2,1)}, u32[]{:S(2)}, u32[]{:S(2)}) collective-permute-start(bf16[512,512]{1,0:T(8,128)(2,1)} %refs_0_.3), channel_id=1, source_target_pairs={{0,2},{1,3},{2,0},{3,1},{4,6},{5,7},{6,4},{7,5},{8,10},{9,11},{10,... | collective-permute-start | bytes 1572872 | tf_op jit(solution)/shard_map/ppermute | solution.py:29
  7.8 24.8 %collective-permute-start.3 = (bf16[256,2048]{1,0:T(8,128)(2,1)}, bf16[256,2048]{1,0:T(8,128)(2,1)}, u32[]{:S(2)}, u32[]{:S(2)}) collective-permute-start(bf16[256,2048]{1,0:T(8,128)(2,1)} %refs_0_.5), channel_id=1, source_target_pairs={{0,4},{4,0},{8,12},{12,8},{16,20},{20,16},{24,28},{28,24},{1,5},{5... | collective-permute-start | bytes 3145736 | tf_op jit(solution)/shard_map/ppermute | solution.py:29
  7.8 24.8 %collective-permute-start = (bf16[512,512]{1,0:T(8,128)(2,1)}, bf16[512,512]{1,0:T(8,128)(2,1)}, u32[]{:S(2)}, u32[]{:S(2)}) collective-permute-start(bf16[512,512]{1,0:T(8,128)(2,1)} %refs_0_.3), channel_id=1, source_target_pairs={{0,1},{1,0},{2,3},{3,2},{4,5},{5,4},{6,7},{7,6},{8,9},{9,8},{10,11... | collective-permute-start | bytes 1572872 | tf_op jit(solution)/shard_map/ppermute | solution.py:29
  30.8 15.7 %collective-permute-start.6 = (bf16[256,2048]{1,0:T(8,128)(2,1)S(1)}, bf16[256,2048]{1,0:T(8,128)(2,1)S(1)}, u32[]{:S(2)}, u32[]{:S(2)}) collective-permute-start(bf16[256,2048]{1,0:T(8,128)(2,1)S(1)} %collective-permute-done.4.refs_6_.refs_2_), channel_id=1, source_target_pairs={{0,4},{4,0},{8,12},{12,8},{16,20},{20,16},{24,28},{28,24},{1,5},{5... | collective-permute-start | bytes 3145736 | tf_op jit(solution)/shard_map/ppermute | solution.py:29
  30.8 15.7 %collective-permute-start.7 = (bf16[256,2048]{1,0:T(8,128)(2,1)S(1)}, bf16[256,2048]{1,0:T(8,128)(2,1)S(1)}, u32[]{:S(2)}, u32[]{:S(2)}) collective-permute-start(bf16[256,2048]{1,0:T(8,128)(2,1)S(1)} %collective-permute-done.5.refs_8_.refs_4_), channel_id=1, source_target_pairs={{0,4},{4,0},{8,12},{12,8},{16,20},{20,16},{24,28},{28,24},{1,5},{5... | collective-permute-start | bytes 3145736 | tf_op jit(solution)/shard_map/ppermute | solution.py:29
  32.5 19.9 %collective-permute-start.8 = (bf16[256,2048]{1,0:T(8,128)(2,1)S(1)}, bf16[256,2048]{1,0:T(8,128)(2,1)S(1)}, u32[]{:S(2)}, u32[]{:S(2)}) collective-permute-start(bf16[256,2048]{1,0:T(8,128)(2,1)S(1)} %broadcast_select_fusion), channel_id=1, source_target_pairs={{0,16},{4,12},{8,24},{12,4},{16,0},{20,28},{24,8},{28,20},{1,17},{... | collective-permute-start | bytes 3145736 | tf_op jit(solution)/shard_map/ppermute | solution.py:34
  33.0 13.5 %collective-permute-start.2 = (bf16[512,512]{1,0:T(8,128)(2,1)}, bf16[512,512]{1,0:T(8,128)(2,1)S(1)}, u32[]{:S(2)}, u32[]{:S(2)}) collective-permute-start(bf16[512,512]{1,0:T(8,128)(2,1)} %collective-permute-done.1.refs_2_), channel_id=1, source_target_pairs={{0,1},{1,0},{2,3},{3,2},{4,5},{5,4},{6,7},{7,6},{8,9},{9,8},{10,11... | collective-permute-start | bytes 1572872 | tf_op jit(solution)/shard_map/ppermute | solution.py:29
  46.6 64.6 %copy-start.1 = (bf16[256,2048]{1,0:T(8,128)(2,1)}, bf16[256,2048]{1,0:T(8,128)(2,1)S(1)}, u32[]{:S(2)}) copy-start(bf16[256,2048]{1,0:T(8,128)(2,1)S(1)} %collective-permute-done.6.refs_7_.refs_3_) | copy-start | bytes 3145732
  46.6 64.5 %copy-start.3 = (bf16[256,2048]{1,0:T(8,128)(2,1)}, bf16[256,2048]{1,0:T(8,128)(2,1)S(1)}, u32[]{:S(2)}) copy-start(bf16[256,2048]{1,0:T(8,128)(2,1)S(1)} %collective-permute-done.7.refs_9_.refs_5_) | copy-start | bytes 3145732
  52.5 58.7 %copy-start.5 = (bf16[256,2048]{1,0:T(8,128)(2,1)}, bf16[256,2048]{1,0:T(8,128)(2,1)S(1)}, u32[]{:S(2)}) copy-start(bf16[256,2048]{1,0:T(8,128)(2,1)S(1)} %collective-permute-done.8.refs_0_.refs_6_) | copy-start | bytes 3145732
  52.5 2.7 %collective-permute-start.9 = (bf16[256,2048]{1,0:T(8,128)(2,1)S(1)}, bf16[256,2048]{1,0:T(8,128)(2,1)S(1)}, u32[]{:S(2)}, u32[]{:S(2)}) collective-permute-start(bf16[256,2048]{1,0:T(8,128)(2,1)S(1)} %collective-permute-done.8.refs_0_.refs_6_), channel_id=1, source_target_pairs={{0,4},{4,0},{8,12},{12,8},{16,20},{20,16},{24,28},{28,24},{1,5},{5... | collective-permute-start | bytes 3145736 | tf_op jit(solution)/shard_map/ppermute | solution.py:29
  55.2 56.0 %copy-start.7 = (bf16[256,2048]{1,0:T(8,128)(2,1)}, bf16[256,2048]{1,0:T(8,128)(2,1)S(1)}, u32[]{:S(2)}) copy-start(bf16[256,2048]{1,0:T(8,128)(2,1)S(1)} %collective-permute-done.9.refs_1_.refs_7_) | copy-start | bytes 3145732
  57.7 5.5 %collective-permute-start.10 = (f32[2,512]{1,0:T(2,128)S(1)}, f32[2,512]{1,0:T(2,128)S(1)}, u32[]{:S(2)}, u32[]{:S(2)}) collective-permute-start(f32[2,512]{1,0:T(2,128)S(1)} %get-tuple-element.53), channel_id=1, source_target_pairs={{0,3},{1,2},{2,1},{3,0},{4,7},{5,6},{6,5},{7,4},{8,11},{9,10},{10,... | collective-permute-start | bytes 12296 | tf_op jit(solution)/shard_map/ppermute | solution.py:29
  60.6 4.5 %collective-permute-start.11 = (f32[2,512]{1,0:T(2,128)S(1)}, f32[2,512]{1,0:T(2,128)S(1)}, u32[]{:S(2)}, u32[]{:S(2)}) collective-permute-start(f32[2,512]{1,0:T(2,128)S(1)} %get-tuple-element.53), channel_id=1, source_target_pairs={{0,2},{1,3},{2,0},{3,1},{4,6},{5,7},{6,4},{7,5},{8,10},{9,11},{10,... | collective-permute-start | bytes 12296 | tf_op jit(solution)/shard_map/ppermute | solution.py:29
  60.6 4.5 %collective-permute-start.12 = (f32[2,512]{1,0:T(2,128)S(1)}, f32[2,512]{1,0:T(2,128)S(1)}, u32[]{:S(2)}, u32[]{:S(2)}) collective-permute-start(f32[2,512]{1,0:T(2,128)S(1)} %get-tuple-element.53), channel_id=1, source_target_pairs={{0,1},{1,0},{2,3},{3,2},{4,5},{5,4},{6,7},{7,6},{8,9},{9,8},{10,11... | collective-permute-start | bytes 12296 | tf_op jit(solution)/shard_map/ppermute | solution.py:29
  65.8 1.2 collective-permute-start.13
  67.1 4.6 %collective-permute-start.14 = (f32[1,2048]{1,0:T(1,128)S(1)}, f32[1,2048]{1,0:T(1,128)S(1)}, u32[]{:S(2)}, u32[]{:S(2)}) collective-permute-start(f32[1,2048]{1,0:T(1,128)S(1)} %add.114), channel_id=1, source_target_pairs={{0,24},{4,28},{8,16},{12,20},{16,8},{20,12},{24,0},{28,4},{1,25},{... | collective-permute-start | bytes 24584 | tf_op jit(solution)/shard_map/ppermute | solution.py:29
  68.6 3.7 %collective-permute-start.15 = (f32[1,2048]{1,0:T(1,128)S(1)}, f32[1,2048]{1,0:T(1,128)S(1)}, u32[]{:S(2)}, u32[]{:S(2)}) collective-permute-start(f32[1,2048]{1,0:T(1,128)S(1)} %add.114), channel_id=1, source_target_pairs={{0,16},{4,20},{8,24},{12,28},{16,0},{20,4},{24,8},{28,12},{1,17},{... | collective-permute-start | bytes 24584 | tf_op jit(solution)/shard_map/ppermute | solution.py:29
  70.1 3.7 %collective-permute-start.16 = (f32[1,2048]{1,0:T(1,128)S(1)}, f32[1,2048]{1,0:T(1,128)S(1)}, u32[]{:S(2)}, u32[]{:S(2)}) collective-permute-start(f32[1,2048]{1,0:T(1,128)S(1)} %add.114), channel_id=1, source_target_pairs={{0,8},{4,12},{8,0},{12,4},{16,24},{20,28},{24,16},{28,20},{1,9},{5... | collective-permute-start | bytes 24584 | tf_op jit(solution)/shard_map/ppermute | solution.py:29
  74.4 5.4 %collective-permute-start.17 = (f32[1,512]{1,0:T(1,128)S(1)}, f32[1,512]{1,0:T(1,128)S(1)}, u32[]{:S(2)}, u32[]{:S(2)}) collective-permute-start(f32[1,512]{1,0:T(1,128)S(1)} %get-tuple-element.55), channel_id=1, source_target_pairs={{0,3},{1,2},{2,1},{3,0},{4,7},{5,6},{6,5},{7,4},{8,11},{9,10},{10,... | collective-permute-start | bytes 6152 | tf_op jit(solution)/shard_map/ppermute | solution.py:29
  75.9 4.5 %collective-permute-start.18 = (f32[1,512]{1,0:T(1,128)S(1)}, f32[1,512]{1,0:T(1,128)S(1)}, u32[]{:S(2)}, u32[]{:S(2)}) collective-permute-start(f32[1,512]{1,0:T(1,128)S(1)} %get-tuple-element.55), channel_id=1, source_target_pairs={{0,2},{1,3},{2,0},{3,1},{4,6},{5,7},{6,4},{7,5},{8,10},{9,11},{10,... | collective-permute-start | bytes 6152 | tf_op jit(solution)/shard_map/ppermute | solution.py:29
  76.5 3.9 %collective-permute-start.19 = (f32[1,512]{1,0:T(1,128)S(1)}, f32[1,512]{1,0:T(1,128)S(1)}, u32[]{:S(2)}, u32[]{:S(2)}) collective-permute-start(f32[1,512]{1,0:T(1,128)S(1)} %get-tuple-element.55), channel_id=1, source_target_pairs={{0,1},{1,0},{2,3},{3,2},{4,5},{5,4},{6,7},{7,6},{8,9},{9,8},{10,11... | collective-permute-start | bytes 6152 | tf_op jit(solution)/shard_map/ppermute | solution.py:29
  81.1 1.2 collective-permute-start.20
  82.3 4.6 %collective-permute-start.21 = (f32[1,2048]{1,0:T(1,128)S(1)}, f32[1,2048]{1,0:T(1,128)S(1)}, u32[]{:S(2)}, u32[]{:S(2)}) collective-permute-start(f32[1,2048]{1,0:T(1,128)S(1)} %add.121), channel_id=1, source_target_pairs={{0,24},{4,28},{8,16},{12,20},{16,8},{20,12},{24,0},{28,4},{1,25},{... | collective-permute-start | bytes 24584 | tf_op jit(solution)/shard_map/ppermute | solution.py:29
  82.9 4.1 %collective-permute-start.22 = (f32[1,2048]{1,0:T(1,128)S(1)}, f32[1,2048]{1,0:T(1,128)S(1)}, u32[]{:S(2)}, u32[]{:S(2)}) collective-permute-start(f32[1,2048]{1,0:T(1,128)S(1)} %add.121), channel_id=1, source_target_pairs={{0,16},{4,20},{8,24},{12,28},{16,0},{20,4},{24,8},{28,12},{1,17},{... | collective-permute-start | bytes 24584 | tf_op jit(solution)/shard_map/ppermute | solution.py:29
  84.4 3.7 %collective-permute-start.23 = (f32[1,2048]{1,0:T(1,128)S(1)}, f32[1,2048]{1,0:T(1,128)S(1)}, u32[]{:S(2)}, u32[]{:S(2)}) collective-permute-start(f32[1,2048]{1,0:T(1,128)S(1)} %add.121), channel_id=1, source_target_pairs={{0,8},{4,12},{8,0},{12,4},{16,24},{20,28},{24,16},{28,20},{1,9},{5... | collective-permute-start | bytes 24584 | tf_op jit(solution)/shard_map/ppermute | solution.py:29
  88.7 5.4 %collective-permute-start.24 = (f32[1,512]{1,0:T(1,128)S(1)}, f32[1,512]{1,0:T(1,128)S(1)}, u32[]{:S(2)}, u32[]{:S(2)}) collective-permute-start(f32[1,512]{1,0:T(1,128)S(1)} %get-tuple-element.57), channel_id=1, source_target_pairs={{0,3},{1,2},{2,1},{3,0},{4,7},{5,6},{6,5},{7,4},{8,11},{9,10},{10,... | collective-permute-start | bytes 6152 | tf_op jit(solution)/shard_map/ppermute | solution.py:29
  91.3 4.5 %collective-permute-start.25 = (f32[1,512]{1,0:T(1,128)S(1)}, f32[1,512]{1,0:T(1,128)S(1)}, u32[]{:S(2)}, u32[]{:S(2)}) collective-permute-start(f32[1,512]{1,0:T(1,128)S(1)} %get-tuple-element.57), channel_id=1, source_target_pairs={{0,2},{1,3},{2,0},{3,1},{4,6},{5,7},{6,4},{7,5},{8,10},{9,11},{10,... | collective-permute-start | bytes 6152 | tf_op jit(solution)/shard_map/ppermute | solution.py:29
  92.3 3.6 %collective-permute-start.26 = (f32[1,512]{1,0:T(1,128)S(1)}, f32[1,512]{1,0:T(1,128)S(1)}, u32[]{:S(2)}, u32[]{:S(2)}) collective-permute-start(f32[1,512]{1,0:T(1,128)S(1)} %get-tuple-element.57), channel_id=1, source_target_pairs={{0,1},{1,0},{2,3},{3,2},{4,5},{5,4},{6,7},{7,6},{8,9},{9,8},{10,11... | collective-permute-start | bytes 6152 | tf_op jit(solution)/shard_map/ppermute | solution.py:29
  96.5 1.2 collective-permute-start.27
  97.8 4.6 %collective-permute-start.28 = (f32[1,2048]{1,0:T(1,128)S(1)}, f32[1,2048]{1,0:T(1,128)S(1)}, u32[]{:S(2)}, u32[]{:S(2)}) collective-permute-start(f32[1,2048]{1,0:T(1,128)S(1)} %add.128), channel_id=1, source_target_pairs={{0,24},{4,28},{8,16},{12,20},{16,8},{20,12},{24,0},{28,4},{1,25},{... | collective-permute-start | bytes 24584 | tf_op jit(solution)/shard_map/ppermute | solution.py:29
  99.3 3.7 %collective-permute-start.29 = (f32[1,2048]{1,0:T(1,128)S(1)}, f32[1,2048]{1,0:T(1,128)S(1)}, u32[]{:S(2)}, u32[]{:S(2)}) collective-permute-start(f32[1,2048]{1,0:T(1,128)S(1)} %add.128), channel_id=1, source_target_pairs={{0,16},{4,20},{8,24},{12,28},{16,0},{20,4},{24,8},{28,12},{1,17},{... | collective-permute-start | bytes 24584 | tf_op jit(solution)/shard_map/ppermute | solution.py:29
  100.8 3.7 %collective-permute-start.30 = (f32[1,2048]{1,0:T(1,128)S(1)}, f32[1,2048]{1,0:T(1,128)S(1)}, u32[]{:S(2)}, u32[]{:S(2)}) collective-permute-start(f32[1,2048]{1,0:T(1,128)S(1)} %add.128), channel_id=1, source_target_pairs={{0,8},{4,12},{8,0},{12,4},{16,24},{20,28},{24,16},{28,20},{1,9},{5... | collective-permute-start | bytes 24584 | tf_op jit(solution)/shard_map/ppermute | solution.py:29
  105.1 5.4 %collective-permute-start.31 = (f32[1,512]{1,0:T(1,128)S(1)}, f32[1,512]{1,0:T(1,128)S(1)}, u32[]{:S(2)}, u32[]{:S(2)}) collective-permute-start(f32[1,512]{1,0:T(1,128)S(1)} %get-tuple-element.59), channel_id=1, source_target_pairs={{0,3},{1,2},{2,1},{3,0},{4,7},{5,6},{6,5},{7,4},{8,11},{9,10},{10,... | collective-permute-start | bytes 6152 | tf_op jit(solution)/shard_map/ppermute | solution.py:29
  106.6 4.5 %collective-permute-start.32 = (f32[1,512]{1,0:T(1,128)S(1)}, f32[1,512]{1,0:T(1,128)S(1)}, u32[]{:S(2)}, u32[]{:S(2)}) collective-permute-start(f32[1,512]{1,0:T(1,128)S(1)} %get-tuple-element.59), channel_id=1, source_target_pairs={{0,2},{1,3},{2,0},{3,1},{4,6},{5,7},{6,4},{7,5},{8,10},{9,11},{10,... | collective-permute-start | bytes 6152 | tf_op jit(solution)/shard_map/ppermute | solution.py:29
  107.5 3.6 %collective-permute-start.33 = (f32[1,512]{1,0:T(1,128)S(1)}, f32[1,512]{1,0:T(1,128)S(1)}, u32[]{:S(2)}, u32[]{:S(2)}) collective-permute-start(f32[1,512]{1,0:T(1,128)S(1)} %get-tuple-element.59), channel_id=1, source_target_pairs={{0,1},{1,0},{2,3},{3,2},{4,5},{5,4},{6,7},{7,6},{8,9},{9,8},{10,11... | collective-permute-start | bytes 6152 | tf_op jit(solution)/shard_map/ppermute | solution.py:29
  117.4 4.5 %collective-permute-start.34 = (bf16[256,2048]{1,0:T(8,128)(2,1)S(1)}, bf16[256,2048]{1,0:T(8,128)(2,1)S(1)}, u32[]{:S(2)}, u32[]{:S(2)}) collective-permute-start(bf16[256,2048]{1,0:T(8,128)(2,1)S(1)} %get-tuple-element.61), channel_id=1, source_target_pairs={{0,4},{4,0},{8,12},{12,8},{16,20},{20,16},{24,28},{28,24},{1,5},{5... | collective-permute-start | bytes 3145736 | tf_op jit(solution)/shard_map/ppermute | solution.py:29
  123.6 21.6 %collective-permute-start.38 = (bf16[256,2048]{1,0:T(8,128)(2,1)}, bf16[256,2048]{1,0:T(8,128)(2,1)}, u32[]{:S(2)}, u32[]{:S(2)}) collective-permute-start(bf16[256,2048]{1,0:T(8,128)(2,1)} %add_convert_fusion.1.refs_8_), channel_id=1, source_target_pairs={{0,8},{4,20},{8,0},{12,28},{16,24},{20,4},{24,16},{28,12},{1,9},{5... | collective-permute-start | bytes 3145736 | tf_op jit(solution)/shard_map/ppermute | solution.py:34
  124.2 21.1 %collective-permute-start.36 = (bf16[256,2048]{1,0:T(8,128)(2,1)}, bf16[256,2048]{1,0:T(8,128)(2,1)}, u32[]{:S(2)}, u32[]{:S(2)}) collective-permute-start(bf16[256,2048]{1,0:T(8,128)(2,1)} %get-tuple-element.73), channel_id=1, source_target_pairs={{0,4},{4,0},{8,12},{12,8},{16,20},{20,16},{24,28},{28,24},{1,5},{5... | collective-permute-start | bytes 3145736 | tf_op jit(solution)/shard_map/ppermute | solution.py:29
  124.3 20.9 %collective-permute-start.37 = (bf16[256,2048]{1,0:T(8,128)(2,1)}, bf16[256,2048]{1,0:T(8,128)(2,1)}, u32[]{:S(2)}, u32[]{:S(2)}) collective-permute-start(bf16[256,2048]{1,0:T(8,128)(2,1)} %get-tuple-element.74), channel_id=1, source_target_pairs={{0,4},{4,0},{8,12},{12,8},{16,20},{20,16},{24,28},{28,24},{1,5},{5... | collective-permute-start | bytes 3145736 | tf_op jit(solution)/shard_map/ppermute | solution.py:29
  124.7 19.3 %collective-permute-start.35 = (bf16[512,512]{1,0:T(8,128)(2,1)}, bf16[512,512]{1,0:T(8,128)(2,1)}, u32[]{:S(2)}, u32[]{:S(2)}) collective-permute-start(bf16[512,512]{1,0:T(8,128)(2,1)} %get-tuple-element.72), channel_id=1, source_target_pairs={{0,1},{1,0},{2,3},{3,2},{4,5},{5,4},{6,7},{7,6},{8,9},{9,8},{10,11... | collective-permute-start | bytes 1572872 | tf_op jit(solution)/shard_map/ppermute | solution.py:29
  148.6 29.6 %collective-permute-start.39 = (bf16[256,2048]{1,0:T(8,128)(2,1)S(1)}, bf16[256,2048]{1,0:T(8,128)(2,1)S(1)}, u32[]{:S(2)}, u32[]{:S(2)}) collective-permute-start(bf16[256,2048]{1,0:T(8,128)(2,1)S(1)} %get-tuple-element.88), channel_id=1, source_target_pairs={{0,8},{4,12},{8,0},{12,4},{16,24},{20,28},{24,16},{28,20},{1,9},{5... | collective-permute-start | bytes 3145736 | tf_op jit(solution)/shard_map/ppermute | solution.py:29
  150.2 28.0 %collective-permute-start.40 = (bf16[256,2048]{1,0:T(8,128)(2,1)S(1)}, bf16[256,2048]{1,0:T(8,128)(2,1)S(1)}, u32[]{:S(2)}, u32[]{:S(2)}) collective-permute-start(bf16[256,2048]{1,0:T(8,128)(2,1)S(1)} %get-tuple-element.87), channel_id=1, source_target_pairs={{0,16},{4,20},{8,24},{12,28},{16,0},{20,4},{24,8},{28,12},{1,17},{... | collective-permute-start | bytes 3145736 | tf_op jit(solution)/shard_map/ppermute | solution.py:29
  150.7 27.5 %collective-permute-start.43 = (bf16[256,2048]{1,0:T(8,128)(2,1)S(1)}, bf16[256,2048]{1,0:T(8,128)(2,1)S(1)}, u32[]{:S(2)}, u32[]{:S(2)}) collective-permute-start(bf16[256,2048]{1,0:T(8,128)(2,1)S(1)} %copy-done.19), channel_id=1, source_target_pairs={{0,4},{4,0},{8,12},{12,8},{16,20},{20,16},{24,28},{28,24},{1,5},{5... | collective-permute-start | bytes 3145736 | tf_op jit(solution)/shard_map/ppermute | solution.py:29
  150.7 25.3 %collective-permute-start.41 = (bf16[512,512]{1,0:T(8,128)(2,1)S(1)}, bf16[512,512]{1,0:T(8,128)(2,1)S(1)}, u32[]{:S(2)}, u32[]{:S(2)}) collective-permute-start(bf16[512,512]{1,0:T(8,128)(2,1)S(1)} %slice_bitcast_fusion.2), channel_id=1, source_target_pairs={{0,1},{1,0},{2,3},{3,2},{4,5},{5,4},{6,7},{7,6},{8,9},{9,8},{10,11... | collective-permute-start | bytes 1572872 | tf_op jit(solution)/shard_map/ppermute | solution.py:29
  150.7 26.5 %collective-permute-start.42 = (bf16[512,512]{1,0:T(8,128)(2,1)S(1)}, bf16[512,512]{1,0:T(8,128)(2,1)S(1)}, u32[]{:S(2)}, u32[]{:S(2)}) collective-permute-start(bf16[512,512]{1,0:T(8,128)(2,1)S(1)} %fusion.6), channel_id=1, source_target_pairs={{0,2},{1,3},{2,0},{3,1},{4,6},{5,7},{6,4},{7,5},{8,10},{9,11},{10,... | collective-permute-start | bytes 1572872 | tf_op jit(solution)/shard_map/ppermute | solution.py:29
  (17 other events, 144.1 us)

commit v13 on v8

--- a/solution.py
+++ b/solution.py
@@ -224,18 +224,23 @@
             share_ref[:, at] = matmul(grad_ref[...], ref[...], ((1,), (1,))).astype(bf16)
 
 
-def products_kernel(count, depth, paired, near, parts, grad_ref, turned_ref, *refs):
-    head_refs, refs = refs[: len(parts)], refs[len(parts) + count :]
-    pairs, (shares_ref,) = refs[:-1], refs[-1:]
+def near_kernel(depth, near, grad_ref, turned_ref, *refs):
     me, place = lax.axis_index("sample"), lax.axis_index("cls")
     chip, core = me // 2, me % 2
     columns = grad_ref.shape[1]
     tile = min(256, columns)
+    pairs = refs[len(refs) - 2 * len(near) :]
     for index, mask in enumerate(near):
-        mine_ref, theirs_ref = pairs[2 * index], pairs[2 * index + 1]
         turned = turned_ref.at[place ^ chip ^ mask]
         for i in range(0, columns, tile):
-            head_products(turned, core, depth, grad_ref, slice(i, i + tile), mine_ref, theirs_ref)
+            at = slice(i, i + tile)
+            head_products(turned, core, depth, grad_ref, at, pairs[2 * index], pairs[2 * index + 1])
+
+
+def products_kernel(depth, paired, near, parts, grad_ref, turned_ref, *refs):
+    head_refs, pairs, shares_ref = refs[: len(parts)], refs[-1 - 2 * len(near) : -1], refs[-1]
+    chip, place = lax.axis_index("sample") // 2, lax.axis_index("cls")
+    near_kernel(depth, near, grad_ref, turned_ref, *pairs)
     for (mask, side), ref in zip(parts, head_refs):
         at = pl.ds(rows_at(depth, side, paired), ref.shape[0])
         shares_ref[chip ^ mask ^ place, :, at] = matmul(grad_ref[...], ref[...], ((1,), (1,))).astype(bf16)
@@ -312,7 +317,7 @@
 
     head_at = [at for at, _ in early + late]
     head_list = [part for _, part in early + late]
-    near = [mask // 2 for mask in first + second] + [0]
+    near = [mask // 2 for mask in first + second]
     diagonal = [(a, b) for a in first for b in second]
     far = (diagonal[-1][0] | diagonal[-1][1]) // 2
     near = [(a | b) // 2 for a, b in diagonal[:-1]] + near
@@ -327,7 +332,7 @@
     share_from = {groups - 2: flip(share, "cls", 1)}
 
     results = call(
-        functools.partial(products_kernel, 1, depth, paired, near, head_at),
+        functools.partial(products_kernel, depth, paired, near, head_at),
         [((depth, classes), bf16)] * (2 * len(near)) + [((groups, rows, width), bf16)],
         [grad, turned] + head_list,
         extra=[block],
@@ -353,16 +358,24 @@
     }
     for a, b in diagonal[:-1]:
         passed[a, b] = cross(mixed[a | b].astype(bf16), a, b)
-    received = []
+    sent = {}
     for mask in first + second:
         block = mixed[mask]
         for (a, b), more in passed.items():
             if mask == (b if mask in second else a):
                 block = block + jnp.where((core == 0) == (mask in second), wide(more), 0.0)
-        received.append(flip(block.astype(bf16), "sample", mask))
+        sent[mask] = block.astype(bf16)
+    received = [flip(value, "sample", mask) for mask, value in sent.items()]
+    mine, theirs = call(
+        functools.partial(near_kernel, depth, [0]),
+        [((depth, classes), bf16)] * 2,
+        [grad, turned],
+        extra=list(sent.values()),
+    )
+    own = wide(mine) + wide(flip(theirs, "sample", 1))
     received = lax.optimization_barrier((*received, grad_features))
     grad_features = received[-1]
-    grad_head = sum([wide(part) for part in received[:-1]], mixed[0]).astype(bf16)
+    grad_head = sum([wide(part) for part in received[:-1]], own).astype(bf16)
     return (targets, grad_features, grad_head)
 
 

time: 176 us -> 177 us (level)
  local copies, waits for them, and re-layouts: 4.83 us -> 2.33 us
  starting transfers between devices: 47.5 us -> 49.7 us
    unnamed x33 -> x31, local copies, waits for them, and re-layouts: 3.98 us -> 1.39 us
    ppermute x42, starting transfers between devices: 44.5 us -> 46.7 us  [flip(): lax.ppermute(value, axis, [(i, i ^ mask) for i in range(lax.axis_size(axi...]
    pallas_call x10 -> x11, Pallas kernels: 26.7 us -> 26.9 us  [call(): pl.pallas_call(kernel, out_shape=tuple((pltpu.VMEM(shape, dtype) for shap...]
  transfers between devices with their start and end apart: 44 -> 44, of which waited for: 29 -> 31; matrix products, arithmetic and copies ran while one was open for 3% -> 3% of each run, Pallas kernels for 9% -> 9%
where the time goes in v13:
time: 177 us
  waiting for transfers between devices  88.4 us (50%)
  starting transfers between devices  49.7 us (28%)
  Pallas kernels  26.9 us (15%)
  other arithmetic  8.71 us (5%)
  local copies, waits for them, and re-layouts  2.33 us (1%)
    ppermute x42, waiting for transfers between devices, flip(): lax.ppermute(value, axis, [(i, i ^ mask) for i in range(lax.axis_size(axi...  88 us
    ppermute x42, starting transfers between devices, flip(): lax.ppermute(value, axis, [(i, i ^ mask) for i in range(lax.axis_size(axi...  46.7 us
    pallas_call x11, Pallas kernels, call(): pl.pallas_call(kernel, out_shape=tuple((pltpu.VMEM(shape, dtype) for shap...  26.9 us
  transfers between devices with their start and end apart: 44, of which 31 were waited for; matrix products, arithmetic and copies ran while one was open for 3% of the time, Pallas kernels for 9%

profile of v13, /device:TPU:0, one launch (start us, length us, event | category | flops | bytes accessed | tf_op | source)
XLA Modules:
  0.0 177.1 jit_solution(5622815468265298756)
XLA Ops:
  0.6 3.0 %collective-permute-start.4 = (bf16[256,2048]{1,0:T(8,128)(2,1)}, bf16[256,2048]{1,0:T(8,128)(2,1)S(1)}, u32[]{:S(2)}, u32[]{:S(2)}) collective-permute-start(bf16[256,2048]{1,0:T(8,128)(2,1)} %refs_0_.5), channel_id=1, source_target_pairs={{0,8},{4,12},{8,0},{12,4},{16,24},{20,28},{24,16},{28,20},{1,9},{5... | collective-permute-start | bytes 3145736 | tf_op jit(solution)/shard_map/ppermute | solution.py:29
  3.6 1.5 collective-permute-start.6
  5.2 1.6 collective-permute-start
  6.7 2.6 %collective-permute-start.1 = (bf16[512,512]{1,0:T(8,128)(2,1)}, bf16[512,512]{1,0:T(8,128)(2,1)}, u32[]{:S(2)}, u32[]{:S(2)}) collective-permute-start(bf16[512,512]{1,0:T(8,128)(2,1)} %refs_0_.3), channel_id=1, source_target_pairs={{0,2},{1,3},{2,0},{3,1},{4,6},{5,7},{6,4},{7,5},{8,10},{9,11},{10,... | collective-permute-start | bytes 1572872 | tf_op jit(solution)/shard_map/ppermute | solution.py:29
  9.3 17.7 %collective-permute-done.4.refs_6_.refs_2_ = bf16[256,2048]{1,0:T(8,128)(2,1)S(1)} collective-permute-done((bf16[256,2048]{1,0:T(8,128)(2,1)}, bf16[256,2048]{1,0:T(8,128)(2,1)S(1)}, u32[]{:S(2)}, u32[]{:S(2)}) %collective-permute-start.4) | collective-permute-done | bytes 1048608 | tf_op jit(solution)/shard_map/ppermute | solution.py:29
  27.0 1.5 collective-permute-done.6.refs_8_.refs_4_
  29.2 1.5 collective-permute-start.8
  30.9 2.4 %collective-permute-done.1.refs_2_ = bf16[512,512]{1,0:T(8,128)(2,1)} collective-permute-done((bf16[512,512]{1,0:T(8,128)(2,1)}, bf16[512,512]{1,0:T(8,128)(2,1)}, u32[]{:S(2)}, u32[]{:S(2)}) %collective-permute-start.1) | collective-permute-done | bytes 524320 | tf_op jit(solution)/shard_map/ppermute | solution.py:29
  33.7 12.0 %collective-permute-done.2.refs_3_ = bf16[512,512]{1,0:T(8,128)(2,1)S(1)} collective-permute-done((bf16[512,512]{1,0:T(8,128)(2,1)}, bf16[512,512]{1,0:T(8,128)(2,1)S(1)}, u32[]{:S(2)}, u32[]{:S(2)}) %collective-permute-start.2) | collective-permute-done | bytes 524320 | tf_op jit(solution)/shard_map/ppermute | solution.py:29
  45.7 5.1 %shard_map.58 = (bf16[4,512,512]{2,1,0:T(8,128)(2,1)S(1)}, bf16[4,512,512]{2,1,0:T(8,128)(2,1)S(1)}, f32[512,2048]{1,0:T(8,128)S(1)}) custom-call(bf16[512,512]{1,0:T(8,128)(2,1)S(1)} %copy-done.11, bf16[512,512]{1,0:T(8,128)(2,1)} %collective-permute-done.refs_1_, bf16[512,512]{1,0:T(8,128)(2,1)} %collective-permute-done.1.refs_2_, ...), custom_call_target="tpu_custom_call" | custom-call | flops 1 | bytes 1 | tf_op jit(solution)/shard_map/pallas_call | solution.py:76
  51.0 2.6 %collective-permute-done.9.refs_1_.refs_7_ = bf16[256,2048]{1,0:T(8,128)(2,1)S(1)} collective-permute-done((bf16[256,2048]{1,0:T(8,128)(2,1)S(1)}, bf16[256,2048]{1,0:T(8,128)(2,1)S(1)}, u32[]{:S(2)}, u32[]{:S(2)}) %collective-permute-start.9) | collective-permute-done | bytes 1048608 | tf_op jit(solution)/shard_map/ppermute | solution.py:29
  53.6 2.4 %shard_map.59 = (f32[512,2048]{1,0:T(8,128)S(1)}, bf16[512,2048]{1,0:T(8,128)(2,1)S(1)}, f32[2,512]{1,0:T(2,128)S(1)}) custom-call(f32[512,2048]{1,0:T(8,128)S(1)} %get-tuple-element.42.logits_ref, bf16[4,512,512]{2,1,0:T(8,128)(2,1)S(1)} %get-tuple-element.43.blocks_ref, bf16[256,2048]{1,0:T(8,128)(2,1)S(1)} %collective-permute-done.8.refs_0_.refs_6_, ...), custom_call_target="tpu_custom_call" | custom-call | flops 1 | bytes 1 | tf_op jit(solution)/shard_map/pallas_call | solution.py:76
  56.0 3.6 %collective-permute-start.10 = (f32[2,512]{1,0:T(2,128)S(1)}, f32[2,512]{1,0:T(2,128)S(1)}, u32[]{:S(2)}, u32[]{:S(2)}) collective-permute-start(f32[2,512]{1,0:T(2,128)S(1)} %get-tuple-element.48), channel_id=1, source_target_pairs={{0,3},{1,2},{2,1},{3,0},{4,7},{5,6},{6,5},{7,4},{8,11},{9,10},{10,... | collective-permute-start | bytes 12296 | tf_op jit(solution)/shard_map/ppermute | solution.py:29
  61.5 2.6 %collective-permute-done.11 = f32[2,512]{1,0:T(2,128)S(1)} collective-permute-done((f32[2,512]{1,0:T(2,128)S(1)}, f32[2,512]{1,0:T(2,128)S(1)}, u32[]{:S(2)}, u32[]{:S(2)}) %collective-permute-start.11) | collective-permute-done | bytes 4128 | tf_op jit(solution)/shard_map/ppermute | solution.py:29
  64.9 1.2 collective-permute-done.13
  66.6 1.5 collective-permute-start.15
  68.2 1.5 collective-permute-start.16
  72.5 1.5 collective-permute-start.17
  74.6 2.3 %collective-permute-start.19 = (f32[1,512]{1,0:T(1,128)S(1)}, f32[1,512]{1,0:T(1,128)S(1)}, u32[]{:S(2)}, u32[]{:S(2)}) collective-permute-start(f32[1,512]{1,0:T(1,128)S(1)} %get-tuple-element.50), channel_id=1, source_target_pairs={{0,1},{1,0},{2,3},{3,2},{4,5},{5,4},{6,7},{7,6},{8,9},{9,8},{10,11... | collective-permute-start | bytes 6152 | tf_op jit(solution)/shard_map/ppermute | solution.py:29
  79.2 1.2 collective-permute-done.20
  80.4 1.5 collective-permute-start.21
  81.9 1.5 collective-permute-start.22
  84.0 1.1 collective-permute-done.21
  85.6 1.5 collective-permute-done.23
  87.7 2.6 %collective-permute-start.24 = (f32[1,512]{1,0:T(1,128)S(1)}, f32[1,512]{1,0:T(1,128)S(1)}, u32[]{:S(2)}, u32[]{:S(2)}) collective-permute-start(f32[1,512]{1,0:T(1,128)S(1)} %get-tuple-element.52), channel_id=1, source_target_pairs={{0,3},{1,2},{2,1},{3,0},{4,7},{5,6},{6,5},{7,4},{8,11},{9,10},{10,... | collective-permute-start | bytes 6152 | tf_op jit(solution)/shard_map/ppermute | solution.py:29
  93.2 1.7 collective-permute-done.25
  95.6 1.2 collective-permute-done.27
  97.4 1.5 collective-permute-start.29
  98.9 1.5 collective-permute-start.30
  100.4 1.1 collective-permute-done.28
  103.2 1.5 collective-permute-start.31
  105.6 2.0 %collective-permute-start.33 = (f32[1,512]{1,0:T(1,128)S(1)}, f32[1,512]{1,0:T(1,128)S(1)}, u32[]{:S(2)}, u32[]{:S(2)}) collective-permute-start(f32[1,512]{1,0:T(1,128)S(1)} %get-tuple-element.54), channel_id=1, source_target_pairs={{0,1},{1,0},{2,3},{3,2},{4,5},{5,4},{6,7},{7,6},{8,9},{9,8},{10,11... | collective-permute-start | bytes 6152 | tf_op jit(solution)/shard_map/ppermute | solution.py:29
  109.2 5.2 %shard_map.66 = (bf16[512,2048]{1,0:T(8,128)(2,1)S(1)}, bf16[512,2048]{1,0:T(8,128)(2,1)S(1)}, bf16[256,2048]{1,0:T(8,128)(2,1)S(1)}, bf16[256,2048]{1,0:T(8,128)(2,1)S(1)}, bf16[512,512]{1,0:T(8,128)(2,1)S(1)}) custom-call(f32[512,2048]{1,0:T(8,128)S(1)} %get-tuple-element.46.student_ref, bf16[512,2048]{1,0:T(8,128)(2,1)S(1)} %get-tuple-element.47.slope_ref, ...), custom_call_target="tpu_custom_call" | custom-call | flops 1 | bytes 1 | tf_op jit(solution)/shard_map/pallas_call | solution.py:76
  114.6 2.6 %collective-permute-done.34 = bf16[256,2048]{1,0:T(8,128)(2,1)S(1)} collective-permute-done((bf16[256,2048]{1,0:T(8,128)(2,1)S(1)}, bf16[256,2048]{1,0:T(8,128)(2,1)S(1)}, u32[]{:S(2)}, u32[]{:S(2)}) %collective-permute-start.34) | collective-permute-done | bytes 1048608 | tf_op jit(solution)/shard_map/ppermute | solution.py:29
  117.6 1.6 collective-permute-start.35
  119.2 2.0 %collective-permute-start.36 = (bf16[512,512]{1,0:T(8,128)(2,1)S(1)}, bf16[512,512]{1,0:T(8,128)(2,1)S(1)}, u32[]{:S(2)}, u32[]{:S(2)}) collective-permute-start(bf16[512,512]{1,0:T(8,128)(2,1)S(1)} %get-tuple-element.64), channel_id=1, source_target_pairs={{0,1},{1,0},{2,3},{3,2},{4,5},{5,4},{6,7},{7,6},{8,9},{9,8},{10,11... | collective-permute-start | bytes 1572872 | tf_op jit(solution)/shard_map/ppermute | solution.py:29
  121.2 9.0 %shard_map.67 = (bf16[256,2048]{1,0:T(8,128)(2,1)S(1)}, bf16[256,2048]{1,0:T(8,128)(2,1)}, bf16[256,2048]{1,0:T(8,128)(2,1)S(1)}, bf16[256,2048]{1,0:T(8,128)(2,1)}, bf16[4,512,512]{2,1,0:T(8,128)(2,1)S(1)}) custom-call(bf16[512,2048]{1,0:T(8,128)(2,1)S(1)} %get-tuple-element.57.grad_ref, bf16[4,512,512]{2,1,0:T(8,128)(2,1)S(1)} %get-tuple-element.55.turned_ref, ...), custom_call_target="tpu_custom_call" | custom-call | flops 1 | bytes 1 | tf_op jit(solution)/shard_map/pallas_call | solution.py:76
  134.0 3.1 %collective-permute-done.37 = bf16[256,2048]{1,0:T(8,128)(2,1)S(1)} collective-permute-done((bf16[256,2048]{1,0:T(8,128)(2,1)}, bf16[256,2048]{1,0:T(8,128)(2,1)S(1)}, u32[]{:S(2)}, u32[]{:S(2)}) %collective-permute-start.37) | collective-permute-done | bytes 1048608 | tf_op jit(solution)/shard_map/ppermute | solution.py:29
  138.0 3.4 %fusion.3 = (bf16[256,2048]{1,0:T(8,128)(2,1)S(1)}, bf16[256,2048]{1,0:T(8,128)(2,1)S(1)}) fusion(bf16[256,2048]{1,0:T(8,128)(2,1)} %collective-permute-done.35, bf16[256,2048]{1,0:T(8,128)(2,1)} %collective-permute-done.39, bf16[256,2048]{1,0:T(8,128)(2,1)} %copy-done.10, pred[]{:T(512)S(6)} %eq.11, pred[]{:T(512)S(6)} %eq.12, ...), kind=kLoop, calls=%fused_computation.5 | loop fusion | flops 6815744 | bytes 7340034 | tf_op jit(solution)/shard_map/convert_element_type | solution.py:367
  141.4 1.6 collective-permute-start.38
  143.8 1.3 shard_map.68
  145.1 2.1 %collective-permute-start.41 = (bf16[512,512]{1,0:T(8,128)(2,1)S(1)}, bf16[512,512]{1,0:T(8,128)(2,1)S(1)}, u32[]{:S(2)}, u32[]{:S(2)}) collective-permute-start(bf16[512,512]{1,0:T(8,128)(2,1)S(1)} %copy-done.13), channel_id=1, source_target_pairs={{0,1},{1,0},{2,3},{3,2},{4,5},{5,4},{6,7},{7,6},{8,9},{9,8},{10,11... | collective-permute-start | bytes 1572872 | tf_op jit(solution)/shard_map/ppermute | solution.py:29
  147.2 1.1 collective-permute-start.42
  148.3 1.3 copy.6
  149.7 20.2 %collective-permute-done.41 = bf16[512,512]{1,0:T(8,128)(2,1)S(1)} collective-permute-done((bf16[512,512]{1,0:T(8,128)(2,1)S(1)}, bf16[512,512]{1,0:T(8,128)(2,1)S(1)}, u32[]{:S(2)}, u32[]{:S(2)}) %collective-permute-start.41) | collective-permute-done | bytes 524320 | tf_op jit(solution)/shard_map/ppermute | solution.py:29
  169.8 3.6 %collective-permute-done.42 = bf16[512,512]{1,0:T(8,128)(2,1)S(1)} collective-permute-done((bf16[512,512]{1,0:T(8,128)(2,1)S(1)}, bf16[512,512]{1,0:T(8,128)(2,1)S(1)}, u32[]{:S(2)}, u32[]{:S(2)}) %collective-permute-start.42) | collective-permute-done | bytes 524320 | tf_op jit(solution)/shard_map/ppermute | solution.py:29
  173.4 2.0 %fusion.5 = bf16[512,512]{1,0:T(8,128)(2,1)} fusion(bf16[512,512]{1,0:T(8,128)(2,1)S(1)} %collective-permute-done.42, bf16[512,512]{1,0:T(8,128)(2,1)S(1)} %collective-permute-done.41, bf16[4,512,512]{2,1,0:T(8,128)(2,1)} %copy-done.8), kind=kLoop, calls=%fused_computation.10 | loop fusion | flops 1572864 | bytes 2097152 | tf_op jit(solution)/shard_map/convert_element_type | solution.py:354
  175.5 1.7 add_convert_fusion
  (116 shorter events, 26.6 us)
Async XLA Ops:
  0.6 45.1 %copy-start.4 = (bf16[256,2048]{1,0:T(8,128)(2,1)S(1)}, bf16[256,2048]{1,0:T(8,128)(2,1)}, u32[]{:S(2)}) copy-start(bf16[256,2048]{1,0:T(8,128)(2,1)} %refs_0_.5) | copy-start | bytes 3145732
  0.6 26.4 %collective-permute-start.4 = (bf16[256,2048]{1,0:T(8,128)(2,1)}, bf16[256,2048]{1,0:T(8,128)(2,1)S(1)}, u32[]{:S(2)}, u32[]{:S(2)}) collective-permute-start(bf16[256,2048]{1,0:T(8,128)(2,1)} %refs_0_.5), channel_id=1, source_target_pairs={{0,8},{4,12},{8,0},{12,4},{16,24},{20,28},{24,16},{28,20},{1,9},{5... | collective-permute-start | bytes 3145736 | tf_op jit(solution)/shard_map/ppermute | solution.py:29
  3.6 24.8 %collective-permute-start.6 = (bf16[256,2048]{1,0:T(8,128)(2,1)}, bf16[256,2048]{1,0:T(8,128)(2,1)S(1)}, u32[]{:S(2)}, u32[]{:S(2)}) collective-permute-start(bf16[256,2048]{1,0:T(8,128)(2,1)} %refs_0_.5), channel_id=1, source_target_pairs={{0,16},{4,20},{8,24},{12,28},{16,0},{20,4},{24,8},{28,12},{1,17},{... | collective-permute-start | bytes 3145736 | tf_op jit(solution)/shard_map/ppermute | solution.py:29
  5.2 23.4 %collective-permute-start.3 = (bf16[256,2048]{1,0:T(8,128)(2,1)}, bf16[256,2048]{1,0:T(8,128)(2,1)}, u32[]{:S(2)}, u32[]{:S(2)}) collective-permute-start(bf16[256,2048]{1,0:T(8,128)(2,1)} %refs_0_.5), channel_id=1, source_target_pairs={{0,4},{4,0},{8,12},{12,8},{16,20},{20,16},{24,28},{28,24},{1,5},{5... | collective-permute-start | bytes 3145736 | tf_op jit(solution)/shard_map/ppermute | solution.py:29
  5.2 25.8 %collective-permute-start = (bf16[512,512]{1,0:T(8,128)(2,1)}, bf16[512,512]{1,0:T(8,128)(2,1)}, u32[]{:S(2)}, u32[]{:S(2)}) collective-permute-start(bf16[512,512]{1,0:T(8,128)(2,1)} %refs_0_.3), channel_id=1, source_target_pairs={{0,1},{1,0},{2,3},{3,2},{4,5},{5,4},{6,7},{7,6},{8,9},{9,8},{10,11... | collective-permute-start | bytes 1572872 | tf_op jit(solution)/shard_map/ppermute | solution.py:29
  6.7 26.6 %collective-permute-start.1 = (bf16[512,512]{1,0:T(8,128)(2,1)}, bf16[512,512]{1,0:T(8,128)(2,1)}, u32[]{:S(2)}, u32[]{:S(2)}) collective-permute-start(bf16[512,512]{1,0:T(8,128)(2,1)} %refs_0_.3), channel_id=1, source_target_pairs={{0,2},{1,3},{2,0},{3,1},{4,6},{5,7},{6,4},{7,5},{8,10},{9,11},{10,... | collective-permute-start | bytes 1572872 | tf_op jit(solution)/shard_map/ppermute | solution.py:29
  9.3 36.4 %copy-start.11 = (bf16[512,512]{1,0:T(8,128)(2,1)S(1)}, bf16[512,512]{1,0:T(8,128)(2,1)}, u32[]{:S(2)}) copy-start(bf16[512,512]{1,0:T(8,128)(2,1)} %refs_0_.3) | copy-start | bytes 1572868
  28.5 22.4 %copy-start.2 = (bf16[256,2048]{1,0:T(8,128)(2,1)}, bf16[256,2048]{1,0:T(8,128)(2,1)S(1)}, u32[]{:S(2)}) copy-start(bf16[256,2048]{1,0:T(8,128)(2,1)S(1)} %collective-permute-done.6.refs_8_.refs_4_) | copy-start | bytes 3145732
  28.6 17.1 %collective-permute-start.5 = (bf16[256,2048]{1,0:T(8,128)(2,1)S(1)}, bf16[256,2048]{1,0:T(8,128)(2,1)S(1)}, u32[]{:S(2)}, u32[]{:S(2)}) collective-permute-start(bf16[256,2048]{1,0:T(8,128)(2,1)S(1)} %collective-permute-done.4.refs_6_.refs_2_), channel_id=1, source_target_pairs={{0,4},{4,0},{8,12},{12,8},{16,20},{20,16},{24,28},{28,24},{1,5},{5... | collective-permute-start | bytes 3145736 | tf_op jit(solution)/shard_map/ppermute | solution.py:29
  28.7 17.0 %collective-permute-start.7 = (bf16[256,2048]{1,0:T(8,128)(2,1)S(1)}, bf16[256,2048]{1,0:T(8,128)(2,1)S(1)}, u32[]{:S(2)}, u32[]{:S(2)}) collective-permute-start(bf16[256,2048]{1,0:T(8,128)(2,1)S(1)} %collective-permute-done.6.refs_8_.refs_4_), channel_id=1, source_target_pairs={{0,4},{4,0},{8,12},{12,8},{16,20},{20,16},{24,28},{28,24},{1,5},{5... | collective-permute-start | bytes 3145736 | tf_op jit(solution)/shard_map/ppermute | solution.py:29
  29.2 21.7 %collective-permute-start.8 = (bf16[256,2048]{1,0:T(8,128)(2,1)S(1)}, bf16[256,2048]{1,0:T(8,128)(2,1)S(1)}, u32[]{:S(2)}, u32[]{:S(2)}) collective-permute-start(bf16[256,2048]{1,0:T(8,128)(2,1)S(1)} %broadcast_select_fusion), channel_id=1, source_target_pairs={{0,16},{4,12},{8,24},{12,4},{16,0},{20,28},{24,8},{28,20},{1,17},{... | collective-permute-start | bytes 3145736 | tf_op jit(solution)/shard_map/ppermute | solution.py:34
  33.3 12.4 %collective-permute-start.2 = (bf16[512,512]{1,0:T(8,128)(2,1)}, bf16[512,512]{1,0:T(8,128)(2,1)S(1)}, u32[]{:S(2)}, u32[]{:S(2)}) collective-permute-start(bf16[512,512]{1,0:T(8,128)(2,1)} %collective-permute-done.1.refs_2_), channel_id=1, source_target_pairs={{0,1},{1,0},{2,3},{3,2},{4,5},{5,4},{6,7},{7,6},{8,9},{9,8},{10,11... | collective-permute-start | bytes 1572872 | tf_op jit(solution)/shard_map/ppermute | solution.py:29
  50.9 70.3 %copy-start = (bf16[4,512,512]{2,1,0:T(8,128)(2,1)}, bf16[4,512,512]{2,1,0:T(8,128)(2,1)S(1)}, u32[]{:S(2)}) copy-start(bf16[4,512,512]{2,1,0:T(8,128)(2,1)S(1)} %get-tuple-element.55.turned_ref) | copy-start | bytes 6291460
  50.9 2.7 %collective-permute-start.9 = (bf16[256,2048]{1,0:T(8,128)(2,1)S(1)}, bf16[256,2048]{1,0:T(8,128)(2,1)S(1)}, u32[]{:S(2)}, u32[]{:S(2)}) collective-permute-start(bf16[256,2048]{1,0:T(8,128)(2,1)S(1)} %collective-permute-done.8.refs_0_.refs_6_), channel_id=1, source_target_pairs={{0,4},{4,0},{8,12},{12,8},{16,20},{20,16},{24,28},{28,24},{1,5},{5... | collective-permute-start | bytes 3145736 | tf_op jit(solution)/shard_map/ppermute | solution.py:29
  56.0 5.5 %collective-permute-start.10 = (f32[2,512]{1,0:T(2,128)S(1)}, f32[2,512]{1,0:T(2,128)S(1)}, u32[]{:S(2)}, u32[]{:S(2)}) collective-permute-start(f32[2,512]{1,0:T(2,128)S(1)} %get-tuple-element.48), channel_id=1, source_target_pairs={{0,3},{1,2},{2,1},{3,0},{4,7},{5,6},{6,5},{7,4},{8,11},{9,10},{10,... | collective-permute-start | bytes 12296 | tf_op jit(solution)/shard_map/ppermute | solution.py:29
  59.6 4.5 %collective-permute-start.11 = (f32[2,512]{1,0:T(2,128)S(1)}, f32[2,512]{1,0:T(2,128)S(1)}, u32[]{:S(2)}, u32[]{:S(2)}) collective-permute-start(f32[2,512]{1,0:T(2,128)S(1)} %get-tuple-element.48), channel_id=1, source_target_pairs={{0,2},{1,3},{2,0},{3,1},{4,6},{5,7},{6,4},{7,5},{8,10},{9,11},{10,... | collective-permute-start | bytes 12296 | tf_op jit(solution)/shard_map/ppermute | solution.py:29
  59.6 4.5 %collective-permute-start.12 = (f32[2,512]{1,0:T(2,128)S(1)}, f32[2,512]{1,0:T(2,128)S(1)}, u32[]{:S(2)}, u32[]{:S(2)}) collective-permute-start(f32[2,512]{1,0:T(2,128)S(1)} %get-tuple-element.48), channel_id=1, source_target_pairs={{0,1},{1,0},{2,3},{3,2},{4,5},{5,4},{6,7},{7,6},{8,9},{9,8},{10,11... | collective-permute-start | bytes 12296 | tf_op jit(solution)/shard_map/ppermute | solution.py:29
  64.8 1.2 collective-permute-start.13
  66.1 4.6 %collective-permute-start.14 = (f32[1,2048]{1,0:T(1,128)S(1)}, f32[1,2048]{1,0:T(1,128)S(1)}, u32[]{:S(2)}, u32[]{:S(2)}) collective-permute-start(f32[1,2048]{1,0:T(1,128)S(1)} %add.114), channel_id=1, source_target_pairs={{0,24},{4,28},{8,16},{12,20},{16,8},{20,12},{24,0},{28,4},{1,25},{... | collective-permute-start | bytes 24584 | tf_op jit(solution)/shard_map/ppermute | solution.py:29
  66.6 4.1 %collective-permute-start.15 = (f32[1,2048]{1,0:T(1,128)S(1)}, f32[1,2048]{1,0:T(1,128)S(1)}, u32[]{:S(2)}, u32[]{:S(2)}) collective-permute-start(f32[1,2048]{1,0:T(1,128)S(1)} %add.114), channel_id=1, source_target_pairs={{0,16},{4,20},{8,24},{12,28},{16,0},{20,4},{24,8},{28,12},{1,17},{... | collective-permute-start | bytes 24584 | tf_op jit(solution)/shard_map/ppermute | solution.py:29
  68.2 3.7 %collective-permute-start.16 = (f32[1,2048]{1,0:T(1,128)S(1)}, f32[1,2048]{1,0:T(1,128)S(1)}, u32[]{:S(2)}, u32[]{:S(2)}) collective-permute-start(f32[1,2048]{1,0:T(1,128)S(1)} %add.114), channel_id=1, source_target_pairs={{0,8},{4,12},{8,0},{12,4},{16,24},{20,28},{24,16},{28,20},{1,9},{5... | collective-permute-start | bytes 24584 | tf_op jit(solution)/shard_map/ppermute | solution.py:29
  72.5 5.4 %collective-permute-start.17 = (f32[1,512]{1,0:T(1,128)S(1)}, f32[1,512]{1,0:T(1,128)S(1)}, u32[]{:S(2)}, u32[]{:S(2)}) collective-permute-start(f32[1,512]{1,0:T(1,128)S(1)} %get-tuple-element.50), channel_id=1, source_target_pairs={{0,3},{1,2},{2,1},{3,0},{4,7},{5,6},{6,5},{7,4},{8,11},{9,10},{10,... | collective-permute-start | bytes 6152 | tf_op jit(solution)/shard_map/ppermute | solution.py:29
  74.0 4.5 %collective-permute-start.18 = (f32[1,512]{1,0:T(1,128)S(1)}, f32[1,512]{1,0:T(1,128)S(1)}, u32[]{:S(2)}, u32[]{:S(2)}) collective-permute-start(f32[1,512]{1,0:T(1,128)S(1)} %get-tuple-element.50), channel_id=1, source_target_pairs={{0,2},{1,3},{2,0},{3,1},{4,6},{5,7},{6,4},{7,5},{8,10},{9,11},{10,... | collective-permute-start | bytes 6152 | tf_op jit(solution)/shard_map/ppermute | solution.py:29
  74.6 3.9 %collective-permute-start.19 = (f32[1,512]{1,0:T(1,128)S(1)}, f32[1,512]{1,0:T(1,128)S(1)}, u32[]{:S(2)}, u32[]{:S(2)}) collective-permute-start(f32[1,512]{1,0:T(1,128)S(1)} %get-tuple-element.50), channel_id=1, source_target_pairs={{0,1},{1,0},{2,3},{3,2},{4,5},{5,4},{6,7},{7,6},{8,9},{9,8},{10,11... | collective-permute-start | bytes 6152 | tf_op jit(solution)/shard_map/ppermute | solution.py:29
  79.2 1.2 collective-permute-start.20
  80.4 4.6 %collective-permute-start.21 = (f32[1,2048]{1,0:T(1,128)S(1)}, f32[1,2048]{1,0:T(1,128)S(1)}, u32[]{:S(2)}, u32[]{:S(2)}) collective-permute-start(f32[1,2048]{1,0:T(1,128)S(1)} %add.121), channel_id=1, source_target_pairs={{0,24},{4,28},{8,16},{12,20},{16,8},{20,12},{24,0},{28,4},{1,25},{... | collective-permute-start | bytes 24584 | tf_op jit(solution)/shard_map/ppermute | solution.py:29
  81.9 3.7 %collective-permute-start.22 = (f32[1,2048]{1,0:T(1,128)S(1)}, f32[1,2048]{1,0:T(1,128)S(1)}, u32[]{:S(2)}, u32[]{:S(2)}) collective-permute-start(f32[1,2048]{1,0:T(1,128)S(1)} %add.121), channel_id=1, source_target_pairs={{0,16},{4,20},{8,24},{12,28},{16,0},{20,4},{24,8},{28,12},{1,17},{... | collective-permute-start | bytes 24584 | tf_op jit(solution)/shard_map/ppermute | solution.py:29
  83.4 3.7 %collective-permute-start.23 = (f32[1,2048]{1,0:T(1,128)S(1)}, f32[1,2048]{1,0:T(1,128)S(1)}, u32[]{:S(2)}, u32[]{:S(2)}) collective-permute-start(f32[1,2048]{1,0:T(1,128)S(1)} %add.121), channel_id=1, source_target_pairs={{0,8},{4,12},{8,0},{12,4},{16,24},{20,28},{24,16},{28,20},{1,9},{5... | collective-permute-start | bytes 24584 | tf_op jit(solution)/shard_map/ppermute | solution.py:29
  87.7 5.4 %collective-permute-start.24 = (f32[1,512]{1,0:T(1,128)S(1)}, f32[1,512]{1,0:T(1,128)S(1)}, u32[]{:S(2)}, u32[]{:S(2)}) collective-permute-start(f32[1,512]{1,0:T(1,128)S(1)} %get-tuple-element.52), channel_id=1, source_target_pairs={{0,3},{1,2},{2,1},{3,0},{4,7},{5,6},{6,5},{7,4},{8,11},{9,10},{10,... | collective-permute-start | bytes 6152 | tf_op jit(solution)/shard_map/ppermute | solution.py:29
  90.4 4.5 %collective-permute-start.25 = (f32[1,512]{1,0:T(1,128)S(1)}, f32[1,512]{1,0:T(1,128)S(1)}, u32[]{:S(2)}, u32[]{:S(2)}) collective-permute-start(f32[1,512]{1,0:T(1,128)S(1)} %get-tuple-element.52), channel_id=1, source_target_pairs={{0,2},{1,3},{2,0},{3,1},{4,6},{5,7},{6,4},{7,5},{8,10},{9,11},{10,... | collective-permute-start | bytes 6152 | tf_op jit(solution)/shard_map/ppermute | solution.py:29
  91.3 3.6 %collective-permute-start.26 = (f32[1,512]{1,0:T(1,128)S(1)}, f32[1,512]{1,0:T(1,128)S(1)}, u32[]{:S(2)}, u32[]{:S(2)}) collective-permute-start(f32[1,512]{1,0:T(1,128)S(1)} %get-tuple-element.52), channel_id=1, source_target_pairs={{0,1},{1,0},{2,3},{3,2},{4,5},{5,4},{6,7},{7,6},{8,9},{9,8},{10,11... | collective-permute-start | bytes 6152 | tf_op jit(solution)/shard_map/ppermute | solution.py:29
  95.6 1.2 collective-permute-start.27
  96.8 4.6 %collective-permute-start.28 = (f32[1,2048]{1,0:T(1,128)S(1)}, f32[1,2048]{1,0:T(1,128)S(1)}, u32[]{:S(2)}, u32[]{:S(2)}) collective-permute-start(f32[1,2048]{1,0:T(1,128)S(1)} %add.128), channel_id=1, source_target_pairs={{0,24},{4,28},{8,16},{12,20},{16,8},{20,12},{24,0},{28,4},{1,25},{... | collective-permute-start | bytes 24584 | tf_op jit(solution)/shard_map/ppermute | solution.py:29
  97.4 4.1 %collective-permute-start.29 = (f32[1,2048]{1,0:T(1,128)S(1)}, f32[1,2048]{1,0:T(1,128)S(1)}, u32[]{:S(2)}, u32[]{:S(2)}) collective-permute-start(f32[1,2048]{1,0:T(1,128)S(1)} %add.128), channel_id=1, source_target_pairs={{0,16},{4,20},{8,24},{12,28},{16,0},{20,4},{24,8},{28,12},{1,17},{... | collective-permute-start | bytes 24584 | tf_op jit(solution)/shard_map/ppermute | solution.py:29
  98.9 3.7 %collective-permute-start.30 = (f32[1,2048]{1,0:T(1,128)S(1)}, f32[1,2048]{1,0:T(1,128)S(1)}, u32[]{:S(2)}, u32[]{:S(2)}) collective-permute-start(f32[1,2048]{1,0:T(1,128)S(1)} %add.128), channel_id=1, source_target_pairs={{0,8},{4,12},{8,0},{12,4},{16,24},{20,28},{24,16},{28,20},{1,9},{5... | collective-permute-start | bytes 24584 | tf_op jit(solution)/shard_map/ppermute | solution.py:29
  103.2 5.4 %collective-permute-start.31 = (f32[1,512]{1,0:T(1,128)S(1)}, f32[1,512]{1,0:T(1,128)S(1)}, u32[]{:S(2)}, u32[]{:S(2)}) collective-permute-start(f32[1,512]{1,0:T(1,128)S(1)} %get-tuple-element.54), channel_id=1, source_target_pairs={{0,3},{1,2},{2,1},{3,0},{4,7},{5,6},{6,5},{7,4},{8,11},{9,10},{10,... | collective-permute-start | bytes 6152 | tf_op jit(solution)/shard_map/ppermute | solution.py:29
  104.7 4.5 %collective-permute-start.32 = (f32[1,512]{1,0:T(1,128)S(1)}, f32[1,512]{1,0:T(1,128)S(1)}, u32[]{:S(2)}, u32[]{:S(2)}) collective-permute-start(f32[1,512]{1,0:T(1,128)S(1)} %get-tuple-element.54), channel_id=1, source_target_pairs={{0,2},{1,3},{2,0},{3,1},{4,6},{5,7},{6,4},{7,5},{8,10},{9,11},{10,... | collective-permute-start | bytes 6152 | tf_op jit(solution)/shard_map/ppermute | solution.py:29
  105.6 3.6 %collective-permute-start.33 = (f32[1,512]{1,0:T(1,128)S(1)}, f32[1,512]{1,0:T(1,128)S(1)}, u32[]{:S(2)}, u32[]{:S(2)}) collective-permute-start(f32[1,512]{1,0:T(1,128)S(1)} %get-tuple-element.54), channel_id=1, source_target_pairs={{0,1},{1,0},{2,3},{3,2},{4,5},{5,4},{6,7},{7,6},{8,9},{9,8},{10,11... | collective-permute-start | bytes 6152 | tf_op jit(solution)/shard_map/ppermute | solution.py:29
  114.5 2.7 %collective-permute-start.34 = (bf16[256,2048]{1,0:T(8,128)(2,1)S(1)}, bf16[256,2048]{1,0:T(8,128)(2,1)S(1)}, u32[]{:S(2)}, u32[]{:S(2)}) collective-permute-start(bf16[256,2048]{1,0:T(8,128)(2,1)S(1)} %get-tuple-element.59), channel_id=1, source_target_pairs={{0,4},{4,0},{8,12},{12,8},{16,20},{20,16},{24,28},{28,24},{1,5},{5... | collective-permute-start | bytes 3145736 | tf_op jit(solution)/shard_map/ppermute | solution.py:29
  117.6 15.0 %collective-permute-start.35 = (bf16[256,2048]{1,0:T(8,128)(2,1)S(1)}, bf16[256,2048]{1,0:T(8,128)(2,1)}, u32[]{:S(2)}, u32[]{:S(2)}) collective-permute-start(bf16[256,2048]{1,0:T(8,128)(2,1)S(1)} %add_convert_fusion.1.refs_8_), channel_id=1, source_target_pairs={{0,8},{4,20},{8,0},{12,28},{16,24},{20,4},{24,16},{28,12},{1,9},{5... | collective-permute-start | bytes 3145736 | tf_op jit(solution)/shard_map/ppermute | solution.py:34
  119.2 13.0 %collective-permute-start.36 = (bf16[512,512]{1,0:T(8,128)(2,1)S(1)}, bf16[512,512]{1,0:T(8,128)(2,1)S(1)}, u32[]{:S(2)}, u32[]{:S(2)}) collective-permute-start(bf16[512,512]{1,0:T(8,128)(2,1)S(1)} %get-tuple-element.64), channel_id=1, source_target_pairs={{0,1},{1,0},{2,3},{3,2},{4,5},{5,4},{6,7},{7,6},{8,9},{9,8},{10,11... | collective-permute-start | bytes 1572872 | tf_op jit(solution)/shard_map/ppermute | solution.py:29
  133.5 3.6 %collective-permute-start.37 = (bf16[256,2048]{1,0:T(8,128)(2,1)}, bf16[256,2048]{1,0:T(8,128)(2,1)S(1)}, u32[]{:S(2)}, u32[]{:S(2)}) collective-permute-start(bf16[256,2048]{1,0:T(8,128)(2,1)} %get-tuple-element.68), channel_id=1, source_target_pairs={{0,4},{4,0},{8,12},{12,8},{16,20},{20,16},{24,28},{28,24},{1,5},{5... | collective-permute-start | bytes 3145736 | tf_op jit(solution)/shard_map/ppermute | solution.py:29
  133.5 4.5 %collective-permute-start.39 = (bf16[256,2048]{1,0:T(8,128)(2,1)}, bf16[256,2048]{1,0:T(8,128)(2,1)}, u32[]{:S(2)}, u32[]{:S(2)}) collective-permute-start(bf16[256,2048]{1,0:T(8,128)(2,1)} %get-tuple-element.71), channel_id=1, source_target_pairs={{0,4},{4,0},{8,12},{12,8},{16,20},{20,16},{24,28},{28,24},{1,5},{5... | collective-permute-start | bytes 3145736 | tf_op jit(solution)/shard_map/ppermute | solution.py:29
  141.4 34.0 %collective-permute-start.38 = (bf16[256,2048]{1,0:T(8,128)(2,1)S(1)}, bf16[256,2048]{1,0:T(8,128)(2,1)S(1)}, u32[]{:S(2)}, u32[]{:S(2)}) collective-permute-start(bf16[256,2048]{1,0:T(8,128)(2,1)S(1)} %get-tuple-element.80.refs_0_), channel_id=1, source_target_pairs={{0,8},{4,12},{8,0},{12,4},{16,24},{20,28},{24,16},{28,20},{1,9},{5... | collective-permute-start | bytes 3145736 | tf_op jit(solution)/shard_map/ppermute | solution.py:29
  143.0 32.5 %collective-permute-start.40 = (bf16[256,2048]{1,0:T(8,128)(2,1)S(1)}, bf16[256,2048]{1,0:T(8,128)(2,1)S(1)}, u32[]{:S(2)}, u32[]{:S(2)}) collective-permute-start(bf16[256,2048]{1,0:T(8,128)(2,1)S(1)} %get-tuple-element.79.refs_1_), channel_id=1, source_target_pairs={{0,16},{4,20},{8,24},{12,28},{16,0},{20,4},{24,8},{28,12},{1,17},{... | collective-permute-start | bytes 3145736 | tf_op jit(solution)/shard_map/ppermute | solution.py:29
  145.1 30.4 %collective-permute-start.43 = (bf16[256,2048]{1,0:T(8,128)(2,1)S(1)}, bf16[256,2048]{1,0:T(8,128)(2,1)S(1)}, u32[]{:S(2)}, u32[]{:S(2)}) collective-permute-start(bf16[256,2048]{1,0:T(8,128)(2,1)S(1)} %get-tuple-element.76), channel_id=1, source_target_pairs={{0,4},{4,0},{8,12},{12,8},{16,20},{20,16},{24,28},{28,24},{1,5},{5... | collective-permute-start | bytes 3145736 | tf_op jit(solution)/shard_map/ppermute | solution.py:29
  145.1 24.7 %collective-permute-start.41 = (bf16[512,512]{1,0:T(8,128)(2,1)S(1)}, bf16[512,512]{1,0:T(8,128)(2,1)S(1)}, u32[]{:S(2)}, u32[]{:S(2)}) collective-permute-start(bf16[512,512]{1,0:T(8,128)(2,1)S(1)} %copy-done.13), channel_id=1, source_target_pairs={{0,1},{1,0},{2,3},{3,2},{4,5},{5,4},{6,7},{7,6},{8,9},{9,8},{10,11... | collective-permute-start | bytes 1572872 | tf_op jit(solution)/shard_map/ppermute | solution.py:29
  147.2 26.2 %collective-permute-start.42 = (bf16[512,512]{1,0:T(8,128)(2,1)S(1)}, bf16[512,512]{1,0:T(8,128)(2,1)S(1)}, u32[]{:S(2)}, u32[]{:S(2)}) collective-permute-start(bf16[512,512]{1,0:T(8,128)(2,1)S(1)} %copy-done.12), channel_id=1, source_target_pairs={{0,2},{1,3},{2,0},{3,1},{4,6},{5,7},{6,4},{7,5},{8,10},{9,11},{10,... | collective-permute-start | bytes 1572872 | tf_op jit(solution)/shard_map/ppermute | solution.py:29
  (11 other events, 61.6 us)

commit v14 on v11

--- a/solution.py
+++ b/solution.py
@@ -233,6 +233,7 @@
 
 
 def near_kernel(depth, near, grad_ref, turned_ref, *refs):
+    refs = refs[len(refs) - 2 * len(near) :]
     me, place = lax.axis_index("sample"), lax.axis_index("cls")
     chip, core = me // 2, me % 2
     columns = grad_ref.shape[1]
@@ -337,7 +338,7 @@
     pairs = call(
         functools.partial(near_kernel, depth, [mask // 2 for mask in near]),
         [((depth, classes), bf16)] * (2 * len(near)),
-        [grad, turned],
+        [grad, turned] + head_list,
     )
     theirs, *pairs = lax.optimization_barrier((theirs, *pairs))
     block = lax.optimization_barrier((wide(mine) + wide(theirs)).astype(bf16))

time: 177 us -> 179 us (1.011)
  Pallas kernels: 28.2 us -> 30.1 us
    pallas_call x12, Pallas kernels: 28.2 us -> 30.1 us  [call(): pl.pallas_call(kernel, out_shape=tuple((jax.ShapeDtypeStruct(shape, dtype...]
  transfers between devices with their start and end apart: 44 -> 44, of which waited for: 26 -> 25; matrix products, arithmetic and copies ran while one was open for 1% -> 1% of each run, Pallas kernels for 9% -> 10%
where the time goes in v14:
time: 179 us
  waiting for transfers between devices  83.8 us (47%)
  starting transfers between devices  46.1 us (26%)
  Pallas kernels  30.1 us (17%)
  other arithmetic  8.97 us (5%)
  local copies, waits for them, and re-layouts  8.84 us (5%)
    ppermute x42, waiting for transfers between devices, flip(): lax.ppermute(value, axis, [(i, i ^ mask) for i in range(lax.axis_size(axi...  83.8 us
    ppermute x42, starting transfers between devices, flip(): lax.ppermute(value, axis, [(i, i ^ mask) for i in range(lax.axis_size(axi...  45.1 us
    pallas_call x12, Pallas kernels, call(): pl.pallas_call(kernel, out_shape=tuple((jax.ShapeDtypeStruct(shape, dtype...  30.1 us
    unnamed x42, local copies, waits for them, and re-layouts  8.8 us
  transfers between devices with their start and end apart: 44, of which 25 were waited for; matrix products, arithmetic and copies ran while one was open for 1% of the time, Pallas kernels for 10%

profile of v14, /device:TPU:0, one launch (start us, length us, event | category | flops | bytes accessed | tf_op | source)
XLA Modules:
  0.0 178.9 jit_solution(5335378769115321531)
XLA Ops:
  0.6 3.0 %collective-permute-start.4 = (bf16[256,2048]{1,0:T(8,128)(2,1)}, bf16[256,2048]{1,0:T(8,128)(2,1)S(1)}, u32[]{:S(2)}, u32[]{:S(2)}) collective-permute-start(bf16[256,2048]{1,0:T(8,128)(2,1)} %refs_0_.7), channel_id=1, source_target_pairs={{0,8},{4,12},{8,0},{12,4},{16,24},{20,28},{24,16},{28,20},{1,9},{5... | collective-permute-start | bytes 3145736 | tf_op jit(solution)/shard_map/ppermute | solution.py:29
  3.6 1.5 collective-permute-start.5
  5.2 2.6 %collective-permute-start.1 = (bf16[512,512]{1,0:T(8,128)(2,1)}, bf16[512,512]{1,0:T(8,128)(2,1)}, u32[]{:S(2)}, u32[]{:S(2)}) collective-permute-start(bf16[512,512]{1,0:T(8,128)(2,1)} %refs_0_.4), channel_id=1, source_target_pairs={{0,2},{1,3},{2,0},{3,1},{4,6},{5,7},{6,4},{7,5},{8,10},{9,11},{10,... | collective-permute-start | bytes 1572872 | tf_op jit(solution)/shard_map/ppermute | solution.py:29
  7.8 1.6 collective-permute-start
  9.3 21.5 %collective-permute-done.1.refs_2_ = bf16[512,512]{1,0:T(8,128)(2,1)} collective-permute-done((bf16[512,512]{1,0:T(8,128)(2,1)}, bf16[512,512]{1,0:T(8,128)(2,1)}, u32[]{:S(2)}, u32[]{:S(2)}) %collective-permute-start.1) | collective-permute-done | bytes 524320 | tf_op jit(solution)/shard_map/ppermute | solution.py:29
  31.5 1.1 collective-permute-done.refs_1_
  33.0 13.5 %collective-permute-done.2.refs_3_ = bf16[512,512]{1,0:T(8,128)(2,1)S(1)} collective-permute-done((bf16[512,512]{1,0:T(8,128)(2,1)}, bf16[512,512]{1,0:T(8,128)(2,1)S(1)}, u32[]{:S(2)}, u32[]{:S(2)}) %collective-permute-start.2) | collective-permute-done | bytes 524320 | tf_op jit(solution)/shard_map/ppermute | solution.py:29
  46.6 5.8 %shard_map.58 = (bf16[4,512,512]{2,1,0:T(8,128)(2,1)S(1)}, f32[512,2048]{1,0:T(8,128)S(1)}) custom-call(bf16[512,512]{1,0:T(8,128)(2,1)S(1)} %copy-done.17, bf16[512,512]{1,0:T(8,128)(2,1)} %collective-permute-done.refs_1_, bf16[512,512]{1,0:T(8,128)(2,1)} %collective-permute-done.1.refs_2_, bf16[512,512]{1,0:T(8,128)(2,1)S(1)} %collective-permute-done.2.refs_3_, ...), custom_call_target="tpu_custom_call" | custom-call | flops 1 | bytes 1 | tf_op jit(solution)/shard_map/pallas_call | solution.py:73
  52.5 2.6 %collective-permute-done.9.refs_1_.refs_7_ = bf16[256,2048]{1,0:T(8,128)(2,1)S(1)} collective-permute-done((bf16[256,2048]{1,0:T(8,128)(2,1)S(1)}, bf16[256,2048]{1,0:T(8,128)(2,1)S(1)}, u32[]{:S(2)}, u32[]{:S(2)}) %collective-permute-start.9) | collective-permute-done | bytes 1048608 | tf_op jit(solution)/shard_map/ppermute | solution.py:29
  55.2 2.5 %shard_map.59 = (f32[512,2048]{1,0:T(8,128)S(1)}, bf16[512,2048]{1,0:T(8,128)(2,1)S(1)}, f32[2,512]{1,0:T(2,128)S(1)}) custom-call(f32[512,2048]{1,0:T(8,128)S(1)} %get-tuple-element.47.logits_ref, bf16[4,512,512]{2,1,0:T(8,128)(2,1)S(1)} %get-tuple-element.48.blocks_ref, bf16[256,2048]{1,0:T(8,128)(2,1)S(1)} %collective-permute-done.8.refs_0_.refs_6_, ...), custom_call_target="tpu_custom_call" | custom-call | flops 1 | bytes 1 | tf_op jit(solution)/shard_map/pallas_call | solution.py:73
  57.7 2.9 %collective-permute-start.10 = (f32[2,512]{1,0:T(2,128)S(1)}, f32[2,512]{1,0:T(2,128)S(1)}, u32[]{:S(2)}, u32[]{:S(2)}) collective-permute-start(f32[2,512]{1,0:T(2,128)S(1)} %get-tuple-element.53), channel_id=1, source_target_pairs={{0,3},{1,2},{2,1},{3,0},{4,7},{5,6},{6,5},{7,4},{8,11},{9,10},{10,... | collective-permute-start | bytes 12296 | tf_op jit(solution)/shard_map/ppermute | solution.py:29
  60.6 1.5 collective-permute-start.12
  63.1 1.9 %collective-permute-done.11 = f32[2,512]{1,0:T(2,128)S(1)} collective-permute-done((f32[2,512]{1,0:T(2,128)S(1)}, f32[2,512]{1,0:T(2,128)S(1)}, u32[]{:S(2)}, u32[]{:S(2)}) %collective-permute-start.11) | collective-permute-done | bytes 4128 | tf_op jit(solution)/shard_map/ppermute | solution.py:29
  65.9 1.2 collective-permute-done.13
  67.1 1.5 collective-permute-start.14
  68.6 1.5 collective-permute-start.15
  72.2 1.5 collective-permute-done.16
  74.4 1.5 collective-permute-start.17
  76.5 2.3 %collective-permute-start.19 = (f32[1,512]{1,0:T(1,128)S(1)}, f32[1,512]{1,0:T(1,128)S(1)}, u32[]{:S(2)}, u32[]{:S(2)}) collective-permute-start(f32[1,512]{1,0:T(1,128)S(1)} %get-tuple-element.55), channel_id=1, source_target_pairs={{0,1},{1,0},{2,3},{3,2},{4,5},{5,4},{6,7},{7,6},{8,9},{9,8},{10,11... | collective-permute-start | bytes 6152 | tf_op jit(solution)/shard_map/ppermute | solution.py:29
  81.2 1.2 collective-permute-done.20
  82.9 1.5 collective-permute-start.22
  84.4 1.5 collective-permute-start.23
  88.7 2.6 %collective-permute-start.24 = (f32[1,512]{1,0:T(1,128)S(1)}, f32[1,512]{1,0:T(1,128)S(1)}, u32[]{:S(2)}, u32[]{:S(2)}) collective-permute-start(f32[1,512]{1,0:T(1,128)S(1)} %get-tuple-element.57), channel_id=1, source_target_pairs={{0,3},{1,2},{2,1},{3,0},{4,7},{5,6},{6,5},{7,4},{8,11},{9,10},{10,... | collective-permute-start | bytes 6152 | tf_op jit(solution)/shard_map/ppermute | solution.py:29
  94.2 1.7 collective-permute-done.25
  96.6 1.2 collective-permute-done.27
  97.8 1.5 collective-permute-start.28
  99.3 1.5 collective-permute-start.29
  102.9 1.5 collective-permute-done.30
  105.1 1.5 collective-permute-start.31
  107.5 2.0 %collective-permute-start.33 = (f32[1,512]{1,0:T(1,128)S(1)}, f32[1,512]{1,0:T(1,128)S(1)}, u32[]{:S(2)}, u32[]{:S(2)}) collective-permute-start(f32[1,512]{1,0:T(1,128)S(1)} %get-tuple-element.59), channel_id=1, source_target_pairs={{0,1},{1,0},{2,3},{3,2},{4,5},{5,4},{6,7},{7,6},{8,9},{9,8},{10,11... | collective-permute-start | bytes 6152 | tf_op jit(solution)/shard_map/ppermute | solution.py:29
  111.1 6.0 %shard_map.67 = (bf16[512,2048]{1,0:T(8,128)(2,1)}, bf16[512,2048]{1,0:T(8,128)(2,1)S(1)}, bf16[256,2048]{1,0:T(8,128)(2,1)S(1)}, bf16[256,2048]{1,0:T(8,128)(2,1)S(1)}, bf16[512,512]{1,0:T(8,128)(2,1)}) custom-call(f32[512,2048]{1,0:T(8,128)S(1)} %get-tuple-element.51.student_ref, bf16[512,2048]{1,0:T(8,128)(2,1)S(1)} %get-tuple-element.52.slope_ref, ...), custom_call_target="tpu_custom_call" | custom-call | flops 1 | bytes 1 | tf_op jit(solution)/shard_map/pallas_call | solution.py:73
  117.3 5.4 %shard_map.68 = (bf16[256,2048]{1,0:T(8,128)(2,1)S(1)}, bf16[256,2048]{1,0:T(8,128)(2,1)}, bf16[256,2048]{1,0:T(8,128)(2,1)S(1)}, bf16[256,2048]{1,0:T(8,128)(2,...) custom-call(bf16[512,2048]{1,0:T(8,128)(2,1)S(1)} %get-tuple-element.62.grad_ref, ...), custom_call_target="tpu_custom_call" | custom-call | flops 1 | bytes 1 | tf_op jit(solution)/shard_map/pallas_call | solution.py:73
  124.7 1.7 add_convert_fusion.1.refs_8_
  127.4 2.0 %collective-permute-start.35 = (bf16[512,512]{1,0:T(8,128)(2,1)}, bf16[512,512]{1,0:T(8,128)(2,1)}, u32[]{:S(2)}, u32[]{:S(2)}) collective-permute-start(bf16[512,512]{1,0:T(8,128)(2,1)} %get-tuple-element.72), channel_id=1, source_target_pairs={{0,1},{1,0},{2,3},{3,2},{4,5},{5,4},{6,7},{7,6},{8,9},{9,8},{10,11... | collective-permute-start | bytes 1572872 | tf_op jit(solution)/shard_map/ppermute | solution.py:29
  129.4 1.2 copy-done.2
  130.7 1.2 copy-done.4
  131.9 1.2 copy-done.6
  133.1 1.2 copy-done.8
  134.3 1.6 copy-done.10
  135.9 5.9 %shard_map.69 = bf16[4,512,512]{2,1,0:T(8,128)(2,1)S(1)} custom-call(bf16[512,2048]{1,0:T(8,128)(2,1)S(1)} %copy-done.10, bf16[256,2048]{1,0:T(8,128)(2,1)S(1)} %copy-done, bf16[256,2048]{1,0:T(8,128)(2,1)} %collective-permute-done.3.refs_5_.refs_1_, bf16[256,2048]{1,0:T(8,128)(2,1)S(1)} %collective-permute-done.4.refs_6_.refs_2_, ...), custom_call_target="tpu_custom_call" | custom-call | flops 1 | bytes 1 | tf_op jit(solution)/shard_map/pallas_call | solution.py:73
  141.9 1.3 fusion.6
  143.5 3.0 %fusion.3 = (bf16[256,2048]{1,0:T(8,128)(2,1)S(1)}, bf16[256,2048]{1,0:T(8,128)(2,1)S(1)}) fusion(bf16[256,2048]{1,0:T(8,128)(2,1)} %collective-permute-done.38, bf16[256,2048]{1,0:T(8,128)(2,1)} %collective-permute-done.37, bf16[256,2048]{1,0:T(8,128)(2,1)S(1)} %copy-done.16, pred[]{:T(512)S(6)} %eq.11, pred[]{:T(512)S(6)} %eq.12, ...), kind=kLoop, calls=%fused_computation.5 | loop fusion | flops 6815744 | bytes 7340034 | tf_op jit(solution)/shard_map/convert_element_type | solution.py:376
  146.6 1.6 collective-permute-start.39
  148.6 1.4 collective-permute-start.41
  150.0 1.1 collective-permute-start.42
  151.1 22.0 %collective-permute-done.41 = bf16[512,512]{1,0:T(8,128)(2,1)S(1)} collective-permute-done((bf16[512,512]{1,0:T(8,128)(2,1)S(1)}, bf16[512,512]{1,0:T(8,128)(2,1)S(1)}, u32[]{:S(2)}, u32[]{:S(2)}) %collective-permute-start.41) | collective-permute-done | bytes 524320 | tf_op jit(solution)/shard_map/ppermute | solution.py:29
  173.1 3.2 %collective-permute-done.42 = bf16[512,512]{1,0:T(8,128)(2,1)S(1)} collective-permute-done((bf16[512,512]{1,0:T(8,128)(2,1)S(1)}, bf16[512,512]{1,0:T(8,128)(2,1)S(1)}, u32[]{:S(2)}, u32[]{:S(2)}) %collective-permute-start.42) | collective-permute-done | bytes 524320 | tf_op jit(solution)/shard_map/ppermute | solution.py:29
  177.2 1.7 add_convert_fusion
  (128 shorter events, 25.9 us)
Async XLA Ops:
  0.6 30.2 %collective-permute-start.4 = (bf16[256,2048]{1,0:T(8,128)(2,1)}, bf16[256,2048]{1,0:T(8,128)(2,1)S(1)}, u32[]{:S(2)}, u32[]{:S(2)}) collective-permute-start(bf16[256,2048]{1,0:T(8,128)(2,1)} %refs_0_.7), channel_id=1, source_target_pairs={{0,8},{4,12},{8,0},{12,4},{16,24},{20,28},{24,16},{28,20},{1,9},{5... | collective-permute-start | bytes 3145736 | tf_op jit(solution)/shard_map/ppermute | solution.py:29
  3.6 27.2 %collective-permute-start.5 = (bf16[256,2048]{1,0:T(8,128)(2,1)}, bf16[256,2048]{1,0:T(8,128)(2,1)S(1)}, u32[]{:S(2)}, u32[]{:S(2)}) collective-permute-start(bf16[256,2048]{1,0:T(8,128)(2,1)} %refs_0_.7), channel_id=1, source_target_pairs={{0,16},{4,20},{8,24},{12,28},{16,0},{20,4},{24,8},{28,12},{1,17},{... | collective-permute-start | bytes 3145736 | tf_op jit(solution)/shard_map/ppermute | solution.py:29
  5.2 25.7 %collective-permute-start.1 = (bf16[512,512]{1,0:T(8,128)(2,1)}, bf16[512,512]{1,0:T(8,128)(2,1)}, u32[]{:S(2)}, u32[]{:S(2)}) collective-permute-start(bf16[512,512]{1,0:T(8,128)(2,1)} %refs_0_.4), channel_id=1, source_target_pairs={{0,2},{1,3},{2,0},{3,1},{4,6},{5,7},{6,4},{7,5},{8,10},{9,11},{10,... | collective-permute-start | bytes 1572872 | tf_op jit(solution)/shard_map/ppermute | solution.py:29
  7.8 24.8 %collective-permute-start.3 = (bf16[256,2048]{1,0:T(8,128)(2,1)}, bf16[256,2048]{1,0:T(8,128)(2,1)}, u32[]{:S(2)}, u32[]{:S(2)}) collective-permute-start(bf16[256,2048]{1,0:T(8,128)(2,1)} %refs_0_.7), channel_id=1, source_target_pairs={{0,4},{4,0},{8,12},{12,8},{16,20},{20,16},{24,28},{28,24},{1,5},{5... | collective-permute-start | bytes 3145736 | tf_op jit(solution)/shard_map/ppermute | solution.py:29
  7.8 24.8 %collective-permute-start = (bf16[512,512]{1,0:T(8,128)(2,1)}, bf16[512,512]{1,0:T(8,128)(2,1)}, u32[]{:S(2)}, u32[]{:S(2)}) collective-permute-start(bf16[512,512]{1,0:T(8,128)(2,1)} %refs_0_.4), channel_id=1, source_target_pairs={{0,1},{1,0},{2,3},{3,2},{4,5},{5,4},{6,7},{7,6},{8,9},{9,8},{10,11... | collective-permute-start | bytes 1572872 | tf_op jit(solution)/shard_map/ppermute | solution.py:29
  30.8 15.7 %collective-permute-start.6 = (bf16[256,2048]{1,0:T(8,128)(2,1)S(1)}, bf16[256,2048]{1,0:T(8,128)(2,1)S(1)}, u32[]{:S(2)}, u32[]{:S(2)}) collective-permute-start(bf16[256,2048]{1,0:T(8,128)(2,1)S(1)} %collective-permute-done.4.refs_6_.refs_2_), channel_id=1, source_target_pairs={{0,4},{4,0},{8,12},{12,8},{16,20},{20,16},{24,28},{28,24},{1,5},{5... | collective-permute-start | bytes 3145736 | tf_op jit(solution)/shard_map/ppermute | solution.py:29
  30.8 15.7 %collective-permute-start.7 = (bf16[256,2048]{1,0:T(8,128)(2,1)S(1)}, bf16[256,2048]{1,0:T(8,128)(2,1)S(1)}, u32[]{:S(2)}, u32[]{:S(2)}) collective-permute-start(bf16[256,2048]{1,0:T(8,128)(2,1)S(1)} %collective-permute-done.5.refs_8_.refs_4_), channel_id=1, source_target_pairs={{0,4},{4,0},{8,12},{12,8},{16,20},{20,16},{24,28},{28,24},{1,5},{5... | collective-permute-start | bytes 3145736 | tf_op jit(solution)/shard_map/ppermute | solution.py:29
  32.5 19.9 %collective-permute-start.8 = (bf16[256,2048]{1,0:T(8,128)(2,1)S(1)}, bf16[256,2048]{1,0:T(8,128)(2,1)S(1)}, u32[]{:S(2)}, u32[]{:S(2)}) collective-permute-start(bf16[256,2048]{1,0:T(8,128)(2,1)S(1)} %broadcast_select_fusion), channel_id=1, source_target_pairs={{0,16},{4,12},{8,24},{12,4},{16,0},{20,28},{24,8},{28,20},{1,17},{... | collective-permute-start | bytes 3145736 | tf_op jit(solution)/shard_map/ppermute | solution.py:34
  33.0 13.5 %collective-permute-start.2 = (bf16[512,512]{1,0:T(8,128)(2,1)}, bf16[512,512]{1,0:T(8,128)(2,1)S(1)}, u32[]{:S(2)}, u32[]{:S(2)}) collective-permute-start(bf16[512,512]{1,0:T(8,128)(2,1)} %collective-permute-done.1.refs_2_), channel_id=1, source_target_pairs={{0,1},{1,0},{2,3},{3,2},{4,5},{5,4},{6,7},{7,6},{8,9},{9,8},{10,11... | collective-permute-start | bytes 1572872 | tf_op jit(solution)/shard_map/ppermute | solution.py:29
  46.6 70.7 %copy-start.1 = (bf16[256,2048]{1,0:T(8,128)(2,1)}, bf16[256,2048]{1,0:T(8,128)(2,1)S(1)}, u32[]{:S(2)}) copy-start(bf16[256,2048]{1,0:T(8,128)(2,1)S(1)} %collective-permute-done.6.refs_7_.refs_3_) | copy-start | bytes 3145732
  46.6 70.7 %copy-start.3 = (bf16[256,2048]{1,0:T(8,128)(2,1)}, bf16[256,2048]{1,0:T(8,128)(2,1)S(1)}, u32[]{:S(2)}) copy-start(bf16[256,2048]{1,0:T(8,128)(2,1)S(1)} %collective-permute-done.7.refs_9_.refs_5_) | copy-start | bytes 3145732
  52.4 64.8 %copy-start.5 = (bf16[256,2048]{1,0:T(8,128)(2,1)}, bf16[256,2048]{1,0:T(8,128)(2,1)S(1)}, u32[]{:S(2)}) copy-start(bf16[256,2048]{1,0:T(8,128)(2,1)S(1)} %collective-permute-done.8.refs_0_.refs_6_) | copy-start | bytes 3145732
  52.5 2.7 %collective-permute-start.9 = (bf16[256,2048]{1,0:T(8,128)(2,1)S(1)}, bf16[256,2048]{1,0:T(8,128)(2,1)S(1)}, u32[]{:S(2)}, u32[]{:S(2)}) collective-permute-start(bf16[256,2048]{1,0:T(8,128)(2,1)S(1)} %collective-permute-done.8.refs_0_.refs_6_), channel_id=1, source_target_pairs={{0,4},{4,0},{8,12},{12,8},{16,20},{20,16},{24,28},{28,24},{1,5},{5... | collective-permute-start | bytes 3145736 | tf_op jit(solution)/shard_map/ppermute | solution.py:29
  55.2 62.1 %copy-start.7 = (bf16[256,2048]{1,0:T(8,128)(2,1)}, bf16[256,2048]{1,0:T(8,128)(2,1)S(1)}, u32[]{:S(2)}) copy-start(bf16[256,2048]{1,0:T(8,128)(2,1)S(1)} %collective-permute-done.9.refs_1_.refs_7_) | copy-start | bytes 3145732
  57.7 5.5 %collective-permute-start.10 = (f32[2,512]{1,0:T(2,128)S(1)}, f32[2,512]{1,0:T(2,128)S(1)}, u32[]{:S(2)}, u32[]{:S(2)}) collective-permute-start(f32[2,512]{1,0:T(2,128)S(1)} %get-tuple-element.53), channel_id=1, source_target_pairs={{0,3},{1,2},{2,1},{3,0},{4,7},{5,6},{6,5},{7,4},{8,11},{9,10},{10,... | collective-permute-start | bytes 12296 | tf_op jit(solution)/shard_map/ppermute | solution.py:29
  60.6 4.5 %collective-permute-start.11 = (f32[2,512]{1,0:T(2,128)S(1)}, f32[2,512]{1,0:T(2,128)S(1)}, u32[]{:S(2)}, u32[]{:S(2)}) collective-permute-start(f32[2,512]{1,0:T(2,128)S(1)} %get-tuple-element.53), channel_id=1, source_target_pairs={{0,2},{1,3},{2,0},{3,1},{4,6},{5,7},{6,4},{7,5},{8,10},{9,11},{10,... | collective-permute-start | bytes 12296 | tf_op jit(solution)/shard_map/ppermute | solution.py:29
  60.6 4.5 %collective-permute-start.12 = (f32[2,512]{1,0:T(2,128)S(1)}, f32[2,512]{1,0:T(2,128)S(1)}, u32[]{:S(2)}, u32[]{:S(2)}) collective-permute-start(f32[2,512]{1,0:T(2,128)S(1)} %get-tuple-element.53), channel_id=1, source_target_pairs={{0,1},{1,0},{2,3},{3,2},{4,5},{5,4},{6,7},{7,6},{8,9},{9,8},{10,11... | collective-permute-start | bytes 12296 | tf_op jit(solution)/shard_map/ppermute | solution.py:29
  65.8 1.2 collective-permute-start.13
  67.1 4.6 %collective-permute-start.14 = (f32[1,2048]{1,0:T(1,128)S(1)}, f32[1,2048]{1,0:T(1,128)S(1)}, u32[]{:S(2)}, u32[]{:S(2)}) collective-permute-start(f32[1,2048]{1,0:T(1,128)S(1)} %add.114), channel_id=1, source_target_pairs={{0,24},{4,28},{8,16},{12,20},{16,8},{20,12},{24,0},{28,4},{1,25},{... | collective-permute-start | bytes 24584 | tf_op jit(solution)/shard_map/ppermute | solution.py:29
  68.6 3.7 %collective-permute-start.15 = (f32[1,2048]{1,0:T(1,128)S(1)}, f32[1,2048]{1,0:T(1,128)S(1)}, u32[]{:S(2)}, u32[]{:S(2)}) collective-permute-start(f32[1,2048]{1,0:T(1,128)S(1)} %add.114), channel_id=1, source_target_pairs={{0,16},{4,20},{8,24},{12,28},{16,0},{20,4},{24,8},{28,12},{1,17},{... | collective-permute-start | bytes 24584 | tf_op jit(solution)/shard_map/ppermute | solution.py:29
  70.1 3.7 %collective-permute-start.16 = (f32[1,2048]{1,0:T(1,128)S(1)}, f32[1,2048]{1,0:T(1,128)S(1)}, u32[]{:S(2)}, u32[]{:S(2)}) collective-permute-start(f32[1,2048]{1,0:T(1,128)S(1)} %add.114), channel_id=1, source_target_pairs={{0,8},{4,12},{8,0},{12,4},{16,24},{20,28},{24,16},{28,20},{1,9},{5... | collective-permute-start | bytes 24584 | tf_op jit(solution)/shard_map/ppermute | solution.py:29
  74.4 5.4 %collective-permute-start.17 = (f32[1,512]{1,0:T(1,128)S(1)}, f32[1,512]{1,0:T(1,128)S(1)}, u32[]{:S(2)}, u32[]{:S(2)}) collective-permute-start(f32[1,512]{1,0:T(1,128)S(1)} %get-tuple-element.55), channel_id=1, source_target_pairs={{0,3},{1,2},{2,1},{3,0},{4,7},{5,6},{6,5},{7,4},{8,11},{9,10},{10,... | collective-permute-start | bytes 6152 | tf_op jit(solution)/shard_map/ppermute | solution.py:29
  75.9 4.5 %collective-permute-start.18 = (f32[1,512]{1,0:T(1,128)S(1)}, f32[1,512]{1,0:T(1,128)S(1)}, u32[]{:S(2)}, u32[]{:S(2)}) collective-permute-start(f32[1,512]{1,0:T(1,128)S(1)} %get-tuple-element.55), channel_id=1, source_target_pairs={{0,2},{1,3},{2,0},{3,1},{4,6},{5,7},{6,4},{7,5},{8,10},{9,11},{10,... | collective-permute-start | bytes 6152 | tf_op jit(solution)/shard_map/ppermute | solution.py:29
  76.5 3.9 %collective-permute-start.19 = (f32[1,512]{1,0:T(1,128)S(1)}, f32[1,512]{1,0:T(1,128)S(1)}, u32[]{:S(2)}, u32[]{:S(2)}) collective-permute-start(f32[1,512]{1,0:T(1,128)S(1)} %get-tuple-element.55), channel_id=1, source_target_pairs={{0,1},{1,0},{2,3},{3,2},{4,5},{5,4},{6,7},{7,6},{8,9},{9,8},{10,11... | collective-permute-start | bytes 6152 | tf_op jit(solution)/shard_map/ppermute | solution.py:29
  81.1 1.2 collective-permute-start.20
  82.3 4.6 %collective-permute-start.21 = (f32[1,2048]{1,0:T(1,128)S(1)}, f32[1,2048]{1,0:T(1,128)S(1)}, u32[]{:S(2)}, u32[]{:S(2)}) collective-permute-start(f32[1,2048]{1,0:T(1,128)S(1)} %add.121), channel_id=1, source_target_pairs={{0,24},{4,28},{8,16},{12,20},{16,8},{20,12},{24,0},{28,4},{1,25},{... | collective-permute-start | bytes 24584 | tf_op jit(solution)/shard_map/ppermute | solution.py:29
  82.9 4.1 %collective-permute-start.22 = (f32[1,2048]{1,0:T(1,128)S(1)}, f32[1,2048]{1,0:T(1,128)S(1)}, u32[]{:S(2)}, u32[]{:S(2)}) collective-permute-start(f32[1,2048]{1,0:T(1,128)S(1)} %add.121), channel_id=1, source_target_pairs={{0,16},{4,20},{8,24},{12,28},{16,0},{20,4},{24,8},{28,12},{1,17},{... | collective-permute-start | bytes 24584 | tf_op jit(solution)/shard_map/ppermute | solution.py:29
  84.4 3.7 %collective-permute-start.23 = (f32[1,2048]{1,0:T(1,128)S(1)}, f32[1,2048]{1,0:T(1,128)S(1)}, u32[]{:S(2)}, u32[]{:S(2)}) collective-permute-start(f32[1,2048]{1,0:T(1,128)S(1)} %add.121), channel_id=1, source_target_pairs={{0,8},{4,12},{8,0},{12,4},{16,24},{20,28},{24,16},{28,20},{1,9},{5... | collective-permute-start | bytes 24584 | tf_op jit(solution)/shard_map/ppermute | solution.py:29
  88.7 5.4 %collective-permute-start.24 = (f32[1,512]{1,0:T(1,128)S(1)}, f32[1,512]{1,0:T(1,128)S(1)}, u32[]{:S(2)}, u32[]{:S(2)}) collective-permute-start(f32[1,512]{1,0:T(1,128)S(1)} %get-tuple-element.57), channel_id=1, source_target_pairs={{0,3},{1,2},{2,1},{3,0},{4,7},{5,6},{6,5},{7,4},{8,11},{9,10},{10,... | collective-permute-start | bytes 6152 | tf_op jit(solution)/shard_map/ppermute | solution.py:29
  91.3 4.5 %collective-permute-start.25 = (f32[1,512]{1,0:T(1,128)S(1)}, f32[1,512]{1,0:T(1,128)S(1)}, u32[]{:S(2)}, u32[]{:S(2)}) collective-permute-start(f32[1,512]{1,0:T(1,128)S(1)} %get-tuple-element.57), channel_id=1, source_target_pairs={{0,2},{1,3},{2,0},{3,1},{4,6},{5,7},{6,4},{7,5},{8,10},{9,11},{10,... | collective-permute-start | bytes 6152 | tf_op jit(solution)/shard_map/ppermute | solution.py:29
  92.2 3.6 %collective-permute-start.26 = (f32[1,512]{1,0:T(1,128)S(1)}, f32[1,512]{1,0:T(1,128)S(1)}, u32[]{:S(2)}, u32[]{:S(2)}) collective-permute-start(f32[1,512]{1,0:T(1,128)S(1)} %get-tuple-element.57), channel_id=1, source_target_pairs={{0,1},{1,0},{2,3},{3,2},{4,5},{5,4},{6,7},{7,6},{8,9},{9,8},{10,11... | collective-permute-start | bytes 6152 | tf_op jit(solution)/shard_map/ppermute | solution.py:29
  96.5 1.2 collective-permute-start.27
  97.8 4.6 %collective-permute-start.28 = (f32[1,2048]{1,0:T(1,128)S(1)}, f32[1,2048]{1,0:T(1,128)S(1)}, u32[]{:S(2)}, u32[]{:S(2)}) collective-permute-start(f32[1,2048]{1,0:T(1,128)S(1)} %add.128), channel_id=1, source_target_pairs={{0,24},{4,28},{8,16},{12,20},{16,8},{20,12},{24,0},{28,4},{1,25},{... | collective-permute-start | bytes 24584 | tf_op jit(solution)/shard_map/ppermute | solution.py:29
  99.3 3.7 %collective-permute-start.29 = (f32[1,2048]{1,0:T(1,128)S(1)}, f32[1,2048]{1,0:T(1,128)S(1)}, u32[]{:S(2)}, u32[]{:S(2)}) collective-permute-start(f32[1,2048]{1,0:T(1,128)S(1)} %add.128), channel_id=1, source_target_pairs={{0,16},{4,20},{8,24},{12,28},{16,0},{20,4},{24,8},{28,12},{1,17},{... | collective-permute-start | bytes 24584 | tf_op jit(solution)/shard_map/ppermute | solution.py:29
  100.8 3.7 %collective-permute-start.30 = (f32[1,2048]{1,0:T(1,128)S(1)}, f32[1,2048]{1,0:T(1,128)S(1)}, u32[]{:S(2)}, u32[]{:S(2)}) collective-permute-start(f32[1,2048]{1,0:T(1,128)S(1)} %add.128), channel_id=1, source_target_pairs={{0,8},{4,12},{8,0},{12,4},{16,24},{20,28},{24,16},{28,20},{1,9},{5... | collective-permute-start | bytes 24584 | tf_op jit(solution)/shard_map/ppermute | solution.py:29
  105.1 5.4 %collective-permute-start.31 = (f32[1,512]{1,0:T(1,128)S(1)}, f32[1,512]{1,0:T(1,128)S(1)}, u32[]{:S(2)}, u32[]{:S(2)}) collective-permute-start(f32[1,512]{1,0:T(1,128)S(1)} %get-tuple-element.59), channel_id=1, source_target_pairs={{0,3},{1,2},{2,1},{3,0},{4,7},{5,6},{6,5},{7,4},{8,11},{9,10},{10,... | collective-permute-start | bytes 6152 | tf_op jit(solution)/shard_map/ppermute | solution.py:29
  106.6 4.5 %collective-permute-start.32 = (f32[1,512]{1,0:T(1,128)S(1)}, f32[1,512]{1,0:T(1,128)S(1)}, u32[]{:S(2)}, u32[]{:S(2)}) collective-permute-start(f32[1,512]{1,0:T(1,128)S(1)} %get-tuple-element.59), channel_id=1, source_target_pairs={{0,2},{1,3},{2,0},{3,1},{4,6},{5,7},{6,4},{7,5},{8,10},{9,11},{10,... | collective-permute-start | bytes 6152 | tf_op jit(solution)/shard_map/ppermute | solution.py:29
  107.5 3.6 %collective-permute-start.33 = (f32[1,512]{1,0:T(1,128)S(1)}, f32[1,512]{1,0:T(1,128)S(1)}, u32[]{:S(2)}, u32[]{:S(2)}) collective-permute-start(f32[1,512]{1,0:T(1,128)S(1)} %get-tuple-element.59), channel_id=1, source_target_pairs={{0,1},{1,0},{2,3},{3,2},{4,5},{5,4},{6,7},{7,6},{8,9},{9,8},{10,11... | collective-permute-start | bytes 6152 | tf_op jit(solution)/shard_map/ppermute | solution.py:29
  117.1 7.6 %collective-permute-start.34 = (bf16[256,2048]{1,0:T(8,128)(2,1)S(1)}, bf16[256,2048]{1,0:T(8,128)(2,1)S(1)}, u32[]{:S(2)}, u32[]{:S(2)}) collective-permute-start(bf16[256,2048]{1,0:T(8,128)(2,1)S(1)} %get-tuple-element.61), channel_id=1, source_target_pairs={{0,4},{4,0},{8,12},{12,8},{16,20},{20,16},{24,28},{28,24},{1,5},{5... | collective-permute-start | bytes 3145736 | tf_op jit(solution)/shard_map/ppermute | solution.py:29
  126.4 16.9 %collective-permute-start.38 = (bf16[256,2048]{1,0:T(8,128)(2,1)}, bf16[256,2048]{1,0:T(8,128)(2,1)}, u32[]{:S(2)}, u32[]{:S(2)}) collective-permute-start(bf16[256,2048]{1,0:T(8,128)(2,1)} %add_convert_fusion.1.refs_8_), channel_id=1, source_target_pairs={{0,8},{4,20},{8,0},{12,28},{16,24},{20,4},{24,16},{28,12},{1,9},{5... | collective-permute-start | bytes 3145736 | tf_op jit(solution)/shard_map/ppermute | solution.py:34
  126.9 16.3 %collective-permute-start.36 = (bf16[256,2048]{1,0:T(8,128)(2,1)}, bf16[256,2048]{1,0:T(8,128)(2,1)}, u32[]{:S(2)}, u32[]{:S(2)}) collective-permute-start(bf16[256,2048]{1,0:T(8,128)(2,1)} %get-tuple-element.73), channel_id=1, source_target_pairs={{0,4},{4,0},{8,12},{12,8},{16,20},{20,16},{24,28},{28,24},{1,5},{5... | collective-permute-start | bytes 3145736 | tf_op jit(solution)/shard_map/ppermute | solution.py:29
  126.9 16.3 %collective-permute-start.37 = (bf16[256,2048]{1,0:T(8,128)(2,1)}, bf16[256,2048]{1,0:T(8,128)(2,1)}, u32[]{:S(2)}, u32[]{:S(2)}) collective-permute-start(bf16[256,2048]{1,0:T(8,128)(2,1)} %get-tuple-element.74), channel_id=1, source_target_pairs={{0,4},{4,0},{8,12},{12,8},{16,20},{20,16},{24,28},{28,24},{1,5},{5... | collective-permute-start | bytes 3145736 | tf_op jit(solution)/shard_map/ppermute | solution.py:29
  127.4 14.5 %collective-permute-start.35 = (bf16[512,512]{1,0:T(8,128)(2,1)}, bf16[512,512]{1,0:T(8,128)(2,1)}, u32[]{:S(2)}, u32[]{:S(2)}) collective-permute-start(bf16[512,512]{1,0:T(8,128)(2,1)} %get-tuple-element.72), channel_id=1, source_target_pairs={{0,1},{1,0},{2,3},{3,2},{4,5},{5,4},{6,7},{7,6},{8,9},{9,8},{10,11... | collective-permute-start | bytes 1572872 | tf_op jit(solution)/shard_map/ppermute | solution.py:29
  146.6 30.6 %collective-permute-start.39 = (bf16[256,2048]{1,0:T(8,128)(2,1)S(1)}, bf16[256,2048]{1,0:T(8,128)(2,1)S(1)}, u32[]{:S(2)}, u32[]{:S(2)}) collective-permute-start(bf16[256,2048]{1,0:T(8,128)(2,1)S(1)} %get-tuple-element.88), channel_id=1, source_target_pairs={{0,8},{4,12},{8,0},{12,4},{16,24},{20,28},{24,16},{28,20},{1,9},{5... | collective-permute-start | bytes 3145736 | tf_op jit(solution)/shard_map/ppermute | solution.py:29
  148.1 29.1 %collective-permute-start.40 = (bf16[256,2048]{1,0:T(8,128)(2,1)S(1)}, bf16[256,2048]{1,0:T(8,128)(2,1)S(1)}, u32[]{:S(2)}, u32[]{:S(2)}) collective-permute-start(bf16[256,2048]{1,0:T(8,128)(2,1)S(1)} %get-tuple-element.87), channel_id=1, source_target_pairs={{0,16},{4,20},{8,24},{12,28},{16,0},{20,4},{24,8},{28,12},{1,17},{... | collective-permute-start | bytes 3145736 | tf_op jit(solution)/shard_map/ppermute | solution.py:29
  148.6 28.6 %collective-permute-start.43 = (bf16[256,2048]{1,0:T(8,128)(2,1)S(1)}, bf16[256,2048]{1,0:T(8,128)(2,1)S(1)}, u32[]{:S(2)}, u32[]{:S(2)}) collective-permute-start(bf16[256,2048]{1,0:T(8,128)(2,1)S(1)} %copy-done.19), channel_id=1, source_target_pairs={{0,4},{4,0},{8,12},{12,8},{16,20},{20,16},{24,28},{28,24},{1,5},{5... | collective-permute-start | bytes 3145736 | tf_op jit(solution)/shard_map/ppermute | solution.py:29
  148.6 24.4 %collective-permute-start.41 = (bf16[512,512]{1,0:T(8,128)(2,1)S(1)}, bf16[512,512]{1,0:T(8,128)(2,1)S(1)}, u32[]{:S(2)}, u32[]{:S(2)}) collective-permute-start(bf16[512,512]{1,0:T(8,128)(2,1)S(1)} %slice_bitcast_fusion.2), channel_id=1, source_target_pairs={{0,1},{1,0},{2,3},{3,2},{4,5},{5,4},{6,7},{7,6},{8,9},{9,8},{10,11... | collective-permute-start | bytes 1572872 | tf_op jit(solution)/shard_map/ppermute | solution.py:29
  150.0 26.2 %collective-permute-start.42 = (bf16[512,512]{1,0:T(8,128)(2,1)S(1)}, bf16[512,512]{1,0:T(8,128)(2,1)S(1)}, u32[]{:S(2)}, u32[]{:S(2)}) collective-permute-start(bf16[512,512]{1,0:T(8,128)(2,1)S(1)} %fusion.6), channel_id=1, source_target_pairs={{0,2},{1,3},{2,0},{3,1},{4,6},{5,7},{6,4},{7,5},{8,10},{9,11},{10,... | collective-permute-start | bytes 1572872 | tf_op jit(solution)/shard_map/ppermute | solution.py:29
  (17 other events, 145.8 us)

commit v15 on v11

--- a/solution.py
+++ b/solution.py
@@ -243,6 +243,27 @@
             head_products(turned, core, depth, grad_ref, slice(i, i + tile), refs[2 * index], refs[2 * index + 1])
 
 
+def sum_kernel(count, chosen, *refs):
+    core = lax.axis_index("sample") % 2
+    out_ref = refs[-1]
+    for first in range(0, out_ref.shape[0], 16):
+        at = slice(first, first + 16)
+        total = wide(refs[0][at, :])
+        for i, ref in enumerate(refs[1:-1], 1):
+            value = wide(ref[at, :])
+            total = total + (value if i < count else jnp.where(core == chosen, value, 0.0))
+        out_ref[at, :] = total.astype(bf16)
+
+
+def onward_kernel(count, shares_ref, *refs):
+    received, outputs = refs[:count], refs[count:]
+    outputs[0][...] = shares_ref[1]
+    for i, ref in enumerate(received):
+        for first in range(0, ref.shape[0], 16):
+            at = slice(first, first + 16)
+            outputs[1 + i][at, :] = (wide(shares_ref[2 + 2 * i, at, :]) + wide(ref[at, :])).astype(bf16)
+
+
 def shares_kernel(depth, paired, parts, grad_ref, *refs):
     head_refs, shares_ref = refs[: len(parts)], refs[-1]
     chip, place = lax.axis_index("sample") // 2, lax.axis_index("cls")
@@ -340,7 +361,12 @@
         [grad, turned],
     )
     theirs, *pairs = lax.optimization_barrier((theirs, *pairs))
-    block = lax.optimization_barrier((wide(mine) + wide(theirs)).astype(bf16))
+
+    def head_sum(values, more=(), chosen=0):
+        kernel = functools.partial(sum_kernel, len(values), chosen)
+        return call(kernel, [((depth, classes), bf16)], list(values) + list(more))[0]
+
+    block = head_sum([mine, theirs])
     passed = {diagonal[-1]: cross(block, *diagonal[-1])}
     share_from = {groups - 2: flip(share, "cls", 1)}
     others = {mask: flip(pairs[2 * i + 1], "sample", 1) for i, mask in enumerate(near) if mask}
@@ -351,10 +377,10 @@
         extra=[block],
     )
 
-    onward = {1: shares[1]}
-    for mask in range(2, groups, 2):
-        received = share_from[mask] if mask in share_from else flip(shares[mask | 1], "cls", 1)
-        onward[mask] = (wide(shares[mask]) + wide(received)).astype(bf16)
+    evens = range(2, groups, 2)
+    came = [share_from[mask] if mask in share_from else flip(shares[mask | 1], "cls", 1) for mask in evens]
+    made = call(functools.partial(onward_kernel, len(came)), [((rows, width), bf16)] * (1 + len(came)), [shares] + came)
+    onward = dict(zip([1, *evens], made))
     ready = lax.optimization_barrier((*onward.values(), *others.values(), *passed.values(), pairs[-1]))
     onward = dict(zip(onward, ready))
     others = dict(zip(others, ready[len(onward) :]))
@@ -363,16 +389,14 @@
     returned = [flip(value, "cls", mask) for mask, value in onward.items()]
     grad_features = sum([wide(value) for value in returned], wide(shares[0])).astype(bf16)
 
-    mixed = {mask: wide(pairs[2 * i]) + wide(others[mask]) for i, mask in enumerate(near) if mask}
+    mine_of = {mask: pairs[2 * i] for i, mask in enumerate(near)}
     for a, b in diagonal[:-1]:
-        passed[a, b] = cross(mixed[a | b].astype(bf16), a, b)
+        passed[a, b] = cross(head_sum([mine_of[a | b], others[a | b]]), a, b)
     received = []
     for mask in first + second:
-        total_of = mixed[mask]
-        for (a, b), more in passed.items():
-            if mask == (b if mask in second else a):
-                total_of = total_of + jnp.where((core == 0) == (mask in second), wide(more), 0.0)
-        received.append(flip(total_of.astype(bf16), "sample", mask))
+        chosen = 0 if mask in second else 1
+        more = [value for (a, b), value in passed.items() if mask == (a if chosen else b)]
+        received.append(flip(head_sum([mine_of[mask], others[mask]], more, chosen), "sample", mask))
     received = lax.optimization_barrier((*received, grad_features))
     grad_features = received[-1]
     grad_head = sum([wide(part) for part in received[:-1]], own).astype(bf16)

time: 177 us -> 170 us (0.960)
  local copies, waits for them, and re-layouts: 7.75 us -> 0.03 us
  waiting for transfers between devices: 83.9 us -> 90.5 us
  other arithmetic: 9.01 us -> 2.95 us
    unnamed x42 -> x6, local copies, waits for them, and re-layouts: 7.7 us -> 0.01 us
    ppermute x42, waiting for transfers between devices: 83.9 us -> 90.5 us  [flip(): lax.ppermute(value, axis, [(i, i ^ mask) for i in range(lax.axis_size(axi...]
    convert_element_type x3 -> x0, other arithmetic: 6.05 us -> none  [the longest x1 3.1 us: per_device(): received.append(flip(total_of.astype(bf16), 'sample', mask))]
    pallas_call x12 -> x16, Pallas kernels: 28.2 us -> 27.9 us  [call(): pl.pallas_call(kernel, out_shape=tuple((jax.ShapeDtypeStruct(shape, dtype...]
  transfers between devices with their start and end apart: 44 -> 44, of which waited for: 26 -> 25; matrix products, arithmetic and copies ran while one was open for 1% -> 1% of each run, Pallas kernels for 9% -> 9%
where the time goes in v15:
time: 170 us; the launch traced here: 169 us
  waiting for transfers between devices  90.5 us (53%)
  starting transfers between devices  47.1 us (28%)
  Pallas kernels  27.9 us (16%)
  other arithmetic  2.95 us (2%)
    ppermute x42, waiting for transfers between devices, flip(): lax.ppermute(value, axis, [(i, i ^ mask) for i in range(lax.axis_size(axi...  90.5 us
    ppermute x42, starting transfers between devices, flip(): lax.ppermute(value, axis, [(i, i ^ mask) for i in range(lax.axis_size(axi...  46 us
    pallas_call x16, Pallas kernels, call(): pl.pallas_call(kernel, out_shape=tuple((jax.ShapeDtypeStruct(shape, dtype...  27.9 us
  transfers between devices with their start and end apart: 44, of which 25 were waited for; matrix products, arithmetic and copies ran while one was open for 1% of the time, Pallas kernels for 9%

profile of v15, /device:TPU:0, one launch (start us, length us, event | category | flops | bytes accessed | tf_op | source)
XLA Modules:
  0.0 169.4 jit_solution(10594090179184310965)
XLA Ops:
  0.6 3.0 %collective-permute-start.5 = (bf16[256,2048]{1,0:T(8,128)(2,1)}, bf16[256,2048]{1,0:T(8,128)(2,1)S(1)}, u32[]{:S(2)}, u32[]{:S(2)}) collective-permute-start(bf16[256,2048]{1,0:T(8,128)(2,1)} %refs_0_.5), channel_id=1, source_target_pairs={{0,16},{4,20},{8,24},{12,28},{16,0},{20,4},{24,8},{28,12},{1,17},{... | collective-permute-start | bytes 3145736 | tf_op jit(solution)/shard_map/ppermute | solution.py:29
  3.7 1.5 collective-permute-start.4
  5.2 2.6 %collective-permute-start.1 = (bf16[512,512]{1,0:T(8,128)(2,1)}, bf16[512,512]{1,0:T(8,128)(2,1)}, u32[]{:S(2)}, u32[]{:S(2)}) collective-permute-start(bf16[512,512]{1,0:T(8,128)(2,1)} %refs_0_.3), channel_id=1, source_target_pairs={{0,2},{1,3},{2,0},{3,1},{4,6},{5,7},{6,4},{7,5},{8,10},{9,11},{10,... | collective-permute-start | bytes 1572872 | tf_op jit(solution)/shard_map/ppermute | solution.py:29
  7.8 1.6 collective-permute-start
  9.3 21.5 %collective-permute-done.1.refs_2_ = bf16[512,512]{1,0:T(8,128)(2,1)} collective-permute-done((bf16[512,512]{1,0:T(8,128)(2,1)}, bf16[512,512]{1,0:T(8,128)(2,1)}, u32[]{:S(2)}, u32[]{:S(2)}) %collective-permute-start.1) | collective-permute-done | bytes 524320 | tf_op jit(solution)/shard_map/ppermute | solution.py:29
  31.5 1.1 collective-permute-done.refs_1_
  33.0 13.5 %collective-permute-done.2.refs_3_ = bf16[512,512]{1,0:T(8,128)(2,1)S(1)} collective-permute-done((bf16[512,512]{1,0:T(8,128)(2,1)}, bf16[512,512]{1,0:T(8,128)(2,1)S(1)}, u32[]{:S(2)}, u32[]{:S(2)}) %collective-permute-start.2) | collective-permute-done | bytes 524320 | tf_op jit(solution)/shard_map/ppermute | solution.py:29
  46.6 5.1 %shard_map.58 = (bf16[4,512,512]{2,1,0:T(8,128)(2,1)S(1)}, f32[512,2048]{1,0:T(8,128)S(1)}) custom-call(bf16[512,512]{1,0:T(8,128)(2,1)S(1)} %copy-done.1, bf16[512,512]{1,0:T(8,128)(2,1)} %collective-permute-done.refs_1_, bf16[512,512]{1,0:T(8,128)(2,1)} %collective-permute-done.1.refs_2_, bf16[512,512]{1,0:T(8,128)(2,1)S(1)} %collective-permute-done.2.refs_3_, ...), custom_call_target="tpu_custom_call" | custom-call | flops 1 | bytes 1 | tf_op jit(solution)/shard_map/pallas_call | solution.py:73
  51.8 2.6 %collective-permute-done.9.refs_1_.refs_7_ = bf16[256,2048]{1,0:T(8,128)(2,1)S(1)} collective-permute-done((bf16[256,2048]{1,0:T(8,128)(2,1)S(1)}, bf16[256,2048]{1,0:T(8,128)(2,1)S(1)}, u32[]{:S(2)}, u32[]{:S(2)}) %collective-permute-start.9) | collective-permute-done | bytes 1048608 | tf_op jit(solution)/shard_map/ppermute | solution.py:29
  54.4 2.4 %shard_map.59 = (f32[512,2048]{1,0:T(8,128)S(1)}, bf16[512,2048]{1,0:T(8,128)(2,1)S(1)}, f32[2,512]{1,0:T(2,128)S(1)}) custom-call(f32[512,2048]{1,0:T(8,128)S(1)} %get-tuple-element.49.logits_ref, bf16[4,512,512]{2,1,0:T(8,128)(2,1)S(1)} %get-tuple-element.50.blocks_ref, bf16[256,2048]{1,0:T(8,128)(2,1)S(1)} %collective-permute-done.8.refs_0_.refs_6_, ...), custom_call_target="tpu_custom_call" | custom-call | flops 1 | bytes 1 | tf_op jit(solution)/shard_map/pallas_call | solution.py:73
  56.8 2.9 %collective-permute-start.10 = (f32[2,512]{1,0:T(2,128)S(1)}, f32[2,512]{1,0:T(2,128)S(1)}, u32[]{:S(2)}, u32[]{:S(2)}) collective-permute-start(f32[2,512]{1,0:T(2,128)S(1)} %get-tuple-element.55), channel_id=1, source_target_pairs={{0,3},{1,2},{2,1},{3,0},{4,7},{5,6},{6,5},{7,4},{8,11},{9,10},{10,... | collective-permute-start | bytes 12296 | tf_op jit(solution)/shard_map/ppermute | solution.py:29
  59.8 1.5 collective-permute-start.12
  62.3 1.9 %collective-permute-done.11 = f32[2,512]{1,0:T(2,128)S(1)} collective-permute-done((f32[2,512]{1,0:T(2,128)S(1)}, f32[2,512]{1,0:T(2,128)S(1)}, u32[]{:S(2)}, u32[]{:S(2)}) %collective-permute-start.11) | collective-permute-done | bytes 4128 | tf_op jit(solution)/shard_map/ppermute | solution.py:29
  65.1 1.2 collective-permute-done.13
  66.3 1.6 collective-permute-start.16
  68.3 1.5 collective-permute-start.14
  69.8 3.1 %collective-permute-done.14 = f32[1,2048]{1,0:T(1,128)S(1)} collective-permute-done((f32[1,2048]{1,0:T(1,128)S(1)}, f32[1,2048]{1,0:T(1,128)S(1)}, u32[]{:S(2)}, u32[]{:S(2)}) %collective-permute-start.14) | collective-permute-done | bytes 8224 | tf_op jit(solution)/shard_map/ppermute | solution.py:29
  73.6 1.5 collective-permute-start.17
  75.7 2.3 %collective-permute-start.19 = (f32[1,512]{1,0:T(1,128)S(1)}, f32[1,512]{1,0:T(1,128)S(1)}, u32[]{:S(2)}, u32[]{:S(2)}) collective-permute-start(f32[1,512]{1,0:T(1,128)S(1)} %get-tuple-element.57), channel_id=1, source_target_pairs={{0,1},{1,0},{2,3},{3,2},{4,5},{5,4},{6,7},{7,6},{8,9},{9,8},{10,11... | collective-permute-start | bytes 6152 | tf_op jit(solution)/shard_map/ppermute | solution.py:29
  78.0 1.0 collective-permute-done.17
  80.4 1.2 collective-permute-done.20
  81.5 1.6 collective-permute-start.21
  83.6 1.5 collective-permute-start.23
  85.1 1.1 collective-permute-done.21
  87.9 2.6 %collective-permute-start.24 = (f32[1,512]{1,0:T(1,128)S(1)}, f32[1,512]{1,0:T(1,128)S(1)}, u32[]{:S(2)}, u32[]{:S(2)}) collective-permute-start(f32[1,512]{1,0:T(1,128)S(1)} %get-tuple-element.59), channel_id=1, source_target_pairs={{0,3},{1,2},{2,1},{3,0},{4,7},{5,6},{6,5},{7,4},{8,11},{9,10},{10,... | collective-permute-start | bytes 6152 | tf_op jit(solution)/shard_map/ppermute | solution.py:29
  92.4 1.0 collective-permute-done.24
  93.4 1.7 collective-permute-done.25
  95.8 1.2 collective-permute-done.27
  97.0 2.5 %collective-permute-start.28 = (f32[1,2048]{1,0:T(1,128)S(1)}, f32[1,2048]{1,0:T(1,128)S(1)}, u32[]{:S(2)}, u32[]{:S(2)}) collective-permute-start(f32[1,2048]{1,0:T(1,128)S(1)} %add.109), channel_id=1, source_target_pairs={{0,24},{4,28},{8,16},{12,20},{16,8},{20,12},{24,0},{28,4},{1,25},{... | collective-permute-start | bytes 24584 | tf_op jit(solution)/shard_map/ppermute | solution.py:29
  100.5 1.1 collective-permute-done.28
  101.6 1.5 collective-permute-done.29
  104.3 1.5 collective-permute-start.31
  105.8 0.9 collective-permute-start.32
  106.7 2.0 %collective-permute-start.33 = (f32[1,512]{1,0:T(1,128)S(1)}, f32[1,512]{1,0:T(1,128)S(1)}, u32[]{:S(2)}, u32[]{:S(2)}) collective-permute-start(f32[1,512]{1,0:T(1,128)S(1)} %get-tuple-element.61), channel_id=1, source_target_pairs={{0,1},{1,0},{2,3},{3,2},{4,5},{5,4},{6,7},{7,6},{8,9},{9,8},{10,11... | collective-permute-start | bytes 6152 | tf_op jit(solution)/shard_map/ppermute | solution.py:29
  108.8 1.0 collective-permute-done.31
  110.3 5.3 %shard_map.67 = (bf16[512,2048]{1,0:T(8,128)(2,1)}, bf16[512,2048]{1,0:T(8,128)(2,1)S(1)}, bf16[256,2048]{1,0:T(8,128)(2,1)S(1)}, bf16[256,2048]{1,0:T(8,128)(2,1)S(1)}, bf16[512,512]{1,0:T(8,128)(2,1)S(1)}) custom-call(f32[512,2048]{1,0:T(8,128)S(1)} %get-tuple-element.53.student_ref, bf16[512,2048]{1,0:T(8,128)(2,1)S(1)} %get-tuple-element.54.slope_ref, ...), custom_call_target="tpu_custom_call" | custom-call | flops 1 | bytes 1 | tf_op jit(solution)/shard_map/pallas_call | solution.py:73
  115.7 3.4 %shard_map.68 = (bf16[256,2048]{1,0:T(8,128)(2,1)S(1)}, bf16[256,2048]{1,0:T(8,128)(2,1)S(1)}, bf16[256,2048]{1,0:T(8,128)(2,1)S(1)}, bf16[256,2048]{1,0:T(8,128...) custom-call(bf16[512,2048]{1,0:T(8,128)(2,1)S(1)} %get-tuple-element.64.grad_ref, ...), custom_call_target="tpu_custom_call" | custom-call | flops 1 | bytes 1 | tf_op jit(solution)/shard_map/pallas_call | solution.py:73
  120.0 1.2 collective-permute-start.36
  121.2 2.0 %collective-permute-start.35 = (bf16[512,512]{1,0:T(8,128)(2,1)S(1)}, bf16[512,512]{1,0:T(8,128)(2,1)S(1)}, u32[]{:S(2)}, u32[]{:S(2)}) collective-permute-start(bf16[512,512]{1,0:T(8,128)(2,1)S(1)} %get-tuple-element.74), channel_id=1, source_target_pairs={{0,1},{1,0},{2,3},{3,2},{4,5},{5,4},{6,7},{7,6},{8,9},{9,8},{10,11... | collective-permute-start | bytes 1572872 | tf_op jit(solution)/shard_map/ppermute | solution.py:29
  123.2 5.9 %shard_map.70.shares_ref = bf16[4,512,512]{2,1,0:T(8,128)(2,1)S(1)} custom-call(bf16[512,2048]{1,0:T(8,128)(2,1)S(1)} %get-tuple-element.64.grad_ref, bf16[256,2048]{1,0:T(8,128)(2,1)S(1)} %copy-done, bf16[256,2048]{1,0:T(8,128)(2,1)} %collective-permute-done.3.refs_5_.refs_1_, bf16[256,2048]{1,0:T(8,128)(2,1)S(1)} %collective-permute-done.4.refs_6_.refs_2_, ...), custom_call_target="tpu_custom_call" | custom-call | flops 1 | bytes 1 | tf_op jit(solution)/shard_map/pallas_call | solution.py:73
  129.1 6.7 %collective-permute-done.35.refs_0_ = bf16[512,512]{1,0:T(8,128)(2,1)S(1)} collective-permute-done((bf16[512,512]{1,0:T(8,128)(2,1)S(1)}, bf16[512,512]{1,0:T(8,128)(2,1)S(1)}, u32[]{:S(2)}, u32[]{:S(2)}) %collective-permute-start.35) | collective-permute-done | bytes 524320 | tf_op jit(solution)/shard_map/ppermute | solution.py:29
  137.4 1.4 collective-permute-start.39
  138.8 1.7 %collective-permute-start.41 = (bf16[512,512]{1,0:T(8,128)(2,1)S(1)}, bf16[512,512]{1,0:T(8,128)(2,1)S(1)}, u32[]{:S(2)}, u32[]{:S(2)}) collective-permute-start(bf16[512,512]{1,0:T(8,128)(2,1)S(1)} %get-tuple-element.84), channel_id=1, source_target_pairs={{0,1},{1,0},{2,3},{3,2},{4,5},{5,4},{6,7},{7,6},{8,9},{9,8},{10,11... | collective-permute-start | bytes 1572872 | tf_op jit(solution)/shard_map/ppermute | solution.py:29
  140.5 1.1 collective-permute-start.42
  141.7 21.6 %collective-permute-done.41 = bf16[512,512]{1,0:T(8,128)(2,1)S(1)} collective-permute-done((bf16[512,512]{1,0:T(8,128)(2,1)S(1)}, bf16[512,512]{1,0:T(8,128)(2,1)S(1)}, u32[]{:S(2)}, u32[]{:S(2)}) %collective-permute-start.41) | collective-permute-done | bytes 524320 | tf_op jit(solution)/shard_map/ppermute | solution.py:29
  163.2 3.5 %collective-permute-done.42 = bf16[512,512]{1,0:T(8,128)(2,1)S(1)} collective-permute-done((bf16[512,512]{1,0:T(8,128)(2,1)S(1)}, bf16[512,512]{1,0:T(8,128)(2,1)S(1)}, u32[]{:S(2)}, u32[]{:S(2)}) %collective-permute-start.42) | collective-permute-done | bytes 524320 | tf_op jit(solution)/shard_map/ppermute | solution.py:29
  166.8 1.0 fusion.1
  167.8 1.7 add_convert_fusion
  (92 shorter events, 16.3 us)
Async XLA Ops:
  0.6 45.9 %copy-start = (bf16[256,2048]{1,0:T(8,128)(2,1)S(1)}, bf16[256,2048]{1,0:T(8,128)(2,1)}, u32[]{:S(2)}) copy-start(bf16[256,2048]{1,0:T(8,128)(2,1)} %refs_0_.5) | copy-start | bytes 3145732
  0.6 30.2 %collective-permute-start.5 = (bf16[256,2048]{1,0:T(8,128)(2,1)}, bf16[256,2048]{1,0:T(8,128)(2,1)S(1)}, u32[]{:S(2)}, u32[]{:S(2)}) collective-permute-start(bf16[256,2048]{1,0:T(8,128)(2,1)} %refs_0_.5), channel_id=1, source_target_pairs={{0,16},{4,20},{8,24},{12,28},{16,0},{20,4},{24,8},{28,12},{1,17},{... | collective-permute-start | bytes 3145736 | tf_op jit(solution)/shard_map/ppermute | solution.py:29
  3.7 27.2 %collective-permute-start.4 = (bf16[256,2048]{1,0:T(8,128)(2,1)}, bf16[256,2048]{1,0:T(8,128)(2,1)S(1)}, u32[]{:S(2)}, u32[]{:S(2)}) collective-permute-start(bf16[256,2048]{1,0:T(8,128)(2,1)} %refs_0_.5), channel_id=1, source_target_pairs={{0,8},{4,12},{8,0},{12,4},{16,24},{20,28},{24,16},{28,20},{1,9},{5... | collective-permute-start | bytes 3145736 | tf_op jit(solution)/shard_map/ppermute | solution.py:29
  5.2 25.7 %collective-permute-start.1 = (bf16[512,512]{1,0:T(8,128)(2,1)}, bf16[512,512]{1,0:T(8,128)(2,1)}, u32[]{:S(2)}, u32[]{:S(2)}) collective-permute-start(bf16[512,512]{1,0:T(8,128)(2,1)} %refs_0_.3), channel_id=1, source_target_pairs={{0,2},{1,3},{2,0},{3,1},{4,6},{5,7},{6,4},{7,5},{8,10},{9,11},{10,... | collective-permute-start | bytes 1572872 | tf_op jit(solution)/shard_map/ppermute | solution.py:29
  7.8 24.8 %collective-permute-start.3 = (bf16[256,2048]{1,0:T(8,128)(2,1)}, bf16[256,2048]{1,0:T(8,128)(2,1)}, u32[]{:S(2)}, u32[]{:S(2)}) collective-permute-start(bf16[256,2048]{1,0:T(8,128)(2,1)} %refs_0_.5), channel_id=1, source_target_pairs={{0,4},{4,0},{8,12},{12,8},{16,20},{20,16},{24,28},{28,24},{1,5},{5... | collective-permute-start | bytes 3145736 | tf_op jit(solution)/shard_map/ppermute | solution.py:29
  7.8 24.8 %collective-permute-start = (bf16[512,512]{1,0:T(8,128)(2,1)}, bf16[512,512]{1,0:T(8,128)(2,1)}, u32[]{:S(2)}, u32[]{:S(2)}) collective-permute-start(bf16[512,512]{1,0:T(8,128)(2,1)} %refs_0_.3), channel_id=1, source_target_pairs={{0,1},{1,0},{2,3},{3,2},{4,5},{5,4},{6,7},{7,6},{8,9},{9,8},{10,11... | collective-permute-start | bytes 1572872 | tf_op jit(solution)/shard_map/ppermute | solution.py:29
  9.3 37.2 %copy-start.1 = (bf16[512,512]{1,0:T(8,128)(2,1)S(1)}, bf16[512,512]{1,0:T(8,128)(2,1)}, u32[]{:S(2)}) copy-start(bf16[512,512]{1,0:T(8,128)(2,1)} %refs_0_.3) | copy-start | bytes 1572868
  30.8 15.7 %collective-permute-start.6 = (bf16[256,2048]{1,0:T(8,128)(2,1)S(1)}, bf16[256,2048]{1,0:T(8,128)(2,1)S(1)}, u32[]{:S(2)}, u32[]{:S(2)}) collective-permute-start(bf16[256,2048]{1,0:T(8,128)(2,1)S(1)} %collective-permute-done.4.refs_6_.refs_2_), channel_id=1, source_target_pairs={{0,4},{4,0},{8,12},{12,8},{16,20},{20,16},{24,28},{28,24},{1,5},{5... | collective-permute-start | bytes 3145736 | tf_op jit(solution)/shard_map/ppermute | solution.py:29
  30.8 15.7 %collective-permute-start.7 = (bf16[256,2048]{1,0:T(8,128)(2,1)S(1)}, bf16[256,2048]{1,0:T(8,128)(2,1)S(1)}, u32[]{:S(2)}, u32[]{:S(2)}) collective-permute-start(bf16[256,2048]{1,0:T(8,128)(2,1)S(1)} %collective-permute-done.5.refs_8_.refs_4_), channel_id=1, source_target_pairs={{0,4},{4,0},{8,12},{12,8},{16,20},{20,16},{24,28},{28,24},{1,5},{5... | collective-permute-start | bytes 3145736 | tf_op jit(solution)/shard_map/ppermute | solution.py:29
  32.5 19.2 %collective-permute-start.8 = (bf16[256,2048]{1,0:T(8,128)(2,1)S(1)}, bf16[256,2048]{1,0:T(8,128)(2,1)S(1)}, u32[]{:S(2)}, u32[]{:S(2)}) collective-permute-start(bf16[256,2048]{1,0:T(8,128)(2,1)S(1)} %broadcast_select_fusion), channel_id=1, source_target_pairs={{0,16},{4,12},{8,24},{12,4},{16,0},{20,28},{24,8},{28,20},{1,17},{... | collective-permute-start | bytes 3145736 | tf_op jit(solution)/shard_map/ppermute | solution.py:34
  33.0 13.5 %collective-permute-start.2 = (bf16[512,512]{1,0:T(8,128)(2,1)}, bf16[512,512]{1,0:T(8,128)(2,1)S(1)}, u32[]{:S(2)}, u32[]{:S(2)}) collective-permute-start(bf16[512,512]{1,0:T(8,128)(2,1)} %collective-permute-done.1.refs_2_), channel_id=1, source_target_pairs={{0,1},{1,0},{2,3},{3,2},{4,5},{5,4},{6,7},{7,6},{8,9},{9,8},{10,11... | collective-permute-start | bytes 1572872 | tf_op jit(solution)/shard_map/ppermute | solution.py:29
  51.7 2.7 %collective-permute-start.9 = (bf16[256,2048]{1,0:T(8,128)(2,1)S(1)}, bf16[256,2048]{1,0:T(8,128)(2,1)S(1)}, u32[]{:S(2)}, u32[]{:S(2)}) collective-permute-start(bf16[256,2048]{1,0:T(8,128)(2,1)S(1)} %collective-permute-done.8.refs_0_.refs_6_), channel_id=1, source_target_pairs={{0,4},{4,0},{8,12},{12,8},{16,20},{20,16},{24,28},{28,24},{1,5},{5... | collective-permute-start | bytes 3145736 | tf_op jit(solution)/shard_map/ppermute | solution.py:29
  56.8 5.5 %collective-permute-start.10 = (f32[2,512]{1,0:T(2,128)S(1)}, f32[2,512]{1,0:T(2,128)S(1)}, u32[]{:S(2)}, u32[]{:S(2)}) collective-permute-start(f32[2,512]{1,0:T(2,128)S(1)} %get-tuple-element.55), channel_id=1, source_target_pairs={{0,3},{1,2},{2,1},{3,0},{4,7},{5,6},{6,5},{7,4},{8,11},{9,10},{10,... | collective-permute-start | bytes 12296 | tf_op jit(solution)/shard_map/ppermute | solution.py:29
  59.8 4.5 %collective-permute-start.11 = (f32[2,512]{1,0:T(2,128)S(1)}, f32[2,512]{1,0:T(2,128)S(1)}, u32[]{:S(2)}, u32[]{:S(2)}) collective-permute-start(f32[2,512]{1,0:T(2,128)S(1)} %get-tuple-element.55), channel_id=1, source_target_pairs={{0,2},{1,3},{2,0},{3,1},{4,6},{5,7},{6,4},{7,5},{8,10},{9,11},{10,... | collective-permute-start | bytes 12296 | tf_op jit(solution)/shard_map/ppermute | solution.py:29
  59.8 4.5 %collective-permute-start.12 = (f32[2,512]{1,0:T(2,128)S(1)}, f32[2,512]{1,0:T(2,128)S(1)}, u32[]{:S(2)}, u32[]{:S(2)}) collective-permute-start(f32[2,512]{1,0:T(2,128)S(1)} %get-tuple-element.55), channel_id=1, source_target_pairs={{0,1},{1,0},{2,3},{3,2},{4,5},{5,4},{6,7},{7,6},{8,9},{9,8},{10,11... | collective-permute-start | bytes 12296 | tf_op jit(solution)/shard_map/ppermute | solution.py:29
  64.3 5.5 %copy-start.2 = (bf16[2048]{0:T(1024)(128)(2,1)S(1)}, bf16[2048]{0:T(1024)(128)(2,1)}, u32[]{:S(2)}) copy-start(bf16[2048]{0:T(1024)(128)(2,1)} %param.5) | copy-start | bytes 12292
  65.0 1.2 collective-permute-start.13
  66.3 6.7 %collective-permute-start.16 = (f32[1,2048]{1,0:T(1,128)S(1)}, f32[1,2048]{1,0:T(1,128)S(1)}, u32[]{:S(2)}, u32[]{:S(2)}) collective-permute-start(f32[1,2048]{1,0:T(1,128)S(1)} %add.95), channel_id=1, source_target_pairs={{0,8},{4,12},{8,0},{12,4},{16,24},{20,28},{24,16},{28,20},{1,9},{5... | collective-permute-start | bytes 24584 | tf_op jit(solution)/shard_map/ppermute | solution.py:29
  67.8 5.1 %collective-permute-start.15 = (f32[1,2048]{1,0:T(1,128)S(1)}, f32[1,2048]{1,0:T(1,128)S(1)}, u32[]{:S(2)}, u32[]{:S(2)}) collective-permute-start(f32[1,2048]{1,0:T(1,128)S(1)} %add.95), channel_id=1, source_target_pairs={{0,16},{4,20},{8,24},{12,28},{16,0},{20,4},{24,8},{28,12},{1,17},{... | collective-permute-start | bytes 24584 | tf_op jit(solution)/shard_map/ppermute | solution.py:29
  68.3 4.5 %collective-permute-start.14 = (f32[1,2048]{1,0:T(1,128)S(1)}, f32[1,2048]{1,0:T(1,128)S(1)}, u32[]{:S(2)}, u32[]{:S(2)}) collective-permute-start(f32[1,2048]{1,0:T(1,128)S(1)} %add.95), channel_id=1, source_target_pairs={{0,24},{4,28},{8,16},{12,20},{16,8},{20,12},{24,0},{28,4},{1,25},{... | collective-permute-start | bytes 24584 | tf_op jit(solution)/shard_map/ppermute | solution.py:29
  73.6 5.4 %collective-permute-start.17 = (f32[1,512]{1,0:T(1,128)S(1)}, f32[1,512]{1,0:T(1,128)S(1)}, u32[]{:S(2)}, u32[]{:S(2)}) collective-permute-start(f32[1,512]{1,0:T(1,128)S(1)} %get-tuple-element.57), channel_id=1, source_target_pairs={{0,3},{1,2},{2,1},{3,0},{4,7},{5,6},{6,5},{7,4},{8,11},{9,10},{10,... | collective-permute-start | bytes 6152 | tf_op jit(solution)/shard_map/ppermute | solution.py:29
  75.1 4.5 %collective-permute-start.18 = (f32[1,512]{1,0:T(1,128)S(1)}, f32[1,512]{1,0:T(1,128)S(1)}, u32[]{:S(2)}, u32[]{:S(2)}) collective-permute-start(f32[1,512]{1,0:T(1,128)S(1)} %get-tuple-element.57), channel_id=1, source_target_pairs={{0,2},{1,3},{2,0},{3,1},{4,6},{5,7},{6,4},{7,5},{8,10},{9,11},{10,... | collective-permute-start | bytes 6152 | tf_op jit(solution)/shard_map/ppermute | solution.py:29
  75.7 3.9 %collective-permute-start.19 = (f32[1,512]{1,0:T(1,128)S(1)}, f32[1,512]{1,0:T(1,128)S(1)}, u32[]{:S(2)}, u32[]{:S(2)}) collective-permute-start(f32[1,512]{1,0:T(1,128)S(1)} %get-tuple-element.57), channel_id=1, source_target_pairs={{0,1},{1,0},{2,3},{3,2},{4,5},{5,4},{6,7},{7,6},{8,9},{9,8},{10,11... | collective-permute-start | bytes 6152 | tf_op jit(solution)/shard_map/ppermute | solution.py:29
  80.3 1.2 collective-permute-start.20
  81.5 4.6 %collective-permute-start.21 = (f32[1,2048]{1,0:T(1,128)S(1)}, f32[1,2048]{1,0:T(1,128)S(1)}, u32[]{:S(2)}, u32[]{:S(2)}) collective-permute-start(f32[1,2048]{1,0:T(1,128)S(1)} %add.102), channel_id=1, source_target_pairs={{0,24},{4,28},{8,16},{12,20},{16,8},{20,12},{24,0},{28,4},{1,25},{... | collective-permute-start | bytes 24584 | tf_op jit(solution)/shard_map/ppermute | solution.py:29
  83.1 3.7 %collective-permute-start.22 = (f32[1,2048]{1,0:T(1,128)S(1)}, f32[1,2048]{1,0:T(1,128)S(1)}, u32[]{:S(2)}, u32[]{:S(2)}) collective-permute-start(f32[1,2048]{1,0:T(1,128)S(1)} %add.102), channel_id=1, source_target_pairs={{0,16},{4,20},{8,24},{12,28},{16,0},{20,4},{24,8},{28,12},{1,17},{... | collective-permute-start | bytes 24584 | tf_op jit(solution)/shard_map/ppermute | solution.py:29
  83.6 3.7 %collective-permute-start.23 = (f32[1,2048]{1,0:T(1,128)S(1)}, f32[1,2048]{1,0:T(1,128)S(1)}, u32[]{:S(2)}, u32[]{:S(2)}) collective-permute-start(f32[1,2048]{1,0:T(1,128)S(1)} %add.102), channel_id=1, source_target_pairs={{0,8},{4,12},{8,0},{12,4},{16,24},{20,28},{24,16},{28,20},{1,9},{5... | collective-permute-start | bytes 24584 | tf_op jit(solution)/shard_map/ppermute | solution.py:29
  87.9 5.4 %collective-permute-start.24 = (f32[1,512]{1,0:T(1,128)S(1)}, f32[1,512]{1,0:T(1,128)S(1)}, u32[]{:S(2)}, u32[]{:S(2)}) collective-permute-start(f32[1,512]{1,0:T(1,128)S(1)} %get-tuple-element.59), channel_id=1, source_target_pairs={{0,3},{1,2},{2,1},{3,0},{4,7},{5,6},{6,5},{7,4},{8,11},{9,10},{10,... | collective-permute-start | bytes 6152 | tf_op jit(solution)/shard_map/ppermute | solution.py:29
  90.5 4.5 %collective-permute-start.25 = (f32[1,512]{1,0:T(1,128)S(1)}, f32[1,512]{1,0:T(1,128)S(1)}, u32[]{:S(2)}, u32[]{:S(2)}) collective-permute-start(f32[1,512]{1,0:T(1,128)S(1)} %get-tuple-element.59), channel_id=1, source_target_pairs={{0,2},{1,3},{2,0},{3,1},{4,6},{5,7},{6,4},{7,5},{8,10},{9,11},{10,... | collective-permute-start | bytes 6152 | tf_op jit(solution)/shard_map/ppermute | solution.py:29
  91.4 3.6 %collective-permute-start.26 = (f32[1,512]{1,0:T(1,128)S(1)}, f32[1,512]{1,0:T(1,128)S(1)}, u32[]{:S(2)}, u32[]{:S(2)}) collective-permute-start(f32[1,512]{1,0:T(1,128)S(1)} %get-tuple-element.59), channel_id=1, source_target_pairs={{0,1},{1,0},{2,3},{3,2},{4,5},{5,4},{6,7},{7,6},{8,9},{9,8},{10,11... | collective-permute-start | bytes 6152 | tf_op jit(solution)/shard_map/ppermute | solution.py:29
  95.7 1.2 collective-permute-start.27
  97.0 4.6 %collective-permute-start.28 = (f32[1,2048]{1,0:T(1,128)S(1)}, f32[1,2048]{1,0:T(1,128)S(1)}, u32[]{:S(2)}, u32[]{:S(2)}) collective-permute-start(f32[1,2048]{1,0:T(1,128)S(1)} %add.109), channel_id=1, source_target_pairs={{0,24},{4,28},{8,16},{12,20},{16,8},{20,12},{24,0},{28,4},{1,25},{... | collective-permute-start | bytes 24584 | tf_op jit(solution)/shard_map/ppermute | solution.py:29
  99.5 3.7 %collective-permute-start.29 = (f32[1,2048]{1,0:T(1,128)S(1)}, f32[1,2048]{1,0:T(1,128)S(1)}, u32[]{:S(2)}, u32[]{:S(2)}) collective-permute-start(f32[1,2048]{1,0:T(1,128)S(1)} %add.109), channel_id=1, source_target_pairs={{0,16},{4,20},{8,24},{12,28},{16,0},{20,4},{24,8},{28,12},{1,17},{... | collective-permute-start | bytes 24584 | tf_op jit(solution)/shard_map/ppermute | solution.py:29
  100.0 3.7 %collective-permute-start.30 = (f32[1,2048]{1,0:T(1,128)S(1)}, f32[1,2048]{1,0:T(1,128)S(1)}, u32[]{:S(2)}, u32[]{:S(2)}) collective-permute-start(f32[1,2048]{1,0:T(1,128)S(1)} %add.109), channel_id=1, source_target_pairs={{0,8},{4,12},{8,0},{12,4},{16,24},{20,28},{24,16},{28,20},{1,9},{5... | collective-permute-start | bytes 24584 | tf_op jit(solution)/shard_map/ppermute | solution.py:29
  104.3 5.4 %collective-permute-start.31 = (f32[1,512]{1,0:T(1,128)S(1)}, f32[1,512]{1,0:T(1,128)S(1)}, u32[]{:S(2)}, u32[]{:S(2)}) collective-permute-start(f32[1,512]{1,0:T(1,128)S(1)} %get-tuple-element.61), channel_id=1, source_target_pairs={{0,3},{1,2},{2,1},{3,0},{4,7},{5,6},{6,5},{7,4},{8,11},{9,10},{10,... | collective-permute-start | bytes 6152 | tf_op jit(solution)/shard_map/ppermute | solution.py:29
  105.8 4.5 %collective-permute-start.32 = (f32[1,512]{1,0:T(1,128)S(1)}, f32[1,512]{1,0:T(1,128)S(1)}, u32[]{:S(2)}, u32[]{:S(2)}) collective-permute-start(f32[1,512]{1,0:T(1,128)S(1)} %get-tuple-element.61), channel_id=1, source_target_pairs={{0,2},{1,3},{2,0},{3,1},{4,6},{5,7},{6,4},{7,5},{8,10},{9,11},{10,... | collective-permute-start | bytes 6152 | tf_op jit(solution)/shard_map/ppermute | solution.py:29
  106.7 3.6 %collective-permute-start.33 = (f32[1,512]{1,0:T(1,128)S(1)}, f32[1,512]{1,0:T(1,128)S(1)}, u32[]{:S(2)}, u32[]{:S(2)}) collective-permute-start(f32[1,512]{1,0:T(1,128)S(1)} %get-tuple-element.61), channel_id=1, source_target_pairs={{0,1},{1,0},{2,3},{3,2},{4,5},{5,4},{6,7},{7,6},{8,9},{9,8},{10,11... | collective-permute-start | bytes 6152 | tf_op jit(solution)/shard_map/ppermute | solution.py:29
  115.6 3.5 %collective-permute-start.34 = (bf16[256,2048]{1,0:T(8,128)(2,1)S(1)}, bf16[256,2048]{1,0:T(8,128)(2,1)S(1)}, u32[]{:S(2)}, u32[]{:S(2)}) collective-permute-start(bf16[256,2048]{1,0:T(8,128)(2,1)S(1)} %get-tuple-element.63), channel_id=1, source_target_pairs={{0,4},{4,0},{8,12},{12,8},{16,20},{20,16},{24,28},{28,24},{1,5},{5... | collective-permute-start | bytes 3145736 | tf_op jit(solution)/shard_map/ppermute | solution.py:29
  119.4 16.6 %collective-permute-start.38 = (bf16[256,2048]{1,0:T(8,128)(2,1)S(1)}, bf16[256,2048]{1,0:T(8,128)(2,1)S(1)}, u32[]{:S(2)}, u32[]{:S(2)}) collective-permute-start(bf16[256,2048]{1,0:T(8,128)(2,1)S(1)} %shard_map.69.refs_8_), channel_id=1, source_target_pairs={{0,8},{4,20},{8,0},{12,28},{16,24},{20,4},{24,16},{28,12},{1,9},{5... | collective-permute-start | bytes 3145736 | tf_op jit(solution)/shard_map/ppermute | solution.py:34
  120.0 16.0 %collective-permute-start.36 = (bf16[256,2048]{1,0:T(8,128)(2,1)S(1)}, bf16[256,2048]{1,0:T(8,128)(2,1)S(1)}, u32[]{:S(2)}, u32[]{:S(2)}) collective-permute-start(bf16[256,2048]{1,0:T(8,128)(2,1)S(1)} %get-tuple-element.77), channel_id=1, source_target_pairs={{0,4},{4,0},{8,12},{12,8},{16,20},{20,16},{24,28},{28,24},{1,5},{5... | collective-permute-start | bytes 3145736 | tf_op jit(solution)/shard_map/ppermute | solution.py:29
  121.2 14.8 %collective-permute-start.37 = (bf16[256,2048]{1,0:T(8,128)(2,1)S(1)}, bf16[256,2048]{1,0:T(8,128)(2,1)S(1)}, u32[]{:S(2)}, u32[]{:S(2)}) collective-permute-start(bf16[256,2048]{1,0:T(8,128)(2,1)S(1)} %get-tuple-element.78), channel_id=1, source_target_pairs={{0,4},{4,0},{8,12},{12,8},{16,20},{20,16},{24,28},{28,24},{1,5},{5... | collective-permute-start | bytes 3145736 | tf_op jit(solution)/shard_map/ppermute | solution.py:29
  121.2 14.6 %collective-permute-start.35 = (bf16[512,512]{1,0:T(8,128)(2,1)S(1)}, bf16[512,512]{1,0:T(8,128)(2,1)S(1)}, u32[]{:S(2)}, u32[]{:S(2)}) collective-permute-start(bf16[512,512]{1,0:T(8,128)(2,1)S(1)} %get-tuple-element.74), channel_id=1, source_target_pairs={{0,1},{1,0},{2,3},{3,2},{4,5},{5,4},{6,7},{7,6},{8,9},{9,8},{10,11... | collective-permute-start | bytes 1572872 | tf_op jit(solution)/shard_map/ppermute | solution.py:29
  136.4 31.4 %collective-permute-start.40 = (bf16[256,2048]{1,0:T(8,128)(2,1)S(1)}, bf16[256,2048]{1,0:T(8,128)(2,1)S(1)}, u32[]{:S(2)}, u32[]{:S(2)}) collective-permute-start(bf16[256,2048]{1,0:T(8,128)(2,1)S(1)} %shard_map.73), channel_id=1, source_target_pairs={{0,16},{4,20},{8,24},{12,28},{16,0},{20,4},{24,8},{28,12},{1,17},{... | collective-permute-start | bytes 3145736 | tf_op jit(solution)/shard_map/ppermute | solution.py:29
  137.4 30.3 %collective-permute-start.39 = (bf16[256,2048]{1,0:T(8,128)(2,1)S(1)}, bf16[256,2048]{1,0:T(8,128)(2,1)S(1)}, u32[]{:S(2)}, u32[]{:S(2)}) collective-permute-start(bf16[256,2048]{1,0:T(8,128)(2,1)S(1)} %shard_map.72), channel_id=1, source_target_pairs={{0,8},{4,12},{8,0},{12,4},{16,24},{20,28},{24,16},{28,20},{1,9},{5... | collective-permute-start | bytes 3145736 | tf_op jit(solution)/shard_map/ppermute | solution.py:29
  138.8 29.0 %collective-permute-start.43 = (bf16[256,2048]{1,0:T(8,128)(2,1)S(1)}, bf16[256,2048]{1,0:T(8,128)(2,1)S(1)}, u32[]{:S(2)}, u32[]{:S(2)}) collective-permute-start(bf16[256,2048]{1,0:T(8,128)(2,1)S(1)} %get-tuple-element.88), channel_id=1, source_target_pairs={{0,4},{4,0},{8,12},{12,8},{16,20},{20,16},{24,28},{28,24},{1,5},{5... | collective-permute-start | bytes 3145736 | tf_op jit(solution)/shard_map/ppermute | solution.py:29
  138.8 24.4 %collective-permute-start.41 = (bf16[512,512]{1,0:T(8,128)(2,1)S(1)}, bf16[512,512]{1,0:T(8,128)(2,1)S(1)}, u32[]{:S(2)}, u32[]{:S(2)}) collective-permute-start(bf16[512,512]{1,0:T(8,128)(2,1)S(1)} %get-tuple-element.84), channel_id=1, source_target_pairs={{0,1},{1,0},{2,3},{3,2},{4,5},{5,4},{6,7},{7,6},{8,9},{9,8},{10,11... | collective-permute-start | bytes 1572872 | tf_op jit(solution)/shard_map/ppermute | solution.py:29
  140.5 26.2 %collective-permute-start.42 = (bf16[512,512]{1,0:T(8,128)(2,1)S(1)}, bf16[512,512]{1,0:T(8,128)(2,1)S(1)}, u32[]{:S(2)}, u32[]{:S(2)}) collective-permute-start(bf16[512,512]{1,0:T(8,128)(2,1)S(1)} %get-tuple-element.85), channel_id=1, source_target_pairs={{0,2},{1,3},{2,0},{3,1},{4,6},{5,7},{6,4},{7,5},{8,10},{9,11},{10,... | collective-permute-start | bytes 1572872 | tf_op jit(solution)/shard_map/ppermute | solution.py:29

commit v16 on v15

--- a/solution.py
+++ b/solution.py
@@ -381,11 +381,10 @@
     came = [share_from[mask] if mask in share_from else flip(shares[mask | 1], "cls", 1) for mask in evens]
     made = call(functools.partial(onward_kernel, len(came)), [((rows, width), bf16)] * (1 + len(came)), [shares] + came)
     onward = dict(zip([1, *evens], made))
-    ready = lax.optimization_barrier((*onward.values(), *others.values(), *passed.values(), pairs[-1]))
-    onward = dict(zip(onward, ready))
-    others = dict(zip(others, ready[len(onward) :]))
-    passed = dict(zip(passed, ready[len(onward) + len(others) :]))
-    own = wide(pairs[-2]) + wide(flip(ready[-1], "sample", 1))
+    ready = lax.optimization_barrier((*others.values(), *passed.values(), pairs[-1], shares))
+    others = dict(zip(others, ready))
+    passed = dict(zip(passed, ready[len(others) :]))
+    own = wide(pairs[-2]) + wide(flip(ready[-2], "sample", 1))
     returned = [flip(value, "cls", mask) for mask, value in onward.items()]
     grad_features = sum([wide(value) for value in returned], wide(shares[0])).astype(bf16)
 

time: 170 us -> 169 us (level)
    ppermute x42, waiting for transfers between devices: 90.5 us -> 83.8 us  [flip(): lax.ppermute(value, axis, [(i, i ^ mask) for i in range(lax.axis_size(axi...]
    ppermute x2, waiting for transfers between devices: 0.01 us -> 6.34 us  [cross(): lax.ppermute(value, 'sample', [(i, i ^ (odd if i % 2 else even)) for i in...]
  transfers between devices with their start and end apart: 44 -> 44, of which waited for: 25 -> 25; matrix products, arithmetic and copies ran while one was open for 1% -> 1% of each run, Pallas kernels for 9% -> 10%
where the time goes in v16:
time: 169 us
  waiting for transfers between devices  90.1 us (53%)
  starting transfers between devices  47.2 us (28%)
  Pallas kernels  27.9 us (17%)
  other arithmetic  3.02 us (2%)
    ppermute x42, waiting for transfers between devices, flip(): lax.ppermute(value, axis, [(i, i ^ mask) for i in range(lax.axis_size(axi...  83.8 us
    ppermute x42, starting transfers between devices, flip(): lax.ppermute(value, axis, [(i, i ^ mask) for i in range(lax.axis_size(axi...  46.1 us
    pallas_call x16, Pallas kernels, call(): pl.pallas_call(kernel, out_shape=tuple((jax.ShapeDtypeStruct(shape, dtype...  27.9 us
    ppermute x2, waiting for transfers between devices, cross(): lax.ppermute(value, 'sample', [(i, i ^ (odd if i % 2 else even)) for i in...  6.34 us
  transfers between devices with their start and end apart: 44, of which 25 were waited for; matrix products, arithmetic and copies ran while one was open for 1% of the time, Pallas kernels for 10%

profile of v16, /device:TPU:0, one launch (start us, length us, event | category | flops | bytes accessed | tf_op | source)
XLA Modules:
  0.0 169.2 jit_solution(17884366840776734264)
XLA Ops:
  0.6 3.0 %collective-permute-start.5 = (bf16[256,2048]{1,0:T(8,128)(2,1)}, bf16[256,2048]{1,0:T(8,128)(2,1)S(1)}, u32[]{:S(2)}, u32[]{:S(2)}) collective-permute-start(bf16[256,2048]{1,0:T(8,128)(2,1)} %refs_0_.5), channel_id=1, source_target_pairs={{0,16},{4,20},{8,24},{12,28},{16,0},{20,4},{24,8},{28,12},{1,17},{... | collective-permute-start | bytes 3145736 | tf_op jit(solution)/shard_map/ppermute | solution.py:29
  3.7 1.5 collective-permute-start.4
  5.2 2.6 %collective-permute-start.1 = (bf16[512,512]{1,0:T(8,128)(2,1)}, bf16[512,512]{1,0:T(8,128)(2,1)}, u32[]{:S(2)}, u32[]{:S(2)}) collective-permute-start(bf16[512,512]{1,0:T(8,128)(2,1)} %refs_0_.3), channel_id=1, source_target_pairs={{0,2},{1,3},{2,0},{3,1},{4,6},{5,7},{6,4},{7,5},{8,10},{9,11},{10,... | collective-permute-start | bytes 1572872 | tf_op jit(solution)/shard_map/ppermute | solution.py:29
  7.8 1.6 collective-permute-start
  9.3 21.5 %collective-permute-done.1.refs_2_ = bf16[512,512]{1,0:T(8,128)(2,1)} collective-permute-done((bf16[512,512]{1,0:T(8,128)(2,1)}, bf16[512,512]{1,0:T(8,128)(2,1)}, u32[]{:S(2)}, u32[]{:S(2)}) %collective-permute-start.1) | collective-permute-done | bytes 524320 | tf_op jit(solution)/shard_map/ppermute | solution.py:29
  31.5 1.1 collective-permute-done.refs_1_
  33.0 13.5 %collective-permute-done.2.refs_3_ = bf16[512,512]{1,0:T(8,128)(2,1)S(1)} collective-permute-done((bf16[512,512]{1,0:T(8,128)(2,1)}, bf16[512,512]{1,0:T(8,128)(2,1)S(1)}, u32[]{:S(2)}, u32[]{:S(2)}) %collective-permute-start.2) | collective-permute-done | bytes 524320 | tf_op jit(solution)/shard_map/ppermute | solution.py:29
  46.6 5.1 %shard_map.58 = (bf16[4,512,512]{2,1,0:T(8,128)(2,1)S(1)}, f32[512,2048]{1,0:T(8,128)S(1)}) custom-call(bf16[512,512]{1,0:T(8,128)(2,1)S(1)} %copy-done.1, bf16[512,512]{1,0:T(8,128)(2,1)} %collective-permute-done.refs_1_, bf16[512,512]{1,0:T(8,128)(2,1)} %collective-permute-done.1.refs_2_, bf16[512,512]{1,0:T(8,128)(2,1)S(1)} %collective-permute-done.2.refs_3_, ...), custom_call_target="tpu_custom_call" | custom-call | flops 1 | bytes 1 | tf_op jit(solution)/shard_map/pallas_call | solution.py:73
  51.8 2.6 %collective-permute-done.9.refs_1_.refs_7_ = bf16[256,2048]{1,0:T(8,128)(2,1)S(1)} collective-permute-done((bf16[256,2048]{1,0:T(8,128)(2,1)S(1)}, bf16[256,2048]{1,0:T(8,128)(2,1)S(1)}, u32[]{:S(2)}, u32[]{:S(2)}) %collective-permute-start.9) | collective-permute-done | bytes 1048608 | tf_op jit(solution)/shard_map/ppermute | solution.py:29
  54.4 2.4 %shard_map.59 = (f32[512,2048]{1,0:T(8,128)S(1)}, bf16[512,2048]{1,0:T(8,128)(2,1)S(1)}, f32[2,512]{1,0:T(2,128)S(1)}) custom-call(f32[512,2048]{1,0:T(8,128)S(1)} %get-tuple-element.47.logits_ref, bf16[4,512,512]{2,1,0:T(8,128)(2,1)S(1)} %get-tuple-element.48.blocks_ref, bf16[256,2048]{1,0:T(8,128)(2,1)S(1)} %collective-permute-done.8.refs_0_.refs_6_, ...), custom_call_target="tpu_custom_call" | custom-call | flops 1 | bytes 1 | tf_op jit(solution)/shard_map/pallas_call | solution.py:73
  56.8 2.9 %collective-permute-start.10 = (f32[2,512]{1,0:T(2,128)S(1)}, f32[2,512]{1,0:T(2,128)S(1)}, u32[]{:S(2)}, u32[]{:S(2)}) collective-permute-start(f32[2,512]{1,0:T(2,128)S(1)} %get-tuple-element.53), channel_id=1, source_target_pairs={{0,3},{1,2},{2,1},{3,0},{4,7},{5,6},{6,5},{7,4},{8,11},{9,10},{10,... | collective-permute-start | bytes 12296 | tf_op jit(solution)/shard_map/ppermute | solution.py:29
  59.8 1.5 collective-permute-start.12
  62.3 1.9 %collective-permute-done.11 = f32[2,512]{1,0:T(2,128)S(1)} collective-permute-done((f32[2,512]{1,0:T(2,128)S(1)}, f32[2,512]{1,0:T(2,128)S(1)}, u32[]{:S(2)}, u32[]{:S(2)}) %collective-permute-start.11) | collective-permute-done | bytes 4128 | tf_op jit(solution)/shard_map/ppermute | solution.py:29
  65.1 1.2 collective-permute-done.13
  66.3 1.6 collective-permute-start.16
  68.3 1.5 collective-permute-start.14
  69.8 3.1 %collective-permute-done.14 = f32[1,2048]{1,0:T(1,128)S(1)} collective-permute-done((f32[1,2048]{1,0:T(1,128)S(1)}, f32[1,2048]{1,0:T(1,128)S(1)}, u32[]{:S(2)}, u32[]{:S(2)}) %collective-permute-start.14) | collective-permute-done | bytes 8224 | tf_op jit(solution)/shard_map/ppermute | solution.py:29
  73.6 1.5 collective-permute-start.17
  75.7 2.3 %collective-permute-start.19 = (f32[1,512]{1,0:T(1,128)S(1)}, f32[1,512]{1,0:T(1,128)S(1)}, u32[]{:S(2)}, u32[]{:S(2)}) collective-permute-start(f32[1,512]{1,0:T(1,128)S(1)} %get-tuple-element.55), channel_id=1, source_target_pairs={{0,1},{1,0},{2,3},{3,2},{4,5},{5,4},{6,7},{7,6},{8,9},{9,8},{10,11... | collective-permute-start | bytes 6152 | tf_op jit(solution)/shard_map/ppermute | solution.py:29
  78.0 1.0 collective-permute-done.17
  80.4 1.2 collective-permute-done.20
  81.5 1.6 collective-permute-start.21
  83.6 1.5 collective-permute-start.23
  85.1 1.1 collective-permute-done.21
  87.9 2.6 %collective-permute-start.24 = (f32[1,512]{1,0:T(1,128)S(1)}, f32[1,512]{1,0:T(1,128)S(1)}, u32[]{:S(2)}, u32[]{:S(2)}) collective-permute-start(f32[1,512]{1,0:T(1,128)S(1)} %get-tuple-element.57), channel_id=1, source_target_pairs={{0,3},{1,2},{2,1},{3,0},{4,7},{5,6},{6,5},{7,4},{8,11},{9,10},{10,... | collective-permute-start | bytes 6152 | tf_op jit(solution)/shard_map/ppermute | solution.py:29
  90.5 0.9 collective-permute-start.25
  92.4 1.0 collective-permute-done.24
  93.4 1.7 collective-permute-done.25
  95.8 1.2 collective-permute-done.27
  97.0 2.5 %collective-permute-start.28 = (f32[1,2048]{1,0:T(1,128)S(1)}, f32[1,2048]{1,0:T(1,128)S(1)}, u32[]{:S(2)}, u32[]{:S(2)}) collective-permute-start(f32[1,2048]{1,0:T(1,128)S(1)} %add.109), channel_id=1, source_target_pairs={{0,24},{4,28},{8,16},{12,20},{16,8},{20,12},{24,0},{28,4},{1,25},{... | collective-permute-start | bytes 24584 | tf_op jit(solution)/shard_map/ppermute | solution.py:29
  100.5 1.1 collective-permute-done.28
  101.6 1.5 collective-permute-done.29
  104.3 1.5 collective-permute-start.31
  105.8 0.9 collective-permute-start.32
  106.7 2.0 %collective-permute-start.33 = (f32[1,512]{1,0:T(1,128)S(1)}, f32[1,512]{1,0:T(1,128)S(1)}, u32[]{:S(2)}, u32[]{:S(2)}) collective-permute-start(f32[1,512]{1,0:T(1,128)S(1)} %get-tuple-element.59), channel_id=1, source_target_pairs={{0,1},{1,0},{2,3},{3,2},{4,5},{5,4},{6,7},{7,6},{8,9},{9,8},{10,11... | collective-permute-start | bytes 6152 | tf_op jit(solution)/shard_map/ppermute | solution.py:29
  108.8 1.0 collective-permute-done.31
  110.3 5.3 %shard_map.67 = (bf16[512,2048]{1,0:T(8,128)(2,1)}, bf16[512,2048]{1,0:T(8,128)(2,1)S(1)}, bf16[256,2048]{1,0:T(8,128)(2,1)S(1)}, bf16[256,2048]{1,0:T(8,128)(2,1)S(1)}, bf16[512,512]{1,0:T(8,128)(2,1)S(1)}) custom-call(f32[512,2048]{1,0:T(8,128)S(1)} %get-tuple-element.51.student_ref, bf16[512,2048]{1,0:T(8,128)(2,1)S(1)} %get-tuple-element.52.slope_ref, ...), custom_call_target="tpu_custom_call" | custom-call | flops 1 | bytes 1 | tf_op jit(solution)/shard_map/pallas_call | solution.py:73
  115.7 3.4 %shard_map.68 = (bf16[256,2048]{1,0:T(8,128)(2,1)S(1)}, bf16[256,2048]{1,0:T(8,128)(2,1)S(1)}, bf16[256,2048]{1,0:T(8,128)(2,1)S(1)}, bf16[256,2048]{1,0:T(8,128...) custom-call(bf16[512,2048]{1,0:T(8,128)(2,1)S(1)} %get-tuple-element.62.grad_ref, ...), custom_call_target="tpu_custom_call" | custom-call | flops 1 | bytes 1 | tf_op jit(solution)/shard_map/pallas_call | solution.py:73
  120.6 2.0 %collective-permute-start.40 = (bf16[512,512]{1,0:T(8,128)(2,1)S(1)}, bf16[512,512]{1,0:T(8,128)(2,1)S(1)}, u32[]{:S(2)}, u32[]{:S(2)}) collective-permute-start(bf16[512,512]{1,0:T(8,128)(2,1)S(1)} %get-tuple-element.79), channel_id=1, source_target_pairs={{0,1},{1,0},{2,3},{3,2},{4,5},{5,4},{6,7},{7,6},{8,9},{9,8},{10,11... | collective-permute-start | bytes 1572872 | tf_op jit(solution)/shard_map/ppermute | solution.py:29
  122.6 5.9 %shard_map.70.shares_ref = bf16[4,512,512]{2,1,0:T(8,128)(2,1)S(1)} custom-call(bf16[512,2048]{1,0:T(8,128)(2,1)S(1)} %get-tuple-element.62.grad_ref, bf16[256,2048]{1,0:T(8,128)(2,1)S(1)} %copy-done, bf16[256,2048]{1,0:T(8,128)(2,1)} %collective-permute-done.3.refs_5_.refs_1_, bf16[256,2048]{1,0:T(8,128)(2,1)S(1)} %collective-permute-done.4.refs_6_.refs_2_, ...), custom_call_target="tpu_custom_call" | custom-call | flops 1 | bytes 1 | tf_op jit(solution)/shard_map/pallas_call | solution.py:73
  128.5 6.3 %collective-permute-done.37.refs_2_ = bf16[256,2048]{1,0:T(8,128)(2,1)S(1)} collective-permute-done((bf16[256,2048]{1,0:T(8,128)(2,1)S(1)}, bf16[256,2048]{1,0:T(8,128)(2,1)S(1)}, u32[]{:S(2)}, u32[]{:S(2)}) %collective-permute-start.37) | collective-permute-done | bytes 1048608 | tf_op jit(solution)/shard_map/ppermute | solution.py:34
  135.3 1.6 collective-permute-start.39
  138.1 2.1 %collective-permute-start.41 = (bf16[512,512]{1,0:T(8,128)(2,1)S(1)}, bf16[512,512]{1,0:T(8,128)(2,1)S(1)}, u32[]{:S(2)}, u32[]{:S(2)}) collective-permute-start(bf16[512,512]{1,0:T(8,128)(2,1)S(1)} %get-tuple-element.80), channel_id=1, source_target_pairs={{0,1},{1,0},{2,3},{3,2},{4,5},{5,4},{6,7},{7,6},{8,9},{9,8},{10,11... | collective-permute-start | bytes 1572872 | tf_op jit(solution)/shard_map/ppermute | solution.py:29
  140.2 1.1 collective-permute-start.42
  141.3 21.6 %collective-permute-done.41 = bf16[512,512]{1,0:T(8,128)(2,1)S(1)} collective-permute-done((bf16[512,512]{1,0:T(8,128)(2,1)S(1)}, bf16[512,512]{1,0:T(8,128)(2,1)S(1)}, u32[]{:S(2)}, u32[]{:S(2)}) %collective-permute-start.41) | collective-permute-done | bytes 524320 | tf_op jit(solution)/shard_map/ppermute | solution.py:29
  162.9 3.6 %collective-permute-done.42 = bf16[512,512]{1,0:T(8,128)(2,1)S(1)} collective-permute-done((bf16[512,512]{1,0:T(8,128)(2,1)S(1)}, bf16[512,512]{1,0:T(8,128)(2,1)S(1)}, u32[]{:S(2)}, u32[]{:S(2)}) %collective-permute-start.42) | collective-permute-done | bytes 524320 | tf_op jit(solution)/shard_map/ppermute | solution.py:29
  166.4 1.0 fusion.1
  167.4 1.7 %add_convert_fusion = bf16[256,2048]{1,0:T(8,128)(2,1)} fusion(bf16[256,2048]{1,0:T(8,128)(2,1)S(1)} %collective-permute-done.39, bf16[256,2048]{1,0:T(8,128)(2,1)S(1)} %collective-permute-done.38, bf16[256,2048]{1,0:T(8,128)(2,1)S(1)} %collective-permute-done.43, bf16[256,2048]{1,0:T(8,128)(2,1)S(1)} %get-tuple-element.83), kind=kLoop, calls=%fused_computation | loop fusion | flops 4194304 | bytes 5242880 | tf_op jit(solution)/shard_map/convert_element_type | solution.py:401
  (92 shorter events, 16.0 us)
Async XLA Ops:
  0.6 45.9 %copy-start = (bf16[256,2048]{1,0:T(8,128)(2,1)S(1)}, bf16[256,2048]{1,0:T(8,128)(2,1)}, u32[]{:S(2)}) copy-start(bf16[256,2048]{1,0:T(8,128)(2,1)} %refs_0_.5) | copy-start | bytes 3145732
  0.6 30.2 %collective-permute-start.5 = (bf16[256,2048]{1,0:T(8,128)(2,1)}, bf16[256,2048]{1,0:T(8,128)(2,1)S(1)}, u32[]{:S(2)}, u32[]{:S(2)}) collective-permute-start(bf16[256,2048]{1,0:T(8,128)(2,1)} %refs_0_.5), channel_id=1, source_target_pairs={{0,16},{4,20},{8,24},{12,28},{16,0},{20,4},{24,8},{28,12},{1,17},{... | collective-permute-start | bytes 3145736 | tf_op jit(solution)/shard_map/ppermute | solution.py:29
  3.7 27.2 %collective-permute-start.4 = (bf16[256,2048]{1,0:T(8,128)(2,1)}, bf16[256,2048]{1,0:T(8,128)(2,1)S(1)}, u32[]{:S(2)}, u32[]{:S(2)}) collective-permute-start(bf16[256,2048]{1,0:T(8,128)(2,1)} %refs_0_.5), channel_id=1, source_target_pairs={{0,8},{4,12},{8,0},{12,4},{16,24},{20,28},{24,16},{28,20},{1,9},{5... | collective-permute-start | bytes 3145736 | tf_op jit(solution)/shard_map/ppermute | solution.py:29
  5.2 25.7 %collective-permute-start.1 = (bf16[512,512]{1,0:T(8,128)(2,1)}, bf16[512,512]{1,0:T(8,128)(2,1)}, u32[]{:S(2)}, u32[]{:S(2)}) collective-permute-start(bf16[512,512]{1,0:T(8,128)(2,1)} %refs_0_.3), channel_id=1, source_target_pairs={{0,2},{1,3},{2,0},{3,1},{4,6},{5,7},{6,4},{7,5},{8,10},{9,11},{10,... | collective-permute-start | bytes 1572872 | tf_op jit(solution)/shard_map/ppermute | solution.py:29
  7.8 24.8 %collective-permute-start.3 = (bf16[256,2048]{1,0:T(8,128)(2,1)}, bf16[256,2048]{1,0:T(8,128)(2,1)}, u32[]{:S(2)}, u32[]{:S(2)}) collective-permute-start(bf16[256,2048]{1,0:T(8,128)(2,1)} %refs_0_.5), channel_id=1, source_target_pairs={{0,4},{4,0},{8,12},{12,8},{16,20},{20,16},{24,28},{28,24},{1,5},{5... | collective-permute-start | bytes 3145736 | tf_op jit(solution)/shard_map/ppermute | solution.py:29
  7.8 24.8 %collective-permute-start = (bf16[512,512]{1,0:T(8,128)(2,1)}, bf16[512,512]{1,0:T(8,128)(2,1)}, u32[]{:S(2)}, u32[]{:S(2)}) collective-permute-start(bf16[512,512]{1,0:T(8,128)(2,1)} %refs_0_.3), channel_id=1, source_target_pairs={{0,1},{1,0},{2,3},{3,2},{4,5},{5,4},{6,7},{7,6},{8,9},{9,8},{10,11... | collective-permute-start | bytes 1572872 | tf_op jit(solution)/shard_map/ppermute | solution.py:29
  9.3 37.2 %copy-start.1 = (bf16[512,512]{1,0:T(8,128)(2,1)S(1)}, bf16[512,512]{1,0:T(8,128)(2,1)}, u32[]{:S(2)}) copy-start(bf16[512,512]{1,0:T(8,128)(2,1)} %refs_0_.3) | copy-start | bytes 1572868
  30.8 15.7 %collective-permute-start.6 = (bf16[256,2048]{1,0:T(8,128)(2,1)S(1)}, bf16[256,2048]{1,0:T(8,128)(2,1)S(1)}, u32[]{:S(2)}, u32[]{:S(2)}) collective-permute-start(bf16[256,2048]{1,0:T(8,128)(2,1)S(1)} %collective-permute-done.4.refs_6_.refs_2_), channel_id=1, source_target_pairs={{0,4},{4,0},{8,12},{12,8},{16,20},{20,16},{24,28},{28,24},{1,5},{5... | collective-permute-start | bytes 3145736 | tf_op jit(solution)/shard_map/ppermute | solution.py:29
  30.8 15.7 %collective-permute-start.7 = (bf16[256,2048]{1,0:T(8,128)(2,1)S(1)}, bf16[256,2048]{1,0:T(8,128)(2,1)S(1)}, u32[]{:S(2)}, u32[]{:S(2)}) collective-permute-start(bf16[256,2048]{1,0:T(8,128)(2,1)S(1)} %collective-permute-done.5.refs_8_.refs_4_), channel_id=1, source_target_pairs={{0,4},{4,0},{8,12},{12,8},{16,20},{20,16},{24,28},{28,24},{1,5},{5... | collective-permute-start | bytes 3145736 | tf_op jit(solution)/shard_map/ppermute | solution.py:29
  32.5 19.2 %collective-permute-start.8 = (bf16[256,2048]{1,0:T(8,128)(2,1)S(1)}, bf16[256,2048]{1,0:T(8,128)(2,1)S(1)}, u32[]{:S(2)}, u32[]{:S(2)}) collective-permute-start(bf16[256,2048]{1,0:T(8,128)(2,1)S(1)} %broadcast_select_fusion), channel_id=1, source_target_pairs={{0,16},{4,12},{8,24},{12,4},{16,0},{20,28},{24,8},{28,20},{1,17},{... | collective-permute-start | bytes 3145736 | tf_op jit(solution)/shard_map/ppermute | solution.py:34
  33.0 13.5 %collective-permute-start.2 = (bf16[512,512]{1,0:T(8,128)(2,1)}, bf16[512,512]{1,0:T(8,128)(2,1)S(1)}, u32[]{:S(2)}, u32[]{:S(2)}) collective-permute-start(bf16[512,512]{1,0:T(8,128)(2,1)} %collective-permute-done.1.refs_2_), channel_id=1, source_target_pairs={{0,1},{1,0},{2,3},{3,2},{4,5},{5,4},{6,7},{7,6},{8,9},{9,8},{10,11... | collective-permute-start | bytes 1572872 | tf_op jit(solution)/shard_map/ppermute | solution.py:29
  51.7 2.7 %collective-permute-start.9 = (bf16[256,2048]{1,0:T(8,128)(2,1)S(1)}, bf16[256,2048]{1,0:T(8,128)(2,1)S(1)}, u32[]{:S(2)}, u32[]{:S(2)}) collective-permute-start(bf16[256,2048]{1,0:T(8,128)(2,1)S(1)} %collective-permute-done.8.refs_0_.refs_6_), channel_id=1, source_target_pairs={{0,4},{4,0},{8,12},{12,8},{16,20},{20,16},{24,28},{28,24},{1,5},{5... | collective-permute-start | bytes 3145736 | tf_op jit(solution)/shard_map/ppermute | solution.py:29
  56.8 5.5 %collective-permute-start.10 = (f32[2,512]{1,0:T(2,128)S(1)}, f32[2,512]{1,0:T(2,128)S(1)}, u32[]{:S(2)}, u32[]{:S(2)}) collective-permute-start(f32[2,512]{1,0:T(2,128)S(1)} %get-tuple-element.53), channel_id=1, source_target_pairs={{0,3},{1,2},{2,1},{3,0},{4,7},{5,6},{6,5},{7,4},{8,11},{9,10},{10,... | collective-permute-start | bytes 12296 | tf_op jit(solution)/shard_map/ppermute | solution.py:29
  59.8 4.5 %collective-permute-start.11 = (f32[2,512]{1,0:T(2,128)S(1)}, f32[2,512]{1,0:T(2,128)S(1)}, u32[]{:S(2)}, u32[]{:S(2)}) collective-permute-start(f32[2,512]{1,0:T(2,128)S(1)} %get-tuple-element.53), channel_id=1, source_target_pairs={{0,2},{1,3},{2,0},{3,1},{4,6},{5,7},{6,4},{7,5},{8,10},{9,11},{10,... | collective-permute-start | bytes 12296 | tf_op jit(solution)/shard_map/ppermute | solution.py:29
  59.8 4.5 %collective-permute-start.12 = (f32[2,512]{1,0:T(2,128)S(1)}, f32[2,512]{1,0:T(2,128)S(1)}, u32[]{:S(2)}, u32[]{:S(2)}) collective-permute-start(f32[2,512]{1,0:T(2,128)S(1)} %get-tuple-element.53), channel_id=1, source_target_pairs={{0,1},{1,0},{2,3},{3,2},{4,5},{5,4},{6,7},{7,6},{8,9},{9,8},{10,11... | collective-permute-start | bytes 12296 | tf_op jit(solution)/shard_map/ppermute | solution.py:29
  64.3 5.5 %copy-start.2 = (bf16[2048]{0:T(1024)(128)(2,1)S(1)}, bf16[2048]{0:T(1024)(128)(2,1)}, u32[]{:S(2)}) copy-start(bf16[2048]{0:T(1024)(128)(2,1)} %param.5) | copy-start | bytes 12292
  65.0 1.2 collective-permute-start.13
  66.3 6.7 %collective-permute-start.16 = (f32[1,2048]{1,0:T(1,128)S(1)}, f32[1,2048]{1,0:T(1,128)S(1)}, u32[]{:S(2)}, u32[]{:S(2)}) collective-permute-start(f32[1,2048]{1,0:T(1,128)S(1)} %add.95), channel_id=1, source_target_pairs={{0,8},{4,12},{8,0},{12,4},{16,24},{20,28},{24,16},{28,20},{1,9},{5... | collective-permute-start | bytes 24584 | tf_op jit(solution)/shard_map/ppermute | solution.py:29
  67.8 5.1 %collective-permute-start.15 = (f32[1,2048]{1,0:T(1,128)S(1)}, f32[1,2048]{1,0:T(1,128)S(1)}, u32[]{:S(2)}, u32[]{:S(2)}) collective-permute-start(f32[1,2048]{1,0:T(1,128)S(1)} %add.95), channel_id=1, source_target_pairs={{0,16},{4,20},{8,24},{12,28},{16,0},{20,4},{24,8},{28,12},{1,17},{... | collective-permute-start | bytes 24584 | tf_op jit(solution)/shard_map/ppermute | solution.py:29
  68.3 4.5 %collective-permute-start.14 = (f32[1,2048]{1,0:T(1,128)S(1)}, f32[1,2048]{1,0:T(1,128)S(1)}, u32[]{:S(2)}, u32[]{:S(2)}) collective-permute-start(f32[1,2048]{1,0:T(1,128)S(1)} %add.95), channel_id=1, source_target_pairs={{0,24},{4,28},{8,16},{12,20},{16,8},{20,12},{24,0},{28,4},{1,25},{... | collective-permute-start | bytes 24584 | tf_op jit(solution)/shard_map/ppermute | solution.py:29
  73.6 5.4 %collective-permute-start.17 = (f32[1,512]{1,0:T(1,128)S(1)}, f32[1,512]{1,0:T(1,128)S(1)}, u32[]{:S(2)}, u32[]{:S(2)}) collective-permute-start(f32[1,512]{1,0:T(1,128)S(1)} %get-tuple-element.55), channel_id=1, source_target_pairs={{0,3},{1,2},{2,1},{3,0},{4,7},{5,6},{6,5},{7,4},{8,11},{9,10},{10,... | collective-permute-start | bytes 6152 | tf_op jit(solution)/shard_map/ppermute | solution.py:29
  75.1 4.5 %collective-permute-start.18 = (f32[1,512]{1,0:T(1,128)S(1)}, f32[1,512]{1,0:T(1,128)S(1)}, u32[]{:S(2)}, u32[]{:S(2)}) collective-permute-start(f32[1,512]{1,0:T(1,128)S(1)} %get-tuple-element.55), channel_id=1, source_target_pairs={{0,2},{1,3},{2,0},{3,1},{4,6},{5,7},{6,4},{7,5},{8,10},{9,11},{10,... | collective-permute-start | bytes 6152 | tf_op jit(solution)/shard_map/ppermute | solution.py:29
  75.7 3.9 %collective-permute-start.19 = (f32[1,512]{1,0:T(1,128)S(1)}, f32[1,512]{1,0:T(1,128)S(1)}, u32[]{:S(2)}, u32[]{:S(2)}) collective-permute-start(f32[1,512]{1,0:T(1,128)S(1)} %get-tuple-element.55), channel_id=1, source_target_pairs={{0,1},{1,0},{2,3},{3,2},{4,5},{5,4},{6,7},{7,6},{8,9},{9,8},{10,11... | collective-permute-start | bytes 6152 | tf_op jit(solution)/shard_map/ppermute | solution.py:29
  80.3 1.2 collective-permute-start.20
  81.5 4.6 %collective-permute-start.21 = (f32[1,2048]{1,0:T(1,128)S(1)}, f32[1,2048]{1,0:T(1,128)S(1)}, u32[]{:S(2)}, u32[]{:S(2)}) collective-permute-start(f32[1,2048]{1,0:T(1,128)S(1)} %add.102), channel_id=1, source_target_pairs={{0,24},{4,28},{8,16},{12,20},{16,8},{20,12},{24,0},{28,4},{1,25},{... | collective-permute-start | bytes 24584 | tf_op jit(solution)/shard_map/ppermute | solution.py:29
  83.1 3.7 %collective-permute-start.22 = (f32[1,2048]{1,0:T(1,128)S(1)}, f32[1,2048]{1,0:T(1,128)S(1)}, u32[]{:S(2)}, u32[]{:S(2)}) collective-permute-start(f32[1,2048]{1,0:T(1,128)S(1)} %add.102), channel_id=1, source_target_pairs={{0,16},{4,20},{8,24},{12,28},{16,0},{20,4},{24,8},{28,12},{1,17},{... | collective-permute-start | bytes 24584 | tf_op jit(solution)/shard_map/ppermute | solution.py:29
  83.6 3.7 %collective-permute-start.23 = (f32[1,2048]{1,0:T(1,128)S(1)}, f32[1,2048]{1,0:T(1,128)S(1)}, u32[]{:S(2)}, u32[]{:S(2)}) collective-permute-start(f32[1,2048]{1,0:T(1,128)S(1)} %add.102), channel_id=1, source_target_pairs={{0,8},{4,12},{8,0},{12,4},{16,24},{20,28},{24,16},{28,20},{1,9},{5... | collective-permute-start | bytes 24584 | tf_op jit(solution)/shard_map/ppermute | solution.py:29
  87.9 5.4 %collective-permute-start.24 = (f32[1,512]{1,0:T(1,128)S(1)}, f32[1,512]{1,0:T(1,128)S(1)}, u32[]{:S(2)}, u32[]{:S(2)}) collective-permute-start(f32[1,512]{1,0:T(1,128)S(1)} %get-tuple-element.57), channel_id=1, source_target_pairs={{0,3},{1,2},{2,1},{3,0},{4,7},{5,6},{6,5},{7,4},{8,11},{9,10},{10,... | collective-permute-start | bytes 6152 | tf_op jit(solution)/shard_map/ppermute | solution.py:29
  90.5 4.5 %collective-permute-start.25 = (f32[1,512]{1,0:T(1,128)S(1)}, f32[1,512]{1,0:T(1,128)S(1)}, u32[]{:S(2)}, u32[]{:S(2)}) collective-permute-start(f32[1,512]{1,0:T(1,128)S(1)} %get-tuple-element.57), channel_id=1, source_target_pairs={{0,2},{1,3},{2,0},{3,1},{4,6},{5,7},{6,4},{7,5},{8,10},{9,11},{10,... | collective-permute-start | bytes 6152 | tf_op jit(solution)/shard_map/ppermute | solution.py:29
  91.4 3.6 %collective-permute-start.26 = (f32[1,512]{1,0:T(1,128)S(1)}, f32[1,512]{1,0:T(1,128)S(1)}, u32[]{:S(2)}, u32[]{:S(2)}) collective-permute-start(f32[1,512]{1,0:T(1,128)S(1)} %get-tuple-element.57), channel_id=1, source_target_pairs={{0,1},{1,0},{2,3},{3,2},{4,5},{5,4},{6,7},{7,6},{8,9},{9,8},{10,11... | collective-permute-start | bytes 6152 | tf_op jit(solution)/shard_map/ppermute | solution.py:29
  95.7 1.2 collective-permute-start.27
  97.0 4.6 %collective-permute-start.28 = (f32[1,2048]{1,0:T(1,128)S(1)}, f32[1,2048]{1,0:T(1,128)S(1)}, u32[]{:S(2)}, u32[]{:S(2)}) collective-permute-start(f32[1,2048]{1,0:T(1,128)S(1)} %add.109), channel_id=1, source_target_pairs={{0,24},{4,28},{8,16},{12,20},{16,8},{20,12},{24,0},{28,4},{1,25},{... | collective-permute-start | bytes 24584 | tf_op jit(solution)/shard_map/ppermute | solution.py:29
  99.5 3.7 %collective-permute-start.29 = (f32[1,2048]{1,0:T(1,128)S(1)}, f32[1,2048]{1,0:T(1,128)S(1)}, u32[]{:S(2)}, u32[]{:S(2)}) collective-permute-start(f32[1,2048]{1,0:T(1,128)S(1)} %add.109), channel_id=1, source_target_pairs={{0,16},{4,20},{8,24},{12,28},{16,0},{20,4},{24,8},{28,12},{1,17},{... | collective-permute-start | bytes 24584 | tf_op jit(solution)/shard_map/ppermute | solution.py:29
  100.0 3.7 %collective-permute-start.30 = (f32[1,2048]{1,0:T(1,128)S(1)}, f32[1,2048]{1,0:T(1,128)S(1)}, u32[]{:S(2)}, u32[]{:S(2)}) collective-permute-start(f32[1,2048]{1,0:T(1,128)S(1)} %add.109), channel_id=1, source_target_pairs={{0,8},{4,12},{8,0},{12,4},{16,24},{20,28},{24,16},{28,20},{1,9},{5... | collective-permute-start | bytes 24584 | tf_op jit(solution)/shard_map/ppermute | solution.py:29
  104.3 5.4 %collective-permute-start.31 = (f32[1,512]{1,0:T(1,128)S(1)}, f32[1,512]{1,0:T(1,128)S(1)}, u32[]{:S(2)}, u32[]{:S(2)}) collective-permute-start(f32[1,512]{1,0:T(1,128)S(1)} %get-tuple-element.59), channel_id=1, source_target_pairs={{0,3},{1,2},{2,1},{3,0},{4,7},{5,6},{6,5},{7,4},{8,11},{9,10},{10,... | collective-permute-start | bytes 6152 | tf_op jit(solution)/shard_map/ppermute | solution.py:29
  105.8 4.5 %collective-permute-start.32 = (f32[1,512]{1,0:T(1,128)S(1)}, f32[1,512]{1,0:T(1,128)S(1)}, u32[]{:S(2)}, u32[]{:S(2)}) collective-permute-start(f32[1,512]{1,0:T(1,128)S(1)} %get-tuple-element.59), channel_id=1, source_target_pairs={{0,2},{1,3},{2,0},{3,1},{4,6},{5,7},{6,4},{7,5},{8,10},{9,11},{10,... | collective-permute-start | bytes 6152 | tf_op jit(solution)/shard_map/ppermute | solution.py:29
  106.7 3.6 %collective-permute-start.33 = (f32[1,512]{1,0:T(1,128)S(1)}, f32[1,512]{1,0:T(1,128)S(1)}, u32[]{:S(2)}, u32[]{:S(2)}) collective-permute-start(f32[1,512]{1,0:T(1,128)S(1)} %get-tuple-element.59), channel_id=1, source_target_pairs={{0,1},{1,0},{2,3},{3,2},{4,5},{5,4},{6,7},{7,6},{8,9},{9,8},{10,11... | collective-permute-start | bytes 6152 | tf_op jit(solution)/shard_map/ppermute | solution.py:29
  115.6 3.5 %collective-permute-start.34 = (bf16[256,2048]{1,0:T(8,128)(2,1)S(1)}, bf16[256,2048]{1,0:T(8,128)(2,1)S(1)}, u32[]{:S(2)}, u32[]{:S(2)}) collective-permute-start(bf16[256,2048]{1,0:T(8,128)(2,1)S(1)} %get-tuple-element.61), channel_id=1, source_target_pairs={{0,4},{4,0},{8,12},{12,8},{16,20},{20,16},{24,28},{28,24},{1,5},{5... | collective-permute-start | bytes 3145736 | tf_op jit(solution)/shard_map/ppermute | solution.py:29
  119.1 9.4 %collective-permute-start.35 = (bf16[256,2048]{1,0:T(8,128)(2,1)S(1)}, bf16[256,2048]{1,0:T(8,128)(2,1)S(1)}, u32[]{:S(2)}, u32[]{:S(2)}) collective-permute-start(bf16[256,2048]{1,0:T(8,128)(2,1)S(1)} %get-tuple-element.70), channel_id=1, source_target_pairs={{0,4},{4,0},{8,12},{12,8},{16,20},{20,16},{24,28},{28,24},{1,5},{5... | collective-permute-start | bytes 3145736 | tf_op jit(solution)/shard_map/ppermute | solution.py:29
  119.7 8.8 %collective-permute-start.36 = (bf16[256,2048]{1,0:T(8,128)(2,1)S(1)}, bf16[256,2048]{1,0:T(8,128)(2,1)S(1)}, u32[]{:S(2)}, u32[]{:S(2)}) collective-permute-start(bf16[256,2048]{1,0:T(8,128)(2,1)S(1)} %get-tuple-element.71), channel_id=1, source_target_pairs={{0,4},{4,0},{8,12},{12,8},{16,20},{20,16},{24,28},{28,24},{1,5},{5... | collective-permute-start | bytes 3145736 | tf_op jit(solution)/shard_map/ppermute | solution.py:29
  120.0 14.9 %collective-permute-start.37 = (bf16[256,2048]{1,0:T(8,128)(2,1)S(1)}, bf16[256,2048]{1,0:T(8,128)(2,1)S(1)}, u32[]{:S(2)}, u32[]{:S(2)}) collective-permute-start(bf16[256,2048]{1,0:T(8,128)(2,1)S(1)} %shard_map.69.refs_8_), channel_id=1, source_target_pairs={{0,8},{4,20},{8,0},{12,28},{16,24},{20,4},{24,16},{28,12},{1,9},{5... | collective-permute-start | bytes 3145736 | tf_op jit(solution)/shard_map/ppermute | solution.py:34
  120.6 17.3 %collective-permute-start.40 = (bf16[512,512]{1,0:T(8,128)(2,1)S(1)}, bf16[512,512]{1,0:T(8,128)(2,1)S(1)}, u32[]{:S(2)}, u32[]{:S(2)}) collective-permute-start(bf16[512,512]{1,0:T(8,128)(2,1)S(1)} %get-tuple-element.79), channel_id=1, source_target_pairs={{0,1},{1,0},{2,3},{3,2},{4,5},{5,4},{6,7},{7,6},{8,9},{9,8},{10,11... | collective-permute-start | bytes 1572872 | tf_op jit(solution)/shard_map/ppermute | solution.py:29
  135.3 32.1 %collective-permute-start.39 = (bf16[256,2048]{1,0:T(8,128)(2,1)S(1)}, bf16[256,2048]{1,0:T(8,128)(2,1)S(1)}, u32[]{:S(2)}, u32[]{:S(2)}) collective-permute-start(bf16[256,2048]{1,0:T(8,128)(2,1)S(1)} %shard_map.72), channel_id=1, source_target_pairs={{0,16},{4,20},{8,24},{12,28},{16,0},{20,4},{24,8},{28,12},{1,17},{... | collective-permute-start | bytes 3145736 | tf_op jit(solution)/shard_map/ppermute | solution.py:29
  137.3 30.1 %collective-permute-start.38 = (bf16[256,2048]{1,0:T(8,128)(2,1)S(1)}, bf16[256,2048]{1,0:T(8,128)(2,1)S(1)}, u32[]{:S(2)}, u32[]{:S(2)}) collective-permute-start(bf16[256,2048]{1,0:T(8,128)(2,1)S(1)} %shard_map.71), channel_id=1, source_target_pairs={{0,8},{4,12},{8,0},{12,4},{16,24},{20,28},{24,16},{28,20},{1,9},{5... | collective-permute-start | bytes 3145736 | tf_op jit(solution)/shard_map/ppermute | solution.py:29
  137.9 29.5 %collective-permute-start.43 = (bf16[256,2048]{1,0:T(8,128)(2,1)S(1)}, bf16[256,2048]{1,0:T(8,128)(2,1)S(1)}, u32[]{:S(2)}, u32[]{:S(2)}) collective-permute-start(bf16[256,2048]{1,0:T(8,128)(2,1)S(1)} %get-tuple-element.84), channel_id=1, source_target_pairs={{0,4},{4,0},{8,12},{12,8},{16,20},{20,16},{24,28},{28,24},{1,5},{5... | collective-permute-start | bytes 3145736 | tf_op jit(solution)/shard_map/ppermute | solution.py:29
  138.1 24.8 %collective-permute-start.41 = (bf16[512,512]{1,0:T(8,128)(2,1)S(1)}, bf16[512,512]{1,0:T(8,128)(2,1)S(1)}, u32[]{:S(2)}, u32[]{:S(2)}) collective-permute-start(bf16[512,512]{1,0:T(8,128)(2,1)S(1)} %get-tuple-element.80), channel_id=1, source_target_pairs={{0,1},{1,0},{2,3},{3,2},{4,5},{5,4},{6,7},{7,6},{8,9},{9,8},{10,11... | collective-permute-start | bytes 1572872 | tf_op jit(solution)/shard_map/ppermute | solution.py:29
  140.2 26.2 %collective-permute-start.42 = (bf16[512,512]{1,0:T(8,128)(2,1)S(1)}, bf16[512,512]{1,0:T(8,128)(2,1)S(1)}, u32[]{:S(2)}, u32[]{:S(2)}) collective-permute-start(bf16[512,512]{1,0:T(8,128)(2,1)S(1)} %get-tuple-element.81), channel_id=1, source_target_pairs={{0,2},{1,3},{2,0},{3,1},{4,6},{5,7},{6,4},{7,5},{8,10},{9,11},{10,... | collective-permute-start | bytes 1572872 | tf_op jit(solution)/shard_map/ppermute | solution.py:29
